TPU v7x, 32 devices: a whole 2x2x4 slice. The times are simulated.
32 devices in a mesh: rep: 2 (over y), hid: 4 (over z), wid: 4 (over x, core).
Axes of the slice: x: 2, y: 2, z: 4, core: 2. Of those that a mesh axis runs over, the one named last changes fastest.
Arguments:
- tokens: bfloat16 [128, 8192], P(('rep', 'hid'), 'wid'), parts along dimension 0, may hold values from -6 to 6
- gate_weight: bfloat16 [8192, 26624], P('wid', 'hid'), may hold values from -0.0625 to 0.0625
- up_weight: bfloat16 [8192, 26624], P('wid', 'hid'), may hold values from -0.0625 to 0.0625
- down_weight: bfloat16 [26624, 8192], P('hid', 'wid'), may hold values from -0.0390625 to 0.0390625
Outputs:
- mixed: bfloat16 [128, 8192], P(('rep', 'hid'), 'wid'), parts along dimension 0
There are 2 independent parts, one for each index of `rep`. A program takes and returns all parts, laid end to end along the dimension named above; an argument that names none is the same for every part. Nothing has to cross between parts.
All inputs are finite; a program needn't handle non-finite values.
Results may differ from a plain program's by a relative error of at most 0.02.
Values may be sent and summed in bfloat16 or wider, within the bound.
No kernel may reach another device: no remote copies, remote signals or barrier semaphores. Data moves between devices by JAX's collectives and lax.ppermute only.
A program may use at most 192 MiB of HBM per device.

v0:
```python
import jax
import jax.numpy as jnp
from jax import lax
from jax.sharding import PartitionSpec as P


def on_device(tokens, gate_weight, up_weight, down_weight):
    piece = lax.all_gather(tokens, "hid", axis=0, tiled=True)
    gate_rows = jnp.dot(piece, gate_weight, preferred_element_type=jnp.float32)
    up_rows = jnp.dot(piece, up_weight, preferred_element_type=jnp.float32)
    partial_terms = jnp.stack([gate_rows, up_rows], 0)
    summed = lax.psum(partial_terms.astype(jnp.bfloat16), "wid").astype(jnp.float32)
    hidden = (jax.nn.silu(summed[0]) * summed[1]).astype(jnp.bfloat16)
    return lax.psum_scatter(
        jnp.dot(hidden, down_weight, preferred_element_type=jnp.float32).astype(jnp.bfloat16),
        "hid",
        scatter_dimension=0,
        tiled=True,
    )


def solution(mesh):
    return jax.shard_map(
        on_device,
        mesh=mesh,
        in_specs=(P(("rep", "hid"), "wid"), P("wid", "hid"), P("wid", "hid"), P("hid", "wid")),
        out_specs=P(("rep", "hid"), "wid"),
        check_vma=False,
    )
```

profile of v0, /device:TPU:0, one launch (start us, length us, event | category | flops | bytes accessed | tf_op | source)
XLA Modules:
  0.0 133.6 jit_solution(14873530212754971117)
XLA Ops:
  6.5 0.0 all-reduce.2.cloned.1.call-start
  6.5 15.8 %all_gather.3 = bf16[64,2048]{1,0:T(8,128)(2,1)S(1)} all-gather(bf16[16,2048]{1,0:T(8,128)(2,1)} %param.4), channel_id=1, replica_groups=mesh['rep'=2,'hid'=4,'wid'=4] {'hid'}, dimensions={0}, use_global_device_ids=true | all-gather | bytes 327680 | tf_op jit(solution)/shard_map/all_gather | solution.py:8
  22.4 11.3 %fusion.1 = bf16[1,64,6656]{2,1,0:T(8,128)(2,1)S(1)} fusion(bf16[64,2048]{1,0:T(8,128)(2,1)S(1)} %all_gather.3, bf16[2048,6656]{1,0:T(8,128)(2,1)} %param.6), kind=kOutput, calls=%fused_computation.3 | convolution fusion | flops 1745256448 | bytes 28377088 | tf_op jit(solution)/shard_map/dot_general | solution.py:10
  33.7 11.3 %fusion = bf16[1,64,6656]{2,1,0:T(8,128)(2,1)S(1)} fusion(bf16[64,2048]{1,0:T(8,128)(2,1)S(1)} %all_gather.3, bf16[2048,6656]{1,0:T(8,128)(2,1)} %param.5), kind=kOutput, calls=%fused_computation.2 | convolution fusion | flops 1745256448 | bytes 28377088 | tf_op jit(solution)/shard_map/dot_general | solution.py:9
  45.0 1.3 pad_maximum_fusion
  46.4 0.0 all-reduce.2.cloned.1.call-update
  46.4 0.0 reduce-scatter.2.cloned.1.call-start
  46.4 46.6 %all-reduce.2.cloned.1.call-done = bf16[2,64,6656]{2,1,0:T(8,128)(2,1)} async-done(((bf16[2,64,6656]{2,1,0:T(8,128)(2,1)}), bf16[2,64,6656]{2,1,0:T(8,128)(2,1)}) %all-reduce.2.cloned.1.call-update) | async-done | bytes 1703952 | tf_op jit(solution)/shard_map/psum | solution.py:12
  93.1 1.8 %convert_element_type.10 = f32[2,64,6656]{2,1,0:T(8,128)S(1)} convert(bf16[2,64,6656]{2,1,0:T(8,128)(2,1)} %all-reduce.2.cloned.1.call-done) | non-fusion elementwise | flops 851968 | bytes 5111808 | tf_op jit(solution)/shard_map/convert_element_type | solution.py:12
  94.9 12.0 %convolution_convert_fusion.2 = bf16[64,2048]{1,0:T(8,128)(2,1)} fusion(bf16[6656,2048]{1,0:T(8,128)(2,1)} %param.7, f32[2,64,6656]{2,1,0:T(8,128)S(1)} %convert_element_type.10), kind=kOutput, calls=%fused_computation.4 | convolution fusion | flops 1747517440 | bytes 30932992 | tf_op jit(solution)/shard_map/dot_general | solution.py:15
  106.9 0.0 reduce-scatter.2.cloned.1.call-update
  106.9 19.9 %reduce-scatter.2.cloned.1.call-done = bf16[16,2048]{1,0:T(8,128)(2,1)} async-done(((bf16[64,2048]{1,0:T(8,128)(2,1)}), bf16[16,2048]{1,0:T(8,128)(2,1)}) %reduce-scatter.2.cloned.1.call-update) | async-done | bytes 65552 | tf_op jit(solution)/shard_map/reduce_scatter | solution.py:14
Async XLA Ops:
  6.5 86.5 %all-reduce.2.cloned.1.call-start = ((), (), s32[]{:S(2)}) async-start(), calls=%async_computation.1 | async-start | bytes 3407872 | tf_op jit(solution)/shard_map/psum | solution.py:12
  46.4 80.4 %reduce-scatter.2.cloned.1.call-start = ((), (), s32[]{:S(2)}) async-start(), calls=%async_computation.2 | async-start | bytes 327680 | tf_op jit(solution)/shard_map/reduce_scatter | solution.py:14
Sparse Core Ops, SparseCore 0:
  46.5 46.5 all-reduce.1
  107.0 19.7 reduce-scatter.1
where the time goes:
time: 134 us
  waiting for transfers between devices  66.5 us (50%)
  matrix products  34.7 us (26%)
  blocking collectives  15.8 us (12%)
  between operations  13.4 us (10%)
  other arithmetic  3.12 us (2%)
    psum x1, waiting for transfers between devices, on_device(): lax.psum(partial_terms.astype(jnp.bfloat16), 'wid').astype(jnp.float32)  46.6 us
    reduce_scatter x1, waiting for transfers between devices, on_device(): lax.psum_scatter(jnp.dot(hidden, down_weight, preferred_element_type=jnp....  19.9 us
    all_gather x1, blocking collectives, on_device(): piece = lax.all_gather(tokens, 'hid', axis=0, tiled=True)  15.8 us
    dot_general x1, matrix products, on_device(): jnp.dot(hidden, down_weight, preferred_element_type=jnp.float32)  12 us
    dot_general x1, matrix products, on_device(): gate_rows = jnp.dot(piece, gate_weight, preferred_element_type=jnp.float32)  11.3 us
    dot_general x1, matrix products, on_device(): up_rows = jnp.dot(piece, up_weight, preferred_element_type=jnp.float32)  11.3 us
  transfers between devices with their start and end apart: 2, of which 2 were waited for; matrix products, arithmetic and copies ran while one was open for 0% of the time, Pallas kernels for 0%

commit v1 on v0

--- a/solution.py
+++ b/solution.py
@@ -1,10 +1,17 @@
+import functools
+
 import jax
 import jax.numpy as jnp
 from jax import lax
+from jax.experimental import pallas as pl
+from jax.experimental.pallas import tpu as pltpu
 from jax.sharding import PartitionSpec as P
 
-
-def on_device(tokens, gate_weight, up_weight, down_weight):
+TILE = 256
+CHUNKS = 2
+
+
+def plain(tokens, gate_weight, up_weight, down_weight):
     piece = lax.all_gather(tokens, "hid", axis=0, tiled=True)
     gate_rows = jnp.dot(piece, gate_weight, preferred_element_type=jnp.float32)
     up_rows = jnp.dot(piece, up_weight, preferred_element_type=jnp.float32)
@@ -19,7 +26,180 @@
     )
 
 
+ORDER = (0, 2, 1, 3)
+PLACE = (0, 2, 1, 3)
+
+
+def gate_up_kernel(n_blocks, rows, scalars, *refs):
+    blocks, (gate_ref, up_ref, mine_ref, theirs_ref, x_ref) = refs[:n_blocks], refs[n_blocks:]
+
+    @pl.when(pl.program_id(0) == 0)
+    def _():
+        for b in range(n_blocks):
+            start = pl.multiple_of(scalars[1 + b] * rows, rows)
+            x_ref[pl.ds(start, rows), :] = blocks[b][...]
+
+    half = x_ref.shape[0] // 2
+    for k, w_ref in enumerate((gate_ref, up_ref)):
+        part = jnp.dot(x_ref[...], w_ref[...], preferred_element_type=jnp.float32).astype(jnp.bfloat16)
+        mine_ref[k] = part[:half]
+        theirs_ref[k] = part[half:]
+
+
+def gate_up(scalars, blocks, gate_weight, up_weight, first, tiles):
+    depth = gate_weight.shape[0]
+    rows = blocks[0].shape[0]
+    n = len(blocks)
+    total = n * rows
+    width = tiles * TILE
+    weight_spec = pl.BlockSpec((depth, TILE), lambda i, s: (0, s[0] + first + i))
+    out_spec = pl.BlockSpec((2, total // 2, TILE), lambda i, s: (0, 0, i))
+    return pl.pallas_call(
+        functools.partial(gate_up_kernel, n, rows),
+        grid_spec=pltpu.PrefetchScalarGridSpec(
+            num_scalar_prefetch=1,
+            grid=(tiles,),
+            in_specs=[pl.BlockSpec((rows, depth), lambda i, s: (0, 0))] * n + [weight_spec] * 2,
+            out_specs=[out_spec] * 2,
+            scratch_shapes=[pltpu.VMEM((total, depth), jnp.bfloat16)],
+        ),
+        out_shape=[jax.ShapeDtypeStruct((2, total // 2, width), jnp.bfloat16)] * 2,
+        compiler_params=pltpu.CompilerParams(vmem_limit_bytes=32 * 2**20),
+        cost_estimate=pl.CostEstimate(
+            flops=4 * total * depth * width, bytes_accessed=4 * depth * width, transcendentals=0
+        ),
+        name="gate_up",
+    )(scalars, *blocks, gate_weight, up_weight)
+
+
+def down_kernel(n_pieces, n_blocks, has_acc, last, scalars, *refs):
+    pieces, refs = refs[:n_pieces], refs[n_pieces:]
+    w_ref, refs = refs[0], refs[1:]
+    prev_ref, refs = (refs[0], refs[1:]) if has_acc else (None, refs)
+    outs, acc_ref = (refs[:-1], refs[-1]) if last else ((), refs[0])
+    step = pl.program_id(0)
+
+    @pl.when(step == 0)
+    def _():
+        acc_ref[...] = prev_ref[...] if has_acc else jnp.zeros_like(acc_ref)
+
+    at = 0
+    for piece in pieces:
+        n = piece.shape[0]
+        acc_ref[at : at + n, :] += jnp.dot(piece[...], w_ref[...], preferred_element_type=jnp.float32)
+        at += n
+
+    if last:
+
+        @pl.when(step == pl.num_programs(0) - 1)
+        def _():
+            for b in range(n_blocks):
+                rows = outs[b].shape[0]
+                start = pl.multiple_of(scalars[1 + b] * rows, rows)
+                outs[b][...] = acc_ref[pl.ds(start, rows), :].astype(jnp.bfloat16)
+
+
+def down(scalars, pieces, down_weight, prev, first, tiles, n_blocks, last):
+    width = down_weight.shape[1]
+    total = sum(p.shape[0] for p in pieces)
+    rows = total // n_blocks
+    whole = pl.BlockSpec((total, width), lambda i, s: (0, 0))
+    in_specs = [pl.BlockSpec((p.shape[0], TILE), lambda i, s: (0, i)) for p in pieces]
+    in_specs.append(pl.BlockSpec((TILE, width), lambda i, s: (s[0] + first + i, 0)))
+    args = [*pieces, down_weight]
+    if prev is not None:
+        in_specs.append(whole)
+        args.append(prev)
+    if last:
+        out_specs = [pl.BlockSpec((rows, width), lambda i, s: (0, 0))] * n_blocks
+        out_shape = [jax.ShapeDtypeStruct((rows, width), jnp.bfloat16)] * n_blocks
+        scratch = [pltpu.VMEM((total, width), jnp.float32)]
+    else:
+        out_specs, out_shape, scratch = whole, jax.ShapeDtypeStruct((total, width), jnp.float32), []
+    return pl.pallas_call(
+        functools.partial(down_kernel, len(pieces), n_blocks, prev is not None, last),
+        grid_spec=pltpu.PrefetchScalarGridSpec(
+            num_scalar_prefetch=1,
+            grid=(tiles,),
+            in_specs=in_specs,
+            out_specs=out_specs,
+            scratch_shapes=scratch,
+        ),
+        out_shape=out_shape,
+        compiler_params=pltpu.CompilerParams(vmem_limit_bytes=32 * 2**20),
+        cost_estimate=pl.CostEstimate(
+            flops=2 * total * width * tiles * TILE, bytes_accessed=2 * width * tiles * TILE, transcendentals=0
+        ),
+        name="down",
+    )(scalars, *args)
+
+
+def split_by_rep(n_rep, n_hid, n_wid, tokens, gate_weight, up_weight, down_weight):
+    rep, hid, wid = lax.axis_index("rep"), lax.axis_index("hid"), lax.axis_index("wid")
+    n = n_rep * n_hid
+    per = n // n_wid
+    tiles = gate_weight.shape[1] // (n_rep * TILE)
+
+    def shift(b, back):
+        r, h = divmod(b, n_hid)
+        sign = -1 if back else 1
+        pairs = []
+        for i in range(n_rep):
+            for j in range(n_hid):
+                here = i * n_hid + j
+                there = ((i + r) % n_rep) * n_hid + (j + h) % n_hid
+                pairs.append((here, there) if back else (there, here))
+        return pairs
+
+    place = jnp.asarray(PLACE, jnp.int32)
+    owner = jnp.arange(n, dtype=jnp.int32)
+    at = place[wid ^ (owner // per)] * per + owner % per
+    scalars = jnp.concatenate([jnp.asarray([rep * tiles], jnp.int32), at])
+
+    blocks = [tokens] + [lax.ppermute(tokens, ("rep", "hid"), shift(b, False)) for b in range(1, n)]
+
+    core = [(w, w ^ 1) for w in range(n_wid)]
+    chip = [(w, w ^ 2) for w in range(n_wid)]
+    f32 = jnp.float32
+
+    bounds = [tiles * c // CHUNKS for c in range(CHUNKS + 1)]
+    acc = None
+    for c in range(CHUNKS):
+        first, count = bounds[c], bounds[c + 1] - bounds[c]
+        mine, theirs = gate_up(scalars, blocks, gate_weight, up_weight, first, count)
+        got = lax.ppermute(theirs, "wid", core)
+        quarter = mine.shape[1] // 2
+        to_chip = (mine[:, quarter:].astype(f32) + got[:, quarter:].astype(f32)).astype(jnp.bfloat16)
+        from_chip = lax.ppermute(to_chip, "wid", chip)
+        summed = mine[:, :quarter].astype(f32) + got[:, :quarter].astype(f32) + from_chip.astype(f32)
+        own = (jax.nn.silu(summed[0]) * summed[1]).astype(jnp.bfloat16)
+        other = lax.ppermute(own, "wid", chip)
+        own_core = lax.ppermute(own, "wid", core)
+        other_core = lax.ppermute(other, "wid", core)
+        acc = down(
+            scalars, [own, other, own_core, other_core], down_weight, acc, first, count, n, c == CHUNKS - 1
+        )
+
+    mixed = acc[0].astype(f32)
+    for b in range(1, n):
+        mixed = mixed + lax.ppermute(acc[b], ("rep", "hid"), shift(b, True)).astype(f32)
+    return mixed.astype(jnp.bfloat16)
+
+
 def solution(mesh):
+    n_rep, n_hid, n_wid = (mesh.shape[a] for a in ("rep", "hid", "wid"))
+
+    def on_device(tokens, gate_weight, up_weight, down_weight):
+        fits = (
+            n_wid == len(ORDER)
+            and n_rep * n_hid % n_wid == 0
+            and gate_weight.shape[1] % (n_rep * TILE) == 0
+            and tokens.shape[0] % 16 == 0
+        )
+        if not fits:
+            return plain(tokens, gate_weight, up_weight, down_weight)
+        return split_by_rep(n_rep, n_hid, n_wid, tokens, gate_weight, up_weight, down_weight)
+
     return jax.shard_map(
         on_device,
         mesh=mesh,

time: 134 us -> 88.2 us (0.66)
  waiting for transfers between devices: 66.5 us -> 16.5 us
  matrix products: 34.7 us -> 0 us
  starting transfers between devices: 0.04 us -> 34.2 us
  Pallas kernels: 0 us -> 33.5 us
  blocking collectives: 15.8 us -> 0 us
  between operations: 13.4 us -> 0.14 us
  local copies, waits for them, and re-layouts: 0 us -> 2.14 us
  other arithmetic: 3.12 us -> 1.19 us
    psum x1 -> x0, waiting for transfers between devices: 46.6 us -> none  [on_device(): lax.psum(partial_terms.astype(jnp.bfloat16), 'wid').astype(jnp.float32)]
    dot_general x3 -> x0, matrix products: 34.7 us -> none  [the longest x1 12 us: on_device(): jnp.dot(hidden, down_weight, preferred_element_type=jnp.float32)]
    ppermute x0 -> x24, starting transfers between devices: none -> 34.2 us  [the longest x7 13.5 us: split_by_rep(): lax.ppermute(tokens, ('rep', 'hid'), shift(b, False))]
    pallas_call x0 -> x4, Pallas kernels: none -> 33.5 us  [the longest x2 17 us: down(): pl.pallas_call(functools.partial(down_kernel, len(pieces), n_blocks, prev...]
    reduce_scatter x1 -> x0, waiting for transfers between devices: 19.9 us -> none  [on_device(): lax.psum_scatter(jnp.dot(hidden, down_weight, preferred_element_type=jnp....]
    ppermute x0 -> x24, waiting for transfers between devices: none -> 16.5 us  [the longest x2 8.02 us: split_by_rep(): from_chip = lax.ppermute(to_chip, 'wid', chip)]
    all_gather x1 -> x0, blocking collectives: 15.8 us -> none  [on_device(): piece = lax.all_gather(tokens, 'hid', axis=0, tiled=True)]
  transfers between devices with their start and end apart: 2 -> 24, of which waited for: 2 -> 9; matrix products, arithmetic and copies ran while one was open for 0% -> 2% of each run, Pallas kernels for 0% -> 19%
where the time goes in v1:
time: 88.2 us; the launch traced here: 87.7 us
  starting transfers between devices  34.2 us (39%)
  Pallas kernels  33.5 us (38%)
  waiting for transfers between devices  16.5 us (19%)
  local copies, waits for them, and re-layouts  2.14 us (2%)
  other arithmetic  1.19 us (1%)
    pallas_call x2, Pallas kernels, down(): pl.pallas_call(functools.partial(down_kernel, len(pieces), n_blocks, prev...  17 us
    pallas_call x2, Pallas kernels, gate_up(): pl.pallas_call(functools.partial(gate_up_kernel, n, rows), grid_spec=pltp...  16.6 us
    ppermute x7, starting transfers between devices, split_by_rep(): lax.ppermute(tokens, ('rep', 'hid'), shift(b, False))  13.5 us
    ppermute x7, starting transfers between devices, split_by_rep(): lax.ppermute(acc[b], ('rep', 'hid'), shift(b, True)).astype(f32)  13.4 us
    ppermute x2, waiting for transfers between devices, split_by_rep(): from_chip = lax.ppermute(to_chip, 'wid', chip)  8.02 us
    ppermute x7, waiting for transfers between devices, split_by_rep(): lax.ppermute(tokens, ('rep', 'hid'), shift(b, False))  3.27 us
    ppermute x2, starting transfers between devices, split_by_rep(): other = lax.ppermute(own, 'wid', chip)  3.13 us
    ppermute x2, starting transfers between devices, split_by_rep(): from_chip = lax.ppermute(to_chip, 'wid', chip)  2.96 us
  transfers between devices with their start and end apart: 24, of which 9 were waited for; matrix products, arithmetic and copies ran while one was open for 2% of the time, Pallas kernels for 19%

profile of v1, /device:TPU:0, one launch (start us, length us, event | category | flops | bytes accessed | tf_op | source)
XLA Modules:
  0.0 87.7 jit_solution(6489142605383837480)
XLA Ops:
  0.0 4.0 %collective-permute-start.6 = (bf16[16,2048]{1,0:T(8,128)(2,1)}, bf16[16,2048]{1,0:T(8,128)(2,1)S(1)}, u32[]{:S(2)}, u32[]{:S(2)}) collective-permute-start(bf16[16,2048]{1,0:T(8,128)(2,1)} %refs_0_.3), channel_id=1, source_target_pairs={{28,0},{16,4},{20,8},{24,12},{12,16},{0,20},{4,24},{8,28},{29,1},{... | collective-permute-start | bytes 196616 | tf_op jit(solution)/shard_map/ppermute | solution.py:159
  4.0 2.5 %collective-permute-start.5 = (bf16[16,2048]{1,0:T(8,128)(2,1)}, bf16[16,2048]{1,0:T(8,128)(2,1)S(1)}, u32[]{:S(2)}, u32[]{:S(2)}) collective-permute-start(bf16[16,2048]{1,0:T(8,128)(2,1)} %refs_0_.3), channel_id=1, source_target_pairs={{24,0},{28,4},{16,8},{20,12},{8,16},{12,20},{0,24},{4,28},{25,1},{... | collective-permute-start | bytes 196616 | tf_op jit(solution)/shard_map/ppermute | solution.py:159
  6.5 2.3 %collective-permute-start.4 = (bf16[16,2048]{1,0:T(8,128)(2,1)}, bf16[16,2048]{1,0:T(8,128)(2,1)S(1)}, u32[]{:S(2)}, u32[]{:S(2)}) collective-permute-start(bf16[16,2048]{1,0:T(8,128)(2,1)} %refs_0_.3), channel_id=1, source_target_pairs={{20,0},{24,4},{28,8},{16,12},{4,16},{8,20},{12,24},{0,28},{21,1},{... | collective-permute-start | bytes 196616 | tf_op jit(solution)/shard_map/ppermute | solution.py:159
  8.8 0.5 collective-permute-start.3
  9.3 0.7 collective-permute-start.2
  10.0 1.3 %gather_fusion = s32[8]{0:T(128)S(1)} fusion(s32[4]{0:T(128)} %constant.52.clone, s32[1024]{0:T(1024)S(1)} %pad_clamp_fusion), kind=kCustom, calls=%fused_computation | custom fusion | bytes 96 | tf_op jit(solution)/shard_map/gather | solution.py:156
  11.4 0.4 collective-permute-start.1
  11.8 0.4 collective-permute-done.5.refs_6_
  12.2 3.1 %collective-permute-start = (bf16[16,2048]{1,0:T(8,128)(2,1)}, bf16[16,2048]{1,0:T(8,128)(2,1)S(1)}, u32[]{:S(2)}, u32[]{:S(2)}) collective-permute-start(bf16[16,2048]{1,0:T(8,128)(2,1)} %refs_0_.3), channel_id=1, source_target_pairs={{4,0},{8,4},{12,8},{0,12},{20,16},{24,20},{28,24},{16,28},{5,1},{9... | collective-permute-start | bytes 196616 | tf_op jit(solution)/shard_map/ppermute | solution.py:159
  15.3 0.1 pad_add_fusion.scalars
  15.4 0.0 collective-permute-done.4.refs_5_
  15.4 0.0 collective-permute-done.3.refs_4_
  15.4 0.8 collective-permute-done.2.refs_3_
  16.2 1.9 %collective-permute-done.1.refs_2_ = bf16[16,2048]{1,0:T(8,128)(2,1)S(1)} collective-permute-done((bf16[16,2048]{1,0:T(8,128)(2,1)}, bf16[16,2048]{1,0:T(8,128)(2,1)S(1)}, u32[]{:S(2)}, u32[]{:S(2)}) %collective-permute-start.1) | collective-permute-done | bytes 65568 | tf_op jit(solution)/shard_map/ppermute | solution.py:159
  18.1 0.1 collective-permute-done.refs_1_
  18.2 0.8 copy-done
  19.1 7.7 %gate_up.3 = (bf16[2,64,1536]{2,1,0:T(8,128)(2,1)S(1)}, bf16[2,64,1536]{2,1,0:T(8,128)(2,1)S(1)}) custom-call(s32[9]{0:T(128)S(1)} %pad_add_fusion.scalars, bf16[16,2048]{1,0:T(8,128)(2,1)S(1)} %copy-done, bf16[16,2048]{1,0:T(8,128)(2,1)S(1)} %collective-permute-done.refs_1_, bf16[16,2048]{1,0:T(8,128)(2,1)S(1)} %collective-permute-done.1.refs_2_, ...), custom_call_target="tpu_custom_call" | custom-call | flops 1610612736 | bytes 12582912 | tf_op jit(solution)/shard_map/gate_up/pallas_call | solution.py:57
  26.7 0.1 collective-permute-start.12
  26.8 8.9 %gate_up.2 = (bf16[2,64,1792]{2,1,0:T(8,128)(2,1)S(1)}, bf16[2,64,1792]{2,1,0:T(8,128)(2,1)S(1)}) custom-call(s32[9]{0:T(128)S(1)} %pad_add_fusion.scalars, bf16[16,2048]{1,0:T(8,128)(2,1)S(1)} %copy-done, bf16[16,2048]{1,0:T(8,128)(2,1)S(1)} %collective-permute-done.refs_1_, bf16[16,2048]{1,0:T(8,128)(2,1)S(1)} %collective-permute-done.1.refs_2_, ...), custom_call_target="tpu_custom_call" | custom-call | flops 1879048192 | bytes 14680064 | tf_op jit(solution)/shard_map/gate_up/pallas_call | solution.py:57
  35.8 0.6 collective-permute-start.7
  36.3 0.0 collective-permute-done.12
  36.4 1.6 %collective-permute-start.13 = (bf16[2,32,1536]{2,1,0:T(8,128)(2,1)S(1)}, bf16[2,32,1536]{2,1,0:T(8,128)(2,1)S(1)}, u32[]{:S(2)}, u32[]{:S(2)}) collective-permute-start(bf16[2,32,1536]{2,1,0:T(8,128)(2,1)S(1)} %add_convert_fusion.1), channel_id=1, source_target_pairs={{0,2},{1,3},{2,0},{3,1},{4,6},{5,7},{6,4},{7,5},{8,10},{9,11},{10,... | collective-permute-start | bytes 589832 | tf_op jit(solution)/shard_map/ppermute | solution.py:173
  37.9 0.0 collective-permute-done.7
  37.9 0.1 add_convert_fusion
  38.0 1.4 %collective-permute-start.8 = (bf16[2,32,1792]{2,1,0:T(8,128)(2,1)S(1)}, bf16[2,32,1792]{2,1,0:T(8,128)(2,1)S(1)}, u32[]{:S(2)}, u32[]{:S(2)}) collective-permute-start(bf16[2,32,1792]{2,1,0:T(8,128)(2,1)S(1)} %add_convert_fusion), channel_id=1, source_target_pairs={{0,2},{1,3},{2,0},{3,1},{4,6},{5,7},{6,4},{7,5},{8,10},{9,11},{10,... | collective-permute-start | bytes 688136 | tf_op jit(solution)/shard_map/ppermute | solution.py:173
  39.4 4.8 %collective-permute-done.13 = bf16[2,32,1536]{2,1,0:T(8,128)(2,1)S(1)} collective-permute-done((bf16[2,32,1536]{2,1,0:T(8,128)(2,1)S(1)}, bf16[2,32,1536]{2,1,0:T(8,128)(2,1)S(1)}, u32[]{:S(2)}, u32[]{:S(2)}) %collective-permute-start.13) | collective-permute-done | bytes 196640 | tf_op jit(solution)/shard_map/ppermute | solution.py:173
  44.2 0.1 convert_add_fusion.1
  44.3 0.1 fusion.3.refs_0_
  44.4 1.6 %collective-permute-start.14 = (bf16[32,1536]{1,0:T(8,128)(2,1)S(1)}, bf16[32,1536]{1,0:T(8,128)(2,1)S(1)}, u32[]{:S(2)}, u32[]{:S(2)}) collective-permute-start(bf16[32,1536]{1,0:T(8,128)(2,1)S(1)} %fusion.3.refs_0_), channel_id=1, source_target_pairs={{0,2},{1,3},{2,0},{3,1},{4,6},{5,7},{6,4},{7,5},{8,10},{9,11},{10,... | collective-permute-start | bytes 294920 | tf_op jit(solution)/shard_map/ppermute | solution.py:176
  45.9 3.2 %collective-permute-done.8 = bf16[2,32,1792]{2,1,0:T(8,128)(2,1)S(1)} collective-permute-done((bf16[2,32,1792]{2,1,0:T(8,128)(2,1)S(1)}, bf16[2,32,1792]{2,1,0:T(8,128)(2,1)S(1)}, u32[]{:S(2)}, u32[]{:S(2)}) %collective-permute-start.8) | collective-permute-done | bytes 229408 | tf_op jit(solution)/shard_map/ppermute | solution.py:173
  49.1 0.1 convert_add_fusion
  49.2 0.1 fusion.1.refs_0_
  49.3 1.6 %collective-permute-start.9 = (bf16[32,1792]{1,0:T(8,128)(2,1)S(1)}, bf16[32,1792]{1,0:T(8,128)(2,1)S(1)}, u32[]{:S(2)}, u32[]{:S(2)}) collective-permute-start(bf16[32,1792]{1,0:T(8,128)(2,1)S(1)} %fusion.1.refs_0_), channel_id=1, source_target_pairs={{0,2},{1,3},{2,0},{3,1},{4,6},{5,7},{6,4},{7,5},{8,10},{9,11},{10,... | collective-permute-start | bytes 344072 | tf_op jit(solution)/shard_map/ppermute | solution.py:176
  50.9 0.5 collective-permute-start.16
  51.4 0.0 collective-permute-start.10
  51.4 2.8 %collective-permute-done.9.refs_1_ = bf16[32,1792]{1,0:T(8,128)(2,1)S(1)} collective-permute-done((bf16[32,1792]{1,0:T(8,128)(2,1)S(1)}, bf16[32,1792]{1,0:T(8,128)(2,1)S(1)}, u32[]{:S(2)}, u32[]{:S(2)}) %collective-permute-start.9) | collective-permute-done | bytes 114720 | tf_op jit(solution)/shard_map/ppermute | solution.py:176
  54.2 7.9 %down.2.refs_5_ = f32[128,2048]{1,0:T(8,128)S(1)} custom-call(s32[9]{0:T(128)S(1)} %pad_add_fusion.scalars, bf16[32,1536]{1,0:T(8,128)(2,1)S(1)} %fusion.3.refs_0_, bf16[32,1536]{1,0:T(8,128)(2,1)S(1)} %collective-permute-done.14.refs_1_, bf16[32,1536]{1,0:T(8,128)(2,1)S(1)} %collective-permute-done.15.refs_2_, ...), custom_call_target="tpu_custom_call" | custom-call | flops 805306368 | bytes 6291456 | tf_op jit(solution)/shard_map/down/pallas_call | solution.py:119
  62.0 0.0 collective-permute-done.10.refs_2_
  62.1 9.1 %down.3 = (bf16[16,2048]{1,0:T(8,128)(2,1)S(1)}, bf16[16,2048]{1,0:T(8,128)(2,1)S(1)}, bf16[16,2048]{1,0:T(8,128)(2,1)S(1)}, bf16[16,2048]{1,0:T(8,128)(2,1)S(1)...) custom-call(s32[9]{0:T(128)S(1)} %pad_add_fusion.scalars, ...), custom_call_target="tpu_custom_call" | custom-call | flops 939524096 | bytes 7340032 | tf_op jit(solution)/shard_map/down/pallas_call | solution.py:119
  71.1 1.4 %collective-permute-start.17 = (bf16[16,2048]{1,0:T(8,128)(2,1)S(1)}, bf16[16,2048]{1,0:T(8,128)(2,1)S(1)}, u32[]{:S(2)}, u32[]{:S(2)}) collective-permute-start(bf16[16,2048]{1,0:T(8,128)(2,1)S(1)} %get-tuple-element.22), channel_id=1, source_target_pairs={{0,4},{4,8},{8,12},{12,0},{16,20},{20,24},{24,28},{28,16},{1,5},{5... | collective-permute-start | bytes 196616 | tf_op jit(solution)/shard_map/ppermute | solution.py:185
  72.6 2.5 %collective-permute-start.18 = (bf16[16,2048]{1,0:T(8,128)(2,1)S(1)}, bf16[16,2048]{1,0:T(8,128)(2,1)S(1)}, u32[]{:S(2)}, u32[]{:S(2)}) collective-permute-start(bf16[16,2048]{1,0:T(8,128)(2,1)S(1)} %get-tuple-element.23), channel_id=1, source_target_pairs={{0,8},{4,12},{8,0},{12,4},{16,24},{20,28},{24,16},{28,20},{1,9},{5... | collective-permute-start | bytes 196616 | tf_op jit(solution)/shard_map/ppermute | solution.py:185
  75.1 1.4 %collective-permute-start.20 = (bf16[16,2048]{1,0:T(8,128)(2,1)S(1)}, bf16[16,2048]{1,0:T(8,128)(2,1)S(1)}, u32[]{:S(2)}, u32[]{:S(2)}) collective-permute-start(bf16[16,2048]{1,0:T(8,128)(2,1)S(1)} %get-tuple-element.25), channel_id=1, source_target_pairs={{0,16},{4,20},{8,24},{12,28},{16,0},{20,4},{24,8},{28,12},{1,17},{... | collective-permute-start | bytes 196616 | tf_op jit(solution)/shard_map/ppermute | solution.py:185
  76.6 2.1 %collective-permute-start.21 = (bf16[16,2048]{1,0:T(8,128)(2,1)S(1)}, bf16[16,2048]{1,0:T(8,128)(2,1)S(1)}, u32[]{:S(2)}, u32[]{:S(2)}) collective-permute-start(bf16[16,2048]{1,0:T(8,128)(2,1)S(1)} %get-tuple-element.26), channel_id=1, source_target_pairs={{0,20},{4,24},{8,28},{12,16},{16,4},{20,8},{24,12},{28,0},{1,21},{... | collective-permute-start | bytes 196616 | tf_op jit(solution)/shard_map/ppermute | solution.py:185
  78.6 1.3 %collective-permute-start.22 = (bf16[16,2048]{1,0:T(8,128)(2,1)S(1)}, bf16[16,2048]{1,0:T(8,128)(2,1)S(1)}, u32[]{:S(2)}, u32[]{:S(2)}) collective-permute-start(bf16[16,2048]{1,0:T(8,128)(2,1)S(1)} %get-tuple-element.27), channel_id=1, source_target_pairs={{0,24},{4,28},{8,16},{12,20},{16,8},{20,12},{24,0},{28,4},{1,25},{... | collective-permute-start | bytes 196616 | tf_op jit(solution)/shard_map/ppermute | solution.py:185
  80.0 0.5 collective-permute-done.18
  80.4 4.6 %collective-permute-start.23 = (bf16[16,2048]{1,0:T(8,128)(2,1)S(1)}, bf16[16,2048]{1,0:T(8,128)(2,1)S(1)}, u32[]{:S(2)}, u32[]{:S(2)}) collective-permute-start(bf16[16,2048]{1,0:T(8,128)(2,1)S(1)} %get-tuple-element.28), channel_id=1, source_target_pairs={{0,28},{4,16},{8,20},{12,24},{16,12},{20,0},{24,4},{28,8},{1,29},{... | collective-permute-start | bytes 196616 | tf_op jit(solution)/shard_map/ppermute | solution.py:185
  85.0 1.9 %collective-permute-done.22 = bf16[16,2048]{1,0:T(8,128)(2,1)S(1)} collective-permute-done((bf16[16,2048]{1,0:T(8,128)(2,1)S(1)}, bf16[16,2048]{1,0:T(8,128)(2,1)S(1)}, u32[]{:S(2)}, u32[]{:S(2)}) %collective-permute-start.22) | collective-permute-done | bytes 65568 | tf_op jit(solution)/shard_map/ppermute | solution.py:185
  87.0 0.7 add_convert_fusion.2
  (18 shorter events, 0.1 us)
Async XLA Ops:
  0.0 11.3 %collective-permute-start.6 = (bf16[16,2048]{1,0:T(8,128)(2,1)}, bf16[16,2048]{1,0:T(8,128)(2,1)S(1)}, u32[]{:S(2)}, u32[]{:S(2)}) collective-permute-start(bf16[16,2048]{1,0:T(8,128)(2,1)} %refs_0_.3), channel_id=1, source_target_pairs={{28,0},{16,4},{20,8},{24,12},{12,16},{0,20},{4,24},{8,28},{29,1},{... | collective-permute-start | bytes 196616 | tf_op jit(solution)/shard_map/ppermute | solution.py:159
  4.0 8.2 %collective-permute-start.5 = (bf16[16,2048]{1,0:T(8,128)(2,1)}, bf16[16,2048]{1,0:T(8,128)(2,1)S(1)}, u32[]{:S(2)}, u32[]{:S(2)}) collective-permute-start(bf16[16,2048]{1,0:T(8,128)(2,1)} %refs_0_.3), channel_id=1, source_target_pairs={{24,0},{28,4},{16,8},{20,12},{8,16},{12,20},{0,24},{4,28},{25,1},{... | collective-permute-start | bytes 196616 | tf_op jit(solution)/shard_map/ppermute | solution.py:159
  6.5 8.9 %collective-permute-start.4 = (bf16[16,2048]{1,0:T(8,128)(2,1)}, bf16[16,2048]{1,0:T(8,128)(2,1)S(1)}, u32[]{:S(2)}, u32[]{:S(2)}) collective-permute-start(bf16[16,2048]{1,0:T(8,128)(2,1)} %refs_0_.3), channel_id=1, source_target_pairs={{20,0},{24,4},{28,8},{16,12},{4,16},{8,20},{12,24},{0,28},{21,1},{... | collective-permute-start | bytes 196616 | tf_op jit(solution)/shard_map/ppermute | solution.py:159
  8.8 6.6 %collective-permute-start.3 = (bf16[16,2048]{1,0:T(8,128)(2,1)}, bf16[16,2048]{1,0:T(8,128)(2,1)S(1)}, u32[]{:S(2)}, u32[]{:S(2)}) collective-permute-start(bf16[16,2048]{1,0:T(8,128)(2,1)} %refs_0_.3), channel_id=1, source_target_pairs={{16,0},{20,4},{24,8},{28,12},{0,16},{4,20},{8,24},{12,28},{17,1},{... | collective-permute-start | bytes 196616 | tf_op jit(solution)/shard_map/ppermute | solution.py:159
  9.3 6.8 %collective-permute-start.2 = (bf16[16,2048]{1,0:T(8,128)(2,1)}, bf16[16,2048]{1,0:T(8,128)(2,1)S(1)}, u32[]{:S(2)}, u32[]{:S(2)}) collective-permute-start(bf16[16,2048]{1,0:T(8,128)(2,1)} %refs_0_.3), channel_id=1, source_target_pairs={{12,0},{0,4},{4,8},{8,12},{28,16},{16,20},{20,24},{24,28},{13,1},{... | collective-permute-start | bytes 196616 | tf_op jit(solution)/shard_map/ppermute | solution.py:159
  11.4 6.8 %collective-permute-start.1 = (bf16[16,2048]{1,0:T(8,128)(2,1)}, bf16[16,2048]{1,0:T(8,128)(2,1)S(1)}, u32[]{:S(2)}, u32[]{:S(2)}) collective-permute-start(bf16[16,2048]{1,0:T(8,128)(2,1)} %refs_0_.3), channel_id=1, source_target_pairs={{8,0},{12,4},{0,8},{4,12},{24,16},{28,20},{16,24},{20,28},{9,1},{1... | collective-permute-start | bytes 196616 | tf_op jit(solution)/shard_map/ppermute | solution.py:159
  12.2 6.1 %collective-permute-start = (bf16[16,2048]{1,0:T(8,128)(2,1)}, bf16[16,2048]{1,0:T(8,128)(2,1)S(1)}, u32[]{:S(2)}, u32[]{:S(2)}) collective-permute-start(bf16[16,2048]{1,0:T(8,128)(2,1)} %refs_0_.3), channel_id=1, source_target_pairs={{4,0},{8,4},{12,8},{0,12},{20,16},{24,20},{28,24},{16,28},{5,1},{9... | collective-permute-start | bytes 196616 | tf_op jit(solution)/shard_map/ppermute | solution.py:159
  18.2 0.8 copy-start
  26.7 9.6 %collective-permute-start.12 = (bf16[2,64,1536]{2,1,0:T(8,128)(2,1)S(1)}, bf16[2,64,1536]{2,1,0:T(8,128)(2,1)S(1)}, u32[]{:S(2)}, u32[]{:S(2)}) collective-permute-start(bf16[2,64,1536]{2,1,0:T(8,128)(2,1)S(1)} %get-tuple-element.20), channel_id=1, source_target_pairs={{0,1},{1,0},{2,3},{3,2},{4,5},{5,4},{6,7},{7,6},{8,9},{9,8},{10,11... | collective-permute-start | bytes 1179656 | tf_op jit(solution)/shard_map/ppermute | solution.py:170
  35.8 2.2 %collective-permute-start.7 = (bf16[2,64,1792]{2,1,0:T(8,128)(2,1)S(1)}, bf16[2,64,1792]{2,1,0:T(8,128)(2,1)S(1)}, u32[]{:S(2)}, u32[]{:S(2)}) collective-permute-start(bf16[2,64,1792]{2,1,0:T(8,128)(2,1)S(1)} %get-tuple-element.18), channel_id=1, source_target_pairs={{0,1},{1,0},{2,3},{3,2},{4,5},{5,4},{6,7},{7,6},{8,9},{9,8},{10,11... | collective-permute-start | bytes 1376264 | tf_op jit(solution)/shard_map/ppermute | solution.py:170
  36.4 7.8 %collective-permute-start.13 = (bf16[2,32,1536]{2,1,0:T(8,128)(2,1)S(1)}, bf16[2,32,1536]{2,1,0:T(8,128)(2,1)S(1)}, u32[]{:S(2)}, u32[]{:S(2)}) collective-permute-start(bf16[2,32,1536]{2,1,0:T(8,128)(2,1)S(1)} %add_convert_fusion.1), channel_id=1, source_target_pairs={{0,2},{1,3},{2,0},{3,1},{4,6},{5,7},{6,4},{7,5},{8,10},{9,11},{10,... | collective-permute-start | bytes 589832 | tf_op jit(solution)/shard_map/ppermute | solution.py:173
  38.0 11.1 %collective-permute-start.8 = (bf16[2,32,1792]{2,1,0:T(8,128)(2,1)S(1)}, bf16[2,32,1792]{2,1,0:T(8,128)(2,1)S(1)}, u32[]{:S(2)}, u32[]{:S(2)}) collective-permute-start(bf16[2,32,1792]{2,1,0:T(8,128)(2,1)S(1)} %add_convert_fusion), channel_id=1, source_target_pairs={{0,2},{1,3},{2,0},{3,1},{4,6},{5,7},{6,4},{7,5},{8,10},{9,11},{10,... | collective-permute-start | bytes 688136 | tf_op jit(solution)/shard_map/ppermute | solution.py:173
  44.4 6.5 %collective-permute-start.14 = (bf16[32,1536]{1,0:T(8,128)(2,1)S(1)}, bf16[32,1536]{1,0:T(8,128)(2,1)S(1)}, u32[]{:S(2)}, u32[]{:S(2)}) collective-permute-start(bf16[32,1536]{1,0:T(8,128)(2,1)S(1)} %fusion.3.refs_0_), channel_id=1, source_target_pairs={{0,2},{1,3},{2,0},{3,1},{4,6},{5,7},{6,4},{7,5},{8,10},{9,11},{10,... | collective-permute-start | bytes 294920 | tf_op jit(solution)/shard_map/ppermute | solution.py:176
  49.3 4.9 %collective-permute-start.9 = (bf16[32,1792]{1,0:T(8,128)(2,1)S(1)}, bf16[32,1792]{1,0:T(8,128)(2,1)S(1)}, u32[]{:S(2)}, u32[]{:S(2)}) collective-permute-start(bf16[32,1792]{1,0:T(8,128)(2,1)S(1)} %fusion.1.refs_0_), channel_id=1, source_target_pairs={{0,2},{1,3},{2,0},{3,1},{4,6},{5,7},{6,4},{7,5},{8,10},{9,11},{10,... | collective-permute-start | bytes 344072 | tf_op jit(solution)/shard_map/ppermute | solution.py:176
  50.8 3.3 %collective-permute-start.15 = (bf16[32,1536]{1,0:T(8,128)(2,1)S(1)}, bf16[32,1536]{1,0:T(8,128)(2,1)S(1)}, u32[]{:S(2)}, u32[]{:S(2)}) collective-permute-start(bf16[32,1536]{1,0:T(8,128)(2,1)S(1)} %fusion.3.refs_0_), channel_id=1, source_target_pairs={{0,1},{1,0},{2,3},{3,2},{4,5},{5,4},{6,7},{7,6},{8,9},{9,8},{10,11... | collective-permute-start | bytes 294920 | tf_op jit(solution)/shard_map/ppermute | solution.py:177
  50.9 3.3 %collective-permute-start.16 = (bf16[32,1536]{1,0:T(8,128)(2,1)S(1)}, bf16[32,1536]{1,0:T(8,128)(2,1)S(1)}, u32[]{:S(2)}, u32[]{:S(2)}) collective-permute-start(bf16[32,1536]{1,0:T(8,128)(2,1)S(1)} %collective-permute-done.14.refs_1_), channel_id=1, source_target_pairs={{0,1},{1,0},{2,3},{3,2},{4,5},{5,4},{6,7},{7,6},{8,9},{9,8},{10,11... | collective-permute-start | bytes 294920 | tf_op jit(solution)/shard_map/ppermute | solution.py:178
  51.4 10.7 %collective-permute-start.10 = (bf16[32,1792]{1,0:T(8,128)(2,1)S(1)}, bf16[32,1792]{1,0:T(8,128)(2,1)S(1)}, u32[]{:S(2)}, u32[]{:S(2)}) collective-permute-start(bf16[32,1792]{1,0:T(8,128)(2,1)S(1)} %fusion.1.refs_0_), channel_id=1, source_target_pairs={{0,1},{1,0},{2,3},{3,2},{4,5},{5,4},{6,7},{7,6},{8,9},{9,8},{10,11... | collective-permute-start | bytes 344072 | tf_op jit(solution)/shard_map/ppermute | solution.py:177
  54.1 7.9 %collective-permute-start.11 = (bf16[32,1792]{1,0:T(8,128)(2,1)S(1)}, bf16[32,1792]{1,0:T(8,128)(2,1)S(1)}, u32[]{:S(2)}, u32[]{:S(2)}) collective-permute-start(bf16[32,1792]{1,0:T(8,128)(2,1)S(1)} %collective-permute-done.9.refs_1_), channel_id=1, source_target_pairs={{0,1},{1,0},{2,3},{3,2},{4,5},{5,4},{6,7},{7,6},{8,9},{9,8},{10,11... | collective-permute-start | bytes 344072 | tf_op jit(solution)/shard_map/ppermute | solution.py:178
  71.1 7.5 %collective-permute-start.17 = (bf16[16,2048]{1,0:T(8,128)(2,1)S(1)}, bf16[16,2048]{1,0:T(8,128)(2,1)S(1)}, u32[]{:S(2)}, u32[]{:S(2)}) collective-permute-start(bf16[16,2048]{1,0:T(8,128)(2,1)S(1)} %get-tuple-element.22), channel_id=1, source_target_pairs={{0,4},{4,8},{8,12},{12,0},{16,20},{20,24},{24,28},{28,16},{1,5},{5... | collective-permute-start | bytes 196616 | tf_op jit(solution)/shard_map/ppermute | solution.py:185
  72.6 7.8 %collective-permute-start.18 = (bf16[16,2048]{1,0:T(8,128)(2,1)S(1)}, bf16[16,2048]{1,0:T(8,128)(2,1)S(1)}, u32[]{:S(2)}, u32[]{:S(2)}) collective-permute-start(bf16[16,2048]{1,0:T(8,128)(2,1)S(1)} %get-tuple-element.23), channel_id=1, source_target_pairs={{0,8},{4,12},{8,0},{12,4},{16,24},{20,28},{24,16},{28,20},{1,9},{5... | collective-permute-start | bytes 196616 | tf_op jit(solution)/shard_map/ppermute | solution.py:185
  75.1 9.9 %collective-permute-start.19 = (bf16[16,2048]{1,0:T(8,128)(2,1)S(1)}, bf16[16,2048]{1,0:T(8,128)(2,1)S(1)}, u32[]{:S(2)}, u32[]{:S(2)}) collective-permute-start(bf16[16,2048]{1,0:T(8,128)(2,1)S(1)} %get-tuple-element.24), channel_id=1, source_target_pairs={{0,12},{4,0},{8,4},{12,8},{16,28},{20,16},{24,20},{28,24},{1,13},{... | collective-permute-start | bytes 196616 | tf_op jit(solution)/shard_map/ppermute | solution.py:185
  75.1 9.9 %collective-permute-start.20 = (bf16[16,2048]{1,0:T(8,128)(2,1)S(1)}, bf16[16,2048]{1,0:T(8,128)(2,1)S(1)}, u32[]{:S(2)}, u32[]{:S(2)}) collective-permute-start(bf16[16,2048]{1,0:T(8,128)(2,1)S(1)} %get-tuple-element.25), channel_id=1, source_target_pairs={{0,16},{4,20},{8,24},{12,28},{16,0},{20,4},{24,8},{28,12},{1,17},{... | collective-permute-start | bytes 196616 | tf_op jit(solution)/shard_map/ppermute | solution.py:185
  76.6 8.5 %collective-permute-start.21 = (bf16[16,2048]{1,0:T(8,128)(2,1)S(1)}, bf16[16,2048]{1,0:T(8,128)(2,1)S(1)}, u32[]{:S(2)}, u32[]{:S(2)}) collective-permute-start(bf16[16,2048]{1,0:T(8,128)(2,1)S(1)} %get-tuple-element.26), channel_id=1, source_target_pairs={{0,20},{4,24},{8,28},{12,16},{16,4},{20,8},{24,12},{28,0},{1,21},{... | collective-permute-start | bytes 196616 | tf_op jit(solution)/shard_map/ppermute | solution.py:185
  78.6 8.4 %collective-permute-start.22 = (bf16[16,2048]{1,0:T(8,128)(2,1)S(1)}, bf16[16,2048]{1,0:T(8,128)(2,1)S(1)}, u32[]{:S(2)}, u32[]{:S(2)}) collective-permute-start(bf16[16,2048]{1,0:T(8,128)(2,1)S(1)} %get-tuple-element.27), channel_id=1, source_target_pairs={{0,24},{4,28},{8,16},{12,20},{16,8},{20,12},{24,0},{28,4},{1,25},{... | collective-permute-start | bytes 196616 | tf_op jit(solution)/shard_map/ppermute | solution.py:185
  80.4 6.6 %collective-permute-start.23 = (bf16[16,2048]{1,0:T(8,128)(2,1)S(1)}, bf16[16,2048]{1,0:T(8,128)(2,1)S(1)}, u32[]{:S(2)}, u32[]{:S(2)}) collective-permute-start(bf16[16,2048]{1,0:T(8,128)(2,1)S(1)} %get-tuple-element.28), channel_id=1, source_target_pairs={{0,28},{4,16},{8,20},{12,24},{16,12},{20,0},{24,4},{28,8},{1,29},{... | collective-permute-start | bytes 196616 | tf_op jit(solution)/shard_map/ppermute | solution.py:185

commit v2 on v0

--- a/solution.py
+++ b/solution.py
@@ -1,10 +1,17 @@
+import functools
+
 import jax
 import jax.numpy as jnp
 from jax import lax
+from jax.experimental import pallas as pl
+from jax.experimental.pallas import tpu as pltpu
 from jax.sharding import PartitionSpec as P
 
-
-def on_device(tokens, gate_weight, up_weight, down_weight):
+TILE = 256
+CHUNKS = 2
+
+
+def plain(tokens, gate_weight, up_weight, down_weight):
     piece = lax.all_gather(tokens, "hid", axis=0, tiled=True)
     gate_rows = jnp.dot(piece, gate_weight, preferred_element_type=jnp.float32)
     up_rows = jnp.dot(piece, up_weight, preferred_element_type=jnp.float32)
@@ -19,7 +26,196 @@
     )
 
 
+SEND_ORDER = (7, 6, 5, 4, 3, 2, 1, 0)
+ROWS = 16
+
+
+def pieces_of(width, most):
+    first = width % most
+    edges = ([0] if first else []) + list(range(first, width + 1, most))
+    return list(zip(edges[:-1], edges[1:]))
+
+
+def place(wid, b):
+    step = wid ^ (b % 4)
+    return (step % 2) * 4 + (step // 2) * 2 + b // 4
+
+
+def gate_up_kernel(n_blocks, rows, first, width, where, *refs):
+    blocks, refs = refs[:n_blocks], refs[n_blocks:]
+    gate_ref, up_ref, mine_ref, theirs_ref, x_ref, w_ref, sems = refs
+    start = pl.multiple_of(where[0] + first, TILE)
+    cuts = pieces_of(width, 2 * TILE)
+
+    def copy(i, k):
+        a, b = cuts[i]
+        source = (gate_ref, up_ref)[k].at[:, pl.ds(start + a, b - a)]
+        return pltpu.make_async_copy(source, w_ref.at[k, :, a:b], sems.at[k, i])
+
+    for i in range(len(cuts)):
+        for k in range(2):
+            copy(i, k).start()
+    for b in range(n_blocks):
+        at = pl.multiple_of(place(where[1], b) * rows, rows)
+        x_ref[pl.ds(at, rows), :] = blocks[b][...]
+    half = x_ref.shape[0] // 2
+    for i, (a, b) in enumerate(cuts):
+        for k in range(2):
+            copy(i, k).wait()
+            part = jnp.dot(x_ref[...], w_ref[k, :, a:b], preferred_element_type=jnp.float32).astype(jnp.bfloat16)
+            mine_ref[k, :, a:b] = part[:half]
+            theirs_ref[k, :, a:b] = part[half:]
+
+
+def gate_up(where, blocks, gate_weight, up_weight, first, width):
+    depth = gate_weight.shape[0]
+    rows = blocks[0].shape[0]
+    n = len(blocks)
+    total = n * rows
+    n_cuts = len(pieces_of(width, 2 * TILE))
+    vmem, hbm = pl.BlockSpec(memory_space=pltpu.VMEM), pl.BlockSpec(memory_space=pltpu.HBM)
+    return pl.pallas_call(
+        functools.partial(gate_up_kernel, n, rows, first, width),
+        in_specs=[pl.BlockSpec(memory_space=pltpu.SMEM)] + [vmem] * n + [hbm] * 2,
+        out_specs=[vmem] * 2,
+        scratch_shapes=[
+            pltpu.VMEM((total, depth), jnp.bfloat16),
+            pltpu.VMEM((2, depth, width), jnp.bfloat16),
+            pltpu.SemaphoreType.DMA((2, n_cuts)),
+        ],
+        out_shape=[jax.ShapeDtypeStruct((2, total // 2, width), jnp.bfloat16)] * 2,
+        compiler_params=pltpu.CompilerParams(vmem_limit_bytes=28 * 2**20),
+        cost_estimate=pl.CostEstimate(
+            flops=4 * total * depth * width, bytes_accessed=4 * depth * width, transcendentals=0
+        ),
+        name="gate_up",
+    )(where, *blocks, gate_weight, up_weight)
+
+
+def down_kernel(n_pieces, has_acc, last, first, depth, where, *refs):
+    pieces, refs = refs[:n_pieces], refs[n_pieces:]
+    down_ref, refs = refs[0], refs[1:]
+    prev_ref, refs = (refs[0], refs[1:]) if has_acc else (None, refs)
+    outs, (acc_ref, lhs_ref, w_ref, sems) = refs[:-4], refs[-4:]
+    start = pl.multiple_of(where[0] + first, TILE)
+    cuts = pieces_of(depth, 2 * TILE)
+
+    def copy(i):
+        a, b = cuts[i]
+        return pltpu.make_async_copy(down_ref.at[pl.ds(start + a, b - a), :], w_ref.at[a:b, :], sems.at[i])
+
+    for i in range(len(cuts)):
+        copy(i).start()
+    at = 0
+    for piece in pieces:
+        lhs_ref[at : at + piece.shape[0], :] = piece[...]
+        at += piece.shape[0]
+    for i, (a, b) in enumerate(cuts):
+        copy(i).wait()
+        part = jnp.dot(lhs_ref[:, a:b], w_ref[a:b, :], preferred_element_type=jnp.float32)
+        if i > 0:
+            part = part + acc_ref[...]
+        elif has_acc:
+            part = part + prev_ref[...]
+        acc_ref[...] = part
+    if last:
+        order = iter(SEND_ORDER)
+        for out in outs:
+            for at in range(0, out.shape[0], ROWS):
+                source = pl.multiple_of(place(where[1], next(order)) * ROWS, ROWS)
+                out[at : at + ROWS, :] = acc_ref[pl.ds(source, ROWS), :].astype(out.dtype)
+
+
+def down(where, pieces, down_weight, prev, first, depth, out_rows):
+    width = down_weight.shape[1]
+    total = sum(p.shape[0] for p in pieces)
+    last = bool(out_rows)
+    vmem, hbm = pl.BlockSpec(memory_space=pltpu.VMEM), pl.BlockSpec(memory_space=pltpu.HBM)
+    args = [*pieces, down_weight] + ([] if prev is None else [prev])
+    sums = jax.ShapeDtypeStruct((total, width), jnp.float32)
+    scratch = [
+        pltpu.VMEM((total, depth), jnp.bfloat16),
+        pltpu.VMEM((depth, width), jnp.bfloat16),
+        pltpu.SemaphoreType.DMA((len(pieces_of(depth, 2 * TILE)),)),
+    ]
+    if last:
+        scratch = [pltpu.VMEM(sums.shape, sums.dtype)] + scratch
+    return pl.pallas_call(
+        functools.partial(down_kernel, len(pieces), prev is not None, last, first, depth),
+        in_specs=[pl.BlockSpec(memory_space=pltpu.SMEM)]
+        + [vmem] * len(pieces)
+        + [hbm]
+        + ([] if prev is None else [vmem]),
+        out_specs=[vmem] * len(out_rows) if last else vmem,
+        scratch_shapes=scratch,
+        out_shape=[jax.ShapeDtypeStruct((r, width), jnp.bfloat16) for r in out_rows] if last else sums,
+        compiler_params=pltpu.CompilerParams(vmem_limit_bytes=20 * 2**20),
+        cost_estimate=pl.CostEstimate(
+            flops=2 * total * width * depth, bytes_accessed=2 * width * depth, transcendentals=0
+        ),
+        name="down",
+    )(where, *args)
+
+
+def split_by_rep(n_wid, tokens, gate_weight, up_weight, down_weight):
+    rep, wid = lax.axis_index("rep"), lax.axis_index("wid")
+    f32, bf16 = jnp.float32, jnp.bfloat16
+    rows = tokens.shape[0]
+    width = gate_weight.shape[1] // 2
+
+    def swap(x, axis, step):
+        n = {"rep": 2, "hid": 4, "wid": n_wid}[axis]
+        return lax.ppermute(x, axis, [(i, i ^ step) for i in range(n)])
+
+    near = [tokens, swap(tokens, "hid", 1), swap(tokens, "hid", 2)]
+    near.append(swap(near[2], "hid", 1))
+    blocks = near + [swap(x, "rep", 1) for x in near]
+
+    where = jnp.stack([rep * width, wid]).astype(jnp.int32)
+    gate_weight, up_weight, down_weight = (
+        pltpu.with_memory_space_constraint(w, pltpu.HBM) for w in (gate_weight, up_weight, down_weight)
+    )
+
+    tiles = width // TILE
+    bounds = [tiles * c // CHUNKS * TILE for c in range(CHUNKS + 1)]
+    acc = None
+    for c in range(CHUNKS):
+        first, count = bounds[c], bounds[c + 1] - bounds[c]
+        mine, theirs = gate_up(where, blocks, gate_weight, up_weight, first, count)
+        got = swap(theirs, "wid", 1)
+        quarter = 2 * rows
+        to_chip = (mine[:, quarter:].astype(f32) + got[:, quarter:].astype(f32)).astype(bf16)
+        from_chip = swap(to_chip, "wid", 2)
+        summed = mine[:, :quarter].astype(f32) + got[:, :quarter].astype(f32) + from_chip.astype(f32)
+        own = (jax.nn.silu(summed[0]) * summed[1]).astype(bf16)
+        other = swap(own, "wid", 2)
+        pieces = [own, other, swap(own, "wid", 1), swap(other, "wid", 1)]
+        out_rows = [2 * rows, 2 * rows, 4 * rows] if c == CHUNKS - 1 else []
+        acc = down(where, pieces, down_weight, acc, first, count, out_rows)
+
+    far_32, far_10, kept = acc
+    kept = kept.astype(f32)
+    sums_32 = kept[: 2 * rows] + swap(far_32, "rep", 1).astype(f32)
+    sums_10 = kept[2 * rows :] + swap(far_10, "rep", 1).astype(f32)
+    via = sums_32[rows:] + swap(sums_32[:rows].astype(bf16), "hid", 1).astype(f32)
+    mixed = sums_10[rows:] + swap(sums_10[:rows].astype(bf16), "hid", 1).astype(f32)
+    mixed = mixed + swap(via.astype(bf16), "hid", 2).astype(f32)
+    return mixed.astype(bf16)
+
+
 def solution(mesh):
+    n_rep, n_hid, n_wid = (mesh.shape[a] for a in ("rep", "hid", "wid"))
+
+    def on_device(tokens, gate_weight, up_weight, down_weight):
+        fits = (
+            (n_rep, n_hid, n_wid) == (2, 4, 4)
+            and gate_weight.shape[1] % (n_rep * TILE) == 0
+            and tokens.shape[0] == ROWS
+        )
+        if not fits:
+            return plain(tokens, gate_weight, up_weight, down_weight)
+        return split_by_rep(n_wid, tokens, gate_weight, up_weight, down_weight)
+
     return jax.shard_map(
         on_device,
         mesh=mesh,

time: 134 us -> 77.2 us (0.58)
  waiting for transfers between devices: 66.5 us -> 27.5 us
  matrix products: 34.7 us -> 0 us
  starting transfers between devices: 0.04 us -> 26.9 us
  Pallas kernels: 0 us -> 20.5 us
  blocking collectives: 15.8 us -> 0 us
  between operations: 13.4 us -> 0.14 us
  other arithmetic: 3.12 us -> 1.21 us
    psum x1 -> x0, waiting for transfers between devices: 46.6 us -> none  [on_device(): lax.psum(partial_terms.astype(jnp.bfloat16), 'wid').astype(jnp.float32)]
    dot_general x3 -> x0, matrix products: 34.7 us -> none  [the longest x1 12 us: on_device(): jnp.dot(hidden, down_weight, preferred_element_type=jnp.float32)]
    ppermute x0 -> x22, waiting for transfers between devices: none -> 27.5 us  [swap(): return lax.ppermute(x, axis, [(i, i ^ step) for i in range(n)])]
    ppermute x0 -> x22, starting transfers between devices: none -> 26.9 us  [swap(): return lax.ppermute(x, axis, [(i, i ^ step) for i in range(n)])]
    pallas_call x0 -> x4, Pallas kernels: none -> 20.5 us  [the longest x2 12.3 us: gate_up(): pl.pallas_call(functools.partial(gate_up_kernel, n, rows, first, width),...]
    reduce_scatter x1 -> x0, waiting for transfers between devices: 19.9 us -> none  [on_device(): lax.psum_scatter(jnp.dot(hidden, down_weight, preferred_element_type=jnp....]
    all_gather x1 -> x0, blocking collectives: 15.8 us -> none  [on_device(): piece = lax.all_gather(tokens, 'hid', axis=0, tiled=True)]
  transfers between devices with their start and end apart: 2 -> 22, of which waited for: 2 -> 12; matrix products, arithmetic and copies ran while one was open for 0% -> 1% of each run, Pallas kernels for 0% -> 13%
where the time goes in v2:
time: 77.2 us; the launch traced here: 77 us
  waiting for transfers between devices  27.5 us (36%)
  starting transfers between devices  26.9 us (35%)
  Pallas kernels  20.5 us (27%)
  other arithmetic  1.21 us (2%)
  local copies, waits for them, and re-layouts  0.86 us (1%)
    ppermute x22, waiting for transfers between devices, swap(): return lax.ppermute(x, axis, [(i, i ^ step) for i in range(n)])  27.5 us
    ppermute x22, starting transfers between devices, swap(): return lax.ppermute(x, axis, [(i, i ^ step) for i in range(n)])  26.9 us
    pallas_call x2, Pallas kernels, gate_up(): pl.pallas_call(functools.partial(gate_up_kernel, n, rows, first, width),...  12.3 us
    pallas_call x2, Pallas kernels, down(): pl.pallas_call(functools.partial(down_kernel, len(pieces), prev is not No...  8.15 us
  transfers between devices with their start and end apart: 22, of which 12 were waited for; matrix products, arithmetic and copies ran while one was open for 1% of the time, Pallas kernels for 13%

profile of v2, /device:TPU:0, one launch (start us, length us, event | category | flops | bytes accessed | tf_op | source)
XLA Modules:
  0.0 77.0 jit_solution(948156207828428740)
XLA Ops:
  0.0 4.0 %collective-permute-start.1 = (bf16[16,2048]{1,0:T(8,128)(2,1)}, bf16[16,2048]{1,0:T(8,128)(2,1)S(1)}, u32[]{:S(2)}, u32[]{:S(2)}) collective-permute-start(bf16[16,2048]{1,0:T(8,128)(2,1)} %refs_0_.3), channel_id=1, source_target_pairs={{0,8},{4,12},{8,0},{12,4},{1,9},{5,13},{9,1},{13,5},{2,10},{6,14},... | collective-permute-start | bytes 196616 | tf_op jit(solution)/shard_map/ppermute | solution.py:168
  4.0 1.6 %collective-permute-start = (bf16[16,2048]{1,0:T(8,128)(2,1)}, bf16[16,2048]{1,0:T(8,128)(2,1)S(1)}, u32[]{:S(2)}, u32[]{:S(2)}) collective-permute-start(bf16[16,2048]{1,0:T(8,128)(2,1)} %refs_0_.3), channel_id=1, source_target_pairs={{0,4},{4,0},{8,12},{12,8},{1,5},{5,1},{9,13},{13,9},{2,6},{6,2},{1... | collective-permute-start | bytes 196616 | tf_op jit(solution)/shard_map/ppermute | solution.py:168
  5.6 1.7 %collective-permute-done.1.refs_2_ = bf16[16,2048]{1,0:T(8,128)(2,1)S(1)} collective-permute-done((bf16[16,2048]{1,0:T(8,128)(2,1)}, bf16[16,2048]{1,0:T(8,128)(2,1)S(1)}, u32[]{:S(2)}, u32[]{:S(2)}) %collective-permute-start.1) | collective-permute-done | bytes 65568 | tf_op jit(solution)/shard_map/ppermute | solution.py:168
  7.3 1.4 %collective-permute-start.2 = (bf16[16,2048]{1,0:T(8,128)(2,1)S(1)}, bf16[16,2048]{1,0:T(8,128)(2,1)S(1)}, u32[]{:S(2)}, u32[]{:S(2)}) collective-permute-start(bf16[16,2048]{1,0:T(8,128)(2,1)S(1)} %collective-permute-done.1.refs_2_), channel_id=1, source_target_pairs={{0,4},{4,0},{8,12},{12,8},{1,5},{5,1},{9,13},{13,9},{2,6},{6,2},{1... | collective-permute-start | bytes 196616 | tf_op jit(solution)/shard_map/ppermute | solution.py:168
  8.7 1.5 %collective-permute-start.3 = (bf16[16,2048]{1,0:T(8,128)(2,1)}, bf16[16,2048]{1,0:T(8,128)(2,1)S(1)}, u32[]{:S(2)}, u32[]{:S(2)}) collective-permute-start(bf16[16,2048]{1,0:T(8,128)(2,1)} %refs_0_.3), channel_id=1, source_target_pairs={{0,16},{16,0},{1,17},{17,1},{2,18},{18,2},{3,19},{19,3},{4,20},{20... | collective-permute-start | bytes 196616 | tf_op jit(solution)/shard_map/ppermute | solution.py:168
  10.2 0.5 collective-permute-start.5
  10.7 0.0 collective-permute-done.refs_1_
  10.7 1.5 %collective-permute-start.4 = (bf16[16,2048]{1,0:T(8,128)(2,1)S(1)}, bf16[16,2048]{1,0:T(8,128)(2,1)S(1)}, u32[]{:S(2)}, u32[]{:S(2)}) collective-permute-start(bf16[16,2048]{1,0:T(8,128)(2,1)S(1)} %collective-permute-done.refs_1_), channel_id=1, source_target_pairs={{0,16},{16,0},{1,17},{17,1},{2,18},{18,2},{3,19},{19,3},{4,20},{20... | collective-permute-start | bytes 196616 | tf_op jit(solution)/shard_map/ppermute | solution.py:168
  12.2 0.0 collective-permute-done.2.refs_3_
  12.2 1.2 %collective-permute-start.6 = (bf16[16,2048]{1,0:T(8,128)(2,1)S(1)}, bf16[16,2048]{1,0:T(8,128)(2,1)S(1)}, u32[]{:S(2)}, u32[]{:S(2)}) collective-permute-start(bf16[16,2048]{1,0:T(8,128)(2,1)S(1)} %collective-permute-done.2.refs_3_), channel_id=1, source_target_pairs={{0,16},{16,0},{1,17},{17,1},{2,18},{18,2},{3,19},{19,3},{4,20},{20... | collective-permute-start | bytes 196616 | tf_op jit(solution)/shard_map/ppermute | solution.py:168
  13.4 0.1 pad_add_fusion.where
  13.5 0.3 collective-permute-done.3.refs_4_
  13.9 0.9 %collective-permute-done.5.refs_6_ = bf16[16,2048]{1,0:T(8,128)(2,1)S(1)} collective-permute-done((bf16[16,2048]{1,0:T(8,128)(2,1)S(1)}, bf16[16,2048]{1,0:T(8,128)(2,1)S(1)}, u32[]{:S(2)}, u32[]{:S(2)}) %collective-permute-start.5) | collective-permute-done | bytes 65568 | tf_op jit(solution)/shard_map/ppermute | solution.py:168
  14.8 0.7 collective-permute-done.4.refs_5_
  15.5 1.0 %collective-permute-done.6.refs_7_ = bf16[16,2048]{1,0:T(8,128)(2,1)S(1)} collective-permute-done((bf16[16,2048]{1,0:T(8,128)(2,1)S(1)}, bf16[16,2048]{1,0:T(8,128)(2,1)S(1)}, u32[]{:S(2)}, u32[]{:S(2)}) %collective-permute-start.6) | collective-permute-done | bytes 65568 | tf_op jit(solution)/shard_map/ppermute | solution.py:168
  16.5 0.8 %copy-done = bf16[16,2048]{1,0:T(8,128)(2,1)S(1)} copy-done((bf16[16,2048]{1,0:T(8,128)(2,1)S(1)}, bf16[16,2048]{1,0:T(8,128)(2,1)}, u32[]{:S(2)}) %copy-start) | copy-done | bytes 65560
  17.3 5.8 %gate_up.3 = (bf16[2,64,1536]{2,1,0:T(8,128)(2,1)S(1)}, bf16[2,64,1536]{2,1,0:T(8,128)(2,1)S(1)}) custom-call(s32[2]{0:T(128)S(1)} %pad_add_fusion.where, bf16[16,2048]{1,0:T(8,128)(2,1)S(1)} %copy-done, bf16[16,2048]{1,0:T(8,128)(2,1)S(1)} %collective-permute-done.refs_1_, bf16[16,2048]{1,0:T(8,128)(2,1)S(1)} %collective-permute-done.1.refs_2_, ...), custom_call_target="tpu_custom_call" | custom-call | flops 1610612736 | bytes 12582912 | tf_op jit(solution)/shard_map/gate_up/pallas_call | solution.py:77
  23.2 0.1 collective-permute-start.12
  23.3 6.5 %gate_up.2 = (bf16[2,64,1792]{2,1,0:T(8,128)(2,1)S(1)}, bf16[2,64,1792]{2,1,0:T(8,128)(2,1)S(1)}) custom-call(s32[2]{0:T(128)S(1)} %pad_add_fusion.where, bf16[16,2048]{1,0:T(8,128)(2,1)S(1)} %copy-done, bf16[16,2048]{1,0:T(8,128)(2,1)S(1)} %collective-permute-done.refs_1_, bf16[16,2048]{1,0:T(8,128)(2,1)S(1)} %collective-permute-done.1.refs_2_, ...), custom_call_target="tpu_custom_call" | custom-call | flops 1879048192 | bytes 14680064 | tf_op jit(solution)/shard_map/gate_up/pallas_call | solution.py:77
  29.7 0.6 collective-permute-start.7
  30.3 0.0 collective-permute-done.12
  30.3 1.6 %collective-permute-start.13 = (bf16[2,32,1536]{2,1,0:T(8,128)(2,1)S(1)}, bf16[2,32,1536]{2,1,0:T(8,128)(2,1)S(1)}, u32[]{:S(2)}, u32[]{:S(2)}) collective-permute-start(bf16[2,32,1536]{2,1,0:T(8,128)(2,1)S(1)} %add_convert_fusion.1), channel_id=1, source_target_pairs={{0,2},{1,3},{2,0},{3,1},{4,6},{5,7},{6,4},{7,5},{8,10},{9,11},{10,... | collective-permute-start | bytes 589832 | tf_op jit(solution)/shard_map/ppermute | solution.py:168
  31.9 0.0 collective-permute-done.7
  31.9 0.1 add_convert_fusion
  32.0 1.4 %collective-permute-start.8 = (bf16[2,32,1792]{2,1,0:T(8,128)(2,1)S(1)}, bf16[2,32,1792]{2,1,0:T(8,128)(2,1)S(1)}, u32[]{:S(2)}, u32[]{:S(2)}) collective-permute-start(bf16[2,32,1792]{2,1,0:T(8,128)(2,1)S(1)} %add_convert_fusion), channel_id=1, source_target_pairs={{0,2},{1,3},{2,0},{3,1},{4,6},{5,7},{6,4},{7,5},{8,10},{9,11},{10,... | collective-permute-start | bytes 688136 | tf_op jit(solution)/shard_map/ppermute | solution.py:168
  33.4 4.8 %collective-permute-done.13 = bf16[2,32,1536]{2,1,0:T(8,128)(2,1)S(1)} collective-permute-done((bf16[2,32,1536]{2,1,0:T(8,128)(2,1)S(1)}, bf16[2,32,1536]{2,1,0:T(8,128)(2,1)S(1)}, u32[]{:S(2)}, u32[]{:S(2)}) %collective-permute-start.13) | collective-permute-done | bytes 196640 | tf_op jit(solution)/shard_map/ppermute | solution.py:168
  38.2 0.1 convert_add_fusion.1
  38.2 0.1 fusion.3.refs_0_
  38.3 1.6 %collective-permute-start.14 = (bf16[32,1536]{1,0:T(8,128)(2,1)S(1)}, bf16[32,1536]{1,0:T(8,128)(2,1)S(1)}, u32[]{:S(2)}, u32[]{:S(2)}) collective-permute-start(bf16[32,1536]{1,0:T(8,128)(2,1)S(1)} %fusion.3.refs_0_), channel_id=1, source_target_pairs={{0,2},{1,3},{2,0},{3,1},{4,6},{5,7},{6,4},{7,5},{8,10},{9,11},{10,... | collective-permute-start | bytes 294920 | tf_op jit(solution)/shard_map/ppermute | solution.py:168
  39.9 3.2 %collective-permute-done.8 = bf16[2,32,1792]{2,1,0:T(8,128)(2,1)S(1)} collective-permute-done((bf16[2,32,1792]{2,1,0:T(8,128)(2,1)S(1)}, bf16[2,32,1792]{2,1,0:T(8,128)(2,1)S(1)}, u32[]{:S(2)}, u32[]{:S(2)}) %collective-permute-start.8) | collective-permute-done | bytes 229408 | tf_op jit(solution)/shard_map/ppermute | solution.py:168
  43.1 0.1 convert_add_fusion
  43.2 0.1 fusion.1.refs_0_
  43.2 1.6 %collective-permute-start.9 = (bf16[32,1792]{1,0:T(8,128)(2,1)S(1)}, bf16[32,1792]{1,0:T(8,128)(2,1)S(1)}, u32[]{:S(2)}, u32[]{:S(2)}) collective-permute-start(bf16[32,1792]{1,0:T(8,128)(2,1)S(1)} %fusion.1.refs_0_), channel_id=1, source_target_pairs={{0,2},{1,3},{2,0},{3,1},{4,6},{5,7},{6,4},{7,5},{8,10},{9,11},{10,... | collective-permute-start | bytes 344072 | tf_op jit(solution)/shard_map/ppermute | solution.py:168
  44.8 0.5 collective-permute-start.16
  45.3 0.0 collective-permute-start.10
  45.3 2.8 %collective-permute-done.9.refs_1_ = bf16[32,1792]{1,0:T(8,128)(2,1)S(1)} collective-permute-done((bf16[32,1792]{1,0:T(8,128)(2,1)S(1)}, bf16[32,1792]{1,0:T(8,128)(2,1)S(1)}, u32[]{:S(2)}, u32[]{:S(2)}) %collective-permute-start.9) | collective-permute-done | bytes 114720 | tf_op jit(solution)/shard_map/ppermute | solution.py:168
  48.1 3.9 %down.2.refs_5_ = f32[128,2048]{1,0:T(8,128)S(1)} custom-call(s32[2]{0:T(128)S(1)} %pad_add_fusion.where, bf16[32,1536]{1,0:T(8,128)(2,1)S(1)} %fusion.3.refs_0_, bf16[32,1536]{1,0:T(8,128)(2,1)S(1)} %collective-permute-done.14.refs_1_, bf16[32,1536]{1,0:T(8,128)(2,1)S(1)} %collective-permute-done.15.refs_2_, ...), custom_call_target="tpu_custom_call" | custom-call | flops 805306368 | bytes 6291456 | tf_op jit(solution)/shard_map/down/pallas_call | solution.py:143
  52.0 4.3 %down.3 = (bf16[32,2048]{1,0:T(8,128)(2,1)S(1)}, bf16[32,2048]{1,0:T(8,128)(2,1)S(1)}, bf16[64,2048]{1,0:T(8,128)(2,1)S(1)}) custom-call(s32[2]{0:T(128)S(1)} %pad_add_fusion.where, bf16[32,1792]{1,0:T(8,128)(2,1)S(1)} %fusion.1.refs_0_, bf16[32,1792]{1,0:T(8,128)(2,1)S(1)} %collective-permute-done.9.refs_1_, ...), custom_call_target="tpu_custom_call" | custom-call | flops 939524096 | bytes 7340032 | tf_op jit(solution)/shard_map/down/pallas_call | solution.py:143
  56.3 1.3 %collective-permute-start.17 = (bf16[32,2048]{1,0:T(8,128)(2,1)S(1)}, bf16[32,2048]{1,0:T(8,128)(2,1)S(1)}, u32[]{:S(2)}, u32[]{:S(2)}) collective-permute-start(bf16[32,2048]{1,0:T(8,128)(2,1)S(1)} %get-tuple-element.17), channel_id=1, source_target_pairs={{0,16},{16,0},{1,17},{17,1},{2,18},{18,2},{3,19},{19,3},{4,20},{20... | collective-permute-start | bytes 393224 | tf_op jit(solution)/shard_map/ppermute | solution.py:168
  57.6 0.8 %collective-permute-start.19 = (bf16[32,2048]{1,0:T(8,128)(2,1)S(1)}, bf16[32,2048]{1,0:T(8,128)(2,1)S(1)}, u32[]{:S(2)}, u32[]{:S(2)}) collective-permute-start(bf16[32,2048]{1,0:T(8,128)(2,1)S(1)} %get-tuple-element.18), channel_id=1, source_target_pairs={{0,16},{16,0},{1,17},{17,1},{2,18},{18,2},{3,19},{19,3},{4,20},{20... | collective-permute-start | bytes 393224 | tf_op jit(solution)/shard_map/ppermute | solution.py:168
  58.4 4.2 %collective-permute-done.17 = bf16[32,2048]{1,0:T(8,128)(2,1)S(1)} collective-permute-done((bf16[32,2048]{1,0:T(8,128)(2,1)S(1)}, bf16[32,2048]{1,0:T(8,128)(2,1)S(1)}, u32[]{:S(2)}, u32[]{:S(2)}) %collective-permute-start.17) | collective-permute-done | bytes 131104 | tf_op jit(solution)/shard_map/ppermute | solution.py:168
  62.7 2.4 %collective-permute-done.19 = bf16[32,2048]{1,0:T(8,128)(2,1)S(1)} collective-permute-done((bf16[32,2048]{1,0:T(8,128)(2,1)S(1)}, bf16[32,2048]{1,0:T(8,128)(2,1)S(1)}, u32[]{:S(2)}, u32[]{:S(2)}) %collective-permute-start.19) | collective-permute-done | bytes 131104 | tf_op jit(solution)/shard_map/ppermute | solution.py:168
  65.1 1.1 %collective-permute-start.20 = (bf16[16,2048]{1,0:T(8,128)(2,1)S(1)}, bf16[16,2048]{1,0:T(8,128)(2,1)S(1)}, u32[]{:S(2)}, u32[]{:S(2)}) collective-permute-start(bf16[16,2048]{1,0:T(8,128)(2,1)S(1)} %slice.124), channel_id=1, source_target_pairs={{0,4},{4,0},{8,12},{12,8},{1,5},{5,1},{9,13},{13,9},{2,6},{6,2},{1... | collective-permute-start | bytes 196616 | tf_op jit(solution)/shard_map/ppermute | solution.py:168
  66.2 1.1 %collective-permute-start.18 = (bf16[16,2048]{1,0:T(8,128)(2,1)S(1)}, bf16[16,2048]{1,0:T(8,128)(2,1)S(1)}, u32[]{:S(2)}, u32[]{:S(2)}) collective-permute-start(bf16[16,2048]{1,0:T(8,128)(2,1)S(1)} %slice.125), channel_id=1, source_target_pairs={{0,4},{4,0},{8,12},{12,8},{1,5},{5,1},{9,13},{13,9},{2,6},{6,2},{1... | collective-permute-start | bytes 196616 | tf_op jit(solution)/shard_map/ppermute | solution.py:168
  67.3 2.4 %collective-permute-done.20 = bf16[16,2048]{1,0:T(8,128)(2,1)S(1)} collective-permute-done((bf16[16,2048]{1,0:T(8,128)(2,1)S(1)}, bf16[16,2048]{1,0:T(8,128)(2,1)S(1)}, u32[]{:S(2)}, u32[]{:S(2)}) %collective-permute-start.20) | collective-permute-done | bytes 65568 | tf_op jit(solution)/shard_map/ppermute | solution.py:168
  69.8 3.7 %collective-permute-start.21 = (bf16[16,2048]{1,0:T(8,128)(2,1)S(1)}, bf16[16,2048]{1,0:T(8,128)(2,1)S(1)}, u32[]{:S(2)}, u32[]{:S(2)}) collective-permute-start(bf16[16,2048]{1,0:T(8,128)(2,1)S(1)} %fusion.4), channel_id=1, source_target_pairs={{0,8},{4,12},{8,0},{12,4},{1,9},{5,13},{9,1},{13,5},{2,10},{6,14},... | collective-permute-start | bytes 196616 | tf_op jit(solution)/shard_map/ppermute | solution.py:168
  73.5 2.9 %collective-permute-done.21 = bf16[16,2048]{1,0:T(8,128)(2,1)S(1)} collective-permute-done((bf16[16,2048]{1,0:T(8,128)(2,1)S(1)}, bf16[16,2048]{1,0:T(8,128)(2,1)S(1)}, u32[]{:S(2)}, u32[]{:S(2)}) %collective-permute-start.21) | collective-permute-done | bytes 65568 | tf_op jit(solution)/shard_map/ppermute | solution.py:168
  76.4 0.7 fusion.6
  (15 shorter events, 0.2 us)
Async XLA Ops:
  0.0 7.3 %collective-permute-start.1 = (bf16[16,2048]{1,0:T(8,128)(2,1)}, bf16[16,2048]{1,0:T(8,128)(2,1)S(1)}, u32[]{:S(2)}, u32[]{:S(2)}) collective-permute-start(bf16[16,2048]{1,0:T(8,128)(2,1)} %refs_0_.3), channel_id=1, source_target_pairs={{0,8},{4,12},{8,0},{12,4},{1,9},{5,13},{9,1},{13,5},{2,10},{6,14},... | collective-permute-start | bytes 196616 | tf_op jit(solution)/shard_map/ppermute | solution.py:168
  4.0 6.7 %collective-permute-start = (bf16[16,2048]{1,0:T(8,128)(2,1)}, bf16[16,2048]{1,0:T(8,128)(2,1)S(1)}, u32[]{:S(2)}, u32[]{:S(2)}) collective-permute-start(bf16[16,2048]{1,0:T(8,128)(2,1)} %refs_0_.3), channel_id=1, source_target_pairs={{0,4},{4,0},{8,12},{12,8},{1,5},{5,1},{9,13},{13,9},{2,6},{6,2},{1... | collective-permute-start | bytes 196616 | tf_op jit(solution)/shard_map/ppermute | solution.py:168
  7.3 4.9 %collective-permute-start.2 = (bf16[16,2048]{1,0:T(8,128)(2,1)S(1)}, bf16[16,2048]{1,0:T(8,128)(2,1)S(1)}, u32[]{:S(2)}, u32[]{:S(2)}) collective-permute-start(bf16[16,2048]{1,0:T(8,128)(2,1)S(1)} %collective-permute-done.1.refs_2_), channel_id=1, source_target_pairs={{0,4},{4,0},{8,12},{12,8},{1,5},{5,1},{9,13},{13,9},{2,6},{6,2},{1... | collective-permute-start | bytes 196616 | tf_op jit(solution)/shard_map/ppermute | solution.py:168
  8.7 5.2 %collective-permute-start.3 = (bf16[16,2048]{1,0:T(8,128)(2,1)}, bf16[16,2048]{1,0:T(8,128)(2,1)S(1)}, u32[]{:S(2)}, u32[]{:S(2)}) collective-permute-start(bf16[16,2048]{1,0:T(8,128)(2,1)} %refs_0_.3), channel_id=1, source_target_pairs={{0,16},{16,0},{1,17},{17,1},{2,18},{18,2},{3,19},{19,3},{4,20},{20... | collective-permute-start | bytes 196616 | tf_op jit(solution)/shard_map/ppermute | solution.py:168
  10.2 4.6 %collective-permute-start.5 = (bf16[16,2048]{1,0:T(8,128)(2,1)S(1)}, bf16[16,2048]{1,0:T(8,128)(2,1)S(1)}, u32[]{:S(2)}, u32[]{:S(2)}) collective-permute-start(bf16[16,2048]{1,0:T(8,128)(2,1)S(1)} %collective-permute-done.1.refs_2_), channel_id=1, source_target_pairs={{0,16},{16,0},{1,17},{17,1},{2,18},{18,2},{3,19},{19,3},{4,20},{20... | collective-permute-start | bytes 196616 | tf_op jit(solution)/shard_map/ppermute | solution.py:168
  10.7 4.8 %collective-permute-start.4 = (bf16[16,2048]{1,0:T(8,128)(2,1)S(1)}, bf16[16,2048]{1,0:T(8,128)(2,1)S(1)}, u32[]{:S(2)}, u32[]{:S(2)}) collective-permute-start(bf16[16,2048]{1,0:T(8,128)(2,1)S(1)} %collective-permute-done.refs_1_), channel_id=1, source_target_pairs={{0,16},{16,0},{1,17},{17,1},{2,18},{18,2},{3,19},{19,3},{4,20},{20... | collective-permute-start | bytes 196616 | tf_op jit(solution)/shard_map/ppermute | solution.py:168
  12.2 4.3 %collective-permute-start.6 = (bf16[16,2048]{1,0:T(8,128)(2,1)S(1)}, bf16[16,2048]{1,0:T(8,128)(2,1)S(1)}, u32[]{:S(2)}, u32[]{:S(2)}) collective-permute-start(bf16[16,2048]{1,0:T(8,128)(2,1)S(1)} %collective-permute-done.2.refs_3_), channel_id=1, source_target_pairs={{0,16},{16,0},{1,17},{17,1},{2,18},{18,2},{3,19},{19,3},{4,20},{20... | collective-permute-start | bytes 196616 | tf_op jit(solution)/shard_map/ppermute | solution.py:168
  16.5 0.8 %copy-start = (bf16[16,2048]{1,0:T(8,128)(2,1)S(1)}, bf16[16,2048]{1,0:T(8,128)(2,1)}, u32[]{:S(2)}) copy-start(bf16[16,2048]{1,0:T(8,128)(2,1)} %refs_0_.3) | copy-start | bytes 196612
  23.2 7.1 %collective-permute-start.12 = (bf16[2,64,1536]{2,1,0:T(8,128)(2,1)S(1)}, bf16[2,64,1536]{2,1,0:T(8,128)(2,1)S(1)}, u32[]{:S(2)}, u32[]{:S(2)}) collective-permute-start(bf16[2,64,1536]{2,1,0:T(8,128)(2,1)S(1)} %get-tuple-element.15), channel_id=1, source_target_pairs={{0,1},{1,0},{2,3},{3,2},{4,5},{5,4},{6,7},{7,6},{8,9},{9,8},{10,11... | collective-permute-start | bytes 1179656 | tf_op jit(solution)/shard_map/ppermute | solution.py:168
  29.7 2.2 %collective-permute-start.7 = (bf16[2,64,1792]{2,1,0:T(8,128)(2,1)S(1)}, bf16[2,64,1792]{2,1,0:T(8,128)(2,1)S(1)}, u32[]{:S(2)}, u32[]{:S(2)}) collective-permute-start(bf16[2,64,1792]{2,1,0:T(8,128)(2,1)S(1)} %get-tuple-element.13), channel_id=1, source_target_pairs={{0,1},{1,0},{2,3},{3,2},{4,5},{5,4},{6,7},{7,6},{8,9},{9,8},{10,11... | collective-permute-start | bytes 1376264 | tf_op jit(solution)/shard_map/ppermute | solution.py:168
  30.3 7.8 %collective-permute-start.13 = (bf16[2,32,1536]{2,1,0:T(8,128)(2,1)S(1)}, bf16[2,32,1536]{2,1,0:T(8,128)(2,1)S(1)}, u32[]{:S(2)}, u32[]{:S(2)}) collective-permute-start(bf16[2,32,1536]{2,1,0:T(8,128)(2,1)S(1)} %add_convert_fusion.1), channel_id=1, source_target_pairs={{0,2},{1,3},{2,0},{3,1},{4,6},{5,7},{6,4},{7,5},{8,10},{9,11},{10,... | collective-permute-start | bytes 589832 | tf_op jit(solution)/shard_map/ppermute | solution.py:168
  32.0 11.1 %collective-permute-start.8 = (bf16[2,32,1792]{2,1,0:T(8,128)(2,1)S(1)}, bf16[2,32,1792]{2,1,0:T(8,128)(2,1)S(1)}, u32[]{:S(2)}, u32[]{:S(2)}) collective-permute-start(bf16[2,32,1792]{2,1,0:T(8,128)(2,1)S(1)} %add_convert_fusion), channel_id=1, source_target_pairs={{0,2},{1,3},{2,0},{3,1},{4,6},{5,7},{6,4},{7,5},{8,10},{9,11},{10,... | collective-permute-start | bytes 688136 | tf_op jit(solution)/shard_map/ppermute | solution.py:168
  38.3 6.5 %collective-permute-start.14 = (bf16[32,1536]{1,0:T(8,128)(2,1)S(1)}, bf16[32,1536]{1,0:T(8,128)(2,1)S(1)}, u32[]{:S(2)}, u32[]{:S(2)}) collective-permute-start(bf16[32,1536]{1,0:T(8,128)(2,1)S(1)} %fusion.3.refs_0_), channel_id=1, source_target_pairs={{0,2},{1,3},{2,0},{3,1},{4,6},{5,7},{6,4},{7,5},{8,10},{9,11},{10,... | collective-permute-start | bytes 294920 | tf_op jit(solution)/shard_map/ppermute | solution.py:168
  43.2 4.9 %collective-permute-start.9 = (bf16[32,1792]{1,0:T(8,128)(2,1)S(1)}, bf16[32,1792]{1,0:T(8,128)(2,1)S(1)}, u32[]{:S(2)}, u32[]{:S(2)}) collective-permute-start(bf16[32,1792]{1,0:T(8,128)(2,1)S(1)} %fusion.1.refs_0_), channel_id=1, source_target_pairs={{0,2},{1,3},{2,0},{3,1},{4,6},{5,7},{6,4},{7,5},{8,10},{9,11},{10,... | collective-permute-start | bytes 344072 | tf_op jit(solution)/shard_map/ppermute | solution.py:168
  44.8 3.3 %collective-permute-start.15 = (bf16[32,1536]{1,0:T(8,128)(2,1)S(1)}, bf16[32,1536]{1,0:T(8,128)(2,1)S(1)}, u32[]{:S(2)}, u32[]{:S(2)}) collective-permute-start(bf16[32,1536]{1,0:T(8,128)(2,1)S(1)} %fusion.3.refs_0_), channel_id=1, source_target_pairs={{0,1},{1,0},{2,3},{3,2},{4,5},{5,4},{6,7},{7,6},{8,9},{9,8},{10,11... | collective-permute-start | bytes 294920 | tf_op jit(solution)/shard_map/ppermute | solution.py:168
  44.8 3.3 %collective-permute-start.16 = (bf16[32,1536]{1,0:T(8,128)(2,1)S(1)}, bf16[32,1536]{1,0:T(8,128)(2,1)S(1)}, u32[]{:S(2)}, u32[]{:S(2)}) collective-permute-start(bf16[32,1536]{1,0:T(8,128)(2,1)S(1)} %collective-permute-done.14.refs_1_), channel_id=1, source_target_pairs={{0,1},{1,0},{2,3},{3,2},{4,5},{5,4},{6,7},{7,6},{8,9},{9,8},{10,11... | collective-permute-start | bytes 294920 | tf_op jit(solution)/shard_map/ppermute | solution.py:168
  45.3 6.7 %collective-permute-start.10 = (bf16[32,1792]{1,0:T(8,128)(2,1)S(1)}, bf16[32,1792]{1,0:T(8,128)(2,1)S(1)}, u32[]{:S(2)}, u32[]{:S(2)}) collective-permute-start(bf16[32,1792]{1,0:T(8,128)(2,1)S(1)} %fusion.1.refs_0_), channel_id=1, source_target_pairs={{0,1},{1,0},{2,3},{3,2},{4,5},{5,4},{6,7},{7,6},{8,9},{9,8},{10,11... | collective-permute-start | bytes 344072 | tf_op jit(solution)/shard_map/ppermute | solution.py:168
  48.1 3.9 %collective-permute-start.11 = (bf16[32,1792]{1,0:T(8,128)(2,1)S(1)}, bf16[32,1792]{1,0:T(8,128)(2,1)S(1)}, u32[]{:S(2)}, u32[]{:S(2)}) collective-permute-start(bf16[32,1792]{1,0:T(8,128)(2,1)S(1)} %collective-permute-done.9.refs_1_), channel_id=1, source_target_pairs={{0,1},{1,0},{2,3},{3,2},{4,5},{5,4},{6,7},{7,6},{8,9},{9,8},{10,11... | collective-permute-start | bytes 344072 | tf_op jit(solution)/shard_map/ppermute | solution.py:168
  56.3 6.4 %collective-permute-start.17 = (bf16[32,2048]{1,0:T(8,128)(2,1)S(1)}, bf16[32,2048]{1,0:T(8,128)(2,1)S(1)}, u32[]{:S(2)}, u32[]{:S(2)}) collective-permute-start(bf16[32,2048]{1,0:T(8,128)(2,1)S(1)} %get-tuple-element.17), channel_id=1, source_target_pairs={{0,16},{16,0},{1,17},{17,1},{2,18},{18,2},{3,19},{19,3},{4,20},{20... | collective-permute-start | bytes 393224 | tf_op jit(solution)/shard_map/ppermute | solution.py:168
  57.6 7.5 %collective-permute-start.19 = (bf16[32,2048]{1,0:T(8,128)(2,1)S(1)}, bf16[32,2048]{1,0:T(8,128)(2,1)S(1)}, u32[]{:S(2)}, u32[]{:S(2)}) collective-permute-start(bf16[32,2048]{1,0:T(8,128)(2,1)S(1)} %get-tuple-element.18), channel_id=1, source_target_pairs={{0,16},{16,0},{1,17},{17,1},{2,18},{18,2},{3,19},{19,3},{4,20},{20... | collective-permute-start | bytes 393224 | tf_op jit(solution)/shard_map/ppermute | solution.py:168
  65.1 4.6 %collective-permute-start.20 = (bf16[16,2048]{1,0:T(8,128)(2,1)S(1)}, bf16[16,2048]{1,0:T(8,128)(2,1)S(1)}, u32[]{:S(2)}, u32[]{:S(2)}) collective-permute-start(bf16[16,2048]{1,0:T(8,128)(2,1)S(1)} %slice.124), channel_id=1, source_target_pairs={{0,4},{4,0},{8,12},{12,8},{1,5},{5,1},{9,13},{13,9},{2,6},{6,2},{1... | collective-permute-start | bytes 196616 | tf_op jit(solution)/shard_map/ppermute | solution.py:168
  66.2 7.2 %collective-permute-start.18 = (bf16[16,2048]{1,0:T(8,128)(2,1)S(1)}, bf16[16,2048]{1,0:T(8,128)(2,1)S(1)}, u32[]{:S(2)}, u32[]{:S(2)}) collective-permute-start(bf16[16,2048]{1,0:T(8,128)(2,1)S(1)} %slice.125), channel_id=1, source_target_pairs={{0,4},{4,0},{8,12},{12,8},{1,5},{5,1},{9,13},{13,9},{2,6},{6,2},{1... | collective-permute-start | bytes 196616 | tf_op jit(solution)/shard_map/ppermute | solution.py:168
  69.8 6.6 %collective-permute-start.21 = (bf16[16,2048]{1,0:T(8,128)(2,1)S(1)}, bf16[16,2048]{1,0:T(8,128)(2,1)S(1)}, u32[]{:S(2)}, u32[]{:S(2)}) collective-permute-start(bf16[16,2048]{1,0:T(8,128)(2,1)S(1)} %fusion.4), channel_id=1, source_target_pairs={{0,8},{4,12},{8,0},{12,4},{1,9},{5,13},{9,1},{13,5},{2,10},{6,14},... | collective-permute-start | bytes 196616 | tf_op jit(solution)/shard_map/ppermute | solution.py:168

commit v3 on v0

--- a/solution.py
+++ b/solution.py
@@ -1,10 +1,18 @@
+import functools
+
 import jax
 import jax.numpy as jnp
 from jax import lax
+from jax.experimental import pallas as pl
+from jax.experimental.pallas import tpu as pltpu
 from jax.sharding import PartitionSpec as P
 
-
-def on_device(tokens, gate_weight, up_weight, down_weight):
+TILE = 256
+CHUNKS = 3
+ROWS = 16
+
+
+def plain(tokens, gate_weight, up_weight, down_weight):
     piece = lax.all_gather(tokens, "hid", axis=0, tiled=True)
     gate_rows = jnp.dot(piece, gate_weight, preferred_element_type=jnp.float32)
     up_rows = jnp.dot(piece, up_weight, preferred_element_type=jnp.float32)
@@ -19,7 +27,200 @@
     )
 
 
+def pieces_of(width, most):
+    first = width % most
+    edges = ([0] if first else []) + list(range(first, width + 1, most))
+    return list(zip(edges[:-1], edges[1:]))
+
+
+def place(wid, d):
+    step = wid ^ d
+    return (step % 2) * 2 + step // 2
+
+
+def spec(space):
+    return pl.BlockSpec(memory_space=space)
+
+
+def params(mib):
+    return pltpu.CompilerParams(vmem_limit_bytes=mib * 2**20)
+
+
+def fetch_kernel(first, width, where, *refs):
+    n = len(refs) // 2
+    sources, outs, sems = refs[:n], refs[n : 2 * n], refs[-1]
+    start = pl.multiple_of(where[0] + first, TILE)
+    copies = []
+    for source, out in zip(sources, outs):
+        if source.shape != out.shape:
+            source = source.at[:, pl.ds(start, width)]
+        copies.append(pltpu.make_async_copy(source, out, sems.at[len(copies)]))
+        copies[-1].start()
+    for copy in copies:
+        copy.wait()
+
+
+def fetch(where, arrays, first, width):
+    shapes = [a.shape if a.shape[0] == ROWS else (a.shape[0], width) for a in arrays]
+    size = sum(2 * x * y for x, y in shapes)
+    return pl.pallas_call(
+        functools.partial(fetch_kernel, first, width),
+        in_specs=[spec(pltpu.SMEM)] + [spec(pltpu.HBM)] * len(arrays),
+        out_specs=[spec(pltpu.VMEM)] * len(arrays),
+        out_shape=[pltpu.VMEM(x, jnp.bfloat16) for x in shapes],
+        scratch_shapes=[pltpu.SemaphoreType.DMA((len(arrays),))],
+        compiler_params=params(1),
+        cost_estimate=pl.CostEstimate(flops=0, bytes_accessed=size, transcendentals=0),
+        name="fetch",
+    )(where, *arrays)
+
+
+def gate_up_kernel(n_blocks, where, *refs):
+    blocks, (gate_ref, up_ref, mine_ref, theirs_ref, x_ref) = refs[:n_blocks], refs[n_blocks:]
+    for b in range(n_blocks):
+        at = place(where[1], b % 4) * 2 + b // 4
+        x_ref[pl.ds(pl.multiple_of(at * ROWS, ROWS), ROWS), :] = blocks[b][...]
+    half = x_ref.shape[0] // 2
+    for a, b in pieces_of(gate_ref.shape[1], 2 * TILE):
+        for k, w_ref in enumerate((gate_ref, up_ref)):
+            part = jnp.dot(x_ref[...], w_ref[:, a:b], preferred_element_type=jnp.float32).astype(jnp.bfloat16)
+            mine_ref[k, :, a:b] = part[:half]
+            theirs_ref[k, :, a:b] = part[half:]
+
+
+def gate_up(where, blocks, gate, up):
+    depth, width = gate.shape
+    n = len(blocks)
+    total = n * ROWS
+    return pl.pallas_call(
+        functools.partial(gate_up_kernel, n),
+        in_specs=[spec(pltpu.SMEM)] + [spec(pltpu.VMEM)] * (n + 2),
+        out_specs=[spec(pltpu.VMEM)] * 2,
+        scratch_shapes=[pltpu.VMEM((total, depth), jnp.bfloat16)],
+        out_shape=[jax.ShapeDtypeStruct((2, total // 2, width), jnp.bfloat16)] * 2,
+        compiler_params=params(4),
+        cost_estimate=pl.CostEstimate(
+            flops=4 * total * depth * width, bytes_accessed=4 * depth * width, transcendentals=0
+        ),
+        name="gate_up",
+    )(where, *blocks, gate, up)
+
+
+def down_kernel(n_pieces, has_acc, last, first, half, where, *refs):
+    pieces, refs = refs[:n_pieces], refs[n_pieces:]
+    down_ref, refs = refs[0], refs[1:]
+    prev_ref, refs = (refs[0], refs[1:]) if has_acc else (None, refs)
+    outs, (acc_ref, lhs_ref) = refs[:-2], refs[-2:]
+    depth = lhs_ref.shape[2]
+    for p, piece in enumerate(pieces):
+        for k in range(2):
+            lhs_ref[k, p * ROWS : (p + 1) * ROWS, :] = piece[k * ROWS : (k + 1) * ROWS, :]
+    for a, b in pieces_of(down_ref.shape[1], 2 * TILE):
+        part = prev_ref[:, a:b] if has_acc else 0.0
+        for k in range(2):
+            start = where[0] + first if k == 0 else half - where[0] + first
+            rows = pl.ds(pl.multiple_of(start, TILE), depth)
+            part += jnp.dot(lhs_ref[k], down_ref[rows, a:b], preferred_element_type=jnp.float32)
+        acc_ref[:, a:b] = part
+    if last:
+        for d, out in enumerate(outs):
+            source = pl.multiple_of(place(where[1], d) * ROWS, ROWS)
+            out[...] = acc_ref[pl.ds(source, ROWS), :].astype(out.dtype)
+
+
+def down(where, pieces, down_weight, prev, first, last):
+    width = down_weight.shape[1]
+    n, depth = len(pieces), pieces[0].shape[1]
+    total = n * ROWS
+    args = [*pieces, down_weight] + ([] if prev is None else [prev])
+    sums = jax.ShapeDtypeStruct((total, width), jnp.float32)
+    scratch = [pltpu.VMEM((2, total, depth), jnp.bfloat16)]
+    if last:
+        scratch = [pltpu.VMEM(sums.shape, sums.dtype)] + scratch
+    return pl.pallas_call(
+        functools.partial(down_kernel, n, prev is not None, last, first, down_weight.shape[0] // 2),
+        in_specs=[spec(pltpu.SMEM)] + [spec(pltpu.VMEM)] * len(args),
+        out_specs=[spec(pltpu.VMEM)] * n if last else spec(pltpu.VMEM),
+        scratch_shapes=scratch,
+        out_shape=[jax.ShapeDtypeStruct((ROWS, width), jnp.bfloat16)] * n if last else sums,
+        compiler_params=params(4),
+        cost_estimate=pl.CostEstimate(
+            flops=4 * total * width * depth, bytes_accessed=4 * width * depth, transcendentals=0
+        ),
+        name="down",
+    )(where, *args)
+
+
+def split_by_rep(n_wid, tokens, gate_weight, up_weight, down_weight):
+    rep, wid = lax.axis_index("rep"), lax.axis_index("wid")
+    f32, bf16 = jnp.float32, jnp.bfloat16
+    width = gate_weight.shape[1] // 2
+    where = jnp.stack([rep * width, wid]).astype(jnp.int32)
+
+    def swap(x, axis, step):
+        n = {"rep": 2, "hid": 4, "wid": n_wid}[axis]
+        return lax.ppermute(x, axis, [(i, i ^ step) for i in range(n)])
+
+    tiles = width // TILE
+    bounds = [tiles * c // CHUNKS * TILE for c in range(CHUNKS + 1)]
+    sources = [pltpu.with_memory_space_constraint(w, pltpu.HBM) for w in (gate_weight, up_weight, tokens)]
+    weights = [
+        fetch(where, sources[: 2 if c else 3], bounds[c], bounds[c + 1] - bounds[c]) for c in range(CHUNKS)
+    ]
+    own_tokens = weights[0][2]
+    down_weight = pltpu.with_memory_space_constraint(down_weight, pltpu.VMEM)
+
+    far = swap(tokens, "hid", 2)
+    near = [tokens, swap(tokens, "hid", 1), far, swap(far, "hid", 1)]
+    blocks = [own_tokens] + near[1:] + [swap(x, "rep", 1) for x in near]
+
+    quarter = 2 * ROWS
+    parts, to_chips = [], []
+
+    def send_to_chip(c):
+        mine, got = parts[c]
+        to_chips.append((mine[:, quarter:].astype(f32) + got[:, quarter:].astype(f32)).astype(bf16))
+
+    turn = where
+    for c in range(CHUNKS):
+        if c >= 2:
+            send_to_chip(c - 2)
+            turn, to_chips[-1] = lax.optimization_barrier((turn, to_chips[-1]))
+        mine, theirs = gate_up(turn, blocks, *weights[c][:2])
+        parts.append((mine, swap(theirs, "wid", 1)))
+    while len(to_chips) < CHUNKS:
+        send_to_chip(len(to_chips))
+
+    acc = None
+    for c in range(CHUNKS):
+        mine, got = parts[c]
+        from_chip = swap(to_chips[c], "wid", 2)
+        summed = mine[:, :quarter].astype(f32) + got[:, :quarter].astype(f32) + from_chip.astype(f32)
+        hidden = (jax.nn.silu(summed[0]) * summed[1]).astype(bf16)
+        own = jnp.concatenate([hidden[:ROWS], swap(hidden[ROWS:], "rep", 1)], 0)
+        other = swap(own, "wid", 2)
+        pieces = [own, other, swap(own, "wid", 1), swap(other, "wid", 1)]
+        acc = down(where, pieces, down_weight, acc, bounds[c], c == CHUNKS - 1)
+
+    mixed = acc[0].astype(f32)
+    for d in (3, 2, 1):
+        mixed = mixed + swap(acc[d], "hid", d).astype(f32)
+    return mixed.astype(bf16)
+
+
 def solution(mesh):
+    n_rep, n_hid, n_wid = (mesh.shape[a] for a in ("rep", "hid", "wid"))
+
+    def on_device(tokens, gate_weight, up_weight, down_weight):
+        fits = (
+            (n_rep, n_hid, n_wid) == (2, 4, 4)
+            and gate_weight.shape[1] % (n_rep * TILE) == 0
+            and tokens.shape[0] == ROWS
+        )
+        if not fits:
+            return plain(tokens, gate_weight, up_weight, down_weight)
+        return split_by_rep(n_wid, tokens, gate_weight, up_weight, down_weight)
+
     return jax.shard_map(
         on_device,
         mesh=mesh,

time: 134 us -> 72.7 us (0.54)
  waiting for transfers between devices: 66.5 us -> 17.5 us
  matrix products: 34.7 us -> 0 us
  starting transfers between devices: 0.04 us -> 27.9 us
  Pallas kernels: 0 us -> 25.6 us
  blocking collectives: 15.8 us -> 0 us
  between operations: 13.4 us -> 0.34 us
  other arithmetic: 3.12 us -> 1.18 us
    psum x1 -> x0, waiting for transfers between devices: 46.6 us -> none  [on_device(): lax.psum(partial_terms.astype(jnp.bfloat16), 'wid').astype(jnp.float32)]
    dot_general x3 -> x0, matrix products: 34.7 us -> none  [the longest x1 12 us: on_device(): jnp.dot(hidden, down_weight, preferred_element_type=jnp.float32)]
    ppermute x0 -> x28, starting transfers between devices: none -> 27.9 us  [swap(): return lax.ppermute(x, axis, [(i, i ^ step) for i in range(n)])]
    pallas_call x0 -> x9, Pallas kernels: none -> 25.6 us  [the longest x3 13 us: fetch(): pl.pallas_call(functools.partial(fetch_kernel, first, width), in_specs=[s...]
    reduce_scatter x1 -> x0, waiting for transfers between devices: 19.9 us -> none  [on_device(): lax.psum_scatter(jnp.dot(hidden, down_weight, preferred_element_type=jnp....]
    ppermute x0 -> x28, waiting for transfers between devices: none -> 17.5 us  [swap(): return lax.ppermute(x, axis, [(i, i ^ step) for i in range(n)])]
    all_gather x1 -> x0, blocking collectives: 15.8 us -> none  [on_device(): piece = lax.all_gather(tokens, 'hid', axis=0, tiled=True)]
  transfers between devices with their start and end apart: 2 -> 28, of which waited for: 2 -> 8; matrix products, arithmetic and copies ran while one was open for 0% -> 1% of each run, Pallas kernels for 0% -> 29%
where the time goes in v3:
time: 72.7 us; the launch traced here: 72.5 us
  starting transfers between devices  27.9 us (38%)
  Pallas kernels  25.6 us (35%)
  waiting for transfers between devices  17.5 us (24%)
  other arithmetic  1.18 us (2%)
    ppermute x28, starting transfers between devices, swap(): return lax.ppermute(x, axis, [(i, i ^ step) for i in range(n)])  27.9 us
    ppermute x28, waiting for transfers between devices, swap(): return lax.ppermute(x, axis, [(i, i ^ step) for i in range(n)])  17.5 us
    pallas_call x3, Pallas kernels, fetch(): pl.pallas_call(functools.partial(fetch_kernel, first, width), in_specs=[s...  13 us
    pallas_call x3, Pallas kernels, down(): pl.pallas_call(functools.partial(down_kernel, n, prev is not None, last,...  6.73 us
    pallas_call x3, Pallas kernels, gate_up(): pl.pallas_call(functools.partial(gate_up_kernel, n), in_specs=[spec(pltpu...  5.86 us
  transfers between devices with their start and end apart: 28, of which 8 were waited for; matrix products, arithmetic and copies ran while one was open for 1% of the time, Pallas kernels for 29%

profile of v3, /device:TPU:0, one launch (start us, length us, event | category | flops | bytes accessed | tf_op | source)
XLA Modules:
  0.0 72.5 jit_solution(8638427913955245838)
XLA Ops:
  0.0 4.0 %collective-permute-start.1 = (bf16[16,2048]{1,0:T(8,128)(2,1)}, bf16[16,2048]{1,0:T(8,128)(2,1)S(1)}, u32[]{:S(2)}, u32[]{:S(2)}) collective-permute-start(bf16[16,2048]{1,0:T(8,128)(2,1)} %refs_2_.1), channel_id=1, source_target_pairs={{0,8},{4,12},{8,0},{12,4},{1,9},{5,13},{9,1},{13,5},{2,10},{6,14},... | collective-permute-start | bytes 196616 | tf_op jit(solution)/shard_map/ppermute | solution.py:162
  4.0 1.6 %collective-permute-start = (bf16[16,2048]{1,0:T(8,128)(2,1)}, bf16[16,2048]{1,0:T(8,128)(2,1)S(1)}, u32[]{:S(2)}, u32[]{:S(2)}) collective-permute-start(bf16[16,2048]{1,0:T(8,128)(2,1)} %refs_2_.1), channel_id=1, source_target_pairs={{0,4},{4,0},{8,12},{12,8},{1,5},{5,1},{9,13},{13,9},{2,6},{6,2},{1... | collective-permute-start | bytes 196616 | tf_op jit(solution)/shard_map/ppermute | solution.py:162
  5.6 1.7 %collective-permute-done.1.refs_2_ = bf16[16,2048]{1,0:T(8,128)(2,1)S(1)} collective-permute-done((bf16[16,2048]{1,0:T(8,128)(2,1)}, bf16[16,2048]{1,0:T(8,128)(2,1)S(1)}, u32[]{:S(2)}, u32[]{:S(2)}) %collective-permute-start.1) | collective-permute-done | bytes 65568 | tf_op jit(solution)/shard_map/ppermute | solution.py:162
  7.3 1.4 %collective-permute-start.2 = (bf16[16,2048]{1,0:T(8,128)(2,1)S(1)}, bf16[16,2048]{1,0:T(8,128)(2,1)S(1)}, u32[]{:S(2)}, u32[]{:S(2)}) collective-permute-start(bf16[16,2048]{1,0:T(8,128)(2,1)S(1)} %collective-permute-done.1.refs_2_), channel_id=1, source_target_pairs={{0,4},{4,0},{8,12},{12,8},{1,5},{5,1},{9,13},{13,9},{2,6},{6,2},{1... | collective-permute-start | bytes 196616 | tf_op jit(solution)/shard_map/ppermute | solution.py:162
  8.7 1.5 %collective-permute-start.3 = (bf16[16,2048]{1,0:T(8,128)(2,1)}, bf16[16,2048]{1,0:T(8,128)(2,1)S(1)}, u32[]{:S(2)}, u32[]{:S(2)}) collective-permute-start(bf16[16,2048]{1,0:T(8,128)(2,1)} %refs_2_.1), channel_id=1, source_target_pairs={{0,16},{16,0},{1,17},{17,1},{2,18},{18,2},{3,19},{19,3},{4,20},{20... | collective-permute-start | bytes 196616 | tf_op jit(solution)/shard_map/ppermute | solution.py:162
  10.2 0.5 collective-permute-start.5
  10.7 1.5 %collective-permute-start.4 = (bf16[16,2048]{1,0:T(8,128)(2,1)S(1)}, bf16[16,2048]{1,0:T(8,128)(2,1)S(1)}, u32[]{:S(2)}, u32[]{:S(2)}) collective-permute-start(bf16[16,2048]{1,0:T(8,128)(2,1)S(1)} %collective-permute-done.refs_1_), channel_id=1, source_target_pairs={{0,16},{16,0},{1,17},{17,1},{2,18},{18,2},{3,19},{19,3},{4,20},{20... | collective-permute-start | bytes 196616 | tf_op jit(solution)/shard_map/ppermute | solution.py:162
  12.2 1.2 %collective-permute-start.6 = (bf16[16,2048]{1,0:T(8,128)(2,1)S(1)}, bf16[16,2048]{1,0:T(8,128)(2,1)S(1)}, u32[]{:S(2)}, u32[]{:S(2)}) collective-permute-start(bf16[16,2048]{1,0:T(8,128)(2,1)S(1)} %collective-permute-done.2.refs_3_), channel_id=1, source_target_pairs={{0,16},{16,0},{1,17},{17,1},{2,18},{18,2},{3,19},{19,3},{4,20},{20... | collective-permute-start | bytes 196616 | tf_op jit(solution)/shard_map/ppermute | solution.py:162
  13.4 0.1 pad_add_fusion.where
  13.5 4.0 %fetch.3 = (bf16[2048,1024]{1,0:T(8,128)(2,1)S(1)}, bf16[2048,1024]{1,0:T(8,128)(2,1)S(1)}, bf16[16,2048]{1,0:T(8,128)(2,1)S(1)}) custom-call(s32[2]{0:T(128)S(1)} %pad_add_fusion.where, bf16[2048,6656]{1,0:T(8,128)(2,1)} %refs_0_.5, bf16[2048,6656]{1,0:T(8,128)(2,1)} %refs_1_.5, bf16[16,2048]{1,0:T(8,128)(2,1)} %refs_2_.1), custom_call_target="tpu_custom_call" | custom-call | bytes 8454144 | tf_op jit(solution)/shard_map/fetch/pallas_call | solution.py:66
  17.6 1.9 %gate_up.3 = (bf16[2,64,1024]{2,1,0:T(8,128)(2,1)S(1)}, bf16[2,64,1024]{2,1,0:T(8,128)(2,1)S(1)}) custom-call(s32[2]{0:T(128)S(1)} %pad_add_fusion.where, bf16[16,2048]{1,0:T(8,128)(2,1)S(1)} %get-tuple-element.24.refs_0_, bf16[16,2048]{1,0:T(8,128)(2,1)S(1)} %collective-permute-done.refs_1_, bf16[16,2048]{1,0:T(8,128)(2,1)S(1)} %collective-permute-done.1.refs_2_, ...), custom_call_target="tpu_custom_call" | custom-call | flops 1073741824 | bytes 8388608 | tf_op jit(solution)/shard_map/gate_up/pallas_call | solution.py:95
  19.5 0.1 collective-permute-start.7
  19.6 4.0 %fetch.5 = (bf16[2048,1024]{1,0:T(8,128)(2,1)S(1)}, bf16[2048,1024]{1,0:T(8,128)(2,1)S(1)}) custom-call(s32[2]{0:T(128)S(1)} %pad_add_fusion.where, bf16[2048,6656]{1,0:T(8,128)(2,1)} %refs_0_.5, bf16[2048,6656]{1,0:T(8,128)(2,1)} %refs_1_.5), custom_call_target="tpu_custom_call" | custom-call | bytes 8388608 | tf_op jit(solution)/shard_map/fetch/pallas_call | solution.py:66
  23.6 1.8 %gate_up.5 = (bf16[2,64,1024]{2,1,0:T(8,128)(2,1)S(1)}, bf16[2,64,1024]{2,1,0:T(8,128)(2,1)S(1)}) custom-call(s32[2]{0:T(128)S(1)} %pad_add_fusion.where, bf16[16,2048]{1,0:T(8,128)(2,1)S(1)} %get-tuple-element.24.refs_0_, bf16[16,2048]{1,0:T(8,128)(2,1)S(1)} %collective-permute-done.refs_1_, bf16[16,2048]{1,0:T(8,128)(2,1)S(1)} %collective-permute-done.1.refs_2_, ...), custom_call_target="tpu_custom_call" | custom-call | flops 1073741824 | bytes 8388608 | tf_op jit(solution)/shard_map/gate_up/pallas_call | solution.py:95
  25.5 0.6 collective-permute-start.14
  26.0 0.0 slice-start.4
  26.0 0.0 slice-start.5
  26.1 4.9 %fetch.4 = (bf16[2048,1280]{1,0:T(8,128)(2,1)S(1)}, bf16[2048,1280]{1,0:T(8,128)(2,1)S(1)}) custom-call(s32[2]{0:T(128)S(1)} %pad_add_fusion.where, bf16[2048,6656]{1,0:T(8,128)(2,1)} %refs_0_.5, bf16[2048,6656]{1,0:T(8,128)(2,1)} %refs_1_.5), custom_call_target="tpu_custom_call" | custom-call | bytes 10485760 | tf_op jit(solution)/shard_map/fetch/pallas_call | solution.py:66
  31.0 1.6 %collective-permute-start.20 = (bf16[2,32,1024]{2,1,0:T(8,128)(2,1)S(1)}, bf16[2,32,1024]{2,1,0:T(8,128)(2,1)S(1)}, u32[]{:S(2)}, u32[]{:S(2)}) collective-permute-start(bf16[2,32,1024]{2,1,0:T(8,128)(2,1)S(1)} %add_convert_fusion.2), channel_id=1, source_target_pairs={{0,2},{1,3},{2,0},{3,1},{4,6},{5,7},{6,4},{7,5},{8,10},{9,11},{10,... | collective-permute-start | bytes 393224 | tf_op jit(solution)/shard_map/ppermute | solution.py:162
  32.6 0.6 collective-permute-start.15
  33.2 2.2 %gate_up.4 = (bf16[2,64,1280]{2,1,0:T(8,128)(2,1)S(1)}, bf16[2,64,1280]{2,1,0:T(8,128)(2,1)S(1)}) custom-call(s32[2]{0:T(128)S(1)} %pad_add_fusion.where, bf16[16,2048]{1,0:T(8,128)(2,1)S(1)} %get-tuple-element.24.refs_0_, bf16[16,2048]{1,0:T(8,128)(2,1)S(1)} %collective-permute-done.refs_1_, bf16[16,2048]{1,0:T(8,128)(2,1)S(1)} %collective-permute-done.1.refs_2_, ...), custom_call_target="tpu_custom_call" | custom-call | flops 1342177280 | bytes 10485760 | tf_op jit(solution)/shard_map/gate_up/pallas_call | solution.py:95
  35.4 0.1 collective-permute-start.8
  35.5 2.0 %collective-permute-done.20 = bf16[2,32,1024]{2,1,0:T(8,128)(2,1)S(1)} collective-permute-done((bf16[2,32,1024]{2,1,0:T(8,128)(2,1)S(1)}, bf16[2,32,1024]{2,1,0:T(8,128)(2,1)S(1)}, u32[]{:S(2)}, u32[]{:S(2)}) %collective-permute-start.20) | collective-permute-done | bytes 131104 | tf_op jit(solution)/shard_map/ppermute | solution.py:162
  37.6 0.9 %collective-permute-start.21 = (bf16[16,1024]{1,0:T(8,128)(2,1)S(1)}, bf16[16,1024]{1,0:T(8,128)(2,1)S(1)}, u32[]{:S(2)}, u32[]{:S(2)}) collective-permute-start(bf16[16,1024]{1,0:T(8,128)(2,1)S(1)} %get-tuple-element.46), channel_id=1, source_target_pairs={{0,16},{16,0},{1,17},{17,1},{2,18},{18,2},{3,19},{19,3},{4,20},{20... | collective-permute-start | bytes 98312 | tf_op jit(solution)/shard_map/ppermute | solution.py:162
  38.4 0.9 %collective-permute-done.15 = bf16[2,32,1024]{2,1,0:T(8,128)(2,1)S(1)} collective-permute-done((bf16[2,32,1024]{2,1,0:T(8,128)(2,1)S(1)}, bf16[2,32,1024]{2,1,0:T(8,128)(2,1)S(1)}, u32[]{:S(2)}, u32[]{:S(2)}) %collective-permute-start.15) | collective-permute-done | bytes 131104 | tf_op jit(solution)/shard_map/ppermute | solution.py:162
  39.5 1.6 %collective-permute-start.9 = (bf16[2,32,1280]{2,1,0:T(8,128)(2,1)S(1)}, bf16[2,32,1280]{2,1,0:T(8,128)(2,1)S(1)}, u32[]{:S(2)}, u32[]{:S(2)}) collective-permute-start(bf16[2,32,1280]{2,1,0:T(8,128)(2,1)S(1)} %add_convert_fusion), channel_id=1, source_target_pairs={{0,2},{1,3},{2,0},{3,1},{4,6},{5,7},{6,4},{7,5},{8,10},{9,11},{10,... | collective-permute-start | bytes 491528 | tf_op jit(solution)/shard_map/ppermute | solution.py:162
  41.1 0.8 %collective-permute-start.16 = (bf16[16,1024]{1,0:T(8,128)(2,1)S(1)}, bf16[16,1024]{1,0:T(8,128)(2,1)S(1)}, u32[]{:S(2)}, u32[]{:S(2)}) collective-permute-start(bf16[16,1024]{1,0:T(8,128)(2,1)S(1)} %get-tuple-element.48), channel_id=1, source_target_pairs={{0,16},{16,0},{1,17},{17,1},{2,18},{18,2},{3,19},{19,3},{4,20},{20... | collective-permute-start | bytes 98312 | tf_op jit(solution)/shard_map/ppermute | solution.py:162
  41.9 3.0 %collective-permute-done.9 = bf16[2,32,1280]{2,1,0:T(8,128)(2,1)S(1)} collective-permute-done((bf16[2,32,1280]{2,1,0:T(8,128)(2,1)S(1)}, bf16[2,32,1280]{2,1,0:T(8,128)(2,1)S(1)}, u32[]{:S(2)}, u32[]{:S(2)}) %collective-permute-start.9) | collective-permute-done | bytes 163872 | tf_op jit(solution)/shard_map/ppermute | solution.py:162
  44.9 0.1 convert_add_fusion
  45.0 0.1 fusion.1
  45.1 0.9 %collective-permute-start.10 = (bf16[16,1280]{1,0:T(8,128)(2,1)S(1)}, bf16[16,1280]{1,0:T(8,128)(2,1)S(1)}, u32[]{:S(2)}, u32[]{:S(2)}) collective-permute-start(bf16[16,1280]{1,0:T(8,128)(2,1)S(1)} %get-tuple-element.44), channel_id=1, source_target_pairs={{0,16},{16,0},{1,17},{17,1},{2,18},{18,2},{3,19},{19,3},{4,20},{20... | collective-permute-start | bytes 122888 | tf_op jit(solution)/shard_map/ppermute | solution.py:162
  45.9 1.6 %collective-permute-start.22 = (bf16[32,1024]{1,0:T(8,128)(2,1)S(1)}, bf16[32,1024]{1,0:T(8,128)(2,1)S(1)}, u32[]{:S(2)}, u32[]{:S(2)}) collective-permute-start(bf16[32,1024]{1,0:T(8,128)(2,1)S(1)} %pad_maximum_fusion.2.refs_0_), channel_id=1, source_target_pairs={{0,2},{1,3},{2,0},{3,1},{4,6},{5,7},{6,4},{7,5},{8,10},{9,11},{10,... | collective-permute-start | bytes 196616 | tf_op jit(solution)/shard_map/ppermute | solution.py:162
  47.5 1.6 %collective-permute-done.10 = bf16[16,1280]{1,0:T(8,128)(2,1)S(1)} collective-permute-done((bf16[16,1280]{1,0:T(8,128)(2,1)S(1)}, bf16[16,1280]{1,0:T(8,128)(2,1)S(1)}, u32[]{:S(2)}, u32[]{:S(2)}) %collective-permute-start.10) | collective-permute-done | bytes 40992 | tf_op jit(solution)/shard_map/ppermute | solution.py:162
  49.1 1.5 %collective-permute-start.11 = (bf16[32,1280]{1,0:T(8,128)(2,1)S(1)}, bf16[32,1280]{1,0:T(8,128)(2,1)S(1)}, u32[]{:S(2)}, u32[]{:S(2)}) collective-permute-start(bf16[32,1280]{1,0:T(8,128)(2,1)S(1)} %pad_maximum_fusion.refs_0_), channel_id=1, source_target_pairs={{0,2},{1,3},{2,0},{3,1},{4,6},{5,7},{6,4},{7,5},{8,10},{9,11},{10,... | collective-permute-start | bytes 245768 | tf_op jit(solution)/shard_map/ppermute | solution.py:162
  50.6 0.6 collective-permute-start.17
  51.2 0.5 collective-permute-start.24
  51.8 0.0 collective-permute-start.18
  51.8 3.2 %collective-permute-done.17.refs_1_ = bf16[32,1024]{1,0:T(8,128)(2,1)S(1)} collective-permute-done((bf16[32,1024]{1,0:T(8,128)(2,1)S(1)}, bf16[32,1024]{1,0:T(8,128)(2,1)S(1)}, u32[]{:S(2)}, u32[]{:S(2)}) %collective-permute-start.17) | collective-permute-done | bytes 65568 | tf_op jit(solution)/shard_map/ppermute | solution.py:162
  55.0 0.5 collective-permute-start.12
  55.5 0.1 collective-permute-start.13
  55.6 2.1 %down.3.refs_5_ = f32[64,2048]{1,0:T(8,128)S(1)} custom-call(s32[2]{0:T(128)S(1)} %pad_add_fusion.where, bf16[32,1024]{1,0:T(8,128)(2,1)S(1)} %pad_maximum_fusion.2.refs_0_, bf16[32,1024]{1,0:T(8,128)(2,1)S(1)} %collective-permute-done.22.refs_1_, bf16[32,1024]{1,0:T(8,128)(2,1)S(1)} %collective-permute-done.23.refs_2_, ...), custom_call_target="tpu_custom_call" | custom-call | flops 536870912 | bytes 8388608 | tf_op jit(solution)/shard_map/down/pallas_call | solution.py:140
  57.8 2.1 %down.4.refs_5_ = f32[64,2048]{1,0:T(8,128)S(1)} custom-call(s32[2]{0:T(128)S(1)} %pad_add_fusion.where, bf16[32,1024]{1,0:T(8,128)(2,1)S(1)} %pad_maximum_fusion.1.refs_0_, bf16[32,1024]{1,0:T(8,128)(2,1)S(1)} %collective-permute-done.17.refs_1_, bf16[32,1024]{1,0:T(8,128)(2,1)S(1)} %collective-permute-done.18.refs_2_, ...), custom_call_target="tpu_custom_call" | custom-call | flops 536870912 | bytes 8388608 | tf_op jit(solution)/shard_map/down/pallas_call | solution.py:140
  59.9 2.5 %down.5 = (bf16[16,2048]{1,0:T(8,128)(2,1)S(1)}, bf16[16,2048]{1,0:T(8,128)(2,1)S(1)}, bf16[16,2048]{1,0:T(8,128)(2,1)S(1)}, bf16[16,2048]{1,0:T(8,128)(2,1)S(1)}) custom-call(s32[2]{0:T(128)S(1)} %pad_add_fusion.where, bf16[32,1280]{1,0:T(8,128)(2,1)S(1)} %pad_maximum_fusion.refs_0_, bf16[32,1280]{1,0:T(8,128)(2,1)S(1)} %collective-permute-done.11.refs_1_, ...), custom_call_target="tpu_custom_call" | custom-call | flops 671088640 | bytes 10485760 | tf_op jit(solution)/shard_map/down/pallas_call | solution.py:140
  62.4 3.7 %collective-permute-start.25 = (bf16[16,2048]{1,0:T(8,128)(2,1)S(1)}, bf16[16,2048]{1,0:T(8,128)(2,1)S(1)}, u32[]{:S(2)}, u32[]{:S(2)}) collective-permute-start(bf16[16,2048]{1,0:T(8,128)(2,1)S(1)} %get-tuple-element.40), channel_id=1, source_target_pairs={{0,12},{4,8},{8,4},{12,0},{1,13},{5,9},{9,5},{13,1},{2,14},{6,10},... | collective-permute-start | bytes 196616 | tf_op jit(solution)/shard_map/ppermute | solution.py:162
  66.1 0.8 %collective-permute-start.27 = (bf16[16,2048]{1,0:T(8,128)(2,1)S(1)}, bf16[16,2048]{1,0:T(8,128)(2,1)S(1)}, u32[]{:S(2)}, u32[]{:S(2)}) collective-permute-start(bf16[16,2048]{1,0:T(8,128)(2,1)S(1)} %get-tuple-element.42), channel_id=1, source_target_pairs={{0,4},{4,0},{8,12},{12,8},{1,5},{5,1},{9,13},{13,9},{2,6},{6,2},{1... | collective-permute-start | bytes 196616 | tf_op jit(solution)/shard_map/ppermute | solution.py:162
  66.9 2.3 %collective-permute-done.25 = bf16[16,2048]{1,0:T(8,128)(2,1)S(1)} collective-permute-done((bf16[16,2048]{1,0:T(8,128)(2,1)S(1)}, bf16[16,2048]{1,0:T(8,128)(2,1)S(1)}, u32[]{:S(2)}, u32[]{:S(2)}) %collective-permute-start.25) | collective-permute-done | bytes 65568 | tf_op jit(solution)/shard_map/ppermute | solution.py:162
  69.2 2.7 %collective-permute-done.26 = bf16[16,2048]{1,0:T(8,128)(2,1)S(1)} collective-permute-done((bf16[16,2048]{1,0:T(8,128)(2,1)S(1)}, bf16[16,2048]{1,0:T(8,128)(2,1)S(1)}, u32[]{:S(2)}, u32[]{:S(2)}) %collective-permute-start.26) | collective-permute-done | bytes 65568 | tf_op jit(solution)/shard_map/ppermute | solution.py:162
  71.9 0.7 add_convert_fusion.3
  (49 shorter events, 0.4 us)
Async XLA Ops:
  0.0 7.3 %collective-permute-start.1 = (bf16[16,2048]{1,0:T(8,128)(2,1)}, bf16[16,2048]{1,0:T(8,128)(2,1)S(1)}, u32[]{:S(2)}, u32[]{:S(2)}) collective-permute-start(bf16[16,2048]{1,0:T(8,128)(2,1)} %refs_2_.1), channel_id=1, source_target_pairs={{0,8},{4,12},{8,0},{12,4},{1,9},{5,13},{9,1},{13,5},{2,10},{6,14},... | collective-permute-start | bytes 196616 | tf_op jit(solution)/shard_map/ppermute | solution.py:162
  4.0 6.7 %collective-permute-start = (bf16[16,2048]{1,0:T(8,128)(2,1)}, bf16[16,2048]{1,0:T(8,128)(2,1)S(1)}, u32[]{:S(2)}, u32[]{:S(2)}) collective-permute-start(bf16[16,2048]{1,0:T(8,128)(2,1)} %refs_2_.1), channel_id=1, source_target_pairs={{0,4},{4,0},{8,12},{12,8},{1,5},{5,1},{9,13},{13,9},{2,6},{6,2},{1... | collective-permute-start | bytes 196616 | tf_op jit(solution)/shard_map/ppermute | solution.py:162
  7.3 4.9 %collective-permute-start.2 = (bf16[16,2048]{1,0:T(8,128)(2,1)S(1)}, bf16[16,2048]{1,0:T(8,128)(2,1)S(1)}, u32[]{:S(2)}, u32[]{:S(2)}) collective-permute-start(bf16[16,2048]{1,0:T(8,128)(2,1)S(1)} %collective-permute-done.1.refs_2_), channel_id=1, source_target_pairs={{0,4},{4,0},{8,12},{12,8},{1,5},{5,1},{9,13},{13,9},{2,6},{6,2},{1... | collective-permute-start | bytes 196616 | tf_op jit(solution)/shard_map/ppermute | solution.py:162
  8.7 8.9 %collective-permute-start.3 = (bf16[16,2048]{1,0:T(8,128)(2,1)}, bf16[16,2048]{1,0:T(8,128)(2,1)S(1)}, u32[]{:S(2)}, u32[]{:S(2)}) collective-permute-start(bf16[16,2048]{1,0:T(8,128)(2,1)} %refs_2_.1), channel_id=1, source_target_pairs={{0,16},{16,0},{1,17},{17,1},{2,18},{18,2},{3,19},{19,3},{4,20},{20... | collective-permute-start | bytes 196616 | tf_op jit(solution)/shard_map/ppermute | solution.py:162
  10.2 7.4 %collective-permute-start.5 = (bf16[16,2048]{1,0:T(8,128)(2,1)S(1)}, bf16[16,2048]{1,0:T(8,128)(2,1)S(1)}, u32[]{:S(2)}, u32[]{:S(2)}) collective-permute-start(bf16[16,2048]{1,0:T(8,128)(2,1)S(1)} %collective-permute-done.1.refs_2_), channel_id=1, source_target_pairs={{0,16},{16,0},{1,17},{17,1},{2,18},{18,2},{3,19},{19,3},{4,20},{20... | collective-permute-start | bytes 196616 | tf_op jit(solution)/shard_map/ppermute | solution.py:162
  10.7 6.9 %collective-permute-start.4 = (bf16[16,2048]{1,0:T(8,128)(2,1)S(1)}, bf16[16,2048]{1,0:T(8,128)(2,1)S(1)}, u32[]{:S(2)}, u32[]{:S(2)}) collective-permute-start(bf16[16,2048]{1,0:T(8,128)(2,1)S(1)} %collective-permute-done.refs_1_), channel_id=1, source_target_pairs={{0,16},{16,0},{1,17},{17,1},{2,18},{18,2},{3,19},{19,3},{4,20},{20... | collective-permute-start | bytes 196616 | tf_op jit(solution)/shard_map/ppermute | solution.py:162
  12.2 5.4 %collective-permute-start.6 = (bf16[16,2048]{1,0:T(8,128)(2,1)S(1)}, bf16[16,2048]{1,0:T(8,128)(2,1)S(1)}, u32[]{:S(2)}, u32[]{:S(2)}) collective-permute-start(bf16[16,2048]{1,0:T(8,128)(2,1)S(1)} %collective-permute-done.2.refs_3_), channel_id=1, source_target_pairs={{0,16},{16,0},{1,17},{17,1},{2,18},{18,2},{3,19},{19,3},{4,20},{20... | collective-permute-start | bytes 196616 | tf_op jit(solution)/shard_map/ppermute | solution.py:162
  19.5 11.5 %collective-permute-start.7 = (bf16[2,64,1024]{2,1,0:T(8,128)(2,1)S(1)}, bf16[2,64,1024]{2,1,0:T(8,128)(2,1)S(1)}, u32[]{:S(2)}, u32[]{:S(2)}) collective-permute-start(bf16[2,64,1024]{2,1,0:T(8,128)(2,1)S(1)} %get-tuple-element.28), channel_id=1, source_target_pairs={{0,1},{1,0},{2,3},{3,2},{4,5},{5,4},{6,7},{7,6},{8,9},{9,8},{10,11... | collective-permute-start | bytes 786440 | tf_op jit(solution)/shard_map/ppermute | solution.py:162
  25.5 7.1 %collective-permute-start.14 = (bf16[2,64,1024]{2,1,0:T(8,128)(2,1)S(1)}, bf16[2,64,1024]{2,1,0:T(8,128)(2,1)S(1)}, u32[]{:S(2)}, u32[]{:S(2)}) collective-permute-start(bf16[2,64,1024]{2,1,0:T(8,128)(2,1)S(1)} %get-tuple-element.37), channel_id=1, source_target_pairs={{0,1},{1,0},{2,3},{3,2},{4,5},{5,4},{6,7},{7,6},{8,9},{9,8},{10,11... | collective-permute-start | bytes 786440 | tf_op jit(solution)/shard_map/ppermute | solution.py:162
  26.0 29.5 %slice-start = ((s8[27262976]{0:T(1024)(128)(4,1)}), s8[4194304]{0:T(1024)(128)(4,1)S(1)}, s32[]{:S(2)}) async-start(s8[27262976]{0:T(1024)(128)(4,1)} %bitcast.32), calls=%async_computation | async-start | bytes 8388608
  26.0 29.5 %slice-start.1 = ((s8[27262976]{0:T(1024)(128)(4,1)}), s8[4194304]{0:T(1024)(128)(4,1)S(1)}, s32[]{:S(2)}) async-start(s8[27262976]{0:T(1024)(128)(4,1)} %bitcast.32), calls=%async_computation.1 | async-start | bytes 8388608
  26.0 29.5 %slice-start.2 = ((s8[27262976]{0:T(1024)(128)(4,1)}), s8[4194304]{0:T(1024)(128)(4,1)S(1)}, s32[]{:S(2)}) async-start(s8[27262976]{0:T(1024)(128)(4,1)} %bitcast.32), calls=%async_computation.2 | async-start | bytes 8388608
  26.0 29.6 %slice-start.3 = ((s8[27262976]{0:T(1024)(128)(4,1)}), s8[4194304]{0:T(1024)(128)(4,1)S(1)}, s32[]{:S(2)}) async-start(s8[27262976]{0:T(1024)(128)(4,1)} %bitcast.32), calls=%async_computation.3 | async-start | bytes 8388608
  26.0 29.6 %slice-start.4 = ((s8[27262976]{0:T(1024)(128)(4,1)}), s8[4194304]{0:T(1024)(128)(4,1)S(1)}, s32[]{:S(2)}) async-start(s8[27262976]{0:T(1024)(128)(4,1)} %bitcast.32), calls=%async_computation.4 | async-start | bytes 8388608
  26.0 29.6 %slice-start.5 = ((s8[27262976]{0:T(1024)(128)(4,1)}), s8[4194304]{0:T(1024)(128)(4,1)S(1)}, s32[]{:S(2)}) async-start(s8[27262976]{0:T(1024)(128)(4,1)} %bitcast.32), calls=%async_computation.5 | async-start | bytes 8388608
  31.0 6.4 %collective-permute-start.20 = (bf16[2,32,1024]{2,1,0:T(8,128)(2,1)S(1)}, bf16[2,32,1024]{2,1,0:T(8,128)(2,1)S(1)}, u32[]{:S(2)}, u32[]{:S(2)}) collective-permute-start(bf16[2,32,1024]{2,1,0:T(8,128)(2,1)S(1)} %add_convert_fusion.2), channel_id=1, source_target_pairs={{0,2},{1,3},{2,0},{3,1},{4,6},{5,7},{6,4},{7,5},{8,10},{9,11},{10,... | collective-permute-start | bytes 393224 | tf_op jit(solution)/shard_map/ppermute | solution.py:162
  32.6 6.7 %collective-permute-start.15 = (bf16[2,32,1024]{2,1,0:T(8,128)(2,1)S(1)}, bf16[2,32,1024]{2,1,0:T(8,128)(2,1)S(1)}, u32[]{:S(2)}, u32[]{:S(2)}) collective-permute-start(bf16[2,32,1024]{2,1,0:T(8,128)(2,1)S(1)} %add_convert_fusion.1), channel_id=1, source_target_pairs={{0,2},{1,3},{2,0},{3,1},{4,6},{5,7},{6,4},{7,5},{8,10},{9,11},{10,... | collective-permute-start | bytes 393224 | tf_op jit(solution)/shard_map/ppermute | solution.py:162
  33.2 22.4 %slice-start.6 = ((s8[27262976]{0:T(1024)(128)(4,1)}), s8[2097152]{0:T(1024)(128)(4,1)S(1)}, s32[]{:S(2)}) async-start(s8[27262976]{0:T(1024)(128)(4,1)} %bitcast.32), calls=%async_computation.6 | async-start | bytes 4194304
  35.4 4.1 %collective-permute-start.8 = (bf16[2,64,1280]{2,1,0:T(8,128)(2,1)S(1)}, bf16[2,64,1280]{2,1,0:T(8,128)(2,1)S(1)}, u32[]{:S(2)}, u32[]{:S(2)}) collective-permute-start(bf16[2,64,1280]{2,1,0:T(8,128)(2,1)S(1)} %get-tuple-element.33), channel_id=1, source_target_pairs={{0,1},{1,0},{2,3},{3,2},{4,5},{5,4},{6,7},{7,6},{8,9},{9,8},{10,11... | collective-permute-start | bytes 983048 | tf_op jit(solution)/shard_map/ppermute | solution.py:162
  37.6 8.4 %collective-permute-start.21 = (bf16[16,1024]{1,0:T(8,128)(2,1)S(1)}, bf16[16,1024]{1,0:T(8,128)(2,1)S(1)}, u32[]{:S(2)}, u32[]{:S(2)}) collective-permute-start(bf16[16,1024]{1,0:T(8,128)(2,1)S(1)} %get-tuple-element.46), channel_id=1, source_target_pairs={{0,16},{16,0},{1,17},{17,1},{2,18},{18,2},{3,19},{19,3},{4,20},{20... | collective-permute-start | bytes 98312 | tf_op jit(solution)/shard_map/ppermute | solution.py:162
  39.5 5.4 %collective-permute-start.9 = (bf16[2,32,1280]{2,1,0:T(8,128)(2,1)S(1)}, bf16[2,32,1280]{2,1,0:T(8,128)(2,1)S(1)}, u32[]{:S(2)}, u32[]{:S(2)}) collective-permute-start(bf16[2,32,1280]{2,1,0:T(8,128)(2,1)S(1)} %add_convert_fusion), channel_id=1, source_target_pairs={{0,2},{1,3},{2,0},{3,1},{4,6},{5,7},{6,4},{7,5},{8,10},{9,11},{10,... | collective-permute-start | bytes 491528 | tf_op jit(solution)/shard_map/ppermute | solution.py:162
  41.1 9.5 %collective-permute-start.16 = (bf16[16,1024]{1,0:T(8,128)(2,1)S(1)}, bf16[16,1024]{1,0:T(8,128)(2,1)S(1)}, u32[]{:S(2)}, u32[]{:S(2)}) collective-permute-start(bf16[16,1024]{1,0:T(8,128)(2,1)S(1)} %get-tuple-element.48), channel_id=1, source_target_pairs={{0,16},{16,0},{1,17},{17,1},{2,18},{18,2},{3,19},{19,3},{4,20},{20... | collective-permute-start | bytes 98312 | tf_op jit(solution)/shard_map/ppermute | solution.py:162
  45.1 4.1 %collective-permute-start.10 = (bf16[16,1280]{1,0:T(8,128)(2,1)S(1)}, bf16[16,1280]{1,0:T(8,128)(2,1)S(1)}, u32[]{:S(2)}, u32[]{:S(2)}) collective-permute-start(bf16[16,1280]{1,0:T(8,128)(2,1)S(1)} %get-tuple-element.44), channel_id=1, source_target_pairs={{0,16},{16,0},{1,17},{17,1},{2,18},{18,2},{3,19},{19,3},{4,20},{20... | collective-permute-start | bytes 122888 | tf_op jit(solution)/shard_map/ppermute | solution.py:162
  45.9 5.3 %collective-permute-start.22 = (bf16[32,1024]{1,0:T(8,128)(2,1)S(1)}, bf16[32,1024]{1,0:T(8,128)(2,1)S(1)}, u32[]{:S(2)}, u32[]{:S(2)}) collective-permute-start(bf16[32,1024]{1,0:T(8,128)(2,1)S(1)} %pad_maximum_fusion.2.refs_0_), channel_id=1, source_target_pairs={{0,2},{1,3},{2,0},{3,1},{4,6},{5,7},{6,4},{7,5},{8,10},{9,11},{10,... | collective-permute-start | bytes 196616 | tf_op jit(solution)/shard_map/ppermute | solution.py:162
  49.1 6.3 %collective-permute-start.11 = (bf16[32,1280]{1,0:T(8,128)(2,1)S(1)}, bf16[32,1280]{1,0:T(8,128)(2,1)S(1)}, u32[]{:S(2)}, u32[]{:S(2)}) collective-permute-start(bf16[32,1280]{1,0:T(8,128)(2,1)S(1)} %pad_maximum_fusion.refs_0_), channel_id=1, source_target_pairs={{0,2},{1,3},{2,0},{3,1},{4,6},{5,7},{6,4},{7,5},{8,10},{9,11},{10,... | collective-permute-start | bytes 245768 | tf_op jit(solution)/shard_map/ppermute | solution.py:162
  50.6 4.3 %collective-permute-start.17 = (bf16[32,1024]{1,0:T(8,128)(2,1)S(1)}, bf16[32,1024]{1,0:T(8,128)(2,1)S(1)}, u32[]{:S(2)}, u32[]{:S(2)}) collective-permute-start(bf16[32,1024]{1,0:T(8,128)(2,1)S(1)} %pad_maximum_fusion.1.refs_0_), channel_id=1, source_target_pairs={{0,2},{1,3},{2,0},{3,1},{4,6},{5,7},{6,4},{7,5},{8,10},{9,11},{10,... | collective-permute-start | bytes 196616 | tf_op jit(solution)/shard_map/ppermute | solution.py:162
  51.2 3.7 %collective-permute-start.23 = (bf16[32,1024]{1,0:T(8,128)(2,1)S(1)}, bf16[32,1024]{1,0:T(8,128)(2,1)S(1)}, u32[]{:S(2)}, u32[]{:S(2)}) collective-permute-start(bf16[32,1024]{1,0:T(8,128)(2,1)S(1)} %pad_maximum_fusion.2.refs_0_), channel_id=1, source_target_pairs={{0,1},{1,0},{2,3},{3,2},{4,5},{5,4},{6,7},{7,6},{8,9},{9,8},{10,11... | collective-permute-start | bytes 196616 | tf_op jit(solution)/shard_map/ppermute | solution.py:162
  51.2 4.3 %collective-permute-start.24 = (bf16[32,1024]{1,0:T(8,128)(2,1)S(1)}, bf16[32,1024]{1,0:T(8,128)(2,1)S(1)}, u32[]{:S(2)}, u32[]{:S(2)}) collective-permute-start(bf16[32,1024]{1,0:T(8,128)(2,1)S(1)} %collective-permute-done.22.refs_1_), channel_id=1, source_target_pairs={{0,1},{1,0},{2,3},{3,2},{4,5},{5,4},{6,7},{7,6},{8,9},{9,8},{10,11... | collective-permute-start | bytes 196616 | tf_op jit(solution)/shard_map/ppermute | solution.py:162
  51.8 6.0 %collective-permute-start.18 = (bf16[32,1024]{1,0:T(8,128)(2,1)S(1)}, bf16[32,1024]{1,0:T(8,128)(2,1)S(1)}, u32[]{:S(2)}, u32[]{:S(2)}) collective-permute-start(bf16[32,1024]{1,0:T(8,128)(2,1)S(1)} %pad_maximum_fusion.1.refs_0_), channel_id=1, source_target_pairs={{0,1},{1,0},{2,3},{3,2},{4,5},{5,4},{6,7},{7,6},{8,9},{9,8},{10,11... | collective-permute-start | bytes 196616 | tf_op jit(solution)/shard_map/ppermute | solution.py:162
  55.0 2.8 %collective-permute-start.19 = (bf16[32,1024]{1,0:T(8,128)(2,1)S(1)}, bf16[32,1024]{1,0:T(8,128)(2,1)S(1)}, u32[]{:S(2)}, u32[]{:S(2)}) collective-permute-start(bf16[32,1024]{1,0:T(8,128)(2,1)S(1)} %collective-permute-done.17.refs_1_), channel_id=1, source_target_pairs={{0,1},{1,0},{2,3},{3,2},{4,5},{5,4},{6,7},{7,6},{8,9},{9,8},{10,11... | collective-permute-start | bytes 196616 | tf_op jit(solution)/shard_map/ppermute | solution.py:162
  55.0 4.9 %collective-permute-start.12 = (bf16[32,1280]{1,0:T(8,128)(2,1)S(1)}, bf16[32,1280]{1,0:T(8,128)(2,1)S(1)}, u32[]{:S(2)}, u32[]{:S(2)}) collective-permute-start(bf16[32,1280]{1,0:T(8,128)(2,1)S(1)} %pad_maximum_fusion.refs_0_), channel_id=1, source_target_pairs={{0,1},{1,0},{2,3},{3,2},{4,5},{5,4},{6,7},{7,6},{8,9},{9,8},{10,11... | collective-permute-start | bytes 245768 | tf_op jit(solution)/shard_map/ppermute | solution.py:162
  55.5 4.4 %collective-permute-start.13 = (bf16[32,1280]{1,0:T(8,128)(2,1)S(1)}, bf16[32,1280]{1,0:T(8,128)(2,1)S(1)}, u32[]{:S(2)}, u32[]{:S(2)}) collective-permute-start(bf16[32,1280]{1,0:T(8,128)(2,1)S(1)} %collective-permute-done.11.refs_1_), channel_id=1, source_target_pairs={{0,1},{1,0},{2,3},{3,2},{4,5},{5,4},{6,7},{7,6},{8,9},{9,8},{10,11... | collective-permute-start | bytes 245768 | tf_op jit(solution)/shard_map/ppermute | solution.py:162
  62.4 6.8 %collective-permute-start.25 = (bf16[16,2048]{1,0:T(8,128)(2,1)S(1)}, bf16[16,2048]{1,0:T(8,128)(2,1)S(1)}, u32[]{:S(2)}, u32[]{:S(2)}) collective-permute-start(bf16[16,2048]{1,0:T(8,128)(2,1)S(1)} %get-tuple-element.40), channel_id=1, source_target_pairs={{0,12},{4,8},{8,4},{12,0},{1,13},{5,9},{9,5},{13,1},{2,14},{6,10},... | collective-permute-start | bytes 196616 | tf_op jit(solution)/shard_map/ppermute | solution.py:162
  66.1 5.8 %collective-permute-start.26 = (bf16[16,2048]{1,0:T(8,128)(2,1)S(1)}, bf16[16,2048]{1,0:T(8,128)(2,1)S(1)}, u32[]{:S(2)}, u32[]{:S(2)}) collective-permute-start(bf16[16,2048]{1,0:T(8,128)(2,1)S(1)} %get-tuple-element.41), channel_id=1, source_target_pairs={{0,8},{4,12},{8,0},{12,4},{1,9},{5,13},{9,1},{13,5},{2,10},{6,14},... | collective-permute-start | bytes 196616 | tf_op jit(solution)/shard_map/ppermute | solution.py:162
  66.1 5.8 %collective-permute-start.27 = (bf16[16,2048]{1,0:T(8,128)(2,1)S(1)}, bf16[16,2048]{1,0:T(8,128)(2,1)S(1)}, u32[]{:S(2)}, u32[]{:S(2)}) collective-permute-start(bf16[16,2048]{1,0:T(8,128)(2,1)S(1)} %get-tuple-element.42), channel_id=1, source_target_pairs={{0,4},{4,0},{8,12},{12,8},{1,5},{5,1},{9,13},{13,9},{2,6},{6,2},{1... | collective-permute-start | bytes 196616 | tf_op jit(solution)/shard_map/ppermute | solution.py:162

commit v4 on v3

--- a/solution.py
+++ b/solution.py
@@ -47,15 +47,18 @@
 
 
 def fetch_kernel(first, width, where, *refs):
-    n = len(refs) // 2
-    sources, outs, sems = refs[:n], refs[n : 2 * n], refs[-1]
+    n = len(refs) // 2 - 1
+    sources, outs, flag, sems = refs[:n], refs[n : 2 * n], refs[-2], refs[-1]
     start = pl.multiple_of(where[0] + first, TILE)
     copies = []
     for source, out in zip(sources, outs):
-        if source.shape != out.shape:
-            source = source.at[:, pl.ds(start, width)]
-        copies.append(pltpu.make_async_copy(source, out, sems.at[len(copies)]))
-        copies[-1].start()
+        step = out.shape[0] if source.shape == out.shape else TILE
+        for at in range(0, out.shape[0], step):
+            rows = slice(at, at + step)
+            part = source if source.shape == out.shape else source.at[rows, pl.ds(start, width)]
+            copies.append(pltpu.make_async_copy(part, out.at[rows, :], sems.at[len(copies)]))
+            copies[-1].start()
+    flag[...] = jnp.zeros_like(flag)
     for copy in copies:
         copy.wait()
 
@@ -63,12 +66,13 @@
 def fetch(where, arrays, first, width):
     shapes = [a.shape if a.shape[0] == ROWS else (a.shape[0], width) for a in arrays]
     size = sum(2 * x * y for x, y in shapes)
+    n = len(arrays)
     return pl.pallas_call(
         functools.partial(fetch_kernel, first, width),
-        in_specs=[spec(pltpu.SMEM)] + [spec(pltpu.HBM)] * len(arrays),
-        out_specs=[spec(pltpu.VMEM)] * len(arrays),
-        out_shape=[pltpu.VMEM(x, jnp.bfloat16) for x in shapes],
-        scratch_shapes=[pltpu.SemaphoreType.DMA((len(arrays),))],
+        in_specs=[spec(pltpu.SMEM)] + [spec(pltpu.HBM)] * n,
+        out_specs=[spec(pltpu.VMEM)] * (n + 1),
+        out_shape=[pltpu.VMEM(x, jnp.bfloat16) for x in shapes] + [pltpu.VMEM((8, 128), jnp.float32)],
+        scratch_shapes=[pltpu.SemaphoreType.DMA((sum(-(-x // TILE) for x, _ in shapes),))],
         compiler_params=params(1),
         cost_estimate=pl.CostEstimate(flops=0, bytes_accessed=size, transcendentals=0),
         name="fetch",
@@ -76,7 +80,7 @@
 
 
 def gate_up_kernel(n_blocks, where, *refs):
-    blocks, (gate_ref, up_ref, mine_ref, theirs_ref, x_ref) = refs[:n_blocks], refs[n_blocks:]
+    blocks, (gate_ref, up_ref), (mine_ref, theirs_ref, x_ref) = refs[:n_blocks], refs[n_blocks:][:2], refs[-3:]
     for b in range(n_blocks):
         at = place(where[1], b % 4) * 2 + b // 4
         x_ref[pl.ds(pl.multiple_of(at * ROWS, ROWS), ROWS), :] = blocks[b][...]
@@ -88,13 +92,13 @@
             theirs_ref[k, :, a:b] = part[half:]
 
 
-def gate_up(where, blocks, gate, up):
+def gate_up(where, blocks, gate, up, behind):
     depth, width = gate.shape
     n = len(blocks)
     total = n * ROWS
     return pl.pallas_call(
         functools.partial(gate_up_kernel, n),
-        in_specs=[spec(pltpu.SMEM)] + [spec(pltpu.VMEM)] * (n + 2),
+        in_specs=[spec(pltpu.SMEM)] + [spec(pltpu.VMEM)] * (n + 2) + [spec(pl.ANY)] * len(behind),
         out_specs=[spec(pltpu.VMEM)] * 2,
         scratch_shapes=[pltpu.VMEM((total, depth), jnp.bfloat16)],
         out_shape=[jax.ShapeDtypeStruct((2, total // 2, width), jnp.bfloat16)] * 2,
@@ -103,7 +107,7 @@
             flops=4 * total * depth * width, bytes_accessed=4 * depth * width, transcendentals=0
         ),
         name="gate_up",
-    )(where, *blocks, gate, up)
+    )(where, *blocks, gate, up, *behind)
 
 
 def down_kernel(n_pieces, has_acc, last, first, half, where, *refs):
@@ -170,9 +174,8 @@
     own_tokens = weights[0][2]
     down_weight = pltpu.with_memory_space_constraint(down_weight, pltpu.VMEM)
 
-    far = swap(tokens, "hid", 2)
-    near = [tokens, swap(tokens, "hid", 1), far, swap(far, "hid", 1)]
-    blocks = [own_tokens] + near[1:] + [swap(x, "rep", 1) for x in near]
+    near = [swap(tokens, "hid", d) for d in (3, 2, 1)] + [own_tokens]
+    blocks = near[::-1] + [swap(x, "rep", 1) for x in near[::-1]]
 
     quarter = 2 * ROWS
     parts, to_chips = [], []
@@ -181,12 +184,14 @@
         mine, got = parts[c]
         to_chips.append((mine[:, quarter:].astype(f32) + got[:, quarter:].astype(f32)).astype(bf16))
 
-    turn = where
+    behind = [w[-1] for w in weights[1:]]
     for c in range(CHUNKS):
         if c >= 2:
             send_to_chip(c - 2)
-            turn, to_chips[-1] = lax.optimization_barrier((turn, to_chips[-1]))
-        mine, theirs = gate_up(turn, blocks, *weights[c][:2])
+            behind = [to_chips[-1]]
+        elif c == 1:
+            behind = [parts[0][0]]
+        mine, theirs = gate_up(where, blocks, *weights[c][:2], behind)
         parts.append((mine, swap(theirs, "wid", 1)))
     while len(to_chips) < CHUNKS:
         send_to_chip(len(to_chips))

time: 72.7 us -> 71.4 us (0.982)
  waiting for transfers between devices: 17.5 us -> 15.4 us
  Pallas kernels: 25.6 us -> 26.4 us
    ppermute x28, waiting for transfers between devices: 17.5 us -> 15.4 us  [swap(): return lax.ppermute(x, axis, [(i, i ^ step) for i in range(n)])]
    pallas_call x3, Pallas kernels: 13 us -> 13.8 us  [fetch(): pl.pallas_call(functools.partial(fetch_kernel, first, width), in_specs=[s...]
  transfers between devices with their start and end apart: 28 -> 28, of which waited for: 8 -> 9; matrix products, arithmetic and copies ran while one was open for 1% -> 1% of each run, Pallas kernels for 29% -> 28%
where the time goes in v4:
time: 71.4 us; the launch traced here: 71.3 us
  starting transfers between devices  27.9 us (39%)
  Pallas kernels  26.4 us (37%)
  waiting for transfers between devices  15.4 us (22%)
  other arithmetic  1.17 us (2%)
    ppermute x28, starting transfers between devices, swap(): return lax.ppermute(x, axis, [(i, i ^ step) for i in range(n)])  27.9 us
    ppermute x28, waiting for transfers between devices, swap(): return lax.ppermute(x, axis, [(i, i ^ step) for i in range(n)])  15.4 us
    pallas_call x3, Pallas kernels, fetch(): pl.pallas_call(functools.partial(fetch_kernel, first, width), in_specs=[s...  13.8 us
    pallas_call x3, Pallas kernels, down(): pl.pallas_call(functools.partial(down_kernel, n, prev is not None, last,...  6.73 us
    pallas_call x3, Pallas kernels, gate_up(): pl.pallas_call(functools.partial(gate_up_kernel, n), in_specs=[spec(pltpu...  5.86 us
  transfers between devices with their start and end apart: 28, of which 9 were waited for; matrix products, arithmetic and copies ran while one was open for 1% of the time, Pallas kernels for 28%

profile of v4, /device:TPU:0, one launch (start us, length us, event | category | flops | bytes accessed | tf_op | source)
XLA Modules:
  0.0 71.3 jit_solution(6461999213630460274)
XLA Ops:
  0.0 3.0 %collective-permute-start = (bf16[16,2048]{1,0:T(8,128)(2,1)}, bf16[16,2048]{1,0:T(8,128)(2,1)S(1)}, u32[]{:S(2)}, u32[]{:S(2)}) collective-permute-start(bf16[16,2048]{1,0:T(8,128)(2,1)} %refs_2_.1), channel_id=1, source_target_pairs={{0,4},{4,0},{8,12},{12,8},{1,5},{5,1},{9,13},{13,9},{2,6},{6,2},{1... | collective-permute-start | bytes 196616 | tf_op jit(solution)/shard_map/ppermute | solution.py:166
  3.0 2.5 %collective-permute-start.2 = (bf16[16,2048]{1,0:T(8,128)(2,1)}, bf16[16,2048]{1,0:T(8,128)(2,1)S(1)}, u32[]{:S(2)}, u32[]{:S(2)}) collective-permute-start(bf16[16,2048]{1,0:T(8,128)(2,1)} %refs_2_.1), channel_id=1, source_target_pairs={{0,12},{4,8},{8,4},{12,0},{1,13},{5,9},{9,5},{13,1},{2,14},{6,10},... | collective-permute-start | bytes 196616 | tf_op jit(solution)/shard_map/ppermute | solution.py:166
  5.5 0.1 collective-permute-start.1
  5.6 0.1 pad_add_fusion.where
  5.7 4.7 %fetch.3 = (bf16[2048,1024]{1,0:T(8,128)(2,1)S(1)}, bf16[2048,1024]{1,0:T(8,128)(2,1)S(1)}, bf16[16,2048]{1,0:T(8,128)(2,1)S(1)}, f32[8,128]{1,0:T(8,128)}) custom-call(s32[2]{0:T(128)S(1)} %pad_add_fusion.where, bf16[2048,6656]{1,0:T(8,128)(2,1)} %refs_0_.5, bf16[2048,6656]{1,0:T(8,128)(2,1)} %refs_1_.5, bf16[16,2048]{1,0:T(8,128)(2,1)} %refs_2_.1), custom_call_target="tpu_custom_call" | custom-call | bytes 8454144 | tf_op jit(solution)/shard_map/fetch/pallas_call | solution.py:70
  10.4 1.6 %collective-permute-start.3 = (bf16[16,2048]{1,0:T(8,128)(2,1)S(1)}, bf16[16,2048]{1,0:T(8,128)(2,1)S(1)}, u32[]{:S(2)}, u32[]{:S(2)}) collective-permute-start(bf16[16,2048]{1,0:T(8,128)(2,1)S(1)} %get-tuple-element.24.refs_0_), channel_id=1, source_target_pairs={{0,16},{16,0},{1,17},{17,1},{2,18},{18,2},{3,19},{19,3},{4,20},{20... | collective-permute-start | bytes 196616 | tf_op jit(solution)/shard_map/ppermute | solution.py:166
  12.0 0.5 collective-permute-start.4
  12.5 1.5 %collective-permute-start.6 = (bf16[16,2048]{1,0:T(8,128)(2,1)S(1)}, bf16[16,2048]{1,0:T(8,128)(2,1)S(1)}, u32[]{:S(2)}, u32[]{:S(2)}) collective-permute-start(bf16[16,2048]{1,0:T(8,128)(2,1)S(1)} %collective-permute-done.2.refs_3_), channel_id=1, source_target_pairs={{0,16},{16,0},{1,17},{17,1},{2,18},{18,2},{3,19},{19,3},{4,20},{20... | collective-permute-start | bytes 196616 | tf_op jit(solution)/shard_map/ppermute | solution.py:166
  14.0 0.5 collective-permute-start.5
  14.5 4.1 %fetch.5 = (bf16[2048,1024]{1,0:T(8,128)(2,1)S(1)}, bf16[2048,1024]{1,0:T(8,128)(2,1)S(1)}, f32[8,128]{1,0:T(8,128)S(1)}) custom-call(s32[2]{0:T(128)S(1)} %pad_add_fusion.where, bf16[2048,6656]{1,0:T(8,128)(2,1)} %refs_0_.5, bf16[2048,6656]{1,0:T(8,128)(2,1)} %refs_1_.5), custom_call_target="tpu_custom_call" | custom-call | bytes 8388608 | tf_op jit(solution)/shard_map/fetch/pallas_call | solution.py:70
  18.7 5.0 %fetch.4 = (bf16[2048,1280]{1,0:T(8,128)(2,1)S(1)}, bf16[2048,1280]{1,0:T(8,128)(2,1)S(1)}, f32[8,128]{1,0:T(8,128)S(1)}) custom-call(s32[2]{0:T(128)S(1)} %pad_add_fusion.where, bf16[2048,6656]{1,0:T(8,128)(2,1)} %refs_0_.5, bf16[2048,6656]{1,0:T(8,128)(2,1)} %refs_1_.5), custom_call_target="tpu_custom_call" | custom-call | bytes 10485760 | tf_op jit(solution)/shard_map/fetch/pallas_call | solution.py:70
  23.7 1.9 %gate_up.3 = (bf16[2,64,1024]{2,1,0:T(8,128)(2,1)S(1)}, bf16[2,64,1024]{2,1,0:T(8,128)(2,1)S(1)}) custom-call(s32[2]{0:T(128)S(1)} %pad_add_fusion.where, bf16[16,2048]{1,0:T(8,128)(2,1)S(1)} %get-tuple-element.24.refs_0_, bf16[16,2048]{1,0:T(8,128)(2,1)S(1)} %collective-permute-done.refs_1_, bf16[16,2048]{1,0:T(8,128)(2,1)S(1)} %collective-permute-done.1.refs_2_, ...), custom_call_target="tpu_custom_call" | custom-call | flops 1073741824 | bytes 8388608 | tf_op jit(solution)/shard_map/gate_up/pallas_call | solution.py:99
  25.6 1.9 %gate_up.5 = (bf16[2,64,1024]{2,1,0:T(8,128)(2,1)S(1)}, bf16[2,64,1024]{2,1,0:T(8,128)(2,1)S(1)}) custom-call(s32[2]{0:T(128)S(1)} %pad_add_fusion.where, bf16[16,2048]{1,0:T(8,128)(2,1)S(1)} %get-tuple-element.24.refs_0_, bf16[16,2048]{1,0:T(8,128)(2,1)S(1)} %collective-permute-done.refs_1_, bf16[16,2048]{1,0:T(8,128)(2,1)S(1)} %collective-permute-done.1.refs_2_, ...), custom_call_target="tpu_custom_call" | custom-call | flops 1073741824 | bytes 8388608 | tf_op jit(solution)/shard_map/gate_up/pallas_call | solution.py:99
  27.4 0.1 collective-permute-start.14
  27.5 0.5 collective-permute-start.7
  28.0 1.0 %collective-permute-done.14 = bf16[2,64,1024]{2,1,0:T(8,128)(2,1)S(1)} collective-permute-done((bf16[2,64,1024]{2,1,0:T(8,128)(2,1)S(1)}, bf16[2,64,1024]{2,1,0:T(8,128)(2,1)S(1)}, u32[]{:S(2)}, u32[]{:S(2)}) %collective-permute-start.14) | collective-permute-done | bytes 262176 | tf_op jit(solution)/shard_map/ppermute | solution.py:166
  29.1 1.6 %collective-permute-start.15 = (bf16[2,32,1024]{2,1,0:T(8,128)(2,1)S(1)}, bf16[2,32,1024]{2,1,0:T(8,128)(2,1)S(1)}, u32[]{:S(2)}, u32[]{:S(2)}) collective-permute-start(bf16[2,32,1024]{2,1,0:T(8,128)(2,1)S(1)} %add_convert_fusion.1), channel_id=1, source_target_pairs={{0,2},{1,3},{2,0},{3,1},{4,6},{5,7},{6,4},{7,5},{8,10},{9,11},{10,... | collective-permute-start | bytes 393224 | tf_op jit(solution)/shard_map/ppermute | solution.py:166
  30.7 0.6 collective-permute-start.20
  31.3 2.2 %gate_up.4 = (bf16[2,64,1280]{2,1,0:T(8,128)(2,1)S(1)}, bf16[2,64,1280]{2,1,0:T(8,128)(2,1)S(1)}) custom-call(s32[2]{0:T(128)S(1)} %pad_add_fusion.where, bf16[16,2048]{1,0:T(8,128)(2,1)S(1)} %get-tuple-element.24.refs_0_, bf16[16,2048]{1,0:T(8,128)(2,1)S(1)} %collective-permute-done.refs_1_, bf16[16,2048]{1,0:T(8,128)(2,1)S(1)} %collective-permute-done.1.refs_2_, ...), custom_call_target="tpu_custom_call" | custom-call | flops 1342177280 | bytes 10485760 | tf_op jit(solution)/shard_map/gate_up/pallas_call | solution.py:99
  33.5 0.1 collective-permute-start.8
  33.5 2.0 %collective-permute-done.15 = bf16[2,32,1024]{2,1,0:T(8,128)(2,1)S(1)} collective-permute-done((bf16[2,32,1024]{2,1,0:T(8,128)(2,1)S(1)}, bf16[2,32,1024]{2,1,0:T(8,128)(2,1)S(1)}, u32[]{:S(2)}, u32[]{:S(2)}) %collective-permute-start.15) | collective-permute-done | bytes 131104 | tf_op jit(solution)/shard_map/ppermute | solution.py:166
  35.6 1.6 %collective-permute-start.16 = (bf16[16,1024]{1,0:T(8,128)(2,1)S(1)}, bf16[16,1024]{1,0:T(8,128)(2,1)S(1)}, u32[]{:S(2)}, u32[]{:S(2)}) collective-permute-start(bf16[16,1024]{1,0:T(8,128)(2,1)S(1)} %get-tuple-element.48), channel_id=1, source_target_pairs={{0,16},{16,0},{1,17},{17,1},{2,18},{18,2},{3,19},{19,3},{4,20},{20... | collective-permute-start | bytes 98312 | tf_op jit(solution)/shard_map/ppermute | solution.py:166
  37.2 0.3 collective-permute-done.20
  37.7 1.6 %collective-permute-start.9 = (bf16[2,32,1280]{2,1,0:T(8,128)(2,1)S(1)}, bf16[2,32,1280]{2,1,0:T(8,128)(2,1)S(1)}, u32[]{:S(2)}, u32[]{:S(2)}) collective-permute-start(bf16[2,32,1280]{2,1,0:T(8,128)(2,1)S(1)} %add_convert_fusion), channel_id=1, source_target_pairs={{0,2},{1,3},{2,0},{3,1},{4,6},{5,7},{6,4},{7,5},{8,10},{9,11},{10,... | collective-permute-start | bytes 491528 | tf_op jit(solution)/shard_map/ppermute | solution.py:166
  39.2 1.5 %collective-permute-start.21 = (bf16[16,1024]{1,0:T(8,128)(2,1)S(1)}, bf16[16,1024]{1,0:T(8,128)(2,1)S(1)}, u32[]{:S(2)}, u32[]{:S(2)}) collective-permute-start(bf16[16,1024]{1,0:T(8,128)(2,1)S(1)} %get-tuple-element.46), channel_id=1, source_target_pairs={{0,16},{16,0},{1,17},{17,1},{2,18},{18,2},{3,19},{19,3},{4,20},{20... | collective-permute-start | bytes 98312 | tf_op jit(solution)/shard_map/ppermute | solution.py:166
  40.7 2.4 %collective-permute-done.9 = bf16[2,32,1280]{2,1,0:T(8,128)(2,1)S(1)} collective-permute-done((bf16[2,32,1280]{2,1,0:T(8,128)(2,1)S(1)}, bf16[2,32,1280]{2,1,0:T(8,128)(2,1)S(1)}, u32[]{:S(2)}, u32[]{:S(2)}) %collective-permute-start.9) | collective-permute-done | bytes 163872 | tf_op jit(solution)/shard_map/ppermute | solution.py:166
  43.1 0.1 convert_add_fusion
  43.2 0.1 fusion.1
  43.3 1.6 %collective-permute-start.10 = (bf16[16,1280]{1,0:T(8,128)(2,1)S(1)}, bf16[16,1280]{1,0:T(8,128)(2,1)S(1)}, u32[]{:S(2)}, u32[]{:S(2)}) collective-permute-start(bf16[16,1280]{1,0:T(8,128)(2,1)S(1)} %get-tuple-element.44), channel_id=1, source_target_pairs={{0,16},{16,0},{1,17},{17,1},{2,18},{18,2},{3,19},{19,3},{4,20},{20... | collective-permute-start | bytes 122888 | tf_op jit(solution)/shard_map/ppermute | solution.py:166
  44.9 1.6 %collective-permute-start.22 = (bf16[32,1024]{1,0:T(8,128)(2,1)S(1)}, bf16[32,1024]{1,0:T(8,128)(2,1)S(1)}, u32[]{:S(2)}, u32[]{:S(2)}) collective-permute-start(bf16[32,1024]{1,0:T(8,128)(2,1)S(1)} %pad_maximum_fusion.2.refs_0_), channel_id=1, source_target_pairs={{0,2},{1,3},{2,0},{3,1},{4,6},{5,7},{6,4},{7,5},{8,10},{9,11},{10,... | collective-permute-start | bytes 196616 | tf_op jit(solution)/shard_map/ppermute | solution.py:166
  46.4 0.9 %collective-permute-done.10 = bf16[16,1280]{1,0:T(8,128)(2,1)S(1)} collective-permute-done((bf16[16,1280]{1,0:T(8,128)(2,1)S(1)}, bf16[16,1280]{1,0:T(8,128)(2,1)S(1)}, u32[]{:S(2)}, u32[]{:S(2)}) %collective-permute-start.10) | collective-permute-done | bytes 40992 | tf_op jit(solution)/shard_map/ppermute | solution.py:166
  47.4 1.5 %collective-permute-start.11 = (bf16[32,1280]{1,0:T(8,128)(2,1)S(1)}, bf16[32,1280]{1,0:T(8,128)(2,1)S(1)}, u32[]{:S(2)}, u32[]{:S(2)}) collective-permute-start(bf16[32,1280]{1,0:T(8,128)(2,1)S(1)} %pad_maximum_fusion.refs_0_), channel_id=1, source_target_pairs={{0,2},{1,3},{2,0},{3,1},{4,6},{5,7},{6,4},{7,5},{8,10},{9,11},{10,... | collective-permute-start | bytes 245768 | tf_op jit(solution)/shard_map/ppermute | solution.py:166
  48.9 0.6 collective-permute-start.17
  49.5 0.4 collective-permute-done.22.refs_1_
  49.9 0.1 collective-permute-start.24
  50.0 0.4 collective-permute-start.18
  50.4 2.8 %collective-permute-done.17.refs_1_ = bf16[32,1024]{1,0:T(8,128)(2,1)S(1)} collective-permute-done((bf16[32,1024]{1,0:T(8,128)(2,1)S(1)}, bf16[32,1024]{1,0:T(8,128)(2,1)S(1)}, u32[]{:S(2)}, u32[]{:S(2)}) %collective-permute-start.17) | collective-permute-done | bytes 65568 | tf_op jit(solution)/shard_map/ppermute | solution.py:166
  53.2 0.5 collective-permute-start.12
  53.7 0.1 collective-permute-start.13
  53.9 2.1 %down.3.refs_5_ = f32[64,2048]{1,0:T(8,128)S(1)} custom-call(s32[2]{0:T(128)S(1)} %pad_add_fusion.where, bf16[32,1024]{1,0:T(8,128)(2,1)S(1)} %pad_maximum_fusion.2.refs_0_, bf16[32,1024]{1,0:T(8,128)(2,1)S(1)} %collective-permute-done.22.refs_1_, bf16[32,1024]{1,0:T(8,128)(2,1)S(1)} %collective-permute-done.23.refs_2_, ...), custom_call_target="tpu_custom_call" | custom-call | flops 536870912 | bytes 8388608 | tf_op jit(solution)/shard_map/down/pallas_call | solution.py:144
  56.0 2.1 %down.4.refs_5_ = f32[64,2048]{1,0:T(8,128)S(1)} custom-call(s32[2]{0:T(128)S(1)} %pad_add_fusion.where, bf16[32,1024]{1,0:T(8,128)(2,1)S(1)} %pad_maximum_fusion.1.refs_0_, bf16[32,1024]{1,0:T(8,128)(2,1)S(1)} %collective-permute-done.17.refs_1_, bf16[32,1024]{1,0:T(8,128)(2,1)S(1)} %collective-permute-done.18.refs_2_, ...), custom_call_target="tpu_custom_call" | custom-call | flops 536870912 | bytes 8388608 | tf_op jit(solution)/shard_map/down/pallas_call | solution.py:144
  58.1 2.5 %down.5 = (bf16[16,2048]{1,0:T(8,128)(2,1)S(1)}, bf16[16,2048]{1,0:T(8,128)(2,1)S(1)}, bf16[16,2048]{1,0:T(8,128)(2,1)S(1)}, bf16[16,2048]{1,0:T(8,128)(2,1)S(1)}) custom-call(s32[2]{0:T(128)S(1)} %pad_add_fusion.where, bf16[32,1280]{1,0:T(8,128)(2,1)S(1)} %pad_maximum_fusion.refs_0_, bf16[32,1280]{1,0:T(8,128)(2,1)S(1)} %collective-permute-done.11.refs_1_, ...), custom_call_target="tpu_custom_call" | custom-call | flops 671088640 | bytes 10485760 | tf_op jit(solution)/shard_map/down/pallas_call | solution.py:144
  60.6 3.0 %collective-permute-start.25 = (bf16[16,2048]{1,0:T(8,128)(2,1)S(1)}, bf16[16,2048]{1,0:T(8,128)(2,1)S(1)}, u32[]{:S(2)}, u32[]{:S(2)}) collective-permute-start(bf16[16,2048]{1,0:T(8,128)(2,1)S(1)} %get-tuple-element.40), channel_id=1, source_target_pairs={{0,12},{4,8},{8,4},{12,0},{1,13},{5,9},{9,5},{13,1},{2,14},{6,10},... | collective-permute-start | bytes 196616 | tf_op jit(solution)/shard_map/ppermute | solution.py:166
  63.6 0.3 collective-permute-start.26
  64.0 1.1 %collective-permute-start.27 = (bf16[16,2048]{1,0:T(8,128)(2,1)S(1)}, bf16[16,2048]{1,0:T(8,128)(2,1)S(1)}, u32[]{:S(2)}, u32[]{:S(2)}) collective-permute-start(bf16[16,2048]{1,0:T(8,128)(2,1)S(1)} %get-tuple-element.42), channel_id=1, source_target_pairs={{0,4},{4,0},{8,12},{12,8},{1,5},{5,1},{9,13},{13,9},{2,6},{6,2},{1... | collective-permute-start | bytes 196616 | tf_op jit(solution)/shard_map/ppermute | solution.py:166
  65.1 2.0 %collective-permute-done.25 = bf16[16,2048]{1,0:T(8,128)(2,1)S(1)} collective-permute-done((bf16[16,2048]{1,0:T(8,128)(2,1)S(1)}, bf16[16,2048]{1,0:T(8,128)(2,1)S(1)}, u32[]{:S(2)}, u32[]{:S(2)}) %collective-permute-start.25) | collective-permute-done | bytes 65568 | tf_op jit(solution)/shard_map/ppermute | solution.py:166
  67.1 3.5 %collective-permute-done.26 = bf16[16,2048]{1,0:T(8,128)(2,1)S(1)} collective-permute-done((bf16[16,2048]{1,0:T(8,128)(2,1)S(1)}, bf16[16,2048]{1,0:T(8,128)(2,1)S(1)}, u32[]{:S(2)}, u32[]{:S(2)}) %collective-permute-start.26) | collective-permute-done | bytes 65568 | tf_op jit(solution)/shard_map/ppermute | solution.py:166
  70.6 0.7 add_convert_fusion.3
  (49 shorter events, 0.4 us)
Async XLA Ops:
  0.0 12.0 %collective-permute-start = (bf16[16,2048]{1,0:T(8,128)(2,1)}, bf16[16,2048]{1,0:T(8,128)(2,1)S(1)}, u32[]{:S(2)}, u32[]{:S(2)}) collective-permute-start(bf16[16,2048]{1,0:T(8,128)(2,1)} %refs_2_.1), channel_id=1, source_target_pairs={{0,4},{4,0},{8,12},{12,8},{1,5},{5,1},{9,13},{13,9},{2,6},{6,2},{1... | collective-permute-start | bytes 196616 | tf_op jit(solution)/shard_map/ppermute | solution.py:166
  3.0 9.5 %collective-permute-start.2 = (bf16[16,2048]{1,0:T(8,128)(2,1)}, bf16[16,2048]{1,0:T(8,128)(2,1)S(1)}, u32[]{:S(2)}, u32[]{:S(2)}) collective-permute-start(bf16[16,2048]{1,0:T(8,128)(2,1)} %refs_2_.1), channel_id=1, source_target_pairs={{0,12},{4,8},{8,4},{12,0},{1,13},{5,9},{9,5},{13,1},{2,14},{6,10},... | collective-permute-start | bytes 196616 | tf_op jit(solution)/shard_map/ppermute | solution.py:166
  5.5 8.5 %collective-permute-start.1 = (bf16[16,2048]{1,0:T(8,128)(2,1)}, bf16[16,2048]{1,0:T(8,128)(2,1)S(1)}, u32[]{:S(2)}, u32[]{:S(2)}) collective-permute-start(bf16[16,2048]{1,0:T(8,128)(2,1)} %refs_2_.1), channel_id=1, source_target_pairs={{0,8},{4,12},{8,0},{12,4},{1,9},{5,13},{9,1},{13,5},{2,10},{6,14},... | collective-permute-start | bytes 196616 | tf_op jit(solution)/shard_map/ppermute | solution.py:166
  10.4 13.3 %collective-permute-start.3 = (bf16[16,2048]{1,0:T(8,128)(2,1)S(1)}, bf16[16,2048]{1,0:T(8,128)(2,1)S(1)}, u32[]{:S(2)}, u32[]{:S(2)}) collective-permute-start(bf16[16,2048]{1,0:T(8,128)(2,1)S(1)} %get-tuple-element.24.refs_0_), channel_id=1, source_target_pairs={{0,16},{16,0},{1,17},{17,1},{2,18},{18,2},{3,19},{19,3},{4,20},{20... | collective-permute-start | bytes 196616 | tf_op jit(solution)/shard_map/ppermute | solution.py:166
  12.0 11.7 %collective-permute-start.4 = (bf16[16,2048]{1,0:T(8,128)(2,1)S(1)}, bf16[16,2048]{1,0:T(8,128)(2,1)S(1)}, u32[]{:S(2)}, u32[]{:S(2)}) collective-permute-start(bf16[16,2048]{1,0:T(8,128)(2,1)S(1)} %collective-permute-done.refs_1_), channel_id=1, source_target_pairs={{0,16},{16,0},{1,17},{17,1},{2,18},{18,2},{3,19},{19,3},{4,20},{20... | collective-permute-start | bytes 196616 | tf_op jit(solution)/shard_map/ppermute | solution.py:166
  12.5 11.2 %collective-permute-start.6 = (bf16[16,2048]{1,0:T(8,128)(2,1)S(1)}, bf16[16,2048]{1,0:T(8,128)(2,1)S(1)}, u32[]{:S(2)}, u32[]{:S(2)}) collective-permute-start(bf16[16,2048]{1,0:T(8,128)(2,1)S(1)} %collective-permute-done.2.refs_3_), channel_id=1, source_target_pairs={{0,16},{16,0},{1,17},{17,1},{2,18},{18,2},{3,19},{19,3},{4,20},{20... | collective-permute-start | bytes 196616 | tf_op jit(solution)/shard_map/ppermute | solution.py:166
  14.0 9.7 %collective-permute-start.5 = (bf16[16,2048]{1,0:T(8,128)(2,1)S(1)}, bf16[16,2048]{1,0:T(8,128)(2,1)S(1)}, u32[]{:S(2)}, u32[]{:S(2)}) collective-permute-start(bf16[16,2048]{1,0:T(8,128)(2,1)S(1)} %collective-permute-done.1.refs_2_), channel_id=1, source_target_pairs={{0,16},{16,0},{1,17},{17,1},{2,18},{18,2},{3,19},{19,3},{4,20},{20... | collective-permute-start | bytes 196616 | tf_op jit(solution)/shard_map/ppermute | solution.py:166
  18.6 35.2 %slice-start = ((s8[27262976]{0:T(1024)(128)(4,1)}), s8[4194304]{0:T(1024)(128)(4,1)S(1)}, s32[]{:S(2)}) async-start(s8[27262976]{0:T(1024)(128)(4,1)} %bitcast.32), calls=%async_computation | async-start | bytes 8388608
  18.6 35.2 %slice-start.1 = ((s8[27262976]{0:T(1024)(128)(4,1)}), s8[4194304]{0:T(1024)(128)(4,1)S(1)}, s32[]{:S(2)}) async-start(s8[27262976]{0:T(1024)(128)(4,1)} %bitcast.32), calls=%async_computation.1 | async-start | bytes 8388608
  18.7 35.1 %slice-start.2 = ((s8[27262976]{0:T(1024)(128)(4,1)}), s8[4194304]{0:T(1024)(128)(4,1)S(1)}, s32[]{:S(2)}) async-start(s8[27262976]{0:T(1024)(128)(4,1)} %bitcast.32), calls=%async_computation.2 | async-start | bytes 8388608
  18.7 35.1 %slice-start.3 = ((s8[27262976]{0:T(1024)(128)(4,1)}), s8[4194304]{0:T(1024)(128)(4,1)S(1)}, s32[]{:S(2)}) async-start(s8[27262976]{0:T(1024)(128)(4,1)} %bitcast.32), calls=%async_computation.3 | async-start | bytes 8388608
  18.7 35.1 %slice-start.4 = ((s8[27262976]{0:T(1024)(128)(4,1)}), s8[4194304]{0:T(1024)(128)(4,1)S(1)}, s32[]{:S(2)}) async-start(s8[27262976]{0:T(1024)(128)(4,1)} %bitcast.32), calls=%async_computation.4 | async-start | bytes 8388608
  25.6 28.3 %slice-start.5 = ((s8[27262976]{0:T(1024)(128)(4,1)}), s8[4194304]{0:T(1024)(128)(4,1)S(1)}, s32[]{:S(2)}) async-start(s8[27262976]{0:T(1024)(128)(4,1)} %bitcast.32), calls=%async_computation.5 | async-start | bytes 8388608
  27.4 1.6 %collective-permute-start.14 = (bf16[2,64,1024]{2,1,0:T(8,128)(2,1)S(1)}, bf16[2,64,1024]{2,1,0:T(8,128)(2,1)S(1)}, u32[]{:S(2)}, u32[]{:S(2)}) collective-permute-start(bf16[2,64,1024]{2,1,0:T(8,128)(2,1)S(1)} %get-tuple-element.38), channel_id=1, source_target_pairs={{0,1},{1,0},{2,3},{3,2},{4,5},{5,4},{6,7},{7,6},{8,9},{9,8},{10,11... | collective-permute-start | bytes 786440 | tf_op jit(solution)/shard_map/ppermute | solution.py:166
  27.5 3.1 %collective-permute-start.7 = (bf16[2,64,1024]{2,1,0:T(8,128)(2,1)S(1)}, bf16[2,64,1024]{2,1,0:T(8,128)(2,1)S(1)}, u32[]{:S(2)}, u32[]{:S(2)}) collective-permute-start(bf16[2,64,1024]{2,1,0:T(8,128)(2,1)S(1)} %get-tuple-element.32), channel_id=1, source_target_pairs={{0,1},{1,0},{2,3},{3,2},{4,5},{5,4},{6,7},{7,6},{8,9},{9,8},{10,11... | collective-permute-start | bytes 786440 | tf_op jit(solution)/shard_map/ppermute | solution.py:166
  29.1 6.4 %collective-permute-start.15 = (bf16[2,32,1024]{2,1,0:T(8,128)(2,1)S(1)}, bf16[2,32,1024]{2,1,0:T(8,128)(2,1)S(1)}, u32[]{:S(2)}, u32[]{:S(2)}) collective-permute-start(bf16[2,32,1024]{2,1,0:T(8,128)(2,1)S(1)} %add_convert_fusion.1), channel_id=1, source_target_pairs={{0,2},{1,3},{2,0},{3,1},{4,6},{5,7},{6,4},{7,5},{8,10},{9,11},{10,... | collective-permute-start | bytes 393224 | tf_op jit(solution)/shard_map/ppermute | solution.py:166
  30.7 6.8 %collective-permute-start.20 = (bf16[2,32,1024]{2,1,0:T(8,128)(2,1)S(1)}, bf16[2,32,1024]{2,1,0:T(8,128)(2,1)S(1)}, u32[]{:S(2)}, u32[]{:S(2)}) collective-permute-start(bf16[2,32,1024]{2,1,0:T(8,128)(2,1)S(1)} %add_convert_fusion.2.refs_10_), channel_id=1, source_target_pairs={{0,2},{1,3},{2,0},{3,1},{4,6},{5,7},{6,4},{7,5},{8,10},{9,11},{10,... | collective-permute-start | bytes 393224 | tf_op jit(solution)/shard_map/ppermute | solution.py:166
  31.3 22.6 %slice-start.6 = ((s8[27262976]{0:T(1024)(128)(4,1)}), s8[2097152]{0:T(1024)(128)(4,1)S(1)}, s32[]{:S(2)}) async-start(s8[27262976]{0:T(1024)(128)(4,1)} %bitcast.32), calls=%async_computation.6 | async-start | bytes 4194304
  33.5 4.2 %collective-permute-start.8 = (bf16[2,64,1280]{2,1,0:T(8,128)(2,1)S(1)}, bf16[2,64,1280]{2,1,0:T(8,128)(2,1)S(1)}, u32[]{:S(2)}, u32[]{:S(2)}) collective-permute-start(bf16[2,64,1280]{2,1,0:T(8,128)(2,1)S(1)} %get-tuple-element.34), channel_id=1, source_target_pairs={{0,1},{1,0},{2,3},{3,2},{4,5},{5,4},{6,7},{7,6},{8,9},{9,8},{10,11... | collective-permute-start | bytes 983048 | tf_op jit(solution)/shard_map/ppermute | solution.py:166
  35.6 13.2 %collective-permute-start.16 = (bf16[16,1024]{1,0:T(8,128)(2,1)S(1)}, bf16[16,1024]{1,0:T(8,128)(2,1)S(1)}, u32[]{:S(2)}, u32[]{:S(2)}) collective-permute-start(bf16[16,1024]{1,0:T(8,128)(2,1)S(1)} %get-tuple-element.48), channel_id=1, source_target_pairs={{0,16},{16,0},{1,17},{17,1},{2,18},{18,2},{3,19},{19,3},{4,20},{20... | collective-permute-start | bytes 98312 | tf_op jit(solution)/shard_map/ppermute | solution.py:166
  37.7 5.5 %collective-permute-start.9 = (bf16[2,32,1280]{2,1,0:T(8,128)(2,1)S(1)}, bf16[2,32,1280]{2,1,0:T(8,128)(2,1)S(1)}, u32[]{:S(2)}, u32[]{:S(2)}) collective-permute-start(bf16[2,32,1280]{2,1,0:T(8,128)(2,1)S(1)} %add_convert_fusion), channel_id=1, source_target_pairs={{0,2},{1,3},{2,0},{3,1},{4,6},{5,7},{6,4},{7,5},{8,10},{9,11},{10,... | collective-permute-start | bytes 491528 | tf_op jit(solution)/shard_map/ppermute | solution.py:166
  39.2 5.6 %collective-permute-start.21 = (bf16[16,1024]{1,0:T(8,128)(2,1)S(1)}, bf16[16,1024]{1,0:T(8,128)(2,1)S(1)}, u32[]{:S(2)}, u32[]{:S(2)}) collective-permute-start(bf16[16,1024]{1,0:T(8,128)(2,1)S(1)} %get-tuple-element.46), channel_id=1, source_target_pairs={{0,16},{16,0},{1,17},{17,1},{2,18},{18,2},{3,19},{19,3},{4,20},{20... | collective-permute-start | bytes 98312 | tf_op jit(solution)/shard_map/ppermute | solution.py:166
  43.3 4.1 %collective-permute-start.10 = (bf16[16,1280]{1,0:T(8,128)(2,1)S(1)}, bf16[16,1280]{1,0:T(8,128)(2,1)S(1)}, u32[]{:S(2)}, u32[]{:S(2)}) collective-permute-start(bf16[16,1280]{1,0:T(8,128)(2,1)S(1)} %get-tuple-element.44), channel_id=1, source_target_pairs={{0,16},{16,0},{1,17},{17,1},{2,18},{18,2},{3,19},{19,3},{4,20},{20... | collective-permute-start | bytes 122888 | tf_op jit(solution)/shard_map/ppermute | solution.py:166
  44.9 5.0 %collective-permute-start.22 = (bf16[32,1024]{1,0:T(8,128)(2,1)S(1)}, bf16[32,1024]{1,0:T(8,128)(2,1)S(1)}, u32[]{:S(2)}, u32[]{:S(2)}) collective-permute-start(bf16[32,1024]{1,0:T(8,128)(2,1)S(1)} %pad_maximum_fusion.2.refs_0_), channel_id=1, source_target_pairs={{0,2},{1,3},{2,0},{3,1},{4,6},{5,7},{6,4},{7,5},{8,10},{9,11},{10,... | collective-permute-start | bytes 196616 | tf_op jit(solution)/shard_map/ppermute | solution.py:166
  47.4 6.4 %collective-permute-start.11 = (bf16[32,1280]{1,0:T(8,128)(2,1)S(1)}, bf16[32,1280]{1,0:T(8,128)(2,1)S(1)}, u32[]{:S(2)}, u32[]{:S(2)}) collective-permute-start(bf16[32,1280]{1,0:T(8,128)(2,1)S(1)} %pad_maximum_fusion.refs_0_), channel_id=1, source_target_pairs={{0,2},{1,3},{2,0},{3,1},{4,6},{5,7},{6,4},{7,5},{8,10},{9,11},{10,... | collective-permute-start | bytes 245768 | tf_op jit(solution)/shard_map/ppermute | solution.py:166
  48.9 4.3 %collective-permute-start.17 = (bf16[32,1024]{1,0:T(8,128)(2,1)S(1)}, bf16[32,1024]{1,0:T(8,128)(2,1)S(1)}, u32[]{:S(2)}, u32[]{:S(2)}) collective-permute-start(bf16[32,1024]{1,0:T(8,128)(2,1)S(1)} %pad_maximum_fusion.1.refs_0_), channel_id=1, source_target_pairs={{0,2},{1,3},{2,0},{3,1},{4,6},{5,7},{6,4},{7,5},{8,10},{9,11},{10,... | collective-permute-start | bytes 196616 | tf_op jit(solution)/shard_map/ppermute | solution.py:166
  49.5 3.7 %collective-permute-start.23 = (bf16[32,1024]{1,0:T(8,128)(2,1)S(1)}, bf16[32,1024]{1,0:T(8,128)(2,1)S(1)}, u32[]{:S(2)}, u32[]{:S(2)}) collective-permute-start(bf16[32,1024]{1,0:T(8,128)(2,1)S(1)} %pad_maximum_fusion.2.refs_0_), channel_id=1, source_target_pairs={{0,1},{1,0},{2,3},{3,2},{4,5},{5,4},{6,7},{7,6},{8,9},{9,8},{10,11... | collective-permute-start | bytes 196616 | tf_op jit(solution)/shard_map/ppermute | solution.py:166
  49.9 3.9 %collective-permute-start.24 = (bf16[32,1024]{1,0:T(8,128)(2,1)S(1)}, bf16[32,1024]{1,0:T(8,128)(2,1)S(1)}, u32[]{:S(2)}, u32[]{:S(2)}) collective-permute-start(bf16[32,1024]{1,0:T(8,128)(2,1)S(1)} %collective-permute-done.22.refs_1_), channel_id=1, source_target_pairs={{0,1},{1,0},{2,3},{3,2},{4,5},{5,4},{6,7},{7,6},{8,9},{9,8},{10,11... | collective-permute-start | bytes 196616 | tf_op jit(solution)/shard_map/ppermute | solution.py:166
  50.0 6.0 %collective-permute-start.18 = (bf16[32,1024]{1,0:T(8,128)(2,1)S(1)}, bf16[32,1024]{1,0:T(8,128)(2,1)S(1)}, u32[]{:S(2)}, u32[]{:S(2)}) collective-permute-start(bf16[32,1024]{1,0:T(8,128)(2,1)S(1)} %pad_maximum_fusion.1.refs_0_), channel_id=1, source_target_pairs={{0,1},{1,0},{2,3},{3,2},{4,5},{5,4},{6,7},{7,6},{8,9},{9,8},{10,11... | collective-permute-start | bytes 196616 | tf_op jit(solution)/shard_map/ppermute | solution.py:166
  53.2 2.8 %collective-permute-start.19 = (bf16[32,1024]{1,0:T(8,128)(2,1)S(1)}, bf16[32,1024]{1,0:T(8,128)(2,1)S(1)}, u32[]{:S(2)}, u32[]{:S(2)}) collective-permute-start(bf16[32,1024]{1,0:T(8,128)(2,1)S(1)} %collective-permute-done.17.refs_1_), channel_id=1, source_target_pairs={{0,1},{1,0},{2,3},{3,2},{4,5},{5,4},{6,7},{7,6},{8,9},{9,8},{10,11... | collective-permute-start | bytes 196616 | tf_op jit(solution)/shard_map/ppermute | solution.py:166
  53.2 4.9 %collective-permute-start.12 = (bf16[32,1280]{1,0:T(8,128)(2,1)S(1)}, bf16[32,1280]{1,0:T(8,128)(2,1)S(1)}, u32[]{:S(2)}, u32[]{:S(2)}) collective-permute-start(bf16[32,1280]{1,0:T(8,128)(2,1)S(1)} %pad_maximum_fusion.refs_0_), channel_id=1, source_target_pairs={{0,1},{1,0},{2,3},{3,2},{4,5},{5,4},{6,7},{7,6},{8,9},{9,8},{10,11... | collective-permute-start | bytes 245768 | tf_op jit(solution)/shard_map/ppermute | solution.py:166
  53.7 4.4 %collective-permute-start.13 = (bf16[32,1280]{1,0:T(8,128)(2,1)S(1)}, bf16[32,1280]{1,0:T(8,128)(2,1)S(1)}, u32[]{:S(2)}, u32[]{:S(2)}) collective-permute-start(bf16[32,1280]{1,0:T(8,128)(2,1)S(1)} %collective-permute-done.11.refs_1_), channel_id=1, source_target_pairs={{0,1},{1,0},{2,3},{3,2},{4,5},{5,4},{6,7},{7,6},{8,9},{9,8},{10,11... | collective-permute-start | bytes 245768 | tf_op jit(solution)/shard_map/ppermute | solution.py:166
  60.6 6.5 %collective-permute-start.25 = (bf16[16,2048]{1,0:T(8,128)(2,1)S(1)}, bf16[16,2048]{1,0:T(8,128)(2,1)S(1)}, u32[]{:S(2)}, u32[]{:S(2)}) collective-permute-start(bf16[16,2048]{1,0:T(8,128)(2,1)S(1)} %get-tuple-element.40), channel_id=1, source_target_pairs={{0,12},{4,8},{8,4},{12,0},{1,13},{5,9},{9,5},{13,1},{2,14},{6,10},... | collective-permute-start | bytes 196616 | tf_op jit(solution)/shard_map/ppermute | solution.py:166
  63.6 7.0 %collective-permute-start.26 = (bf16[16,2048]{1,0:T(8,128)(2,1)S(1)}, bf16[16,2048]{1,0:T(8,128)(2,1)S(1)}, u32[]{:S(2)}, u32[]{:S(2)}) collective-permute-start(bf16[16,2048]{1,0:T(8,128)(2,1)S(1)} %get-tuple-element.41), channel_id=1, source_target_pairs={{0,8},{4,12},{8,0},{12,4},{1,9},{5,13},{9,1},{13,5},{2,10},{6,14},... | collective-permute-start | bytes 196616 | tf_op jit(solution)/shard_map/ppermute | solution.py:166
  64.0 6.6 %collective-permute-start.27 = (bf16[16,2048]{1,0:T(8,128)(2,1)S(1)}, bf16[16,2048]{1,0:T(8,128)(2,1)S(1)}, u32[]{:S(2)}, u32[]{:S(2)}) collective-permute-start(bf16[16,2048]{1,0:T(8,128)(2,1)S(1)} %get-tuple-element.42), channel_id=1, source_target_pairs={{0,4},{4,0},{8,12},{12,8},{1,5},{5,1},{9,13},{13,9},{2,6},{6,2},{1... | collective-permute-start | bytes 196616 | tf_op jit(solution)/shard_map/ppermute | solution.py:166

commit v5 on v4

--- a/solution.py
+++ b/solution.py
@@ -46,68 +46,110 @@
     return pltpu.CompilerParams(vmem_limit_bytes=mib * 2**20)
 
 
-def fetch_kernel(first, width, where, *refs):
-    n = len(refs) // 2 - 1
-    sources, outs, flag, sems = refs[:n], refs[n : 2 * n], refs[-2], refs[-1]
-    start = pl.multiple_of(where[0] + first, TILE)
-    copies = []
-    for source, out in zip(sources, outs):
-        step = out.shape[0] if source.shape == out.shape else TILE
-        for at in range(0, out.shape[0], step):
-            rows = slice(at, at + step)
-            part = source if source.shape == out.shape else source.at[rows, pl.ds(start, width)]
-            copies.append(pltpu.make_async_copy(part, out.at[rows, :], sems.at[len(copies)]))
-            copies[-1].start()
-    flag[...] = jnp.zeros_like(flag)
+def column_copies(source_ref, start, out_ref, cuts, sems):
+    return [
+        pltpu.make_async_copy(source_ref.at[:, pl.ds(start + a, b - a)], out_ref.at[:, a:b], sems.at[i])
+        for i, (a, b) in enumerate(cuts)
+    ]
+
+
+def fetch_kernel(where, gate_ref, up_ref, tokens_ref, gate_out, up_out, tokens_out, sems):
+    start = pl.multiple_of(where[0], TILE)
+    copies = [pltpu.make_async_copy(tokens_ref, tokens_out, sems.at[2, 0])]
+    for k, (source, out) in enumerate(((gate_ref, gate_out), (up_ref, up_out))):
+        copies += column_copies(source, start, out, pieces_of(out.shape[1], 2 * TILE), sems.at[k])
+    for copy in copies:
+        copy.start()
     for copy in copies:
         copy.wait()
 
 
-def fetch(where, arrays, first, width):
-    shapes = [a.shape if a.shape[0] == ROWS else (a.shape[0], width) for a in arrays]
-    size = sum(2 * x * y for x, y in shapes)
-    n = len(arrays)
-    return pl.pallas_call(
-        functools.partial(fetch_kernel, first, width),
-        in_specs=[spec(pltpu.SMEM)] + [spec(pltpu.HBM)] * n,
-        out_specs=[spec(pltpu.VMEM)] * (n + 1),
-        out_shape=[pltpu.VMEM(x, jnp.bfloat16) for x in shapes] + [pltpu.VMEM((8, 128), jnp.float32)],
-        scratch_shapes=[pltpu.SemaphoreType.DMA((sum(-(-x // TILE) for x, _ in shapes),))],
+def fetch(where, gate, up, tokens, width):
+    depth = gate.shape[0]
+    return pl.pallas_call(
+        fetch_kernel,
+        in_specs=[spec(pltpu.SMEM)] + [spec(pltpu.HBM)] * 3,
+        out_specs=[spec(pltpu.VMEM)] * 3,
+        out_shape=[pltpu.VMEM(x, jnp.bfloat16) for x in ((depth, width), (depth, width), tokens.shape)],
+        scratch_shapes=[pltpu.SemaphoreType.DMA((3, len(pieces_of(width, 2 * TILE))))],
         compiler_params=params(1),
-        cost_estimate=pl.CostEstimate(flops=0, bytes_accessed=size, transcendentals=0),
+        cost_estimate=pl.CostEstimate(flops=0, bytes_accessed=4 * depth * width, transcendentals=0),
         name="fetch",
-    )(where, *arrays)
-
-
-def gate_up_kernel(n_blocks, where, *refs):
-    blocks, (gate_ref, up_ref), (mine_ref, theirs_ref, x_ref) = refs[:n_blocks], refs[n_blocks:][:2], refs[-3:]
+    )(where, gate, up, tokens)
+
+
+def gate_up_kernel(n_blocks, first, streamed, where, *refs):
+    blocks, weights = refs[:n_blocks], refs[n_blocks : n_blocks + 2]
+    if streamed:
+        mine_ref, theirs_ref, x_ref, w_ref, sems = refs[-5:]
+    else:
+        mine_ref, theirs_ref, x_ref = refs[-3:]
+    cuts = pieces_of(mine_ref.shape[2], 2 * TILE)
+    if streamed:
+        start = pl.multiple_of(where[0] + first, TILE)
+        copies = [column_copies(weights[k], start, w_ref.at[k], cuts, sems.at[k]) for k in range(2)]
+        for i in range(len(cuts)):
+            for k in range(2):
+                copies[k][i].start()
     for b in range(n_blocks):
         at = place(where[1], b % 4) * 2 + b // 4
         x_ref[pl.ds(pl.multiple_of(at * ROWS, ROWS), ROWS), :] = blocks[b][...]
     half = x_ref.shape[0] // 2
-    for a, b in pieces_of(gate_ref.shape[1], 2 * TILE):
-        for k, w_ref in enumerate((gate_ref, up_ref)):
-            part = jnp.dot(x_ref[...], w_ref[:, a:b], preferred_element_type=jnp.float32).astype(jnp.bfloat16)
+    for i, (a, b) in enumerate(cuts):
+        for k in range(2):
+            if streamed:
+                copies[k][i].wait()
+                weight = w_ref[k, :, a:b]
+            else:
+                weight = weights[k][:, first + a : first + b]
+            part = jnp.dot(x_ref[...], weight, preferred_element_type=jnp.float32).astype(jnp.bfloat16)
             mine_ref[k, :, a:b] = part[:half]
             theirs_ref[k, :, a:b] = part[half:]
 
 
-def gate_up(where, blocks, gate, up, behind):
-    depth, width = gate.shape
+def gate_up(where, blocks, gate, up, first, width, streamed, behind):
+    depth = gate.shape[0]
     n = len(blocks)
     total = n * ROWS
-    return pl.pallas_call(
-        functools.partial(gate_up_kernel, n),
-        in_specs=[spec(pltpu.SMEM)] + [spec(pltpu.VMEM)] * (n + 2) + [spec(pl.ANY)] * len(behind),
+    scratch = [pltpu.VMEM((total, depth), jnp.bfloat16)]
+    if streamed:
+        scratch.append(pltpu.VMEM((2, depth, width), jnp.bfloat16))
+        scratch.append(pltpu.SemaphoreType.DMA((2, len(pieces_of(width, 2 * TILE)))))
+    return pl.pallas_call(
+        functools.partial(gate_up_kernel, n, first, streamed),
+        in_specs=[spec(pltpu.SMEM)]
+        + [spec(pltpu.VMEM)] * n
+        + [spec(pltpu.HBM if streamed else pltpu.VMEM)] * 2
+        + [spec(pl.ANY)] * len(behind),
         out_specs=[spec(pltpu.VMEM)] * 2,
-        scratch_shapes=[pltpu.VMEM((total, depth), jnp.bfloat16)],
+        scratch_shapes=scratch,
         out_shape=[jax.ShapeDtypeStruct((2, total // 2, width), jnp.bfloat16)] * 2,
-        compiler_params=params(4),
+        compiler_params=params(16 if streamed else 4),
         cost_estimate=pl.CostEstimate(
             flops=4 * total * depth * width, bytes_accessed=4 * depth * width, transcendentals=0
         ),
         name="gate_up",
     )(where, *blocks, gate, up, *behind)
+
+
+def join_kernel(*refs):
+    out_ref = refs[-1]
+    half = out_ref.shape[0] // 2
+    out_ref[:half, :] = refs[0][...]
+    out_ref[half:, :] = refs[1][...]
+
+
+def join(own, other, behind):
+    rows, width = own.shape
+    return pl.pallas_call(
+        join_kernel,
+        in_specs=[spec(pltpu.VMEM)] * 2 + [spec(pl.ANY)],
+        out_specs=spec(pltpu.VMEM),
+        out_shape=jax.ShapeDtypeStruct((2 * rows, width), own.dtype),
+        compiler_params=params(1),
+        cost_estimate=pl.CostEstimate(flops=0, bytes_accessed=8 * rows * width, transcendentals=0),
+        name="join",
+    )(own, other, behind)
 
 
 def down_kernel(n_pieces, has_acc, last, first, half, where, *refs):
@@ -116,9 +158,13 @@
     prev_ref, refs = (refs[0], refs[1:]) if has_acc else (None, refs)
     outs, (acc_ref, lhs_ref) = refs[:-2], refs[-2:]
     depth = lhs_ref.shape[2]
-    for p, piece in enumerate(pieces):
-        for k in range(2):
-            lhs_ref[k, p * ROWS : (p + 1) * ROWS, :] = piece[k * ROWS : (k + 1) * ROWS, :]
+    p = 0
+    for piece in pieces:
+        for at in range(0, piece.shape[0], 2 * ROWS):
+            for k in range(2):
+                rows = slice(at + k * ROWS, at + (k + 1) * ROWS)
+                lhs_ref[k, p * ROWS : (p + 1) * ROWS, :] = piece[rows, :]
+            p += 1
     for a, b in pieces_of(down_ref.shape[1], 2 * TILE):
         part = prev_ref[:, a:b] if has_acc else 0.0
         for k in range(2):
@@ -135,7 +181,7 @@
 def down(where, pieces, down_weight, prev, first, last):
     width = down_weight.shape[1]
     n, depth = len(pieces), pieces[0].shape[1]
-    total = n * ROWS
+    total = sum(p.shape[0] for p in pieces) // 2
     args = [*pieces, down_weight] + ([] if prev is None else [prev])
     sums = jax.ShapeDtypeStruct((total, width), jnp.float32)
     scratch = [pltpu.VMEM((2, total, depth), jnp.bfloat16)]
@@ -144,9 +190,9 @@
     return pl.pallas_call(
         functools.partial(down_kernel, n, prev is not None, last, first, down_weight.shape[0] // 2),
         in_specs=[spec(pltpu.SMEM)] + [spec(pltpu.VMEM)] * len(args),
-        out_specs=[spec(pltpu.VMEM)] * n if last else spec(pltpu.VMEM),
+        out_specs=[spec(pltpu.VMEM)] * 4 if last else spec(pltpu.VMEM),
         scratch_shapes=scratch,
-        out_shape=[jax.ShapeDtypeStruct((ROWS, width), jnp.bfloat16)] * n if last else sums,
+        out_shape=[jax.ShapeDtypeStruct((ROWS, width), jnp.bfloat16)] * 4 if last else sums,
         compiler_params=params(4),
         cost_estimate=pl.CostEstimate(
             flops=4 * total * width * depth, bytes_accessed=4 * width * depth, transcendentals=0
@@ -167,11 +213,9 @@
 
     tiles = width // TILE
     bounds = [tiles * c // CHUNKS * TILE for c in range(CHUNKS + 1)]
-    sources = [pltpu.with_memory_space_constraint(w, pltpu.HBM) for w in (gate_weight, up_weight, tokens)]
-    weights = [
-        fetch(where, sources[: 2 if c else 3], bounds[c], bounds[c + 1] - bounds[c]) for c in range(CHUNKS)
-    ]
-    own_tokens = weights[0][2]
+    gate_weight, up_weight = (pltpu.with_memory_space_constraint(w, pltpu.HBM) for w in (gate_weight, up_weight))
+    hbm_tokens = pltpu.with_memory_space_constraint(tokens, pltpu.HBM)
+    *early, own_tokens = fetch(where, gate_weight, up_weight, hbm_tokens, bounds[-2])
     down_weight = pltpu.with_memory_space_constraint(down_weight, pltpu.VMEM)
 
     near = [swap(tokens, "hid", d) for d in (3, 2, 1)] + [own_tokens]
@@ -184,14 +228,13 @@
         mine, got = parts[c]
         to_chips.append((mine[:, quarter:].astype(f32) + got[:, quarter:].astype(f32)).astype(bf16))
 
-    behind = [w[-1] for w in weights[1:]]
     for c in range(CHUNKS):
-        if c >= 2:
-            send_to_chip(c - 2)
-            behind = [to_chips[-1]]
-        elif c == 1:
-            behind = [parts[0][0]]
-        mine, theirs = gate_up(where, blocks, *weights[c][:2], behind)
+        while len(to_chips) < c and c == CHUNKS - 1:
+            send_to_chip(len(to_chips))
+        behind = to_chips[:] if to_chips else [p[0] for p in parts]
+        last = c == CHUNKS - 1
+        weights = (gate_weight, up_weight) if last else early
+        mine, theirs = gate_up(where, blocks, *weights, bounds[c], bounds[c + 1] - bounds[c], last, behind)
         parts.append((mine, swap(theirs, "wid", 1)))
     while len(to_chips) < CHUNKS:
         send_to_chip(len(to_chips))
@@ -204,7 +247,10 @@
         hidden = (jax.nn.silu(summed[0]) * summed[1]).astype(bf16)
         own = jnp.concatenate([hidden[:ROWS], swap(hidden[ROWS:], "rep", 1)], 0)
         other = swap(own, "wid", 2)
-        pieces = [own, other, swap(own, "wid", 1), swap(other, "wid", 1)]
+        if c < CHUNKS - 1:
+            pieces = [own, other, swap(own, "wid", 1), swap(other, "wid", 1)]
+        else:
+            pieces = [own, other, swap(join(own, other, acc), "wid", 1)]
         acc = down(where, pieces, down_weight, acc, bounds[c], c == CHUNKS - 1)
 
     mixed = acc[0].astype(f32)

time: 71.4 us -> 68.1 us (0.954)
  Pallas kernels: 26.4 us -> 22.9 us
    pallas_call x6 -> x5, Pallas kernels: 19.6 us -> 16.1 us  [the longest x3 9.47 us: gate_up(): pl.pallas_call(functools.partial(gate_up_kernel, n, first, streamed), in_...]
    ppermute x28 -> x27, waiting for transfers between devices: 15.4 us -> 16 us  [swap(): return lax.ppermute(x, axis, [(i, i ^ step) for i in range(n)])]
    ppermute x28 -> x27, starting transfers between devices: 27.9 us -> 27.6 us  [swap(): return lax.ppermute(x, axis, [(i, i ^ step) for i in range(n)])]
  transfers between devices with their start and end apart: 28 -> 27, of which waited for: 9 -> 10; matrix products, arithmetic and copies ran while one was open for 1% -> 1% of each run, Pallas kernels for 28% -> 25%
where the time goes in v5:
time: 68.1 us; the launch traced here: 67.9 us
  starting transfers between devices  27.6 us (41%)
  Pallas kernels  22.9 us (34%)
  waiting for transfers between devices  16 us (23%)
  other arithmetic  1.18 us (2%)
    ppermute x27, starting transfers between devices, swap(): return lax.ppermute(x, axis, [(i, i ^ step) for i in range(n)])  27.6 us
    ppermute x27, waiting for transfers between devices, swap(): return lax.ppermute(x, axis, [(i, i ^ step) for i in range(n)])  16 us
    pallas_call x3, Pallas kernels, gate_up(): pl.pallas_call(functools.partial(gate_up_kernel, n, first, streamed), in_...  9.47 us
    pallas_call x3, Pallas kernels, down(): pl.pallas_call(functools.partial(down_kernel, n, prev is not None, last,...  6.72 us
    pallas_call x1, Pallas kernels, fetch(): pl.pallas_call(fetch_kernel, in_specs=[spec(pltpu.SMEM)] + [spec(pltpu.HB...  6.64 us
  transfers between devices with their start and end apart: 27, of which 10 were waited for; matrix products, arithmetic and copies ran while one was open for 1% of the time, Pallas kernels for 25%

profile of v5, /device:TPU:0, one launch (start us, length us, event | category | flops | bytes accessed | tf_op | source)
XLA Modules:
  0.0 67.9 jit_solution(14018509538573418079)
XLA Ops:
  0.0 3.0 %collective-permute-start = (bf16[16,2048]{1,0:T(8,128)(2,1)}, bf16[16,2048]{1,0:T(8,128)(2,1)S(1)}, u32[]{:S(2)}, u32[]{:S(2)}) collective-permute-start(bf16[16,2048]{1,0:T(8,128)(2,1)} %tokens_ref.1), channel_id=1, source_target_pairs={{0,4},{4,0},{8,12},{12,8},{1,5},{5,1},{9,13},{13,9},{2,6},{6,2},{1... | collective-permute-start | bytes 196616 | tf_op jit(solution)/shard_map/ppermute | solution.py:212
  3.0 2.5 %collective-permute-start.2 = (bf16[16,2048]{1,0:T(8,128)(2,1)}, bf16[16,2048]{1,0:T(8,128)(2,1)S(1)}, u32[]{:S(2)}, u32[]{:S(2)}) collective-permute-start(bf16[16,2048]{1,0:T(8,128)(2,1)} %tokens_ref.1), channel_id=1, source_target_pairs={{0,12},{4,8},{8,4},{12,0},{1,13},{5,9},{9,5},{13,1},{2,14},{6,10},... | collective-permute-start | bytes 196616 | tf_op jit(solution)/shard_map/ppermute | solution.py:212
  5.5 0.1 collective-permute-start.1
  5.6 0.1 pad_add_fusion.where
  5.7 6.6 %fetch.1 = (bf16[2048,2048]{1,0:T(8,128)(2,1)S(1)}, bf16[2048,2048]{1,0:T(8,128)(2,1)S(1)}, bf16[16,2048]{1,0:T(8,128)(2,1)S(1)}) custom-call(s32[2]{0:T(128)S(1)} %pad_add_fusion.where, bf16[2048,6656]{1,0:T(8,128)(2,1)} %refs_8_.1, bf16[2048,6656]{1,0:T(8,128)(2,1)} %refs_9_.1, bf16[16,2048]{1,0:T(8,128)(2,1)} %tokens_ref.1), custom_call_target="tpu_custom_call" | custom-call | bytes 16777216 | tf_op jit(solution)/shard_map/fetch/pallas_call | solution.py:69
  12.3 1.6 %collective-permute-start.3 = (bf16[16,2048]{1,0:T(8,128)(2,1)S(1)}, bf16[16,2048]{1,0:T(8,128)(2,1)S(1)}, u32[]{:S(2)}, u32[]{:S(2)}) collective-permute-start(bf16[16,2048]{1,0:T(8,128)(2,1)S(1)} %get-tuple-element.18.refs_0_), channel_id=1, source_target_pairs={{0,16},{16,0},{1,17},{17,1},{2,18},{18,2},{3,19},{19,3},{4,20},{20... | collective-permute-start | bytes 196616 | tf_op jit(solution)/shard_map/ppermute | solution.py:212
  13.9 0.5 collective-permute-start.4
  14.4 1.5 %collective-permute-start.6 = (bf16[16,2048]{1,0:T(8,128)(2,1)S(1)}, bf16[16,2048]{1,0:T(8,128)(2,1)S(1)}, u32[]{:S(2)}, u32[]{:S(2)}) collective-permute-start(bf16[16,2048]{1,0:T(8,128)(2,1)S(1)} %collective-permute-done.2.refs_3_), channel_id=1, source_target_pairs={{0,16},{16,0},{1,17},{17,1},{2,18},{18,2},{3,19},{19,3},{4,20},{20... | collective-permute-start | bytes 196616 | tf_op jit(solution)/shard_map/ppermute | solution.py:212
  16.0 0.5 collective-permute-start.5
  16.5 0.8 %collective-permute-done.3.refs_4_ = bf16[16,2048]{1,0:T(8,128)(2,1)S(1)} collective-permute-done((bf16[16,2048]{1,0:T(8,128)(2,1)S(1)}, bf16[16,2048]{1,0:T(8,128)(2,1)S(1)}, u32[]{:S(2)}, u32[]{:S(2)}) %collective-permute-start.3) | collective-permute-done | bytes 65568 | tf_op jit(solution)/shard_map/ppermute | solution.py:212
  17.3 1.7 %collective-permute-done.4.refs_5_ = bf16[16,2048]{1,0:T(8,128)(2,1)S(1)} collective-permute-done((bf16[16,2048]{1,0:T(8,128)(2,1)S(1)}, bf16[16,2048]{1,0:T(8,128)(2,1)S(1)}, u32[]{:S(2)}, u32[]{:S(2)}) %collective-permute-start.4) | collective-permute-done | bytes 65568 | tf_op jit(solution)/shard_map/ppermute | solution.py:212
  19.0 0.8 %collective-permute-done.6.refs_7_ = bf16[16,2048]{1,0:T(8,128)(2,1)S(1)} collective-permute-done((bf16[16,2048]{1,0:T(8,128)(2,1)S(1)}, bf16[16,2048]{1,0:T(8,128)(2,1)S(1)}, u32[]{:S(2)}, u32[]{:S(2)}) %collective-permute-start.6) | collective-permute-done | bytes 65568 | tf_op jit(solution)/shard_map/ppermute | solution.py:212
  19.7 0.7 %collective-permute-done.5.refs_6_ = bf16[16,2048]{1,0:T(8,128)(2,1)S(1)} collective-permute-done((bf16[16,2048]{1,0:T(8,128)(2,1)S(1)}, bf16[16,2048]{1,0:T(8,128)(2,1)S(1)}, u32[]{:S(2)}, u32[]{:S(2)}) %collective-permute-start.5) | collective-permute-done | bytes 65568 | tf_op jit(solution)/shard_map/ppermute | solution.py:212
  20.4 1.8 %gate_up.3 = (bf16[2,64,1024]{2,1,0:T(8,128)(2,1)S(1)}, bf16[2,64,1024]{2,1,0:T(8,128)(2,1)S(1)}) custom-call(s32[2]{0:T(128)S(1)} %pad_add_fusion.where, bf16[16,2048]{1,0:T(8,128)(2,1)S(1)} %get-tuple-element.18.refs_0_, bf16[16,2048]{1,0:T(8,128)(2,1)S(1)} %collective-permute-done.refs_1_, bf16[16,2048]{1,0:T(8,128)(2,1)S(1)} %collective-permute-done.1.refs_2_, ...), custom_call_target="tpu_custom_call" | custom-call | flops 1073741824 | bytes 8388608 | tf_op jit(solution)/shard_map/gate_up/pallas_call | solution.py:118
  22.3 1.8 %gate_up.4 = (bf16[2,64,1024]{2,1,0:T(8,128)(2,1)S(1)}, bf16[2,64,1024]{2,1,0:T(8,128)(2,1)S(1)}) custom-call(s32[2]{0:T(128)S(1)} %pad_add_fusion.where, bf16[16,2048]{1,0:T(8,128)(2,1)S(1)} %get-tuple-element.18.refs_0_, bf16[16,2048]{1,0:T(8,128)(2,1)S(1)} %collective-permute-done.refs_1_, bf16[16,2048]{1,0:T(8,128)(2,1)S(1)} %collective-permute-done.1.refs_2_, ...), custom_call_target="tpu_custom_call" | custom-call | flops 1073741824 | bytes 8388608 | tf_op jit(solution)/shard_map/gate_up/pallas_call | solution.py:118
  24.1 0.1 collective-permute-start.8
  24.2 0.5 collective-permute-start.7
  24.7 1.0 %collective-permute-done.8 = bf16[2,64,1024]{2,1,0:T(8,128)(2,1)S(1)} collective-permute-done((bf16[2,64,1024]{2,1,0:T(8,128)(2,1)S(1)}, bf16[2,64,1024]{2,1,0:T(8,128)(2,1)S(1)}, u32[]{:S(2)}, u32[]{:S(2)}) %collective-permute-start.8) | collective-permute-done | bytes 262176 | tf_op jit(solution)/shard_map/ppermute | solution.py:212
  25.8 1.5 %collective-permute-start.13 = (bf16[2,32,1024]{2,1,0:T(8,128)(2,1)S(1)}, bf16[2,32,1024]{2,1,0:T(8,128)(2,1)S(1)}, u32[]{:S(2)}, u32[]{:S(2)}) collective-permute-start(bf16[2,32,1024]{2,1,0:T(8,128)(2,1)S(1)} %add_convert_fusion.1.refs_11_), channel_id=1, source_target_pairs={{0,2},{1,3},{2,0},{3,1},{4,6},{5,7},{6,4},{7,5},{8,10},{9,11},{10,... | collective-permute-start | bytes 393224 | tf_op jit(solution)/shard_map/ppermute | solution.py:212
  27.4 0.0 slice-start.1
  27.4 0.6 collective-permute-start.18
  28.1 5.8 %gate_up.5 = (bf16[2,64,1280]{2,1,0:T(8,128)(2,1)S(1)}, bf16[2,64,1280]{2,1,0:T(8,128)(2,1)S(1)}) custom-call(s32[2]{0:T(128)S(1)} %pad_add_fusion.where, bf16[16,2048]{1,0:T(8,128)(2,1)S(1)} %get-tuple-element.18.refs_0_, bf16[16,2048]{1,0:T(8,128)(2,1)S(1)} %collective-permute-done.refs_1_, bf16[16,2048]{1,0:T(8,128)(2,1)S(1)} %collective-permute-done.1.refs_2_, ...), custom_call_target="tpu_custom_call" | custom-call | flops 1342177280 | bytes 10485760 | tf_op jit(solution)/shard_map/gate_up/pallas_call | solution.py:118
  33.8 0.1 collective-permute-start.9
  34.1 1.1 %collective-permute-start.14 = (bf16[16,1024]{1,0:T(8,128)(2,1)S(1)}, bf16[16,1024]{1,0:T(8,128)(2,1)S(1)}, u32[]{:S(2)}, u32[]{:S(2)}) collective-permute-start(bf16[16,1024]{1,0:T(8,128)(2,1)S(1)} %get-tuple-element.36), channel_id=1, source_target_pairs={{0,16},{16,0},{1,17},{17,1},{2,18},{18,2},{3,19},{19,3},{4,20},{20... | collective-permute-start | bytes 98312 | tf_op jit(solution)/shard_map/ppermute | solution.py:212
  35.3 1.0 %collective-permute-start.19 = (bf16[16,1024]{1,0:T(8,128)(2,1)S(1)}, bf16[16,1024]{1,0:T(8,128)(2,1)S(1)}, u32[]{:S(2)}, u32[]{:S(2)}) collective-permute-start(bf16[16,1024]{1,0:T(8,128)(2,1)S(1)} %get-tuple-element.34), channel_id=1, source_target_pairs={{0,16},{16,0},{1,17},{17,1},{2,18},{18,2},{3,19},{19,3},{4,20},{20... | collective-permute-start | bytes 98312 | tf_op jit(solution)/shard_map/ppermute | solution.py:212
  36.4 1.7 %collective-permute-start.10 = (bf16[2,32,1280]{2,1,0:T(8,128)(2,1)S(1)}, bf16[2,32,1280]{2,1,0:T(8,128)(2,1)S(1)}, u32[]{:S(2)}, u32[]{:S(2)}) collective-permute-start(bf16[2,32,1280]{2,1,0:T(8,128)(2,1)S(1)} %add_convert_fusion), channel_id=1, source_target_pairs={{0,2},{1,3},{2,0},{3,1},{4,6},{5,7},{6,4},{7,5},{8,10},{9,11},{10,... | collective-permute-start | bytes 491528 | tf_op jit(solution)/shard_map/ppermute | solution.py:212
  38.1 1.6 %collective-permute-start.15 = (bf16[32,1024]{1,0:T(8,128)(2,1)S(1)}, bf16[32,1024]{1,0:T(8,128)(2,1)S(1)}, u32[]{:S(2)}, u32[]{:S(2)}) collective-permute-start(bf16[32,1024]{1,0:T(8,128)(2,1)S(1)} %pad_maximum_fusion.1.refs_0_), channel_id=1, source_target_pairs={{0,2},{1,3},{2,0},{3,1},{4,6},{5,7},{6,4},{7,5},{8,10},{9,11},{10,... | collective-permute-start | bytes 196616 | tf_op jit(solution)/shard_map/ppermute | solution.py:212
  39.7 1.2 %collective-permute-start.20 = (bf16[32,1024]{1,0:T(8,128)(2,1)S(1)}, bf16[32,1024]{1,0:T(8,128)(2,1)S(1)}, u32[]{:S(2)}, u32[]{:S(2)}) collective-permute-start(bf16[32,1024]{1,0:T(8,128)(2,1)S(1)} %pad_maximum_fusion.2.refs_0_), channel_id=1, source_target_pairs={{0,2},{1,3},{2,0},{3,1},{4,6},{5,7},{6,4},{7,5},{8,10},{9,11},{10,... | collective-permute-start | bytes 196616 | tf_op jit(solution)/shard_map/ppermute | solution.py:212
  41.0 2.6 %collective-permute-done.10 = bf16[2,32,1280]{2,1,0:T(8,128)(2,1)S(1)} collective-permute-done((bf16[2,32,1280]{2,1,0:T(8,128)(2,1)S(1)}, bf16[2,32,1280]{2,1,0:T(8,128)(2,1)S(1)}, u32[]{:S(2)}, u32[]{:S(2)}) %collective-permute-start.10) | collective-permute-done | bytes 163872 | tf_op jit(solution)/shard_map/ppermute | solution.py:212
  43.5 0.1 convert_add_fusion
  43.6 0.1 fusion.1
  43.7 1.1 %collective-permute-start.11 = (bf16[16,1280]{1,0:T(8,128)(2,1)S(1)}, bf16[16,1280]{1,0:T(8,128)(2,1)S(1)}, u32[]{:S(2)}, u32[]{:S(2)}) collective-permute-start(bf16[16,1280]{1,0:T(8,128)(2,1)S(1)} %get-tuple-element.32), channel_id=1, source_target_pairs={{0,16},{16,0},{1,17},{17,1},{2,18},{18,2},{3,19},{19,3},{4,20},{20... | collective-permute-start | bytes 122888 | tf_op jit(solution)/shard_map/ppermute | solution.py:212
  44.8 0.5 collective-permute-start.21
  45.3 0.0 collective-permute-start.17
  45.3 0.5 collective-permute-start.22
  45.8 1.9 %collective-permute-done.11 = bf16[16,1280]{1,0:T(8,128)(2,1)S(1)} collective-permute-done((bf16[16,1280]{1,0:T(8,128)(2,1)S(1)}, bf16[16,1280]{1,0:T(8,128)(2,1)S(1)}, u32[]{:S(2)}, u32[]{:S(2)}) %collective-permute-start.11) | collective-permute-done | bytes 40992 | tf_op jit(solution)/shard_map/ppermute | solution.py:212
  47.7 1.7 %collective-permute-start.12 = (bf16[32,1280]{1,0:T(8,128)(2,1)S(1)}, bf16[32,1280]{1,0:T(8,128)(2,1)S(1)}, u32[]{:S(2)}, u32[]{:S(2)}) collective-permute-start(bf16[32,1280]{1,0:T(8,128)(2,1)S(1)} %pad_maximum_fusion.refs_0_), channel_id=1, source_target_pairs={{0,2},{1,3},{2,0},{3,1},{4,6},{5,7},{6,4},{7,5},{8,10},{9,11},{10,... | collective-permute-start | bytes 245768 | tf_op jit(solution)/shard_map/ppermute | solution.py:212
  49.5 2.1 %down.3.refs_5_ = f32[64,2048]{1,0:T(8,128)S(1)} custom-call(s32[2]{0:T(128)S(1)} %pad_add_fusion.where, bf16[32,1024]{1,0:T(8,128)(2,1)S(1)} %pad_maximum_fusion.2.refs_0_, bf16[32,1024]{1,0:T(8,128)(2,1)S(1)} %collective-permute-done.20.refs_1_, bf16[32,1024]{1,0:T(8,128)(2,1)S(1)} %collective-permute-done.21.refs_2_, ...), custom_call_target="tpu_custom_call" | custom-call | flops 536870912 | bytes 8388608 | tf_op jit(solution)/shard_map/down/pallas_call | solution.py:190
  51.6 2.1 %down.4.refs_2_.refs_4_ = f32[64,2048]{1,0:T(8,128)S(1)} custom-call(s32[2]{0:T(128)S(1)} %pad_add_fusion.where, bf16[32,1024]{1,0:T(8,128)(2,1)S(1)} %pad_maximum_fusion.1.refs_0_, bf16[32,1024]{1,0:T(8,128)(2,1)S(1)} %collective-permute-done.15.refs_1_, bf16[32,1024]{1,0:T(8,128)(2,1)S(1)} %collective-permute-done.16.refs_2_, ...), custom_call_target="tpu_custom_call" | custom-call | flops 536870912 | bytes 8388608 | tf_op jit(solution)/shard_map/down/pallas_call | solution.py:190
  53.8 0.1 collective-permute-start.23
  53.9 1.4 %collective-permute-done.23.refs_2_ = bf16[64,1280]{1,0:T(8,128)(2,1)S(1)} collective-permute-done((bf16[64,1280]{1,0:T(8,128)(2,1)S(1)}, bf16[64,1280]{1,0:T(8,128)(2,1)S(1)}, u32[]{:S(2)}, u32[]{:S(2)}) %collective-permute-start.23) | collective-permute-done | bytes 163872 | tf_op jit(solution)/shard_map/ppermute | solution.py:212
  55.3 2.5 %down.5 = (bf16[16,2048]{1,0:T(8,128)(2,1)S(1)}, bf16[16,2048]{1,0:T(8,128)(2,1)S(1)}, bf16[16,2048]{1,0:T(8,128)(2,1)S(1)}, bf16[16,2048]{1,0:T(8,128)(2,1)S(1)}) custom-call(s32[2]{0:T(128)S(1)} %pad_add_fusion.where, bf16[32,1280]{1,0:T(8,128)(2,1)S(1)} %pad_maximum_fusion.refs_0_, bf16[32,1280]{1,0:T(8,128)(2,1)S(1)} %collective-permute-done.12.refs_1_, ...), custom_call_target="tpu_custom_call" | custom-call | flops 671088640 | bytes 10485760 | tf_op jit(solution)/shard_map/down/pallas_call | solution.py:190
  57.8 2.8 %collective-permute-start.24 = (bf16[16,2048]{1,0:T(8,128)(2,1)S(1)}, bf16[16,2048]{1,0:T(8,128)(2,1)S(1)}, u32[]{:S(2)}, u32[]{:S(2)}) collective-permute-start(bf16[16,2048]{1,0:T(8,128)(2,1)S(1)} %get-tuple-element.28), channel_id=1, source_target_pairs={{0,12},{4,8},{8,4},{12,0},{1,13},{5,9},{9,5},{13,1},{2,14},{6,10},... | collective-permute-start | bytes 196616 | tf_op jit(solution)/shard_map/ppermute | solution.py:212
  60.5 0.3 collective-permute-start.25
  60.9 1.3 %collective-permute-start.26 = (bf16[16,2048]{1,0:T(8,128)(2,1)S(1)}, bf16[16,2048]{1,0:T(8,128)(2,1)S(1)}, u32[]{:S(2)}, u32[]{:S(2)}) collective-permute-start(bf16[16,2048]{1,0:T(8,128)(2,1)S(1)} %get-tuple-element.30), channel_id=1, source_target_pairs={{0,4},{4,0},{8,12},{12,8},{1,5},{5,1},{9,13},{13,9},{2,6},{6,2},{1... | collective-permute-start | bytes 196616 | tf_op jit(solution)/shard_map/ppermute | solution.py:212
  62.2 1.9 %collective-permute-done.24 = bf16[16,2048]{1,0:T(8,128)(2,1)S(1)} collective-permute-done((bf16[16,2048]{1,0:T(8,128)(2,1)S(1)}, bf16[16,2048]{1,0:T(8,128)(2,1)S(1)}, u32[]{:S(2)}, u32[]{:S(2)}) %collective-permute-start.24) | collective-permute-done | bytes 65568 | tf_op jit(solution)/shard_map/ppermute | solution.py:212
  64.1 3.2 %collective-permute-done.25 = bf16[16,2048]{1,0:T(8,128)(2,1)S(1)} collective-permute-done((bf16[16,2048]{1,0:T(8,128)(2,1)S(1)}, bf16[16,2048]{1,0:T(8,128)(2,1)S(1)}, u32[]{:S(2)}, u32[]{:S(2)}) %collective-permute-start.25) | collective-permute-done | bytes 65568 | tf_op jit(solution)/shard_map/ppermute | solution.py:212
  67.3 0.7 add_convert_fusion.3
  (46 shorter events, 0.4 us)
Async XLA Ops:
  0.0 13.9 %collective-permute-start = (bf16[16,2048]{1,0:T(8,128)(2,1)}, bf16[16,2048]{1,0:T(8,128)(2,1)S(1)}, u32[]{:S(2)}, u32[]{:S(2)}) collective-permute-start(bf16[16,2048]{1,0:T(8,128)(2,1)} %tokens_ref.1), channel_id=1, source_target_pairs={{0,4},{4,0},{8,12},{12,8},{1,5},{5,1},{9,13},{13,9},{2,6},{6,2},{1... | collective-permute-start | bytes 196616 | tf_op jit(solution)/shard_map/ppermute | solution.py:212
  3.0 11.4 %collective-permute-start.2 = (bf16[16,2048]{1,0:T(8,128)(2,1)}, bf16[16,2048]{1,0:T(8,128)(2,1)S(1)}, u32[]{:S(2)}, u32[]{:S(2)}) collective-permute-start(bf16[16,2048]{1,0:T(8,128)(2,1)} %tokens_ref.1), channel_id=1, source_target_pairs={{0,12},{4,8},{8,4},{12,0},{1,13},{5,9},{9,5},{13,1},{2,14},{6,10},... | collective-permute-start | bytes 196616 | tf_op jit(solution)/shard_map/ppermute | solution.py:212
  5.5 10.5 %collective-permute-start.1 = (bf16[16,2048]{1,0:T(8,128)(2,1)}, bf16[16,2048]{1,0:T(8,128)(2,1)S(1)}, u32[]{:S(2)}, u32[]{:S(2)}) collective-permute-start(bf16[16,2048]{1,0:T(8,128)(2,1)} %tokens_ref.1), channel_id=1, source_target_pairs={{0,8},{4,12},{8,0},{12,4},{1,9},{5,13},{9,1},{13,5},{2,10},{6,14},... | collective-permute-start | bytes 196616 | tf_op jit(solution)/shard_map/ppermute | solution.py:212
  12.3 5.0 %collective-permute-start.3 = (bf16[16,2048]{1,0:T(8,128)(2,1)S(1)}, bf16[16,2048]{1,0:T(8,128)(2,1)S(1)}, u32[]{:S(2)}, u32[]{:S(2)}) collective-permute-start(bf16[16,2048]{1,0:T(8,128)(2,1)S(1)} %get-tuple-element.18.refs_0_), channel_id=1, source_target_pairs={{0,16},{16,0},{1,17},{17,1},{2,18},{18,2},{3,19},{19,3},{4,20},{20... | collective-permute-start | bytes 196616 | tf_op jit(solution)/shard_map/ppermute | solution.py:212
  13.9 5.0 %collective-permute-start.4 = (bf16[16,2048]{1,0:T(8,128)(2,1)S(1)}, bf16[16,2048]{1,0:T(8,128)(2,1)S(1)}, u32[]{:S(2)}, u32[]{:S(2)}) collective-permute-start(bf16[16,2048]{1,0:T(8,128)(2,1)S(1)} %collective-permute-done.refs_1_), channel_id=1, source_target_pairs={{0,16},{16,0},{1,17},{17,1},{2,18},{18,2},{3,19},{19,3},{4,20},{20... | collective-permute-start | bytes 196616 | tf_op jit(solution)/shard_map/ppermute | solution.py:212
  14.4 5.3 %collective-permute-start.6 = (bf16[16,2048]{1,0:T(8,128)(2,1)S(1)}, bf16[16,2048]{1,0:T(8,128)(2,1)S(1)}, u32[]{:S(2)}, u32[]{:S(2)}) collective-permute-start(bf16[16,2048]{1,0:T(8,128)(2,1)S(1)} %collective-permute-done.2.refs_3_), channel_id=1, source_target_pairs={{0,16},{16,0},{1,17},{17,1},{2,18},{18,2},{3,19},{19,3},{4,20},{20... | collective-permute-start | bytes 196616 | tf_op jit(solution)/shard_map/ppermute | solution.py:212
  16.0 4.5 %collective-permute-start.5 = (bf16[16,2048]{1,0:T(8,128)(2,1)S(1)}, bf16[16,2048]{1,0:T(8,128)(2,1)S(1)}, u32[]{:S(2)}, u32[]{:S(2)}) collective-permute-start(bf16[16,2048]{1,0:T(8,128)(2,1)S(1)} %collective-permute-done.1.refs_2_), channel_id=1, source_target_pairs={{0,16},{16,0},{1,17},{17,1},{2,18},{18,2},{3,19},{19,3},{4,20},{20... | collective-permute-start | bytes 196616 | tf_op jit(solution)/shard_map/ppermute | solution.py:212
  24.1 1.6 %collective-permute-start.8 = (bf16[2,64,1024]{2,1,0:T(8,128)(2,1)S(1)}, bf16[2,64,1024]{2,1,0:T(8,128)(2,1)S(1)}, u32[]{:S(2)}, u32[]{:S(2)}) collective-permute-start(bf16[2,64,1024]{2,1,0:T(8,128)(2,1)S(1)} %get-tuple-element.24), channel_id=1, source_target_pairs={{0,1},{1,0},{2,3},{3,2},{4,5},{5,4},{6,7},{7,6},{8,9},{9,8},{10,11... | collective-permute-start | bytes 786440 | tf_op jit(solution)/shard_map/ppermute | solution.py:212
  24.2 3.1 %collective-permute-start.7 = (bf16[2,64,1024]{2,1,0:T(8,128)(2,1)S(1)}, bf16[2,64,1024]{2,1,0:T(8,128)(2,1)S(1)}, u32[]{:S(2)}, u32[]{:S(2)}) collective-permute-start(bf16[2,64,1024]{2,1,0:T(8,128)(2,1)S(1)} %get-tuple-element.22), channel_id=1, source_target_pairs={{0,1},{1,0},{2,3},{3,2},{4,5},{5,4},{6,7},{7,6},{8,9},{9,8},{10,11... | collective-permute-start | bytes 786440 | tf_op jit(solution)/shard_map/ppermute | solution.py:212
  25.8 8.1 %collective-permute-start.13 = (bf16[2,32,1024]{2,1,0:T(8,128)(2,1)S(1)}, bf16[2,32,1024]{2,1,0:T(8,128)(2,1)S(1)}, u32[]{:S(2)}, u32[]{:S(2)}) collective-permute-start(bf16[2,32,1024]{2,1,0:T(8,128)(2,1)S(1)} %add_convert_fusion.1.refs_11_), channel_id=1, source_target_pairs={{0,2},{1,3},{2,0},{3,1},{4,6},{5,7},{6,4},{7,5},{8,10},{9,11},{10,... | collective-permute-start | bytes 393224 | tf_op jit(solution)/shard_map/ppermute | solution.py:212
  27.3 22.1 %slice-start = ((s8[27262976]{0:T(1024)(128)(4,1)}), s8[4194304]{0:T(1024)(128)(4,1)S(1)}, s32[]{:S(2)}) async-start(s8[27262976]{0:T(1024)(128)(4,1)} %bitcast.32), calls=%async_computation | async-start | bytes 8388608
  27.4 22.1 %slice-start.1 = ((s8[27262976]{0:T(1024)(128)(4,1)}), s8[4194304]{0:T(1024)(128)(4,1)S(1)}, s32[]{:S(2)}) async-start(s8[27262976]{0:T(1024)(128)(4,1)} %bitcast.32), calls=%async_computation.1 | async-start | bytes 8388608
  27.4 22.1 %slice-start.2 = ((s8[27262976]{0:T(1024)(128)(4,1)}), s8[4194304]{0:T(1024)(128)(4,1)S(1)}, s32[]{:S(2)}) async-start(s8[27262976]{0:T(1024)(128)(4,1)} %bitcast.32), calls=%async_computation.2 | async-start | bytes 8388608
  27.4 22.1 %slice-start.3 = ((s8[27262976]{0:T(1024)(128)(4,1)}), s8[4194304]{0:T(1024)(128)(4,1)S(1)}, s32[]{:S(2)}) async-start(s8[27262976]{0:T(1024)(128)(4,1)} %bitcast.32), calls=%async_computation.3 | async-start | bytes 8388608
  27.4 22.1 %slice-start.4 = ((s8[27262976]{0:T(1024)(128)(4,1)}), s8[4194304]{0:T(1024)(128)(4,1)S(1)}, s32[]{:S(2)}) async-start(s8[27262976]{0:T(1024)(128)(4,1)} %bitcast.32), calls=%async_computation.4 | async-start | bytes 8388608
  27.4 22.0 %slice-start.5 = ((s8[27262976]{0:T(1024)(128)(4,1)}), s8[4194304]{0:T(1024)(128)(4,1)S(1)}, s32[]{:S(2)}) async-start(s8[27262976]{0:T(1024)(128)(4,1)} %bitcast.32), calls=%async_computation.5 | async-start | bytes 8388608
  27.4 22.0 %slice-start.6 = ((s8[27262976]{0:T(1024)(128)(4,1)}), s8[2097152]{0:T(1024)(128)(4,1)S(1)}, s32[]{:S(2)}) async-start(s8[27262976]{0:T(1024)(128)(4,1)} %bitcast.32), calls=%async_computation.6 | async-start | bytes 4194304
  27.4 7.7 %collective-permute-start.18 = (bf16[2,32,1024]{2,1,0:T(8,128)(2,1)S(1)}, bf16[2,32,1024]{2,1,0:T(8,128)(2,1)S(1)}, u32[]{:S(2)}, u32[]{:S(2)}) collective-permute-start(bf16[2,32,1024]{2,1,0:T(8,128)(2,1)S(1)} %add_convert_fusion.2.refs_10_), channel_id=1, source_target_pairs={{0,2},{1,3},{2,0},{3,1},{4,6},{5,7},{6,4},{7,5},{8,10},{9,11},{10,... | collective-permute-start | bytes 393224 | tf_op jit(solution)/shard_map/ppermute | solution.py:212
  33.8 2.5 %collective-permute-start.9 = (bf16[2,64,1280]{2,1,0:T(8,128)(2,1)S(1)}, bf16[2,64,1280]{2,1,0:T(8,128)(2,1)S(1)}, u32[]{:S(2)}, u32[]{:S(2)}) collective-permute-start(bf16[2,64,1280]{2,1,0:T(8,128)(2,1)S(1)} %get-tuple-element.26), channel_id=1, source_target_pairs={{0,1},{1,0},{2,3},{3,2},{4,5},{5,4},{6,7},{7,6},{8,9},{9,8},{10,11... | collective-permute-start | bytes 983048 | tf_op jit(solution)/shard_map/ppermute | solution.py:212
  34.1 4.1 %collective-permute-start.14 = (bf16[16,1024]{1,0:T(8,128)(2,1)S(1)}, bf16[16,1024]{1,0:T(8,128)(2,1)S(1)}, u32[]{:S(2)}, u32[]{:S(2)}) collective-permute-start(bf16[16,1024]{1,0:T(8,128)(2,1)S(1)} %get-tuple-element.36), channel_id=1, source_target_pairs={{0,16},{16,0},{1,17},{17,1},{2,18},{18,2},{3,19},{19,3},{4,20},{20... | collective-permute-start | bytes 98312 | tf_op jit(solution)/shard_map/ppermute | solution.py:212
  35.3 4.4 %collective-permute-start.19 = (bf16[16,1024]{1,0:T(8,128)(2,1)S(1)}, bf16[16,1024]{1,0:T(8,128)(2,1)S(1)}, u32[]{:S(2)}, u32[]{:S(2)}) collective-permute-start(bf16[16,1024]{1,0:T(8,128)(2,1)S(1)} %get-tuple-element.34), channel_id=1, source_target_pairs={{0,16},{16,0},{1,17},{17,1},{2,18},{18,2},{3,19},{19,3},{4,20},{20... | collective-permute-start | bytes 98312 | tf_op jit(solution)/shard_map/ppermute | solution.py:212
  36.4 7.1 %collective-permute-start.10 = (bf16[2,32,1280]{2,1,0:T(8,128)(2,1)S(1)}, bf16[2,32,1280]{2,1,0:T(8,128)(2,1)S(1)}, u32[]{:S(2)}, u32[]{:S(2)}) collective-permute-start(bf16[2,32,1280]{2,1,0:T(8,128)(2,1)S(1)} %add_convert_fusion), channel_id=1, source_target_pairs={{0,2},{1,3},{2,0},{3,1},{4,6},{5,7},{6,4},{7,5},{8,10},{9,11},{10,... | collective-permute-start | bytes 491528 | tf_op jit(solution)/shard_map/ppermute | solution.py:212
  38.1 7.2 %collective-permute-start.15 = (bf16[32,1024]{1,0:T(8,128)(2,1)S(1)}, bf16[32,1024]{1,0:T(8,128)(2,1)S(1)}, u32[]{:S(2)}, u32[]{:S(2)}) collective-permute-start(bf16[32,1024]{1,0:T(8,128)(2,1)S(1)} %pad_maximum_fusion.1.refs_0_), channel_id=1, source_target_pairs={{0,2},{1,3},{2,0},{3,1},{4,6},{5,7},{6,4},{7,5},{8,10},{9,11},{10,... | collective-permute-start | bytes 196616 | tf_op jit(solution)/shard_map/ppermute | solution.py:212
  39.7 5.6 %collective-permute-start.20 = (bf16[32,1024]{1,0:T(8,128)(2,1)S(1)}, bf16[32,1024]{1,0:T(8,128)(2,1)S(1)}, u32[]{:S(2)}, u32[]{:S(2)}) collective-permute-start(bf16[32,1024]{1,0:T(8,128)(2,1)S(1)} %pad_maximum_fusion.2.refs_0_), channel_id=1, source_target_pairs={{0,2},{1,3},{2,0},{3,1},{4,6},{5,7},{6,4},{7,5},{8,10},{9,11},{10,... | collective-permute-start | bytes 196616 | tf_op jit(solution)/shard_map/ppermute | solution.py:212
  43.7 4.1 %collective-permute-start.11 = (bf16[16,1280]{1,0:T(8,128)(2,1)S(1)}, bf16[16,1280]{1,0:T(8,128)(2,1)S(1)}, u32[]{:S(2)}, u32[]{:S(2)}) collective-permute-start(bf16[16,1280]{1,0:T(8,128)(2,1)S(1)} %get-tuple-element.32), channel_id=1, source_target_pairs={{0,16},{16,0},{1,17},{17,1},{2,18},{18,2},{3,19},{19,3},{4,20},{20... | collective-permute-start | bytes 122888 | tf_op jit(solution)/shard_map/ppermute | solution.py:212
  44.8 6.8 %collective-permute-start.16 = (bf16[32,1024]{1,0:T(8,128)(2,1)S(1)}, bf16[32,1024]{1,0:T(8,128)(2,1)S(1)}, u32[]{:S(2)}, u32[]{:S(2)}) collective-permute-start(bf16[32,1024]{1,0:T(8,128)(2,1)S(1)} %pad_maximum_fusion.1.refs_0_), channel_id=1, source_target_pairs={{0,1},{1,0},{2,3},{3,2},{4,5},{5,4},{6,7},{7,6},{8,9},{9,8},{10,11... | collective-permute-start | bytes 196616 | tf_op jit(solution)/shard_map/ppermute | solution.py:212
  44.8 4.6 %collective-permute-start.21 = (bf16[32,1024]{1,0:T(8,128)(2,1)S(1)}, bf16[32,1024]{1,0:T(8,128)(2,1)S(1)}, u32[]{:S(2)}, u32[]{:S(2)}) collective-permute-start(bf16[32,1024]{1,0:T(8,128)(2,1)S(1)} %pad_maximum_fusion.2.refs_0_), channel_id=1, source_target_pairs={{0,1},{1,0},{2,3},{3,2},{4,5},{5,4},{6,7},{7,6},{8,9},{9,8},{10,11... | collective-permute-start | bytes 196616 | tf_op jit(solution)/shard_map/ppermute | solution.py:212
  45.3 6.3 %collective-permute-start.17 = (bf16[32,1024]{1,0:T(8,128)(2,1)S(1)}, bf16[32,1024]{1,0:T(8,128)(2,1)S(1)}, u32[]{:S(2)}, u32[]{:S(2)}) collective-permute-start(bf16[32,1024]{1,0:T(8,128)(2,1)S(1)} %collective-permute-done.15.refs_1_), channel_id=1, source_target_pairs={{0,1},{1,0},{2,3},{3,2},{4,5},{5,4},{6,7},{7,6},{8,9},{9,8},{10,11... | collective-permute-start | bytes 196616 | tf_op jit(solution)/shard_map/ppermute | solution.py:212
  45.3 4.1 %collective-permute-start.22 = (bf16[32,1024]{1,0:T(8,128)(2,1)S(1)}, bf16[32,1024]{1,0:T(8,128)(2,1)S(1)}, u32[]{:S(2)}, u32[]{:S(2)}) collective-permute-start(bf16[32,1024]{1,0:T(8,128)(2,1)S(1)} %collective-permute-done.20.refs_1_), channel_id=1, source_target_pairs={{0,1},{1,0},{2,3},{3,2},{4,5},{5,4},{6,7},{7,6},{8,9},{9,8},{10,11... | collective-permute-start | bytes 196616 | tf_op jit(solution)/shard_map/ppermute | solution.py:212
  47.7 6.0 %collective-permute-start.12 = (bf16[32,1280]{1,0:T(8,128)(2,1)S(1)}, bf16[32,1280]{1,0:T(8,128)(2,1)S(1)}, u32[]{:S(2)}, u32[]{:S(2)}) collective-permute-start(bf16[32,1280]{1,0:T(8,128)(2,1)S(1)} %pad_maximum_fusion.refs_0_), channel_id=1, source_target_pairs={{0,2},{1,3},{2,0},{3,1},{4,6},{5,7},{6,4},{7,5},{8,10},{9,11},{10,... | collective-permute-start | bytes 245768 | tf_op jit(solution)/shard_map/ppermute | solution.py:212
  53.8 1.5 %collective-permute-start.23 = (bf16[64,1280]{1,0:T(8,128)(2,1)S(1)}, bf16[64,1280]{1,0:T(8,128)(2,1)S(1)}, u32[]{:S(2)}, u32[]{:S(2)}) collective-permute-start(bf16[64,1280]{1,0:T(8,128)(2,1)S(1)} %join.1), channel_id=1, source_target_pairs={{0,1},{1,0},{2,3},{3,2},{4,5},{5,4},{6,7},{7,6},{8,9},{9,8},{10,11... | collective-permute-start | bytes 491528 | tf_op jit(solution)/shard_map/ppermute | solution.py:212
  57.8 6.3 %collective-permute-start.24 = (bf16[16,2048]{1,0:T(8,128)(2,1)S(1)}, bf16[16,2048]{1,0:T(8,128)(2,1)S(1)}, u32[]{:S(2)}, u32[]{:S(2)}) collective-permute-start(bf16[16,2048]{1,0:T(8,128)(2,1)S(1)} %get-tuple-element.28), channel_id=1, source_target_pairs={{0,12},{4,8},{8,4},{12,0},{1,13},{5,9},{9,5},{13,1},{2,14},{6,10},... | collective-permute-start | bytes 196616 | tf_op jit(solution)/shard_map/ppermute | solution.py:212
  60.5 6.7 %collective-permute-start.25 = (bf16[16,2048]{1,0:T(8,128)(2,1)S(1)}, bf16[16,2048]{1,0:T(8,128)(2,1)S(1)}, u32[]{:S(2)}, u32[]{:S(2)}) collective-permute-start(bf16[16,2048]{1,0:T(8,128)(2,1)S(1)} %get-tuple-element.29), channel_id=1, source_target_pairs={{0,8},{4,12},{8,0},{12,4},{1,9},{5,13},{9,1},{13,5},{2,10},{6,14},... | collective-permute-start | bytes 196616 | tf_op jit(solution)/shard_map/ppermute | solution.py:212
  60.9 6.4 %collective-permute-start.26 = (bf16[16,2048]{1,0:T(8,128)(2,1)S(1)}, bf16[16,2048]{1,0:T(8,128)(2,1)S(1)}, u32[]{:S(2)}, u32[]{:S(2)}) collective-permute-start(bf16[16,2048]{1,0:T(8,128)(2,1)S(1)} %get-tuple-element.30), channel_id=1, source_target_pairs={{0,4},{4,0},{8,12},{12,8},{1,5},{5,1},{9,13},{13,9},{2,6},{6,2},{1... | collective-permute-start | bytes 196616 | tf_op jit(solution)/shard_map/ppermute | solution.py:212

commit v6 on v5

v6 whole, which is shorter than its diff:
```python
import functools

import jax
import jax.numpy as jnp
from jax import lax
from jax.experimental import pallas as pl
from jax.experimental.pallas import tpu as pltpu
from jax.sharding import PartitionSpec as P

TILE = 256
LAST = 3
ROWS = 16


def plain(tokens, gate_weight, up_weight, down_weight):
    piece = lax.all_gather(tokens, "hid", axis=0, tiled=True)
    gate_rows = jnp.dot(piece, gate_weight, preferred_element_type=jnp.float32)
    up_rows = jnp.dot(piece, up_weight, preferred_element_type=jnp.float32)
    partial_terms = jnp.stack([gate_rows, up_rows], 0)
    summed = lax.psum(partial_terms.astype(jnp.bfloat16), "wid").astype(jnp.float32)
    hidden = (jax.nn.silu(summed[0]) * summed[1]).astype(jnp.bfloat16)
    return lax.psum_scatter(
        jnp.dot(hidden, down_weight, preferred_element_type=jnp.float32).astype(jnp.bfloat16),
        "hid",
        scatter_dimension=0,
        tiled=True,
    )


def pieces_of(width, most):
    first = width % most
    edges = ([0] if first else []) + list(range(first, width + 1, most))
    return list(zip(edges[:-1], edges[1:]))


def place(wid, d):
    step = wid ^ d
    return (step % 2) * 2 + step // 2


def spec(space):
    return pl.BlockSpec(memory_space=space)


def params(mib):
    return pltpu.CompilerParams(vmem_limit_bytes=mib * 2**20)


def column_copies(source_ref, out_ref, segments, sems):
    copies, cuts, at = [], [], 0
    for start, width in segments:
        for a, b in pieces_of(width, 2 * TILE):
            source = source_ref.at[:, pl.ds(pl.multiple_of(start + a, TILE), b - a)]
            copies.append(pltpu.make_async_copy(source, out_ref.at[:, at + a : at + b], sems.at[len(copies)]))
            cuts.append((at + a, at + b))
        at += width
    return copies, cuts


def fetch_kernel(first, where, gate_ref, up_ref, tokens_ref, gate_out, up_out, tokens_out, sems):
    copies = [pltpu.make_async_copy(tokens_ref, tokens_out, sems.at[2, 0])]
    for k, (source, out) in enumerate(((gate_ref, gate_out), (up_ref, up_out))):
        copies += column_copies(source, out, [(where[0] + first, out.shape[1])], sems.at[k])[0]
    for copy in copies:
        copy.start()
    for copy in copies:
        copy.wait()


def fetch(where, gate, up, tokens, first, width):
    depth = gate.shape[0]
    return pl.pallas_call(
        functools.partial(fetch_kernel, first),
        in_specs=[spec(pltpu.SMEM)] + [spec(pltpu.HBM)] * 3,
        out_specs=[spec(pltpu.VMEM)] * 3,
        out_shape=[pltpu.VMEM(x, jnp.bfloat16) for x in ((depth, width), (depth, width), tokens.shape)],
        scratch_shapes=[pltpu.SemaphoreType.DMA((3, len(pieces_of(width, 2 * TILE))))],
        compiler_params=params(1),
        cost_estimate=pl.CostEstimate(flops=0, bytes_accessed=4 * depth * width, transcendentals=0),
        name="fetch",
    )(where, gate, up, tokens)


def join_kernel(n, first, *refs):
    out_ref, at = refs[-1], 0
    for ref in refs[:n]:
        out_ref[at : at + ref.shape[0], :] = ref[:, first : first + out_ref.shape[1]]
        at += ref.shape[0]


def join(arrays, behind, first=0, width=None):
    rows, width = sum(a.shape[0] for a in arrays), width or arrays[0].shape[1]
    return pl.pallas_call(
        functools.partial(join_kernel, len(arrays), first),
        in_specs=[spec(pltpu.VMEM)] * len(arrays) + [spec(pl.ANY)] * len(behind),
        out_specs=spec(pltpu.VMEM),
        out_shape=jax.ShapeDtypeStruct((rows, width), arrays[0].dtype),
        compiler_params=params(1),
        cost_estimate=pl.CostEstimate(flops=0, bytes_accessed=4 * rows * width, transcendentals=0),
        name="join",
    )(*arrays, *behind)


def gate_up_kernel(n_arrays, n_pairs, segments, where, *refs):
    arrays, weights = refs[:n_arrays], refs[n_arrays : n_arrays + 2 * n_pairs]
    if segments:
        mine_ref, theirs_ref, x_ref, w_ref, sems = refs[-5:]
        copies = [column_copies(weights[k], w_ref.at[k], segments, sems.at[k]) for k in range(2)]
        cuts = copies[0][1]
        for i in range(len(cuts)):
            for k in range(2):
                copies[k][0][i].start()
    else:
        mine_ref, theirs_ref, x_ref = refs[-3:]
        step = weights[0].shape[1]
        cuts = [(p * step + a, p * step + b) for p in range(n_pairs) for a, b in pieces_of(step, 2 * TILE)]
    per = x_ref.shape[0] // (4 * ROWS)
    b = 0
    for array in arrays:
        for at in range(0, array.shape[0], ROWS):
            to = (place(where[1], b % 4) * per + b // 4) * ROWS
            x_ref[pl.ds(pl.multiple_of(to, ROWS), ROWS), :] = array[at : at + ROWS, :]
            b += 1
    half = x_ref.shape[0] // 2
    for i, (a, b) in enumerate(cuts):
        for k in range(2):
            if segments:
                copies[k][0][i].wait()
                weight = w_ref[k, :, a:b]
            else:
                p = a // step
                weight = weights[2 * p + k][:, a - p * step : b - p * step]
            part = jnp.dot(x_ref[...], weight, preferred_element_type=jnp.float32).astype(jnp.bfloat16)
            mine_ref[k, :, a:b] = part[:half]
            theirs_ref[k, :, a:b] = part[half:]


def gate_up(where, arrays, weights, segments, behind):
    depth = weights[0].shape[0]
    width = sum(w for _, w in segments) if segments else sum(w.shape[1] for w in weights[::2])
    total = sum(a.shape[0] for a in arrays)
    scratch = [pltpu.VMEM((total, depth), jnp.bfloat16)]
    if segments:
        n_cuts = sum(len(pieces_of(w, 2 * TILE)) for _, w in segments)
        scratch.append(pltpu.VMEM((2, depth, width), jnp.bfloat16))
        scratch.append(pltpu.SemaphoreType.DMA((2, n_cuts)))
    return pl.pallas_call(
        functools.partial(gate_up_kernel, len(arrays), len(weights) // 2, segments),
        in_specs=[spec(pltpu.SMEM)]
        + [spec(pltpu.VMEM)] * len(arrays)
        + [spec(pltpu.HBM if segments else pltpu.VMEM)] * len(weights)
        + [spec(pl.ANY)] * len(behind),
        out_specs=[spec(pltpu.VMEM)] * 2,
        scratch_shapes=scratch,
        out_shape=[jax.ShapeDtypeStruct((2, total // 2, width), jnp.bfloat16)] * 2,
        compiler_params=params(16 if segments else 4),
        cost_estimate=pl.CostEstimate(
            flops=4 * total * depth * width, bytes_accessed=4 * depth * width, transcendentals=0
        ),
        name="gate_up",
    )(where, *arrays, *weights, *behind)


def combine_kernel(n_outs, mine_ref, got_ref, chip_ref, *refs):
    outs = refs[-n_outs:]
    rows = chip_ref.shape[1]
    for a, b in pieces_of(chip_ref.shape[2], TILE):
        gate, up = (
            mine_ref[k, :rows, a:b].astype(jnp.float32)
            + got_ref[k, :rows, a:b].astype(jnp.float32)
            + chip_ref[k, :, a:b].astype(jnp.float32)
            for k in range(2)
        )
        hidden = (gate / (1 + jnp.exp(-gate)) * up).astype(jnp.bfloat16)
        for i, out in enumerate(outs):
            out[:, a:b] = hidden[i * ROWS : (i + 1) * ROWS]


def combine(mine, got, from_chip, behind):
    _, rows, width = from_chip.shape
    n_outs = rows // ROWS
    return pl.pallas_call(
        functools.partial(combine_kernel, n_outs),
        in_specs=[spec(pltpu.VMEM)] * 3 + [spec(pl.ANY)] * len(behind),
        out_specs=[spec(pltpu.VMEM)] * n_outs,
        out_shape=[jax.ShapeDtypeStruct((ROWS, width), jnp.bfloat16)] * n_outs,
        compiler_params=params(1),
        cost_estimate=pl.CostEstimate(
            flops=10 * rows * width, bytes_accessed=14 * rows * width, transcendentals=rows * width
        ),
        name="combine",
    )(mine, got, from_chip, *behind)


def down_kernel(n_pieces, has_acc, last, first, half, where, *refs):
    pieces, refs = refs[:n_pieces], refs[n_pieces:]
    down_ref, refs = refs[0], refs[1:]
    prev_ref, refs = (refs[0], refs[1:]) if has_acc else (None, refs)
    outs, (acc_ref, lhs_ref) = refs[:-2], refs[-2:]
    depth = lhs_ref.shape[2]
    p = 0
    for piece in pieces:
        for at in range(0, piece.shape[0], ROWS if last else 2 * ROWS):
            for k in range(2):
                if last:
                    block = piece[at : at + ROWS, k * depth : (k + 1) * depth]
                else:
                    block = piece[at + k * ROWS : at + (k + 1) * ROWS, :]
                lhs_ref[k, p * ROWS : (p + 1) * ROWS, :] = block
            p += 1
    if last:
        starts = [first, half + first]
    else:
        starts = [where[0] + first, half - where[0] + first]
    for a, b in pieces_of(down_ref.shape[1], 2 * TILE):
        part = prev_ref[:, a:b] if has_acc else 0.0
        for k in range(2):
            rows = pl.ds(pl.multiple_of(starts[k], TILE), depth)
            part += jnp.dot(lhs_ref[k], down_ref[rows, a:b], preferred_element_type=jnp.float32)
        acc_ref[:, a:b] = part
    if last:
        for d, out in enumerate(outs):
            source = pl.multiple_of(place(where[1], d) * ROWS, ROWS)
            out[...] = acc_ref[pl.ds(source, ROWS), :].astype(out.dtype)


def down(where, pieces, down_weight, prev, first, depth, last):
    width = down_weight.shape[1]
    total = 4 * ROWS
    args = [*pieces, down_weight] + ([] if prev is None else [prev])
    sums = jax.ShapeDtypeStruct((total, width), jnp.float32)
    scratch = [pltpu.VMEM((2, total, depth), jnp.bfloat16)]
    if last:
        scratch = [pltpu.VMEM(sums.shape, sums.dtype)] + scratch
    return pl.pallas_call(
        functools.partial(
            down_kernel, len(pieces), prev is not None, last, first, down_weight.shape[0] // 2
        ),
        in_specs=[spec(pltpu.SMEM)] + [spec(pltpu.VMEM)] * len(args),
        out_specs=[spec(pltpu.VMEM)] * 4 if last else spec(pltpu.VMEM),
        scratch_shapes=scratch,
        out_shape=[jax.ShapeDtypeStruct((ROWS, width), jnp.bfloat16)] * 4 if last else sums,
        compiler_params=params(4),
        cost_estimate=pl.CostEstimate(
            flops=4 * total * width * depth, bytes_accessed=4 * width * depth, transcendentals=0
        ),
        name="down",
    )(where, *args)


def split_by_rep(tokens, gate_weight, up_weight, down_weight):
    rep, wid = lax.axis_index("rep"), lax.axis_index("wid")
    f32, bf16 = jnp.float32, jnp.bfloat16
    half = gate_weight.shape[1] // 2
    where = jnp.stack([rep * half, wid]).astype(jnp.int32)

    def swap(x, axis, step):
        n = {"rep": 2, "hid": 4, "wid": 4}[axis]
        return lax.ppermute(x, axis, [(i, i ^ step) for i in range(n)])

    tiles = half // TILE
    bounds = [0, (tiles - LAST) // 2 * TILE, (tiles - LAST) * TILE, half]
    widths = [b - a for a, b in zip(bounds[:-1], bounds[1:])]
    gate_weight, up_weight, hbm_tokens = (
        pltpu.with_memory_space_constraint(w, pltpu.HBM) for w in (gate_weight, up_weight, tokens)
    )
    down_weight = pltpu.with_memory_space_constraint(down_weight, pltpu.VMEM)

    far_own = swap(tokens, "rep", 1)
    by_hid = [swap(tokens, "hid", d) for d in (3, 2, 1)][::-1]
    early = [fetch(where, gate_weight, up_weight, hbm_tokens, bounds[c], widths[c]) for c in range(2)]
    own = early[0][2]
    near = join(by_hid, [own, far_own])
    far = swap(near, "rep", 1)

    def reduce_pair(mine, theirs):
        got = swap(theirs, "wid", 1)
        rows = mine.shape[1] // 2
        return mine, got, (mine[:, rows:].astype(f32) + got[:, rows:].astype(f32)).astype(bf16)

    weights = [w for fetched in early for w in fetched[:2]]
    *parts, to_chip = reduce_pair(*gate_up(where, [own, near, far_own, far], weights, [], []))
    from_chip = swap(to_chip, "wid", 2)
    segments = [(bounds[2], widths[2]), (half + bounds[2], widths[2])]
    *last_parts, last_to_chip = reduce_pair(
        *gate_up(where, [own, near], [gate_weight, up_weight], segments, [to_chip])
    )
    last_from_chip = swap(last_to_chip, "wid", 2)

    keep, give = combine(*parts, from_chip, [last_to_chip])
    got = swap(give, "rep", 1)
    acc = None
    for c in range(2):
        mixed = join([keep, got], [], bounds[c], widths[c])
        other = swap(mixed, "wid", 2)
        pieces = [mixed, other, swap(mixed, "wid", 1), swap(other, "wid", 1)]
        acc = down(where, pieces, down_weight, acc, bounds[c], widths[c], False)
        if c == 0:
            first_sum = acc
    (mixed,) = combine(*last_parts, last_from_chip, [])
    other = swap(mixed, "wid", 2)
    pieces = [mixed, other, swap(join([mixed, other], [first_sum]), "wid", 1)]
    acc = down(where, pieces, down_weight, acc, bounds[2], widths[2], True)

    mixed = acc[0].astype(f32)
    for d in (3, 2, 1):
        mixed = mixed + swap(acc[d], "hid", d).astype(f32)
    return mixed.astype(bf16)


def solution(mesh):
    n_rep, n_hid, n_wid = (mesh.shape[a] for a in ("rep", "hid", "wid"))

    def on_device(tokens, gate_weight, up_weight, down_weight):
        fits = (
            (n_rep, n_hid, n_wid) == (2, 4, 4)
            and gate_weight.shape[1] % (n_rep * TILE) == 0
            and tokens.shape[0] == ROWS
        )
        if not fits:
            return plain(tokens, gate_weight, up_weight, down_weight)
        return split_by_rep(tokens, gate_weight, up_weight, down_weight)

    return jax.shard_map(
        on_device,
        mesh=mesh,
        in_specs=(P(("rep", "hid"), "wid"), P("wid", "hid"), P("wid", "hid"), P("hid", "wid")),
        out_specs=P(("rep", "hid"), "wid"),
        check_vma=False,
    )
```

time: 68.1 us -> 70.4 us (1.034)
  starting transfers between devices: 27.6 us -> 21.5 us
  waiting for transfers between devices: 16 us -> 20.6 us
  Pallas kernels: 22.9 us -> 27 us
    ppermute x27 -> x21, starting transfers between devices: 27.6 us -> 21.5 us  [swap(): return lax.ppermute(x, axis, [(i, i ^ step) for i in range(n)])]
    ppermute x27 -> x21, waiting for transfers between devices: 16 us -> 20.6 us  [swap(): return lax.ppermute(x, axis, [(i, i ^ step) for i in range(n)])]
    pallas_call x8 -> x13, Pallas kernels: 22.9 us -> 27 us  [the longest x2 10.2 us: fetch(): pl.pallas_call(functools.partial(fetch_kernel, first), in_specs=[spec(plt...]
  transfers between devices with their start and end apart: 27 -> 21, of which waited for: 10 -> 7; matrix products, arithmetic and copies ran while one was open for 1% -> 0% of each run, Pallas kernels for 25% -> 22%
where the time goes in v6:
time: 70.4 us; the launch traced here: 70.3 us
  Pallas kernels  27 us (38%)
  starting transfers between devices  21.5 us (31%)
  waiting for transfers between devices  20.6 us (29%)
  other arithmetic  0.84 us (1%)
    ppermute x21, starting transfers between devices, swap(): return lax.ppermute(x, axis, [(i, i ^ step) for i in range(n)])  21.5 us
    ppermute x21, waiting for transfers between devices, swap(): return lax.ppermute(x, axis, [(i, i ^ step) for i in range(n)])  20.6 us
    pallas_call x2, Pallas kernels, fetch(): pl.pallas_call(functools.partial(fetch_kernel, first), in_specs=[spec(plt...  10.2 us
    pallas_call x2, Pallas kernels, gate_up(): pl.pallas_call(functools.partial(gate_up_kernel, len(arrays), len(weights...  9.76 us
    pallas_call x3, Pallas kernels, down(): pl.pallas_call(functools.partial(down_kernel, len(pieces), prev is not No...  6.69 us
  transfers between devices with their start and end apart: 21, of which 7 were waited for; matrix products, arithmetic and copies ran while one was open for 0% of the time, Pallas kernels for 22%

profile of v6, /device:TPU:0, one launch (start us, length us, event | category | flops | bytes accessed | tf_op | source)
XLA Modules:
  0.0 70.3 jit_solution(1138211521803667758)
XLA Ops:
  0.0 5.0 %collective-permute-start.2 = (bf16[16,2048]{1,0:T(8,128)(2,1)}, bf16[16,2048]{1,0:T(8,128)(2,1)S(1)}, u32[]{:S(2)}, u32[]{:S(2)}) collective-permute-start(bf16[16,2048]{1,0:T(8,128)(2,1)} %tokens_ref.3), channel_id=1, source_target_pairs={{0,12},{4,8},{8,4},{12,0},{1,13},{5,9},{9,5},{13,1},{2,14},{6,10},... | collective-permute-start | bytes 196616 | tf_op jit(solution)/shard_map/ppermute | solution.py:259
  5.0 0.0 collective-permute-start.1
  5.1 0.6 collective-permute-start
  5.6 1.7 %collective-permute-start.3 = (bf16[16,2048]{1,0:T(8,128)(2,1)}, bf16[16,2048]{1,0:T(8,128)(2,1)S(1)}, u32[]{:S(2)}, u32[]{:S(2)}) collective-permute-start(bf16[16,2048]{1,0:T(8,128)(2,1)} %tokens_ref.3), channel_id=1, source_target_pairs={{0,16},{16,0},{1,17},{17,1},{2,18},{18,2},{3,19},{19,3},{4,20},{20... | collective-permute-start | bytes 196616 | tf_op jit(solution)/shard_map/ppermute | solution.py:259
  7.4 0.1 pad_add_fusion.where
  7.4 4.8 %fetch.2 = (bf16[2048,1280]{1,0:T(8,128)(2,1)S(1)}, bf16[2048,1280]{1,0:T(8,128)(2,1)S(1)}, bf16[16,2048]{1,0:T(8,128)(2,1)S(1)}) custom-call(s32[2]{0:T(128)S(1)} %pad_add_fusion.where, bf16[2048,6656]{1,0:T(8,128)(2,1)} %refs_2_.1, bf16[2048,6656]{1,0:T(8,128)(2,1)} %refs_3_.2, bf16[16,2048]{1,0:T(8,128)(2,1)} %tokens_ref.3), custom_call_target="tpu_custom_call" | custom-call | bytes 10485760 | tf_op jit(solution)/shard_map/fetch/pallas_call | solution.py:72
  12.3 0.0 collective-permute-done.1.refs_1_
  12.3 0.0 collective-permute-done.refs_0_
  12.3 0.4 collective-permute-start.4
  12.7 5.4 %fetch.3 = (bf16[2048,1280]{1,0:T(8,128)(2,1)S(1)}, bf16[2048,1280]{1,0:T(8,128)(2,1)S(1)}, bf16[16,2048]{1,0:T(8,128)(2,1)}) custom-call(s32[2]{0:T(128)S(1)} %pad_add_fusion.where, bf16[2048,6656]{1,0:T(8,128)(2,1)} %refs_2_.1, bf16[2048,6656]{1,0:T(8,128)(2,1)} %refs_3_.2, bf16[16,2048]{1,0:T(8,128)(2,1)} %tokens_ref.3), custom_call_target="tpu_custom_call" | custom-call | bytes 10485760 | tf_op jit(solution)/shard_map/fetch/pallas_call | solution.py:72
  18.1 0.0 collective-permute-done.4.refs_3_
  18.1 3.6 %gate_up.2 = (bf16[2,64,2560]{2,1,0:T(8,128)(2,1)S(1)}, bf16[2,64,2560]{2,1,0:T(8,128)(2,1)S(1)}) custom-call(s32[2]{0:T(128)S(1)} %pad_add_fusion.where, bf16[16,2048]{1,0:T(8,128)(2,1)S(1)} %get-tuple-element.20.refs_3_.refs_0_, bf16[48,2048]{1,0:T(8,128)(2,1)S(1)} %join.4.refs_1_, bf16[16,2048]{1,0:T(8,128)(2,1)S(1)} %collective-permute-done.3.refs_4_.refs_2_, ...), custom_call_target="tpu_custom_call" | custom-call | flops 2684354560 | bytes 20971520 | tf_op jit(solution)/shard_map/gate_up/pallas_call | solution.py:147
  21.7 0.1 collective-permute-start.5
  21.8 2.1 %collective-permute-done.5.got_ref = bf16[2,64,2560]{2,1,0:T(8,128)(2,1)S(1)} collective-permute-done((bf16[2,64,2560]{2,1,0:T(8,128)(2,1)S(1)}, bf16[2,64,2560]{2,1,0:T(8,128)(2,1)S(1)}, u32[]{:S(2)}, u32[]{:S(2)}) %collective-permute-start.5) | collective-permute-done | bytes 655392 | tf_op jit(solution)/shard_map/ppermute | solution.py:259
  23.9 0.1 add_convert_fusion.refs_4_
  23.9 0.0 slice-start.1
  24.0 0.0 slice-start.2
  24.0 0.0 slice-start.3
  24.0 0.0 slice-start.5
  24.0 0.0 slice-start.6
  24.0 6.2 %gate_up.3 = (bf16[2,32,1536]{2,1,0:T(8,128)(2,1)S(1)}, bf16[2,32,1536]{2,1,0:T(8,128)(2,1)S(1)}) custom-call(s32[2]{0:T(128)S(1)} %pad_add_fusion.where, bf16[16,2048]{1,0:T(8,128)(2,1)S(1)} %get-tuple-element.20.refs_3_.refs_0_, bf16[48,2048]{1,0:T(8,128)(2,1)S(1)} %join.4.refs_1_, bf16[2048,6656]{1,0:T(8,128)(2,1)} %refs_2_.1, ...), custom_call_target="tpu_custom_call" | custom-call | flops 805306368 | bytes 12582912 | tf_op jit(solution)/shard_map/gate_up/pallas_call | solution.py:147
  30.2 0.2 collective-permute-start.6
  30.4 1.7 %collective-permute-start.9 = (bf16[2,32,2560]{2,1,0:T(8,128)(2,1)S(1)}, bf16[2,32,2560]{2,1,0:T(8,128)(2,1)S(1)}, u32[]{:S(2)}, u32[]{:S(2)}) collective-permute-start(bf16[2,32,2560]{2,1,0:T(8,128)(2,1)S(1)} %add_convert_fusion.refs_4_), channel_id=1, source_target_pairs={{0,2},{1,3},{2,0},{3,1},{4,6},{5,7},{6,4},{7,5},{8,10},{9,11},{10,... | collective-permute-start | bytes 983048 | tf_op jit(solution)/shard_map/ppermute | solution.py:259
  32.2 8.2 %collective-permute-done.9.chip_ref = bf16[2,32,2560]{2,1,0:T(8,128)(2,1)S(1)} collective-permute-done((bf16[2,32,2560]{2,1,0:T(8,128)(2,1)S(1)}, bf16[2,32,2560]{2,1,0:T(8,128)(2,1)S(1)}, u32[]{:S(2)}, u32[]{:S(2)}) %collective-permute-start.9) | collective-permute-done | bytes 327712 | tf_op jit(solution)/shard_map/ppermute | solution.py:259
  40.4 0.2 combine.3
  40.6 1.8 %collective-permute-start.10 = (bf16[16,2560]{1,0:T(8,128)(2,1)S(1)}, bf16[16,2560]{1,0:T(8,128)(2,1)S(1)}, u32[]{:S(2)}, u32[]{:S(2)}) collective-permute-start(bf16[16,2560]{1,0:T(8,128)(2,1)S(1)} %get-tuple-element.30), channel_id=1, source_target_pairs={{0,16},{16,0},{1,17},{17,1},{2,18},{18,2},{3,19},{19,3},{4,20},{20... | collective-permute-start | bytes 245768 | tf_op jit(solution)/shard_map/ppermute | solution.py:259
  42.4 2.7 %collective-permute-done.10.refs_1_ = bf16[16,2560]{1,0:T(8,128)(2,1)S(1)} collective-permute-done((bf16[16,2560]{1,0:T(8,128)(2,1)S(1)}, bf16[16,2560]{1,0:T(8,128)(2,1)S(1)}, u32[]{:S(2)}, u32[]{:S(2)}) %collective-permute-start.10) | collective-permute-done | bytes 81952 | tf_op jit(solution)/shard_map/ppermute | solution.py:259
  45.1 1.7 %collective-permute-start.11 = (bf16[32,1280]{1,0:T(8,128)(2,1)S(1)}, bf16[32,1280]{1,0:T(8,128)(2,1)S(1)}, u32[]{:S(2)}, u32[]{:S(2)}) collective-permute-start(bf16[32,1280]{1,0:T(8,128)(2,1)S(1)} %join.5.refs_0_), channel_id=1, source_target_pairs={{0,2},{1,3},{2,0},{3,1},{4,6},{5,7},{6,4},{7,5},{8,10},{9,11},{10,... | collective-permute-start | bytes 245768 | tf_op jit(solution)/shard_map/ppermute | solution.py:259
  46.8 0.3 collective-permute-start.7
  47.1 1.7 %collective-permute-start.15 = (bf16[32,1280]{1,0:T(8,128)(2,1)S(1)}, bf16[32,1280]{1,0:T(8,128)(2,1)S(1)}, u32[]{:S(2)}, u32[]{:S(2)}) collective-permute-start(bf16[32,1280]{1,0:T(8,128)(2,1)S(1)} %join.7.refs_0_), channel_id=1, source_target_pairs={{0,2},{1,3},{2,0},{3,1},{4,6},{5,7},{6,4},{7,5},{8,10},{9,11},{10,... | collective-permute-start | bytes 245768 | tf_op jit(solution)/shard_map/ppermute | solution.py:259
  48.9 1.5 %collective-permute-done.11.refs_1_ = bf16[32,1280]{1,0:T(8,128)(2,1)S(1)} collective-permute-done((bf16[32,1280]{1,0:T(8,128)(2,1)S(1)}, bf16[32,1280]{1,0:T(8,128)(2,1)S(1)}, u32[]{:S(2)}, u32[]{:S(2)}) %collective-permute-start.11) | collective-permute-done | bytes 81952 | tf_op jit(solution)/shard_map/ppermute | solution.py:259
  50.4 0.0 collective-permute-start.13
  50.4 1.1 %collective-permute-done.7.chip_ref = bf16[2,16,1536]{2,1,0:T(8,128)(2,1)S(1)} collective-permute-done((bf16[2,16,1536]{2,1,0:T(8,128)(2,1)S(1)}, bf16[2,16,1536]{2,1,0:T(8,128)(2,1)S(1)}, u32[]{:S(2)}, u32[]{:S(2)}) %collective-permute-start.7) | collective-permute-done | bytes 98336 | tf_op jit(solution)/shard_map/ppermute | solution.py:259
  51.4 0.1 combine.2.refs_0_
  51.5 1.2 %collective-permute-start.8 = (bf16[16,1536]{1,0:T(8,128)(2,1)S(1)}, bf16[16,1536]{1,0:T(8,128)(2,1)S(1)}, u32[]{:S(2)}, u32[]{:S(2)}) collective-permute-start(bf16[16,1536]{1,0:T(8,128)(2,1)S(1)} %combine.2.refs_0_), channel_id=1, source_target_pairs={{0,2},{1,3},{2,0},{3,1},{4,6},{5,7},{6,4},{7,5},{8,10},{9,11},{10,... | collective-permute-start | bytes 147464 | tf_op jit(solution)/shard_map/ppermute | solution.py:259
  52.7 0.0 collective-permute-start.16
  52.7 0.0 collective-permute-done.15.refs_1_
  52.7 0.5 collective-permute-start.17
  53.2 0.0 collective-permute-done.12.refs_2_
  53.3 2.5 %down.3.refs_2_.refs_5_ = f32[64,2048]{1,0:T(8,128)S(1)} custom-call(s32[2]{0:T(128)S(1)} %pad_add_fusion.where, bf16[32,1280]{1,0:T(8,128)(2,1)S(1)} %join.5.refs_0_, bf16[32,1280]{1,0:T(8,128)(2,1)S(1)} %collective-permute-done.11.refs_1_, bf16[32,1280]{1,0:T(8,128)(2,1)S(1)} %collective-permute-done.12.refs_2_, ...), custom_call_target="tpu_custom_call" | custom-call | flops 671088640 | bytes 10485760 | tf_op jit(solution)/shard_map/down/pallas_call | solution.py:235
  55.8 0.1 collective-permute-start.14
  55.9 2.5 %down.4.refs_4_ = f32[64,2048]{1,0:T(8,128)S(1)} custom-call(s32[2]{0:T(128)S(1)} %pad_add_fusion.where, bf16[32,1280]{1,0:T(8,128)(2,1)S(1)} %join.7.refs_0_, bf16[32,1280]{1,0:T(8,128)(2,1)S(1)} %collective-permute-done.15.refs_1_, bf16[32,1280]{1,0:T(8,128)(2,1)S(1)} %collective-permute-done.16.refs_2_, ...), custom_call_target="tpu_custom_call" | custom-call | flops 671088640 | bytes 10485760 | tf_op jit(solution)/shard_map/down/pallas_call | solution.py:235
  58.4 1.8 %down.5 = (bf16[16,2048]{1,0:T(8,128)(2,1)S(1)}, bf16[16,2048]{1,0:T(8,128)(2,1)S(1)}, bf16[16,2048]{1,0:T(8,128)(2,1)S(1)}, bf16[16,2048]{1,0:T(8,128)(2,1)S(1)}) custom-call(s32[2]{0:T(128)S(1)} %pad_add_fusion.where, bf16[16,1536]{1,0:T(8,128)(2,1)S(1)} %combine.2.refs_0_, bf16[16,1536]{1,0:T(8,128)(2,1)S(1)} %collective-permute-done.8.refs_1_, ...), custom_call_target="tpu_custom_call" | custom-call | flops 402653184 | bytes 6291456 | tf_op jit(solution)/shard_map/down/pallas_call | solution.py:235
  60.2 3.7 %collective-permute-start.18 = (bf16[16,2048]{1,0:T(8,128)(2,1)S(1)}, bf16[16,2048]{1,0:T(8,128)(2,1)S(1)}, u32[]{:S(2)}, u32[]{:S(2)}) collective-permute-start(bf16[16,2048]{1,0:T(8,128)(2,1)S(1)} %get-tuple-element.32), channel_id=1, source_target_pairs={{0,12},{4,8},{8,4},{12,0},{1,13},{5,9},{9,5},{13,1},{2,14},{6,10},... | collective-permute-start | bytes 196616 | tf_op jit(solution)/shard_map/ppermute | solution.py:259
  63.8 0.8 %collective-permute-start.20 = (bf16[16,2048]{1,0:T(8,128)(2,1)S(1)}, bf16[16,2048]{1,0:T(8,128)(2,1)S(1)}, u32[]{:S(2)}, u32[]{:S(2)}) collective-permute-start(bf16[16,2048]{1,0:T(8,128)(2,1)S(1)} %get-tuple-element.34), channel_id=1, source_target_pairs={{0,4},{4,0},{8,12},{12,8},{1,5},{5,1},{9,13},{13,9},{2,6},{6,2},{1... | collective-permute-start | bytes 196616 | tf_op jit(solution)/shard_map/ppermute | solution.py:259
  64.6 2.4 %collective-permute-done.18 = bf16[16,2048]{1,0:T(8,128)(2,1)S(1)} collective-permute-done((bf16[16,2048]{1,0:T(8,128)(2,1)S(1)}, bf16[16,2048]{1,0:T(8,128)(2,1)S(1)}, u32[]{:S(2)}, u32[]{:S(2)}) %collective-permute-start.18) | collective-permute-done | bytes 65568 | tf_op jit(solution)/shard_map/ppermute | solution.py:259
  67.0 2.6 %collective-permute-done.19 = bf16[16,2048]{1,0:T(8,128)(2,1)S(1)} collective-permute-done((bf16[16,2048]{1,0:T(8,128)(2,1)S(1)}, bf16[16,2048]{1,0:T(8,128)(2,1)S(1)}, u32[]{:S(2)}, u32[]{:S(2)}) %collective-permute-start.19) | collective-permute-done | bytes 65568 | tf_op jit(solution)/shard_map/ppermute | solution.py:259
  69.6 0.7 add_convert_fusion.2
  (26 shorter events, 0.1 us)
Async XLA Ops:
  0.0 12.2 %collective-permute-start.2 = (bf16[16,2048]{1,0:T(8,128)(2,1)}, bf16[16,2048]{1,0:T(8,128)(2,1)S(1)}, u32[]{:S(2)}, u32[]{:S(2)}) collective-permute-start(bf16[16,2048]{1,0:T(8,128)(2,1)} %tokens_ref.3), channel_id=1, source_target_pairs={{0,12},{4,8},{8,4},{12,0},{1,13},{5,9},{9,5},{13,1},{2,14},{6,10},... | collective-permute-start | bytes 196616 | tf_op jit(solution)/shard_map/ppermute | solution.py:259
  5.0 7.2 %collective-permute-start.1 = (bf16[16,2048]{1,0:T(8,128)(2,1)}, bf16[16,2048]{1,0:T(8,128)(2,1)S(1)}, u32[]{:S(2)}, u32[]{:S(2)}) collective-permute-start(bf16[16,2048]{1,0:T(8,128)(2,1)} %tokens_ref.3), channel_id=1, source_target_pairs={{0,8},{4,12},{8,0},{12,4},{1,9},{5,13},{9,1},{13,5},{2,10},{6,14},... | collective-permute-start | bytes 196616 | tf_op jit(solution)/shard_map/ppermute | solution.py:259
  5.1 7.2 %collective-permute-start = (bf16[16,2048]{1,0:T(8,128)(2,1)}, bf16[16,2048]{1,0:T(8,128)(2,1)S(1)}, u32[]{:S(2)}, u32[]{:S(2)}) collective-permute-start(bf16[16,2048]{1,0:T(8,128)(2,1)} %tokens_ref.3), channel_id=1, source_target_pairs={{0,4},{4,0},{8,12},{12,8},{1,5},{5,1},{9,13},{13,9},{2,6},{6,2},{1... | collective-permute-start | bytes 196616 | tf_op jit(solution)/shard_map/ppermute | solution.py:259
  5.6 6.7 %collective-permute-start.3 = (bf16[16,2048]{1,0:T(8,128)(2,1)}, bf16[16,2048]{1,0:T(8,128)(2,1)S(1)}, u32[]{:S(2)}, u32[]{:S(2)}) collective-permute-start(bf16[16,2048]{1,0:T(8,128)(2,1)} %tokens_ref.3), channel_id=1, source_target_pairs={{0,16},{16,0},{1,17},{17,1},{2,18},{18,2},{3,19},{19,3},{4,20},{20... | collective-permute-start | bytes 196616 | tf_op jit(solution)/shard_map/ppermute | solution.py:259
  12.3 5.8 %collective-permute-start.4 = (bf16[48,2048]{1,0:T(8,128)(2,1)S(1)}, bf16[48,2048]{1,0:T(8,128)(2,1)S(1)}, u32[]{:S(2)}, u32[]{:S(2)}) collective-permute-start(bf16[48,2048]{1,0:T(8,128)(2,1)S(1)} %join.4.refs_1_), channel_id=1, source_target_pairs={{0,16},{16,0},{1,17},{17,1},{2,18},{18,2},{3,19},{19,3},{4,20},{20... | collective-permute-start | bytes 589832 | tf_op jit(solution)/shard_map/ppermute | solution.py:259
  21.7 2.2 %collective-permute-start.5 = (bf16[2,64,2560]{2,1,0:T(8,128)(2,1)S(1)}, bf16[2,64,2560]{2,1,0:T(8,128)(2,1)S(1)}, u32[]{:S(2)}, u32[]{:S(2)}) collective-permute-start(bf16[2,64,2560]{2,1,0:T(8,128)(2,1)S(1)} %get-tuple-element.26), channel_id=1, source_target_pairs={{0,1},{1,0},{2,3},{3,2},{4,5},{5,4},{6,7},{7,6},{8,9},{9,8},{10,11... | collective-permute-start | bytes 1966088 | tf_op jit(solution)/shard_map/ppermute | solution.py:259
  23.9 29.4 %slice-start = ((s8[27262976]{0:T(1024)(128)(4,1)}), s8[4194304]{0:T(1024)(128)(4,1)S(1)}, s32[]{:S(2)}) async-start(s8[27262976]{0:T(1024)(128)(4,1)} %bitcast.2), calls=%async_computation | async-start | bytes 8388608
  23.9 29.3 %slice-start.1 = ((s8[27262976]{0:T(1024)(128)(4,1)}), s8[4194304]{0:T(1024)(128)(4,1)S(1)}, s32[]{:S(2)}) async-start(s8[27262976]{0:T(1024)(128)(4,1)} %bitcast.2), calls=%async_computation.1 | async-start | bytes 8388608
  24.0 29.3 %slice-start.2 = ((s8[27262976]{0:T(1024)(128)(4,1)}), s8[4194304]{0:T(1024)(128)(4,1)S(1)}, s32[]{:S(2)}) async-start(s8[27262976]{0:T(1024)(128)(4,1)} %bitcast.2), calls=%async_computation.2 | async-start | bytes 8388608
  24.0 29.3 %slice-start.3 = ((s8[27262976]{0:T(1024)(128)(4,1)}), s8[4194304]{0:T(1024)(128)(4,1)S(1)}, s32[]{:S(2)}) async-start(s8[27262976]{0:T(1024)(128)(4,1)} %bitcast.2), calls=%async_computation.3 | async-start | bytes 8388608
  24.0 29.3 %slice-start.4 = ((s8[27262976]{0:T(1024)(128)(4,1)}), s8[4194304]{0:T(1024)(128)(4,1)S(1)}, s32[]{:S(2)}) async-start(s8[27262976]{0:T(1024)(128)(4,1)} %bitcast.2), calls=%async_computation.4 | async-start | bytes 8388608
  24.0 29.3 %slice-start.5 = ((s8[27262976]{0:T(1024)(128)(4,1)}), s8[4194304]{0:T(1024)(128)(4,1)S(1)}, s32[]{:S(2)}) async-start(s8[27262976]{0:T(1024)(128)(4,1)} %bitcast.2), calls=%async_computation.5 | async-start | bytes 8388608
  24.0 29.3 %slice-start.6 = ((s8[27262976]{0:T(1024)(128)(4,1)}), s8[2097152]{0:T(1024)(128)(4,1)S(1)}, s32[]{:S(2)}) async-start(s8[27262976]{0:T(1024)(128)(4,1)} %bitcast.2), calls=%async_computation.6 | async-start | bytes 4194304
  30.2 1.9 %collective-permute-start.6 = (bf16[2,32,1536]{2,1,0:T(8,128)(2,1)S(1)}, bf16[2,32,1536]{2,1,0:T(8,128)(2,1)S(1)}, u32[]{:S(2)}, u32[]{:S(2)}) collective-permute-start(bf16[2,32,1536]{2,1,0:T(8,128)(2,1)S(1)} %get-tuple-element.28), channel_id=1, source_target_pairs={{0,1},{1,0},{2,3},{3,2},{4,5},{5,4},{6,7},{7,6},{8,9},{9,8},{10,11... | collective-permute-start | bytes 589832 | tf_op jit(solution)/shard_map/ppermute | solution.py:259
  30.4 10.0 %collective-permute-start.9 = (bf16[2,32,2560]{2,1,0:T(8,128)(2,1)S(1)}, bf16[2,32,2560]{2,1,0:T(8,128)(2,1)S(1)}, u32[]{:S(2)}, u32[]{:S(2)}) collective-permute-start(bf16[2,32,2560]{2,1,0:T(8,128)(2,1)S(1)} %add_convert_fusion.refs_4_), channel_id=1, source_target_pairs={{0,2},{1,3},{2,0},{3,1},{4,6},{5,7},{6,4},{7,5},{8,10},{9,11},{10,... | collective-permute-start | bytes 983048 | tf_op jit(solution)/shard_map/ppermute | solution.py:259
  40.6 4.5 %collective-permute-start.10 = (bf16[16,2560]{1,0:T(8,128)(2,1)S(1)}, bf16[16,2560]{1,0:T(8,128)(2,1)S(1)}, u32[]{:S(2)}, u32[]{:S(2)}) collective-permute-start(bf16[16,2560]{1,0:T(8,128)(2,1)S(1)} %get-tuple-element.30), channel_id=1, source_target_pairs={{0,16},{16,0},{1,17},{17,1},{2,18},{18,2},{3,19},{19,3},{4,20},{20... | collective-permute-start | bytes 245768 | tf_op jit(solution)/shard_map/ppermute | solution.py:259
  45.1 5.2 %collective-permute-start.11 = (bf16[32,1280]{1,0:T(8,128)(2,1)S(1)}, bf16[32,1280]{1,0:T(8,128)(2,1)S(1)}, u32[]{:S(2)}, u32[]{:S(2)}) collective-permute-start(bf16[32,1280]{1,0:T(8,128)(2,1)S(1)} %join.5.refs_0_), channel_id=1, source_target_pairs={{0,2},{1,3},{2,0},{3,1},{4,6},{5,7},{6,4},{7,5},{8,10},{9,11},{10,... | collective-permute-start | bytes 245768 | tf_op jit(solution)/shard_map/ppermute | solution.py:259
  46.8 4.6 %collective-permute-start.7 = (bf16[2,16,1536]{2,1,0:T(8,128)(2,1)S(1)}, bf16[2,16,1536]{2,1,0:T(8,128)(2,1)S(1)}, u32[]{:S(2)}, u32[]{:S(2)}) collective-permute-start(bf16[2,16,1536]{2,1,0:T(8,128)(2,1)S(1)} %add_convert_fusion.1.refs_0_), channel_id=1, source_target_pairs={{0,2},{1,3},{2,0},{3,1},{4,6},{5,7},{6,4},{7,5},{8,10},{9,11},{10,... | collective-permute-start | bytes 294920 | tf_op jit(solution)/shard_map/ppermute | solution.py:259
  47.1 5.6 %collective-permute-start.15 = (bf16[32,1280]{1,0:T(8,128)(2,1)S(1)}, bf16[32,1280]{1,0:T(8,128)(2,1)S(1)}, u32[]{:S(2)}, u32[]{:S(2)}) collective-permute-start(bf16[32,1280]{1,0:T(8,128)(2,1)S(1)} %join.7.refs_0_), channel_id=1, source_target_pairs={{0,2},{1,3},{2,0},{3,1},{4,6},{5,7},{6,4},{7,5},{8,10},{9,11},{10,... | collective-permute-start | bytes 245768 | tf_op jit(solution)/shard_map/ppermute | solution.py:259
  48.9 4.4 %collective-permute-start.12 = (bf16[32,1280]{1,0:T(8,128)(2,1)S(1)}, bf16[32,1280]{1,0:T(8,128)(2,1)S(1)}, u32[]{:S(2)}, u32[]{:S(2)}) collective-permute-start(bf16[32,1280]{1,0:T(8,128)(2,1)S(1)} %join.5.refs_0_), channel_id=1, source_target_pairs={{0,1},{1,0},{2,3},{3,2},{4,5},{5,4},{6,7},{7,6},{8,9},{9,8},{10,11... | collective-permute-start | bytes 245768 | tf_op jit(solution)/shard_map/ppermute | solution.py:259
  50.4 2.9 %collective-permute-start.13 = (bf16[32,1280]{1,0:T(8,128)(2,1)S(1)}, bf16[32,1280]{1,0:T(8,128)(2,1)S(1)}, u32[]{:S(2)}, u32[]{:S(2)}) collective-permute-start(bf16[32,1280]{1,0:T(8,128)(2,1)S(1)} %collective-permute-done.11.refs_1_), channel_id=1, source_target_pairs={{0,1},{1,0},{2,3},{3,2},{4,5},{5,4},{6,7},{7,6},{8,9},{9,8},{10,11... | collective-permute-start | bytes 245768 | tf_op jit(solution)/shard_map/ppermute | solution.py:259
  51.5 4.3 %collective-permute-start.8 = (bf16[16,1536]{1,0:T(8,128)(2,1)S(1)}, bf16[16,1536]{1,0:T(8,128)(2,1)S(1)}, u32[]{:S(2)}, u32[]{:S(2)}) collective-permute-start(bf16[16,1536]{1,0:T(8,128)(2,1)S(1)} %combine.2.refs_0_), channel_id=1, source_target_pairs={{0,2},{1,3},{2,0},{3,1},{4,6},{5,7},{6,4},{7,5},{8,10},{9,11},{10,... | collective-permute-start | bytes 147464 | tf_op jit(solution)/shard_map/ppermute | solution.py:259
  52.7 3.2 %collective-permute-start.16 = (bf16[32,1280]{1,0:T(8,128)(2,1)S(1)}, bf16[32,1280]{1,0:T(8,128)(2,1)S(1)}, u32[]{:S(2)}, u32[]{:S(2)}) collective-permute-start(bf16[32,1280]{1,0:T(8,128)(2,1)S(1)} %join.7.refs_0_), channel_id=1, source_target_pairs={{0,1},{1,0},{2,3},{3,2},{4,5},{5,4},{6,7},{7,6},{8,9},{9,8},{10,11... | collective-permute-start | bytes 245768 | tf_op jit(solution)/shard_map/ppermute | solution.py:259
  52.7 3.2 %collective-permute-start.17 = (bf16[32,1280]{1,0:T(8,128)(2,1)S(1)}, bf16[32,1280]{1,0:T(8,128)(2,1)S(1)}, u32[]{:S(2)}, u32[]{:S(2)}) collective-permute-start(bf16[32,1280]{1,0:T(8,128)(2,1)S(1)} %collective-permute-done.15.refs_1_), channel_id=1, source_target_pairs={{0,1},{1,0},{2,3},{3,2},{4,5},{5,4},{6,7},{7,6},{8,9},{9,8},{10,11... | collective-permute-start | bytes 245768 | tf_op jit(solution)/shard_map/ppermute | solution.py:259
  55.8 2.6 %collective-permute-start.14 = (bf16[32,1536]{1,0:T(8,128)(2,1)S(1)}, bf16[32,1536]{1,0:T(8,128)(2,1)S(1)}, u32[]{:S(2)}, u32[]{:S(2)}) collective-permute-start(bf16[32,1536]{1,0:T(8,128)(2,1)S(1)} %join.6), channel_id=1, source_target_pairs={{0,1},{1,0},{2,3},{3,2},{4,5},{5,4},{6,7},{7,6},{8,9},{9,8},{10,11... | collective-permute-start | bytes 294920 | tf_op jit(solution)/shard_map/ppermute | solution.py:259
  60.2 6.9 %collective-permute-start.18 = (bf16[16,2048]{1,0:T(8,128)(2,1)S(1)}, bf16[16,2048]{1,0:T(8,128)(2,1)S(1)}, u32[]{:S(2)}, u32[]{:S(2)}) collective-permute-start(bf16[16,2048]{1,0:T(8,128)(2,1)S(1)} %get-tuple-element.32), channel_id=1, source_target_pairs={{0,12},{4,8},{8,4},{12,0},{1,13},{5,9},{9,5},{13,1},{2,14},{6,10},... | collective-permute-start | bytes 196616 | tf_op jit(solution)/shard_map/ppermute | solution.py:259
  63.8 5.8 %collective-permute-start.19 = (bf16[16,2048]{1,0:T(8,128)(2,1)S(1)}, bf16[16,2048]{1,0:T(8,128)(2,1)S(1)}, u32[]{:S(2)}, u32[]{:S(2)}) collective-permute-start(bf16[16,2048]{1,0:T(8,128)(2,1)S(1)} %get-tuple-element.33), channel_id=1, source_target_pairs={{0,8},{4,12},{8,0},{12,4},{1,9},{5,13},{9,1},{13,5},{2,10},{6,14},... | collective-permute-start | bytes 196616 | tf_op jit(solution)/shard_map/ppermute | solution.py:259
  63.8 5.8 %collective-permute-start.20 = (bf16[16,2048]{1,0:T(8,128)(2,1)S(1)}, bf16[16,2048]{1,0:T(8,128)(2,1)S(1)}, u32[]{:S(2)}, u32[]{:S(2)}) collective-permute-start(bf16[16,2048]{1,0:T(8,128)(2,1)S(1)} %get-tuple-element.34), channel_id=1, source_target_pairs={{0,4},{4,0},{8,12},{12,8},{1,5},{5,1},{9,13},{13,9},{2,6},{6,2},{1... | collective-permute-start | bytes 196616 | tf_op jit(solution)/shard_map/ppermute | solution.py:259

commit v7 on v6

--- a/solution.py
+++ b/solution.py
@@ -10,6 +10,7 @@
 TILE = 256
 LAST = 3
 ROWS = 16
+COST = pl.CostEstimate(flops=0, bytes_accessed=1024, transcendentals=0)
 
 
 def plain(tokens, gate_weight, up_weight, down_weight):
@@ -76,7 +77,7 @@
         out_shape=[pltpu.VMEM(x, jnp.bfloat16) for x in ((depth, width), (depth, width), tokens.shape)],
         scratch_shapes=[pltpu.SemaphoreType.DMA((3, len(pieces_of(width, 2 * TILE))))],
         compiler_params=params(1),
-        cost_estimate=pl.CostEstimate(flops=0, bytes_accessed=4 * depth * width, transcendentals=0),
+        cost_estimate=COST,
         name="fetch",
     )(where, gate, up, tokens)
 
@@ -96,7 +97,7 @@
         out_specs=spec(pltpu.VMEM),
         out_shape=jax.ShapeDtypeStruct((rows, width), arrays[0].dtype),
         compiler_params=params(1),
-        cost_estimate=pl.CostEstimate(flops=0, bytes_accessed=4 * rows * width, transcendentals=0),
+        cost_estimate=COST,
         name="join",
     )(*arrays, *behind)
 
@@ -154,16 +155,54 @@
         scratch_shapes=scratch,
         out_shape=[jax.ShapeDtypeStruct((2, total // 2, width), jnp.bfloat16)] * 2,
         compiler_params=params(16 if segments else 4),
-        cost_estimate=pl.CostEstimate(
-            flops=4 * total * depth * width, bytes_accessed=4 * depth * width, transcendentals=0
-        ),
+        cost_estimate=COST,
         name="gate_up",
     )(where, *arrays, *weights, *behind)
 
 
-def combine_kernel(n_outs, mine_ref, got_ref, chip_ref, *refs):
+def pair_sum_kernel(mine_ref, got_ref, *refs):
+    out_ref = refs[-1]
+    rows = out_ref.shape[1]
+    for k in range(2):
+        total = mine_ref[k, rows:].astype(jnp.float32) + got_ref[k, rows:].astype(jnp.float32)
+        out_ref[k] = total.astype(out_ref.dtype)
+
+
+def pair_sum(mine, got, behind):
+    _, rows, width = mine.shape
+    return pl.pallas_call(
+        pair_sum_kernel,
+        in_specs=[spec(pltpu.VMEM)] * 2 + [spec(pl.ANY)] * len(behind),
+        out_specs=spec(pltpu.VMEM),
+        out_shape=jax.ShapeDtypeStruct((2, rows // 2, width), mine.dtype),
+        compiler_params=params(2),
+        cost_estimate=COST,
+        name="pair_sum",
+    )(mine, got, *behind)
+
+
+def mark_kernel(_, out_ref):
+    out_ref[...] = jnp.zeros_like(out_ref)
+
+
+def mark(array):
+    return pl.pallas_call(
+        mark_kernel,
+        in_specs=[spec(pl.ANY)],
+        out_specs=spec(pltpu.VMEM),
+        out_shape=jax.ShapeDtypeStruct((8, 128), jnp.float32),
+        compiler_params=params(1),
+        cost_estimate=COST,
+        name="mark",
+    )(array)
+
+
+def combine_kernel(n_left, n_outs, mine_ref, got_ref, chip_ref, *refs):
     outs = refs[-n_outs:]
-    rows = chip_ref.shape[1]
+    rows, first = chip_ref.shape[1], 0
+    for left in refs[:n_left]:
+        first = left.shape[1]
+        outs[0][:, :first] = left[...]
     for a, b in pieces_of(chip_ref.shape[2], TILE):
         gate, up = (
             mine_ref[k, :rows, a:b].astype(jnp.float32)
@@ -173,50 +212,40 @@
         )
         hidden = (gate / (1 + jnp.exp(-gate)) * up).astype(jnp.bfloat16)
         for i, out in enumerate(outs):
-            out[:, a:b] = hidden[i * ROWS : (i + 1) * ROWS]
-
-
-def combine(mine, got, from_chip, behind):
+            out[:, first + a : first + b] = hidden[i * ROWS : (i + 1) * ROWS]
+
+
+def combine(mine, got, from_chip, left, behind):
     _, rows, width = from_chip.shape
     n_outs = rows // ROWS
-    return pl.pallas_call(
-        functools.partial(combine_kernel, n_outs),
-        in_specs=[spec(pltpu.VMEM)] * 3 + [spec(pl.ANY)] * len(behind),
+    width += sum(x.shape[1] for x in left)
+    return pl.pallas_call(
+        functools.partial(combine_kernel, len(left), n_outs),
+        in_specs=[spec(pltpu.VMEM)] * (3 + len(left)) + [spec(pl.ANY)] * len(behind),
         out_specs=[spec(pltpu.VMEM)] * n_outs,
         out_shape=[jax.ShapeDtypeStruct((ROWS, width), jnp.bfloat16)] * n_outs,
-        compiler_params=params(1),
-        cost_estimate=pl.CostEstimate(
-            flops=10 * rows * width, bytes_accessed=14 * rows * width, transcendentals=rows * width
-        ),
+        compiler_params=params(2),
+        cost_estimate=COST,
         name="combine",
-    )(mine, got, from_chip, *behind)
-
-
-def down_kernel(n_pieces, has_acc, last, first, half, where, *refs):
+    )(mine, got, from_chip, *left, *behind)
+
+
+def down_kernel(n_pieces, has_acc, last, segments, where, *refs):
     pieces, refs = refs[:n_pieces], refs[n_pieces:]
     down_ref, refs = refs[0], refs[1:]
     prev_ref, refs = (refs[0], refs[1:]) if has_acc else (None, refs)
     outs, (acc_ref, lhs_ref) = refs[:-2], refs[-2:]
-    depth = lhs_ref.shape[2]
-    p = 0
+    at = 0
     for piece in pieces:
-        for at in range(0, piece.shape[0], ROWS if last else 2 * ROWS):
-            for k in range(2):
-                if last:
-                    block = piece[at : at + ROWS, k * depth : (k + 1) * depth]
-                else:
-                    block = piece[at + k * ROWS : at + (k + 1) * ROWS, :]
-                lhs_ref[k, p * ROWS : (p + 1) * ROWS, :] = block
-            p += 1
-    if last:
-        starts = [first, half + first]
-    else:
-        starts = [where[0] + first, half - where[0] + first]
+        lhs_ref[at : at + piece.shape[0], :] = piece[...]
+        at += piece.shape[0]
     for a, b in pieces_of(down_ref.shape[1], 2 * TILE):
         part = prev_ref[:, a:b] if has_acc else 0.0
-        for k in range(2):
-            rows = pl.ds(pl.multiple_of(starts[k], TILE), depth)
-            part += jnp.dot(lhs_ref[k], down_ref[rows, a:b], preferred_element_type=jnp.float32)
+        at = 0
+        for sign, start, depth in segments:
+            rows = pl.ds(pl.multiple_of(sign * where[0] + start, TILE) if sign else start, depth)
+            part += jnp.dot(lhs_ref[:, at : at + depth], down_ref[rows, a:b], preferred_element_type=jnp.float32)
+            at += depth
         acc_ref[:, a:b] = part
     if last:
         for d, out in enumerate(outs):
@@ -224,26 +253,22 @@
             out[...] = acc_ref[pl.ds(source, ROWS), :].astype(out.dtype)
 
 
-def down(where, pieces, down_weight, prev, first, depth, last):
+def down(where, pieces, down_weight, prev, segments, last):
     width = down_weight.shape[1]
     total = 4 * ROWS
     args = [*pieces, down_weight] + ([] if prev is None else [prev])
     sums = jax.ShapeDtypeStruct((total, width), jnp.float32)
-    scratch = [pltpu.VMEM((2, total, depth), jnp.bfloat16)]
+    scratch = [pltpu.VMEM((total, pieces[0].shape[1]), jnp.bfloat16)]
     if last:
         scratch = [pltpu.VMEM(sums.shape, sums.dtype)] + scratch
     return pl.pallas_call(
-        functools.partial(
-            down_kernel, len(pieces), prev is not None, last, first, down_weight.shape[0] // 2
-        ),
+        functools.partial(down_kernel, len(pieces), prev is not None, last, segments),
         in_specs=[spec(pltpu.SMEM)] + [spec(pltpu.VMEM)] * len(args),
         out_specs=[spec(pltpu.VMEM)] * 4 if last else spec(pltpu.VMEM),
         scratch_shapes=scratch,
         out_shape=[jax.ShapeDtypeStruct((ROWS, width), jnp.bfloat16)] * 4 if last else sums,
         compiler_params=params(4),
-        cost_estimate=pl.CostEstimate(
-            flops=4 * total * width * depth, bytes_accessed=4 * width * depth, transcendentals=0
-        ),
+        cost_estimate=COST,
         name="down",
     )(where, *args)
 
@@ -273,34 +298,27 @@
     near = join(by_hid, [own, far_own])
     far = swap(near, "rep", 1)
 
-    def reduce_pair(mine, theirs):
-        got = swap(theirs, "wid", 1)
-        rows = mine.shape[1] // 2
-        return mine, got, (mine[:, rows:].astype(f32) + got[:, rows:].astype(f32)).astype(bf16)
-
     weights = [w for fetched in early for w in fetched[:2]]
-    *parts, to_chip = reduce_pair(*gate_up(where, [own, near, far_own, far], weights, [], []))
+    mine, theirs = gate_up(where, [own, near, far_own, far], weights, [], [])
+    got = swap(theirs, "wid", 1)
+    to_chip = pair_sum(mine, got, [])
     from_chip = swap(to_chip, "wid", 2)
     segments = [(bounds[2], widths[2]), (half + bounds[2], widths[2])]
-    *last_parts, last_to_chip = reduce_pair(
-        *gate_up(where, [own, near], [gate_weight, up_weight], segments, [to_chip])
-    )
+    last_mine, theirs = gate_up(where, [own, near], [gate_weight, up_weight], segments, [to_chip])
+    last_got = swap(theirs, "wid", 1)
+    last_to_chip = pair_sum(last_mine, last_got, [mark(from_chip)])
     last_from_chip = swap(last_to_chip, "wid", 2)
 
-    keep, give = combine(*parts, from_chip, [last_to_chip])
-    got = swap(give, "rep", 1)
-    acc = None
-    for c in range(2):
-        mixed = join([keep, got], [], bounds[c], widths[c])
-        other = swap(mixed, "wid", 2)
-        pieces = [mixed, other, swap(mixed, "wid", 1), swap(other, "wid", 1)]
-        acc = down(where, pieces, down_weight, acc, bounds[c], widths[c], False)
-        if c == 0:
-            first_sum = acc
-    (mixed,) = combine(*last_parts, last_from_chip, [])
-    other = swap(mixed, "wid", 2)
-    pieces = [mixed, other, swap(join([mixed, other], [first_sum]), "wid", 1)]
-    acc = down(where, pieces, down_weight, acc, bounds[2], widths[2], True)
+    keep, give = combine(mine, got, from_chip, [], [])
+    far_columns = swap(give, "rep", 1)
+    (rest,) = combine(last_mine, last_got, last_from_chip, [far_columns], [])
+    rest_segments = [(-1, half, bounds[2])] + [(0, start, width) for start, width in segments]
+    acc, behind = None, []
+    for hidden, parts in ((keep, [(1, 0, bounds[2])]), (rest, rest_segments)):
+        other = swap(hidden, "wid", 2)
+        crossed = swap(join([hidden, other], behind), "wid", 1)
+        acc = down(where, [hidden, other, crossed], down_weight, acc, parts, bool(behind))
+        behind = [acc]
 
     mixed = acc[0].astype(f32)
     for d in (3, 2, 1):

time: 70.4 us -> 61.4 us (0.87)
  waiting for transfers between devices: 20.6 us -> 13.3 us
  starting transfers between devices: 21.5 us -> 20 us
    ppermute x21 -> x17, waiting for transfers between devices: 20.6 us -> 13.3 us  [swap(): return lax.ppermute(x, axis, [(i, i ^ step) for i in range(n)])]
    ppermute x21 -> x17, starting transfers between devices: 21.5 us -> 20 us  [swap(): return lax.ppermute(x, axis, [(i, i ^ step) for i in range(n)])]
    pallas_call x3 -> x2, Pallas kernels: 6.69 us -> 6.06 us  [down(): pl.pallas_call(functools.partial(down_kernel, len(pieces), prev is not No...]
  transfers between devices with their start and end apart: 21 -> 17, of which waited for: 7 -> 8; matrix products, arithmetic and copies ran while one was open for 0% -> 0% of each run, Pallas kernels for 22% -> 32%
where the time goes in v7:
time: 61.4 us; the launch traced here: 61.2 us
  Pallas kernels  26.9 us (44%)
  starting transfers between devices  20 us (33%)
  waiting for transfers between devices  13.3 us (22%)
  other arithmetic  0.74 us (1%)
    ppermute x17, starting transfers between devices, swap(): return lax.ppermute(x, axis, [(i, i ^ step) for i in range(n)])  20 us
    ppermute x17, waiting for transfers between devices, swap(): return lax.ppermute(x, axis, [(i, i ^ step) for i in range(n)])  13.3 us
    pallas_call x2, Pallas kernels, fetch(): pl.pallas_call(functools.partial(fetch_kernel, first), in_specs=[spec(plt...  10.2 us
    pallas_call x2, Pallas kernels, gate_up(): pl.pallas_call(functools.partial(gate_up_kernel, len(arrays), len(weights...  10.2 us
    pallas_call x2, Pallas kernels, down(): pl.pallas_call(functools.partial(down_kernel, len(pieces), prev is not No...  6.06 us
  transfers between devices with their start and end apart: 17, of which 8 were waited for; matrix products, arithmetic and copies ran while one was open for 0% of the time, Pallas kernels for 32%

profile of v7, /device:TPU:0, one launch (start us, length us, event | category | flops | bytes accessed | tf_op | source)
XLA Modules:
  0.0 61.2 jit_solution(10714882316418195893)
XLA Ops:
  0.0 5.0 %collective-permute-start.2 = (bf16[16,2048]{1,0:T(8,128)(2,1)}, bf16[16,2048]{1,0:T(8,128)(2,1)S(1)}, u32[]{:S(2)}, u32[]{:S(2)}) collective-permute-start(bf16[16,2048]{1,0:T(8,128)(2,1)} %tokens_ref.3), channel_id=1, source_target_pairs={{0,12},{4,8},{8,4},{12,0},{1,13},{5,9},{9,5},{13,1},{2,14},{6,10},... | collective-permute-start | bytes 196616 | tf_op jit(solution)/shard_map/ppermute | solution.py:284
  5.0 0.0 collective-permute-start.1
  5.1 0.6 collective-permute-start
  5.6 1.7 %collective-permute-start.3 = (bf16[16,2048]{1,0:T(8,128)(2,1)}, bf16[16,2048]{1,0:T(8,128)(2,1)S(1)}, u32[]{:S(2)}, u32[]{:S(2)}) collective-permute-start(bf16[16,2048]{1,0:T(8,128)(2,1)} %tokens_ref.3), channel_id=1, source_target_pairs={{0,16},{16,0},{1,17},{17,1},{2,18},{18,2},{3,19},{19,3},{4,20},{20... | collective-permute-start | bytes 196616 | tf_op jit(solution)/shard_map/ppermute | solution.py:284
  7.4 0.1 pad_add_fusion.where
  7.4 4.8 %fetch.2 = (bf16[2048,1280]{1,0:T(8,128)(2,1)S(1)}, bf16[2048,1280]{1,0:T(8,128)(2,1)S(1)}, bf16[16,2048]{1,0:T(8,128)(2,1)S(1)}) custom-call(s32[2]{0:T(128)S(1)} %pad_add_fusion.where, bf16[2048,6656]{1,0:T(8,128)(2,1)} %refs_2_.1, bf16[2048,6656]{1,0:T(8,128)(2,1)} %refs_3_.3, bf16[16,2048]{1,0:T(8,128)(2,1)} %tokens_ref.3), custom_call_target="tpu_custom_call" | custom-call | bytes 1024 | tf_op jit(solution)/shard_map/fetch/pallas_call | solution.py:73
  12.2 0.0 collective-permute-done.2.refs_2_
  12.3 0.0 collective-permute-done.1.refs_1_
  12.3 0.0 collective-permute-done.refs_0_
  12.3 0.0 collective-permute-done.3.refs_4_.refs_2_
  12.3 0.4 collective-permute-start.4
  12.7 5.4 %fetch.3 = (bf16[2048,1280]{1,0:T(8,128)(2,1)S(1)}, bf16[2048,1280]{1,0:T(8,128)(2,1)S(1)}, bf16[16,2048]{1,0:T(8,128)(2,1)}) custom-call(s32[2]{0:T(128)S(1)} %pad_add_fusion.where, bf16[2048,6656]{1,0:T(8,128)(2,1)} %refs_2_.1, bf16[2048,6656]{1,0:T(8,128)(2,1)} %refs_3_.3, bf16[16,2048]{1,0:T(8,128)(2,1)} %tokens_ref.3), custom_call_target="tpu_custom_call" | custom-call | bytes 1024 | tf_op jit(solution)/shard_map/fetch/pallas_call | solution.py:73
  18.1 0.0 collective-permute-done.4.refs_3_
  18.1 3.6 %gate_up.2 = (bf16[2,64,2560]{2,1,0:T(8,128)(2,1)S(1)}, bf16[2,64,2560]{2,1,0:T(8,128)(2,1)S(1)}) custom-call(s32[2]{0:T(128)S(1)} %pad_add_fusion.where, bf16[16,2048]{1,0:T(8,128)(2,1)S(1)} %get-tuple-element.20.refs_3_.refs_0_, bf16[48,2048]{1,0:T(8,128)(2,1)S(1)} %join.3.refs_1_, bf16[16,2048]{1,0:T(8,128)(2,1)S(1)} %collective-permute-done.3.refs_4_.refs_2_, ...), custom_call_target="tpu_custom_call" | custom-call | bytes 1024 | tf_op jit(solution)/shard_map/gate_up/pallas_call | solution.py:148
  21.7 0.1 collective-permute-start.5
  21.8 2.1 %collective-permute-done.5.got_ref = bf16[2,64,2560]{2,1,0:T(8,128)(2,1)S(1)} collective-permute-done((bf16[2,64,2560]{2,1,0:T(8,128)(2,1)S(1)}, bf16[2,64,2560]{2,1,0:T(8,128)(2,1)S(1)}, u32[]{:S(2)}, u32[]{:S(2)}) %collective-permute-start.5) | collective-permute-done | bytes 655392 | tf_op jit(solution)/shard_map/ppermute | solution.py:284
  23.9 0.1 pair_sum.2.refs_4_
  23.9 0.0 slice-start.1
  24.0 0.0 slice-start.2
  24.0 0.0 slice-start.3
  24.0 0.0 slice-start.4
  24.0 0.0 slice-start.6
  24.0 1.8 %collective-permute-start.7 = (bf16[2,32,2560]{2,1,0:T(8,128)(2,1)S(1)}, bf16[2,32,2560]{2,1,0:T(8,128)(2,1)S(1)}, u32[]{:S(2)}, u32[]{:S(2)}) collective-permute-start(bf16[2,32,2560]{2,1,0:T(8,128)(2,1)S(1)} %pair_sum.2.refs_4_), channel_id=1, source_target_pairs={{0,2},{1,3},{2,0},{3,1},{4,6},{5,7},{6,4},{7,5},{8,10},{9,11},{10,... | collective-permute-start | bytes 983048 | tf_op jit(solution)/shard_map/ppermute | solution.py:284
  25.8 6.6 %gate_up.3 = (bf16[2,32,1536]{2,1,0:T(8,128)(2,1)S(1)}, bf16[2,32,1536]{2,1,0:T(8,128)(2,1)S(1)}) custom-call(s32[2]{0:T(128)S(1)} %pad_add_fusion.where, bf16[16,2048]{1,0:T(8,128)(2,1)S(1)} %get-tuple-element.20.refs_3_.refs_0_, bf16[48,2048]{1,0:T(8,128)(2,1)S(1)} %join.3.refs_1_, bf16[2048,6656]{1,0:T(8,128)(2,1)} %refs_2_.1, ...), custom_call_target="tpu_custom_call" | custom-call | bytes 1024 | tf_op jit(solution)/shard_map/gate_up/pallas_call | solution.py:148
  32.4 0.1 collective-permute-start.6
  32.5 1.3 %collective-permute-done.7._.chip_ref = bf16[2,32,2560]{2,1,0:T(8,128)(2,1)S(1)} collective-permute-done((bf16[2,32,2560]{2,1,0:T(8,128)(2,1)S(1)}, bf16[2,32,2560]{2,1,0:T(8,128)(2,1)S(1)}, u32[]{:S(2)}, u32[]{:S(2)}) %collective-permute-start.7) | collective-permute-done | bytes 327712 | tf_op jit(solution)/shard_map/ppermute | solution.py:284
  33.8 0.2 combine.2
  34.0 1.8 %collective-permute-start.11 = (bf16[16,2560]{1,0:T(8,128)(2,1)S(1)}, bf16[16,2560]{1,0:T(8,128)(2,1)S(1)}, u32[]{:S(2)}, u32[]{:S(2)}) collective-permute-start(bf16[16,2560]{1,0:T(8,128)(2,1)S(1)} %get-tuple-element.30.refs_0_), channel_id=1, source_target_pairs={{0,2},{1,3},{2,0},{3,1},{4,6},{5,7},{6,4},{7,5},{8,10},{9,11},{10,... | collective-permute-start | bytes 245768 | tf_op jit(solution)/shard_map/ppermute | solution.py:284
  35.8 0.0 collective-permute-done.6.got_ref
  35.8 0.4 collective-permute-start.8
  36.2 1.7 %collective-permute-start.9 = (bf16[16,2560]{1,0:T(8,128)(2,1)S(1)}, bf16[16,2560]{1,0:T(8,128)(2,1)S(1)}, u32[]{:S(2)}, u32[]{:S(2)}) collective-permute-start(bf16[16,2560]{1,0:T(8,128)(2,1)S(1)} %get-tuple-element.29), channel_id=1, source_target_pairs={{0,16},{16,0},{1,17},{17,1},{2,18},{18,2},{3,19},{19,3},{4,20},{20... | collective-permute-start | bytes 245768 | tf_op jit(solution)/shard_map/ppermute | solution.py:284
  38.0 1.5 %collective-permute-done.11.refs_1_ = bf16[16,2560]{1,0:T(8,128)(2,1)S(1)} collective-permute-done((bf16[16,2560]{1,0:T(8,128)(2,1)S(1)}, bf16[16,2560]{1,0:T(8,128)(2,1)S(1)}, u32[]{:S(2)}, u32[]{:S(2)}) %collective-permute-start.11) | collective-permute-done | bytes 81952 | tf_op jit(solution)/shard_map/ppermute | solution.py:284
  39.4 0.1 collective-permute-start.12
  39.5 1.2 %collective-permute-done.9.refs_0_ = bf16[16,2560]{1,0:T(8,128)(2,1)S(1)} collective-permute-done((bf16[16,2560]{1,0:T(8,128)(2,1)S(1)}, bf16[16,2560]{1,0:T(8,128)(2,1)S(1)}, u32[]{:S(2)}, u32[]{:S(2)}) %collective-permute-start.9) | collective-permute-done | bytes 81952 | tf_op jit(solution)/shard_map/ppermute | solution.py:284
  40.7 0.0 collective-permute-done.8.chip_ref
  40.7 0.1 combine.3.refs_0_
  40.7 1.8 %collective-permute-start.10 = (bf16[16,4096]{1,0:T(8,128)(2,1)S(1)}, bf16[16,4096]{1,0:T(8,128)(2,1)S(1)}, u32[]{:S(2)}, u32[]{:S(2)}) collective-permute-start(bf16[16,4096]{1,0:T(8,128)(2,1)S(1)} %combine.3.refs_0_), channel_id=1, source_target_pairs={{0,2},{1,3},{2,0},{3,1},{4,6},{5,7},{6,4},{7,5},{8,10},{9,11},{10,... | collective-permute-start | bytes 393224 | tf_op jit(solution)/shard_map/ppermute | solution.py:284
  42.6 2.5 %down.2.refs_2_.refs_4_ = f32[64,2048]{1,0:T(8,128)S(1)} custom-call(s32[2]{0:T(128)S(1)} %pad_add_fusion.where, bf16[16,2560]{1,0:T(8,128)(2,1)S(1)} %get-tuple-element.30.refs_0_, bf16[16,2560]{1,0:T(8,128)(2,1)S(1)} %collective-permute-done.11.refs_1_, bf16[32,2560]{1,0:T(8,128)(2,1)S(1)} %collective-permute-done.12.refs_2_, bf16[6656,2048]{1,0:T(8,128)(2,1)S(1)} %bitcast.3), custom_call_target="tpu_custom_call" | custom-call | bytes 1024 | tf_op jit(solution)/shard_map/down/pallas_call | solution.py:264
  45.1 0.7 %collective-permute-done.10.refs_1_ = bf16[16,4096]{1,0:T(8,128)(2,1)S(1)} collective-permute-done((bf16[16,4096]{1,0:T(8,128)(2,1)S(1)}, bf16[16,4096]{1,0:T(8,128)(2,1)S(1)}, u32[]{:S(2)}, u32[]{:S(2)}) %collective-permute-start.10) | collective-permute-done | bytes 131104 | tf_op jit(solution)/shard_map/ppermute | solution.py:284
  45.8 0.1 collective-permute-start.13
  45.9 1.5 %collective-permute-done.13.refs_2_ = bf16[32,4096]{1,0:T(8,128)(2,1)S(1)} collective-permute-done((bf16[32,4096]{1,0:T(8,128)(2,1)S(1)}, bf16[32,4096]{1,0:T(8,128)(2,1)S(1)}, u32[]{:S(2)}, u32[]{:S(2)}) %collective-permute-start.13) | collective-permute-done | bytes 262176 | tf_op jit(solution)/shard_map/ppermute | solution.py:284
  47.4 3.6 %down.3 = (bf16[16,2048]{1,0:T(8,128)(2,1)S(1)}, bf16[16,2048]{1,0:T(8,128)(2,1)S(1)}, bf16[16,2048]{1,0:T(8,128)(2,1)S(1)}, bf16[16,2048]{1,0:T(8,128)(2,1)S(1)}) custom-call(s32[2]{0:T(128)S(1)} %pad_add_fusion.where, bf16[16,4096]{1,0:T(8,128)(2,1)S(1)} %combine.3.refs_0_, bf16[16,4096]{1,0:T(8,128)(2,1)S(1)} %collective-permute-done.10.refs_1_, ...), custom_call_target="tpu_custom_call" | custom-call | bytes 1024 | tf_op jit(solution)/shard_map/down/pallas_call | solution.py:264
  51.0 3.9 %collective-permute-start.14 = (bf16[16,2048]{1,0:T(8,128)(2,1)S(1)}, bf16[16,2048]{1,0:T(8,128)(2,1)S(1)}, u32[]{:S(2)}, u32[]{:S(2)}) collective-permute-start(bf16[16,2048]{1,0:T(8,128)(2,1)S(1)} %get-tuple-element.32), channel_id=1, source_target_pairs={{0,12},{4,8},{8,4},{12,0},{1,13},{5,9},{9,5},{13,1},{2,14},{6,10},... | collective-permute-start | bytes 196616 | tf_op jit(solution)/shard_map/ppermute | solution.py:284
  54.9 0.6 %collective-permute-start.16 = (bf16[16,2048]{1,0:T(8,128)(2,1)S(1)}, bf16[16,2048]{1,0:T(8,128)(2,1)S(1)}, u32[]{:S(2)}, u32[]{:S(2)}) collective-permute-start(bf16[16,2048]{1,0:T(8,128)(2,1)S(1)} %get-tuple-element.34), channel_id=1, source_target_pairs={{0,4},{4,0},{8,12},{12,8},{1,5},{5,1},{9,13},{13,9},{2,6},{6,2},{1... | collective-permute-start | bytes 196616 | tf_op jit(solution)/shard_map/ppermute | solution.py:284
  55.5 2.3 %collective-permute-done.14 = bf16[16,2048]{1,0:T(8,128)(2,1)S(1)} collective-permute-done((bf16[16,2048]{1,0:T(8,128)(2,1)S(1)}, bf16[16,2048]{1,0:T(8,128)(2,1)S(1)}, u32[]{:S(2)}, u32[]{:S(2)}) %collective-permute-start.14) | collective-permute-done | bytes 65568 | tf_op jit(solution)/shard_map/ppermute | solution.py:284
  57.9 2.7 %collective-permute-done.15 = bf16[16,2048]{1,0:T(8,128)(2,1)S(1)} collective-permute-done((bf16[16,2048]{1,0:T(8,128)(2,1)S(1)}, bf16[16,2048]{1,0:T(8,128)(2,1)S(1)}, u32[]{:S(2)}, u32[]{:S(2)}) %collective-permute-start.15) | collective-permute-done | bytes 65568 | tf_op jit(solution)/shard_map/ppermute | solution.py:284
  60.6 0.0 collective-permute-done.16
  60.6 0.7 %add_convert_fusion = bf16[16,2048]{1,0:T(8,128)(2,1)} fusion(bf16[16,2048]{1,0:T(8,128)(2,1)S(1)} %collective-permute-done.16, bf16[16,2048]{1,0:T(8,128)(2,1)S(1)} %collective-permute-done.15, bf16[16,2048]{1,0:T(8,128)(2,1)S(1)} %collective-permute-done.14, bf16[16,2048]{1,0:T(8,128)(2,1)S(1)} %get-tuple-element.31), kind=kLoop, calls=%fused_computation | loop fusion | flops 262144 | bytes 327680 | tf_op jit(solution)/shard_map/convert_element_type | solution.py:326
  (17 shorter events, 0.1 us)
Async XLA Ops:
  0.0 12.2 %collective-permute-start.2 = (bf16[16,2048]{1,0:T(8,128)(2,1)}, bf16[16,2048]{1,0:T(8,128)(2,1)S(1)}, u32[]{:S(2)}, u32[]{:S(2)}) collective-permute-start(bf16[16,2048]{1,0:T(8,128)(2,1)} %tokens_ref.3), channel_id=1, source_target_pairs={{0,12},{4,8},{8,4},{12,0},{1,13},{5,9},{9,5},{13,1},{2,14},{6,10},... | collective-permute-start | bytes 196616 | tf_op jit(solution)/shard_map/ppermute | solution.py:284
  5.0 7.2 %collective-permute-start.1 = (bf16[16,2048]{1,0:T(8,128)(2,1)}, bf16[16,2048]{1,0:T(8,128)(2,1)S(1)}, u32[]{:S(2)}, u32[]{:S(2)}) collective-permute-start(bf16[16,2048]{1,0:T(8,128)(2,1)} %tokens_ref.3), channel_id=1, source_target_pairs={{0,8},{4,12},{8,0},{12,4},{1,9},{5,13},{9,1},{13,5},{2,10},{6,14},... | collective-permute-start | bytes 196616 | tf_op jit(solution)/shard_map/ppermute | solution.py:284
  5.1 7.2 %collective-permute-start = (bf16[16,2048]{1,0:T(8,128)(2,1)}, bf16[16,2048]{1,0:T(8,128)(2,1)S(1)}, u32[]{:S(2)}, u32[]{:S(2)}) collective-permute-start(bf16[16,2048]{1,0:T(8,128)(2,1)} %tokens_ref.3), channel_id=1, source_target_pairs={{0,4},{4,0},{8,12},{12,8},{1,5},{5,1},{9,13},{13,9},{2,6},{6,2},{1... | collective-permute-start | bytes 196616 | tf_op jit(solution)/shard_map/ppermute | solution.py:284
  5.6 6.7 %collective-permute-start.3 = (bf16[16,2048]{1,0:T(8,128)(2,1)}, bf16[16,2048]{1,0:T(8,128)(2,1)S(1)}, u32[]{:S(2)}, u32[]{:S(2)}) collective-permute-start(bf16[16,2048]{1,0:T(8,128)(2,1)} %tokens_ref.3), channel_id=1, source_target_pairs={{0,16},{16,0},{1,17},{17,1},{2,18},{18,2},{3,19},{19,3},{4,20},{20... | collective-permute-start | bytes 196616 | tf_op jit(solution)/shard_map/ppermute | solution.py:284
  12.3 5.8 %collective-permute-start.4 = (bf16[48,2048]{1,0:T(8,128)(2,1)S(1)}, bf16[48,2048]{1,0:T(8,128)(2,1)S(1)}, u32[]{:S(2)}, u32[]{:S(2)}) collective-permute-start(bf16[48,2048]{1,0:T(8,128)(2,1)S(1)} %join.3.refs_1_), channel_id=1, source_target_pairs={{0,16},{16,0},{1,17},{17,1},{2,18},{18,2},{3,19},{19,3},{4,20},{20... | collective-permute-start | bytes 589832 | tf_op jit(solution)/shard_map/ppermute | solution.py:284
  21.7 2.2 %collective-permute-start.5 = (bf16[2,64,2560]{2,1,0:T(8,128)(2,1)S(1)}, bf16[2,64,2560]{2,1,0:T(8,128)(2,1)S(1)}, u32[]{:S(2)}, u32[]{:S(2)}) collective-permute-start(bf16[2,64,2560]{2,1,0:T(8,128)(2,1)S(1)} %get-tuple-element.26), channel_id=1, source_target_pairs={{0,1},{1,0},{2,3},{3,2},{4,5},{5,4},{6,7},{7,6},{8,9},{9,8},{10,11... | collective-permute-start | bytes 1966088 | tf_op jit(solution)/shard_map/ppermute | solution.py:284
  23.9 18.7 %slice-start = ((s8[27262976]{0:T(1024)(128)(4,1)}), s8[4194304]{0:T(1024)(128)(4,1)S(1)}, s32[]{:S(2)}) async-start(s8[27262976]{0:T(1024)(128)(4,1)} %bitcast.2), calls=%async_computation | async-start | bytes 8388608
  23.9 18.6 %slice-start.1 = ((s8[27262976]{0:T(1024)(128)(4,1)}), s8[4194304]{0:T(1024)(128)(4,1)S(1)}, s32[]{:S(2)}) async-start(s8[27262976]{0:T(1024)(128)(4,1)} %bitcast.2), calls=%async_computation.1 | async-start | bytes 8388608
  24.0 18.6 %slice-start.2 = ((s8[27262976]{0:T(1024)(128)(4,1)}), s8[4194304]{0:T(1024)(128)(4,1)S(1)}, s32[]{:S(2)}) async-start(s8[27262976]{0:T(1024)(128)(4,1)} %bitcast.2), calls=%async_computation.2 | async-start | bytes 8388608
  24.0 18.6 %slice-start.3 = ((s8[27262976]{0:T(1024)(128)(4,1)}), s8[4194304]{0:T(1024)(128)(4,1)S(1)}, s32[]{:S(2)}) async-start(s8[27262976]{0:T(1024)(128)(4,1)} %bitcast.2), calls=%async_computation.3 | async-start | bytes 8388608
  24.0 18.6 %slice-start.4 = ((s8[27262976]{0:T(1024)(128)(4,1)}), s8[4194304]{0:T(1024)(128)(4,1)S(1)}, s32[]{:S(2)}) async-start(s8[27262976]{0:T(1024)(128)(4,1)} %bitcast.2), calls=%async_computation.4 | async-start | bytes 8388608
  24.0 18.6 %slice-start.5 = ((s8[27262976]{0:T(1024)(128)(4,1)}), s8[4194304]{0:T(1024)(128)(4,1)S(1)}, s32[]{:S(2)}) async-start(s8[27262976]{0:T(1024)(128)(4,1)} %bitcast.2), calls=%async_computation.5 | async-start | bytes 8388608
  24.0 18.6 %slice-start.6 = ((s8[27262976]{0:T(1024)(128)(4,1)}), s8[2097152]{0:T(1024)(128)(4,1)S(1)}, s32[]{:S(2)}) async-start(s8[27262976]{0:T(1024)(128)(4,1)} %bitcast.2), calls=%async_computation.6 | async-start | bytes 4194304
  24.0 9.8 %collective-permute-start.7 = (bf16[2,32,2560]{2,1,0:T(8,128)(2,1)S(1)}, bf16[2,32,2560]{2,1,0:T(8,128)(2,1)S(1)}, u32[]{:S(2)}, u32[]{:S(2)}) collective-permute-start(bf16[2,32,2560]{2,1,0:T(8,128)(2,1)S(1)} %pair_sum.2.refs_4_), channel_id=1, source_target_pairs={{0,2},{1,3},{2,0},{3,1},{4,6},{5,7},{6,4},{7,5},{8,10},{9,11},{10,... | collective-permute-start | bytes 983048 | tf_op jit(solution)/shard_map/ppermute | solution.py:284
  32.4 3.4 %collective-permute-start.6 = (bf16[2,32,1536]{2,1,0:T(8,128)(2,1)S(1)}, bf16[2,32,1536]{2,1,0:T(8,128)(2,1)S(1)}, u32[]{:S(2)}, u32[]{:S(2)}) collective-permute-start(bf16[2,32,1536]{2,1,0:T(8,128)(2,1)S(1)} %get-tuple-element.28), channel_id=1, source_target_pairs={{0,1},{1,0},{2,3},{3,2},{4,5},{5,4},{6,7},{7,6},{8,9},{9,8},{10,11... | collective-permute-start | bytes 589832 | tf_op jit(solution)/shard_map/ppermute | solution.py:284
  34.0 5.4 %collective-permute-start.11 = (bf16[16,2560]{1,0:T(8,128)(2,1)S(1)}, bf16[16,2560]{1,0:T(8,128)(2,1)S(1)}, u32[]{:S(2)}, u32[]{:S(2)}) collective-permute-start(bf16[16,2560]{1,0:T(8,128)(2,1)S(1)} %get-tuple-element.30.refs_0_), channel_id=1, source_target_pairs={{0,2},{1,3},{2,0},{3,1},{4,6},{5,7},{6,4},{7,5},{8,10},{9,11},{10,... | collective-permute-start | bytes 245768 | tf_op jit(solution)/shard_map/ppermute | solution.py:284
  35.8 4.8 %collective-permute-start.8 = (bf16[2,16,1536]{2,1,0:T(8,128)(2,1)S(1)}, bf16[2,16,1536]{2,1,0:T(8,128)(2,1)S(1)}, u32[]{:S(2)}, u32[]{:S(2)}) collective-permute-start(bf16[2,16,1536]{2,1,0:T(8,128)(2,1)S(1)} %pair_sum.3), channel_id=1, source_target_pairs={{0,2},{1,3},{2,0},{3,1},{4,6},{5,7},{6,4},{7,5},{8,10},{9,11},{10,... | collective-permute-start | bytes 294920 | tf_op jit(solution)/shard_map/ppermute | solution.py:284
  36.2 4.4 %collective-permute-start.9 = (bf16[16,2560]{1,0:T(8,128)(2,1)S(1)}, bf16[16,2560]{1,0:T(8,128)(2,1)S(1)}, u32[]{:S(2)}, u32[]{:S(2)}) collective-permute-start(bf16[16,2560]{1,0:T(8,128)(2,1)S(1)} %get-tuple-element.29), channel_id=1, source_target_pairs={{0,16},{16,0},{1,17},{17,1},{2,18},{18,2},{3,19},{19,3},{4,20},{20... | collective-permute-start | bytes 245768 | tf_op jit(solution)/shard_map/ppermute | solution.py:284
  39.4 3.1 %collective-permute-start.12 = (bf16[32,2560]{1,0:T(8,128)(2,1)S(1)}, bf16[32,2560]{1,0:T(8,128)(2,1)S(1)}, u32[]{:S(2)}, u32[]{:S(2)}) collective-permute-start(bf16[32,2560]{1,0:T(8,128)(2,1)S(1)} %join.4), channel_id=1, source_target_pairs={{0,1},{1,0},{2,3},{3,2},{4,5},{5,4},{6,7},{7,6},{8,9},{9,8},{10,11... | collective-permute-start | bytes 491528 | tf_op jit(solution)/shard_map/ppermute | solution.py:284
  40.7 5.0 %collective-permute-start.10 = (bf16[16,4096]{1,0:T(8,128)(2,1)S(1)}, bf16[16,4096]{1,0:T(8,128)(2,1)S(1)}, u32[]{:S(2)}, u32[]{:S(2)}) collective-permute-start(bf16[16,4096]{1,0:T(8,128)(2,1)S(1)} %combine.3.refs_0_), channel_id=1, source_target_pairs={{0,2},{1,3},{2,0},{3,1},{4,6},{5,7},{6,4},{7,5},{8,10},{9,11},{10,... | collective-permute-start | bytes 393224 | tf_op jit(solution)/shard_map/ppermute | solution.py:284
  45.8 1.6 %collective-permute-start.13 = (bf16[32,4096]{1,0:T(8,128)(2,1)S(1)}, bf16[32,4096]{1,0:T(8,128)(2,1)S(1)}, u32[]{:S(2)}, u32[]{:S(2)}) collective-permute-start(bf16[32,4096]{1,0:T(8,128)(2,1)S(1)} %join.5), channel_id=1, source_target_pairs={{0,1},{1,0},{2,3},{3,2},{4,5},{5,4},{6,7},{7,6},{8,9},{9,8},{10,11... | collective-permute-start | bytes 786440 | tf_op jit(solution)/shard_map/ppermute | solution.py:284
  51.0 6.9 %collective-permute-start.14 = (bf16[16,2048]{1,0:T(8,128)(2,1)S(1)}, bf16[16,2048]{1,0:T(8,128)(2,1)S(1)}, u32[]{:S(2)}, u32[]{:S(2)}) collective-permute-start(bf16[16,2048]{1,0:T(8,128)(2,1)S(1)} %get-tuple-element.32), channel_id=1, source_target_pairs={{0,12},{4,8},{8,4},{12,0},{1,13},{5,9},{9,5},{13,1},{2,14},{6,10},... | collective-permute-start | bytes 196616 | tf_op jit(solution)/shard_map/ppermute | solution.py:284
  54.9 5.7 %collective-permute-start.15 = (bf16[16,2048]{1,0:T(8,128)(2,1)S(1)}, bf16[16,2048]{1,0:T(8,128)(2,1)S(1)}, u32[]{:S(2)}, u32[]{:S(2)}) collective-permute-start(bf16[16,2048]{1,0:T(8,128)(2,1)S(1)} %get-tuple-element.33), channel_id=1, source_target_pairs={{0,8},{4,12},{8,0},{12,4},{1,9},{5,13},{9,1},{13,5},{2,10},{6,14},... | collective-permute-start | bytes 196616 | tf_op jit(solution)/shard_map/ppermute | solution.py:284
  54.9 5.7 %collective-permute-start.16 = (bf16[16,2048]{1,0:T(8,128)(2,1)S(1)}, bf16[16,2048]{1,0:T(8,128)(2,1)S(1)}, u32[]{:S(2)}, u32[]{:S(2)}) collective-permute-start(bf16[16,2048]{1,0:T(8,128)(2,1)S(1)} %get-tuple-element.34), channel_id=1, source_target_pairs={{0,4},{4,0},{8,12},{12,8},{1,5},{5,1},{9,13},{13,9},{2,6},{6,2},{1... | collective-permute-start | bytes 196616 | tf_op jit(solution)/shard_map/ppermute | solution.py:284

commit v8 on v7

--- a/solution.py
+++ b/solution.py
@@ -181,53 +181,57 @@
     )(mine, got, *behind)
 
 
-def mark_kernel(_, out_ref):
-    out_ref[...] = jnp.zeros_like(out_ref)
-
-
-def mark(array):
-    return pl.pallas_call(
-        mark_kernel,
-        in_specs=[spec(pl.ANY)],
+def later_kernel(array_ref, *refs):
+    refs[-1][...] = array_ref[...]
+
+
+def later(array, behind):
+    return pl.pallas_call(
+        later_kernel,
+        in_specs=[spec(pltpu.VMEM)] + [spec(pl.ANY)] * len(behind),
         out_specs=spec(pltpu.VMEM),
-        out_shape=jax.ShapeDtypeStruct((8, 128), jnp.float32),
+        out_shape=jax.ShapeDtypeStruct(array.shape, array.dtype),
         compiler_params=params(1),
         cost_estimate=COST,
-        name="mark",
-    )(array)
-
-
-def combine_kernel(n_left, n_outs, mine_ref, got_ref, chip_ref, *refs):
-    outs = refs[-n_outs:]
-    rows, first = chip_ref.shape[1], 0
-    for left in refs[:n_left]:
-        first = left.shape[1]
-        outs[0][:, :first] = left[...]
-    for a, b in pieces_of(chip_ref.shape[2], TILE):
-        gate, up = (
-            mine_ref[k, :rows, a:b].astype(jnp.float32)
-            + got_ref[k, :rows, a:b].astype(jnp.float32)
-            + chip_ref[k, :, a:b].astype(jnp.float32)
-            for k in range(2)
-        )
-        hidden = (gate / (1 + jnp.exp(-gate)) * up).astype(jnp.bfloat16)
-        for i, out in enumerate(outs):
-            out[:, first + a : first + b] = hidden[i * ROWS : (i + 1) * ROWS]
-
-
-def combine(mine, got, from_chip, left, behind):
-    _, rows, width = from_chip.shape
-    n_outs = rows // ROWS
-    width += sum(x.shape[1] for x in left)
-    return pl.pallas_call(
-        functools.partial(combine_kernel, len(left), n_outs),
-        in_specs=[spec(pltpu.VMEM)] * (3 + len(left)) + [spec(pl.ANY)] * len(behind),
+        name="later",
+    )(array, *behind)
+
+
+def combine_kernel(n_left, n_sums, n_outs, *refs):
+    lefts, refs, outs = refs[:n_left], refs[n_left:], refs[-n_outs:]
+    first = 0
+    for left in lefts:
+        outs[0][:, first : first + left.shape[1]] = left[...]
+        first += left.shape[1]
+    for i in range(n_sums):
+        mine_ref, got_ref, chip_ref = refs[3 * i : 3 * i + 3]
+        _, rows, width = chip_ref.shape
+        for a, b in pieces_of(width, TILE):
+            gate, up = (
+                mine_ref[k, :rows, a:b].astype(jnp.float32)
+                + got_ref[k, :rows, a:b].astype(jnp.float32)
+                + chip_ref[k, :, a:b].astype(jnp.float32)
+                for k in range(2)
+            )
+            hidden = (gate / (1 + jnp.exp(-gate)) * up).astype(jnp.bfloat16)
+            for j, out in enumerate(outs):
+                out[:, first + a : first + b] = hidden[j * ROWS : (j + 1) * ROWS]
+        first += width
+
+
+def combine(sums, left, behind):
+    n_outs = sums[0][2].shape[1] // ROWS
+    width = sum(x.shape[1] for x in left) + sum(chip.shape[2] for _, _, chip in sums)
+    args = [*left, *(x for triple in sums for x in triple)]
+    return pl.pallas_call(
+        functools.partial(combine_kernel, len(left), len(sums), n_outs),
+        in_specs=[spec(pltpu.VMEM)] * len(args) + [spec(pl.ANY)] * len(behind),
         out_specs=[spec(pltpu.VMEM)] * n_outs,
         out_shape=[jax.ShapeDtypeStruct((ROWS, width), jnp.bfloat16)] * n_outs,
         compiler_params=params(2),
         cost_estimate=COST,
         name="combine",
-    )(mine, got, from_chip, *left, *behind)
+    )(*args, *behind)
 
 
 def down_kernel(n_pieces, has_acc, last, segments, where, *refs):
@@ -298,26 +302,27 @@
     near = join(by_hid, [own, far_own])
     far = swap(near, "rep", 1)
 
-    weights = [w for fetched in early for w in fetched[:2]]
-    mine, theirs = gate_up(where, [own, near, far_own, far], weights, [], [])
-    got = swap(theirs, "wid", 1)
+    sums, to_chips, behind = [], [], [early[1][0]]
+    for weights in early:
+        mine, theirs = gate_up(where, [own, near, far_own, far], weights[:2], [], behind)
+        behind = [mine]
+        got = swap(theirs, "wid", 1)
+        to_chips.append(pair_sum(mine, got, []))
+        sums.append((mine, got, swap(to_chips[-1], "wid", 2)))
+    segments = [(bounds[2], widths[2]), (half + bounds[2], widths[2])]
+    mine, theirs = gate_up(where, [own, near], [gate_weight, up_weight], segments, to_chips)
+    got = swap(later(theirs, [s[2] for s in sums]), "wid", 1)
     to_chip = pair_sum(mine, got, [])
-    from_chip = swap(to_chip, "wid", 2)
-    segments = [(bounds[2], widths[2]), (half + bounds[2], widths[2])]
-    last_mine, theirs = gate_up(where, [own, near], [gate_weight, up_weight], segments, [to_chip])
-    last_got = swap(theirs, "wid", 1)
-    last_to_chip = pair_sum(last_mine, last_got, [mark(from_chip)])
-    last_from_chip = swap(last_to_chip, "wid", 2)
-
-    keep, give = combine(mine, got, from_chip, [], [])
-    far_columns = swap(give, "rep", 1)
-    (rest,) = combine(last_mine, last_got, last_from_chip, [far_columns], [])
+    last_sum = (mine, got, swap(to_chip, "wid", 2))
+
+    keep, give = combine(sums, [], [to_chip])
+    (rest,) = combine([last_sum], [swap(give, "rep", 1)], [])
     rest_segments = [(-1, half, bounds[2])] + [(0, start, width) for start, width in segments]
-    acc, behind = None, []
+    acc, behind = None, [rest]
     for hidden, parts in ((keep, [(1, 0, bounds[2])]), (rest, rest_segments)):
         other = swap(hidden, "wid", 2)
         crossed = swap(join([hidden, other], behind), "wid", 1)
-        acc = down(where, [hidden, other, crossed], down_weight, acc, parts, bool(behind))
+        acc = down(where, [hidden, other, crossed], down_weight, acc, parts, hidden is rest)
         behind = [acc]
 
     mixed = acc[0].astype(f32)

time: 61.4 us -> 64.9 us (1.057)
  waiting for transfers between devices: 13.3 us -> 16.7 us
    ppermute x17 -> x19, waiting for transfers between devices: 13.3 us -> 16.7 us  [swap(): return lax.ppermute(x, axis, [(i, i ^ step) for i in range(n)])]
    pallas_call x2 -> x3, Pallas kernels: 10.2 us -> 10.7 us  [gate_up(): pl.pallas_call(functools.partial(gate_up_kernel, len(arrays), len(weights...]
    ppermute x17 -> x19, starting transfers between devices: 20 us -> 19.6 us  [swap(): return lax.ppermute(x, axis, [(i, i ^ step) for i in range(n)])]
  transfers between devices with their start and end apart: 17 -> 19, of which waited for: 8 -> 10; matrix products, arithmetic and copies ran while one was open for 0% -> 0% of each run, Pallas kernels for 32% -> 30%
where the time goes in v8:
time: 64.9 us; the launch traced here: 64.8 us
  Pallas kernels  27.4 us (42%)
  starting transfers between devices  19.6 us (30%)
  waiting for transfers between devices  16.7 us (26%)
  other arithmetic  0.74 us (1%)
    ppermute x19, starting transfers between devices, swap(): return lax.ppermute(x, axis, [(i, i ^ step) for i in range(n)])  19.6 us
    ppermute x19, waiting for transfers between devices, swap(): return lax.ppermute(x, axis, [(i, i ^ step) for i in range(n)])  16.7 us
    pallas_call x3, Pallas kernels, gate_up(): pl.pallas_call(functools.partial(gate_up_kernel, len(arrays), len(weights...  10.7 us
    pallas_call x2, Pallas kernels, fetch(): pl.pallas_call(functools.partial(fetch_kernel, first), in_specs=[spec(plt...  10.2 us
    pallas_call x2, Pallas kernels, down(): pl.pallas_call(functools.partial(down_kernel, len(pieces), prev is not No...  6.06 us
  transfers between devices with their start and end apart: 19, of which 10 were waited for; matrix products, arithmetic and copies ran while one was open for 0% of the time, Pallas kernels for 30%

profile of v8, /device:TPU:0, one launch (start us, length us, event | category | flops | bytes accessed | tf_op | source)
XLA Modules:
  0.0 64.8 jit_solution(2229173959117933699)
XLA Ops:
  0.0 5.0 %collective-permute-start.2 = (bf16[16,2048]{1,0:T(8,128)(2,1)}, bf16[16,2048]{1,0:T(8,128)(2,1)S(1)}, u32[]{:S(2)}, u32[]{:S(2)}) collective-permute-start(bf16[16,2048]{1,0:T(8,128)(2,1)} %tokens_ref.3), channel_id=1, source_target_pairs={{0,12},{4,8},{8,4},{12,0},{1,13},{5,9},{9,5},{13,1},{2,14},{6,10},... | collective-permute-start | bytes 196616 | tf_op jit(solution)/shard_map/ppermute | solution.py:288
  5.0 0.0 collective-permute-start.1
  5.1 0.6 collective-permute-start
  5.6 1.7 %collective-permute-start.3 = (bf16[16,2048]{1,0:T(8,128)(2,1)}, bf16[16,2048]{1,0:T(8,128)(2,1)S(1)}, u32[]{:S(2)}, u32[]{:S(2)}) collective-permute-start(bf16[16,2048]{1,0:T(8,128)(2,1)} %tokens_ref.3), channel_id=1, source_target_pairs={{0,16},{16,0},{1,17},{17,1},{2,18},{18,2},{3,19},{19,3},{4,20},{20... | collective-permute-start | bytes 196616 | tf_op jit(solution)/shard_map/ppermute | solution.py:288
  7.4 0.1 pad_add_fusion.where
  7.4 4.8 %fetch.2 = (bf16[2048,1280]{1,0:T(8,128)(2,1)S(1)}, bf16[2048,1280]{1,0:T(8,128)(2,1)S(1)}, bf16[16,2048]{1,0:T(8,128)(2,1)S(1)}) custom-call(s32[2]{0:T(128)S(1)} %pad_add_fusion.where, bf16[2048,6656]{1,0:T(8,128)(2,1)} %refs_2_.1, bf16[2048,6656]{1,0:T(8,128)(2,1)} %refs_3_.3, bf16[16,2048]{1,0:T(8,128)(2,1)} %tokens_ref.3), custom_call_target="tpu_custom_call" | custom-call | bytes 1024 | tf_op jit(solution)/shard_map/fetch/pallas_call | solution.py:73
  12.3 0.0 collective-permute-done.refs_0_
  12.3 0.4 collective-permute-start.4
  12.7 5.4 %fetch.3 = (bf16[2048,1280]{1,0:T(8,128)(2,1)S(1)}, bf16[2048,1280]{1,0:T(8,128)(2,1)S(1)}, bf16[16,2048]{1,0:T(8,128)(2,1)}) custom-call(s32[2]{0:T(128)S(1)} %pad_add_fusion.where, bf16[2048,6656]{1,0:T(8,128)(2,1)} %refs_2_.1, bf16[2048,6656]{1,0:T(8,128)(2,1)} %refs_3_.3, bf16[16,2048]{1,0:T(8,128)(2,1)} %tokens_ref.3), custom_call_target="tpu_custom_call" | custom-call | bytes 1024 | tf_op jit(solution)/shard_map/fetch/pallas_call | solution.py:73
  18.1 0.0 collective-permute-done.4.refs_3_
  18.1 2.2 %gate_up.3 = (bf16[2,64,1280]{2,1,0:T(8,128)(2,1)S(1)}, bf16[2,64,1280]{2,1,0:T(8,128)(2,1)S(1)}) custom-call(s32[2]{0:T(128)S(1)} %pad_add_fusion.where, bf16[16,2048]{1,0:T(8,128)(2,1)S(1)} %get-tuple-element.22.refs_3_.refs_0_, bf16[48,2048]{1,0:T(8,128)(2,1)S(1)} %join.3.refs_1_, bf16[16,2048]{1,0:T(8,128)(2,1)S(1)} %collective-permute-done.3.refs_4_.refs_2_, ...), custom_call_target="tpu_custom_call" | custom-call | bytes 1024 | tf_op jit(solution)/shard_map/gate_up/pallas_call | solution.py:148
  20.3 2.2 %gate_up.4 = (bf16[2,64,1280]{2,1,0:T(8,128)(2,1)S(1)}, bf16[2,64,1280]{2,1,0:T(8,128)(2,1)S(1)}) custom-call(s32[2]{0:T(128)S(1)} %pad_add_fusion.where, bf16[16,2048]{1,0:T(8,128)(2,1)S(1)} %get-tuple-element.22.refs_3_.refs_0_, bf16[48,2048]{1,0:T(8,128)(2,1)S(1)} %join.3.refs_1_, bf16[16,2048]{1,0:T(8,128)(2,1)S(1)} %collective-permute-done.3.refs_4_.refs_2_, ...), custom_call_target="tpu_custom_call" | custom-call | bytes 1024 | tf_op jit(solution)/shard_map/gate_up/pallas_call | solution.py:148
  22.5 0.1 collective-permute-start.7
  22.5 0.5 collective-permute-start.5
  23.0 1.1 %collective-permute-done.7.got_ref.refs_4_ = bf16[2,64,1280]{2,1,0:T(8,128)(2,1)S(1)} collective-permute-done((bf16[2,64,1280]{2,1,0:T(8,128)(2,1)S(1)}, bf16[2,64,1280]{2,1,0:T(8,128)(2,1)S(1)}, u32[]{:S(2)}, u32[]{:S(2)}) %collective-permute-start.7) | collective-permute-done | bytes 327712 | tf_op jit(solution)/shard_map/ppermute | solution.py:288
  24.2 1.8 %collective-permute-start.8 = (bf16[2,32,1280]{2,1,0:T(8,128)(2,1)S(1)}, bf16[2,32,1280]{2,1,0:T(8,128)(2,1)S(1)}, u32[]{:S(2)}, u32[]{:S(2)}) collective-permute-start(bf16[2,32,1280]{2,1,0:T(8,128)(2,1)S(1)} %pair_sum.4.refs_5_), channel_id=1, source_target_pairs={{0,2},{1,3},{2,0},{3,1},{4,6},{5,7},{6,4},{7,5},{8,10},{9,11},{10,... | collective-permute-start | bytes 491528 | tf_op jit(solution)/shard_map/ppermute | solution.py:288
  26.0 0.0 collective-permute-done.5.got_ref.refs_1_
  26.0 0.0 slice-start.1
  26.0 0.0 slice-start.3
  26.0 0.0 slice-start.4
  26.1 0.4 collective-permute-start.6
  26.5 6.4 %gate_up.5 = (bf16[2,32,1536]{2,1,0:T(8,128)(2,1)S(1)}, bf16[2,32,1536]{2,1,0:T(8,128)(2,1)S(1)}) custom-call(s32[2]{0:T(128)S(1)} %pad_add_fusion.where, bf16[16,2048]{1,0:T(8,128)(2,1)S(1)} %get-tuple-element.22.refs_3_.refs_0_, bf16[48,2048]{1,0:T(8,128)(2,1)S(1)} %join.3.refs_1_, bf16[2048,6656]{1,0:T(8,128)(2,1)} %refs_2_.1, ...), custom_call_target="tpu_custom_call" | custom-call | bytes 1024 | tf_op jit(solution)/shard_map/gate_up/pallas_call | solution.py:148
  32.9 0.0 collective-permute-done.8.refs_1_.refs_5_
  32.9 1.1 %collective-permute-done.6.refs_0_.refs_2_ = bf16[2,32,1280]{2,1,0:T(8,128)(2,1)S(1)} collective-permute-done((bf16[2,32,1280]{2,1,0:T(8,128)(2,1)S(1)}, bf16[2,32,1280]{2,1,0:T(8,128)(2,1)S(1)}, u32[]{:S(2)}, u32[]{:S(2)}) %collective-permute-start.6) | collective-permute-done | bytes 163872 | tf_op jit(solution)/shard_map/ppermute | solution.py:288
  34.0 0.1 collective-permute-start.9
  34.1 1.4 %collective-permute-done.9.got_ref.refs_2_ = bf16[2,32,1536]{2,1,0:T(8,128)(2,1)S(1)} collective-permute-done((bf16[2,32,1536]{2,1,0:T(8,128)(2,1)S(1)}, bf16[2,32,1536]{2,1,0:T(8,128)(2,1)S(1)}, u32[]{:S(2)}, u32[]{:S(2)}) %collective-permute-start.9) | collective-permute-done | bytes 196640 | tf_op jit(solution)/shard_map/ppermute | solution.py:288
  35.6 1.8 %collective-permute-start.11 = (bf16[2,16,1536]{2,1,0:T(8,128)(2,1)S(1)}, bf16[2,16,1536]{2,1,0:T(8,128)(2,1)S(1)}, u32[]{:S(2)}, u32[]{:S(2)}) collective-permute-start(bf16[2,16,1536]{2,1,0:T(8,128)(2,1)S(1)} %pair_sum.5.refs_6_), channel_id=1, source_target_pairs={{0,2},{1,3},{2,0},{3,1},{4,6},{5,7},{6,4},{7,5},{8,10},{9,11},{10,... | collective-permute-start | bytes 294920 | tf_op jit(solution)/shard_map/ppermute | solution.py:288
  37.3 0.2 combine.2
  37.5 1.6 %collective-permute-start.10 = (bf16[16,2560]{1,0:T(8,128)(2,1)S(1)}, bf16[16,2560]{1,0:T(8,128)(2,1)S(1)}, u32[]{:S(2)}, u32[]{:S(2)}) collective-permute-start(bf16[16,2560]{1,0:T(8,128)(2,1)S(1)} %get-tuple-element.33), channel_id=1, source_target_pairs={{0,16},{16,0},{1,17},{17,1},{2,18},{18,2},{3,19},{19,3},{4,20},{20... | collective-permute-start | bytes 245768 | tf_op jit(solution)/shard_map/ppermute | solution.py:288
  39.1 0.5 collective-permute-start.13
  39.7 2.4 %collective-permute-done.10.refs_0_ = bf16[16,2560]{1,0:T(8,128)(2,1)S(1)} collective-permute-done((bf16[16,2560]{1,0:T(8,128)(2,1)S(1)}, bf16[16,2560]{1,0:T(8,128)(2,1)S(1)}, u32[]{:S(2)}, u32[]{:S(2)}) %collective-permute-start.10) | collective-permute-done | bytes 81952 | tf_op jit(solution)/shard_map/ppermute | solution.py:288
  42.0 0.0 collective-permute-done.11.refs_3_
  42.0 0.1 combine.3.refs_2_.refs_0_
  42.1 1.4 %collective-permute-done.13.refs_1_ = bf16[16,2560]{1,0:T(8,128)(2,1)S(1)} collective-permute-done((bf16[16,2560]{1,0:T(8,128)(2,1)S(1)}, bf16[16,2560]{1,0:T(8,128)(2,1)S(1)}, u32[]{:S(2)}, u32[]{:S(2)}) %collective-permute-start.13) | collective-permute-done | bytes 81952 | tf_op jit(solution)/shard_map/ppermute | solution.py:288
  43.6 0.1 collective-permute-start.14
  43.7 0.6 collective-permute-start.12
  44.3 0.8 %collective-permute-done.14.refs_2_ = bf16[32,2560]{1,0:T(8,128)(2,1)S(1)} collective-permute-done((bf16[32,2560]{1,0:T(8,128)(2,1)S(1)}, bf16[32,2560]{1,0:T(8,128)(2,1)S(1)}, u32[]{:S(2)}, u32[]{:S(2)}) %collective-permute-start.14) | collective-permute-done | bytes 163872 | tf_op jit(solution)/shard_map/ppermute | solution.py:288
  45.1 2.5 %down.2.refs_2_.refs_4_ = f32[64,2048]{1,0:T(8,128)S(1)} custom-call(s32[2]{0:T(128)S(1)} %pad_add_fusion.where, bf16[16,2560]{1,0:T(8,128)(2,1)S(1)} %get-tuple-element.34.refs_0_, bf16[16,2560]{1,0:T(8,128)(2,1)S(1)} %collective-permute-done.13.refs_1_, bf16[32,2560]{1,0:T(8,128)(2,1)S(1)} %collective-permute-done.14.refs_2_, bf16[6656,2048]{1,0:T(8,128)(2,1)S(1)} %bitcast.3), custom_call_target="tpu_custom_call" | custom-call | bytes 1024 | tf_op jit(solution)/shard_map/down/pallas_call | solution.py:268
  47.6 2.0 %collective-permute-done.12.refs_1_ = bf16[16,4096]{1,0:T(8,128)(2,1)S(1)} collective-permute-done((bf16[16,4096]{1,0:T(8,128)(2,1)S(1)}, bf16[16,4096]{1,0:T(8,128)(2,1)S(1)}, u32[]{:S(2)}, u32[]{:S(2)}) %collective-permute-start.12) | collective-permute-done | bytes 131104 | tf_op jit(solution)/shard_map/ppermute | solution.py:288
  49.6 0.1 collective-permute-start.15
  49.7 1.5 %collective-permute-done.15.refs_2_ = bf16[32,4096]{1,0:T(8,128)(2,1)S(1)} collective-permute-done((bf16[32,4096]{1,0:T(8,128)(2,1)S(1)}, bf16[32,4096]{1,0:T(8,128)(2,1)S(1)}, u32[]{:S(2)}, u32[]{:S(2)}) %collective-permute-start.15) | collective-permute-done | bytes 262176 | tf_op jit(solution)/shard_map/ppermute | solution.py:288
  51.2 3.6 %down.3 = (bf16[16,2048]{1,0:T(8,128)(2,1)S(1)}, bf16[16,2048]{1,0:T(8,128)(2,1)S(1)}, bf16[16,2048]{1,0:T(8,128)(2,1)S(1)}, bf16[16,2048]{1,0:T(8,128)(2,1)S(1)}) custom-call(s32[2]{0:T(128)S(1)} %pad_add_fusion.where, bf16[16,4096]{1,0:T(8,128)(2,1)S(1)} %combine.3.refs_2_.refs_0_, bf16[16,4096]{1,0:T(8,128)(2,1)S(1)} %collective-permute-done.12.refs_1_, ...), custom_call_target="tpu_custom_call" | custom-call | bytes 1024 | tf_op jit(solution)/shard_map/down/pallas_call | solution.py:268
  54.8 3.7 %collective-permute-start.16 = (bf16[16,2048]{1,0:T(8,128)(2,1)S(1)}, bf16[16,2048]{1,0:T(8,128)(2,1)S(1)}, u32[]{:S(2)}, u32[]{:S(2)}) collective-permute-start(bf16[16,2048]{1,0:T(8,128)(2,1)S(1)} %get-tuple-element.36), channel_id=1, source_target_pairs={{0,12},{4,8},{8,4},{12,0},{1,13},{5,9},{9,5},{13,1},{2,14},{6,10},... | collective-permute-start | bytes 196616 | tf_op jit(solution)/shard_map/ppermute | solution.py:288
  58.5 0.8 %collective-permute-start.18 = (bf16[16,2048]{1,0:T(8,128)(2,1)S(1)}, bf16[16,2048]{1,0:T(8,128)(2,1)S(1)}, u32[]{:S(2)}, u32[]{:S(2)}) collective-permute-start(bf16[16,2048]{1,0:T(8,128)(2,1)S(1)} %get-tuple-element.38), channel_id=1, source_target_pairs={{0,4},{4,0},{8,12},{12,8},{1,5},{5,1},{9,13},{13,9},{2,6},{6,2},{1... | collective-permute-start | bytes 196616 | tf_op jit(solution)/shard_map/ppermute | solution.py:288
  59.3 2.3 %collective-permute-done.16 = bf16[16,2048]{1,0:T(8,128)(2,1)S(1)} collective-permute-done((bf16[16,2048]{1,0:T(8,128)(2,1)S(1)}, bf16[16,2048]{1,0:T(8,128)(2,1)S(1)}, u32[]{:S(2)}, u32[]{:S(2)}) %collective-permute-start.16) | collective-permute-done | bytes 65568 | tf_op jit(solution)/shard_map/ppermute | solution.py:288
  61.6 2.6 %collective-permute-done.17 = bf16[16,2048]{1,0:T(8,128)(2,1)S(1)} collective-permute-done((bf16[16,2048]{1,0:T(8,128)(2,1)S(1)}, bf16[16,2048]{1,0:T(8,128)(2,1)S(1)}, u32[]{:S(2)}, u32[]{:S(2)}) %collective-permute-start.17) | collective-permute-done | bytes 65568 | tf_op jit(solution)/shard_map/ppermute | solution.py:288
  64.1 0.0 collective-permute-done.18
  64.1 0.7 %add_convert_fusion = bf16[16,2048]{1,0:T(8,128)(2,1)} fusion(bf16[16,2048]{1,0:T(8,128)(2,1)S(1)} %collective-permute-done.18, bf16[16,2048]{1,0:T(8,128)(2,1)S(1)} %collective-permute-done.17, bf16[16,2048]{1,0:T(8,128)(2,1)S(1)} %collective-permute-done.16, bf16[16,2048]{1,0:T(8,128)(2,1)S(1)} %get-tuple-element.35), kind=kLoop, calls=%fused_computation | loop fusion | flops 262144 | bytes 327680 | tf_op jit(solution)/shard_map/convert_element_type | solution.py:331
  (23 shorter events, 0.2 us)
Async XLA Ops:
  0.0 12.2 %collective-permute-start.2 = (bf16[16,2048]{1,0:T(8,128)(2,1)}, bf16[16,2048]{1,0:T(8,128)(2,1)S(1)}, u32[]{:S(2)}, u32[]{:S(2)}) collective-permute-start(bf16[16,2048]{1,0:T(8,128)(2,1)} %tokens_ref.3), channel_id=1, source_target_pairs={{0,12},{4,8},{8,4},{12,0},{1,13},{5,9},{9,5},{13,1},{2,14},{6,10},... | collective-permute-start | bytes 196616 | tf_op jit(solution)/shard_map/ppermute | solution.py:288
  5.0 7.2 %collective-permute-start.1 = (bf16[16,2048]{1,0:T(8,128)(2,1)}, bf16[16,2048]{1,0:T(8,128)(2,1)S(1)}, u32[]{:S(2)}, u32[]{:S(2)}) collective-permute-start(bf16[16,2048]{1,0:T(8,128)(2,1)} %tokens_ref.3), channel_id=1, source_target_pairs={{0,8},{4,12},{8,0},{12,4},{1,9},{5,13},{9,1},{13,5},{2,10},{6,14},... | collective-permute-start | bytes 196616 | tf_op jit(solution)/shard_map/ppermute | solution.py:288
  5.1 7.2 %collective-permute-start = (bf16[16,2048]{1,0:T(8,128)(2,1)}, bf16[16,2048]{1,0:T(8,128)(2,1)S(1)}, u32[]{:S(2)}, u32[]{:S(2)}) collective-permute-start(bf16[16,2048]{1,0:T(8,128)(2,1)} %tokens_ref.3), channel_id=1, source_target_pairs={{0,4},{4,0},{8,12},{12,8},{1,5},{5,1},{9,13},{13,9},{2,6},{6,2},{1... | collective-permute-start | bytes 196616 | tf_op jit(solution)/shard_map/ppermute | solution.py:288
  5.6 6.7 %collective-permute-start.3 = (bf16[16,2048]{1,0:T(8,128)(2,1)}, bf16[16,2048]{1,0:T(8,128)(2,1)S(1)}, u32[]{:S(2)}, u32[]{:S(2)}) collective-permute-start(bf16[16,2048]{1,0:T(8,128)(2,1)} %tokens_ref.3), channel_id=1, source_target_pairs={{0,16},{16,0},{1,17},{17,1},{2,18},{18,2},{3,19},{19,3},{4,20},{20... | collective-permute-start | bytes 196616 | tf_op jit(solution)/shard_map/ppermute | solution.py:288
  12.3 5.8 %collective-permute-start.4 = (bf16[48,2048]{1,0:T(8,128)(2,1)S(1)}, bf16[48,2048]{1,0:T(8,128)(2,1)S(1)}, u32[]{:S(2)}, u32[]{:S(2)}) collective-permute-start(bf16[48,2048]{1,0:T(8,128)(2,1)S(1)} %join.3.refs_1_), channel_id=1, source_target_pairs={{0,16},{16,0},{1,17},{17,1},{2,18},{18,2},{3,19},{19,3},{4,20},{20... | collective-permute-start | bytes 589832 | tf_op jit(solution)/shard_map/ppermute | solution.py:288
  22.5 1.7 %collective-permute-start.7 = (bf16[2,64,1280]{2,1,0:T(8,128)(2,1)S(1)}, bf16[2,64,1280]{2,1,0:T(8,128)(2,1)S(1)}, u32[]{:S(2)}, u32[]{:S(2)}) collective-permute-start(bf16[2,64,1280]{2,1,0:T(8,128)(2,1)S(1)} %get-tuple-element.30), channel_id=1, source_target_pairs={{0,1},{1,0},{2,3},{3,2},{4,5},{5,4},{6,7},{7,6},{8,9},{9,8},{10,11... | collective-permute-start | bytes 983048 | tf_op jit(solution)/shard_map/ppermute | solution.py:288
  22.5 3.4 %collective-permute-start.5 = (bf16[2,64,1280]{2,1,0:T(8,128)(2,1)S(1)}, bf16[2,64,1280]{2,1,0:T(8,128)(2,1)S(1)}, u32[]{:S(2)}, u32[]{:S(2)}) collective-permute-start(bf16[2,64,1280]{2,1,0:T(8,128)(2,1)S(1)} %get-tuple-element.27), channel_id=1, source_target_pairs={{0,1},{1,0},{2,3},{3,2},{4,5},{5,4},{6,7},{7,6},{8,9},{9,8},{10,11... | collective-permute-start | bytes 983048 | tf_op jit(solution)/shard_map/ppermute | solution.py:288
  24.2 8.7 %collective-permute-start.8 = (bf16[2,32,1280]{2,1,0:T(8,128)(2,1)S(1)}, bf16[2,32,1280]{2,1,0:T(8,128)(2,1)S(1)}, u32[]{:S(2)}, u32[]{:S(2)}) collective-permute-start(bf16[2,32,1280]{2,1,0:T(8,128)(2,1)S(1)} %pair_sum.4.refs_5_), channel_id=1, source_target_pairs={{0,2},{1,3},{2,0},{3,1},{4,6},{5,7},{6,4},{7,5},{8,10},{9,11},{10,... | collective-permute-start | bytes 491528 | tf_op jit(solution)/shard_map/ppermute | solution.py:288
  26.0 19.1 %slice-start = ((s8[27262976]{0:T(1024)(128)(4,1)}), s8[4194304]{0:T(1024)(128)(4,1)S(1)}, s32[]{:S(2)}) async-start(s8[27262976]{0:T(1024)(128)(4,1)} %bitcast.2), calls=%async_computation | async-start | bytes 8388608
  26.0 19.0 %slice-start.1 = ((s8[27262976]{0:T(1024)(128)(4,1)}), s8[4194304]{0:T(1024)(128)(4,1)S(1)}, s32[]{:S(2)}) async-start(s8[27262976]{0:T(1024)(128)(4,1)} %bitcast.2), calls=%async_computation.1 | async-start | bytes 8388608
  26.0 19.0 %slice-start.2 = ((s8[27262976]{0:T(1024)(128)(4,1)}), s8[4194304]{0:T(1024)(128)(4,1)S(1)}, s32[]{:S(2)}) async-start(s8[27262976]{0:T(1024)(128)(4,1)} %bitcast.2), calls=%async_computation.2 | async-start | bytes 8388608
  26.0 19.0 %slice-start.3 = ((s8[27262976]{0:T(1024)(128)(4,1)}), s8[4194304]{0:T(1024)(128)(4,1)S(1)}, s32[]{:S(2)}) async-start(s8[27262976]{0:T(1024)(128)(4,1)} %bitcast.2), calls=%async_computation.3 | async-start | bytes 8388608
  26.0 19.0 %slice-start.4 = ((s8[27262976]{0:T(1024)(128)(4,1)}), s8[4194304]{0:T(1024)(128)(4,1)S(1)}, s32[]{:S(2)}) async-start(s8[27262976]{0:T(1024)(128)(4,1)} %bitcast.2), calls=%async_computation.4 | async-start | bytes 8388608
  26.1 19.0 %slice-start.5 = ((s8[27262976]{0:T(1024)(128)(4,1)}), s8[4194304]{0:T(1024)(128)(4,1)S(1)}, s32[]{:S(2)}) async-start(s8[27262976]{0:T(1024)(128)(4,1)} %bitcast.2), calls=%async_computation.5 | async-start | bytes 8388608
  26.1 19.0 %slice-start.6 = ((s8[27262976]{0:T(1024)(128)(4,1)}), s8[2097152]{0:T(1024)(128)(4,1)S(1)}, s32[]{:S(2)}) async-start(s8[27262976]{0:T(1024)(128)(4,1)} %bitcast.2), calls=%async_computation.6 | async-start | bytes 4194304
  26.1 7.9 %collective-permute-start.6 = (bf16[2,32,1280]{2,1,0:T(8,128)(2,1)S(1)}, bf16[2,32,1280]{2,1,0:T(8,128)(2,1)S(1)}, u32[]{:S(2)}, u32[]{:S(2)}) collective-permute-start(bf16[2,32,1280]{2,1,0:T(8,128)(2,1)S(1)} %pair_sum.3.refs_4_), channel_id=1, source_target_pairs={{0,2},{1,3},{2,0},{3,1},{4,6},{5,7},{6,4},{7,5},{8,10},{9,11},{10,... | collective-permute-start | bytes 491528 | tf_op jit(solution)/shard_map/ppermute | solution.py:288
  34.0 1.5 %collective-permute-start.9 = (bf16[2,32,1536]{2,1,0:T(8,128)(2,1)S(1)}, bf16[2,32,1536]{2,1,0:T(8,128)(2,1)S(1)}, u32[]{:S(2)}, u32[]{:S(2)}) collective-permute-start(bf16[2,32,1536]{2,1,0:T(8,128)(2,1)S(1)} %later.1), channel_id=1, source_target_pairs={{0,1},{1,0},{2,3},{3,2},{4,5},{5,4},{6,7},{7,6},{8,9},{9,8},{10,11... | collective-permute-start | bytes 589832 | tf_op jit(solution)/shard_map/ppermute | solution.py:288
  35.6 6.5 %collective-permute-start.11 = (bf16[2,16,1536]{2,1,0:T(8,128)(2,1)S(1)}, bf16[2,16,1536]{2,1,0:T(8,128)(2,1)S(1)}, u32[]{:S(2)}, u32[]{:S(2)}) collective-permute-start(bf16[2,16,1536]{2,1,0:T(8,128)(2,1)S(1)} %pair_sum.5.refs_6_), channel_id=1, source_target_pairs={{0,2},{1,3},{2,0},{3,1},{4,6},{5,7},{6,4},{7,5},{8,10},{9,11},{10,... | collective-permute-start | bytes 294920 | tf_op jit(solution)/shard_map/ppermute | solution.py:288
  37.5 4.5 %collective-permute-start.10 = (bf16[16,2560]{1,0:T(8,128)(2,1)S(1)}, bf16[16,2560]{1,0:T(8,128)(2,1)S(1)}, u32[]{:S(2)}, u32[]{:S(2)}) collective-permute-start(bf16[16,2560]{1,0:T(8,128)(2,1)S(1)} %get-tuple-element.33), channel_id=1, source_target_pairs={{0,16},{16,0},{1,17},{17,1},{2,18},{18,2},{3,19},{19,3},{4,20},{20... | collective-permute-start | bytes 245768 | tf_op jit(solution)/shard_map/ppermute | solution.py:288
  39.1 4.4 %collective-permute-start.13 = (bf16[16,2560]{1,0:T(8,128)(2,1)S(1)}, bf16[16,2560]{1,0:T(8,128)(2,1)S(1)}, u32[]{:S(2)}, u32[]{:S(2)}) collective-permute-start(bf16[16,2560]{1,0:T(8,128)(2,1)S(1)} %get-tuple-element.34.refs_0_), channel_id=1, source_target_pairs={{0,2},{1,3},{2,0},{3,1},{4,6},{5,7},{6,4},{7,5},{8,10},{9,11},{10,... | collective-permute-start | bytes 245768 | tf_op jit(solution)/shard_map/ppermute | solution.py:288
  43.6 1.5 %collective-permute-start.14 = (bf16[32,2560]{1,0:T(8,128)(2,1)S(1)}, bf16[32,2560]{1,0:T(8,128)(2,1)S(1)}, u32[]{:S(2)}, u32[]{:S(2)}) collective-permute-start(bf16[32,2560]{1,0:T(8,128)(2,1)S(1)} %join.4), channel_id=1, source_target_pairs={{0,1},{1,0},{2,3},{3,2},{4,5},{5,4},{6,7},{7,6},{8,9},{9,8},{10,11... | collective-permute-start | bytes 491528 | tf_op jit(solution)/shard_map/ppermute | solution.py:288
  43.7 5.9 %collective-permute-start.12 = (bf16[16,4096]{1,0:T(8,128)(2,1)S(1)}, bf16[16,4096]{1,0:T(8,128)(2,1)S(1)}, u32[]{:S(2)}, u32[]{:S(2)}) collective-permute-start(bf16[16,4096]{1,0:T(8,128)(2,1)S(1)} %combine.3.refs_2_.refs_0_), channel_id=1, source_target_pairs={{0,2},{1,3},{2,0},{3,1},{4,6},{5,7},{6,4},{7,5},{8,10},{9,11},{10,... | collective-permute-start | bytes 393224 | tf_op jit(solution)/shard_map/ppermute | solution.py:288
  49.6 1.6 %collective-permute-start.15 = (bf16[32,4096]{1,0:T(8,128)(2,1)S(1)}, bf16[32,4096]{1,0:T(8,128)(2,1)S(1)}, u32[]{:S(2)}, u32[]{:S(2)}) collective-permute-start(bf16[32,4096]{1,0:T(8,128)(2,1)S(1)} %join.5), channel_id=1, source_target_pairs={{0,1},{1,0},{2,3},{3,2},{4,5},{5,4},{6,7},{7,6},{8,9},{9,8},{10,11... | collective-permute-start | bytes 786440 | tf_op jit(solution)/shard_map/ppermute | solution.py:288
  54.8 6.7 %collective-permute-start.16 = (bf16[16,2048]{1,0:T(8,128)(2,1)S(1)}, bf16[16,2048]{1,0:T(8,128)(2,1)S(1)}, u32[]{:S(2)}, u32[]{:S(2)}) collective-permute-start(bf16[16,2048]{1,0:T(8,128)(2,1)S(1)} %get-tuple-element.36), channel_id=1, source_target_pairs={{0,12},{4,8},{8,4},{12,0},{1,13},{5,9},{9,5},{13,1},{2,14},{6,10},... | collective-permute-start | bytes 196616 | tf_op jit(solution)/shard_map/ppermute | solution.py:288
  58.5 5.7 %collective-permute-start.17 = (bf16[16,2048]{1,0:T(8,128)(2,1)S(1)}, bf16[16,2048]{1,0:T(8,128)(2,1)S(1)}, u32[]{:S(2)}, u32[]{:S(2)}) collective-permute-start(bf16[16,2048]{1,0:T(8,128)(2,1)S(1)} %get-tuple-element.37), channel_id=1, source_target_pairs={{0,8},{4,12},{8,0},{12,4},{1,9},{5,13},{9,1},{13,5},{2,10},{6,14},... | collective-permute-start | bytes 196616 | tf_op jit(solution)/shard_map/ppermute | solution.py:288
  58.5 5.7 %collective-permute-start.18 = (bf16[16,2048]{1,0:T(8,128)(2,1)S(1)}, bf16[16,2048]{1,0:T(8,128)(2,1)S(1)}, u32[]{:S(2)}, u32[]{:S(2)}) collective-permute-start(bf16[16,2048]{1,0:T(8,128)(2,1)S(1)} %get-tuple-element.38), channel_id=1, source_target_pairs={{0,4},{4,0},{8,12},{12,8},{1,5},{5,1},{9,13},{13,9},{2,6},{6,2},{1... | collective-permute-start | bytes 196616 | tf_op jit(solution)/shard_map/ppermute | solution.py:288

commit v9 on v7

--- a/solution.py
+++ b/solution.py
@@ -181,22 +181,6 @@
     )(mine, got, *behind)
 
 
-def mark_kernel(_, out_ref):
-    out_ref[...] = jnp.zeros_like(out_ref)
-
-
-def mark(array):
-    return pl.pallas_call(
-        mark_kernel,
-        in_specs=[spec(pl.ANY)],
-        out_specs=spec(pltpu.VMEM),
-        out_shape=jax.ShapeDtypeStruct((8, 128), jnp.float32),
-        compiler_params=params(1),
-        cost_estimate=COST,
-        name="mark",
-    )(array)
-
-
 def combine_kernel(n_left, n_outs, mine_ref, got_ref, chip_ref, *refs):
     outs = refs[-n_outs:]
     rows, first = chip_ref.shape[1], 0
@@ -230,7 +214,7 @@
     )(mine, got, from_chip, *left, *behind)
 
 
-def down_kernel(n_pieces, has_acc, last, segments, where, *refs):
+def down_kernel(n_pieces, has_acc, last, segments, columns, where, *refs):
     pieces, refs = refs[:n_pieces], refs[n_pieces:]
     down_ref, refs = refs[0], refs[1:]
     prev_ref, refs = (refs[0], refs[1:]) if has_acc else (None, refs)
@@ -239,12 +223,13 @@
     for piece in pieces:
         lhs_ref[at : at + piece.shape[0], :] = piece[...]
         at += piece.shape[0]
-    for a, b in pieces_of(down_ref.shape[1], 2 * TILE):
-        part = prev_ref[:, a:b] if has_acc else 0.0
+    left = columns[0]
+    for a, b in pieces_of(acc_ref.shape[1], 2 * TILE):
+        part = prev_ref[:, left + a : left + b] if has_acc else 0.0
         at = 0
         for sign, start, depth in segments:
             rows = pl.ds(pl.multiple_of(sign * where[0] + start, TILE) if sign else start, depth)
-            part += jnp.dot(lhs_ref[:, at : at + depth], down_ref[rows, a:b], preferred_element_type=jnp.float32)
+            part += jnp.dot(lhs_ref[:, at : at + depth], down_ref[rows, left + a : left + b], preferred_element_type=jnp.float32)
             at += depth
         acc_ref[:, a:b] = part
     if last:
@@ -253,8 +238,8 @@
             out[...] = acc_ref[pl.ds(source, ROWS), :].astype(out.dtype)
 
 
-def down(where, pieces, down_weight, prev, segments, last):
-    width = down_weight.shape[1]
+def down(where, pieces, down_weight, prev, segments, columns, last):
+    width = columns[1] - columns[0]
     total = 4 * ROWS
     args = [*pieces, down_weight] + ([] if prev is None else [prev])
     sums = jax.ShapeDtypeStruct((total, width), jnp.float32)
@@ -262,7 +247,7 @@
     if last:
         scratch = [pltpu.VMEM(sums.shape, sums.dtype)] + scratch
     return pl.pallas_call(
-        functools.partial(down_kernel, len(pieces), prev is not None, last, segments),
+        functools.partial(down_kernel, len(pieces), prev is not None, last, segments, columns),
         in_specs=[spec(pltpu.SMEM)] + [spec(pltpu.VMEM)] * len(args),
         out_specs=[spec(pltpu.VMEM)] * 4 if last else spec(pltpu.VMEM),
         scratch_shapes=scratch,
@@ -306,24 +291,27 @@
     segments = [(bounds[2], widths[2]), (half + bounds[2], widths[2])]
     last_mine, theirs = gate_up(where, [own, near], [gate_weight, up_weight], segments, [to_chip])
     last_got = swap(theirs, "wid", 1)
-    last_to_chip = pair_sum(last_mine, last_got, [mark(from_chip)])
+    keep, give = combine(mine, got, from_chip, [], [])
+    last_to_chip = pair_sum(last_mine, last_got, [give])
     last_from_chip = swap(last_to_chip, "wid", 2)
-
-    keep, give = combine(mine, got, from_chip, [], [])
-    far_columns = swap(give, "rep", 1)
-    (rest,) = combine(last_mine, last_got, last_from_chip, [far_columns], [])
+    (rest,) = combine(last_mine, last_got, last_from_chip, [swap(give, "rep", 1)], [])
+
+    def gather(hidden, behind):
+        other = swap(hidden, "wid", 2)
+        return [hidden, other, swap(hidden, "wid", 1), swap(join([other], behind), "wid", 1)]
+
+    features = down_weight.shape[1]
+    acc = down(where, gather(keep, [rest]), down_weight, None, [(1, 0, bounds[2])], (0, features), False)
+    pieces = gather(rest, [acc])
     rest_segments = [(-1, half, bounds[2])] + [(0, start, width) for start, width in segments]
-    acc, behind = None, []
-    for hidden, parts in ((keep, [(1, 0, bounds[2])]), (rest, rest_segments)):
-        other = swap(hidden, "wid", 2)
-        crossed = swap(join([hidden, other], behind), "wid", 1)
-        acc = down(where, [hidden, other, crossed], down_weight, acc, parts, bool(behind))
-        behind = [acc]
-
-    mixed = acc[0].astype(f32)
-    for d in (3, 2, 1):
-        mixed = mixed + swap(acc[d], "hid", d).astype(f32)
-    return mixed.astype(bf16)
+    mixed = []
+    for columns in ((0, features // 2), (features // 2, features)):
+        out = down(where, pieces, down_weight, acc, rest_segments, columns, True)
+        total = out[0].astype(f32)
+        for d in (3, 2, 1):
+            total = total + swap(out[d], "hid", d).astype(f32)
+        mixed.append(total.astype(bf16))
+    return jnp.concatenate(mixed, 1)
 
 
 def solution(mesh):

time: 61.4 us -> 65.7 us (1.070)
  starting transfers between devices: 20 us -> 24 us
  Pallas kernels: 26.9 us -> 27.6 us
    ppermute x17 -> x22, starting transfers between devices: 20 us -> 24 us  [swap(): return lax.ppermute(x, axis, [(i, i ^ step) for i in range(n)])]
    pallas_call x2 -> x3, Pallas kernels: 6.06 us -> 6.74 us  [down(): pl.pallas_call(functools.partial(down_kernel, len(pieces), prev is not No...]
    ppermute x17 -> x22, waiting for transfers between devices: 13.3 us -> 12.9 us  [swap(): return lax.ppermute(x, axis, [(i, i ^ step) for i in range(n)])]
  transfers between devices with their start and end apart: 17 -> 22, of which waited for: 8 -> 8; matrix products, arithmetic and copies ran while one was open for 0% -> 0% of each run, Pallas kernels for 32% -> 33%
where the time goes in v9:
time: 65.7 us; the launch traced here: 65.6 us
  Pallas kernels  27.6 us (42%)
  starting transfers between devices  24 us (37%)
  waiting for transfers between devices  12.9 us (20%)
  other arithmetic  0.75 us (1%)
    ppermute x22, starting transfers between devices, swap(): return lax.ppermute(x, axis, [(i, i ^ step) for i in range(n)])  24 us
    ppermute x22, waiting for transfers between devices, swap(): return lax.ppermute(x, axis, [(i, i ^ step) for i in range(n)])  12.9 us
    pallas_call x2, Pallas kernels, fetch(): pl.pallas_call(functools.partial(fetch_kernel, first), in_specs=[spec(plt...  10.2 us
    pallas_call x2, Pallas kernels, gate_up(): pl.pallas_call(functools.partial(gate_up_kernel, len(arrays), len(weights...  10.2 us
    pallas_call x3, Pallas kernels, down(): pl.pallas_call(functools.partial(down_kernel, len(pieces), prev is not No...  6.74 us
  transfers between devices with their start and end apart: 22, of which 8 were waited for; matrix products, arithmetic and copies ran while one was open for 0% of the time, Pallas kernels for 33%

profile of v9, /device:TPU:0, one launch (start us, length us, event | category | flops | bytes accessed | tf_op | source)
XLA Modules:
  0.0 65.6 jit_solution(1486688380002791345)
XLA Ops:
  0.0 5.0 %collective-permute-start.2 = (bf16[16,2048]{1,0:T(8,128)(2,1)}, bf16[16,2048]{1,0:T(8,128)(2,1)S(1)}, u32[]{:S(2)}, u32[]{:S(2)}) collective-permute-start(bf16[16,2048]{1,0:T(8,128)(2,1)} %tokens_ref.3), channel_id=1, source_target_pairs={{0,12},{4,8},{8,4},{12,0},{1,13},{5,9},{9,5},{13,1},{2,14},{6,10},... | collective-permute-start | bytes 196616 | tf_op jit(solution)/shard_map/ppermute | solution.py:269
  5.0 0.0 collective-permute-start.1
  5.1 0.6 collective-permute-start
  5.6 1.7 %collective-permute-start.3 = (bf16[16,2048]{1,0:T(8,128)(2,1)}, bf16[16,2048]{1,0:T(8,128)(2,1)S(1)}, u32[]{:S(2)}, u32[]{:S(2)}) collective-permute-start(bf16[16,2048]{1,0:T(8,128)(2,1)} %tokens_ref.3), channel_id=1, source_target_pairs={{0,16},{16,0},{1,17},{17,1},{2,18},{18,2},{3,19},{19,3},{4,20},{20... | collective-permute-start | bytes 196616 | tf_op jit(solution)/shard_map/ppermute | solution.py:269
  7.4 0.1 pad_add_fusion.where
  7.4 4.8 %fetch.2 = (bf16[2048,1280]{1,0:T(8,128)(2,1)S(1)}, bf16[2048,1280]{1,0:T(8,128)(2,1)S(1)}, bf16[16,2048]{1,0:T(8,128)(2,1)S(1)}) custom-call(s32[2]{0:T(128)S(1)} %pad_add_fusion.where, bf16[2048,6656]{1,0:T(8,128)(2,1)} %refs_2_.1, bf16[2048,6656]{1,0:T(8,128)(2,1)} %refs_3_.1, bf16[16,2048]{1,0:T(8,128)(2,1)} %tokens_ref.3), custom_call_target="tpu_custom_call" | custom-call | bytes 1024 | tf_op jit(solution)/shard_map/fetch/pallas_call | solution.py:73
  12.3 0.0 collective-permute-done.refs_0_
  12.3 0.0 collective-permute-done.3.refs_4_.refs_2_
  12.3 0.4 collective-permute-start.4
  12.7 5.4 %fetch.3 = (bf16[2048,1280]{1,0:T(8,128)(2,1)S(1)}, bf16[2048,1280]{1,0:T(8,128)(2,1)S(1)}, bf16[16,2048]{1,0:T(8,128)(2,1)}) custom-call(s32[2]{0:T(128)S(1)} %pad_add_fusion.where, bf16[2048,6656]{1,0:T(8,128)(2,1)} %refs_2_.1, bf16[2048,6656]{1,0:T(8,128)(2,1)} %refs_3_.1, bf16[16,2048]{1,0:T(8,128)(2,1)} %tokens_ref.3), custom_call_target="tpu_custom_call" | custom-call | bytes 1024 | tf_op jit(solution)/shard_map/fetch/pallas_call | solution.py:73
  18.1 0.0 collective-permute-done.4.refs_3_
  18.1 3.6 %gate_up.2 = (bf16[2,64,2560]{2,1,0:T(8,128)(2,1)S(1)}, bf16[2,64,2560]{2,1,0:T(8,128)(2,1)S(1)}) custom-call(s32[2]{0:T(128)S(1)} %pad_add_fusion.where, bf16[16,2048]{1,0:T(8,128)(2,1)S(1)} %get-tuple-element.24.refs_3_.refs_0_, bf16[48,2048]{1,0:T(8,128)(2,1)S(1)} %join.3.refs_1_, bf16[16,2048]{1,0:T(8,128)(2,1)S(1)} %collective-permute-done.3.refs_4_.refs_2_, ...), custom_call_target="tpu_custom_call" | custom-call | bytes 1024 | tf_op jit(solution)/shard_map/gate_up/pallas_call | solution.py:148
  21.7 0.1 collective-permute-start.5
  21.8 2.1 %collective-permute-done.5.got_ref = bf16[2,64,2560]{2,1,0:T(8,128)(2,1)S(1)} collective-permute-done((bf16[2,64,2560]{2,1,0:T(8,128)(2,1)S(1)}, bf16[2,64,2560]{2,1,0:T(8,128)(2,1)S(1)}, u32[]{:S(2)}, u32[]{:S(2)}) %collective-permute-start.5) | collective-permute-done | bytes 655392 | tf_op jit(solution)/shard_map/ppermute | solution.py:269
  23.9 0.1 pair_sum.2.refs_4_
  23.9 0.0 slice-start.1
  24.0 0.0 slice-start.2
  24.0 0.0 slice-start.5
  24.0 0.0 slice-start.6
  24.0 1.8 %collective-permute-start.7 = (bf16[2,32,2560]{2,1,0:T(8,128)(2,1)S(1)}, bf16[2,32,2560]{2,1,0:T(8,128)(2,1)S(1)}, u32[]{:S(2)}, u32[]{:S(2)}) collective-permute-start(bf16[2,32,2560]{2,1,0:T(8,128)(2,1)S(1)} %pair_sum.2.refs_4_), channel_id=1, source_target_pairs={{0,2},{1,3},{2,0},{3,1},{4,6},{5,7},{6,4},{7,5},{8,10},{9,11},{10,... | collective-permute-start | bytes 983048 | tf_op jit(solution)/shard_map/ppermute | solution.py:269
  25.8 6.6 %gate_up.3 = (bf16[2,32,1536]{2,1,0:T(8,128)(2,1)S(1)}, bf16[2,32,1536]{2,1,0:T(8,128)(2,1)S(1)}) custom-call(s32[2]{0:T(128)S(1)} %pad_add_fusion.where, bf16[16,2048]{1,0:T(8,128)(2,1)S(1)} %get-tuple-element.24.refs_3_.refs_0_, bf16[48,2048]{1,0:T(8,128)(2,1)S(1)} %join.3.refs_1_, bf16[2048,6656]{1,0:T(8,128)(2,1)} %refs_2_.1, ...), custom_call_target="tpu_custom_call" | custom-call | bytes 1024 | tf_op jit(solution)/shard_map/gate_up/pallas_call | solution.py:148
  32.4 0.1 collective-permute-start.6
  32.5 1.3 %collective-permute-done.7.chip_ref = bf16[2,32,2560]{2,1,0:T(8,128)(2,1)S(1)} collective-permute-done((bf16[2,32,2560]{2,1,0:T(8,128)(2,1)S(1)}, bf16[2,32,2560]{2,1,0:T(8,128)(2,1)S(1)}, u32[]{:S(2)}, u32[]{:S(2)}) %collective-permute-start.7) | collective-permute-done | bytes 327712 | tf_op jit(solution)/shard_map/ppermute | solution.py:269
  33.8 0.2 combine.2
  34.0 0.0 collective-permute-done.6.got_ref
  34.1 1.8 %collective-permute-start.8 = (bf16[2,16,1536]{2,1,0:T(8,128)(2,1)S(1)}, bf16[2,16,1536]{2,1,0:T(8,128)(2,1)S(1)}, u32[]{:S(2)}, u32[]{:S(2)}) collective-permute-start(bf16[2,16,1536]{2,1,0:T(8,128)(2,1)S(1)} %pair_sum.3), channel_id=1, source_target_pairs={{0,2},{1,3},{2,0},{3,1},{4,6},{5,7},{6,4},{7,5},{8,10},{9,11},{10,... | collective-permute-start | bytes 294920 | tf_op jit(solution)/shard_map/ppermute | solution.py:269
  35.8 1.5 %collective-permute-start.9 = (bf16[16,2560]{1,0:T(8,128)(2,1)S(1)}, bf16[16,2560]{1,0:T(8,128)(2,1)S(1)}, u32[]{:S(2)}, u32[]{:S(2)}) collective-permute-start(bf16[16,2560]{1,0:T(8,128)(2,1)S(1)} %get-tuple-element.33.refs_0_), channel_id=1, source_target_pairs={{0,16},{16,0},{1,17},{17,1},{2,18},{18,2},{3,19},{19,3},{4,20},{20... | collective-permute-start | bytes 245768 | tf_op jit(solution)/shard_map/ppermute | solution.py:269
  37.4 0.5 collective-permute-start.12
  37.9 2.4 %collective-permute-done.9.refs_0_ = bf16[16,2560]{1,0:T(8,128)(2,1)S(1)} collective-permute-done((bf16[16,2560]{1,0:T(8,128)(2,1)S(1)}, bf16[16,2560]{1,0:T(8,128)(2,1)S(1)}, u32[]{:S(2)}, u32[]{:S(2)}) %collective-permute-start.9) | collective-permute-done | bytes 81952 | tf_op jit(solution)/shard_map/ppermute | solution.py:269
  40.3 0.1 combine.3.refs_1_.refs_0_
  40.4 1.0 %collective-permute-start.10 = (bf16[16,4096]{1,0:T(8,128)(2,1)S(1)}, bf16[16,4096]{1,0:T(8,128)(2,1)S(1)}, u32[]{:S(2)}, u32[]{:S(2)}) collective-permute-start(bf16[16,4096]{1,0:T(8,128)(2,1)S(1)} %combine.3.refs_1_.refs_0_), channel_id=1, source_target_pairs={{0,2},{1,3},{2,0},{3,1},{4,6},{5,7},{6,4},{7,5},{8,10},{9,11},{10,... | collective-permute-start | bytes 393224 | tf_op jit(solution)/shard_map/ppermute | solution.py:269
  41.3 0.0 collective-permute-start.13
  41.3 1.1 %collective-permute-done.12.refs_0_.refs_1_ = bf16[16,2560]{1,0:T(8,128)(2,1)S(1)} collective-permute-done((bf16[16,2560]{1,0:T(8,128)(2,1)S(1)}, bf16[16,2560]{1,0:T(8,128)(2,1)S(1)}, u32[]{:S(2)}, u32[]{:S(2)}) %collective-permute-start.12) | collective-permute-done | bytes 81952 | tf_op jit(solution)/shard_map/ppermute | solution.py:269
  42.4 0.5 collective-permute-start.11
  42.9 0.0 collective-permute-done.13.refs_2_
  42.9 0.8 %collective-permute-done.14.refs_3_ = bf16[16,2560]{1,0:T(8,128)(2,1)S(1)} collective-permute-done((bf16[16,2560]{1,0:T(8,128)(2,1)S(1)}, bf16[16,2560]{1,0:T(8,128)(2,1)S(1)}, u32[]{:S(2)}, u32[]{:S(2)}) %collective-permute-start.14) | collective-permute-done | bytes 81952 | tf_op jit(solution)/shard_map/ppermute | solution.py:269
  43.8 2.5 %down.3.refs_1_.refs_5_ = f32[64,2048]{1,0:T(8,128)S(1)} custom-call(s32[2]{0:T(128)S(1)} %pad_add_fusion.where, bf16[16,2560]{1,0:T(8,128)(2,1)S(1)} %get-tuple-element.34.refs_0_, bf16[16,2560]{1,0:T(8,128)(2,1)S(1)} %collective-permute-done.12.refs_0_.refs_1_, bf16[16,2560]{1,0:T(8,128)(2,1)S(1)} %collective-permute-done.13.refs_2_, ...), custom_call_target="tpu_custom_call" | custom-call | bytes 1024 | tf_op jit(solution)/shard_map/down/pallas_call | solution.py:249
  46.3 0.2 collective-permute-start.15
  46.5 1.2 %collective-permute-done.15.refs_3_ = bf16[16,4096]{1,0:T(8,128)(2,1)S(1)} collective-permute-done((bf16[16,4096]{1,0:T(8,128)(2,1)S(1)}, bf16[16,4096]{1,0:T(8,128)(2,1)S(1)}, u32[]{:S(2)}, u32[]{:S(2)}) %collective-permute-start.15) | collective-permute-done | bytes 131104 | tf_op jit(solution)/shard_map/ppermute | solution.py:269
  47.7 2.1 %down.5 = (bf16[16,1024]{1,0:T(8,128)(2,1)S(1)}, bf16[16,1024]{1,0:T(8,128)(2,1)S(1)}, bf16[16,1024]{1,0:T(8,128)(2,1)S(1)}, bf16[16,1024]{1,0:T(8,128)(2,1)S(1)}) custom-call(s32[2]{0:T(128)S(1)} %pad_add_fusion.where, bf16[16,4096]{1,0:T(8,128)(2,1)S(1)} %combine.3.refs_1_.refs_0_, bf16[16,4096]{1,0:T(8,128)(2,1)S(1)} %collective-permute-done.10.refs_0_.refs_1_, ...), custom_call_target="tpu_custom_call" | custom-call | bytes 1024 | tf_op jit(solution)/shard_map/down/pallas_call | solution.py:249
  49.8 3.7 %collective-permute-start.19 = (bf16[16,1024]{1,0:T(8,128)(2,1)S(1)}, bf16[16,1024]{1,0:T(8,128)(2,1)S(1)}, u32[]{:S(2)}, u32[]{:S(2)}) collective-permute-start(bf16[16,1024]{1,0:T(8,128)(2,1)S(1)} %get-tuple-element.40), channel_id=1, source_target_pairs={{0,12},{4,8},{8,4},{12,0},{1,13},{5,9},{9,5},{13,1},{2,14},{6,10},... | collective-permute-start | bytes 98312 | tf_op jit(solution)/shard_map/ppermute | solution.py:269
  53.5 0.8 %collective-permute-start.21 = (bf16[16,1024]{1,0:T(8,128)(2,1)S(1)}, bf16[16,1024]{1,0:T(8,128)(2,1)S(1)}, u32[]{:S(2)}, u32[]{:S(2)}) collective-permute-start(bf16[16,1024]{1,0:T(8,128)(2,1)S(1)} %get-tuple-element.42), channel_id=1, source_target_pairs={{0,4},{4,0},{8,12},{12,8},{1,5},{5,1},{9,13},{13,9},{2,6},{6,2},{1... | collective-permute-start | bytes 98312 | tf_op jit(solution)/shard_map/ppermute | solution.py:269
  54.3 2.1 %down.4 = (bf16[16,1024]{1,0:T(8,128)(2,1)S(1)}, bf16[16,1024]{1,0:T(8,128)(2,1)S(1)}, bf16[16,1024]{1,0:T(8,128)(2,1)S(1)}, bf16[16,1024]{1,0:T(8,128)(2,1)S(1)}) custom-call(s32[2]{0:T(128)S(1)} %pad_add_fusion.where, bf16[16,4096]{1,0:T(8,128)(2,1)S(1)} %combine.3.refs_1_.refs_0_, bf16[16,4096]{1,0:T(8,128)(2,1)S(1)} %collective-permute-done.10.refs_0_.refs_1_, ...), custom_call_target="tpu_custom_call" | custom-call | bytes 1024 | tf_op jit(solution)/shard_map/down/pallas_call | solution.py:249
  56.4 3.7 %collective-permute-start.16 = (bf16[16,1024]{1,0:T(8,128)(2,1)S(1)}, bf16[16,1024]{1,0:T(8,128)(2,1)S(1)}, u32[]{:S(2)}, u32[]{:S(2)}) collective-permute-start(bf16[16,1024]{1,0:T(8,128)(2,1)S(1)} %get-tuple-element.36), channel_id=1, source_target_pairs={{0,12},{4,8},{8,4},{12,0},{1,13},{5,9},{9,5},{13,1},{2,14},{6,10},... | collective-permute-start | bytes 98312 | tf_op jit(solution)/shard_map/ppermute | solution.py:269
  60.1 0.8 %collective-permute-start.18 = (bf16[16,1024]{1,0:T(8,128)(2,1)S(1)}, bf16[16,1024]{1,0:T(8,128)(2,1)S(1)}, u32[]{:S(2)}, u32[]{:S(2)}) collective-permute-start(bf16[16,1024]{1,0:T(8,128)(2,1)S(1)} %get-tuple-element.38), channel_id=1, source_target_pairs={{0,4},{4,0},{8,12},{12,8},{1,5},{5,1},{9,13},{13,9},{2,6},{6,2},{1... | collective-permute-start | bytes 98312 | tf_op jit(solution)/shard_map/ppermute | solution.py:269
  60.9 1.4 %collective-permute-done.16 = bf16[16,1024]{1,0:T(8,128)(2,1)S(1)} collective-permute-done((bf16[16,1024]{1,0:T(8,128)(2,1)S(1)}, bf16[16,1024]{1,0:T(8,128)(2,1)S(1)}, u32[]{:S(2)}, u32[]{:S(2)}) %collective-permute-start.16) | collective-permute-done | bytes 32800 | tf_op jit(solution)/shard_map/ppermute | solution.py:269
  62.3 2.6 %collective-permute-done.17 = bf16[16,1024]{1,0:T(8,128)(2,1)S(1)} collective-permute-done((bf16[16,1024]{1,0:T(8,128)(2,1)S(1)}, bf16[16,1024]{1,0:T(8,128)(2,1)S(1)}, u32[]{:S(2)}, u32[]{:S(2)}) %collective-permute-start.17) | collective-permute-done | bytes 32800 | tf_op jit(solution)/shard_map/ppermute | solution.py:269
  64.9 0.6 pad_maximum_fusion
  (29 shorter events, 0.2 us)
Async XLA Ops:
  0.0 12.2 %collective-permute-start.2 = (bf16[16,2048]{1,0:T(8,128)(2,1)}, bf16[16,2048]{1,0:T(8,128)(2,1)S(1)}, u32[]{:S(2)}, u32[]{:S(2)}) collective-permute-start(bf16[16,2048]{1,0:T(8,128)(2,1)} %tokens_ref.3), channel_id=1, source_target_pairs={{0,12},{4,8},{8,4},{12,0},{1,13},{5,9},{9,5},{13,1},{2,14},{6,10},... | collective-permute-start | bytes 196616 | tf_op jit(solution)/shard_map/ppermute | solution.py:269
  5.0 7.2 %collective-permute-start.1 = (bf16[16,2048]{1,0:T(8,128)(2,1)}, bf16[16,2048]{1,0:T(8,128)(2,1)S(1)}, u32[]{:S(2)}, u32[]{:S(2)}) collective-permute-start(bf16[16,2048]{1,0:T(8,128)(2,1)} %tokens_ref.3), channel_id=1, source_target_pairs={{0,8},{4,12},{8,0},{12,4},{1,9},{5,13},{9,1},{13,5},{2,10},{6,14},... | collective-permute-start | bytes 196616 | tf_op jit(solution)/shard_map/ppermute | solution.py:269
  5.1 7.2 %collective-permute-start = (bf16[16,2048]{1,0:T(8,128)(2,1)}, bf16[16,2048]{1,0:T(8,128)(2,1)S(1)}, u32[]{:S(2)}, u32[]{:S(2)}) collective-permute-start(bf16[16,2048]{1,0:T(8,128)(2,1)} %tokens_ref.3), channel_id=1, source_target_pairs={{0,4},{4,0},{8,12},{12,8},{1,5},{5,1},{9,13},{13,9},{2,6},{6,2},{1... | collective-permute-start | bytes 196616 | tf_op jit(solution)/shard_map/ppermute | solution.py:269
  5.6 6.7 %collective-permute-start.3 = (bf16[16,2048]{1,0:T(8,128)(2,1)}, bf16[16,2048]{1,0:T(8,128)(2,1)S(1)}, u32[]{:S(2)}, u32[]{:S(2)}) collective-permute-start(bf16[16,2048]{1,0:T(8,128)(2,1)} %tokens_ref.3), channel_id=1, source_target_pairs={{0,16},{16,0},{1,17},{17,1},{2,18},{18,2},{3,19},{19,3},{4,20},{20... | collective-permute-start | bytes 196616 | tf_op jit(solution)/shard_map/ppermute | solution.py:269
  12.3 5.8 %collective-permute-start.4 = (bf16[48,2048]{1,0:T(8,128)(2,1)S(1)}, bf16[48,2048]{1,0:T(8,128)(2,1)S(1)}, u32[]{:S(2)}, u32[]{:S(2)}) collective-permute-start(bf16[48,2048]{1,0:T(8,128)(2,1)S(1)} %join.3.refs_1_), channel_id=1, source_target_pairs={{0,16},{16,0},{1,17},{17,1},{2,18},{18,2},{3,19},{19,3},{4,20},{20... | collective-permute-start | bytes 589832 | tf_op jit(solution)/shard_map/ppermute | solution.py:269
  21.7 2.2 %collective-permute-start.5 = (bf16[2,64,2560]{2,1,0:T(8,128)(2,1)S(1)}, bf16[2,64,2560]{2,1,0:T(8,128)(2,1)S(1)}, u32[]{:S(2)}, u32[]{:S(2)}) collective-permute-start(bf16[2,64,2560]{2,1,0:T(8,128)(2,1)S(1)} %get-tuple-element.30), channel_id=1, source_target_pairs={{0,1},{1,0},{2,3},{3,2},{4,5},{5,4},{6,7},{7,6},{8,9},{9,8},{10,11... | collective-permute-start | bytes 1966088 | tf_op jit(solution)/shard_map/ppermute | solution.py:269
  23.9 19.8 %slice-start = ((s8[27262976]{0:T(1024)(128)(4,1)}), s8[4194304]{0:T(1024)(128)(4,1)S(1)}, s32[]{:S(2)}) async-start(s8[27262976]{0:T(1024)(128)(4,1)} %bitcast.2), calls=%async_computation | async-start | bytes 8388608
  23.9 19.8 %slice-start.1 = ((s8[27262976]{0:T(1024)(128)(4,1)}), s8[4194304]{0:T(1024)(128)(4,1)S(1)}, s32[]{:S(2)}) async-start(s8[27262976]{0:T(1024)(128)(4,1)} %bitcast.2), calls=%async_computation.1 | async-start | bytes 8388608
  24.0 19.7 %slice-start.2 = ((s8[27262976]{0:T(1024)(128)(4,1)}), s8[4194304]{0:T(1024)(128)(4,1)S(1)}, s32[]{:S(2)}) async-start(s8[27262976]{0:T(1024)(128)(4,1)} %bitcast.2), calls=%async_computation.2 | async-start | bytes 8388608
  24.0 19.7 %slice-start.3 = ((s8[27262976]{0:T(1024)(128)(4,1)}), s8[4194304]{0:T(1024)(128)(4,1)S(1)}, s32[]{:S(2)}) async-start(s8[27262976]{0:T(1024)(128)(4,1)} %bitcast.2), calls=%async_computation.3 | async-start | bytes 8388608
  24.0 19.7 %slice-start.4 = ((s8[27262976]{0:T(1024)(128)(4,1)}), s8[4194304]{0:T(1024)(128)(4,1)S(1)}, s32[]{:S(2)}) async-start(s8[27262976]{0:T(1024)(128)(4,1)} %bitcast.2), calls=%async_computation.4 | async-start | bytes 8388608
  24.0 19.7 %slice-start.5 = ((s8[27262976]{0:T(1024)(128)(4,1)}), s8[4194304]{0:T(1024)(128)(4,1)S(1)}, s32[]{:S(2)}) async-start(s8[27262976]{0:T(1024)(128)(4,1)} %bitcast.2), calls=%async_computation.5 | async-start | bytes 8388608
  24.0 19.7 %slice-start.6 = ((s8[27262976]{0:T(1024)(128)(4,1)}), s8[2097152]{0:T(1024)(128)(4,1)S(1)}, s32[]{:S(2)}) async-start(s8[27262976]{0:T(1024)(128)(4,1)} %bitcast.2), calls=%async_computation.6 | async-start | bytes 4194304
  24.0 9.8 %collective-permute-start.7 = (bf16[2,32,2560]{2,1,0:T(8,128)(2,1)S(1)}, bf16[2,32,2560]{2,1,0:T(8,128)(2,1)S(1)}, u32[]{:S(2)}, u32[]{:S(2)}) collective-permute-start(bf16[2,32,2560]{2,1,0:T(8,128)(2,1)S(1)} %pair_sum.2.refs_4_), channel_id=1, source_target_pairs={{0,2},{1,3},{2,0},{3,1},{4,6},{5,7},{6,4},{7,5},{8,10},{9,11},{10,... | collective-permute-start | bytes 983048 | tf_op jit(solution)/shard_map/ppermute | solution.py:269
  32.4 1.6 %collective-permute-start.6 = (bf16[2,32,1536]{2,1,0:T(8,128)(2,1)S(1)}, bf16[2,32,1536]{2,1,0:T(8,128)(2,1)S(1)}, u32[]{:S(2)}, u32[]{:S(2)}) collective-permute-start(bf16[2,32,1536]{2,1,0:T(8,128)(2,1)S(1)} %get-tuple-element.32), channel_id=1, source_target_pairs={{0,1},{1,0},{2,3},{3,2},{4,5},{5,4},{6,7},{7,6},{8,9},{9,8},{10,11... | collective-permute-start | bytes 589832 | tf_op jit(solution)/shard_map/ppermute | solution.py:269
  34.1 6.2 %collective-permute-start.8 = (bf16[2,16,1536]{2,1,0:T(8,128)(2,1)S(1)}, bf16[2,16,1536]{2,1,0:T(8,128)(2,1)S(1)}, u32[]{:S(2)}, u32[]{:S(2)}) collective-permute-start(bf16[2,16,1536]{2,1,0:T(8,128)(2,1)S(1)} %pair_sum.3), channel_id=1, source_target_pairs={{0,2},{1,3},{2,0},{3,1},{4,6},{5,7},{6,4},{7,5},{8,10},{9,11},{10,... | collective-permute-start | bytes 294920 | tf_op jit(solution)/shard_map/ppermute | solution.py:269
  35.8 4.4 %collective-permute-start.9 = (bf16[16,2560]{1,0:T(8,128)(2,1)S(1)}, bf16[16,2560]{1,0:T(8,128)(2,1)S(1)}, u32[]{:S(2)}, u32[]{:S(2)}) collective-permute-start(bf16[16,2560]{1,0:T(8,128)(2,1)S(1)} %get-tuple-element.33.refs_0_), channel_id=1, source_target_pairs={{0,16},{16,0},{1,17},{17,1},{2,18},{18,2},{3,19},{19,3},{4,20},{20... | collective-permute-start | bytes 245768 | tf_op jit(solution)/shard_map/ppermute | solution.py:269
  37.4 5.0 %collective-permute-start.12 = (bf16[16,2560]{1,0:T(8,128)(2,1)S(1)}, bf16[16,2560]{1,0:T(8,128)(2,1)S(1)}, u32[]{:S(2)}, u32[]{:S(2)}) collective-permute-start(bf16[16,2560]{1,0:T(8,128)(2,1)S(1)} %get-tuple-element.34.refs_0_), channel_id=1, source_target_pairs={{0,2},{1,3},{2,0},{3,1},{4,6},{5,7},{6,4},{7,5},{8,10},{9,11},{10,... | collective-permute-start | bytes 245768 | tf_op jit(solution)/shard_map/ppermute | solution.py:269
  40.4 5.9 %collective-permute-start.10 = (bf16[16,4096]{1,0:T(8,128)(2,1)S(1)}, bf16[16,4096]{1,0:T(8,128)(2,1)S(1)}, u32[]{:S(2)}, u32[]{:S(2)}) collective-permute-start(bf16[16,4096]{1,0:T(8,128)(2,1)S(1)} %combine.3.refs_1_.refs_0_), channel_id=1, source_target_pairs={{0,2},{1,3},{2,0},{3,1},{4,6},{5,7},{6,4},{7,5},{8,10},{9,11},{10,... | collective-permute-start | bytes 393224 | tf_op jit(solution)/shard_map/ppermute | solution.py:269
  41.3 1.6 %collective-permute-start.13 = (bf16[16,2560]{1,0:T(8,128)(2,1)S(1)}, bf16[16,2560]{1,0:T(8,128)(2,1)S(1)}, u32[]{:S(2)}, u32[]{:S(2)}) collective-permute-start(bf16[16,2560]{1,0:T(8,128)(2,1)S(1)} %get-tuple-element.34.refs_0_), channel_id=1, source_target_pairs={{0,1},{1,0},{2,3},{3,2},{4,5},{5,4},{6,7},{7,6},{8,9},{9,8},{10,11... | collective-permute-start | bytes 245768 | tf_op jit(solution)/shard_map/ppermute | solution.py:269
  42.4 1.3 %collective-permute-start.14 = (bf16[16,2560]{1,0:T(8,128)(2,1)S(1)}, bf16[16,2560]{1,0:T(8,128)(2,1)S(1)}, u32[]{:S(2)}, u32[]{:S(2)}) collective-permute-start(bf16[16,2560]{1,0:T(8,128)(2,1)S(1)} %join.4), channel_id=1, source_target_pairs={{0,1},{1,0},{2,3},{3,2},{4,5},{5,4},{6,7},{7,6},{8,9},{9,8},{10,11... | collective-permute-start | bytes 245768 | tf_op jit(solution)/shard_map/ppermute | solution.py:269
  42.4 4.0 %collective-permute-start.11 = (bf16[16,4096]{1,0:T(8,128)(2,1)S(1)}, bf16[16,4096]{1,0:T(8,128)(2,1)S(1)}, u32[]{:S(2)}, u32[]{:S(2)}) collective-permute-start(bf16[16,4096]{1,0:T(8,128)(2,1)S(1)} %combine.3.refs_1_.refs_0_), channel_id=1, source_target_pairs={{0,1},{1,0},{2,3},{3,2},{4,5},{5,4},{6,7},{7,6},{8,9},{9,8},{10,11... | collective-permute-start | bytes 393224 | tf_op jit(solution)/shard_map/ppermute | solution.py:269
  46.3 1.4 %collective-permute-start.15 = (bf16[16,4096]{1,0:T(8,128)(2,1)S(1)}, bf16[16,4096]{1,0:T(8,128)(2,1)S(1)}, u32[]{:S(2)}, u32[]{:S(2)}) collective-permute-start(bf16[16,4096]{1,0:T(8,128)(2,1)S(1)} %join.5), channel_id=1, source_target_pairs={{0,1},{1,0},{2,3},{3,2},{4,5},{5,4},{6,7},{7,6},{8,9},{9,8},{10,11... | collective-permute-start | bytes 393224 | tf_op jit(solution)/shard_map/ppermute | solution.py:269
  49.8 10.3 %collective-permute-start.19 = (bf16[16,1024]{1,0:T(8,128)(2,1)S(1)}, bf16[16,1024]{1,0:T(8,128)(2,1)S(1)}, u32[]{:S(2)}, u32[]{:S(2)}) collective-permute-start(bf16[16,1024]{1,0:T(8,128)(2,1)S(1)} %get-tuple-element.40), channel_id=1, source_target_pairs={{0,12},{4,8},{8,4},{12,0},{1,13},{5,9},{9,5},{13,1},{2,14},{6,10},... | collective-permute-start | bytes 98312 | tf_op jit(solution)/shard_map/ppermute | solution.py:269
  53.5 7.4 %collective-permute-start.20 = (bf16[16,1024]{1,0:T(8,128)(2,1)S(1)}, bf16[16,1024]{1,0:T(8,128)(2,1)S(1)}, u32[]{:S(2)}, u32[]{:S(2)}) collective-permute-start(bf16[16,1024]{1,0:T(8,128)(2,1)S(1)} %get-tuple-element.41), channel_id=1, source_target_pairs={{0,8},{4,12},{8,0},{12,4},{1,9},{5,13},{9,1},{13,5},{2,10},{6,14},... | collective-permute-start | bytes 98312 | tf_op jit(solution)/shard_map/ppermute | solution.py:269
  53.5 7.4 %collective-permute-start.21 = (bf16[16,1024]{1,0:T(8,128)(2,1)S(1)}, bf16[16,1024]{1,0:T(8,128)(2,1)S(1)}, u32[]{:S(2)}, u32[]{:S(2)}) collective-permute-start(bf16[16,1024]{1,0:T(8,128)(2,1)S(1)} %get-tuple-element.42), channel_id=1, source_target_pairs={{0,4},{4,0},{8,12},{12,8},{1,5},{5,1},{9,13},{13,9},{2,6},{6,2},{1... | collective-permute-start | bytes 98312 | tf_op jit(solution)/shard_map/ppermute | solution.py:269
  56.4 5.9 %collective-permute-start.16 = (bf16[16,1024]{1,0:T(8,128)(2,1)S(1)}, bf16[16,1024]{1,0:T(8,128)(2,1)S(1)}, u32[]{:S(2)}, u32[]{:S(2)}) collective-permute-start(bf16[16,1024]{1,0:T(8,128)(2,1)S(1)} %get-tuple-element.36), channel_id=1, source_target_pairs={{0,12},{4,8},{8,4},{12,0},{1,13},{5,9},{9,5},{13,1},{2,14},{6,10},... | collective-permute-start | bytes 98312 | tf_op jit(solution)/shard_map/ppermute | solution.py:269
  60.1 4.8 %collective-permute-start.17 = (bf16[16,1024]{1,0:T(8,128)(2,1)S(1)}, bf16[16,1024]{1,0:T(8,128)(2,1)S(1)}, u32[]{:S(2)}, u32[]{:S(2)}) collective-permute-start(bf16[16,1024]{1,0:T(8,128)(2,1)S(1)} %get-tuple-element.37), channel_id=1, source_target_pairs={{0,8},{4,12},{8,0},{12,4},{1,9},{5,13},{9,1},{13,5},{2,10},{6,14},... | collective-permute-start | bytes 98312 | tf_op jit(solution)/shard_map/ppermute | solution.py:269
  60.1 4.8 %collective-permute-start.18 = (bf16[16,1024]{1,0:T(8,128)(2,1)S(1)}, bf16[16,1024]{1,0:T(8,128)(2,1)S(1)}, u32[]{:S(2)}, u32[]{:S(2)}) collective-permute-start(bf16[16,1024]{1,0:T(8,128)(2,1)S(1)} %get-tuple-element.38), channel_id=1, source_target_pairs={{0,4},{4,0},{8,12},{12,8},{1,5},{5,1},{9,13},{13,9},{2,6},{6,2},{1... | collective-permute-start | bytes 98312 | tf_op jit(solution)/shard_map/ppermute | solution.py:269

commit v10 on v9

--- a/solution.py
+++ b/solution.py
@@ -233,9 +233,10 @@
             at += depth
         acc_ref[:, a:b] = part
     if last:
-        for d, out in enumerate(outs):
-            source = pl.multiple_of(place(where[1], d) * ROWS, ROWS)
-            out[...] = acc_ref[pl.ds(source, ROWS), :].astype(out.dtype)
+        (out,) = outs
+        for h in range(out.shape[0]):
+            source = pl.multiple_of(place(where[1], where[2] ^ h) * ROWS, ROWS)
+            out[h] = acc_ref[pl.ds(source, ROWS), :].astype(out.dtype)
 
 
 def down(where, pieces, down_weight, prev, segments, columns, last):
@@ -249,9 +250,9 @@
     return pl.pallas_call(
         functools.partial(down_kernel, len(pieces), prev is not None, last, segments, columns),
         in_specs=[spec(pltpu.SMEM)] + [spec(pltpu.VMEM)] * len(args),
-        out_specs=[spec(pltpu.VMEM)] * 4 if last else spec(pltpu.VMEM),
+        out_specs=spec(pltpu.VMEM),
         scratch_shapes=scratch,
-        out_shape=[jax.ShapeDtypeStruct((ROWS, width), jnp.bfloat16)] * 4 if last else sums,
+        out_shape=jax.ShapeDtypeStruct((4, ROWS, width), jnp.bfloat16) if last else sums,
         compiler_params=params(4),
         cost_estimate=COST,
         name="down",
@@ -259,10 +260,10 @@
 
 
 def split_by_rep(tokens, gate_weight, up_weight, down_weight):
-    rep, wid = lax.axis_index("rep"), lax.axis_index("wid")
+    rep, hid, wid = lax.axis_index("rep"), lax.axis_index("hid"), lax.axis_index("wid")
     f32, bf16 = jnp.float32, jnp.bfloat16
     half = gate_weight.shape[1] // 2
-    where = jnp.stack([rep * half, wid]).astype(jnp.int32)
+    where = jnp.stack([rep * half, wid, hid]).astype(jnp.int32)
 
     def swap(x, axis, step):
         n = {"rep": 2, "hid": 4, "wid": 4}[axis]
@@ -304,14 +305,8 @@
     acc = down(where, gather(keep, [rest]), down_weight, None, [(1, 0, bounds[2])], (0, features), False)
     pieces = gather(rest, [acc])
     rest_segments = [(-1, half, bounds[2])] + [(0, start, width) for start, width in segments]
-    mixed = []
-    for columns in ((0, features // 2), (features // 2, features)):
-        out = down(where, pieces, down_weight, acc, rest_segments, columns, True)
-        total = out[0].astype(f32)
-        for d in (3, 2, 1):
-            total = total + swap(out[d], "hid", d).astype(f32)
-        mixed.append(total.astype(bf16))
-    return jnp.concatenate(mixed, 1)
+    out = down(where, pieces, down_weight, acc, rest_segments, (0, features), True)
+    return lax.all_to_all(out, "hid", 0, 0).astype(f32).sum(0).astype(bf16)
 
 
 def solution(mesh):

time: 65.7 us -> 66 us (level)
  blocking collectives: 0 us -> 13.9 us
  starting transfers between devices: 24 us -> 15.1 us
  waiting for transfers between devices: 12.9 us -> 8.86 us
  Pallas kernels: 27.6 us -> 26.9 us
    all_to_all x0 -> x1, blocking collectives: none -> 13.9 us  [split_by_rep(): return lax.all_to_all(out, 'hid', 0, 0).astype(f32).sum(0).astype(bf16)]
    ppermute x22 -> x16, starting transfers between devices: 24 us -> 15.1 us  [swap(): return lax.ppermute(x, axis, [(i, i ^ step) for i in range(n)])]
    ppermute x22 -> x16, waiting for transfers between devices: 12.9 us -> 8.86 us  [swap(): return lax.ppermute(x, axis, [(i, i ^ step) for i in range(n)])]
    pallas_call x3 -> x2, Pallas kernels: 6.74 us -> 6.06 us  [down(): pl.pallas_call(functools.partial(down_kernel, len(pieces), prev is not No...]
    reduce_sum x0 -> x1, other arithmetic: none -> 0.67 us  [split_by_rep(): return lax.all_to_all(out, 'hid', 0, 0).astype(f32).sum(0).astype(bf16)]
  transfers between devices with their start and end apart: 22 -> 16, of which waited for: 8 -> 6; matrix products, arithmetic and copies ran while one was open for 0% -> 0% of each run, Pallas kernels for 33% -> 30%
where the time goes in v10:
time: 66 us; the launch traced here: 65.8 us
  Pallas kernels  26.9 us (41%)
  starting transfers between devices  15.1 us (23%)
  blocking collectives  13.9 us (21%)
  waiting for transfers between devices  8.86 us (13%)
  other arithmetic  0.75 us (1%)
    ppermute x16, starting transfers between devices, swap(): return lax.ppermute(x, axis, [(i, i ^ step) for i in range(n)])  15.1 us
    all_to_all x1, blocking collectives, split_by_rep(): return lax.all_to_all(out, 'hid', 0, 0).astype(f32).sum(0).astype(bf16)  13.9 us
    pallas_call x2, Pallas kernels, fetch(): pl.pallas_call(functools.partial(fetch_kernel, first), in_specs=[spec(plt...  10.2 us
    pallas_call x2, Pallas kernels, gate_up(): pl.pallas_call(functools.partial(gate_up_kernel, len(arrays), len(weights...  10.2 us
    ppermute x16, waiting for transfers between devices, swap(): return lax.ppermute(x, axis, [(i, i ^ step) for i in range(n)])  8.86 us
    pallas_call x2, Pallas kernels, down(): pl.pallas_call(functools.partial(down_kernel, len(pieces), prev is not No...  6.06 us
  transfers between devices with their start and end apart: 16, of which 6 were waited for; matrix products, arithmetic and copies ran while one was open for 0% of the time, Pallas kernels for 30%

profile of v10, /device:TPU:0, one launch (start us, length us, event | category | flops | bytes accessed | tf_op | source)
XLA Modules:
  0.0 65.8 jit_solution(6309355652902173294)
XLA Ops:
  0.0 5.0 %collective-permute-start.2 = (bf16[16,2048]{1,0:T(8,128)(2,1)}, bf16[16,2048]{1,0:T(8,128)(2,1)S(1)}, u32[]{:S(2)}, u32[]{:S(2)}) collective-permute-start(bf16[16,2048]{1,0:T(8,128)(2,1)} %tokens_ref.3), channel_id=1, source_target_pairs={{0,12},{4,8},{8,4},{12,0},{1,13},{5,9},{9,5},{13,1},{2,14},{6,10},... | collective-permute-start | bytes 196616 | tf_op jit(solution)/shard_map/ppermute | solution.py:270
  5.0 0.0 collective-permute-start.1
  5.1 0.6 collective-permute-start
  5.6 1.7 %collective-permute-start.3 = (bf16[16,2048]{1,0:T(8,128)(2,1)}, bf16[16,2048]{1,0:T(8,128)(2,1)S(1)}, u32[]{:S(2)}, u32[]{:S(2)}) collective-permute-start(bf16[16,2048]{1,0:T(8,128)(2,1)} %tokens_ref.3), channel_id=1, source_target_pairs={{0,16},{16,0},{1,17},{17,1},{2,18},{18,2},{3,19},{19,3},{4,20},{20... | collective-permute-start | bytes 196616 | tf_op jit(solution)/shard_map/ppermute | solution.py:270
  7.4 0.1 pad_add_fusion.where
  7.4 4.8 %fetch.2 = (bf16[2048,1280]{1,0:T(8,128)(2,1)S(1)}, bf16[2048,1280]{1,0:T(8,128)(2,1)S(1)}, bf16[16,2048]{1,0:T(8,128)(2,1)S(1)}) custom-call(s32[3]{0:T(128)S(1)} %pad_add_fusion.where, bf16[2048,6656]{1,0:T(8,128)(2,1)} %refs_2_.1, bf16[2048,6656]{1,0:T(8,128)(2,1)} %refs_3_.1, bf16[16,2048]{1,0:T(8,128)(2,1)} %tokens_ref.3), custom_call_target="tpu_custom_call" | custom-call | bytes 1024 | tf_op jit(solution)/shard_map/fetch/pallas_call | solution.py:73
  12.2 0.0 collective-permute-done.2.refs_2_
  12.3 0.0 collective-permute-done.1.refs_1_
  12.3 0.0 collective-permute-done.refs_0_
  12.3 0.0 collective-permute-done.3.refs_4_.refs_2_
  12.3 0.4 collective-permute-start.4
  12.7 5.4 %fetch.3 = (bf16[2048,1280]{1,0:T(8,128)(2,1)S(1)}, bf16[2048,1280]{1,0:T(8,128)(2,1)S(1)}, bf16[16,2048]{1,0:T(8,128)(2,1)}) custom-call(s32[3]{0:T(128)S(1)} %pad_add_fusion.where, bf16[2048,6656]{1,0:T(8,128)(2,1)} %refs_2_.1, bf16[2048,6656]{1,0:T(8,128)(2,1)} %refs_3_.1, bf16[16,2048]{1,0:T(8,128)(2,1)} %tokens_ref.3), custom_call_target="tpu_custom_call" | custom-call | bytes 1024 | tf_op jit(solution)/shard_map/fetch/pallas_call | solution.py:73
  18.1 0.0 collective-permute-done.4.refs_3_
  18.1 3.6 %gate_up.2 = (bf16[2,64,2560]{2,1,0:T(8,128)(2,1)S(1)}, bf16[2,64,2560]{2,1,0:T(8,128)(2,1)S(1)}) custom-call(s32[3]{0:T(128)S(1)} %pad_add_fusion.where, bf16[16,2048]{1,0:T(8,128)(2,1)S(1)} %get-tuple-element.16.refs_3_.refs_0_, bf16[48,2048]{1,0:T(8,128)(2,1)S(1)} %join.3.refs_1_, bf16[16,2048]{1,0:T(8,128)(2,1)S(1)} %collective-permute-done.3.refs_4_.refs_2_, ...), custom_call_target="tpu_custom_call" | custom-call | bytes 1024 | tf_op jit(solution)/shard_map/gate_up/pallas_call | solution.py:148
  21.7 0.1 collective-permute-start.5
  21.8 2.1 %collective-permute-done.5.got_ref = bf16[2,64,2560]{2,1,0:T(8,128)(2,1)S(1)} collective-permute-done((bf16[2,64,2560]{2,1,0:T(8,128)(2,1)S(1)}, bf16[2,64,2560]{2,1,0:T(8,128)(2,1)S(1)}, u32[]{:S(2)}, u32[]{:S(2)}) %collective-permute-start.5) | collective-permute-done | bytes 655392 | tf_op jit(solution)/shard_map/ppermute | solution.py:270
  23.9 0.1 pair_sum.2.refs_4_
  23.9 0.0 slice-start.1
  24.0 0.0 slice-start.2
  24.0 0.0 slice-start.3
  24.0 0.0 slice-start.4
  24.0 0.0 slice-start.5
  24.0 0.0 slice-start.6
  24.0 1.8 %collective-permute-start.7 = (bf16[2,32,2560]{2,1,0:T(8,128)(2,1)S(1)}, bf16[2,32,2560]{2,1,0:T(8,128)(2,1)S(1)}, u32[]{:S(2)}, u32[]{:S(2)}) collective-permute-start(bf16[2,32,2560]{2,1,0:T(8,128)(2,1)S(1)} %pair_sum.2.refs_4_), channel_id=1, source_target_pairs={{0,2},{1,3},{2,0},{3,1},{4,6},{5,7},{6,4},{7,5},{8,10},{9,11},{10,... | collective-permute-start | bytes 983048 | tf_op jit(solution)/shard_map/ppermute | solution.py:270
  25.8 6.6 %gate_up.3 = (bf16[2,32,1536]{2,1,0:T(8,128)(2,1)S(1)}, bf16[2,32,1536]{2,1,0:T(8,128)(2,1)S(1)}) custom-call(s32[3]{0:T(128)S(1)} %pad_add_fusion.where, bf16[16,2048]{1,0:T(8,128)(2,1)S(1)} %get-tuple-element.16.refs_3_.refs_0_, bf16[48,2048]{1,0:T(8,128)(2,1)S(1)} %join.3.refs_1_, bf16[2048,6656]{1,0:T(8,128)(2,1)} %refs_2_.1, ...), custom_call_target="tpu_custom_call" | custom-call | bytes 1024 | tf_op jit(solution)/shard_map/gate_up/pallas_call | solution.py:148
  32.4 0.1 collective-permute-start.6
  32.5 1.3 %collective-permute-done.7.chip_ref = bf16[2,32,2560]{2,1,0:T(8,128)(2,1)S(1)} collective-permute-done((bf16[2,32,2560]{2,1,0:T(8,128)(2,1)S(1)}, bf16[2,32,2560]{2,1,0:T(8,128)(2,1)S(1)}, u32[]{:S(2)}, u32[]{:S(2)}) %collective-permute-start.7) | collective-permute-done | bytes 327712 | tf_op jit(solution)/shard_map/ppermute | solution.py:270
  33.8 0.2 combine.2
  34.0 0.0 collective-permute-done.6.got_ref
  34.1 1.8 %collective-permute-start.8 = (bf16[2,16,1536]{2,1,0:T(8,128)(2,1)S(1)}, bf16[2,16,1536]{2,1,0:T(8,128)(2,1)S(1)}, u32[]{:S(2)}, u32[]{:S(2)}) collective-permute-start(bf16[2,16,1536]{2,1,0:T(8,128)(2,1)S(1)} %pair_sum.3), channel_id=1, source_target_pairs={{0,2},{1,3},{2,0},{3,1},{4,6},{5,7},{6,4},{7,5},{8,10},{9,11},{10,... | collective-permute-start | bytes 294920 | tf_op jit(solution)/shard_map/ppermute | solution.py:270
  35.8 1.5 %collective-permute-start.9 = (bf16[16,2560]{1,0:T(8,128)(2,1)S(1)}, bf16[16,2560]{1,0:T(8,128)(2,1)S(1)}, u32[]{:S(2)}, u32[]{:S(2)}) collective-permute-start(bf16[16,2560]{1,0:T(8,128)(2,1)S(1)} %get-tuple-element.25.refs_0_), channel_id=1, source_target_pairs={{0,16},{16,0},{1,17},{17,1},{2,18},{18,2},{3,19},{19,3},{4,20},{20... | collective-permute-start | bytes 245768 | tf_op jit(solution)/shard_map/ppermute | solution.py:270
  37.4 0.5 collective-permute-start.12
  37.9 2.4 %collective-permute-done.9.refs_0_ = bf16[16,2560]{1,0:T(8,128)(2,1)S(1)} collective-permute-done((bf16[16,2560]{1,0:T(8,128)(2,1)S(1)}, bf16[16,2560]{1,0:T(8,128)(2,1)S(1)}, u32[]{:S(2)}, u32[]{:S(2)}) %collective-permute-start.9) | collective-permute-done | bytes 81952 | tf_op jit(solution)/shard_map/ppermute | solution.py:270
  40.3 0.0 collective-permute-done.8.chip_ref
  40.3 0.1 combine.3.refs_1_.refs_0_
  40.4 1.0 %collective-permute-start.10 = (bf16[16,4096]{1,0:T(8,128)(2,1)S(1)}, bf16[16,4096]{1,0:T(8,128)(2,1)S(1)}, u32[]{:S(2)}, u32[]{:S(2)}) collective-permute-start(bf16[16,4096]{1,0:T(8,128)(2,1)S(1)} %combine.3.refs_1_.refs_0_), channel_id=1, source_target_pairs={{0,2},{1,3},{2,0},{3,1},{4,6},{5,7},{6,4},{7,5},{8,10},{9,11},{10,... | collective-permute-start | bytes 393224 | tf_op jit(solution)/shard_map/ppermute | solution.py:270
  41.3 0.0 collective-permute-start.13
  41.3 1.1 %collective-permute-done.12.refs_0_.refs_1_ = bf16[16,2560]{1,0:T(8,128)(2,1)S(1)} collective-permute-done((bf16[16,2560]{1,0:T(8,128)(2,1)S(1)}, bf16[16,2560]{1,0:T(8,128)(2,1)S(1)}, u32[]{:S(2)}, u32[]{:S(2)}) %collective-permute-start.12) | collective-permute-done | bytes 81952 | tf_op jit(solution)/shard_map/ppermute | solution.py:270
  42.4 0.0 collective-permute-start.14
  42.4 0.5 collective-permute-start.11
  42.9 0.0 collective-permute-done.13.refs_2_
  42.9 0.8 %collective-permute-done.14.refs_3_ = bf16[16,2560]{1,0:T(8,128)(2,1)S(1)} collective-permute-done((bf16[16,2560]{1,0:T(8,128)(2,1)S(1)}, bf16[16,2560]{1,0:T(8,128)(2,1)S(1)}, u32[]{:S(2)}, u32[]{:S(2)}) %collective-permute-start.14) | collective-permute-done | bytes 81952 | tf_op jit(solution)/shard_map/ppermute | solution.py:270
  43.8 2.5 %down.2.refs_1_.refs_5_ = f32[64,2048]{1,0:T(8,128)S(1)} custom-call(s32[3]{0:T(128)S(1)} %pad_add_fusion.where, bf16[16,2560]{1,0:T(8,128)(2,1)S(1)} %get-tuple-element.26.refs_0_, bf16[16,2560]{1,0:T(8,128)(2,1)S(1)} %collective-permute-done.12.refs_0_.refs_1_, bf16[16,2560]{1,0:T(8,128)(2,1)S(1)} %collective-permute-done.13.refs_2_, ...), custom_call_target="tpu_custom_call" | custom-call | bytes 1024 | tf_op jit(solution)/shard_map/down/pallas_call | solution.py:250
  46.3 0.2 collective-permute-start.15
  46.5 1.2 %collective-permute-done.15.refs_3_ = bf16[16,4096]{1,0:T(8,128)(2,1)S(1)} collective-permute-done((bf16[16,4096]{1,0:T(8,128)(2,1)S(1)}, bf16[16,4096]{1,0:T(8,128)(2,1)S(1)}, u32[]{:S(2)}, u32[]{:S(2)}) %collective-permute-start.15) | collective-permute-done | bytes 131104 | tf_op jit(solution)/shard_map/ppermute | solution.py:270
  47.7 3.6 %down.3 = bf16[4,16,2048]{2,1,0:T(8,128)(2,1)S(1)} custom-call(s32[3]{0:T(128)S(1)} %pad_add_fusion.where, bf16[16,4096]{1,0:T(8,128)(2,1)S(1)} %combine.3.refs_1_.refs_0_, bf16[16,4096]{1,0:T(8,128)(2,1)S(1)} %collective-permute-done.10.refs_0_.refs_1_, bf16[16,4096]{1,0:T(8,128)(2,1)S(1)} %collective-permute-done.11.refs_2_, ...), custom_call_target="tpu_custom_call" | custom-call | bytes 1024 | tf_op jit(solution)/shard_map/down/pallas_call | solution.py:250
  51.3 13.9 %all_to_all.5 = bf16[4,16,2048]{2,1,0:T(8,128)(2,1)S(1)} all-to-all(bf16[4,16,2048]{2,1,0:T(8,128)(2,1)S(1)} %down.3), channel_id=1, replica_groups=mesh['rep'=2,'hid'=4,'wid'=4] {'hid'}, dimensions={0} | all-to-all | bytes 524288 | tf_op jit(solution)/shard_map/all_to_all | solution.py:309
  65.1 0.7 %reduce_sum.12 = bf16[16,2048]{1,0:T(8,128)(2,1)} reduce(bf16[4,16,2048]{2,1,0:T(8,128)(2,1)S(1)} %all_to_all.5, bf16[]{:T(256)} %constant.17.clone.1), dimensions={0}, to_apply=%region_0.0 | reduce | flops 98304 | bytes 327682 | tf_op jit(solution)/shard_map/reduce_sum | solution.py:309
  (15 shorter events, 0.1 us)
Async XLA Ops:
  0.0 12.3 %collective-permute-start.2 = (bf16[16,2048]{1,0:T(8,128)(2,1)}, bf16[16,2048]{1,0:T(8,128)(2,1)S(1)}, u32[]{:S(2)}, u32[]{:S(2)}) collective-permute-start(bf16[16,2048]{1,0:T(8,128)(2,1)} %tokens_ref.3), channel_id=1, source_target_pairs={{0,12},{4,8},{8,4},{12,0},{1,13},{5,9},{9,5},{13,1},{2,14},{6,10},... | collective-permute-start | bytes 196616 | tf_op jit(solution)/shard_map/ppermute | solution.py:270
  5.0 7.2 %collective-permute-start.1 = (bf16[16,2048]{1,0:T(8,128)(2,1)}, bf16[16,2048]{1,0:T(8,128)(2,1)S(1)}, u32[]{:S(2)}, u32[]{:S(2)}) collective-permute-start(bf16[16,2048]{1,0:T(8,128)(2,1)} %tokens_ref.3), channel_id=1, source_target_pairs={{0,8},{4,12},{8,0},{12,4},{1,9},{5,13},{9,1},{13,5},{2,10},{6,14},... | collective-permute-start | bytes 196616 | tf_op jit(solution)/shard_map/ppermute | solution.py:270
  5.1 7.2 %collective-permute-start = (bf16[16,2048]{1,0:T(8,128)(2,1)}, bf16[16,2048]{1,0:T(8,128)(2,1)S(1)}, u32[]{:S(2)}, u32[]{:S(2)}) collective-permute-start(bf16[16,2048]{1,0:T(8,128)(2,1)} %tokens_ref.3), channel_id=1, source_target_pairs={{0,4},{4,0},{8,12},{12,8},{1,5},{5,1},{9,13},{13,9},{2,6},{6,2},{1... | collective-permute-start | bytes 196616 | tf_op jit(solution)/shard_map/ppermute | solution.py:270
  5.6 6.7 %collective-permute-start.3 = (bf16[16,2048]{1,0:T(8,128)(2,1)}, bf16[16,2048]{1,0:T(8,128)(2,1)S(1)}, u32[]{:S(2)}, u32[]{:S(2)}) collective-permute-start(bf16[16,2048]{1,0:T(8,128)(2,1)} %tokens_ref.3), channel_id=1, source_target_pairs={{0,16},{16,0},{1,17},{17,1},{2,18},{18,2},{3,19},{19,3},{4,20},{20... | collective-permute-start | bytes 196616 | tf_op jit(solution)/shard_map/ppermute | solution.py:270
  12.3 5.8 %collective-permute-start.4 = (bf16[48,2048]{1,0:T(8,128)(2,1)S(1)}, bf16[48,2048]{1,0:T(8,128)(2,1)S(1)}, u32[]{:S(2)}, u32[]{:S(2)}) collective-permute-start(bf16[48,2048]{1,0:T(8,128)(2,1)S(1)} %join.3.refs_1_), channel_id=1, source_target_pairs={{0,16},{16,0},{1,17},{17,1},{2,18},{18,2},{3,19},{19,3},{4,20},{20... | collective-permute-start | bytes 589832 | tf_op jit(solution)/shard_map/ppermute | solution.py:270
  21.7 2.2 %collective-permute-start.5 = (bf16[2,64,2560]{2,1,0:T(8,128)(2,1)S(1)}, bf16[2,64,2560]{2,1,0:T(8,128)(2,1)S(1)}, u32[]{:S(2)}, u32[]{:S(2)}) collective-permute-start(bf16[2,64,2560]{2,1,0:T(8,128)(2,1)S(1)} %get-tuple-element.22), channel_id=1, source_target_pairs={{0,1},{1,0},{2,3},{3,2},{4,5},{5,4},{6,7},{7,6},{8,9},{9,8},{10,11... | collective-permute-start | bytes 1966088 | tf_op jit(solution)/shard_map/ppermute | solution.py:270
  23.9 19.8 %slice-start = ((s8[27262976]{0:T(1024)(128)(4,1)}), s8[4194304]{0:T(1024)(128)(4,1)S(1)}, s32[]{:S(2)}) async-start(s8[27262976]{0:T(1024)(128)(4,1)} %bitcast.3), calls=%async_computation.1 | async-start | bytes 8388608
  23.9 19.8 %slice-start.1 = ((s8[27262976]{0:T(1024)(128)(4,1)}), s8[4194304]{0:T(1024)(128)(4,1)S(1)}, s32[]{:S(2)}) async-start(s8[27262976]{0:T(1024)(128)(4,1)} %bitcast.3), calls=%async_computation.2 | async-start | bytes 8388608
  24.0 19.7 %slice-start.2 = ((s8[27262976]{0:T(1024)(128)(4,1)}), s8[4194304]{0:T(1024)(128)(4,1)S(1)}, s32[]{:S(2)}) async-start(s8[27262976]{0:T(1024)(128)(4,1)} %bitcast.3), calls=%async_computation.3 | async-start | bytes 8388608
  24.0 19.7 %slice-start.3 = ((s8[27262976]{0:T(1024)(128)(4,1)}), s8[4194304]{0:T(1024)(128)(4,1)S(1)}, s32[]{:S(2)}) async-start(s8[27262976]{0:T(1024)(128)(4,1)} %bitcast.3), calls=%async_computation.4 | async-start | bytes 8388608
  24.0 19.7 %slice-start.4 = ((s8[27262976]{0:T(1024)(128)(4,1)}), s8[4194304]{0:T(1024)(128)(4,1)S(1)}, s32[]{:S(2)}) async-start(s8[27262976]{0:T(1024)(128)(4,1)} %bitcast.3), calls=%async_computation.5 | async-start | bytes 8388608
  24.0 19.7 %slice-start.5 = ((s8[27262976]{0:T(1024)(128)(4,1)}), s8[4194304]{0:T(1024)(128)(4,1)S(1)}, s32[]{:S(2)}) async-start(s8[27262976]{0:T(1024)(128)(4,1)} %bitcast.3), calls=%async_computation.6 | async-start | bytes 8388608
  24.0 19.7 %slice-start.6 = ((s8[27262976]{0:T(1024)(128)(4,1)}), s8[2097152]{0:T(1024)(128)(4,1)S(1)}, s32[]{:S(2)}) async-start(s8[27262976]{0:T(1024)(128)(4,1)} %bitcast.3), calls=%async_computation.7 | async-start | bytes 4194304
  24.0 9.8 %collective-permute-start.7 = (bf16[2,32,2560]{2,1,0:T(8,128)(2,1)S(1)}, bf16[2,32,2560]{2,1,0:T(8,128)(2,1)S(1)}, u32[]{:S(2)}, u32[]{:S(2)}) collective-permute-start(bf16[2,32,2560]{2,1,0:T(8,128)(2,1)S(1)} %pair_sum.2.refs_4_), channel_id=1, source_target_pairs={{0,2},{1,3},{2,0},{3,1},{4,6},{5,7},{6,4},{7,5},{8,10},{9,11},{10,... | collective-permute-start | bytes 983048 | tf_op jit(solution)/shard_map/ppermute | solution.py:270
  32.4 1.6 %collective-permute-start.6 = (bf16[2,32,1536]{2,1,0:T(8,128)(2,1)S(1)}, bf16[2,32,1536]{2,1,0:T(8,128)(2,1)S(1)}, u32[]{:S(2)}, u32[]{:S(2)}) collective-permute-start(bf16[2,32,1536]{2,1,0:T(8,128)(2,1)S(1)} %get-tuple-element.24), channel_id=1, source_target_pairs={{0,1},{1,0},{2,3},{3,2},{4,5},{5,4},{6,7},{7,6},{8,9},{9,8},{10,11... | collective-permute-start | bytes 589832 | tf_op jit(solution)/shard_map/ppermute | solution.py:270
  34.1 6.2 %collective-permute-start.8 = (bf16[2,16,1536]{2,1,0:T(8,128)(2,1)S(1)}, bf16[2,16,1536]{2,1,0:T(8,128)(2,1)S(1)}, u32[]{:S(2)}, u32[]{:S(2)}) collective-permute-start(bf16[2,16,1536]{2,1,0:T(8,128)(2,1)S(1)} %pair_sum.3), channel_id=1, source_target_pairs={{0,2},{1,3},{2,0},{3,1},{4,6},{5,7},{6,4},{7,5},{8,10},{9,11},{10,... | collective-permute-start | bytes 294920 | tf_op jit(solution)/shard_map/ppermute | solution.py:270
  35.8 4.4 %collective-permute-start.9 = (bf16[16,2560]{1,0:T(8,128)(2,1)S(1)}, bf16[16,2560]{1,0:T(8,128)(2,1)S(1)}, u32[]{:S(2)}, u32[]{:S(2)}) collective-permute-start(bf16[16,2560]{1,0:T(8,128)(2,1)S(1)} %get-tuple-element.25.refs_0_), channel_id=1, source_target_pairs={{0,16},{16,0},{1,17},{17,1},{2,18},{18,2},{3,19},{19,3},{4,20},{20... | collective-permute-start | bytes 245768 | tf_op jit(solution)/shard_map/ppermute | solution.py:270
  37.4 5.0 %collective-permute-start.12 = (bf16[16,2560]{1,0:T(8,128)(2,1)S(1)}, bf16[16,2560]{1,0:T(8,128)(2,1)S(1)}, u32[]{:S(2)}, u32[]{:S(2)}) collective-permute-start(bf16[16,2560]{1,0:T(8,128)(2,1)S(1)} %get-tuple-element.26.refs_0_), channel_id=1, source_target_pairs={{0,2},{1,3},{2,0},{3,1},{4,6},{5,7},{6,4},{7,5},{8,10},{9,11},{10,... | collective-permute-start | bytes 245768 | tf_op jit(solution)/shard_map/ppermute | solution.py:270
  40.4 5.9 %collective-permute-start.10 = (bf16[16,4096]{1,0:T(8,128)(2,1)S(1)}, bf16[16,4096]{1,0:T(8,128)(2,1)S(1)}, u32[]{:S(2)}, u32[]{:S(2)}) collective-permute-start(bf16[16,4096]{1,0:T(8,128)(2,1)S(1)} %combine.3.refs_1_.refs_0_), channel_id=1, source_target_pairs={{0,2},{1,3},{2,0},{3,1},{4,6},{5,7},{6,4},{7,5},{8,10},{9,11},{10,... | collective-permute-start | bytes 393224 | tf_op jit(solution)/shard_map/ppermute | solution.py:270
  41.3 1.6 %collective-permute-start.13 = (bf16[16,2560]{1,0:T(8,128)(2,1)S(1)}, bf16[16,2560]{1,0:T(8,128)(2,1)S(1)}, u32[]{:S(2)}, u32[]{:S(2)}) collective-permute-start(bf16[16,2560]{1,0:T(8,128)(2,1)S(1)} %get-tuple-element.26.refs_0_), channel_id=1, source_target_pairs={{0,1},{1,0},{2,3},{3,2},{4,5},{5,4},{6,7},{7,6},{8,9},{9,8},{10,11... | collective-permute-start | bytes 245768 | tf_op jit(solution)/shard_map/ppermute | solution.py:270
  42.4 1.3 %collective-permute-start.14 = (bf16[16,2560]{1,0:T(8,128)(2,1)S(1)}, bf16[16,2560]{1,0:T(8,128)(2,1)S(1)}, u32[]{:S(2)}, u32[]{:S(2)}) collective-permute-start(bf16[16,2560]{1,0:T(8,128)(2,1)S(1)} %join.4), channel_id=1, source_target_pairs={{0,1},{1,0},{2,3},{3,2},{4,5},{5,4},{6,7},{7,6},{8,9},{9,8},{10,11... | collective-permute-start | bytes 245768 | tf_op jit(solution)/shard_map/ppermute | solution.py:270
  42.4 4.0 %collective-permute-start.11 = (bf16[16,4096]{1,0:T(8,128)(2,1)S(1)}, bf16[16,4096]{1,0:T(8,128)(2,1)S(1)}, u32[]{:S(2)}, u32[]{:S(2)}) collective-permute-start(bf16[16,4096]{1,0:T(8,128)(2,1)S(1)} %combine.3.refs_1_.refs_0_), channel_id=1, source_target_pairs={{0,1},{1,0},{2,3},{3,2},{4,5},{5,4},{6,7},{7,6},{8,9},{9,8},{10,11... | collective-permute-start | bytes 393224 | tf_op jit(solution)/shard_map/ppermute | solution.py:270
  46.3 1.4 %collective-permute-start.15 = (bf16[16,4096]{1,0:T(8,128)(2,1)S(1)}, bf16[16,4096]{1,0:T(8,128)(2,1)S(1)}, u32[]{:S(2)}, u32[]{:S(2)}) collective-permute-start(bf16[16,4096]{1,0:T(8,128)(2,1)S(1)} %join.5), channel_id=1, source_target_pairs={{0,1},{1,0},{2,3},{3,2},{4,5},{5,4},{6,7},{7,6},{8,9},{9,8},{10,11... | collective-permute-start | bytes 393224 | tf_op jit(solution)/shard_map/ppermute | solution.py:270

commit v11 on v8

--- a/solution.py
+++ b/solution.py
@@ -8,7 +8,7 @@
 from jax.sharding import PartitionSpec as P
 
 TILE = 256
-LAST = 3
+CHUNKS = (6, 3, 4)
 ROWS = 16
 COST = pl.CostEstimate(flops=0, bytes_accessed=1024, transcendentals=0)
 
@@ -154,7 +154,7 @@
         out_specs=[spec(pltpu.VMEM)] * 2,
         scratch_shapes=scratch,
         out_shape=[jax.ShapeDtypeStruct((2, total // 2, width), jnp.bfloat16)] * 2,
-        compiler_params=params(16 if segments else 4),
+        compiler_params=params(20 if segments else 4),
         cost_estimate=COST,
         name="gate_up",
     )(where, *arrays, *weights, *behind)
@@ -199,7 +199,7 @@
 
 def combine_kernel(n_left, n_sums, n_outs, *refs):
     lefts, refs, outs = refs[:n_left], refs[n_left:], refs[-n_outs:]
-    first = 0
+    first, total = 0, sum(refs[3 * i + 2].shape[2] for i in range(n_sums))
     for left in lefts:
         outs[0][:, first : first + left.shape[1]] = left[...]
         first += left.shape[1]
@@ -215,19 +215,21 @@
             )
             hidden = (gate / (1 + jnp.exp(-gate)) * up).astype(jnp.bfloat16)
             for j, out in enumerate(outs):
-                out[:, first + a : first + b] = hidden[j * ROWS : (j + 1) * ROWS]
-        first += width
+                at = out.shape[1] - total + a
+                out[:, at : at + b - a] = hidden[j * ROWS : (j + 1) * ROWS]
+        total -= width
 
 
 def combine(sums, left, behind):
     n_outs = sums[0][2].shape[1] // ROWS
-    width = sum(x.shape[1] for x in left) + sum(chip.shape[2] for _, _, chip in sums)
+    width = sum(chip.shape[2] for _, _, chip in sums)
+    widths = [width + sum(x.shape[1] for x in left)] + [width] * (n_outs - 1)
     args = [*left, *(x for triple in sums for x in triple)]
     return pl.pallas_call(
         functools.partial(combine_kernel, len(left), len(sums), n_outs),
         in_specs=[spec(pltpu.VMEM)] * len(args) + [spec(pl.ANY)] * len(behind),
         out_specs=[spec(pltpu.VMEM)] * n_outs,
-        out_shape=[jax.ShapeDtypeStruct((ROWS, width), jnp.bfloat16)] * n_outs,
+        out_shape=[jax.ShapeDtypeStruct((ROWS, w), jnp.bfloat16) for w in widths],
         compiler_params=params(2),
         cost_estimate=COST,
         name="combine",
@@ -287,9 +289,8 @@
         n = {"rep": 2, "hid": 4, "wid": 4}[axis]
         return lax.ppermute(x, axis, [(i, i ^ step) for i in range(n)])
 
-    tiles = half // TILE
-    bounds = [0, (tiles - LAST) // 2 * TILE, (tiles - LAST) * TILE, half]
-    widths = [b - a for a, b in zip(bounds[:-1], bounds[1:])]
+    bounds = [sum(CHUNKS[:c]) * TILE for c in range(4)]
+    both = [[(r * half + a, b - a) for r in range(2)] for a, b in zip(bounds[:-1], bounds[1:])]
     gate_weight, up_weight, hbm_tokens = (
         pltpu.with_memory_space_constraint(w, pltpu.HBM) for w in (gate_weight, up_weight, tokens)
     )
@@ -297,32 +298,37 @@
 
     far_own = swap(tokens, "rep", 1)
     by_hid = [swap(tokens, "hid", d) for d in (3, 2, 1)][::-1]
-    early = [fetch(where, gate_weight, up_weight, hbm_tokens, bounds[c], widths[c]) for c in range(2)]
-    own = early[0][2]
+    *early, own = fetch(where, gate_weight, up_weight, hbm_tokens, 0, bounds[1])
     near = join(by_hid, [own, far_own])
     far = swap(near, "rep", 1)
 
-    sums, to_chips, behind = [], [], [early[1][0]]
-    for weights in early:
-        mine, theirs = gate_up(where, [own, near, far_own, far], weights[:2], [], behind)
-        behind = [mine]
-        got = swap(theirs, "wid", 1)
-        to_chips.append(pair_sum(mine, got, []))
-        sums.append((mine, got, swap(to_chips[-1], "wid", 2)))
-    segments = [(bounds[2], widths[2]), (half + bounds[2], widths[2])]
-    mine, theirs = gate_up(where, [own, near], [gate_weight, up_weight], segments, to_chips)
-    got = swap(later(theirs, [s[2] for s in sums]), "wid", 1)
-    to_chip = pair_sum(mine, got, [])
-    last_sum = (mine, got, swap(to_chip, "wid", 2))
-
-    keep, give = combine(sums, [], [to_chip])
-    (rest,) = combine([last_sum], [swap(give, "rep", 1)], [])
-    rest_segments = [(-1, half, bounds[2])] + [(0, start, width) for start, width in segments]
-    acc, behind = None, [rest]
-    for hidden, parts in ((keep, [(1, 0, bounds[2])]), (rest, rest_segments)):
+    def reduce(mine, got):
+        to_chip = pair_sum(mine, got, [])
+        return to_chip, (mine, got, swap(to_chip, "wid", 2))
+
+    weights = [gate_weight, up_weight]
+    mine_1, theirs_1 = gate_up(where, [own, near], weights, both[1], [])
+    mine_0, theirs_0 = gate_up(where, [own, near, far_own, far], early, [], [mine_1])
+    to_chip_1, sum_1 = reduce(mine_1, swap(theirs_1, "wid", 1))
+    to_chip_0, sum_0 = reduce(mine_0, swap(theirs_0, "wid", 1))
+    mine_2, theirs_2 = gate_up(where, [own, near], weights, both[2], [to_chip_1, to_chip_0])
+    theirs_2 = later(theirs_2, [sum_1[2], sum_0[2]])
+    _, sum_2 = reduce(mine_2, swap(theirs_2, "wid", 1))
+
+    (first,) = combine([sum_1], [], [])
+    first, give = combine([sum_0], [first], [])
+    second = swap(give, "rep", 1)
+    (third,) = combine([sum_2], [], [])
+    static = [[(0, *segment) for segment in segments] for segments in both]
+    acc, behind = None, [second]
+    for hidden, segments in (
+        (first, static[1] + [(1, 0, bounds[1])]),
+        (second, [(-1, half, bounds[1])]),
+        (third, static[2]),
+    ):
         other = swap(hidden, "wid", 2)
-        crossed = swap(join([hidden, other], behind), "wid", 1)
-        acc = down(where, [hidden, other, crossed], down_weight, acc, parts, hidden is rest)
+        pieces = [hidden, other, swap(hidden, "wid", 1), swap(join([other], behind), "wid", 1)]
+        acc = down(where, pieces, down_weight, acc, segments, hidden is third)
         behind = [acc]
 
     mixed = acc[0].astype(f32)
@@ -337,7 +343,7 @@
     def on_device(tokens, gate_weight, up_weight, down_weight):
         fits = (
             (n_rep, n_hid, n_wid) == (2, 4, 4)
-            and gate_weight.shape[1] % (n_rep * TILE) == 0
+            and gate_weight.shape[1] == n_rep * sum(CHUNKS) * TILE
             and tokens.shape[0] == ROWS
         )
         if not fits:

time: 64.9 us -> 64.3 us (level)
  waiting for transfers between devices: 16.7 us -> 11.6 us
  starting transfers between devices: 19.6 us -> 22.8 us
  Pallas kernels: 27.4 us -> 28.6 us
    pallas_call x3, Pallas kernels: 10.7 us -> 16 us  [gate_up(): pl.pallas_call(functools.partial(gate_up_kernel, len(arrays), len(weights...]
    ppermute x19 -> x24, waiting for transfers between devices: 16.7 us -> 11.6 us  [swap(): return lax.ppermute(x, axis, [(i, i ^ step) for i in range(n)])]
    pallas_call x2 -> x1, Pallas kernels: 10.2 us -> 5.4 us  [fetch(): pl.pallas_call(functools.partial(fetch_kernel, first), in_specs=[spec(plt...]
    ppermute x19 -> x24, starting transfers between devices: 19.6 us -> 22.8 us  [swap(): return lax.ppermute(x, axis, [(i, i ^ step) for i in range(n)])]
    pallas_call x2 -> x3, Pallas kernels: 6.06 us -> 6.71 us  [down(): pl.pallas_call(functools.partial(down_kernel, len(pieces), prev is not No...]
  transfers between devices with their start and end apart: 19 -> 24, of which waited for: 10 -> 10; matrix products, arithmetic and copies ran while one was open for 0% -> 0% of each run, Pallas kernels for 30% -> 37%
where the time goes in v11:
time: 64.3 us; the launch traced here: 64.1 us
  Pallas kernels  28.6 us (44%)
  starting transfers between devices  22.8 us (35%)
  waiting for transfers between devices  11.6 us (18%)
  other arithmetic  0.74 us (1%)
    ppermute x24, starting transfers between devices, swap(): return lax.ppermute(x, axis, [(i, i ^ step) for i in range(n)])  22.8 us
    pallas_call x3, Pallas kernels, gate_up(): pl.pallas_call(functools.partial(gate_up_kernel, len(arrays), len(weights...  16 us
    ppermute x24, waiting for transfers between devices, swap(): return lax.ppermute(x, axis, [(i, i ^ step) for i in range(n)])  11.6 us
    pallas_call x3, Pallas kernels, down(): pl.pallas_call(functools.partial(down_kernel, len(pieces), prev is not No...  6.71 us
    pallas_call x1, Pallas kernels, fetch(): pl.pallas_call(functools.partial(fetch_kernel, first), in_specs=[spec(plt...  5.4 us
  transfers between devices with their start and end apart: 24, of which 10 were waited for; matrix products, arithmetic and copies ran while one was open for 0% of the time, Pallas kernels for 37%

profile of v11, /device:TPU:0, one launch (start us, length us, event | category | flops | bytes accessed | tf_op | source)
XLA Modules:
  0.0 64.1 jit_solution(3132520898600644866)
XLA Ops:
  0.0 4.0 %collective-permute-start.1 = (bf16[16,2048]{1,0:T(8,128)(2,1)}, bf16[16,2048]{1,0:T(8,128)(2,1)S(1)}, u32[]{:S(2)}, u32[]{:S(2)}) collective-permute-start(bf16[16,2048]{1,0:T(8,128)(2,1)} %tokens_ref.1), channel_id=1, source_target_pairs={{0,8},{4,12},{8,0},{12,4},{1,9},{5,13},{9,1},{13,5},{2,10},{6,14},... | collective-permute-start | bytes 196616 | tf_op jit(solution)/shard_map/ppermute | solution.py:290
  4.0 1.6 %collective-permute-start = (bf16[16,2048]{1,0:T(8,128)(2,1)}, bf16[16,2048]{1,0:T(8,128)(2,1)S(1)}, u32[]{:S(2)}, u32[]{:S(2)}) collective-permute-start(bf16[16,2048]{1,0:T(8,128)(2,1)} %tokens_ref.1), channel_id=1, source_target_pairs={{0,4},{4,0},{8,12},{12,8},{1,5},{5,1},{9,13},{13,9},{2,6},{6,2},{1... | collective-permute-start | bytes 196616 | tf_op jit(solution)/shard_map/ppermute | solution.py:290
  5.6 1.5 %collective-permute-start.3 = (bf16[16,2048]{1,0:T(8,128)(2,1)}, bf16[16,2048]{1,0:T(8,128)(2,1)S(1)}, u32[]{:S(2)}, u32[]{:S(2)}) collective-permute-start(bf16[16,2048]{1,0:T(8,128)(2,1)} %tokens_ref.1), channel_id=1, source_target_pairs={{0,16},{16,0},{1,17},{17,1},{2,18},{18,2},{3,19},{19,3},{4,20},{20... | collective-permute-start | bytes 196616 | tf_op jit(solution)/shard_map/ppermute | solution.py:290
  7.1 0.2 collective-permute-start.2
  7.4 0.1 pad_add_fusion.where
  7.4 5.4 %fetch.1 = (bf16[2048,1536]{1,0:T(8,128)(2,1)S(1)}, bf16[2048,1536]{1,0:T(8,128)(2,1)S(1)}, bf16[16,2048]{1,0:T(8,128)(2,1)S(1)}) custom-call(s32[2]{0:T(128)S(1)} %pad_add_fusion.where, bf16[2048,6656]{1,0:T(8,128)(2,1)} %refs_2_.3, bf16[2048,6656]{1,0:T(8,128)(2,1)} %refs_3_.3, bf16[16,2048]{1,0:T(8,128)(2,1)} %tokens_ref.1), custom_call_target="tpu_custom_call" | custom-call | bytes 1024 | tf_op jit(solution)/shard_map/fetch/pallas_call | solution.py:73
  12.8 0.0 collective-permute-done.1.refs_1_
  12.9 0.0 collective-permute-done.refs_0_
  12.9 0.5 collective-permute-done.2.refs_2_
  13.4 0.6 collective-permute-start.5
  14.0 5.9 %gate_up.3 = (bf16[2,32,1536]{2,1,0:T(8,128)(2,1)S(1)}, bf16[2,32,1536]{2,1,0:T(8,128)(2,1)S(1)}) custom-call(s32[2]{0:T(128)S(1)} %pad_add_fusion.where, bf16[16,2048]{1,0:T(8,128)(2,1)S(1)} %get-tuple-element.20.refs_3_.refs_0_, bf16[48,2048]{1,0:T(8,128)(2,1)S(1)} %join.4.refs_1_, bf16[2048,6656]{1,0:T(8,128)(2,1)} %refs_2_.3, bf16[2048,6656]{1,0:T(8,128)(2,1)} %refs_3_.3), custom_call_target="tpu_custom_call" | custom-call | bytes 1024 | tf_op jit(solution)/shard_map/gate_up/pallas_call | solution.py:148
  19.9 2.5 %gate_up.4 = (bf16[2,64,1536]{2,1,0:T(8,128)(2,1)S(1)}, bf16[2,64,1536]{2,1,0:T(8,128)(2,1)S(1)}) custom-call(s32[2]{0:T(128)S(1)} %pad_add_fusion.where, bf16[16,2048]{1,0:T(8,128)(2,1)S(1)} %get-tuple-element.20.refs_3_.refs_0_, bf16[48,2048]{1,0:T(8,128)(2,1)S(1)} %join.4.refs_1_, bf16[16,2048]{1,0:T(8,128)(2,1)S(1)} %collective-permute-done.3.refs_4_.refs_2_, ...), custom_call_target="tpu_custom_call" | custom-call | bytes 1024 | tf_op jit(solution)/shard_map/gate_up/pallas_call | solution.py:148
  22.4 0.1 collective-permute-start.6
  22.5 0.5 collective-permute-start.4
  23.0 1.2 %collective-permute-done.6.got_ref.refs_2_ = bf16[2,64,1536]{2,1,0:T(8,128)(2,1)S(1)} collective-permute-done((bf16[2,64,1536]{2,1,0:T(8,128)(2,1)S(1)}, bf16[2,64,1536]{2,1,0:T(8,128)(2,1)S(1)}, u32[]{:S(2)}, u32[]{:S(2)}) %collective-permute-start.6) | collective-permute-done | bytes 393248 | tf_op jit(solution)/shard_map/ppermute | solution.py:290
  24.3 1.5 %collective-permute-start.8 = (bf16[2,32,1536]{2,1,0:T(8,128)(2,1)S(1)}, bf16[2,32,1536]{2,1,0:T(8,128)(2,1)S(1)}, u32[]{:S(2)}, u32[]{:S(2)}) collective-permute-start(bf16[2,32,1536]{2,1,0:T(8,128)(2,1)S(1)} %pair_sum.4.refs_5_), channel_id=1, source_target_pairs={{0,2},{1,3},{2,0},{3,1},{4,6},{5,7},{6,4},{7,5},{8,10},{9,11},{10,... | collective-permute-start | bytes 589832 | tf_op jit(solution)/shard_map/ppermute | solution.py:290
  25.9 0.0 slice-start.1
  25.9 0.0 slice-start.2
  25.9 0.0 slice-start.4
  25.9 0.6 collective-permute-start.7
  26.5 7.6 %gate_up.5 = (bf16[2,32,2048]{2,1,0:T(8,128)(2,1)S(1)}, bf16[2,32,2048]{2,1,0:T(8,128)(2,1)S(1)}) custom-call(s32[2]{0:T(128)S(1)} %pad_add_fusion.where, bf16[16,2048]{1,0:T(8,128)(2,1)S(1)} %get-tuple-element.20.refs_3_.refs_0_, bf16[48,2048]{1,0:T(8,128)(2,1)S(1)} %join.4.refs_1_, bf16[2048,6656]{1,0:T(8,128)(2,1)} %refs_2_.3, ...), custom_call_target="tpu_custom_call" | custom-call | bytes 1024 | tf_op jit(solution)/shard_map/gate_up/pallas_call | solution.py:148
  34.2 0.1 collective-permute-start.9
  34.3 0.1 combine.4.refs_0_
  34.4 0.1 combine.5
  34.5 1.7 %collective-permute-start.16 = (bf16[16,3072]{1,0:T(8,128)(2,1)S(1)}, bf16[16,3072]{1,0:T(8,128)(2,1)S(1)}, u32[]{:S(2)}, u32[]{:S(2)}) collective-permute-start(bf16[16,3072]{1,0:T(8,128)(2,1)S(1)} %get-tuple-element.30.refs_0_), channel_id=1, source_target_pairs={{0,2},{1,3},{2,0},{3,1},{4,6},{5,7},{6,4},{7,5},{8,10},{9,11},{10,... | collective-permute-start | bytes 294920 | tf_op jit(solution)/shard_map/ppermute | solution.py:290
  36.3 1.5 %collective-permute-start.13 = (bf16[16,1536]{1,0:T(8,128)(2,1)S(1)}, bf16[16,1536]{1,0:T(8,128)(2,1)S(1)}, u32[]{:S(2)}, u32[]{:S(2)}) collective-permute-start(bf16[16,1536]{1,0:T(8,128)(2,1)S(1)} %get-tuple-element.29), channel_id=1, source_target_pairs={{0,16},{16,0},{1,17},{17,1},{2,18},{18,2},{3,19},{19,3},{4,20},{20... | collective-permute-start | bytes 147464 | tf_op jit(solution)/shard_map/ppermute | solution.py:290
  37.8 0.4 collective-permute-start.10
  38.2 2.1 %collective-permute-done.13.refs_1_.refs_0_ = bf16[16,1536]{1,0:T(8,128)(2,1)S(1)} collective-permute-done((bf16[16,1536]{1,0:T(8,128)(2,1)S(1)}, bf16[16,1536]{1,0:T(8,128)(2,1)S(1)}, u32[]{:S(2)}, u32[]{:S(2)}) %collective-permute-start.13) | collective-permute-done | bytes 49184 | tf_op jit(solution)/shard_map/ppermute | solution.py:290
  40.4 0.1 collective-permute-start.18
  40.4 1.6 %collective-permute-start.14 = (bf16[16,1536]{1,0:T(8,128)(2,1)S(1)}, bf16[16,1536]{1,0:T(8,128)(2,1)S(1)}, u32[]{:S(2)}, u32[]{:S(2)}) collective-permute-start(bf16[16,1536]{1,0:T(8,128)(2,1)S(1)} %collective-permute-done.13.refs_1_.refs_0_), channel_id=1, source_target_pairs={{0,2},{1,3},{2,0},{3,1},{4,6},{5,7},{6,4},{7,5},{8,10},{9,11},{10,... | collective-permute-start | bytes 147464 | tf_op jit(solution)/shard_map/ppermute | solution.py:290
  42.0 1.2 %collective-permute-done.10.refs_2_ = bf16[2,16,2048]{2,1,0:T(8,128)(2,1)S(1)} collective-permute-done((bf16[2,16,2048]{2,1,0:T(8,128)(2,1)S(1)}, bf16[2,16,2048]{2,1,0:T(8,128)(2,1)S(1)}, u32[]{:S(2)}, u32[]{:S(2)}) %collective-permute-start.10) | collective-permute-done | bytes 131104 | tf_op jit(solution)/shard_map/ppermute | solution.py:290
  43.2 0.1 combine.3.refs_0_
  43.3 1.1 %collective-permute-start.11 = (bf16[16,2048]{1,0:T(8,128)(2,1)S(1)}, bf16[16,2048]{1,0:T(8,128)(2,1)S(1)}, u32[]{:S(2)}, u32[]{:S(2)}) collective-permute-start(bf16[16,2048]{1,0:T(8,128)(2,1)S(1)} %combine.3.refs_0_), channel_id=1, source_target_pairs={{0,2},{1,3},{2,0},{3,1},{4,6},{5,7},{6,4},{7,5},{8,10},{9,11},{10,... | collective-permute-start | bytes 196616 | tf_op jit(solution)/shard_map/ppermute | solution.py:290
  44.5 2.8 %down.3.refs_1_.refs_5_ = f32[64,2048]{1,0:T(8,128)S(1)} custom-call(s32[2]{0:T(128)S(1)} %pad_add_fusion.where, bf16[16,3072]{1,0:T(8,128)(2,1)S(1)} %get-tuple-element.30.refs_0_, bf16[16,3072]{1,0:T(8,128)(2,1)S(1)} %collective-permute-done.16.refs_0_.refs_1_, bf16[16,3072]{1,0:T(8,128)(2,1)S(1)} %collective-permute-done.17.refs_2_, ...), custom_call_target="tpu_custom_call" | custom-call | bytes 1024 | tf_op jit(solution)/shard_map/down/pallas_call | solution.py:270
  47.4 0.6 collective-permute-start.19
  47.9 0.9 %collective-permute-done.19.refs_3_ = bf16[16,1536]{1,0:T(8,128)(2,1)S(1)} collective-permute-done((bf16[16,1536]{1,0:T(8,128)(2,1)S(1)}, bf16[16,1536]{1,0:T(8,128)(2,1)S(1)}, u32[]{:S(2)}, u32[]{:S(2)}) %collective-permute-start.19) | collective-permute-done | bytes 49184 | tf_op jit(solution)/shard_map/ppermute | solution.py:290
  48.8 1.7 %down.4.refs_1_.refs_5_ = f32[64,2048]{1,0:T(8,128)S(1)} custom-call(s32[2]{0:T(128)S(1)} %pad_add_fusion.where, bf16[16,1536]{1,0:T(8,128)(2,1)S(1)} %collective-permute-done.13.refs_1_.refs_0_, bf16[16,1536]{1,0:T(8,128)(2,1)S(1)} %collective-permute-done.14.refs_0_.refs_1_, bf16[16,1536]{1,0:T(8,128)(2,1)S(1)} %collective-permute-done.15.refs_2_, ...), custom_call_target="tpu_custom_call" | custom-call | bytes 1024 | tf_op jit(solution)/shard_map/down/pallas_call | solution.py:270
  50.6 0.4 collective-permute-start.12
  51.0 0.2 collective-permute-start.20
  51.2 0.7 %collective-permute-done.12.refs_2_ = bf16[16,2048]{1,0:T(8,128)(2,1)S(1)} collective-permute-done((bf16[16,2048]{1,0:T(8,128)(2,1)S(1)}, bf16[16,2048]{1,0:T(8,128)(2,1)S(1)}, u32[]{:S(2)}, u32[]{:S(2)}) %collective-permute-start.12) | collective-permute-done | bytes 65568 | tf_op jit(solution)/shard_map/ppermute | solution.py:290
  51.9 0.4 collective-permute-done.20.refs_3_
  52.3 2.1 %down.5 = (bf16[16,2048]{1,0:T(8,128)(2,1)S(1)}, bf16[16,2048]{1,0:T(8,128)(2,1)S(1)}, bf16[16,2048]{1,0:T(8,128)(2,1)S(1)}, bf16[16,2048]{1,0:T(8,128)(2,1)S(1)}) custom-call(s32[2]{0:T(128)S(1)} %pad_add_fusion.where, bf16[16,2048]{1,0:T(8,128)(2,1)S(1)} %combine.3.refs_0_, bf16[16,2048]{1,0:T(8,128)(2,1)S(1)} %collective-permute-done.11.refs_0_.refs_1_, ...), custom_call_target="tpu_custom_call" | custom-call | bytes 1024 | tf_op jit(solution)/shard_map/down/pallas_call | solution.py:270
  54.5 3.1 %collective-permute-start.21 = (bf16[16,2048]{1,0:T(8,128)(2,1)S(1)}, bf16[16,2048]{1,0:T(8,128)(2,1)S(1)}, u32[]{:S(2)}, u32[]{:S(2)}) collective-permute-start(bf16[16,2048]{1,0:T(8,128)(2,1)S(1)} %get-tuple-element.32), channel_id=1, source_target_pairs={{0,12},{4,8},{8,4},{12,0},{1,13},{5,9},{9,5},{13,1},{2,14},{6,10},... | collective-permute-start | bytes 196616 | tf_op jit(solution)/shard_map/ppermute | solution.py:290
  57.6 1.3 %collective-permute-start.23 = (bf16[16,2048]{1,0:T(8,128)(2,1)S(1)}, bf16[16,2048]{1,0:T(8,128)(2,1)S(1)}, u32[]{:S(2)}, u32[]{:S(2)}) collective-permute-start(bf16[16,2048]{1,0:T(8,128)(2,1)S(1)} %get-tuple-element.34), channel_id=1, source_target_pairs={{0,4},{4,0},{8,12},{12,8},{1,5},{5,1},{9,13},{13,9},{2,6},{6,2},{1... | collective-permute-start | bytes 196616 | tf_op jit(solution)/shard_map/ppermute | solution.py:290
  58.9 2.4 %collective-permute-done.21 = bf16[16,2048]{1,0:T(8,128)(2,1)S(1)} collective-permute-done((bf16[16,2048]{1,0:T(8,128)(2,1)S(1)}, bf16[16,2048]{1,0:T(8,128)(2,1)S(1)}, u32[]{:S(2)}, u32[]{:S(2)}) %collective-permute-start.21) | collective-permute-done | bytes 65568 | tf_op jit(solution)/shard_map/ppermute | solution.py:290
  61.3 2.1 %collective-permute-done.22 = bf16[16,2048]{1,0:T(8,128)(2,1)S(1)} collective-permute-done((bf16[16,2048]{1,0:T(8,128)(2,1)S(1)}, bf16[16,2048]{1,0:T(8,128)(2,1)S(1)}, u32[]{:S(2)}, u32[]{:S(2)}) %collective-permute-start.22) | collective-permute-done | bytes 65568 | tf_op jit(solution)/shard_map/ppermute | solution.py:290
  63.3 0.1 collective-permute-done.23
  63.5 0.7 %add_convert_fusion = bf16[16,2048]{1,0:T(8,128)(2,1)} fusion(bf16[16,2048]{1,0:T(8,128)(2,1)S(1)} %collective-permute-done.23, bf16[16,2048]{1,0:T(8,128)(2,1)S(1)} %collective-permute-done.22, bf16[16,2048]{1,0:T(8,128)(2,1)S(1)} %collective-permute-done.21, bf16[16,2048]{1,0:T(8,128)(2,1)S(1)} %get-tuple-element.31), kind=kLoop, calls=%fused_computation | loop fusion | flops 262144 | bytes 327680 | tf_op jit(solution)/shard_map/convert_element_type | solution.py:337
  (35 shorter events, 0.2 us)
Async XLA Ops:
  0.0 12.8 %collective-permute-start.1 = (bf16[16,2048]{1,0:T(8,128)(2,1)}, bf16[16,2048]{1,0:T(8,128)(2,1)S(1)}, u32[]{:S(2)}, u32[]{:S(2)}) collective-permute-start(bf16[16,2048]{1,0:T(8,128)(2,1)} %tokens_ref.1), channel_id=1, source_target_pairs={{0,8},{4,12},{8,0},{12,4},{1,9},{5,13},{9,1},{13,5},{2,10},{6,14},... | collective-permute-start | bytes 196616 | tf_op jit(solution)/shard_map/ppermute | solution.py:290
  4.0 8.8 %collective-permute-start = (bf16[16,2048]{1,0:T(8,128)(2,1)}, bf16[16,2048]{1,0:T(8,128)(2,1)S(1)}, u32[]{:S(2)}, u32[]{:S(2)}) collective-permute-start(bf16[16,2048]{1,0:T(8,128)(2,1)} %tokens_ref.1), channel_id=1, source_target_pairs={{0,4},{4,0},{8,12},{12,8},{1,5},{5,1},{9,13},{13,9},{2,6},{6,2},{1... | collective-permute-start | bytes 196616 | tf_op jit(solution)/shard_map/ppermute | solution.py:290
  5.6 7.3 %collective-permute-start.3 = (bf16[16,2048]{1,0:T(8,128)(2,1)}, bf16[16,2048]{1,0:T(8,128)(2,1)S(1)}, u32[]{:S(2)}, u32[]{:S(2)}) collective-permute-start(bf16[16,2048]{1,0:T(8,128)(2,1)} %tokens_ref.1), channel_id=1, source_target_pairs={{0,16},{16,0},{1,17},{17,1},{2,18},{18,2},{3,19},{19,3},{4,20},{20... | collective-permute-start | bytes 196616 | tf_op jit(solution)/shard_map/ppermute | solution.py:290
  7.1 6.3 %collective-permute-start.2 = (bf16[16,2048]{1,0:T(8,128)(2,1)}, bf16[16,2048]{1,0:T(8,128)(2,1)S(1)}, u32[]{:S(2)}, u32[]{:S(2)}) collective-permute-start(bf16[16,2048]{1,0:T(8,128)(2,1)} %tokens_ref.1), channel_id=1, source_target_pairs={{0,12},{4,8},{8,4},{12,0},{1,13},{5,9},{9,5},{13,1},{2,14},{6,10},... | collective-permute-start | bytes 196616 | tf_op jit(solution)/shard_map/ppermute | solution.py:290
  13.4 6.5 %collective-permute-start.5 = (bf16[48,2048]{1,0:T(8,128)(2,1)S(1)}, bf16[48,2048]{1,0:T(8,128)(2,1)S(1)}, u32[]{:S(2)}, u32[]{:S(2)}) collective-permute-start(bf16[48,2048]{1,0:T(8,128)(2,1)S(1)} %join.4.refs_1_), channel_id=1, source_target_pairs={{0,16},{16,0},{1,17},{17,1},{2,18},{18,2},{3,19},{19,3},{4,20},{20... | collective-permute-start | bytes 589832 | tf_op jit(solution)/shard_map/ppermute | solution.py:290
  22.4 1.8 %collective-permute-start.6 = (bf16[2,64,1536]{2,1,0:T(8,128)(2,1)S(1)}, bf16[2,64,1536]{2,1,0:T(8,128)(2,1)S(1)}, u32[]{:S(2)}, u32[]{:S(2)}) collective-permute-start(bf16[2,64,1536]{2,1,0:T(8,128)(2,1)S(1)} %get-tuple-element.26), channel_id=1, source_target_pairs={{0,1},{1,0},{2,3},{3,2},{4,5},{5,4},{6,7},{7,6},{8,9},{9,8},{10,11... | collective-permute-start | bytes 1179656 | tf_op jit(solution)/shard_map/ppermute | solution.py:290
  22.5 3.3 %collective-permute-start.4 = (bf16[2,32,1536]{2,1,0:T(8,128)(2,1)S(1)}, bf16[2,32,1536]{2,1,0:T(8,128)(2,1)S(1)}, u32[]{:S(2)}, u32[]{:S(2)}) collective-permute-start(bf16[2,32,1536]{2,1,0:T(8,128)(2,1)S(1)} %get-tuple-element.22), channel_id=1, source_target_pairs={{0,1},{1,0},{2,3},{3,2},{4,5},{5,4},{6,7},{7,6},{8,9},{9,8},{10,11... | collective-permute-start | bytes 589832 | tf_op jit(solution)/shard_map/ppermute | solution.py:290
  24.3 9.9 %collective-permute-start.8 = (bf16[2,32,1536]{2,1,0:T(8,128)(2,1)S(1)}, bf16[2,32,1536]{2,1,0:T(8,128)(2,1)S(1)}, u32[]{:S(2)}, u32[]{:S(2)}) collective-permute-start(bf16[2,32,1536]{2,1,0:T(8,128)(2,1)S(1)} %pair_sum.4.refs_5_), channel_id=1, source_target_pairs={{0,2},{1,3},{2,0},{3,1},{4,6},{5,7},{6,4},{7,5},{8,10},{9,11},{10,... | collective-permute-start | bytes 589832 | tf_op jit(solution)/shard_map/ppermute | solution.py:290
  25.8 18.6 %slice-start = ((s8[27262976]{0:T(1024)(128)(4,1)}), s8[4194304]{0:T(1024)(128)(4,1)S(1)}, s32[]{:S(2)}) async-start(s8[27262976]{0:T(1024)(128)(4,1)} %bitcast.2), calls=%async_computation | async-start | bytes 8388608
  25.9 18.6 %slice-start.1 = ((s8[27262976]{0:T(1024)(128)(4,1)}), s8[4194304]{0:T(1024)(128)(4,1)S(1)}, s32[]{:S(2)}) async-start(s8[27262976]{0:T(1024)(128)(4,1)} %bitcast.2), calls=%async_computation.1 | async-start | bytes 8388608
  25.9 18.6 %slice-start.2 = ((s8[27262976]{0:T(1024)(128)(4,1)}), s8[4194304]{0:T(1024)(128)(4,1)S(1)}, s32[]{:S(2)}) async-start(s8[27262976]{0:T(1024)(128)(4,1)} %bitcast.2), calls=%async_computation.2 | async-start | bytes 8388608
  25.9 18.6 %slice-start.3 = ((s8[27262976]{0:T(1024)(128)(4,1)}), s8[4194304]{0:T(1024)(128)(4,1)S(1)}, s32[]{:S(2)}) async-start(s8[27262976]{0:T(1024)(128)(4,1)} %bitcast.2), calls=%async_computation.3 | async-start | bytes 8388608
  25.9 18.6 %slice-start.4 = ((s8[27262976]{0:T(1024)(128)(4,1)}), s8[4194304]{0:T(1024)(128)(4,1)S(1)}, s32[]{:S(2)}) async-start(s8[27262976]{0:T(1024)(128)(4,1)} %bitcast.2), calls=%async_computation.4 | async-start | bytes 8388608
  25.9 18.6 %slice-start.5 = ((s8[27262976]{0:T(1024)(128)(4,1)}), s8[4194304]{0:T(1024)(128)(4,1)S(1)}, s32[]{:S(2)}) async-start(s8[27262976]{0:T(1024)(128)(4,1)} %bitcast.2), calls=%async_computation.5 | async-start | bytes 8388608
  25.9 18.6 %slice-start.6 = ((s8[27262976]{0:T(1024)(128)(4,1)}), s8[2097152]{0:T(1024)(128)(4,1)S(1)}, s32[]{:S(2)}) async-start(s8[27262976]{0:T(1024)(128)(4,1)} %bitcast.2), calls=%async_computation.6 | async-start | bytes 4194304
  25.9 8.3 %collective-permute-start.7 = (bf16[2,16,1536]{2,1,0:T(8,128)(2,1)S(1)}, bf16[2,16,1536]{2,1,0:T(8,128)(2,1)S(1)}, u32[]{:S(2)}, u32[]{:S(2)}) collective-permute-start(bf16[2,16,1536]{2,1,0:T(8,128)(2,1)S(1)} %pair_sum.3.refs_4_), channel_id=1, source_target_pairs={{0,2},{1,3},{2,0},{3,1},{4,6},{5,7},{6,4},{7,5},{8,10},{9,11},{10,... | collective-permute-start | bytes 294920 | tf_op jit(solution)/shard_map/ppermute | solution.py:290
  34.2 3.6 %collective-permute-start.9 = (bf16[2,32,2048]{2,1,0:T(8,128)(2,1)S(1)}, bf16[2,32,2048]{2,1,0:T(8,128)(2,1)S(1)}, u32[]{:S(2)}, u32[]{:S(2)}) collective-permute-start(bf16[2,32,2048]{2,1,0:T(8,128)(2,1)S(1)} %later.1), channel_id=1, source_target_pairs={{0,1},{1,0},{2,3},{3,2},{4,5},{5,4},{6,7},{7,6},{8,9},{9,8},{10,11... | collective-permute-start | bytes 786440 | tf_op jit(solution)/shard_map/ppermute | solution.py:290
  34.5 5.8 %collective-permute-start.16 = (bf16[16,3072]{1,0:T(8,128)(2,1)S(1)}, bf16[16,3072]{1,0:T(8,128)(2,1)S(1)}, u32[]{:S(2)}, u32[]{:S(2)}) collective-permute-start(bf16[16,3072]{1,0:T(8,128)(2,1)S(1)} %get-tuple-element.30.refs_0_), channel_id=1, source_target_pairs={{0,2},{1,3},{2,0},{3,1},{4,6},{5,7},{6,4},{7,5},{8,10},{9,11},{10,... | collective-permute-start | bytes 294920 | tf_op jit(solution)/shard_map/ppermute | solution.py:290
  36.3 4.1 %collective-permute-start.13 = (bf16[16,1536]{1,0:T(8,128)(2,1)S(1)}, bf16[16,1536]{1,0:T(8,128)(2,1)S(1)}, u32[]{:S(2)}, u32[]{:S(2)}) collective-permute-start(bf16[16,1536]{1,0:T(8,128)(2,1)S(1)} %get-tuple-element.29), channel_id=1, source_target_pairs={{0,16},{16,0},{1,17},{17,1},{2,18},{18,2},{3,19},{19,3},{4,20},{20... | collective-permute-start | bytes 147464 | tf_op jit(solution)/shard_map/ppermute | solution.py:290
  37.8 5.4 %collective-permute-start.10 = (bf16[2,16,2048]{2,1,0:T(8,128)(2,1)S(1)}, bf16[2,16,2048]{2,1,0:T(8,128)(2,1)S(1)}, u32[]{:S(2)}, u32[]{:S(2)}) collective-permute-start(bf16[2,16,2048]{2,1,0:T(8,128)(2,1)S(1)} %pair_sum.5), channel_id=1, source_target_pairs={{0,2},{1,3},{2,0},{3,1},{4,6},{5,7},{6,4},{7,5},{8,10},{9,11},{10,... | collective-permute-start | bytes 393224 | tf_op jit(solution)/shard_map/ppermute | solution.py:290
  38.2 6.2 %collective-permute-start.17 = (bf16[16,3072]{1,0:T(8,128)(2,1)S(1)}, bf16[16,3072]{1,0:T(8,128)(2,1)S(1)}, u32[]{:S(2)}, u32[]{:S(2)}) collective-permute-start(bf16[16,3072]{1,0:T(8,128)(2,1)S(1)} %get-tuple-element.30.refs_0_), channel_id=1, source_target_pairs={{0,1},{1,0},{2,3},{3,2},{4,5},{5,4},{6,7},{7,6},{8,9},{9,8},{10,11... | collective-permute-start | bytes 294920 | tf_op jit(solution)/shard_map/ppermute | solution.py:290
  40.4 4.1 %collective-permute-start.18 = (bf16[16,3072]{1,0:T(8,128)(2,1)S(1)}, bf16[16,3072]{1,0:T(8,128)(2,1)S(1)}, u32[]{:S(2)}, u32[]{:S(2)}) collective-permute-start(bf16[16,3072]{1,0:T(8,128)(2,1)S(1)} %join.5), channel_id=1, source_target_pairs={{0,1},{1,0},{2,3},{3,2},{4,5},{5,4},{6,7},{7,6},{8,9},{9,8},{10,11... | collective-permute-start | bytes 294920 | tf_op jit(solution)/shard_map/ppermute | solution.py:290
  40.4 6.9 %collective-permute-start.14 = (bf16[16,1536]{1,0:T(8,128)(2,1)S(1)}, bf16[16,1536]{1,0:T(8,128)(2,1)S(1)}, u32[]{:S(2)}, u32[]{:S(2)}) collective-permute-start(bf16[16,1536]{1,0:T(8,128)(2,1)S(1)} %collective-permute-done.13.refs_1_.refs_0_), channel_id=1, source_target_pairs={{0,2},{1,3},{2,0},{3,1},{4,6},{5,7},{6,4},{7,5},{8,10},{9,11},{10,... | collective-permute-start | bytes 147464 | tf_op jit(solution)/shard_map/ppermute | solution.py:290
  43.3 7.7 %collective-permute-start.11 = (bf16[16,2048]{1,0:T(8,128)(2,1)S(1)}, bf16[16,2048]{1,0:T(8,128)(2,1)S(1)}, u32[]{:S(2)}, u32[]{:S(2)}) collective-permute-start(bf16[16,2048]{1,0:T(8,128)(2,1)S(1)} %combine.3.refs_0_), channel_id=1, source_target_pairs={{0,2},{1,3},{2,0},{3,1},{4,6},{5,7},{6,4},{7,5},{8,10},{9,11},{10,... | collective-permute-start | bytes 196616 | tf_op jit(solution)/shard_map/ppermute | solution.py:290
  44.4 3.5 %collective-permute-start.15 = (bf16[16,1536]{1,0:T(8,128)(2,1)S(1)}, bf16[16,1536]{1,0:T(8,128)(2,1)S(1)}, u32[]{:S(2)}, u32[]{:S(2)}) collective-permute-start(bf16[16,1536]{1,0:T(8,128)(2,1)S(1)} %collective-permute-done.13.refs_1_.refs_0_), channel_id=1, source_target_pairs={{0,1},{1,0},{2,3},{3,2},{4,5},{5,4},{6,7},{7,6},{8,9},{9,8},{10,11... | collective-permute-start | bytes 147464 | tf_op jit(solution)/shard_map/ppermute | solution.py:290
  47.4 1.4 %collective-permute-start.19 = (bf16[16,1536]{1,0:T(8,128)(2,1)S(1)}, bf16[16,1536]{1,0:T(8,128)(2,1)S(1)}, u32[]{:S(2)}, u32[]{:S(2)}) collective-permute-start(bf16[16,1536]{1,0:T(8,128)(2,1)S(1)} %join.6), channel_id=1, source_target_pairs={{0,1},{1,0},{2,3},{3,2},{4,5},{5,4},{6,7},{7,6},{8,9},{9,8},{10,11... | collective-permute-start | bytes 147464 | tf_op jit(solution)/shard_map/ppermute | solution.py:290
  50.6 1.3 %collective-permute-start.12 = (bf16[16,2048]{1,0:T(8,128)(2,1)S(1)}, bf16[16,2048]{1,0:T(8,128)(2,1)S(1)}, u32[]{:S(2)}, u32[]{:S(2)}) collective-permute-start(bf16[16,2048]{1,0:T(8,128)(2,1)S(1)} %combine.3.refs_0_), channel_id=1, source_target_pairs={{0,1},{1,0},{2,3},{3,2},{4,5},{5,4},{6,7},{7,6},{8,9},{9,8},{10,11... | collective-permute-start | bytes 196616 | tf_op jit(solution)/shard_map/ppermute | solution.py:290
  51.0 1.3 %collective-permute-start.20 = (bf16[16,2048]{1,0:T(8,128)(2,1)S(1)}, bf16[16,2048]{1,0:T(8,128)(2,1)S(1)}, u32[]{:S(2)}, u32[]{:S(2)}) collective-permute-start(bf16[16,2048]{1,0:T(8,128)(2,1)S(1)} %join.7), channel_id=1, source_target_pairs={{0,1},{1,0},{2,3},{3,2},{4,5},{5,4},{6,7},{7,6},{8,9},{9,8},{10,11... | collective-permute-start | bytes 196616 | tf_op jit(solution)/shard_map/ppermute | solution.py:290
  54.5 6.8 %collective-permute-start.21 = (bf16[16,2048]{1,0:T(8,128)(2,1)S(1)}, bf16[16,2048]{1,0:T(8,128)(2,1)S(1)}, u32[]{:S(2)}, u32[]{:S(2)}) collective-permute-start(bf16[16,2048]{1,0:T(8,128)(2,1)S(1)} %get-tuple-element.32), channel_id=1, source_target_pairs={{0,12},{4,8},{8,4},{12,0},{1,13},{5,9},{9,5},{13,1},{2,14},{6,10},... | collective-permute-start | bytes 196616 | tf_op jit(solution)/shard_map/ppermute | solution.py:290
  57.6 5.7 %collective-permute-start.22 = (bf16[16,2048]{1,0:T(8,128)(2,1)S(1)}, bf16[16,2048]{1,0:T(8,128)(2,1)S(1)}, u32[]{:S(2)}, u32[]{:S(2)}) collective-permute-start(bf16[16,2048]{1,0:T(8,128)(2,1)S(1)} %get-tuple-element.33), channel_id=1, source_target_pairs={{0,8},{4,12},{8,0},{12,4},{1,9},{5,13},{9,1},{13,5},{2,10},{6,14},... | collective-permute-start | bytes 196616 | tf_op jit(solution)/shard_map/ppermute | solution.py:290
  57.6 5.9 %collective-permute-start.23 = (bf16[16,2048]{1,0:T(8,128)(2,1)S(1)}, bf16[16,2048]{1,0:T(8,128)(2,1)S(1)}, u32[]{:S(2)}, u32[]{:S(2)}) collective-permute-start(bf16[16,2048]{1,0:T(8,128)(2,1)S(1)} %get-tuple-element.34), channel_id=1, source_target_pairs={{0,4},{4,0},{8,12},{12,8},{1,5},{5,1},{9,13},{13,9},{2,6},{6,2},{1... | collective-permute-start | bytes 196616 | tf_op jit(solution)/shard_map/ppermute | solution.py:290

commit v12 on v7

--- a/solution.py
+++ b/solution.py
@@ -160,54 +160,74 @@
     )(where, *arrays, *weights, *behind)
 
 
-def pair_sum_kernel(mine_ref, got_ref, *refs):
-    out_ref = refs[-1]
-    rows = out_ref.shape[1]
+def pair_sum_kernel(n_outs, mine_ref, got_ref, *refs):
+    outs = refs[-n_outs:]
+    rows = mine_ref.shape[1] // 2
     for k in range(2):
         total = mine_ref[k, rows:].astype(jnp.float32) + got_ref[k, rows:].astype(jnp.float32)
-        out_ref[k] = total.astype(out_ref.dtype)
-
-
-def pair_sum(mine, got, behind):
+        if n_outs == 1:
+            outs[0][k] = total.astype(jnp.bfloat16)
+        else:
+            outs[k][...] = total.astype(jnp.bfloat16)
+
+
+def pair_sum(mine, got, apart, behind):
     _, rows, width = mine.shape
-    return pl.pallas_call(
-        pair_sum_kernel,
+    shapes = [(rows // 2, width)] * 2 if apart else [(2, rows // 2, width)]
+    return pl.pallas_call(
+        functools.partial(pair_sum_kernel, len(shapes)),
         in_specs=[spec(pltpu.VMEM)] * 2 + [spec(pl.ANY)] * len(behind),
-        out_specs=spec(pltpu.VMEM),
-        out_shape=jax.ShapeDtypeStruct((2, rows // 2, width), mine.dtype),
+        out_specs=[spec(pltpu.VMEM)] * len(shapes),
+        out_shape=[jax.ShapeDtypeStruct(x, mine.dtype) for x in shapes],
         compiler_params=params(2),
         cost_estimate=COST,
         name="pair_sum",
     )(mine, got, *behind)
 
 
-def mark_kernel(_, out_ref):
-    out_ref[...] = jnp.zeros_like(out_ref)
-
-
-def mark(array):
-    return pl.pallas_call(
-        mark_kernel,
-        in_specs=[spec(pl.ANY)],
+def later_kernel(array_ref, *refs):
+    refs[-1][...] = array_ref[...]
+
+
+def later(array, behind):
+    return pl.pallas_call(
+        later_kernel,
+        in_specs=[spec(pltpu.VMEM)] + [spec(pl.ANY)] * len(behind),
         out_specs=spec(pltpu.VMEM),
-        out_shape=jax.ShapeDtypeStruct((8, 128), jnp.float32),
+        out_shape=jax.ShapeDtypeStruct(array.shape, array.dtype),
         compiler_params=params(1),
         cost_estimate=COST,
-        name="mark",
-    )(array)
-
-
-def combine_kernel(n_left, n_outs, mine_ref, got_ref, chip_ref, *refs):
-    outs = refs[-n_outs:]
-    rows, first = chip_ref.shape[1], 0
+        name="later",
+    )(array, *behind)
+
+
+def add_kernel(left_ref, right_ref, out_ref):
+    out_ref[...] = left_ref[...].astype(jnp.float32) + right_ref[...].astype(jnp.float32)
+
+
+def add(left, right):
+    return pl.pallas_call(
+        add_kernel,
+        in_specs=[spec(pltpu.VMEM)] * 2,
+        out_specs=spec(pltpu.VMEM),
+        out_shape=jax.ShapeDtypeStruct(left.shape, jnp.float32),
+        compiler_params=params(1),
+        cost_estimate=COST,
+        name="add",
+    )(left, right)
+
+
+def combine_kernel(n_chips, n_left, n_outs, mine_ref, got_ref, *refs):
+    chips, refs, outs = refs[:n_chips], refs[n_chips:], refs[-n_outs:]
+    rows, first = mine_ref.shape[1] // 2, 0
     for left in refs[:n_left]:
         first = left.shape[1]
         outs[0][:, :first] = left[...]
-    for a, b in pieces_of(chip_ref.shape[2], TILE):
+    for a, b in pieces_of(mine_ref.shape[2], TILE):
         gate, up = (
             mine_ref[k, :rows, a:b].astype(jnp.float32)
             + got_ref[k, :rows, a:b].astype(jnp.float32)
-            + chip_ref[k, :, a:b].astype(jnp.float32)
+            + (chips[k][:, a:b] if n_chips == 2 else chips[0][k, :, a:b]).astype(jnp.float32)
             for k in range(2)
         )
         hidden = (gate / (1 + jnp.exp(-gate)) * up).astype(jnp.bfloat16)
@@ -215,19 +235,19 @@
             out[:, first + a : first + b] = hidden[i * ROWS : (i + 1) * ROWS]
 
 
-def combine(mine, got, from_chip, left, behind):
-    _, rows, width = from_chip.shape
-    n_outs = rows // ROWS
+def combine(mine, got, from_chips, left, behind):
+    _, rows, width = mine.shape
+    n_outs = rows // (2 * ROWS)
     width += sum(x.shape[1] for x in left)
     return pl.pallas_call(
-        functools.partial(combine_kernel, len(left), n_outs),
-        in_specs=[spec(pltpu.VMEM)] * (3 + len(left)) + [spec(pl.ANY)] * len(behind),
+        functools.partial(combine_kernel, len(from_chips), len(left), n_outs),
+        in_specs=[spec(pltpu.VMEM)] * (2 + len(from_chips) + len(left)) + [spec(pl.ANY)] * len(behind),
         out_specs=[spec(pltpu.VMEM)] * n_outs,
         out_shape=[jax.ShapeDtypeStruct((ROWS, width), jnp.bfloat16)] * n_outs,
         compiler_params=params(2),
         cost_estimate=COST,
         name="combine",
-    )(mine, got, from_chip, *left, *behind)
+    )(mine, got, *from_chips, *left, *behind)
 
 
 def down_kernel(n_pieces, has_acc, last, segments, where, *refs):
@@ -301,28 +321,27 @@
     weights = [w for fetched in early for w in fetched[:2]]
     mine, theirs = gate_up(where, [own, near, far_own, far], weights, [], [])
     got = swap(theirs, "wid", 1)
-    to_chip = pair_sum(mine, got, [])
+    (to_chip,) = pair_sum(mine, got, False, [])
     from_chip = swap(to_chip, "wid", 2)
     segments = [(bounds[2], widths[2]), (half + bounds[2], widths[2])]
     last_mine, theirs = gate_up(where, [own, near], [gate_weight, up_weight], segments, [to_chip])
     last_got = swap(theirs, "wid", 1)
-    last_to_chip = pair_sum(last_mine, last_got, [mark(from_chip)])
-    last_from_chip = swap(last_to_chip, "wid", 2)
-
-    keep, give = combine(mine, got, from_chip, [], [])
+
+    keep, give = combine(mine, got, [from_chip], [], [])
     far_columns = swap(give, "rep", 1)
+    last_from_chip = [swap(x, "wid", 2) for x in pair_sum(last_mine, last_got, True, [give])]
     (rest,) = combine(last_mine, last_got, last_from_chip, [far_columns], [])
     rest_segments = [(-1, half, bounds[2])] + [(0, start, width) for start, width in segments]
-    acc, behind = None, []
+    acc, behind = None, [rest]
     for hidden, parts in ((keep, [(1, 0, bounds[2])]), (rest, rest_segments)):
         other = swap(hidden, "wid", 2)
-        crossed = swap(join([hidden, other], behind), "wid", 1)
-        acc = down(where, [hidden, other, crossed], down_weight, acc, parts, bool(behind))
+        pieces = [hidden, other, swap(hidden, "wid", 1), swap(join([other], behind), "wid", 1)]
+        acc = down(where, pieces, down_weight, acc, parts, hidden is rest)
         behind = [acc]
 
-    mixed = acc[0].astype(f32)
-    for d in (3, 2, 1):
-        mixed = mixed + swap(acc[d], "hid", d).astype(f32)
+    via = (acc[2].astype(f32) + swap(acc[3], "hid", 1).astype(f32)).astype(bf16)
+    mixed = add(acc[0], swap(via, "hid", 2))
+    mixed = mixed + swap(later(acc[1], [via]), "hid", 1).astype(f32)
     return mixed.astype(bf16)
 
 

time: 61.4 us -> 63.7 us (1.037)
  starting transfers between devices: 20 us -> 22.4 us
    ppermute x17 -> x20, starting transfers between devices: 20 us -> 22.4 us  [swap(): return lax.ppermute(x, axis, [(i, i ^ step) for i in range(n)])]
    ppermute x17 -> x20, waiting for transfers between devices: 13.3 us -> 13.2 us  [swap(): return lax.ppermute(x, axis, [(i, i ^ step) for i in range(n)])]
  transfers between devices with their start and end apart: 17 -> 20, of which waited for: 8 -> 11; matrix products, arithmetic and copies ran while one was open for 0% -> 0% of each run, Pallas kernels for 32% -> 31%
where the time goes in v12:
time: 63.7 us; the launch traced here: 63.5 us
  Pallas kernels  26.9 us (42%)
  starting transfers between devices  22.4 us (35%)
  waiting for transfers between devices  13.2 us (21%)
  other arithmetic  0.74 us (1%)
    ppermute x20, starting transfers between devices, swap(): return lax.ppermute(x, axis, [(i, i ^ step) for i in range(n)])  22.4 us
    ppermute x20, waiting for transfers between devices, swap(): return lax.ppermute(x, axis, [(i, i ^ step) for i in range(n)])  13.2 us
    pallas_call x2, Pallas kernels, fetch(): pl.pallas_call(functools.partial(fetch_kernel, first), in_specs=[spec(plt...  10.2 us
    pallas_call x2, Pallas kernels, gate_up(): pl.pallas_call(functools.partial(gate_up_kernel, len(arrays), len(weights...  10.2 us
    pallas_call x2, Pallas kernels, down(): pl.pallas_call(functools.partial(down_kernel, len(pieces), prev is not No...  6.06 us
  transfers between devices with their start and end apart: 20, of which 11 were waited for; matrix products, arithmetic and copies ran while one was open for 0% of the time, Pallas kernels for 31%

profile of v12, /device:TPU:0, one launch (start us, length us, event | category | flops | bytes accessed | tf_op | source)
XLA Modules:
  0.0 63.5 jit_solution(17251259591433625744)
XLA Ops:
  0.0 5.0 %collective-permute-start.2 = (bf16[16,2048]{1,0:T(8,128)(2,1)}, bf16[16,2048]{1,0:T(8,128)(2,1)S(1)}, u32[]{:S(2)}, u32[]{:S(2)}) collective-permute-start(bf16[16,2048]{1,0:T(8,128)(2,1)} %tokens_ref.3), channel_id=1, source_target_pairs={{0,12},{4,8},{8,4},{12,0},{1,13},{5,9},{9,5},{13,1},{2,14},{6,10},... | collective-permute-start | bytes 196616 | tf_op jit(solution)/shard_map/ppermute | solution.py:304
  5.0 0.0 collective-permute-start.1
  5.1 0.6 collective-permute-start
  5.6 1.7 %collective-permute-start.3 = (bf16[16,2048]{1,0:T(8,128)(2,1)}, bf16[16,2048]{1,0:T(8,128)(2,1)S(1)}, u32[]{:S(2)}, u32[]{:S(2)}) collective-permute-start(bf16[16,2048]{1,0:T(8,128)(2,1)} %tokens_ref.3), channel_id=1, source_target_pairs={{0,16},{16,0},{1,17},{17,1},{2,18},{18,2},{3,19},{19,3},{4,20},{20... | collective-permute-start | bytes 196616 | tf_op jit(solution)/shard_map/ppermute | solution.py:304
  7.4 0.1 pad_add_fusion.where
  7.4 4.8 %fetch.2 = (bf16[2048,1280]{1,0:T(8,128)(2,1)S(1)}, bf16[2048,1280]{1,0:T(8,128)(2,1)S(1)}, bf16[16,2048]{1,0:T(8,128)(2,1)S(1)}) custom-call(s32[2]{0:T(128)S(1)} %pad_add_fusion.where, bf16[2048,6656]{1,0:T(8,128)(2,1)} %refs_2_.1, bf16[2048,6656]{1,0:T(8,128)(2,1)} %refs_3_.1, bf16[16,2048]{1,0:T(8,128)(2,1)} %tokens_ref.3), custom_call_target="tpu_custom_call" | custom-call | bytes 1024 | tf_op jit(solution)/shard_map/fetch/pallas_call | solution.py:73
  12.3 0.0 collective-permute-done.1.refs_1_
  12.3 0.0 collective-permute-done.refs_0_
  12.3 0.4 collective-permute-start.4
  12.7 5.4 %fetch.3 = (bf16[2048,1280]{1,0:T(8,128)(2,1)S(1)}, bf16[2048,1280]{1,0:T(8,128)(2,1)S(1)}, bf16[16,2048]{1,0:T(8,128)(2,1)}) custom-call(s32[2]{0:T(128)S(1)} %pad_add_fusion.where, bf16[2048,6656]{1,0:T(8,128)(2,1)} %refs_2_.1, bf16[2048,6656]{1,0:T(8,128)(2,1)} %refs_3_.1, bf16[16,2048]{1,0:T(8,128)(2,1)} %tokens_ref.3), custom_call_target="tpu_custom_call" | custom-call | bytes 1024 | tf_op jit(solution)/shard_map/fetch/pallas_call | solution.py:73
  18.1 0.0 collective-permute-done.4.refs_3_
  18.1 3.6 %gate_up.2 = (bf16[2,64,2560]{2,1,0:T(8,128)(2,1)S(1)}, bf16[2,64,2560]{2,1,0:T(8,128)(2,1)S(1)}) custom-call(s32[2]{0:T(128)S(1)} %pad_add_fusion.where, bf16[16,2048]{1,0:T(8,128)(2,1)S(1)} %get-tuple-element.22.refs_3_.refs_0_, bf16[48,2048]{1,0:T(8,128)(2,1)S(1)} %join.3.refs_1_, bf16[16,2048]{1,0:T(8,128)(2,1)S(1)} %collective-permute-done.3.refs_4_.refs_2_, ...), custom_call_target="tpu_custom_call" | custom-call | bytes 1024 | tf_op jit(solution)/shard_map/gate_up/pallas_call | solution.py:148
  21.7 0.1 collective-permute-start.5
  21.8 2.1 %collective-permute-done.5.got_ref = bf16[2,64,2560]{2,1,0:T(8,128)(2,1)S(1)} collective-permute-done((bf16[2,64,2560]{2,1,0:T(8,128)(2,1)S(1)}, bf16[2,64,2560]{2,1,0:T(8,128)(2,1)S(1)}, u32[]{:S(2)}, u32[]{:S(2)}) %collective-permute-start.5) | collective-permute-done | bytes 655392 | tf_op jit(solution)/shard_map/ppermute | solution.py:304
  23.9 0.1 pair_sum.2.refs_4_
  23.9 0.0 slice-start.1
  24.0 0.0 slice-start.2
  24.0 0.0 slice-start.4
  24.0 0.0 slice-start.5
  24.0 1.8 %collective-permute-start.7 = (bf16[2,32,2560]{2,1,0:T(8,128)(2,1)S(1)}, bf16[2,32,2560]{2,1,0:T(8,128)(2,1)S(1)}, u32[]{:S(2)}, u32[]{:S(2)}) collective-permute-start(bf16[2,32,2560]{2,1,0:T(8,128)(2,1)S(1)} %pair_sum.2.refs_4_), channel_id=1, source_target_pairs={{0,2},{1,3},{2,0},{3,1},{4,6},{5,7},{6,4},{7,5},{8,10},{9,11},{10,... | collective-permute-start | bytes 983048 | tf_op jit(solution)/shard_map/ppermute | solution.py:304
  25.8 6.6 %gate_up.3 = (bf16[2,32,1536]{2,1,0:T(8,128)(2,1)S(1)}, bf16[2,32,1536]{2,1,0:T(8,128)(2,1)S(1)}) custom-call(s32[2]{0:T(128)S(1)} %pad_add_fusion.where, bf16[16,2048]{1,0:T(8,128)(2,1)S(1)} %get-tuple-element.22.refs_3_.refs_0_, bf16[48,2048]{1,0:T(8,128)(2,1)S(1)} %join.3.refs_1_, bf16[2048,6656]{1,0:T(8,128)(2,1)} %refs_2_.1, ...), custom_call_target="tpu_custom_call" | custom-call | bytes 1024 | tf_op jit(solution)/shard_map/gate_up/pallas_call | solution.py:148
  32.4 0.1 collective-permute-start.6
  32.5 1.3 %collective-permute-done.7.refs_0_ = bf16[2,32,2560]{2,1,0:T(8,128)(2,1)S(1)} collective-permute-done((bf16[2,32,2560]{2,1,0:T(8,128)(2,1)S(1)}, bf16[2,32,2560]{2,1,0:T(8,128)(2,1)S(1)}, u32[]{:S(2)}, u32[]{:S(2)}) %collective-permute-start.7) | collective-permute-done | bytes 327712 | tf_op jit(solution)/shard_map/ppermute | solution.py:304
  33.8 0.2 combine.2
  34.0 1.8 %collective-permute-start.10 = (bf16[16,2560]{1,0:T(8,128)(2,1)S(1)}, bf16[16,2560]{1,0:T(8,128)(2,1)S(1)}, u32[]{:S(2)}, u32[]{:S(2)}) collective-permute-start(bf16[16,2560]{1,0:T(8,128)(2,1)S(1)} %get-tuple-element.31.refs_0_), channel_id=1, source_target_pairs={{0,16},{16,0},{1,17},{17,1},{2,18},{18,2},{3,19},{19,3},{4,20},{20... | collective-permute-start | bytes 245768 | tf_op jit(solution)/shard_map/ppermute | solution.py:304
  35.9 1.6 %collective-permute-start.8 = (bf16[16,1536]{1,0:T(8,128)(2,1)S(1)}, bf16[16,1536]{1,0:T(8,128)(2,1)S(1)}, u32[]{:S(2)}, u32[]{:S(2)}) collective-permute-start(bf16[16,1536]{1,0:T(8,128)(2,1)S(1)} %get-tuple-element.32), channel_id=1, source_target_pairs={{0,2},{1,3},{2,0},{3,1},{4,6},{5,7},{6,4},{7,5},{8,10},{9,11},{10,... | collective-permute-start | bytes 147464 | tf_op jit(solution)/shard_map/ppermute | solution.py:304
  37.4 0.5 collective-permute-start.9
  38.0 1.5 %collective-permute-start.13 = (bf16[16,2560]{1,0:T(8,128)(2,1)S(1)}, bf16[16,2560]{1,0:T(8,128)(2,1)S(1)}, u32[]{:S(2)}, u32[]{:S(2)}) collective-permute-start(bf16[16,2560]{1,0:T(8,128)(2,1)S(1)} %get-tuple-element.34.refs_0_), channel_id=1, source_target_pairs={{0,2},{1,3},{2,0},{3,1},{4,6},{5,7},{6,4},{7,5},{8,10},{9,11},{10,... | collective-permute-start | bytes 245768 | tf_op jit(solution)/shard_map/ppermute | solution.py:304
  39.4 1.1 %collective-permute-done.8.refs_0_ = bf16[16,1536]{1,0:T(8,128)(2,1)S(1)} collective-permute-done((bf16[16,1536]{1,0:T(8,128)(2,1)S(1)}, bf16[16,1536]{1,0:T(8,128)(2,1)S(1)}, u32[]{:S(2)}, u32[]{:S(2)}) %collective-permute-start.8) | collective-permute-done | bytes 49184 | tf_op jit(solution)/shard_map/ppermute | solution.py:304
  40.5 1.0 %collective-permute-done.9.refs_1_ = bf16[16,1536]{1,0:T(8,128)(2,1)S(1)} collective-permute-done((bf16[16,1536]{1,0:T(8,128)(2,1)S(1)}, bf16[16,1536]{1,0:T(8,128)(2,1)S(1)}, u32[]{:S(2)}, u32[]{:S(2)}) %collective-permute-start.9) | collective-permute-done | bytes 49184 | tf_op jit(solution)/shard_map/ppermute | solution.py:304
  41.5 0.1 combine.3.refs_1_.refs_0_
  41.6 1.0 %collective-permute-start.11 = (bf16[16,4096]{1,0:T(8,128)(2,1)S(1)}, bf16[16,4096]{1,0:T(8,128)(2,1)S(1)}, u32[]{:S(2)}, u32[]{:S(2)}) collective-permute-start(bf16[16,4096]{1,0:T(8,128)(2,1)S(1)} %combine.3.refs_1_.refs_0_), channel_id=1, source_target_pairs={{0,2},{1,3},{2,0},{3,1},{4,6},{5,7},{6,4},{7,5},{8,10},{9,11},{10,... | collective-permute-start | bytes 393224 | tf_op jit(solution)/shard_map/ppermute | solution.py:304
  42.6 0.3 collective-permute-done.13.refs_0_.refs_1_
  42.9 0.2 collective-permute-start.15
  43.2 0.3 collective-permute-start.12
  43.4 0.4 collective-permute-done.14.refs_2_
  43.9 0.3 collective-permute-done.15.refs_3_
  44.3 2.5 %down.2.refs_1_.refs_5_ = f32[64,2048]{1,0:T(8,128)S(1)} custom-call(s32[2]{0:T(128)S(1)} %pad_add_fusion.where, bf16[16,2560]{1,0:T(8,128)(2,1)S(1)} %get-tuple-element.34.refs_0_, bf16[16,2560]{1,0:T(8,128)(2,1)S(1)} %collective-permute-done.13.refs_0_.refs_1_, bf16[16,2560]{1,0:T(8,128)(2,1)S(1)} %collective-permute-done.14.refs_2_, ...), custom_call_target="tpu_custom_call" | custom-call | bytes 1024 | tf_op jit(solution)/shard_map/down/pallas_call | solution.py:284
  46.8 0.3 collective-permute-start.16
  47.1 1.1 %collective-permute-done.16.refs_3_ = bf16[16,4096]{1,0:T(8,128)(2,1)S(1)} collective-permute-done((bf16[16,4096]{1,0:T(8,128)(2,1)S(1)}, bf16[16,4096]{1,0:T(8,128)(2,1)S(1)}, u32[]{:S(2)}, u32[]{:S(2)}) %collective-permute-start.16) | collective-permute-done | bytes 131104 | tf_op jit(solution)/shard_map/ppermute | solution.py:304
  48.2 3.6 %down.3 = (bf16[16,2048]{1,0:T(8,128)(2,1)S(1)}, bf16[16,2048]{1,0:T(8,128)(2,1)S(1)}, bf16[16,2048]{1,0:T(8,128)(2,1)S(1)}, bf16[16,2048]{1,0:T(8,128)(2,1)S(1)}) custom-call(s32[2]{0:T(128)S(1)} %pad_add_fusion.where, bf16[16,4096]{1,0:T(8,128)(2,1)S(1)} %combine.3.refs_1_.refs_0_, bf16[16,4096]{1,0:T(8,128)(2,1)S(1)} %collective-permute-done.11.refs_0_.refs_1_, ...), custom_call_target="tpu_custom_call" | custom-call | bytes 1024 | tf_op jit(solution)/shard_map/down/pallas_call | solution.py:284
  51.8 1.3 %collective-permute-start.17 = (bf16[16,2048]{1,0:T(8,128)(2,1)S(1)}, bf16[16,2048]{1,0:T(8,128)(2,1)S(1)}, u32[]{:S(2)}, u32[]{:S(2)}) collective-permute-start(bf16[16,2048]{1,0:T(8,128)(2,1)S(1)} %get-tuple-element.37), channel_id=1, source_target_pairs={{0,4},{4,0},{8,12},{12,8},{1,5},{5,1},{9,13},{13,9},{2,6},{6,2},{1... | collective-permute-start | bytes 196616 | tf_op jit(solution)/shard_map/ppermute | solution.py:304
  53.1 3.0 %collective-permute-done.17 = bf16[16,2048]{1,0:T(8,128)(2,1)S(1)} collective-permute-done((bf16[16,2048]{1,0:T(8,128)(2,1)S(1)}, bf16[16,2048]{1,0:T(8,128)(2,1)S(1)}, u32[]{:S(2)}, u32[]{:S(2)}) %collective-permute-start.17) | collective-permute-done | bytes 65568 | tf_op jit(solution)/shard_map/ppermute | solution.py:304
  56.1 2.5 %collective-permute-start.18 = (bf16[16,2048]{1,0:T(8,128)(2,1)S(1)}, bf16[16,2048]{1,0:T(8,128)(2,1)S(1)}, u32[]{:S(2)}, u32[]{:S(2)}) collective-permute-start(bf16[16,2048]{1,0:T(8,128)(2,1)S(1)} %add_convert_fusion.1.refs_0_), channel_id=1, source_target_pairs={{0,8},{4,12},{8,0},{12,4},{1,9},{5,13},{9,1},{13,5},{2,10},{6,14},... | collective-permute-start | bytes 196616 | tf_op jit(solution)/shard_map/ppermute | solution.py:304
  58.6 1.8 %collective-permute-start.19 = (bf16[16,2048]{1,0:T(8,128)(2,1)S(1)}, bf16[16,2048]{1,0:T(8,128)(2,1)S(1)}, u32[]{:S(2)}, u32[]{:S(2)}) collective-permute-start(bf16[16,2048]{1,0:T(8,128)(2,1)S(1)} %later.1), channel_id=1, source_target_pairs={{0,4},{4,0},{8,12},{12,8},{1,5},{5,1},{9,13},{13,9},{2,6},{6,2},{1... | collective-permute-start | bytes 196616 | tf_op jit(solution)/shard_map/ppermute | solution.py:304
  60.4 1.1 %collective-permute-done.18.right_ref = bf16[16,2048]{1,0:T(8,128)(2,1)S(1)} collective-permute-done((bf16[16,2048]{1,0:T(8,128)(2,1)S(1)}, bf16[16,2048]{1,0:T(8,128)(2,1)S(1)}, u32[]{:S(2)}, u32[]{:S(2)}) %collective-permute-start.18) | collective-permute-done | bytes 65568 | tf_op jit(solution)/shard_map/ppermute | solution.py:304
  61.5 1.4 %collective-permute-done.19 = bf16[16,2048]{1,0:T(8,128)(2,1)S(1)} collective-permute-done((bf16[16,2048]{1,0:T(8,128)(2,1)S(1)}, bf16[16,2048]{1,0:T(8,128)(2,1)S(1)}, u32[]{:S(2)}, u32[]{:S(2)}) %collective-permute-start.19) | collective-permute-done | bytes 65568 | tf_op jit(solution)/shard_map/ppermute | solution.py:304
  62.9 0.6 %add_convert_fusion = bf16[16,2048]{1,0:T(8,128)(2,1)} fusion(f32[16,2048]{1,0:T(8,128)S(1)} %add.13, bf16[16,2048]{1,0:T(8,128)(2,1)S(1)} %collective-permute-done.19), kind=kLoop, calls=%fused_computation | loop fusion | flops 98304 | bytes 262144 | tf_op jit(solution)/shard_map/convert_element_type | solution.py:345
  (25 shorter events, 0.1 us)
Async XLA Ops:
  0.0 12.2 %collective-permute-start.2 = (bf16[16,2048]{1,0:T(8,128)(2,1)}, bf16[16,2048]{1,0:T(8,128)(2,1)S(1)}, u32[]{:S(2)}, u32[]{:S(2)}) collective-permute-start(bf16[16,2048]{1,0:T(8,128)(2,1)} %tokens_ref.3), channel_id=1, source_target_pairs={{0,12},{4,8},{8,4},{12,0},{1,13},{5,9},{9,5},{13,1},{2,14},{6,10},... | collective-permute-start | bytes 196616 | tf_op jit(solution)/shard_map/ppermute | solution.py:304
  5.0 7.2 %collective-permute-start.1 = (bf16[16,2048]{1,0:T(8,128)(2,1)}, bf16[16,2048]{1,0:T(8,128)(2,1)S(1)}, u32[]{:S(2)}, u32[]{:S(2)}) collective-permute-start(bf16[16,2048]{1,0:T(8,128)(2,1)} %tokens_ref.3), channel_id=1, source_target_pairs={{0,8},{4,12},{8,0},{12,4},{1,9},{5,13},{9,1},{13,5},{2,10},{6,14},... | collective-permute-start | bytes 196616 | tf_op jit(solution)/shard_map/ppermute | solution.py:304
  5.1 7.2 %collective-permute-start = (bf16[16,2048]{1,0:T(8,128)(2,1)}, bf16[16,2048]{1,0:T(8,128)(2,1)S(1)}, u32[]{:S(2)}, u32[]{:S(2)}) collective-permute-start(bf16[16,2048]{1,0:T(8,128)(2,1)} %tokens_ref.3), channel_id=1, source_target_pairs={{0,4},{4,0},{8,12},{12,8},{1,5},{5,1},{9,13},{13,9},{2,6},{6,2},{1... | collective-permute-start | bytes 196616 | tf_op jit(solution)/shard_map/ppermute | solution.py:304
  5.6 6.7 %collective-permute-start.3 = (bf16[16,2048]{1,0:T(8,128)(2,1)}, bf16[16,2048]{1,0:T(8,128)(2,1)S(1)}, u32[]{:S(2)}, u32[]{:S(2)}) collective-permute-start(bf16[16,2048]{1,0:T(8,128)(2,1)} %tokens_ref.3), channel_id=1, source_target_pairs={{0,16},{16,0},{1,17},{17,1},{2,18},{18,2},{3,19},{19,3},{4,20},{20... | collective-permute-start | bytes 196616 | tf_op jit(solution)/shard_map/ppermute | solution.py:304
  12.3 5.8 %collective-permute-start.4 = (bf16[48,2048]{1,0:T(8,128)(2,1)S(1)}, bf16[48,2048]{1,0:T(8,128)(2,1)S(1)}, u32[]{:S(2)}, u32[]{:S(2)}) collective-permute-start(bf16[48,2048]{1,0:T(8,128)(2,1)S(1)} %join.3.refs_1_), channel_id=1, source_target_pairs={{0,16},{16,0},{1,17},{17,1},{2,18},{18,2},{3,19},{19,3},{4,20},{20... | collective-permute-start | bytes 589832 | tf_op jit(solution)/shard_map/ppermute | solution.py:304
  21.7 2.2 %collective-permute-start.5 = (bf16[2,64,2560]{2,1,0:T(8,128)(2,1)S(1)}, bf16[2,64,2560]{2,1,0:T(8,128)(2,1)S(1)}, u32[]{:S(2)}, u32[]{:S(2)}) collective-permute-start(bf16[2,64,2560]{2,1,0:T(8,128)(2,1)S(1)} %get-tuple-element.28), channel_id=1, source_target_pairs={{0,1},{1,0},{2,3},{3,2},{4,5},{5,4},{6,7},{7,6},{8,9},{9,8},{10,11... | collective-permute-start | bytes 1966088 | tf_op jit(solution)/shard_map/ppermute | solution.py:304
  23.9 20.4 %slice-start = ((s8[27262976]{0:T(1024)(128)(4,1)}), s8[4194304]{0:T(1024)(128)(4,1)S(1)}, s32[]{:S(2)}) async-start(s8[27262976]{0:T(1024)(128)(4,1)} %bitcast.2), calls=%async_computation | async-start | bytes 8388608
  23.9 20.3 %slice-start.1 = ((s8[27262976]{0:T(1024)(128)(4,1)}), s8[4194304]{0:T(1024)(128)(4,1)S(1)}, s32[]{:S(2)}) async-start(s8[27262976]{0:T(1024)(128)(4,1)} %bitcast.2), calls=%async_computation.1 | async-start | bytes 8388608
  24.0 20.3 %slice-start.2 = ((s8[27262976]{0:T(1024)(128)(4,1)}), s8[4194304]{0:T(1024)(128)(4,1)S(1)}, s32[]{:S(2)}) async-start(s8[27262976]{0:T(1024)(128)(4,1)} %bitcast.2), calls=%async_computation.2 | async-start | bytes 8388608
  24.0 20.3 %slice-start.3 = ((s8[27262976]{0:T(1024)(128)(4,1)}), s8[4194304]{0:T(1024)(128)(4,1)S(1)}, s32[]{:S(2)}) async-start(s8[27262976]{0:T(1024)(128)(4,1)} %bitcast.2), calls=%async_computation.3 | async-start | bytes 8388608
  24.0 20.3 %slice-start.4 = ((s8[27262976]{0:T(1024)(128)(4,1)}), s8[4194304]{0:T(1024)(128)(4,1)S(1)}, s32[]{:S(2)}) async-start(s8[27262976]{0:T(1024)(128)(4,1)} %bitcast.2), calls=%async_computation.4 | async-start | bytes 8388608
  24.0 20.3 %slice-start.5 = ((s8[27262976]{0:T(1024)(128)(4,1)}), s8[4194304]{0:T(1024)(128)(4,1)S(1)}, s32[]{:S(2)}) async-start(s8[27262976]{0:T(1024)(128)(4,1)} %bitcast.2), calls=%async_computation.5 | async-start | bytes 8388608
  24.0 20.3 %slice-start.6 = ((s8[27262976]{0:T(1024)(128)(4,1)}), s8[2097152]{0:T(1024)(128)(4,1)S(1)}, s32[]{:S(2)}) async-start(s8[27262976]{0:T(1024)(128)(4,1)} %bitcast.2), calls=%async_computation.6 | async-start | bytes 4194304
  24.0 9.8 %collective-permute-start.7 = (bf16[2,32,2560]{2,1,0:T(8,128)(2,1)S(1)}, bf16[2,32,2560]{2,1,0:T(8,128)(2,1)S(1)}, u32[]{:S(2)}, u32[]{:S(2)}) collective-permute-start(bf16[2,32,2560]{2,1,0:T(8,128)(2,1)S(1)} %pair_sum.2.refs_4_), channel_id=1, source_target_pairs={{0,2},{1,3},{2,0},{3,1},{4,6},{5,7},{6,4},{7,5},{8,10},{9,11},{10,... | collective-permute-start | bytes 983048 | tf_op jit(solution)/shard_map/ppermute | solution.py:304
  32.4 3.4 %collective-permute-start.6 = (bf16[2,32,1536]{2,1,0:T(8,128)(2,1)S(1)}, bf16[2,32,1536]{2,1,0:T(8,128)(2,1)S(1)}, u32[]{:S(2)}, u32[]{:S(2)}) collective-permute-start(bf16[2,32,1536]{2,1,0:T(8,128)(2,1)S(1)} %get-tuple-element.30), channel_id=1, source_target_pairs={{0,1},{1,0},{2,3},{3,2},{4,5},{5,4},{6,7},{7,6},{8,9},{9,8},{10,11... | collective-permute-start | bytes 589832 | tf_op jit(solution)/shard_map/ppermute | solution.py:304
  34.0 7.5 %collective-permute-start.10 = (bf16[16,2560]{1,0:T(8,128)(2,1)S(1)}, bf16[16,2560]{1,0:T(8,128)(2,1)S(1)}, u32[]{:S(2)}, u32[]{:S(2)}) collective-permute-start(bf16[16,2560]{1,0:T(8,128)(2,1)S(1)} %get-tuple-element.31.refs_0_), channel_id=1, source_target_pairs={{0,16},{16,0},{1,17},{17,1},{2,18},{18,2},{3,19},{19,3},{4,20},{20... | collective-permute-start | bytes 245768 | tf_op jit(solution)/shard_map/ppermute | solution.py:304
  35.9 4.6 %collective-permute-start.8 = (bf16[16,1536]{1,0:T(8,128)(2,1)S(1)}, bf16[16,1536]{1,0:T(8,128)(2,1)S(1)}, u32[]{:S(2)}, u32[]{:S(2)}) collective-permute-start(bf16[16,1536]{1,0:T(8,128)(2,1)S(1)} %get-tuple-element.32), channel_id=1, source_target_pairs={{0,2},{1,3},{2,0},{3,1},{4,6},{5,7},{6,4},{7,5},{8,10},{9,11},{10,... | collective-permute-start | bytes 147464 | tf_op jit(solution)/shard_map/ppermute | solution.py:304
  37.4 4.1 %collective-permute-start.9 = (bf16[16,1536]{1,0:T(8,128)(2,1)S(1)}, bf16[16,1536]{1,0:T(8,128)(2,1)S(1)}, u32[]{:S(2)}, u32[]{:S(2)}) collective-permute-start(bf16[16,1536]{1,0:T(8,128)(2,1)S(1)} %get-tuple-element.33), channel_id=1, source_target_pairs={{0,2},{1,3},{2,0},{3,1},{4,6},{5,7},{6,4},{7,5},{8,10},{9,11},{10,... | collective-permute-start | bytes 147464 | tf_op jit(solution)/shard_map/ppermute | solution.py:304
  38.0 5.0 %collective-permute-start.13 = (bf16[16,2560]{1,0:T(8,128)(2,1)S(1)}, bf16[16,2560]{1,0:T(8,128)(2,1)S(1)}, u32[]{:S(2)}, u32[]{:S(2)}) collective-permute-start(bf16[16,2560]{1,0:T(8,128)(2,1)S(1)} %get-tuple-element.34.refs_0_), channel_id=1, source_target_pairs={{0,2},{1,3},{2,0},{3,1},{4,6},{5,7},{6,4},{7,5},{8,10},{9,11},{10,... | collective-permute-start | bytes 245768 | tf_op jit(solution)/shard_map/ppermute | solution.py:304
  41.6 5.2 %collective-permute-start.11 = (bf16[16,4096]{1,0:T(8,128)(2,1)S(1)}, bf16[16,4096]{1,0:T(8,128)(2,1)S(1)}, u32[]{:S(2)}, u32[]{:S(2)}) collective-permute-start(bf16[16,4096]{1,0:T(8,128)(2,1)S(1)} %combine.3.refs_1_.refs_0_), channel_id=1, source_target_pairs={{0,2},{1,3},{2,0},{3,1},{4,6},{5,7},{6,4},{7,5},{8,10},{9,11},{10,... | collective-permute-start | bytes 393224 | tf_op jit(solution)/shard_map/ppermute | solution.py:304
  42.6 1.3 %collective-permute-start.14 = (bf16[16,2560]{1,0:T(8,128)(2,1)S(1)}, bf16[16,2560]{1,0:T(8,128)(2,1)S(1)}, u32[]{:S(2)}, u32[]{:S(2)}) collective-permute-start(bf16[16,2560]{1,0:T(8,128)(2,1)S(1)} %get-tuple-element.34.refs_0_), channel_id=1, source_target_pairs={{0,1},{1,0},{2,3},{3,2},{4,5},{5,4},{6,7},{7,6},{8,9},{9,8},{10,11... | collective-permute-start | bytes 245768 | tf_op jit(solution)/shard_map/ppermute | solution.py:304
  42.9 1.3 %collective-permute-start.15 = (bf16[16,2560]{1,0:T(8,128)(2,1)S(1)}, bf16[16,2560]{1,0:T(8,128)(2,1)S(1)}, u32[]{:S(2)}, u32[]{:S(2)}) collective-permute-start(bf16[16,2560]{1,0:T(8,128)(2,1)S(1)} %join.4), channel_id=1, source_target_pairs={{0,1},{1,0},{2,3},{3,2},{4,5},{5,4},{6,7},{7,6},{8,9},{9,8},{10,11... | collective-permute-start | bytes 245768 | tf_op jit(solution)/shard_map/ppermute | solution.py:304
  43.2 3.9 %collective-permute-start.12 = (bf16[16,4096]{1,0:T(8,128)(2,1)S(1)}, bf16[16,4096]{1,0:T(8,128)(2,1)S(1)}, u32[]{:S(2)}, u32[]{:S(2)}) collective-permute-start(bf16[16,4096]{1,0:T(8,128)(2,1)S(1)} %combine.3.refs_1_.refs_0_), channel_id=1, source_target_pairs={{0,1},{1,0},{2,3},{3,2},{4,5},{5,4},{6,7},{7,6},{8,9},{9,8},{10,11... | collective-permute-start | bytes 393224 | tf_op jit(solution)/shard_map/ppermute | solution.py:304
  46.8 1.4 %collective-permute-start.16 = (bf16[16,4096]{1,0:T(8,128)(2,1)S(1)}, bf16[16,4096]{1,0:T(8,128)(2,1)S(1)}, u32[]{:S(2)}, u32[]{:S(2)}) collective-permute-start(bf16[16,4096]{1,0:T(8,128)(2,1)S(1)} %join.5), channel_id=1, source_target_pairs={{0,1},{1,0},{2,3},{3,2},{4,5},{5,4},{6,7},{7,6},{8,9},{9,8},{10,11... | collective-permute-start | bytes 393224 | tf_op jit(solution)/shard_map/ppermute | solution.py:304
  51.8 4.3 %collective-permute-start.17 = (bf16[16,2048]{1,0:T(8,128)(2,1)S(1)}, bf16[16,2048]{1,0:T(8,128)(2,1)S(1)}, u32[]{:S(2)}, u32[]{:S(2)}) collective-permute-start(bf16[16,2048]{1,0:T(8,128)(2,1)S(1)} %get-tuple-element.37), channel_id=1, source_target_pairs={{0,4},{4,0},{8,12},{12,8},{1,5},{5,1},{9,13},{13,9},{2,6},{6,2},{1... | collective-permute-start | bytes 196616 | tf_op jit(solution)/shard_map/ppermute | solution.py:304
  56.1 5.3 %collective-permute-start.18 = (bf16[16,2048]{1,0:T(8,128)(2,1)S(1)}, bf16[16,2048]{1,0:T(8,128)(2,1)S(1)}, u32[]{:S(2)}, u32[]{:S(2)}) collective-permute-start(bf16[16,2048]{1,0:T(8,128)(2,1)S(1)} %add_convert_fusion.1.refs_0_), channel_id=1, source_target_pairs={{0,8},{4,12},{8,0},{12,4},{1,9},{5,13},{9,1},{13,5},{2,10},{6,14},... | collective-permute-start | bytes 196616 | tf_op jit(solution)/shard_map/ppermute | solution.py:304
  58.6 4.3 %collective-permute-start.19 = (bf16[16,2048]{1,0:T(8,128)(2,1)S(1)}, bf16[16,2048]{1,0:T(8,128)(2,1)S(1)}, u32[]{:S(2)}, u32[]{:S(2)}) collective-permute-start(bf16[16,2048]{1,0:T(8,128)(2,1)S(1)} %later.1), channel_id=1, source_target_pairs={{0,4},{4,0},{8,12},{12,8},{1,5},{5,1},{9,13},{13,9},{2,6},{6,2},{1... | collective-permute-start | bytes 196616 | tf_op jit(solution)/shard_map/ppermute | solution.py:304

commit v13 on v8

--- a/solution.py
+++ b/solution.py
@@ -102,17 +102,18 @@
     )(*arrays, *behind)
 
 
-def gate_up_kernel(n_arrays, n_pairs, segments, where, *refs):
+def gate_up_kernel(n_arrays, n_pairs, n_parts, segments, where, *refs):
     arrays, weights = refs[:n_arrays], refs[n_arrays : n_arrays + 2 * n_pairs]
     if segments:
-        mine_ref, theirs_ref, x_ref, w_ref, sems = refs[-5:]
+        refs, (w_ref, sems) = refs[:-2], refs[-2:]
+    mine_ref, theirs, x_ref = refs[-n_parts - 2], refs[-n_parts - 1 : -1], refs[-1]
+    if segments:
         copies = [column_copies(weights[k], w_ref.at[k], segments, sems.at[k]) for k in range(2)]
         cuts = copies[0][1]
         for i in range(len(cuts)):
             for k in range(2):
                 copies[k][0][i].start()
     else:
-        mine_ref, theirs_ref, x_ref = refs[-3:]
         step = weights[0].shape[1]
         cuts = [(p * step + a, p * step + b) for p in range(n_pairs) for a, b in pieces_of(step, 2 * TILE)]
     per = x_ref.shape[0] // (4 * ROWS)
@@ -133,10 +134,12 @@
                 weight = weights[2 * p + k][:, a - p * step : b - p * step]
             part = jnp.dot(x_ref[...], weight, preferred_element_type=jnp.float32).astype(jnp.bfloat16)
             mine_ref[k, :, a:b] = part[:half]
-            theirs_ref[k, :, a:b] = part[half:]
-
-
-def gate_up(where, arrays, weights, segments, behind):
+            part_width = theirs[0].shape[2]
+            i_part = a // part_width
+            theirs[i_part][k, :, a - i_part * part_width : b - i_part * part_width] = part[half:]
+
+
+def gate_up(where, arrays, weights, segments, n_parts, behind):
     depth = weights[0].shape[0]
     width = sum(w for _, w in segments) if segments else sum(w.shape[1] for w in weights[::2])
     total = sum(a.shape[0] for a in arrays)
@@ -146,39 +149,38 @@
         scratch.append(pltpu.VMEM((2, depth, width), jnp.bfloat16))
         scratch.append(pltpu.SemaphoreType.DMA((2, n_cuts)))
     return pl.pallas_call(
-        functools.partial(gate_up_kernel, len(arrays), len(weights) // 2, segments),
+        functools.partial(gate_up_kernel, len(arrays), len(weights) // 2, n_parts, segments),
         in_specs=[spec(pltpu.SMEM)]
         + [spec(pltpu.VMEM)] * len(arrays)
         + [spec(pltpu.HBM if segments else pltpu.VMEM)] * len(weights)
         + [spec(pl.ANY)] * len(behind),
-        out_specs=[spec(pltpu.VMEM)] * 2,
+        out_specs=[spec(pltpu.VMEM)] * (1 + n_parts),
         scratch_shapes=scratch,
-        out_shape=[jax.ShapeDtypeStruct((2, total // 2, width), jnp.bfloat16)] * 2,
+        out_shape=[jax.ShapeDtypeStruct((2, total // 2, w), jnp.bfloat16) for w in [width] + [width // n_parts] * n_parts],
         compiler_params=params(16 if segments else 4),
         cost_estimate=COST,
         name="gate_up",
     )(where, *arrays, *weights, *behind)
 
 
-def pair_sum_kernel(mine_ref, got_ref, *refs):
-    out_ref = refs[-1]
-    rows = out_ref.shape[1]
+def pair_sum_kernel(first, mine_ref, got_ref, out_ref):
+    rows, width = out_ref.shape[1:]
     for k in range(2):
-        total = mine_ref[k, rows:].astype(jnp.float32) + got_ref[k, rows:].astype(jnp.float32)
-        out_ref[k] = total.astype(out_ref.dtype)
-
-
-def pair_sum(mine, got, behind):
-    _, rows, width = mine.shape
-    return pl.pallas_call(
-        pair_sum_kernel,
-        in_specs=[spec(pltpu.VMEM)] * 2 + [spec(pl.ANY)] * len(behind),
+        mine = mine_ref[k, rows:, first : first + width].astype(jnp.float32)
+        out_ref[k] = (mine + got_ref[k, rows:].astype(jnp.float32)).astype(out_ref.dtype)
+
+
+def pair_sum(mine, got, first):
+    _, rows, width = got.shape
+    return pl.pallas_call(
+        functools.partial(pair_sum_kernel, first),
+        in_specs=[spec(pltpu.VMEM)] * 2,
         out_specs=spec(pltpu.VMEM),
         out_shape=jax.ShapeDtypeStruct((2, rows // 2, width), mine.dtype),
         compiler_params=params(2),
         cost_estimate=COST,
         name="pair_sum",
-    )(mine, got, *behind)
+    )(mine, got)
 
 
 def later_kernel(array_ref, *refs):
@@ -197,41 +199,42 @@
     )(array, *behind)
 
 
-def combine_kernel(n_left, n_sums, n_outs, *refs):
+def combine_kernel(n_left, n_parts, n_outs, mine_ref, *refs):
     lefts, refs, outs = refs[:n_left], refs[n_left:], refs[-n_outs:]
     first = 0
     for left in lefts:
-        outs[0][:, first : first + left.shape[1]] = left[...]
-        first += left.shape[1]
-    for i in range(n_sums):
-        mine_ref, got_ref, chip_ref = refs[3 * i : 3 * i + 3]
+        first = left.shape[1]
+        outs[0][:, :first] = left[...]
+    at = 0
+    for got_ref, chip_ref in zip(refs[:n_parts], refs[n_parts : 2 * n_parts]):
         _, rows, width = chip_ref.shape
         for a, b in pieces_of(width, TILE):
             gate, up = (
-                mine_ref[k, :rows, a:b].astype(jnp.float32)
+                mine_ref[k, :rows, at + a : at + b].astype(jnp.float32)
                 + got_ref[k, :rows, a:b].astype(jnp.float32)
                 + chip_ref[k, :, a:b].astype(jnp.float32)
                 for k in range(2)
             )
             hidden = (gate / (1 + jnp.exp(-gate)) * up).astype(jnp.bfloat16)
-            for j, out in enumerate(outs):
-                out[:, first + a : first + b] = hidden[j * ROWS : (j + 1) * ROWS]
-        first += width
-
-
-def combine(sums, left, behind):
-    n_outs = sums[0][2].shape[1] // ROWS
-    width = sum(x.shape[1] for x in left) + sum(chip.shape[2] for _, _, chip in sums)
-    args = [*left, *(x for triple in sums for x in triple)]
-    return pl.pallas_call(
-        functools.partial(combine_kernel, len(left), len(sums), n_outs),
-        in_specs=[spec(pltpu.VMEM)] * len(args) + [spec(pl.ANY)] * len(behind),
+            for i, out in enumerate(outs):
+                out[:, first + at + a : first + at + b] = hidden[i * ROWS : (i + 1) * ROWS]
+        at += width
+
+
+def combine(mine, gots, from_chips, left):
+    _, rows, width = mine.shape
+    n_outs = rows // (2 * ROWS)
+    width += sum(x.shape[1] for x in left)
+    args = [mine, *left, *gots, *from_chips]
+    return pl.pallas_call(
+        functools.partial(combine_kernel, len(left), len(gots), n_outs),
+        in_specs=[spec(pltpu.VMEM)] * len(args),
         out_specs=[spec(pltpu.VMEM)] * n_outs,
         out_shape=[jax.ShapeDtypeStruct((ROWS, width), jnp.bfloat16)] * n_outs,
         compiler_params=params(2),
         cost_estimate=COST,
         name="combine",
-    )(*args, *behind)
+    )(*args)
 
 
 def down_kernel(n_pieces, has_acc, last, segments, where, *refs):
@@ -243,7 +246,7 @@
     for piece in pieces:
         lhs_ref[at : at + piece.shape[0], :] = piece[...]
         at += piece.shape[0]
-    for a, b in pieces_of(down_ref.shape[1], 2 * TILE):
+    for a, b in pieces_of(down_ref.shape[1], 4 * TILE):
         part = prev_ref[:, a:b] if has_acc else 0.0
         at = 0
         for sign, start, depth in segments:
@@ -302,28 +305,27 @@
     near = join(by_hid, [own, far_own])
     far = swap(near, "rep", 1)
 
-    sums, to_chips, behind = [], [], [early[1][0]]
-    for weights in early:
-        mine, theirs = gate_up(where, [own, near, far_own, far], weights[:2], [], behind)
-        behind = [mine]
-        got = swap(theirs, "wid", 1)
-        to_chips.append(pair_sum(mine, got, []))
-        sums.append((mine, got, swap(to_chips[-1], "wid", 2)))
+    weights = [w for fetched in early for w in fetched[:2]]
+    mine, *theirs = gate_up(where, [own, near, far_own, far], weights, [], 2, [])
+    gots = [swap(x, "wid", 1) for x in theirs]
+    to_chips = [pair_sum(mine, got, first) for got, first in zip(gots, bounds)]
+    from_chips = [swap(x, "wid", 2) for x in to_chips]
     segments = [(bounds[2], widths[2]), (half + bounds[2], widths[2])]
-    mine, theirs = gate_up(where, [own, near], [gate_weight, up_weight], segments, to_chips)
-    got = swap(later(theirs, [s[2] for s in sums]), "wid", 1)
-    to_chip = pair_sum(mine, got, [])
-    last_sum = (mine, got, swap(to_chip, "wid", 2))
-
-    keep, give = combine(sums, [], [to_chip])
-    (rest,) = combine([last_sum], [swap(give, "rep", 1)], [])
+    last_mine, theirs = gate_up(where, [own, near], [gate_weight, up_weight], segments, 1, to_chips)
+    last_got = swap(later(theirs, from_chips), "wid", 1)
+    last_from_chip = swap(pair_sum(last_mine, last_got, 0), "wid", 2)
+
+    keep, give = combine(mine, gots, from_chips, [])
+    far_columns = swap(give, "rep", 1)
+    (rest,) = combine(last_mine, [last_got], [last_from_chip], [far_columns])
     rest_segments = [(-1, half, bounds[2])] + [(0, start, width) for start, width in segments]
-    acc, behind = None, [rest]
-    for hidden, parts in ((keep, [(1, 0, bounds[2])]), (rest, rest_segments)):
-        other = swap(hidden, "wid", 2)
-        crossed = swap(join([hidden, other], behind), "wid", 1)
-        acc = down(where, [hidden, other, crossed], down_weight, acc, parts, hidden is rest)
-        behind = [acc]
+
+    other = swap(keep, "wid", 2)
+    pieces = [keep, other, swap(join([keep, other], []), "wid", 1)]
+    acc = down(where, pieces, down_weight, None, [(1, 0, bounds[2])], False)
+    other = swap(rest, "wid", 2)
+    pieces = [rest, other, swap(rest, "wid", 1), swap(join([other], [acc]), "wid", 1)]
+    acc = down(where, pieces, down_weight, acc, rest_segments, True)
 
     mixed = acc[0].astype(f32)
     for d in (3, 2, 1):

time: 64.9 us -> 61.3 us (0.945)
  waiting for transfers between devices: 16.7 us -> 12.4 us
  starting transfers between devices: 19.6 us -> 21 us
  Pallas kernels: 27.4 us -> 26.7 us
    ppermute x19 -> x20, waiting for transfers between devices: 16.7 us -> 12.4 us  [swap(): return lax.ppermute(x, axis, [(i, i ^ step) for i in range(n)])]
    ppermute x19 -> x20, starting transfers between devices: 19.6 us -> 21 us  [swap(): return lax.ppermute(x, axis, [(i, i ^ step) for i in range(n)])]
    pallas_call x3 -> x2, Pallas kernels: 10.7 us -> 9.93 us  [gate_up(): pl.pallas_call(functools.partial(gate_up_kernel, len(arrays), len(weights...]
  transfers between devices with their start and end apart: 19 -> 20, of which waited for: 10 -> 9; matrix products, arithmetic and copies ran while one was open for 0% -> 0% of each run, Pallas kernels for 30% -> 32%
where the time goes in v13:
time: 61.3 us; the launch traced here: 61.2 us
  Pallas kernels  26.7 us (44%)
  starting transfers between devices  21 us (34%)
  waiting for transfers between devices  12.4 us (20%)
  other arithmetic  0.74 us (1%)
    ppermute x20, starting transfers between devices, swap(): return lax.ppermute(x, axis, [(i, i ^ step) for i in range(n)])  21 us
    ppermute x20, waiting for transfers between devices, swap(): return lax.ppermute(x, axis, [(i, i ^ step) for i in range(n)])  12.4 us
    pallas_call x2, Pallas kernels, fetch(): pl.pallas_call(functools.partial(fetch_kernel, first), in_specs=[spec(plt...  10.2 us
    pallas_call x2, Pallas kernels, gate_up(): pl.pallas_call(functools.partial(gate_up_kernel, len(arrays), len(weights...  9.93 us
    pallas_call x2, Pallas kernels, down(): pl.pallas_call(functools.partial(down_kernel, len(pieces), prev is not No...  6.06 us
  transfers between devices with their start and end apart: 20, of which 9 were waited for; matrix products, arithmetic and copies ran while one was open for 0% of the time, Pallas kernels for 32%

profile of v13, /device:TPU:0, one launch (start us, length us, event | category | flops | bytes accessed | tf_op | source)
XLA Modules:
  0.0 61.2 jit_solution(12720910837552754247)
XLA Ops:
  0.0 5.0 %collective-permute-start.2 = (bf16[16,2048]{1,0:T(8,128)(2,1)}, bf16[16,2048]{1,0:T(8,128)(2,1)S(1)}, u32[]{:S(2)}, u32[]{:S(2)}) collective-permute-start(bf16[16,2048]{1,0:T(8,128)(2,1)} %tokens_ref.3), channel_id=1, source_target_pairs={{0,12},{4,8},{8,4},{12,0},{1,13},{5,9},{9,5},{13,1},{2,14},{6,10},... | collective-permute-start | bytes 196616 | tf_op jit(solution)/shard_map/ppermute | solution.py:291
  5.1 0.6 collective-permute-start
  5.6 1.7 %collective-permute-start.3 = (bf16[16,2048]{1,0:T(8,128)(2,1)}, bf16[16,2048]{1,0:T(8,128)(2,1)S(1)}, u32[]{:S(2)}, u32[]{:S(2)}) collective-permute-start(bf16[16,2048]{1,0:T(8,128)(2,1)} %tokens_ref.3), channel_id=1, source_target_pairs={{0,16},{16,0},{1,17},{17,1},{2,18},{18,2},{3,19},{19,3},{4,20},{20... | collective-permute-start | bytes 196616 | tf_op jit(solution)/shard_map/ppermute | solution.py:291
  7.4 0.1 pad_add_fusion.where
  7.4 4.8 %fetch.2 = (bf16[2048,1280]{1,0:T(8,128)(2,1)S(1)}, bf16[2048,1280]{1,0:T(8,128)(2,1)S(1)}, bf16[16,2048]{1,0:T(8,128)(2,1)S(1)}) custom-call(s32[2]{0:T(128)S(1)} %pad_add_fusion.where, bf16[2048,6656]{1,0:T(8,128)(2,1)} %refs_2_.1, bf16[2048,6656]{1,0:T(8,128)(2,1)} %refs_3_.2, bf16[16,2048]{1,0:T(8,128)(2,1)} %tokens_ref.3), custom_call_target="tpu_custom_call" | custom-call | bytes 1024 | tf_op jit(solution)/shard_map/fetch/pallas_call | solution.py:73
  12.2 0.0 collective-permute-done.2.refs_2_
  12.3 0.0 collective-permute-done.1.refs_1_
  12.3 0.0 collective-permute-done.3.refs_4_.refs_2_
  12.3 0.4 collective-permute-start.4
  12.7 5.4 %fetch.3 = (bf16[2048,1280]{1,0:T(8,128)(2,1)S(1)}, bf16[2048,1280]{1,0:T(8,128)(2,1)S(1)}, bf16[16,2048]{1,0:T(8,128)(2,1)}) custom-call(s32[2]{0:T(128)S(1)} %pad_add_fusion.where, bf16[2048,6656]{1,0:T(8,128)(2,1)} %refs_2_.1, bf16[2048,6656]{1,0:T(8,128)(2,1)} %refs_3_.2, bf16[16,2048]{1,0:T(8,128)(2,1)} %tokens_ref.3), custom_call_target="tpu_custom_call" | custom-call | bytes 1024 | tf_op jit(solution)/shard_map/fetch/pallas_call | solution.py:73
  18.1 3.6 %gate_up.2 = (bf16[2,64,2560]{2,1,0:T(8,128)(2,1)S(1)}, bf16[2,64,1280]{2,1,0:T(8,128)(2,1)S(1)}, bf16[2,64,1280]{2,1,0:T(8,128)(2,1)S(1)}) custom-call(s32[2]{0:T(128)S(1)} %pad_add_fusion.where, bf16[16,2048]{1,0:T(8,128)(2,1)S(1)} %get-tuple-element.21.refs_3_.refs_0_, bf16[48,2048]{1,0:T(8,128)(2,1)S(1)} %join.3.refs_1_, ...), custom_call_target="tpu_custom_call" | custom-call | bytes 1024 | tf_op jit(solution)/shard_map/gate_up/pallas_call | solution.py:151
  21.7 0.1 collective-permute-start.5
  21.8 0.5 collective-permute-start.6
  22.3 1.1 %collective-permute-done.5.got_ref.refs_0_ = bf16[2,64,1280]{2,1,0:T(8,128)(2,1)S(1)} collective-permute-done((bf16[2,64,1280]{2,1,0:T(8,128)(2,1)S(1)}, bf16[2,64,1280]{2,1,0:T(8,128)(2,1)S(1)}, u32[]{:S(2)}, u32[]{:S(2)}) %collective-permute-start.5) | collective-permute-done | bytes 327712 | tf_op jit(solution)/shard_map/ppermute | solution.py:291
  23.4 1.8 %collective-permute-start.7 = (bf16[2,32,1280]{2,1,0:T(8,128)(2,1)S(1)}, bf16[2,32,1280]{2,1,0:T(8,128)(2,1)S(1)}, u32[]{:S(2)}, u32[]{:S(2)}) collective-permute-start(bf16[2,32,1280]{2,1,0:T(8,128)(2,1)S(1)} %pair_sum.3.refs_4_), channel_id=1, source_target_pairs={{0,2},{1,3},{2,0},{3,1},{4,6},{5,7},{6,4},{7,5},{8,10},{9,11},{10,... | collective-permute-start | bytes 491528 | tf_op jit(solution)/shard_map/ppermute | solution.py:291
  25.3 0.0 slice-start.1
  25.3 0.0 slice-start.2
  25.3 0.0 slice-start.4
  25.3 0.0 slice-start.5
  25.3 0.4 collective-permute-start.8
  25.7 6.4 %gate_up.3 = (bf16[2,32,1536]{2,1,0:T(8,128)(2,1)S(1)}, bf16[2,32,1536]{2,1,0:T(8,128)(2,1)S(1)}) custom-call(s32[2]{0:T(128)S(1)} %pad_add_fusion.where, bf16[16,2048]{1,0:T(8,128)(2,1)S(1)} %get-tuple-element.21.refs_3_.refs_0_, bf16[48,2048]{1,0:T(8,128)(2,1)S(1)} %join.3.refs_1_, bf16[2048,6656]{1,0:T(8,128)(2,1)} %refs_2_.1, ...), custom_call_target="tpu_custom_call" | custom-call | bytes 1024 | tf_op jit(solution)/shard_map/gate_up/pallas_call | solution.py:151
  32.1 0.0 collective-permute-done.7.refs_2_.refs_0_
  32.1 1.1 %collective-permute-done.8.refs_3_.refs_1_ = bf16[2,32,1280]{2,1,0:T(8,128)(2,1)S(1)} collective-permute-done((bf16[2,32,1280]{2,1,0:T(8,128)(2,1)S(1)}, bf16[2,32,1280]{2,1,0:T(8,128)(2,1)S(1)}, u32[]{:S(2)}, u32[]{:S(2)}) %collective-permute-start.8) | collective-permute-done | bytes 163872 | tf_op jit(solution)/shard_map/ppermute | solution.py:291
  33.3 0.1 collective-permute-start.10
  33.4 0.2 combine.2
  33.6 1.8 %collective-permute-start.14 = (bf16[16,2560]{1,0:T(8,128)(2,1)S(1)}, bf16[16,2560]{1,0:T(8,128)(2,1)S(1)}, u32[]{:S(2)}, u32[]{:S(2)}) collective-permute-start(bf16[16,2560]{1,0:T(8,128)(2,1)S(1)} %get-tuple-element.32.refs_0_), channel_id=1, source_target_pairs={{0,2},{1,3},{2,0},{3,1},{4,6},{5,7},{6,4},{7,5},{8,10},{9,11},{10,... | collective-permute-start | bytes 245768 | tf_op jit(solution)/shard_map/ppermute | solution.py:291
  35.3 0.0 collective-permute-done.10.got_ref.refs_1_
  35.4 1.2 %collective-permute-start.11 = (bf16[2,16,1536]{2,1,0:T(8,128)(2,1)S(1)}, bf16[2,16,1536]{2,1,0:T(8,128)(2,1)S(1)}, u32[]{:S(2)}, u32[]{:S(2)}) collective-permute-start(bf16[2,16,1536]{2,1,0:T(8,128)(2,1)S(1)} %pair_sum.5), channel_id=1, source_target_pairs={{0,2},{1,3},{2,0},{3,1},{4,6},{5,7},{6,4},{7,5},{8,10},{9,11},{10,... | collective-permute-start | bytes 294920 | tf_op jit(solution)/shard_map/ppermute | solution.py:291
  36.6 1.5 %collective-permute-start.9 = (bf16[16,2560]{1,0:T(8,128)(2,1)S(1)}, bf16[16,2560]{1,0:T(8,128)(2,1)S(1)}, u32[]{:S(2)}, u32[]{:S(2)}) collective-permute-start(bf16[16,2560]{1,0:T(8,128)(2,1)S(1)} %get-tuple-element.30), channel_id=1, source_target_pairs={{0,16},{16,0},{1,17},{17,1},{2,18},{18,2},{3,19},{19,3},{4,20},{20... | collective-permute-start | bytes 245768 | tf_op jit(solution)/shard_map/ppermute | solution.py:291
  38.1 0.6 collective-permute-done.14.refs_1_
  38.7 0.1 collective-permute-start.15
  38.8 2.3 %collective-permute-done.9.refs_0_ = bf16[16,2560]{1,0:T(8,128)(2,1)S(1)} collective-permute-done((bf16[16,2560]{1,0:T(8,128)(2,1)S(1)}, bf16[16,2560]{1,0:T(8,128)(2,1)S(1)}, u32[]{:S(2)}, u32[]{:S(2)}) %collective-permute-start.9) | collective-permute-done | bytes 81952 | tf_op jit(solution)/shard_map/ppermute | solution.py:291
  41.0 0.1 combine.3.refs_0_
  41.1 1.3 %collective-permute-start.12 = (bf16[16,4096]{1,0:T(8,128)(2,1)S(1)}, bf16[16,4096]{1,0:T(8,128)(2,1)S(1)}, u32[]{:S(2)}, u32[]{:S(2)}) collective-permute-start(bf16[16,4096]{1,0:T(8,128)(2,1)S(1)} %combine.3.refs_0_), channel_id=1, source_target_pairs={{0,2},{1,3},{2,0},{3,1},{4,6},{5,7},{6,4},{7,5},{8,10},{9,11},{10,... | collective-permute-start | bytes 393224 | tf_op jit(solution)/shard_map/ppermute | solution.py:291
  42.5 2.5 %down.2.refs_1_.refs_5_ = f32[64,2048]{1,0:T(8,128)S(1)} custom-call(s32[2]{0:T(128)S(1)} %pad_add_fusion.where, bf16[16,2560]{1,0:T(8,128)(2,1)S(1)} %get-tuple-element.32.refs_0_, bf16[16,2560]{1,0:T(8,128)(2,1)S(1)} %collective-permute-done.14.refs_1_, bf16[32,2560]{1,0:T(8,128)(2,1)S(1)} %collective-permute-done.15.refs_2_, bf16[6656,2048]{1,0:T(8,128)(2,1)S(1)} %bitcast.3), custom_call_target="tpu_custom_call" | custom-call | bytes 1024 | tf_op jit(solution)/shard_map/down/pallas_call | solution.py:271
  45.0 0.1 collective-permute-start.13
  45.0 1.1 %collective-permute-done.12.refs_0_.refs_1_ = bf16[16,4096]{1,0:T(8,128)(2,1)S(1)} collective-permute-done((bf16[16,4096]{1,0:T(8,128)(2,1)S(1)}, bf16[16,4096]{1,0:T(8,128)(2,1)S(1)}, u32[]{:S(2)}, u32[]{:S(2)}) %collective-permute-start.12) | collective-permute-done | bytes 131104 | tf_op jit(solution)/shard_map/ppermute | solution.py:291
  46.2 0.1 collective-permute-start.16
  46.2 0.1 collective-permute-done.13.refs_2_
  46.4 1.2 %collective-permute-done.16.refs_3_ = bf16[16,4096]{1,0:T(8,128)(2,1)S(1)} collective-permute-done((bf16[16,4096]{1,0:T(8,128)(2,1)S(1)}, bf16[16,4096]{1,0:T(8,128)(2,1)S(1)}, u32[]{:S(2)}, u32[]{:S(2)}) %collective-permute-start.16) | collective-permute-done | bytes 131104 | tf_op jit(solution)/shard_map/ppermute | solution.py:291
  47.6 3.6 %down.3 = (bf16[16,2048]{1,0:T(8,128)(2,1)S(1)}, bf16[16,2048]{1,0:T(8,128)(2,1)S(1)}, bf16[16,2048]{1,0:T(8,128)(2,1)S(1)}, bf16[16,2048]{1,0:T(8,128)(2,1)S(1)}) custom-call(s32[2]{0:T(128)S(1)} %pad_add_fusion.where, bf16[16,4096]{1,0:T(8,128)(2,1)S(1)} %combine.3.refs_0_, bf16[16,4096]{1,0:T(8,128)(2,1)S(1)} %collective-permute-done.12.refs_0_.refs_1_, ...), custom_call_target="tpu_custom_call" | custom-call | bytes 1024 | tf_op jit(solution)/shard_map/down/pallas_call | solution.py:271
  51.2 3.7 %collective-permute-start.17 = (bf16[16,2048]{1,0:T(8,128)(2,1)S(1)}, bf16[16,2048]{1,0:T(8,128)(2,1)S(1)}, u32[]{:S(2)}, u32[]{:S(2)}) collective-permute-start(bf16[16,2048]{1,0:T(8,128)(2,1)S(1)} %get-tuple-element.34), channel_id=1, source_target_pairs={{0,12},{4,8},{8,4},{12,0},{1,13},{5,9},{9,5},{13,1},{2,14},{6,10},... | collective-permute-start | bytes 196616 | tf_op jit(solution)/shard_map/ppermute | solution.py:291
  54.8 0.0 collective-permute-start.18
  54.8 0.8 %collective-permute-start.19 = (bf16[16,2048]{1,0:T(8,128)(2,1)S(1)}, bf16[16,2048]{1,0:T(8,128)(2,1)S(1)}, u32[]{:S(2)}, u32[]{:S(2)}) collective-permute-start(bf16[16,2048]{1,0:T(8,128)(2,1)S(1)} %get-tuple-element.36), channel_id=1, source_target_pairs={{0,4},{4,0},{8,12},{12,8},{1,5},{5,1},{9,13},{13,9},{2,6},{6,2},{1... | collective-permute-start | bytes 196616 | tf_op jit(solution)/shard_map/ppermute | solution.py:291
  55.6 2.3 %collective-permute-done.17 = bf16[16,2048]{1,0:T(8,128)(2,1)S(1)} collective-permute-done((bf16[16,2048]{1,0:T(8,128)(2,1)S(1)}, bf16[16,2048]{1,0:T(8,128)(2,1)S(1)}, u32[]{:S(2)}, u32[]{:S(2)}) %collective-permute-start.17) | collective-permute-done | bytes 65568 | tf_op jit(solution)/shard_map/ppermute | solution.py:291
  57.9 2.6 %collective-permute-done.18 = bf16[16,2048]{1,0:T(8,128)(2,1)S(1)} collective-permute-done((bf16[16,2048]{1,0:T(8,128)(2,1)S(1)}, bf16[16,2048]{1,0:T(8,128)(2,1)S(1)}, u32[]{:S(2)}, u32[]{:S(2)}) %collective-permute-start.18) | collective-permute-done | bytes 65568 | tf_op jit(solution)/shard_map/ppermute | solution.py:291
  60.5 0.0 collective-permute-done.19
  60.5 0.7 %add_convert_fusion = bf16[16,2048]{1,0:T(8,128)(2,1)} fusion(bf16[16,2048]{1,0:T(8,128)(2,1)S(1)} %collective-permute-done.19, bf16[16,2048]{1,0:T(8,128)(2,1)S(1)} %collective-permute-done.18, bf16[16,2048]{1,0:T(8,128)(2,1)S(1)} %collective-permute-done.17, bf16[16,2048]{1,0:T(8,128)(2,1)S(1)} %get-tuple-element.33), kind=kLoop, calls=%fused_computation | loop fusion | flops 262144 | bytes 327680 | tf_op jit(solution)/shard_map/convert_element_type | solution.py:333
  (24 shorter events, 0.2 us)
Async XLA Ops:
  0.0 12.2 %collective-permute-start.2 = (bf16[16,2048]{1,0:T(8,128)(2,1)}, bf16[16,2048]{1,0:T(8,128)(2,1)S(1)}, u32[]{:S(2)}, u32[]{:S(2)}) collective-permute-start(bf16[16,2048]{1,0:T(8,128)(2,1)} %tokens_ref.3), channel_id=1, source_target_pairs={{0,12},{4,8},{8,4},{12,0},{1,13},{5,9},{9,5},{13,1},{2,14},{6,10},... | collective-permute-start | bytes 196616 | tf_op jit(solution)/shard_map/ppermute | solution.py:291
  5.0 7.2 %collective-permute-start.1 = (bf16[16,2048]{1,0:T(8,128)(2,1)}, bf16[16,2048]{1,0:T(8,128)(2,1)S(1)}, u32[]{:S(2)}, u32[]{:S(2)}) collective-permute-start(bf16[16,2048]{1,0:T(8,128)(2,1)} %tokens_ref.3), channel_id=1, source_target_pairs={{0,8},{4,12},{8,0},{12,4},{1,9},{5,13},{9,1},{13,5},{2,10},{6,14},... | collective-permute-start | bytes 196616 | tf_op jit(solution)/shard_map/ppermute | solution.py:291
  5.1 7.2 %collective-permute-start = (bf16[16,2048]{1,0:T(8,128)(2,1)}, bf16[16,2048]{1,0:T(8,128)(2,1)S(1)}, u32[]{:S(2)}, u32[]{:S(2)}) collective-permute-start(bf16[16,2048]{1,0:T(8,128)(2,1)} %tokens_ref.3), channel_id=1, source_target_pairs={{0,4},{4,0},{8,12},{12,8},{1,5},{5,1},{9,13},{13,9},{2,6},{6,2},{1... | collective-permute-start | bytes 196616 | tf_op jit(solution)/shard_map/ppermute | solution.py:291
  5.6 6.7 %collective-permute-start.3 = (bf16[16,2048]{1,0:T(8,128)(2,1)}, bf16[16,2048]{1,0:T(8,128)(2,1)S(1)}, u32[]{:S(2)}, u32[]{:S(2)}) collective-permute-start(bf16[16,2048]{1,0:T(8,128)(2,1)} %tokens_ref.3), channel_id=1, source_target_pairs={{0,16},{16,0},{1,17},{17,1},{2,18},{18,2},{3,19},{19,3},{4,20},{20... | collective-permute-start | bytes 196616 | tf_op jit(solution)/shard_map/ppermute | solution.py:291
  12.3 5.8 %collective-permute-start.4 = (bf16[48,2048]{1,0:T(8,128)(2,1)S(1)}, bf16[48,2048]{1,0:T(8,128)(2,1)S(1)}, u32[]{:S(2)}, u32[]{:S(2)}) collective-permute-start(bf16[48,2048]{1,0:T(8,128)(2,1)S(1)} %join.3.refs_1_), channel_id=1, source_target_pairs={{0,16},{16,0},{1,17},{17,1},{2,18},{18,2},{3,19},{19,3},{4,20},{20... | collective-permute-start | bytes 589832 | tf_op jit(solution)/shard_map/ppermute | solution.py:291
  21.7 1.7 %collective-permute-start.5 = (bf16[2,64,1280]{2,1,0:T(8,128)(2,1)S(1)}, bf16[2,64,1280]{2,1,0:T(8,128)(2,1)S(1)}, u32[]{:S(2)}, u32[]{:S(2)}) collective-permute-start(bf16[2,64,1280]{2,1,0:T(8,128)(2,1)S(1)} %get-tuple-element.27), channel_id=1, source_target_pairs={{0,1},{1,0},{2,3},{3,2},{4,5},{5,4},{6,7},{7,6},{8,9},{9,8},{10,11... | collective-permute-start | bytes 983048 | tf_op jit(solution)/shard_map/ppermute | solution.py:291
  21.8 3.4 %collective-permute-start.6 = (bf16[2,64,1280]{2,1,0:T(8,128)(2,1)S(1)}, bf16[2,64,1280]{2,1,0:T(8,128)(2,1)S(1)}, u32[]{:S(2)}, u32[]{:S(2)}) collective-permute-start(bf16[2,64,1280]{2,1,0:T(8,128)(2,1)S(1)} %get-tuple-element.28), channel_id=1, source_target_pairs={{0,1},{1,0},{2,3},{3,2},{4,5},{5,4},{6,7},{7,6},{8,9},{9,8},{10,11... | collective-permute-start | bytes 983048 | tf_op jit(solution)/shard_map/ppermute | solution.py:291
  23.4 8.7 %collective-permute-start.7 = (bf16[2,32,1280]{2,1,0:T(8,128)(2,1)S(1)}, bf16[2,32,1280]{2,1,0:T(8,128)(2,1)S(1)}, u32[]{:S(2)}, u32[]{:S(2)}) collective-permute-start(bf16[2,32,1280]{2,1,0:T(8,128)(2,1)S(1)} %pair_sum.3.refs_4_), channel_id=1, source_target_pairs={{0,2},{1,3},{2,0},{3,1},{4,6},{5,7},{6,4},{7,5},{8,10},{9,11},{10,... | collective-permute-start | bytes 491528 | tf_op jit(solution)/shard_map/ppermute | solution.py:291
  25.2 17.2 %slice-start = ((s8[27262976]{0:T(1024)(128)(4,1)}), s8[4194304]{0:T(1024)(128)(4,1)S(1)}, s32[]{:S(2)}) async-start(s8[27262976]{0:T(1024)(128)(4,1)} %bitcast.2), calls=%async_computation | async-start | bytes 8388608
  25.3 17.2 %slice-start.1 = ((s8[27262976]{0:T(1024)(128)(4,1)}), s8[4194304]{0:T(1024)(128)(4,1)S(1)}, s32[]{:S(2)}) async-start(s8[27262976]{0:T(1024)(128)(4,1)} %bitcast.2), calls=%async_computation.1 | async-start | bytes 8388608
  25.3 17.2 %slice-start.2 = ((s8[27262976]{0:T(1024)(128)(4,1)}), s8[4194304]{0:T(1024)(128)(4,1)S(1)}, s32[]{:S(2)}) async-start(s8[27262976]{0:T(1024)(128)(4,1)} %bitcast.2), calls=%async_computation.2 | async-start | bytes 8388608
  25.3 17.2 %slice-start.3 = ((s8[27262976]{0:T(1024)(128)(4,1)}), s8[4194304]{0:T(1024)(128)(4,1)S(1)}, s32[]{:S(2)}) async-start(s8[27262976]{0:T(1024)(128)(4,1)} %bitcast.2), calls=%async_computation.3 | async-start | bytes 8388608
  25.3 17.2 %slice-start.4 = ((s8[27262976]{0:T(1024)(128)(4,1)}), s8[4194304]{0:T(1024)(128)(4,1)S(1)}, s32[]{:S(2)}) async-start(s8[27262976]{0:T(1024)(128)(4,1)} %bitcast.2), calls=%async_computation.4 | async-start | bytes 8388608
  25.3 17.2 %slice-start.5 = ((s8[27262976]{0:T(1024)(128)(4,1)}), s8[4194304]{0:T(1024)(128)(4,1)S(1)}, s32[]{:S(2)}) async-start(s8[27262976]{0:T(1024)(128)(4,1)} %bitcast.2), calls=%async_computation.5 | async-start | bytes 8388608
  25.3 17.2 %slice-start.6 = ((s8[27262976]{0:T(1024)(128)(4,1)}), s8[2097152]{0:T(1024)(128)(4,1)S(1)}, s32[]{:S(2)}) async-start(s8[27262976]{0:T(1024)(128)(4,1)} %bitcast.2), calls=%async_computation.6 | async-start | bytes 4194304
  25.3 7.9 %collective-permute-start.8 = (bf16[2,32,1280]{2,1,0:T(8,128)(2,1)S(1)}, bf16[2,32,1280]{2,1,0:T(8,128)(2,1)S(1)}, u32[]{:S(2)}, u32[]{:S(2)}) collective-permute-start(bf16[2,32,1280]{2,1,0:T(8,128)(2,1)S(1)} %pair_sum.4.refs_5_), channel_id=1, source_target_pairs={{0,2},{1,3},{2,0},{3,1},{4,6},{5,7},{6,4},{7,5},{8,10},{9,11},{10,... | collective-permute-start | bytes 491528 | tf_op jit(solution)/shard_map/ppermute | solution.py:291
  33.3 2.1 %collective-permute-start.10 = (bf16[2,32,1536]{2,1,0:T(8,128)(2,1)S(1)}, bf16[2,32,1536]{2,1,0:T(8,128)(2,1)S(1)}, u32[]{:S(2)}, u32[]{:S(2)}) collective-permute-start(bf16[2,32,1536]{2,1,0:T(8,128)(2,1)S(1)} %later.1), channel_id=1, source_target_pairs={{0,1},{1,0},{2,3},{3,2},{4,5},{5,4},{6,7},{7,6},{8,9},{9,8},{10,11... | collective-permute-start | bytes 589832 | tf_op jit(solution)/shard_map/ppermute | solution.py:291
  33.6 5.1 %collective-permute-start.14 = (bf16[16,2560]{1,0:T(8,128)(2,1)S(1)}, bf16[16,2560]{1,0:T(8,128)(2,1)S(1)}, u32[]{:S(2)}, u32[]{:S(2)}) collective-permute-start(bf16[16,2560]{1,0:T(8,128)(2,1)S(1)} %get-tuple-element.32.refs_0_), channel_id=1, source_target_pairs={{0,2},{1,3},{2,0},{3,1},{4,6},{5,7},{6,4},{7,5},{8,10},{9,11},{10,... | collective-permute-start | bytes 245768 | tf_op jit(solution)/shard_map/ppermute | solution.py:291
  35.4 5.7 %collective-permute-start.11 = (bf16[2,16,1536]{2,1,0:T(8,128)(2,1)S(1)}, bf16[2,16,1536]{2,1,0:T(8,128)(2,1)S(1)}, u32[]{:S(2)}, u32[]{:S(2)}) collective-permute-start(bf16[2,16,1536]{2,1,0:T(8,128)(2,1)S(1)} %pair_sum.5), channel_id=1, source_target_pairs={{0,2},{1,3},{2,0},{3,1},{4,6},{5,7},{6,4},{7,5},{8,10},{9,11},{10,... | collective-permute-start | bytes 294920 | tf_op jit(solution)/shard_map/ppermute | solution.py:291
  36.6 4.4 %collective-permute-start.9 = (bf16[16,2560]{1,0:T(8,128)(2,1)S(1)}, bf16[16,2560]{1,0:T(8,128)(2,1)S(1)}, u32[]{:S(2)}, u32[]{:S(2)}) collective-permute-start(bf16[16,2560]{1,0:T(8,128)(2,1)S(1)} %get-tuple-element.30), channel_id=1, source_target_pairs={{0,16},{16,0},{1,17},{17,1},{2,18},{18,2},{3,19},{19,3},{4,20},{20... | collective-permute-start | bytes 245768 | tf_op jit(solution)/shard_map/ppermute | solution.py:291
  38.7 3.7 %collective-permute-start.15 = (bf16[32,2560]{1,0:T(8,128)(2,1)S(1)}, bf16[32,2560]{1,0:T(8,128)(2,1)S(1)}, u32[]{:S(2)}, u32[]{:S(2)}) collective-permute-start(bf16[32,2560]{1,0:T(8,128)(2,1)S(1)} %join.4), channel_id=1, source_target_pairs={{0,1},{1,0},{2,3},{3,2},{4,5},{5,4},{6,7},{7,6},{8,9},{9,8},{10,11... | collective-permute-start | bytes 491528 | tf_op jit(solution)/shard_map/ppermute | solution.py:291
  41.1 5.0 %collective-permute-start.12 = (bf16[16,4096]{1,0:T(8,128)(2,1)S(1)}, bf16[16,4096]{1,0:T(8,128)(2,1)S(1)}, u32[]{:S(2)}, u32[]{:S(2)}) collective-permute-start(bf16[16,4096]{1,0:T(8,128)(2,1)S(1)} %combine.3.refs_0_), channel_id=1, source_target_pairs={{0,2},{1,3},{2,0},{3,1},{4,6},{5,7},{6,4},{7,5},{8,10},{9,11},{10,... | collective-permute-start | bytes 393224 | tf_op jit(solution)/shard_map/ppermute | solution.py:291
  45.0 1.4 %collective-permute-start.13 = (bf16[16,4096]{1,0:T(8,128)(2,1)S(1)}, bf16[16,4096]{1,0:T(8,128)(2,1)S(1)}, u32[]{:S(2)}, u32[]{:S(2)}) collective-permute-start(bf16[16,4096]{1,0:T(8,128)(2,1)S(1)} %combine.3.refs_0_), channel_id=1, source_target_pairs={{0,1},{1,0},{2,3},{3,2},{4,5},{5,4},{6,7},{7,6},{8,9},{9,8},{10,11... | collective-permute-start | bytes 393224 | tf_op jit(solution)/shard_map/ppermute | solution.py:291
  46.2 1.4 %collective-permute-start.16 = (bf16[16,4096]{1,0:T(8,128)(2,1)S(1)}, bf16[16,4096]{1,0:T(8,128)(2,1)S(1)}, u32[]{:S(2)}, u32[]{:S(2)}) collective-permute-start(bf16[16,4096]{1,0:T(8,128)(2,1)S(1)} %join.5), channel_id=1, source_target_pairs={{0,1},{1,0},{2,3},{3,2},{4,5},{5,4},{6,7},{7,6},{8,9},{9,8},{10,11... | collective-permute-start | bytes 393224 | tf_op jit(solution)/shard_map/ppermute | solution.py:291
  51.2 6.7 %collective-permute-start.17 = (bf16[16,2048]{1,0:T(8,128)(2,1)S(1)}, bf16[16,2048]{1,0:T(8,128)(2,1)S(1)}, u32[]{:S(2)}, u32[]{:S(2)}) collective-permute-start(bf16[16,2048]{1,0:T(8,128)(2,1)S(1)} %get-tuple-element.34), channel_id=1, source_target_pairs={{0,12},{4,8},{8,4},{12,0},{1,13},{5,9},{9,5},{13,1},{2,14},{6,10},... | collective-permute-start | bytes 196616 | tf_op jit(solution)/shard_map/ppermute | solution.py:291
  54.8 5.7 %collective-permute-start.18 = (bf16[16,2048]{1,0:T(8,128)(2,1)S(1)}, bf16[16,2048]{1,0:T(8,128)(2,1)S(1)}, u32[]{:S(2)}, u32[]{:S(2)}) collective-permute-start(bf16[16,2048]{1,0:T(8,128)(2,1)S(1)} %get-tuple-element.35), channel_id=1, source_target_pairs={{0,8},{4,12},{8,0},{12,4},{1,9},{5,13},{9,1},{13,5},{2,10},{6,14},... | collective-permute-start | bytes 196616 | tf_op jit(solution)/shard_map/ppermute | solution.py:291
  54.8 5.7 %collective-permute-start.19 = (bf16[16,2048]{1,0:T(8,128)(2,1)S(1)}, bf16[16,2048]{1,0:T(8,128)(2,1)S(1)}, u32[]{:S(2)}, u32[]{:S(2)}) collective-permute-start(bf16[16,2048]{1,0:T(8,128)(2,1)S(1)} %get-tuple-element.36), channel_id=1, source_target_pairs={{0,4},{4,0},{8,12},{12,8},{1,5},{5,1},{9,13},{13,9},{2,6},{6,2},{1... | collective-permute-start | bytes 196616 | tf_op jit(solution)/shard_map/ppermute | solution.py:291

commit v14 on v13

--- a/solution.py
+++ b/solution.py
@@ -246,14 +246,18 @@
     for piece in pieces:
         lhs_ref[at : at + piece.shape[0], :] = piece[...]
         at += piece.shape[0]
-    for a, b in pieces_of(down_ref.shape[1], 4 * TILE):
-        part = prev_ref[:, a:b] if has_acc else 0.0
+
+    @pl.loop(0, down_ref.shape[1] // (2 * TILE))
+    def _(i):
+        columns = pl.ds(pl.multiple_of(i * 2 * TILE, 2 * TILE), 2 * TILE)
+        part = prev_ref[:, columns] if has_acc else 0.0
         at = 0
         for sign, start, depth in segments:
             rows = pl.ds(pl.multiple_of(sign * where[0] + start, TILE) if sign else start, depth)
-            part += jnp.dot(lhs_ref[:, at : at + depth], down_ref[rows, a:b], preferred_element_type=jnp.float32)
+            part += jnp.dot(lhs_ref[:, at : at + depth], down_ref[rows, columns], preferred_element_type=jnp.float32)
             at += depth
-        acc_ref[:, a:b] = part
+        acc_ref[:, columns] = part
+
     if last:
         for d, out in enumerate(outs):
             source = pl.multiple_of(place(where[1], d) * ROWS, ROWS)
@@ -328,7 +332,7 @@
     acc = down(where, pieces, down_weight, acc, rest_segments, True)
 
     mixed = acc[0].astype(f32)
-    for d in (3, 2, 1):
+    for d in (1, 2, 3):
         mixed = mixed + swap(acc[d], "hid", d).astype(f32)
     return mixed.astype(bf16)
 

time: 61.3 us -> 62.8 us (1.024)
  Pallas kernels: 26.7 us -> 27.5 us
  waiting for transfers between devices: 12.4 us -> 13.1 us
    pallas_call x2, Pallas kernels: 6.06 us -> 6.93 us  [down(): pl.pallas_call(functools.partial(down_kernel, len(pieces), prev is not No...]
    ppermute x20, waiting for transfers between devices: 12.4 us -> 13.1 us  [swap(): return lax.ppermute(x, axis, [(i, i ^ step) for i in range(n)])]
where the time goes in v14:
time: 62.8 us; the launch traced here: 62.7 us
  Pallas kernels  27.5 us (44%)
  starting transfers between devices  21 us (33%)
  waiting for transfers between devices  13.1 us (21%)
  other arithmetic  0.74 us (1%)
    ppermute x20, starting transfers between devices, swap(): return lax.ppermute(x, axis, [(i, i ^ step) for i in range(n)])  21 us
    ppermute x20, waiting for transfers between devices, swap(): return lax.ppermute(x, axis, [(i, i ^ step) for i in range(n)])  13.1 us
    pallas_call x2, Pallas kernels, fetch(): pl.pallas_call(functools.partial(fetch_kernel, first), in_specs=[spec(plt...  10.2 us
    pallas_call x2, Pallas kernels, gate_up(): pl.pallas_call(functools.partial(gate_up_kernel, len(arrays), len(weights...  9.93 us
    pallas_call x2, Pallas kernels, down(): pl.pallas_call(functools.partial(down_kernel, len(pieces), prev is not No...  6.93 us
  transfers between devices with their start and end apart: 20, of which 9 were waited for; matrix products, arithmetic and copies ran while one was open for 0% of the time, Pallas kernels for 32%

profile of v14, /device:TPU:0, one launch (start us, length us, event | category | flops | bytes accessed | tf_op | source)
XLA Modules:
  0.0 62.7 jit_solution(16447509152597470126)
XLA Ops:
  0.0 5.0 %collective-permute-start.2 = (bf16[16,2048]{1,0:T(8,128)(2,1)}, bf16[16,2048]{1,0:T(8,128)(2,1)S(1)}, u32[]{:S(2)}, u32[]{:S(2)}) collective-permute-start(bf16[16,2048]{1,0:T(8,128)(2,1)} %tokens_ref.3), channel_id=1, source_target_pairs={{0,12},{4,8},{8,4},{12,0},{1,13},{5,9},{9,5},{13,1},{2,14},{6,10},... | collective-permute-start | bytes 196616 | tf_op jit(solution)/shard_map/ppermute | solution.py:295
  5.0 0.0 collective-permute-start.1
  5.1 0.6 collective-permute-start
  5.6 1.7 %collective-permute-start.3 = (bf16[16,2048]{1,0:T(8,128)(2,1)}, bf16[16,2048]{1,0:T(8,128)(2,1)S(1)}, u32[]{:S(2)}, u32[]{:S(2)}) collective-permute-start(bf16[16,2048]{1,0:T(8,128)(2,1)} %tokens_ref.3), channel_id=1, source_target_pairs={{0,16},{16,0},{1,17},{17,1},{2,18},{18,2},{3,19},{19,3},{4,20},{20... | collective-permute-start | bytes 196616 | tf_op jit(solution)/shard_map/ppermute | solution.py:295
  7.4 0.1 pad_add_fusion.where
  7.4 4.8 %fetch.2 = (bf16[2048,1280]{1,0:T(8,128)(2,1)S(1)}, bf16[2048,1280]{1,0:T(8,128)(2,1)S(1)}, bf16[16,2048]{1,0:T(8,128)(2,1)S(1)}) custom-call(s32[2]{0:T(128)S(1)} %pad_add_fusion.where, bf16[2048,6656]{1,0:T(8,128)(2,1)} %refs_2_.1, bf16[2048,6656]{1,0:T(8,128)(2,1)} %refs_3_.2, bf16[16,2048]{1,0:T(8,128)(2,1)} %tokens_ref.3), custom_call_target="tpu_custom_call" | custom-call | bytes 1024 | tf_op jit(solution)/shard_map/fetch/pallas_call | solution.py:73
  12.2 0.0 collective-permute-done.2.refs_2_
  12.3 0.0 collective-permute-done.refs_0_
  12.3 0.0 collective-permute-done.3.refs_4_.refs_2_
  12.3 0.4 collective-permute-start.4
  12.7 5.4 %fetch.3 = (bf16[2048,1280]{1,0:T(8,128)(2,1)S(1)}, bf16[2048,1280]{1,0:T(8,128)(2,1)S(1)}, bf16[16,2048]{1,0:T(8,128)(2,1)}) custom-call(s32[2]{0:T(128)S(1)} %pad_add_fusion.where, bf16[2048,6656]{1,0:T(8,128)(2,1)} %refs_2_.1, bf16[2048,6656]{1,0:T(8,128)(2,1)} %refs_3_.2, bf16[16,2048]{1,0:T(8,128)(2,1)} %tokens_ref.3), custom_call_target="tpu_custom_call" | custom-call | bytes 1024 | tf_op jit(solution)/shard_map/fetch/pallas_call | solution.py:73
  18.1 0.0 collective-permute-done.4.refs_3_
  18.1 3.6 %gate_up.2 = (bf16[2,64,2560]{2,1,0:T(8,128)(2,1)S(1)}, bf16[2,64,1280]{2,1,0:T(8,128)(2,1)S(1)}, bf16[2,64,1280]{2,1,0:T(8,128)(2,1)S(1)}) custom-call(s32[2]{0:T(128)S(1)} %pad_add_fusion.where, bf16[16,2048]{1,0:T(8,128)(2,1)S(1)} %get-tuple-element.21.refs_3_.refs_0_, bf16[48,2048]{1,0:T(8,128)(2,1)S(1)} %join.3.refs_1_, ...), custom_call_target="tpu_custom_call" | custom-call | bytes 1024 | tf_op jit(solution)/shard_map/gate_up/pallas_call | solution.py:151
  21.7 0.1 collective-permute-start.5
  21.8 0.5 collective-permute-start.6
  22.3 1.1 %collective-permute-done.5.got_ref.refs_0_ = bf16[2,64,1280]{2,1,0:T(8,128)(2,1)S(1)} collective-permute-done((bf16[2,64,1280]{2,1,0:T(8,128)(2,1)S(1)}, bf16[2,64,1280]{2,1,0:T(8,128)(2,1)S(1)}, u32[]{:S(2)}, u32[]{:S(2)}) %collective-permute-start.5) | collective-permute-done | bytes 327712 | tf_op jit(solution)/shard_map/ppermute | solution.py:295
  23.4 1.8 %collective-permute-start.7 = (bf16[2,32,1280]{2,1,0:T(8,128)(2,1)S(1)}, bf16[2,32,1280]{2,1,0:T(8,128)(2,1)S(1)}, u32[]{:S(2)}, u32[]{:S(2)}) collective-permute-start(bf16[2,32,1280]{2,1,0:T(8,128)(2,1)S(1)} %pair_sum.3.refs_4_), channel_id=1, source_target_pairs={{0,2},{1,3},{2,0},{3,1},{4,6},{5,7},{6,4},{7,5},{8,10},{9,11},{10,... | collective-permute-start | bytes 491528 | tf_op jit(solution)/shard_map/ppermute | solution.py:295
  25.2 0.0 collective-permute-done.6.got_ref.refs_1_
  25.3 0.0 slice-start.1
  25.3 0.0 slice-start.3
  25.3 0.0 slice-start.4
  25.3 0.0 slice-start.6
  25.3 0.4 collective-permute-start.8
  25.7 6.4 %gate_up.3 = (bf16[2,32,1536]{2,1,0:T(8,128)(2,1)S(1)}, bf16[2,32,1536]{2,1,0:T(8,128)(2,1)S(1)}) custom-call(s32[2]{0:T(128)S(1)} %pad_add_fusion.where, bf16[16,2048]{1,0:T(8,128)(2,1)S(1)} %get-tuple-element.21.refs_3_.refs_0_, bf16[48,2048]{1,0:T(8,128)(2,1)S(1)} %join.3.refs_1_, bf16[2048,6656]{1,0:T(8,128)(2,1)} %refs_2_.1, ...), custom_call_target="tpu_custom_call" | custom-call | bytes 1024 | tf_op jit(solution)/shard_map/gate_up/pallas_call | solution.py:151
  32.1 1.1 %collective-permute-done.8.refs_3_.refs_1_ = bf16[2,32,1280]{2,1,0:T(8,128)(2,1)S(1)} collective-permute-done((bf16[2,32,1280]{2,1,0:T(8,128)(2,1)S(1)}, bf16[2,32,1280]{2,1,0:T(8,128)(2,1)S(1)}, u32[]{:S(2)}, u32[]{:S(2)}) %collective-permute-start.8) | collective-permute-done | bytes 163872 | tf_op jit(solution)/shard_map/ppermute | solution.py:295
  33.3 0.1 collective-permute-start.10
  33.4 0.2 combine.2
  33.6 1.8 %collective-permute-start.14 = (bf16[16,2560]{1,0:T(8,128)(2,1)S(1)}, bf16[16,2560]{1,0:T(8,128)(2,1)S(1)}, u32[]{:S(2)}, u32[]{:S(2)}) collective-permute-start(bf16[16,2560]{1,0:T(8,128)(2,1)S(1)} %get-tuple-element.32.refs_0_), channel_id=1, source_target_pairs={{0,2},{1,3},{2,0},{3,1},{4,6},{5,7},{6,4},{7,5},{8,10},{9,11},{10,... | collective-permute-start | bytes 245768 | tf_op jit(solution)/shard_map/ppermute | solution.py:295
  35.4 1.2 %collective-permute-start.11 = (bf16[2,16,1536]{2,1,0:T(8,128)(2,1)S(1)}, bf16[2,16,1536]{2,1,0:T(8,128)(2,1)S(1)}, u32[]{:S(2)}, u32[]{:S(2)}) collective-permute-start(bf16[2,16,1536]{2,1,0:T(8,128)(2,1)S(1)} %pair_sum.5), channel_id=1, source_target_pairs={{0,2},{1,3},{2,0},{3,1},{4,6},{5,7},{6,4},{7,5},{8,10},{9,11},{10,... | collective-permute-start | bytes 294920 | tf_op jit(solution)/shard_map/ppermute | solution.py:295
  36.6 1.5 %collective-permute-start.9 = (bf16[16,2560]{1,0:T(8,128)(2,1)S(1)}, bf16[16,2560]{1,0:T(8,128)(2,1)S(1)}, u32[]{:S(2)}, u32[]{:S(2)}) collective-permute-start(bf16[16,2560]{1,0:T(8,128)(2,1)S(1)} %get-tuple-element.30), channel_id=1, source_target_pairs={{0,16},{16,0},{1,17},{17,1},{2,18},{18,2},{3,19},{19,3},{4,20},{20... | collective-permute-start | bytes 245768 | tf_op jit(solution)/shard_map/ppermute | solution.py:295
  38.1 0.6 collective-permute-done.14.refs_1_
  38.7 0.1 collective-permute-start.15
  38.8 2.3 %collective-permute-done.9.refs_0_ = bf16[16,2560]{1,0:T(8,128)(2,1)S(1)} collective-permute-done((bf16[16,2560]{1,0:T(8,128)(2,1)S(1)}, bf16[16,2560]{1,0:T(8,128)(2,1)S(1)}, u32[]{:S(2)}, u32[]{:S(2)}) %collective-permute-start.9) | collective-permute-done | bytes 81952 | tf_op jit(solution)/shard_map/ppermute | solution.py:295
  41.0 0.1 combine.3.refs_0_
  41.1 1.3 %collective-permute-start.12 = (bf16[16,4096]{1,0:T(8,128)(2,1)S(1)}, bf16[16,4096]{1,0:T(8,128)(2,1)S(1)}, u32[]{:S(2)}, u32[]{:S(2)}) collective-permute-start(bf16[16,4096]{1,0:T(8,128)(2,1)S(1)} %combine.3.refs_0_), channel_id=1, source_target_pairs={{0,2},{1,3},{2,0},{3,1},{4,6},{5,7},{6,4},{7,5},{8,10},{9,11},{10,... | collective-permute-start | bytes 393224 | tf_op jit(solution)/shard_map/ppermute | solution.py:295
  42.5 2.9 %down.2.refs_1_.refs_5_ = f32[64,2048]{1,0:T(8,128)S(1)} custom-call(s32[2]{0:T(128)S(1)} %pad_add_fusion.where, bf16[16,2560]{1,0:T(8,128)(2,1)S(1)} %get-tuple-element.32.refs_0_, bf16[16,2560]{1,0:T(8,128)(2,1)S(1)} %collective-permute-done.14.refs_1_, bf16[32,2560]{1,0:T(8,128)(2,1)S(1)} %collective-permute-done.15.refs_2_, bf16[6656,2048]{1,0:T(8,128)(2,1)S(1)} %bitcast.3), custom_call_target="tpu_custom_call" | custom-call | bytes 1024 | tf_op jit(solution)/shard_map/down/pallas_call | solution.py:275
  45.4 0.1 collective-permute-start.13
  45.5 0.7 %collective-permute-done.12.refs_0_.refs_1_ = bf16[16,4096]{1,0:T(8,128)(2,1)S(1)} collective-permute-done((bf16[16,4096]{1,0:T(8,128)(2,1)S(1)}, bf16[16,4096]{1,0:T(8,128)(2,1)S(1)}, u32[]{:S(2)}, u32[]{:S(2)}) %collective-permute-start.12) | collective-permute-done | bytes 131104 | tf_op jit(solution)/shard_map/ppermute | solution.py:295
  46.2 0.1 collective-permute-start.16
  46.2 0.6 collective-permute-done.13.refs_2_
  46.8 0.8 %collective-permute-done.16.refs_3_ = bf16[16,4096]{1,0:T(8,128)(2,1)S(1)} collective-permute-done((bf16[16,4096]{1,0:T(8,128)(2,1)S(1)}, bf16[16,4096]{1,0:T(8,128)(2,1)S(1)}, u32[]{:S(2)}, u32[]{:S(2)}) %collective-permute-start.16) | collective-permute-done | bytes 131104 | tf_op jit(solution)/shard_map/ppermute | solution.py:295
  47.6 4.0 %down.3 = (bf16[16,2048]{1,0:T(8,128)(2,1)S(1)}, bf16[16,2048]{1,0:T(8,128)(2,1)S(1)}, bf16[16,2048]{1,0:T(8,128)(2,1)S(1)}, bf16[16,2048]{1,0:T(8,128)(2,1)S(1)}) custom-call(s32[2]{0:T(128)S(1)} %pad_add_fusion.where, bf16[16,4096]{1,0:T(8,128)(2,1)S(1)} %combine.3.refs_0_, bf16[16,4096]{1,0:T(8,128)(2,1)S(1)} %collective-permute-done.12.refs_0_.refs_1_, ...), custom_call_target="tpu_custom_call" | custom-call | bytes 1024 | tf_op jit(solution)/shard_map/down/pallas_call | solution.py:275
  51.6 1.3 %collective-permute-start.17 = (bf16[16,2048]{1,0:T(8,128)(2,1)S(1)}, bf16[16,2048]{1,0:T(8,128)(2,1)S(1)}, u32[]{:S(2)}, u32[]{:S(2)}) collective-permute-start(bf16[16,2048]{1,0:T(8,128)(2,1)S(1)} %get-tuple-element.34), channel_id=1, source_target_pairs={{0,4},{4,0},{8,12},{12,8},{1,5},{5,1},{9,13},{13,9},{2,6},{6,2},{1... | collective-permute-start | bytes 196616 | tf_op jit(solution)/shard_map/ppermute | solution.py:295
  52.9 2.9 %collective-permute-start.18 = (bf16[16,2048]{1,0:T(8,128)(2,1)S(1)}, bf16[16,2048]{1,0:T(8,128)(2,1)S(1)}, u32[]{:S(2)}, u32[]{:S(2)}) collective-permute-start(bf16[16,2048]{1,0:T(8,128)(2,1)S(1)} %get-tuple-element.35), channel_id=1, source_target_pairs={{0,8},{4,12},{8,0},{12,4},{1,9},{5,13},{9,1},{13,5},{2,10},{6,14},... | collective-permute-start | bytes 196616 | tf_op jit(solution)/shard_map/ppermute | solution.py:295
  55.9 0.2 collective-permute-start.19
  56.1 3.8 %collective-permute-done.18 = bf16[16,2048]{1,0:T(8,128)(2,1)S(1)} collective-permute-done((bf16[16,2048]{1,0:T(8,128)(2,1)S(1)}, bf16[16,2048]{1,0:T(8,128)(2,1)S(1)}, u32[]{:S(2)}, u32[]{:S(2)}) %collective-permute-start.18) | collective-permute-done | bytes 65568 | tf_op jit(solution)/shard_map/ppermute | solution.py:295
  59.9 2.1 %collective-permute-done.19 = bf16[16,2048]{1,0:T(8,128)(2,1)S(1)} collective-permute-done((bf16[16,2048]{1,0:T(8,128)(2,1)S(1)}, bf16[16,2048]{1,0:T(8,128)(2,1)S(1)}, u32[]{:S(2)}, u32[]{:S(2)}) %collective-permute-start.19) | collective-permute-done | bytes 65568 | tf_op jit(solution)/shard_map/ppermute | solution.py:295
  62.0 0.7 %add_convert_fusion = bf16[16,2048]{1,0:T(8,128)(2,1)} fusion(bf16[16,2048]{1,0:T(8,128)(2,1)S(1)} %collective-permute-done.19, bf16[16,2048]{1,0:T(8,128)(2,1)S(1)} %collective-permute-done.18, bf16[16,2048]{1,0:T(8,128)(2,1)S(1)} %collective-permute-done.17, bf16[16,2048]{1,0:T(8,128)(2,1)S(1)} %get-tuple-element.33), kind=kLoop, calls=%fused_computation | loop fusion | flops 262144 | bytes 327680 | tf_op jit(solution)/shard_map/convert_element_type | solution.py:337
  (24 shorter events, 0.2 us)
Async XLA Ops:
  0.0 12.2 %collective-permute-start.2 = (bf16[16,2048]{1,0:T(8,128)(2,1)}, bf16[16,2048]{1,0:T(8,128)(2,1)S(1)}, u32[]{:S(2)}, u32[]{:S(2)}) collective-permute-start(bf16[16,2048]{1,0:T(8,128)(2,1)} %tokens_ref.3), channel_id=1, source_target_pairs={{0,12},{4,8},{8,4},{12,0},{1,13},{5,9},{9,5},{13,1},{2,14},{6,10},... | collective-permute-start | bytes 196616 | tf_op jit(solution)/shard_map/ppermute | solution.py:295
  5.0 7.2 %collective-permute-start.1 = (bf16[16,2048]{1,0:T(8,128)(2,1)}, bf16[16,2048]{1,0:T(8,128)(2,1)S(1)}, u32[]{:S(2)}, u32[]{:S(2)}) collective-permute-start(bf16[16,2048]{1,0:T(8,128)(2,1)} %tokens_ref.3), channel_id=1, source_target_pairs={{0,8},{4,12},{8,0},{12,4},{1,9},{5,13},{9,1},{13,5},{2,10},{6,14},... | collective-permute-start | bytes 196616 | tf_op jit(solution)/shard_map/ppermute | solution.py:295
  5.1 7.2 %collective-permute-start = (bf16[16,2048]{1,0:T(8,128)(2,1)}, bf16[16,2048]{1,0:T(8,128)(2,1)S(1)}, u32[]{:S(2)}, u32[]{:S(2)}) collective-permute-start(bf16[16,2048]{1,0:T(8,128)(2,1)} %tokens_ref.3), channel_id=1, source_target_pairs={{0,4},{4,0},{8,12},{12,8},{1,5},{5,1},{9,13},{13,9},{2,6},{6,2},{1... | collective-permute-start | bytes 196616 | tf_op jit(solution)/shard_map/ppermute | solution.py:295
  5.6 6.7 %collective-permute-start.3 = (bf16[16,2048]{1,0:T(8,128)(2,1)}, bf16[16,2048]{1,0:T(8,128)(2,1)S(1)}, u32[]{:S(2)}, u32[]{:S(2)}) collective-permute-start(bf16[16,2048]{1,0:T(8,128)(2,1)} %tokens_ref.3), channel_id=1, source_target_pairs={{0,16},{16,0},{1,17},{17,1},{2,18},{18,2},{3,19},{19,3},{4,20},{20... | collective-permute-start | bytes 196616 | tf_op jit(solution)/shard_map/ppermute | solution.py:295
  12.3 5.8 %collective-permute-start.4 = (bf16[48,2048]{1,0:T(8,128)(2,1)S(1)}, bf16[48,2048]{1,0:T(8,128)(2,1)S(1)}, u32[]{:S(2)}, u32[]{:S(2)}) collective-permute-start(bf16[48,2048]{1,0:T(8,128)(2,1)S(1)} %join.3.refs_1_), channel_id=1, source_target_pairs={{0,16},{16,0},{1,17},{17,1},{2,18},{18,2},{3,19},{19,3},{4,20},{20... | collective-permute-start | bytes 589832 | tf_op jit(solution)/shard_map/ppermute | solution.py:295
  21.7 1.7 %collective-permute-start.5 = (bf16[2,64,1280]{2,1,0:T(8,128)(2,1)S(1)}, bf16[2,64,1280]{2,1,0:T(8,128)(2,1)S(1)}, u32[]{:S(2)}, u32[]{:S(2)}) collective-permute-start(bf16[2,64,1280]{2,1,0:T(8,128)(2,1)S(1)} %get-tuple-element.27), channel_id=1, source_target_pairs={{0,1},{1,0},{2,3},{3,2},{4,5},{5,4},{6,7},{7,6},{8,9},{9,8},{10,11... | collective-permute-start | bytes 983048 | tf_op jit(solution)/shard_map/ppermute | solution.py:295
  21.8 3.4 %collective-permute-start.6 = (bf16[2,64,1280]{2,1,0:T(8,128)(2,1)S(1)}, bf16[2,64,1280]{2,1,0:T(8,128)(2,1)S(1)}, u32[]{:S(2)}, u32[]{:S(2)}) collective-permute-start(bf16[2,64,1280]{2,1,0:T(8,128)(2,1)S(1)} %get-tuple-element.28), channel_id=1, source_target_pairs={{0,1},{1,0},{2,3},{3,2},{4,5},{5,4},{6,7},{7,6},{8,9},{9,8},{10,11... | collective-permute-start | bytes 983048 | tf_op jit(solution)/shard_map/ppermute | solution.py:295
  23.4 8.7 %collective-permute-start.7 = (bf16[2,32,1280]{2,1,0:T(8,128)(2,1)S(1)}, bf16[2,32,1280]{2,1,0:T(8,128)(2,1)S(1)}, u32[]{:S(2)}, u32[]{:S(2)}) collective-permute-start(bf16[2,32,1280]{2,1,0:T(8,128)(2,1)S(1)} %pair_sum.3.refs_4_), channel_id=1, source_target_pairs={{0,2},{1,3},{2,0},{3,1},{4,6},{5,7},{6,4},{7,5},{8,10},{9,11},{10,... | collective-permute-start | bytes 491528 | tf_op jit(solution)/shard_map/ppermute | solution.py:295
  25.2 17.2 %slice-start = ((s8[27262976]{0:T(1024)(128)(4,1)}), s8[4194304]{0:T(1024)(128)(4,1)S(1)}, s32[]{:S(2)}) async-start(s8[27262976]{0:T(1024)(128)(4,1)} %bitcast.2), calls=%async_computation | async-start | bytes 8388608
  25.3 17.2 %slice-start.1 = ((s8[27262976]{0:T(1024)(128)(4,1)}), s8[4194304]{0:T(1024)(128)(4,1)S(1)}, s32[]{:S(2)}) async-start(s8[27262976]{0:T(1024)(128)(4,1)} %bitcast.2), calls=%async_computation.1 | async-start | bytes 8388608
  25.3 17.2 %slice-start.2 = ((s8[27262976]{0:T(1024)(128)(4,1)}), s8[4194304]{0:T(1024)(128)(4,1)S(1)}, s32[]{:S(2)}) async-start(s8[27262976]{0:T(1024)(128)(4,1)} %bitcast.2), calls=%async_computation.2 | async-start | bytes 8388608
  25.3 17.2 %slice-start.3 = ((s8[27262976]{0:T(1024)(128)(4,1)}), s8[4194304]{0:T(1024)(128)(4,1)S(1)}, s32[]{:S(2)}) async-start(s8[27262976]{0:T(1024)(128)(4,1)} %bitcast.2), calls=%async_computation.3 | async-start | bytes 8388608
  25.3 17.2 %slice-start.4 = ((s8[27262976]{0:T(1024)(128)(4,1)}), s8[4194304]{0:T(1024)(128)(4,1)S(1)}, s32[]{:S(2)}) async-start(s8[27262976]{0:T(1024)(128)(4,1)} %bitcast.2), calls=%async_computation.4 | async-start | bytes 8388608
  25.3 17.2 %slice-start.5 = ((s8[27262976]{0:T(1024)(128)(4,1)}), s8[4194304]{0:T(1024)(128)(4,1)S(1)}, s32[]{:S(2)}) async-start(s8[27262976]{0:T(1024)(128)(4,1)} %bitcast.2), calls=%async_computation.5 | async-start | bytes 8388608
  25.3 17.2 %slice-start.6 = ((s8[27262976]{0:T(1024)(128)(4,1)}), s8[2097152]{0:T(1024)(128)(4,1)S(1)}, s32[]{:S(2)}) async-start(s8[27262976]{0:T(1024)(128)(4,1)} %bitcast.2), calls=%async_computation.6 | async-start | bytes 4194304
  25.3 7.9 %collective-permute-start.8 = (bf16[2,32,1280]{2,1,0:T(8,128)(2,1)S(1)}, bf16[2,32,1280]{2,1,0:T(8,128)(2,1)S(1)}, u32[]{:S(2)}, u32[]{:S(2)}) collective-permute-start(bf16[2,32,1280]{2,1,0:T(8,128)(2,1)S(1)} %pair_sum.4.refs_5_), channel_id=1, source_target_pairs={{0,2},{1,3},{2,0},{3,1},{4,6},{5,7},{6,4},{7,5},{8,10},{9,11},{10,... | collective-permute-start | bytes 491528 | tf_op jit(solution)/shard_map/ppermute | solution.py:295
  33.3 2.1 %collective-permute-start.10 = (bf16[2,32,1536]{2,1,0:T(8,128)(2,1)S(1)}, bf16[2,32,1536]{2,1,0:T(8,128)(2,1)S(1)}, u32[]{:S(2)}, u32[]{:S(2)}) collective-permute-start(bf16[2,32,1536]{2,1,0:T(8,128)(2,1)S(1)} %later.1), channel_id=1, source_target_pairs={{0,1},{1,0},{2,3},{3,2},{4,5},{5,4},{6,7},{7,6},{8,9},{9,8},{10,11... | collective-permute-start | bytes 589832 | tf_op jit(solution)/shard_map/ppermute | solution.py:295
  33.6 5.1 %collective-permute-start.14 = (bf16[16,2560]{1,0:T(8,128)(2,1)S(1)}, bf16[16,2560]{1,0:T(8,128)(2,1)S(1)}, u32[]{:S(2)}, u32[]{:S(2)}) collective-permute-start(bf16[16,2560]{1,0:T(8,128)(2,1)S(1)} %get-tuple-element.32.refs_0_), channel_id=1, source_target_pairs={{0,2},{1,3},{2,0},{3,1},{4,6},{5,7},{6,4},{7,5},{8,10},{9,11},{10,... | collective-permute-start | bytes 245768 | tf_op jit(solution)/shard_map/ppermute | solution.py:295
  35.4 5.7 %collective-permute-start.11 = (bf16[2,16,1536]{2,1,0:T(8,128)(2,1)S(1)}, bf16[2,16,1536]{2,1,0:T(8,128)(2,1)S(1)}, u32[]{:S(2)}, u32[]{:S(2)}) collective-permute-start(bf16[2,16,1536]{2,1,0:T(8,128)(2,1)S(1)} %pair_sum.5), channel_id=1, source_target_pairs={{0,2},{1,3},{2,0},{3,1},{4,6},{5,7},{6,4},{7,5},{8,10},{9,11},{10,... | collective-permute-start | bytes 294920 | tf_op jit(solution)/shard_map/ppermute | solution.py:295
  36.6 4.4 %collective-permute-start.9 = (bf16[16,2560]{1,0:T(8,128)(2,1)S(1)}, bf16[16,2560]{1,0:T(8,128)(2,1)S(1)}, u32[]{:S(2)}, u32[]{:S(2)}) collective-permute-start(bf16[16,2560]{1,0:T(8,128)(2,1)S(1)} %get-tuple-element.30), channel_id=1, source_target_pairs={{0,16},{16,0},{1,17},{17,1},{2,18},{18,2},{3,19},{19,3},{4,20},{20... | collective-permute-start | bytes 245768 | tf_op jit(solution)/shard_map/ppermute | solution.py:295
  38.7 3.7 %collective-permute-start.15 = (bf16[32,2560]{1,0:T(8,128)(2,1)S(1)}, bf16[32,2560]{1,0:T(8,128)(2,1)S(1)}, u32[]{:S(2)}, u32[]{:S(2)}) collective-permute-start(bf16[32,2560]{1,0:T(8,128)(2,1)S(1)} %join.4), channel_id=1, source_target_pairs={{0,1},{1,0},{2,3},{3,2},{4,5},{5,4},{6,7},{7,6},{8,9},{9,8},{10,11... | collective-permute-start | bytes 491528 | tf_op jit(solution)/shard_map/ppermute | solution.py:295
  41.1 5.0 %collective-permute-start.12 = (bf16[16,4096]{1,0:T(8,128)(2,1)S(1)}, bf16[16,4096]{1,0:T(8,128)(2,1)S(1)}, u32[]{:S(2)}, u32[]{:S(2)}) collective-permute-start(bf16[16,4096]{1,0:T(8,128)(2,1)S(1)} %combine.3.refs_0_), channel_id=1, source_target_pairs={{0,2},{1,3},{2,0},{3,1},{4,6},{5,7},{6,4},{7,5},{8,10},{9,11},{10,... | collective-permute-start | bytes 393224 | tf_op jit(solution)/shard_map/ppermute | solution.py:295
  45.4 1.4 %collective-permute-start.13 = (bf16[16,4096]{1,0:T(8,128)(2,1)S(1)}, bf16[16,4096]{1,0:T(8,128)(2,1)S(1)}, u32[]{:S(2)}, u32[]{:S(2)}) collective-permute-start(bf16[16,4096]{1,0:T(8,128)(2,1)S(1)} %combine.3.refs_0_), channel_id=1, source_target_pairs={{0,1},{1,0},{2,3},{3,2},{4,5},{5,4},{6,7},{7,6},{8,9},{9,8},{10,11... | collective-permute-start | bytes 393224 | tf_op jit(solution)/shard_map/ppermute | solution.py:295
  46.2 1.4 %collective-permute-start.16 = (bf16[16,4096]{1,0:T(8,128)(2,1)S(1)}, bf16[16,4096]{1,0:T(8,128)(2,1)S(1)}, u32[]{:S(2)}, u32[]{:S(2)}) collective-permute-start(bf16[16,4096]{1,0:T(8,128)(2,1)S(1)} %join.5), channel_id=1, source_target_pairs={{0,1},{1,0},{2,3},{3,2},{4,5},{5,4},{6,7},{7,6},{8,9},{9,8},{10,11... | collective-permute-start | bytes 393224 | tf_op jit(solution)/shard_map/ppermute | solution.py:295
  51.6 4.5 %collective-permute-start.17 = (bf16[16,2048]{1,0:T(8,128)(2,1)S(1)}, bf16[16,2048]{1,0:T(8,128)(2,1)S(1)}, u32[]{:S(2)}, u32[]{:S(2)}) collective-permute-start(bf16[16,2048]{1,0:T(8,128)(2,1)S(1)} %get-tuple-element.34), channel_id=1, source_target_pairs={{0,4},{4,0},{8,12},{12,8},{1,5},{5,1},{9,13},{13,9},{2,6},{6,2},{1... | collective-permute-start | bytes 196616 | tf_op jit(solution)/shard_map/ppermute | solution.py:295
  52.9 7.0 %collective-permute-start.18 = (bf16[16,2048]{1,0:T(8,128)(2,1)S(1)}, bf16[16,2048]{1,0:T(8,128)(2,1)S(1)}, u32[]{:S(2)}, u32[]{:S(2)}) collective-permute-start(bf16[16,2048]{1,0:T(8,128)(2,1)S(1)} %get-tuple-element.35), channel_id=1, source_target_pairs={{0,8},{4,12},{8,0},{12,4},{1,9},{5,13},{9,1},{13,5},{2,10},{6,14},... | collective-permute-start | bytes 196616 | tf_op jit(solution)/shard_map/ppermute | solution.py:295
  55.9 6.2 %collective-permute-start.19 = (bf16[16,2048]{1,0:T(8,128)(2,1)S(1)}, bf16[16,2048]{1,0:T(8,128)(2,1)S(1)}, u32[]{:S(2)}, u32[]{:S(2)}) collective-permute-start(bf16[16,2048]{1,0:T(8,128)(2,1)S(1)} %get-tuple-element.36), channel_id=1, source_target_pairs={{0,12},{4,8},{8,4},{12,0},{1,13},{5,9},{9,5},{13,1},{2,14},{6,10},... | collective-permute-start | bytes 196616 | tf_op jit(solution)/shard_map/ppermute | solution.py:295

commit v15 on v13

--- a/solution.py
+++ b/solution.py
@@ -246,12 +246,15 @@
     for piece in pieces:
         lhs_ref[at : at + piece.shape[0], :] = piece[...]
         at += piece.shape[0]
-    for a, b in pieces_of(down_ref.shape[1], 4 * TILE):
+    lhs_ref[at:, :] = jnp.zeros_like(lhs_ref[at:, :])
+    total = at
+    for a, b in pieces_of(down_ref.shape[1], 2 * TILE):
         part = prev_ref[:, a:b] if has_acc else 0.0
         at = 0
         for sign, start, depth in segments:
             rows = pl.ds(pl.multiple_of(sign * where[0] + start, TILE) if sign else start, depth)
-            part += jnp.dot(lhs_ref[:, at : at + depth], down_ref[rows, a:b], preferred_element_type=jnp.float32)
+            product = jnp.dot(lhs_ref[:, at : at + depth], down_ref[rows, a:b], preferred_element_type=jnp.float32)
+            part += product[:total]
             at += depth
         acc_ref[:, a:b] = part
     if last:
@@ -265,7 +268,7 @@
     total = 4 * ROWS
     args = [*pieces, down_weight] + ([] if prev is None else [prev])
     sums = jax.ShapeDtypeStruct((total, width), jnp.float32)
-    scratch = [pltpu.VMEM((total, pieces[0].shape[1]), jnp.bfloat16)]
+    scratch = [pltpu.VMEM((max(total, 128), pieces[0].shape[1]), jnp.bfloat16)]
     if last:
         scratch = [pltpu.VMEM(sums.shape, sums.dtype)] + scratch
     return pl.pallas_call(

time: 61.3 us -> 60.7 us (level)
  Pallas kernels: 26.7 us -> 25.6 us
    pallas_call x2, Pallas kernels: 6.06 us -> 5.01 us  [down(): pl.pallas_call(functools.partial(down_kernel, len(pieces), prev is not No...]
  transfers between devices with their start and end apart: 20 -> 20, of which waited for: 9 -> 8; matrix products, arithmetic and copies ran while one was open for 0% -> 0% of each run, Pallas kernels for 32% -> 32%
where the time goes in v15:
time: 60.7 us; the launch traced here: 60.5 us
  Pallas kernels  25.6 us (42%)
  starting transfers between devices  21 us (35%)
  waiting for transfers between devices  12.8 us (21%)
  other arithmetic  0.74 us (1%)
    ppermute x20, starting transfers between devices, swap(): return lax.ppermute(x, axis, [(i, i ^ step) for i in range(n)])  21 us
    ppermute x20, waiting for transfers between devices, swap(): return lax.ppermute(x, axis, [(i, i ^ step) for i in range(n)])  12.8 us
    pallas_call x2, Pallas kernels, fetch(): pl.pallas_call(functools.partial(fetch_kernel, first), in_specs=[spec(plt...  10.2 us
    pallas_call x2, Pallas kernels, gate_up(): pl.pallas_call(functools.partial(gate_up_kernel, len(arrays), len(weights...  9.93 us
    pallas_call x2, Pallas kernels, down(): pl.pallas_call(functools.partial(down_kernel, len(pieces), prev is not No...  5.01 us
  transfers between devices with their start and end apart: 20, of which 8 were waited for; matrix products, arithmetic and copies ran while one was open for 0% of the time, Pallas kernels for 32%

profile of v15, /device:TPU:0, one launch (start us, length us, event | category | flops | bytes accessed | tf_op | source)
XLA Modules:
  0.0 60.5 jit_solution(310946802661603769)
XLA Ops:
  0.0 5.0 %collective-permute-start.2 = (bf16[16,2048]{1,0:T(8,128)(2,1)}, bf16[16,2048]{1,0:T(8,128)(2,1)S(1)}, u32[]{:S(2)}, u32[]{:S(2)}) collective-permute-start(bf16[16,2048]{1,0:T(8,128)(2,1)} %tokens_ref.3), channel_id=1, source_target_pairs={{0,12},{4,8},{8,4},{12,0},{1,13},{5,9},{9,5},{13,1},{2,14},{6,10},... | collective-permute-start | bytes 196616 | tf_op jit(solution)/shard_map/ppermute | solution.py:294
  5.0 0.0 collective-permute-start.1
  5.1 0.6 collective-permute-start
  5.6 1.7 %collective-permute-start.3 = (bf16[16,2048]{1,0:T(8,128)(2,1)}, bf16[16,2048]{1,0:T(8,128)(2,1)S(1)}, u32[]{:S(2)}, u32[]{:S(2)}) collective-permute-start(bf16[16,2048]{1,0:T(8,128)(2,1)} %tokens_ref.3), channel_id=1, source_target_pairs={{0,16},{16,0},{1,17},{17,1},{2,18},{18,2},{3,19},{19,3},{4,20},{20... | collective-permute-start | bytes 196616 | tf_op jit(solution)/shard_map/ppermute | solution.py:294
  7.4 0.1 pad_add_fusion.where
  7.4 4.8 %fetch.2 = (bf16[2048,1280]{1,0:T(8,128)(2,1)S(1)}, bf16[2048,1280]{1,0:T(8,128)(2,1)S(1)}, bf16[16,2048]{1,0:T(8,128)(2,1)S(1)}) custom-call(s32[2]{0:T(128)S(1)} %pad_add_fusion.where, bf16[2048,6656]{1,0:T(8,128)(2,1)} %refs_2_.1, bf16[2048,6656]{1,0:T(8,128)(2,1)} %refs_3_.2, bf16[16,2048]{1,0:T(8,128)(2,1)} %tokens_ref.3), custom_call_target="tpu_custom_call" | custom-call | bytes 1024 | tf_op jit(solution)/shard_map/fetch/pallas_call | solution.py:73
  12.3 0.0 collective-permute-done.1.refs_1_
  12.3 0.0 collective-permute-done.refs_0_
  12.3 0.4 collective-permute-start.4
  12.7 5.4 %fetch.3 = (bf16[2048,1280]{1,0:T(8,128)(2,1)S(1)}, bf16[2048,1280]{1,0:T(8,128)(2,1)S(1)}, bf16[16,2048]{1,0:T(8,128)(2,1)}) custom-call(s32[2]{0:T(128)S(1)} %pad_add_fusion.where, bf16[2048,6656]{1,0:T(8,128)(2,1)} %refs_2_.1, bf16[2048,6656]{1,0:T(8,128)(2,1)} %refs_3_.2, bf16[16,2048]{1,0:T(8,128)(2,1)} %tokens_ref.3), custom_call_target="tpu_custom_call" | custom-call | bytes 1024 | tf_op jit(solution)/shard_map/fetch/pallas_call | solution.py:73
  18.1 0.0 collective-permute-done.4.refs_3_
  18.1 3.6 %gate_up.2 = (bf16[2,64,2560]{2,1,0:T(8,128)(2,1)S(1)}, bf16[2,64,1280]{2,1,0:T(8,128)(2,1)S(1)}, bf16[2,64,1280]{2,1,0:T(8,128)(2,1)S(1)}) custom-call(s32[2]{0:T(128)S(1)} %pad_add_fusion.where, bf16[16,2048]{1,0:T(8,128)(2,1)S(1)} %get-tuple-element.21.refs_3_.refs_0_, bf16[48,2048]{1,0:T(8,128)(2,1)S(1)} %join.3.refs_1_, ...), custom_call_target="tpu_custom_call" | custom-call | bytes 1024 | tf_op jit(solution)/shard_map/gate_up/pallas_call | solution.py:151
  21.7 0.1 collective-permute-start.5
  21.8 0.5 collective-permute-start.6
  22.3 1.1 %collective-permute-done.5.got_ref.refs_0_ = bf16[2,64,1280]{2,1,0:T(8,128)(2,1)S(1)} collective-permute-done((bf16[2,64,1280]{2,1,0:T(8,128)(2,1)S(1)}, bf16[2,64,1280]{2,1,0:T(8,128)(2,1)S(1)}, u32[]{:S(2)}, u32[]{:S(2)}) %collective-permute-start.5) | collective-permute-done | bytes 327712 | tf_op jit(solution)/shard_map/ppermute | solution.py:294
  23.4 1.8 %collective-permute-start.7 = (bf16[2,32,1280]{2,1,0:T(8,128)(2,1)S(1)}, bf16[2,32,1280]{2,1,0:T(8,128)(2,1)S(1)}, u32[]{:S(2)}, u32[]{:S(2)}) collective-permute-start(bf16[2,32,1280]{2,1,0:T(8,128)(2,1)S(1)} %pair_sum.3.refs_4_), channel_id=1, source_target_pairs={{0,2},{1,3},{2,0},{3,1},{4,6},{5,7},{6,4},{7,5},{8,10},{9,11},{10,... | collective-permute-start | bytes 491528 | tf_op jit(solution)/shard_map/ppermute | solution.py:294
  25.2 0.0 collective-permute-done.6.got_ref.refs_1_
  25.3 0.0 slice-start.1
  25.3 0.0 slice-start.2
  25.3 0.0 slice-start.3
  25.3 0.0 slice-start.5
  25.3 0.0 slice-start.6
  25.3 0.4 collective-permute-start.8
  25.7 6.4 %gate_up.3 = (bf16[2,32,1536]{2,1,0:T(8,128)(2,1)S(1)}, bf16[2,32,1536]{2,1,0:T(8,128)(2,1)S(1)}) custom-call(s32[2]{0:T(128)S(1)} %pad_add_fusion.where, bf16[16,2048]{1,0:T(8,128)(2,1)S(1)} %get-tuple-element.21.refs_3_.refs_0_, bf16[48,2048]{1,0:T(8,128)(2,1)S(1)} %join.3.refs_1_, bf16[2048,6656]{1,0:T(8,128)(2,1)} %refs_2_.1, ...), custom_call_target="tpu_custom_call" | custom-call | bytes 1024 | tf_op jit(solution)/shard_map/gate_up/pallas_call | solution.py:151
  32.1 0.0 collective-permute-done.7.refs_2_.refs_0_
  32.1 1.1 %collective-permute-done.8.refs_3_.refs_1_ = bf16[2,32,1280]{2,1,0:T(8,128)(2,1)S(1)} collective-permute-done((bf16[2,32,1280]{2,1,0:T(8,128)(2,1)S(1)}, bf16[2,32,1280]{2,1,0:T(8,128)(2,1)S(1)}, u32[]{:S(2)}, u32[]{:S(2)}) %collective-permute-start.8) | collective-permute-done | bytes 163872 | tf_op jit(solution)/shard_map/ppermute | solution.py:294
  33.3 0.1 collective-permute-start.10
  33.4 0.2 combine.2
  33.6 1.8 %collective-permute-start.14 = (bf16[16,2560]{1,0:T(8,128)(2,1)S(1)}, bf16[16,2560]{1,0:T(8,128)(2,1)S(1)}, u32[]{:S(2)}, u32[]{:S(2)}) collective-permute-start(bf16[16,2560]{1,0:T(8,128)(2,1)S(1)} %get-tuple-element.32.refs_0_), channel_id=1, source_target_pairs={{0,2},{1,3},{2,0},{3,1},{4,6},{5,7},{6,4},{7,5},{8,10},{9,11},{10,... | collective-permute-start | bytes 245768 | tf_op jit(solution)/shard_map/ppermute | solution.py:294
  35.4 1.2 %collective-permute-start.11 = (bf16[2,16,1536]{2,1,0:T(8,128)(2,1)S(1)}, bf16[2,16,1536]{2,1,0:T(8,128)(2,1)S(1)}, u32[]{:S(2)}, u32[]{:S(2)}) collective-permute-start(bf16[2,16,1536]{2,1,0:T(8,128)(2,1)S(1)} %pair_sum.5), channel_id=1, source_target_pairs={{0,2},{1,3},{2,0},{3,1},{4,6},{5,7},{6,4},{7,5},{8,10},{9,11},{10,... | collective-permute-start | bytes 294920 | tf_op jit(solution)/shard_map/ppermute | solution.py:294
  36.6 1.5 %collective-permute-start.9 = (bf16[16,2560]{1,0:T(8,128)(2,1)S(1)}, bf16[16,2560]{1,0:T(8,128)(2,1)S(1)}, u32[]{:S(2)}, u32[]{:S(2)}) collective-permute-start(bf16[16,2560]{1,0:T(8,128)(2,1)S(1)} %get-tuple-element.30), channel_id=1, source_target_pairs={{0,16},{16,0},{1,17},{17,1},{2,18},{18,2},{3,19},{19,3},{4,20},{20... | collective-permute-start | bytes 245768 | tf_op jit(solution)/shard_map/ppermute | solution.py:294
  38.1 0.6 collective-permute-done.14.refs_1_
  38.7 0.1 collective-permute-start.15
  38.8 2.3 %collective-permute-done.9.refs_0_ = bf16[16,2560]{1,0:T(8,128)(2,1)S(1)} collective-permute-done((bf16[16,2560]{1,0:T(8,128)(2,1)S(1)}, bf16[16,2560]{1,0:T(8,128)(2,1)S(1)}, u32[]{:S(2)}, u32[]{:S(2)}) %collective-permute-start.9) | collective-permute-done | bytes 81952 | tf_op jit(solution)/shard_map/ppermute | solution.py:294
  41.0 0.1 combine.3.refs_0_
  41.1 1.3 %collective-permute-start.12 = (bf16[16,4096]{1,0:T(8,128)(2,1)S(1)}, bf16[16,4096]{1,0:T(8,128)(2,1)S(1)}, u32[]{:S(2)}, u32[]{:S(2)}) collective-permute-start(bf16[16,4096]{1,0:T(8,128)(2,1)S(1)} %combine.3.refs_0_), channel_id=1, source_target_pairs={{0,2},{1,3},{2,0},{3,1},{4,6},{5,7},{6,4},{7,5},{8,10},{9,11},{10,... | collective-permute-start | bytes 393224 | tf_op jit(solution)/shard_map/ppermute | solution.py:294
  42.5 2.1 %down.2.refs_1_.refs_5_ = f32[64,2048]{1,0:T(8,128)S(1)} custom-call(s32[2]{0:T(128)S(1)} %pad_add_fusion.where, bf16[16,2560]{1,0:T(8,128)(2,1)S(1)} %get-tuple-element.32.refs_0_, bf16[16,2560]{1,0:T(8,128)(2,1)S(1)} %collective-permute-done.14.refs_1_, bf16[32,2560]{1,0:T(8,128)(2,1)S(1)} %collective-permute-done.15.refs_2_, bf16[6656,2048]{1,0:T(8,128)(2,1)S(1)} %bitcast.3), custom_call_target="tpu_custom_call" | custom-call | bytes 1024 | tf_op jit(solution)/shard_map/down/pallas_call | solution.py:274
  44.6 0.1 collective-permute-start.13
  44.6 1.5 %collective-permute-done.12.refs_0_.refs_1_ = bf16[16,4096]{1,0:T(8,128)(2,1)S(1)} collective-permute-done((bf16[16,4096]{1,0:T(8,128)(2,1)S(1)}, bf16[16,4096]{1,0:T(8,128)(2,1)S(1)}, u32[]{:S(2)}, u32[]{:S(2)}) %collective-permute-start.12) | collective-permute-done | bytes 131104 | tf_op jit(solution)/shard_map/ppermute | solution.py:294
  46.2 0.1 collective-permute-start.16
  46.2 1.3 %collective-permute-done.16.refs_3_ = bf16[16,4096]{1,0:T(8,128)(2,1)S(1)} collective-permute-done((bf16[16,4096]{1,0:T(8,128)(2,1)S(1)}, bf16[16,4096]{1,0:T(8,128)(2,1)S(1)}, u32[]{:S(2)}, u32[]{:S(2)}) %collective-permute-start.16) | collective-permute-done | bytes 131104 | tf_op jit(solution)/shard_map/ppermute | solution.py:294
  47.6 2.9 %down.3 = (bf16[16,2048]{1,0:T(8,128)(2,1)S(1)}, bf16[16,2048]{1,0:T(8,128)(2,1)S(1)}, bf16[16,2048]{1,0:T(8,128)(2,1)S(1)}, bf16[16,2048]{1,0:T(8,128)(2,1)S(1)}) custom-call(s32[2]{0:T(128)S(1)} %pad_add_fusion.where, bf16[16,4096]{1,0:T(8,128)(2,1)S(1)} %combine.3.refs_0_, bf16[16,4096]{1,0:T(8,128)(2,1)S(1)} %collective-permute-done.12.refs_0_.refs_1_, ...), custom_call_target="tpu_custom_call" | custom-call | bytes 1024 | tf_op jit(solution)/shard_map/down/pallas_call | solution.py:274
  50.5 3.7 %collective-permute-start.17 = (bf16[16,2048]{1,0:T(8,128)(2,1)S(1)}, bf16[16,2048]{1,0:T(8,128)(2,1)S(1)}, u32[]{:S(2)}, u32[]{:S(2)}) collective-permute-start(bf16[16,2048]{1,0:T(8,128)(2,1)S(1)} %get-tuple-element.34), channel_id=1, source_target_pairs={{0,12},{4,8},{8,4},{12,0},{1,13},{5,9},{9,5},{13,1},{2,14},{6,10},... | collective-permute-start | bytes 196616 | tf_op jit(solution)/shard_map/ppermute | solution.py:294
  54.2 0.8 %collective-permute-start.19 = (bf16[16,2048]{1,0:T(8,128)(2,1)S(1)}, bf16[16,2048]{1,0:T(8,128)(2,1)S(1)}, u32[]{:S(2)}, u32[]{:S(2)}) collective-permute-start(bf16[16,2048]{1,0:T(8,128)(2,1)S(1)} %get-tuple-element.36), channel_id=1, source_target_pairs={{0,4},{4,0},{8,12},{12,8},{1,5},{5,1},{9,13},{13,9},{2,6},{6,2},{1... | collective-permute-start | bytes 196616 | tf_op jit(solution)/shard_map/ppermute | solution.py:294
  55.0 2.3 %collective-permute-done.17 = bf16[16,2048]{1,0:T(8,128)(2,1)S(1)} collective-permute-done((bf16[16,2048]{1,0:T(8,128)(2,1)S(1)}, bf16[16,2048]{1,0:T(8,128)(2,1)S(1)}, u32[]{:S(2)}, u32[]{:S(2)}) %collective-permute-start.17) | collective-permute-done | bytes 65568 | tf_op jit(solution)/shard_map/ppermute | solution.py:294
  57.3 2.6 %collective-permute-done.18 = bf16[16,2048]{1,0:T(8,128)(2,1)S(1)} collective-permute-done((bf16[16,2048]{1,0:T(8,128)(2,1)S(1)}, bf16[16,2048]{1,0:T(8,128)(2,1)S(1)}, u32[]{:S(2)}, u32[]{:S(2)}) %collective-permute-start.18) | collective-permute-done | bytes 65568 | tf_op jit(solution)/shard_map/ppermute | solution.py:294
  59.9 0.0 collective-permute-done.19
  59.9 0.7 %add_convert_fusion = bf16[16,2048]{1,0:T(8,128)(2,1)} fusion(bf16[16,2048]{1,0:T(8,128)(2,1)S(1)} %collective-permute-done.19, bf16[16,2048]{1,0:T(8,128)(2,1)S(1)} %collective-permute-done.18, bf16[16,2048]{1,0:T(8,128)(2,1)S(1)} %collective-permute-done.17, bf16[16,2048]{1,0:T(8,128)(2,1)S(1)} %get-tuple-element.33), kind=kLoop, calls=%fused_computation | loop fusion | flops 262144 | bytes 327680 | tf_op jit(solution)/shard_map/convert_element_type | solution.py:336
  (24 shorter events, 0.2 us)
Async XLA Ops:
  0.0 12.2 %collective-permute-start.2 = (bf16[16,2048]{1,0:T(8,128)(2,1)}, bf16[16,2048]{1,0:T(8,128)(2,1)S(1)}, u32[]{:S(2)}, u32[]{:S(2)}) collective-permute-start(bf16[16,2048]{1,0:T(8,128)(2,1)} %tokens_ref.3), channel_id=1, source_target_pairs={{0,12},{4,8},{8,4},{12,0},{1,13},{5,9},{9,5},{13,1},{2,14},{6,10},... | collective-permute-start | bytes 196616 | tf_op jit(solution)/shard_map/ppermute | solution.py:294
  5.0 7.2 %collective-permute-start.1 = (bf16[16,2048]{1,0:T(8,128)(2,1)}, bf16[16,2048]{1,0:T(8,128)(2,1)S(1)}, u32[]{:S(2)}, u32[]{:S(2)}) collective-permute-start(bf16[16,2048]{1,0:T(8,128)(2,1)} %tokens_ref.3), channel_id=1, source_target_pairs={{0,8},{4,12},{8,0},{12,4},{1,9},{5,13},{9,1},{13,5},{2,10},{6,14},... | collective-permute-start | bytes 196616 | tf_op jit(solution)/shard_map/ppermute | solution.py:294
  5.1 7.2 %collective-permute-start = (bf16[16,2048]{1,0:T(8,128)(2,1)}, bf16[16,2048]{1,0:T(8,128)(2,1)S(1)}, u32[]{:S(2)}, u32[]{:S(2)}) collective-permute-start(bf16[16,2048]{1,0:T(8,128)(2,1)} %tokens_ref.3), channel_id=1, source_target_pairs={{0,4},{4,0},{8,12},{12,8},{1,5},{5,1},{9,13},{13,9},{2,6},{6,2},{1... | collective-permute-start | bytes 196616 | tf_op jit(solution)/shard_map/ppermute | solution.py:294
  5.6 6.7 %collective-permute-start.3 = (bf16[16,2048]{1,0:T(8,128)(2,1)}, bf16[16,2048]{1,0:T(8,128)(2,1)S(1)}, u32[]{:S(2)}, u32[]{:S(2)}) collective-permute-start(bf16[16,2048]{1,0:T(8,128)(2,1)} %tokens_ref.3), channel_id=1, source_target_pairs={{0,16},{16,0},{1,17},{17,1},{2,18},{18,2},{3,19},{19,3},{4,20},{20... | collective-permute-start | bytes 196616 | tf_op jit(solution)/shard_map/ppermute | solution.py:294
  12.3 5.8 %collective-permute-start.4 = (bf16[48,2048]{1,0:T(8,128)(2,1)S(1)}, bf16[48,2048]{1,0:T(8,128)(2,1)S(1)}, u32[]{:S(2)}, u32[]{:S(2)}) collective-permute-start(bf16[48,2048]{1,0:T(8,128)(2,1)S(1)} %join.3.refs_1_), channel_id=1, source_target_pairs={{0,16},{16,0},{1,17},{17,1},{2,18},{18,2},{3,19},{19,3},{4,20},{20... | collective-permute-start | bytes 589832 | tf_op jit(solution)/shard_map/ppermute | solution.py:294
  21.7 1.7 %collective-permute-start.5 = (bf16[2,64,1280]{2,1,0:T(8,128)(2,1)S(1)}, bf16[2,64,1280]{2,1,0:T(8,128)(2,1)S(1)}, u32[]{:S(2)}, u32[]{:S(2)}) collective-permute-start(bf16[2,64,1280]{2,1,0:T(8,128)(2,1)S(1)} %get-tuple-element.27), channel_id=1, source_target_pairs={{0,1},{1,0},{2,3},{3,2},{4,5},{5,4},{6,7},{7,6},{8,9},{9,8},{10,11... | collective-permute-start | bytes 983048 | tf_op jit(solution)/shard_map/ppermute | solution.py:294
  21.8 3.4 %collective-permute-start.6 = (bf16[2,64,1280]{2,1,0:T(8,128)(2,1)S(1)}, bf16[2,64,1280]{2,1,0:T(8,128)(2,1)S(1)}, u32[]{:S(2)}, u32[]{:S(2)}) collective-permute-start(bf16[2,64,1280]{2,1,0:T(8,128)(2,1)S(1)} %get-tuple-element.28), channel_id=1, source_target_pairs={{0,1},{1,0},{2,3},{3,2},{4,5},{5,4},{6,7},{7,6},{8,9},{9,8},{10,11... | collective-permute-start | bytes 983048 | tf_op jit(solution)/shard_map/ppermute | solution.py:294
  23.4 8.7 %collective-permute-start.7 = (bf16[2,32,1280]{2,1,0:T(8,128)(2,1)S(1)}, bf16[2,32,1280]{2,1,0:T(8,128)(2,1)S(1)}, u32[]{:S(2)}, u32[]{:S(2)}) collective-permute-start(bf16[2,32,1280]{2,1,0:T(8,128)(2,1)S(1)} %pair_sum.3.refs_4_), channel_id=1, source_target_pairs={{0,2},{1,3},{2,0},{3,1},{4,6},{5,7},{6,4},{7,5},{8,10},{9,11},{10,... | collective-permute-start | bytes 491528 | tf_op jit(solution)/shard_map/ppermute | solution.py:294
  25.2 17.2 %slice-start = ((s8[27262976]{0:T(1024)(128)(4,1)}), s8[4194304]{0:T(1024)(128)(4,1)S(1)}, s32[]{:S(2)}) async-start(s8[27262976]{0:T(1024)(128)(4,1)} %bitcast.2), calls=%async_computation | async-start | bytes 8388608
  25.3 17.2 %slice-start.1 = ((s8[27262976]{0:T(1024)(128)(4,1)}), s8[4194304]{0:T(1024)(128)(4,1)S(1)}, s32[]{:S(2)}) async-start(s8[27262976]{0:T(1024)(128)(4,1)} %bitcast.2), calls=%async_computation.1 | async-start | bytes 8388608
  25.3 17.2 %slice-start.2 = ((s8[27262976]{0:T(1024)(128)(4,1)}), s8[4194304]{0:T(1024)(128)(4,1)S(1)}, s32[]{:S(2)}) async-start(s8[27262976]{0:T(1024)(128)(4,1)} %bitcast.2), calls=%async_computation.2 | async-start | bytes 8388608
  25.3 17.2 %slice-start.3 = ((s8[27262976]{0:T(1024)(128)(4,1)}), s8[4194304]{0:T(1024)(128)(4,1)S(1)}, s32[]{:S(2)}) async-start(s8[27262976]{0:T(1024)(128)(4,1)} %bitcast.2), calls=%async_computation.3 | async-start | bytes 8388608
  25.3 17.2 %slice-start.4 = ((s8[27262976]{0:T(1024)(128)(4,1)}), s8[4194304]{0:T(1024)(128)(4,1)S(1)}, s32[]{:S(2)}) async-start(s8[27262976]{0:T(1024)(128)(4,1)} %bitcast.2), calls=%async_computation.4 | async-start | bytes 8388608
  25.3 17.2 %slice-start.5 = ((s8[27262976]{0:T(1024)(128)(4,1)}), s8[4194304]{0:T(1024)(128)(4,1)S(1)}, s32[]{:S(2)}) async-start(s8[27262976]{0:T(1024)(128)(4,1)} %bitcast.2), calls=%async_computation.5 | async-start | bytes 8388608
  25.3 17.2 %slice-start.6 = ((s8[27262976]{0:T(1024)(128)(4,1)}), s8[2097152]{0:T(1024)(128)(4,1)S(1)}, s32[]{:S(2)}) async-start(s8[27262976]{0:T(1024)(128)(4,1)} %bitcast.2), calls=%async_computation.6 | async-start | bytes 4194304
  25.3 7.9 %collective-permute-start.8 = (bf16[2,32,1280]{2,1,0:T(8,128)(2,1)S(1)}, bf16[2,32,1280]{2,1,0:T(8,128)(2,1)S(1)}, u32[]{:S(2)}, u32[]{:S(2)}) collective-permute-start(bf16[2,32,1280]{2,1,0:T(8,128)(2,1)S(1)} %pair_sum.4.refs_5_), channel_id=1, source_target_pairs={{0,2},{1,3},{2,0},{3,1},{4,6},{5,7},{6,4},{7,5},{8,10},{9,11},{10,... | collective-permute-start | bytes 491528 | tf_op jit(solution)/shard_map/ppermute | solution.py:294
  33.3 2.1 %collective-permute-start.10 = (bf16[2,32,1536]{2,1,0:T(8,128)(2,1)S(1)}, bf16[2,32,1536]{2,1,0:T(8,128)(2,1)S(1)}, u32[]{:S(2)}, u32[]{:S(2)}) collective-permute-start(bf16[2,32,1536]{2,1,0:T(8,128)(2,1)S(1)} %later.1), channel_id=1, source_target_pairs={{0,1},{1,0},{2,3},{3,2},{4,5},{5,4},{6,7},{7,6},{8,9},{9,8},{10,11... | collective-permute-start | bytes 589832 | tf_op jit(solution)/shard_map/ppermute | solution.py:294
  33.6 5.1 %collective-permute-start.14 = (bf16[16,2560]{1,0:T(8,128)(2,1)S(1)}, bf16[16,2560]{1,0:T(8,128)(2,1)S(1)}, u32[]{:S(2)}, u32[]{:S(2)}) collective-permute-start(bf16[16,2560]{1,0:T(8,128)(2,1)S(1)} %get-tuple-element.32.refs_0_), channel_id=1, source_target_pairs={{0,2},{1,3},{2,0},{3,1},{4,6},{5,7},{6,4},{7,5},{8,10},{9,11},{10,... | collective-permute-start | bytes 245768 | tf_op jit(solution)/shard_map/ppermute | solution.py:294
  35.4 5.7 %collective-permute-start.11 = (bf16[2,16,1536]{2,1,0:T(8,128)(2,1)S(1)}, bf16[2,16,1536]{2,1,0:T(8,128)(2,1)S(1)}, u32[]{:S(2)}, u32[]{:S(2)}) collective-permute-start(bf16[2,16,1536]{2,1,0:T(8,128)(2,1)S(1)} %pair_sum.5), channel_id=1, source_target_pairs={{0,2},{1,3},{2,0},{3,1},{4,6},{5,7},{6,4},{7,5},{8,10},{9,11},{10,... | collective-permute-start | bytes 294920 | tf_op jit(solution)/shard_map/ppermute | solution.py:294
  36.6 4.4 %collective-permute-start.9 = (bf16[16,2560]{1,0:T(8,128)(2,1)S(1)}, bf16[16,2560]{1,0:T(8,128)(2,1)S(1)}, u32[]{:S(2)}, u32[]{:S(2)}) collective-permute-start(bf16[16,2560]{1,0:T(8,128)(2,1)S(1)} %get-tuple-element.30), channel_id=1, source_target_pairs={{0,16},{16,0},{1,17},{17,1},{2,18},{18,2},{3,19},{19,3},{4,20},{20... | collective-permute-start | bytes 245768 | tf_op jit(solution)/shard_map/ppermute | solution.py:294
  38.7 3.7 %collective-permute-start.15 = (bf16[32,2560]{1,0:T(8,128)(2,1)S(1)}, bf16[32,2560]{1,0:T(8,128)(2,1)S(1)}, u32[]{:S(2)}, u32[]{:S(2)}) collective-permute-start(bf16[32,2560]{1,0:T(8,128)(2,1)S(1)} %join.4), channel_id=1, source_target_pairs={{0,1},{1,0},{2,3},{3,2},{4,5},{5,4},{6,7},{7,6},{8,9},{9,8},{10,11... | collective-permute-start | bytes 491528 | tf_op jit(solution)/shard_map/ppermute | solution.py:294
  41.1 5.0 %collective-permute-start.12 = (bf16[16,4096]{1,0:T(8,128)(2,1)S(1)}, bf16[16,4096]{1,0:T(8,128)(2,1)S(1)}, u32[]{:S(2)}, u32[]{:S(2)}) collective-permute-start(bf16[16,4096]{1,0:T(8,128)(2,1)S(1)} %combine.3.refs_0_), channel_id=1, source_target_pairs={{0,2},{1,3},{2,0},{3,1},{4,6},{5,7},{6,4},{7,5},{8,10},{9,11},{10,... | collective-permute-start | bytes 393224 | tf_op jit(solution)/shard_map/ppermute | solution.py:294
  44.6 1.7 %collective-permute-start.13 = (bf16[16,4096]{1,0:T(8,128)(2,1)S(1)}, bf16[16,4096]{1,0:T(8,128)(2,1)S(1)}, u32[]{:S(2)}, u32[]{:S(2)}) collective-permute-start(bf16[16,4096]{1,0:T(8,128)(2,1)S(1)} %combine.3.refs_0_), channel_id=1, source_target_pairs={{0,1},{1,0},{2,3},{3,2},{4,5},{5,4},{6,7},{7,6},{8,9},{9,8},{10,11... | collective-permute-start | bytes 393224 | tf_op jit(solution)/shard_map/ppermute | solution.py:294
  46.2 1.4 %collective-permute-start.16 = (bf16[16,4096]{1,0:T(8,128)(2,1)S(1)}, bf16[16,4096]{1,0:T(8,128)(2,1)S(1)}, u32[]{:S(2)}, u32[]{:S(2)}) collective-permute-start(bf16[16,4096]{1,0:T(8,128)(2,1)S(1)} %join.5), channel_id=1, source_target_pairs={{0,1},{1,0},{2,3},{3,2},{4,5},{5,4},{6,7},{7,6},{8,9},{9,8},{10,11... | collective-permute-start | bytes 393224 | tf_op jit(solution)/shard_map/ppermute | solution.py:294
  50.5 6.7 %collective-permute-start.17 = (bf16[16,2048]{1,0:T(8,128)(2,1)S(1)}, bf16[16,2048]{1,0:T(8,128)(2,1)S(1)}, u32[]{:S(2)}, u32[]{:S(2)}) collective-permute-start(bf16[16,2048]{1,0:T(8,128)(2,1)S(1)} %get-tuple-element.34), channel_id=1, source_target_pairs={{0,12},{4,8},{8,4},{12,0},{1,13},{5,9},{9,5},{13,1},{2,14},{6,10},... | collective-permute-start | bytes 196616 | tf_op jit(solution)/shard_map/ppermute | solution.py:294
  54.2 5.7 %collective-permute-start.18 = (bf16[16,2048]{1,0:T(8,128)(2,1)S(1)}, bf16[16,2048]{1,0:T(8,128)(2,1)S(1)}, u32[]{:S(2)}, u32[]{:S(2)}) collective-permute-start(bf16[16,2048]{1,0:T(8,128)(2,1)S(1)} %get-tuple-element.35), channel_id=1, source_target_pairs={{0,8},{4,12},{8,0},{12,4},{1,9},{5,13},{9,1},{13,5},{2,10},{6,14},... | collective-permute-start | bytes 196616 | tf_op jit(solution)/shard_map/ppermute | solution.py:294
  54.2 5.7 %collective-permute-start.19 = (bf16[16,2048]{1,0:T(8,128)(2,1)S(1)}, bf16[16,2048]{1,0:T(8,128)(2,1)S(1)}, u32[]{:S(2)}, u32[]{:S(2)}) collective-permute-start(bf16[16,2048]{1,0:T(8,128)(2,1)S(1)} %get-tuple-element.36), channel_id=1, source_target_pairs={{0,4},{4,0},{8,12},{12,8},{1,5},{5,1},{9,13},{13,9},{2,6},{6,2},{1... | collective-permute-start | bytes 196616 | tf_op jit(solution)/shard_map/ppermute | solution.py:294

commit v16 on v15

--- a/solution.py
+++ b/solution.py
@@ -320,15 +320,14 @@
 
     keep, give = combine(mine, gots, from_chips, [])
     far_columns = swap(give, "rep", 1)
-    (rest,) = combine(last_mine, [last_got], [last_from_chip], [far_columns])
-    rest_segments = [(-1, half, bounds[2])] + [(0, start, width) for start, width in segments]
-
-    other = swap(keep, "wid", 2)
-    pieces = [keep, other, swap(join([keep, other], []), "wid", 1)]
-    acc = down(where, pieces, down_weight, None, [(1, 0, bounds[2])], False)
-    other = swap(rest, "wid", 2)
-    pieces = [rest, other, swap(rest, "wid", 1), swap(join([other], [acc]), "wid", 1)]
-    acc = down(where, pieces, down_weight, acc, rest_segments, True)
+    (rest,) = combine(last_mine, [last_got], [last_from_chip], [])
+    static = [(0, start, width) for start, width in segments]
+    acc, behind = None, [far_columns]
+    for hidden, parts in ((keep, [(1, 0, bounds[2])]), (far_columns, [(-1, half, bounds[2])]), (rest, static)):
+        other = swap(hidden, "wid", 2)
+        pieces = [hidden, other, swap(hidden, "wid", 1), swap(join([other], behind), "wid", 1)]
+        acc = down(where, pieces, down_weight, acc, parts, hidden is rest)
+        behind = [acc] if hidden is keep else []
 
     mixed = acc[0].astype(f32)
     for d in (3, 2, 1):

time: 60.7 us -> 61.2 us (level)
  waiting for transfers between devices: 12.8 us -> 10.5 us
  starting transfers between devices: 21 us -> 23.2 us
  Pallas kernels: 25.6 us -> 26.3 us
    ppermute x20 -> x24, waiting for transfers between devices: 12.8 us -> 10.5 us  [swap(): return lax.ppermute(x, axis, [(i, i ^ step) for i in range(n)])]
    ppermute x20 -> x24, starting transfers between devices: 21 us -> 23.2 us  [swap(): return lax.ppermute(x, axis, [(i, i ^ step) for i in range(n)])]
    pallas_call x2 -> x3, Pallas kernels: 5.01 us -> 5.7 us  [down(): pl.pallas_call(functools.partial(down_kernel, len(pieces), prev is not No...]
  transfers between devices with their start and end apart: 20 -> 24, of which waited for: 8 -> 7; matrix products, arithmetic and copies ran while one was open for 0% -> 0% of each run, Pallas kernels for 32% -> 35%
where the time goes in v16:
time: 61.2 us; the launch traced here: 61.1 us
  Pallas kernels  26.3 us (43%)
  starting transfers between devices  23.2 us (38%)
  waiting for transfers between devices  10.5 us (17%)
  other arithmetic  0.74 us (1%)
    ppermute x24, starting transfers between devices, swap(): return lax.ppermute(x, axis, [(i, i ^ step) for i in range(n)])  23.2 us
    ppermute x24, waiting for transfers between devices, swap(): return lax.ppermute(x, axis, [(i, i ^ step) for i in range(n)])  10.5 us
    pallas_call x2, Pallas kernels, fetch(): pl.pallas_call(functools.partial(fetch_kernel, first), in_specs=[spec(plt...  10.2 us
    pallas_call x2, Pallas kernels, gate_up(): pl.pallas_call(functools.partial(gate_up_kernel, len(arrays), len(weights...  9.93 us
    pallas_call x3, Pallas kernels, down(): pl.pallas_call(functools.partial(down_kernel, len(pieces), prev is not No...  5.7 us
  transfers between devices with their start and end apart: 24, of which 7 were waited for; matrix products, arithmetic and copies ran while one was open for 0% of the time, Pallas kernels for 35%

profile of v16, /device:TPU:0, one launch (start us, length us, event | category | flops | bytes accessed | tf_op | source)
XLA Modules:
  0.0 61.1 jit_solution(5108078706112022263)
XLA Ops:
  0.0 5.0 %collective-permute-start.2 = (bf16[16,2048]{1,0:T(8,128)(2,1)}, bf16[16,2048]{1,0:T(8,128)(2,1)S(1)}, u32[]{:S(2)}, u32[]{:S(2)}) collective-permute-start(bf16[16,2048]{1,0:T(8,128)(2,1)} %tokens_ref.3), channel_id=1, source_target_pairs={{0,12},{4,8},{8,4},{12,0},{1,13},{5,9},{9,5},{13,1},{2,14},{6,10},... | collective-permute-start | bytes 196616 | tf_op jit(solution)/shard_map/ppermute | solution.py:294
  5.1 0.6 collective-permute-start
  5.6 1.7 %collective-permute-start.3 = (bf16[16,2048]{1,0:T(8,128)(2,1)}, bf16[16,2048]{1,0:T(8,128)(2,1)S(1)}, u32[]{:S(2)}, u32[]{:S(2)}) collective-permute-start(bf16[16,2048]{1,0:T(8,128)(2,1)} %tokens_ref.3), channel_id=1, source_target_pairs={{0,16},{16,0},{1,17},{17,1},{2,18},{18,2},{3,19},{19,3},{4,20},{20... | collective-permute-start | bytes 196616 | tf_op jit(solution)/shard_map/ppermute | solution.py:294
  7.4 0.1 pad_add_fusion.where
  7.4 4.8 %fetch.2 = (bf16[2048,1280]{1,0:T(8,128)(2,1)S(1)}, bf16[2048,1280]{1,0:T(8,128)(2,1)S(1)}, bf16[16,2048]{1,0:T(8,128)(2,1)S(1)}) custom-call(s32[2]{0:T(128)S(1)} %pad_add_fusion.where, bf16[2048,6656]{1,0:T(8,128)(2,1)} %refs_2_.1, bf16[2048,6656]{1,0:T(8,128)(2,1)} %refs_3_.1, bf16[16,2048]{1,0:T(8,128)(2,1)} %tokens_ref.3), custom_call_target="tpu_custom_call" | custom-call | bytes 1024 | tf_op jit(solution)/shard_map/fetch/pallas_call | solution.py:73
  12.2 0.0 collective-permute-done.2.refs_2_
  12.3 0.0 collective-permute-done.refs_0_
  12.3 0.0 collective-permute-done.3.refs_4_.refs_2_
  12.3 0.4 collective-permute-start.4
  12.7 5.4 %fetch.3 = (bf16[2048,1280]{1,0:T(8,128)(2,1)S(1)}, bf16[2048,1280]{1,0:T(8,128)(2,1)S(1)}, bf16[16,2048]{1,0:T(8,128)(2,1)}) custom-call(s32[2]{0:T(128)S(1)} %pad_add_fusion.where, bf16[2048,6656]{1,0:T(8,128)(2,1)} %refs_2_.1, bf16[2048,6656]{1,0:T(8,128)(2,1)} %refs_3_.1, bf16[16,2048]{1,0:T(8,128)(2,1)} %tokens_ref.3), custom_call_target="tpu_custom_call" | custom-call | bytes 1024 | tf_op jit(solution)/shard_map/fetch/pallas_call | solution.py:73
  18.1 3.6 %gate_up.2 = (bf16[2,64,2560]{2,1,0:T(8,128)(2,1)S(1)}, bf16[2,64,1280]{2,1,0:T(8,128)(2,1)S(1)}, bf16[2,64,1280]{2,1,0:T(8,128)(2,1)S(1)}) custom-call(s32[2]{0:T(128)S(1)} %pad_add_fusion.where, bf16[16,2048]{1,0:T(8,128)(2,1)S(1)} %get-tuple-element.21.refs_3_.refs_0_, bf16[48,2048]{1,0:T(8,128)(2,1)S(1)} %join.4.refs_1_, ...), custom_call_target="tpu_custom_call" | custom-call | bytes 1024 | tf_op jit(solution)/shard_map/gate_up/pallas_call | solution.py:151
  21.7 0.1 collective-permute-start.5
  21.8 0.5 collective-permute-start.6
  22.3 1.1 %collective-permute-done.5.got_ref.refs_0_ = bf16[2,64,1280]{2,1,0:T(8,128)(2,1)S(1)} collective-permute-done((bf16[2,64,1280]{2,1,0:T(8,128)(2,1)S(1)}, bf16[2,64,1280]{2,1,0:T(8,128)(2,1)S(1)}, u32[]{:S(2)}, u32[]{:S(2)}) %collective-permute-start.5) | collective-permute-done | bytes 327712 | tf_op jit(solution)/shard_map/ppermute | solution.py:294
  23.4 1.8 %collective-permute-start.7 = (bf16[2,32,1280]{2,1,0:T(8,128)(2,1)S(1)}, bf16[2,32,1280]{2,1,0:T(8,128)(2,1)S(1)}, u32[]{:S(2)}, u32[]{:S(2)}) collective-permute-start(bf16[2,32,1280]{2,1,0:T(8,128)(2,1)S(1)} %pair_sum.3.refs_4_), channel_id=1, source_target_pairs={{0,2},{1,3},{2,0},{3,1},{4,6},{5,7},{6,4},{7,5},{8,10},{9,11},{10,... | collective-permute-start | bytes 491528 | tf_op jit(solution)/shard_map/ppermute | solution.py:294
  25.2 0.0 collective-permute-done.6.got_ref.refs_1_
  25.3 0.0 slice-start.1
  25.3 0.0 slice-start.3
  25.3 0.0 slice-start.4
  25.3 0.0 slice-start.6
  25.3 0.4 collective-permute-start.8
  25.7 6.4 %gate_up.3 = (bf16[2,32,1536]{2,1,0:T(8,128)(2,1)S(1)}, bf16[2,32,1536]{2,1,0:T(8,128)(2,1)S(1)}) custom-call(s32[2]{0:T(128)S(1)} %pad_add_fusion.where, bf16[16,2048]{1,0:T(8,128)(2,1)S(1)} %get-tuple-element.21.refs_3_.refs_0_, bf16[48,2048]{1,0:T(8,128)(2,1)S(1)} %join.4.refs_1_, bf16[2048,6656]{1,0:T(8,128)(2,1)} %refs_2_.1, ...), custom_call_target="tpu_custom_call" | custom-call | bytes 1024 | tf_op jit(solution)/shard_map/gate_up/pallas_call | solution.py:151
  32.1 1.1 %collective-permute-done.8.refs_1_.refs_3_ = bf16[2,32,1280]{2,1,0:T(8,128)(2,1)S(1)} collective-permute-done((bf16[2,32,1280]{2,1,0:T(8,128)(2,1)S(1)}, bf16[2,32,1280]{2,1,0:T(8,128)(2,1)S(1)}, u32[]{:S(2)}, u32[]{:S(2)}) %collective-permute-start.8) | collective-permute-done | bytes 163872 | tf_op jit(solution)/shard_map/ppermute | solution.py:294
  33.3 0.1 collective-permute-start.9
  33.4 0.2 combine.3
  33.6 1.8 %collective-permute-start.14 = (bf16[16,2560]{1,0:T(8,128)(2,1)S(1)}, bf16[16,2560]{1,0:T(8,128)(2,1)S(1)}, u32[]{:S(2)}, u32[]{:S(2)}) collective-permute-start(bf16[16,2560]{1,0:T(8,128)(2,1)S(1)} %get-tuple-element.31), channel_id=1, source_target_pairs={{0,16},{16,0},{1,17},{17,1},{2,18},{18,2},{3,19},{19,3},{4,20},{20... | collective-permute-start | bytes 245768 | tf_op jit(solution)/shard_map/ppermute | solution.py:294
  35.4 1.5 %collective-permute-start.17 = (bf16[16,2560]{1,0:T(8,128)(2,1)S(1)}, bf16[16,2560]{1,0:T(8,128)(2,1)S(1)}, u32[]{:S(2)}, u32[]{:S(2)}) collective-permute-start(bf16[16,2560]{1,0:T(8,128)(2,1)S(1)} %get-tuple-element.32.refs_0_), channel_id=1, source_target_pairs={{0,2},{1,3},{2,0},{3,1},{4,6},{5,7},{6,4},{7,5},{8,10},{9,11},{10,... | collective-permute-start | bytes 245768 | tf_op jit(solution)/shard_map/ppermute | solution.py:294
  36.9 0.0 collective-permute-done.9.got_ref.refs_0_
  36.9 0.6 collective-permute-start.10
  37.5 1.0 %collective-permute-done.14.refs_1_.refs_0_ = bf16[16,2560]{1,0:T(8,128)(2,1)S(1)} collective-permute-done((bf16[16,2560]{1,0:T(8,128)(2,1)S(1)}, bf16[16,2560]{1,0:T(8,128)(2,1)S(1)}, u32[]{:S(2)}, u32[]{:S(2)}) %collective-permute-start.14) | collective-permute-done | bytes 81952 | tf_op jit(solution)/shard_map/ppermute | solution.py:294
  38.5 2.0 %collective-permute-done.17.refs_0_.refs_1_ = bf16[16,2560]{1,0:T(8,128)(2,1)S(1)} collective-permute-done((bf16[16,2560]{1,0:T(8,128)(2,1)S(1)}, bf16[16,2560]{1,0:T(8,128)(2,1)S(1)}, u32[]{:S(2)}, u32[]{:S(2)}) %collective-permute-start.17) | collective-permute-done | bytes 81952 | tf_op jit(solution)/shard_map/ppermute | solution.py:294
  40.4 0.0 collective-permute-start.19
  40.4 1.8 %collective-permute-start.15 = (bf16[16,2560]{1,0:T(8,128)(2,1)S(1)}, bf16[16,2560]{1,0:T(8,128)(2,1)S(1)}, u32[]{:S(2)}, u32[]{:S(2)}) collective-permute-start(bf16[16,2560]{1,0:T(8,128)(2,1)S(1)} %collective-permute-done.14.refs_1_.refs_0_), channel_id=1, source_target_pairs={{0,2},{1,3},{2,0},{3,1},{4,6},{5,7},{6,4},{7,5},{8,10},{9,11},{10,... | collective-permute-start | bytes 245768 | tf_op jit(solution)/shard_map/ppermute | solution.py:294
  42.2 0.1 combine.2.refs_0_
  42.3 1.4 %collective-permute-start.11 = (bf16[16,1536]{1,0:T(8,128)(2,1)S(1)}, bf16[16,1536]{1,0:T(8,128)(2,1)S(1)}, u32[]{:S(2)}, u32[]{:S(2)}) collective-permute-start(bf16[16,1536]{1,0:T(8,128)(2,1)S(1)} %combine.2.refs_0_), channel_id=1, source_target_pairs={{0,2},{1,3},{2,0},{3,1},{4,6},{5,7},{6,4},{7,5},{8,10},{9,11},{10,... | collective-permute-start | bytes 147464 | tf_op jit(solution)/shard_map/ppermute | solution.py:294
  43.7 0.0 collective-permute-start.16
  43.7 2.1 %down.3.refs_1_.refs_5_ = f32[64,2048]{1,0:T(8,128)S(1)} custom-call(s32[2]{0:T(128)S(1)} %pad_add_fusion.where, bf16[16,2560]{1,0:T(8,128)(2,1)S(1)} %get-tuple-element.32.refs_0_, bf16[16,2560]{1,0:T(8,128)(2,1)S(1)} %collective-permute-done.17.refs_0_.refs_1_, bf16[16,2560]{1,0:T(8,128)(2,1)S(1)} %collective-permute-done.18.refs_2_, ...), custom_call_target="tpu_custom_call" | custom-call | bytes 1024 | tf_op jit(solution)/shard_map/down/pallas_call | solution.py:274
  45.9 0.6 collective-permute-start.20
  46.4 0.1 collective-permute-start.12
  46.5 0.5 collective-permute-start.13
  47.0 0.3 collective-permute-done.20.refs_3_
  47.3 2.1 %down.4.refs_5_ = f32[64,2048]{1,0:T(8,128)S(1)} custom-call(s32[2]{0:T(128)S(1)} %pad_add_fusion.where, bf16[16,2560]{1,0:T(8,128)(2,1)S(1)} %collective-permute-done.14.refs_1_.refs_0_, bf16[16,2560]{1,0:T(8,128)(2,1)S(1)} %collective-permute-done.15.refs_0_.refs_1_, bf16[16,2560]{1,0:T(8,128)(2,1)S(1)} %collective-permute-done.16.refs_2_, ...), custom_call_target="tpu_custom_call" | custom-call | bytes 1024 | tf_op jit(solution)/shard_map/down/pallas_call | solution.py:274
  49.5 1.5 %down.5 = (bf16[16,2048]{1,0:T(8,128)(2,1)S(1)}, bf16[16,2048]{1,0:T(8,128)(2,1)S(1)}, bf16[16,2048]{1,0:T(8,128)(2,1)S(1)}, bf16[16,2048]{1,0:T(8,128)(2,1)S(1)}) custom-call(s32[2]{0:T(128)S(1)} %pad_add_fusion.where, bf16[16,1536]{1,0:T(8,128)(2,1)S(1)} %combine.2.refs_0_, bf16[16,1536]{1,0:T(8,128)(2,1)S(1)} %collective-permute-done.11.refs_0_.refs_1_, ...), custom_call_target="tpu_custom_call" | custom-call | bytes 1024 | tf_op jit(solution)/shard_map/down/pallas_call | solution.py:274
  51.0 3.7 %collective-permute-start.21 = (bf16[16,2048]{1,0:T(8,128)(2,1)S(1)}, bf16[16,2048]{1,0:T(8,128)(2,1)S(1)}, u32[]{:S(2)}, u32[]{:S(2)}) collective-permute-start(bf16[16,2048]{1,0:T(8,128)(2,1)S(1)} %get-tuple-element.34), channel_id=1, source_target_pairs={{0,12},{4,8},{8,4},{12,0},{1,13},{5,9},{9,5},{13,1},{2,14},{6,10},... | collective-permute-start | bytes 196616 | tf_op jit(solution)/shard_map/ppermute | solution.py:294
  54.7 0.8 %collective-permute-start.23 = (bf16[16,2048]{1,0:T(8,128)(2,1)S(1)}, bf16[16,2048]{1,0:T(8,128)(2,1)S(1)}, u32[]{:S(2)}, u32[]{:S(2)}) collective-permute-start(bf16[16,2048]{1,0:T(8,128)(2,1)S(1)} %get-tuple-element.36), channel_id=1, source_target_pairs={{0,4},{4,0},{8,12},{12,8},{1,5},{5,1},{9,13},{13,9},{2,6},{6,2},{1... | collective-permute-start | bytes 196616 | tf_op jit(solution)/shard_map/ppermute | solution.py:294
  55.5 2.4 %collective-permute-done.21 = bf16[16,2048]{1,0:T(8,128)(2,1)S(1)} collective-permute-done((bf16[16,2048]{1,0:T(8,128)(2,1)S(1)}, bf16[16,2048]{1,0:T(8,128)(2,1)S(1)}, u32[]{:S(2)}, u32[]{:S(2)}) %collective-permute-start.21) | collective-permute-done | bytes 65568 | tf_op jit(solution)/shard_map/ppermute | solution.py:294
  57.9 2.5 %collective-permute-done.22 = bf16[16,2048]{1,0:T(8,128)(2,1)S(1)} collective-permute-done((bf16[16,2048]{1,0:T(8,128)(2,1)S(1)}, bf16[16,2048]{1,0:T(8,128)(2,1)S(1)}, u32[]{:S(2)}, u32[]{:S(2)}) %collective-permute-start.22) | collective-permute-done | bytes 65568 | tf_op jit(solution)/shard_map/ppermute | solution.py:294
  60.4 0.7 %add_convert_fusion = bf16[16,2048]{1,0:T(8,128)(2,1)} fusion(bf16[16,2048]{1,0:T(8,128)(2,1)S(1)} %collective-permute-done.23, bf16[16,2048]{1,0:T(8,128)(2,1)S(1)} %collective-permute-done.22, bf16[16,2048]{1,0:T(8,128)(2,1)S(1)} %collective-permute-done.21, bf16[16,2048]{1,0:T(8,128)(2,1)S(1)} %get-tuple-element.33), kind=kLoop, calls=%fused_computation | loop fusion | flops 262144 | bytes 327680 | tf_op jit(solution)/shard_map/convert_element_type | solution.py:335
  (34 shorter events, 0.2 us)
Async XLA Ops:
  0.0 12.2 %collective-permute-start.2 = (bf16[16,2048]{1,0:T(8,128)(2,1)}, bf16[16,2048]{1,0:T(8,128)(2,1)S(1)}, u32[]{:S(2)}, u32[]{:S(2)}) collective-permute-start(bf16[16,2048]{1,0:T(8,128)(2,1)} %tokens_ref.3), channel_id=1, source_target_pairs={{0,12},{4,8},{8,4},{12,0},{1,13},{5,9},{9,5},{13,1},{2,14},{6,10},... | collective-permute-start | bytes 196616 | tf_op jit(solution)/shard_map/ppermute | solution.py:294
  5.0 7.2 %collective-permute-start.1 = (bf16[16,2048]{1,0:T(8,128)(2,1)}, bf16[16,2048]{1,0:T(8,128)(2,1)S(1)}, u32[]{:S(2)}, u32[]{:S(2)}) collective-permute-start(bf16[16,2048]{1,0:T(8,128)(2,1)} %tokens_ref.3), channel_id=1, source_target_pairs={{0,8},{4,12},{8,0},{12,4},{1,9},{5,13},{9,1},{13,5},{2,10},{6,14},... | collective-permute-start | bytes 196616 | tf_op jit(solution)/shard_map/ppermute | solution.py:294
  5.1 7.2 %collective-permute-start = (bf16[16,2048]{1,0:T(8,128)(2,1)}, bf16[16,2048]{1,0:T(8,128)(2,1)S(1)}, u32[]{:S(2)}, u32[]{:S(2)}) collective-permute-start(bf16[16,2048]{1,0:T(8,128)(2,1)} %tokens_ref.3), channel_id=1, source_target_pairs={{0,4},{4,0},{8,12},{12,8},{1,5},{5,1},{9,13},{13,9},{2,6},{6,2},{1... | collective-permute-start | bytes 196616 | tf_op jit(solution)/shard_map/ppermute | solution.py:294
  5.6 6.7 %collective-permute-start.3 = (bf16[16,2048]{1,0:T(8,128)(2,1)}, bf16[16,2048]{1,0:T(8,128)(2,1)S(1)}, u32[]{:S(2)}, u32[]{:S(2)}) collective-permute-start(bf16[16,2048]{1,0:T(8,128)(2,1)} %tokens_ref.3), channel_id=1, source_target_pairs={{0,16},{16,0},{1,17},{17,1},{2,18},{18,2},{3,19},{19,3},{4,20},{20... | collective-permute-start | bytes 196616 | tf_op jit(solution)/shard_map/ppermute | solution.py:294
  12.3 5.8 %collective-permute-start.4 = (bf16[48,2048]{1,0:T(8,128)(2,1)S(1)}, bf16[48,2048]{1,0:T(8,128)(2,1)S(1)}, u32[]{:S(2)}, u32[]{:S(2)}) collective-permute-start(bf16[48,2048]{1,0:T(8,128)(2,1)S(1)} %join.4.refs_1_), channel_id=1, source_target_pairs={{0,16},{16,0},{1,17},{17,1},{2,18},{18,2},{3,19},{19,3},{4,20},{20... | collective-permute-start | bytes 589832 | tf_op jit(solution)/shard_map/ppermute | solution.py:294
  21.7 1.7 %collective-permute-start.5 = (bf16[2,64,1280]{2,1,0:T(8,128)(2,1)S(1)}, bf16[2,64,1280]{2,1,0:T(8,128)(2,1)S(1)}, u32[]{:S(2)}, u32[]{:S(2)}) collective-permute-start(bf16[2,64,1280]{2,1,0:T(8,128)(2,1)S(1)} %get-tuple-element.27), channel_id=1, source_target_pairs={{0,1},{1,0},{2,3},{3,2},{4,5},{5,4},{6,7},{7,6},{8,9},{9,8},{10,11... | collective-permute-start | bytes 983048 | tf_op jit(solution)/shard_map/ppermute | solution.py:294
  21.8 3.4 %collective-permute-start.6 = (bf16[2,64,1280]{2,1,0:T(8,128)(2,1)S(1)}, bf16[2,64,1280]{2,1,0:T(8,128)(2,1)S(1)}, u32[]{:S(2)}, u32[]{:S(2)}) collective-permute-start(bf16[2,64,1280]{2,1,0:T(8,128)(2,1)S(1)} %get-tuple-element.28), channel_id=1, source_target_pairs={{0,1},{1,0},{2,3},{3,2},{4,5},{5,4},{6,7},{7,6},{8,9},{9,8},{10,11... | collective-permute-start | bytes 983048 | tf_op jit(solution)/shard_map/ppermute | solution.py:294
  23.4 8.7 %collective-permute-start.7 = (bf16[2,32,1280]{2,1,0:T(8,128)(2,1)S(1)}, bf16[2,32,1280]{2,1,0:T(8,128)(2,1)S(1)}, u32[]{:S(2)}, u32[]{:S(2)}) collective-permute-start(bf16[2,32,1280]{2,1,0:T(8,128)(2,1)S(1)} %pair_sum.3.refs_4_), channel_id=1, source_target_pairs={{0,2},{1,3},{2,0},{3,1},{4,6},{5,7},{6,4},{7,5},{8,10},{9,11},{10,... | collective-permute-start | bytes 491528 | tf_op jit(solution)/shard_map/ppermute | solution.py:294
  25.2 18.5 %slice-start = ((s8[27262976]{0:T(1024)(128)(4,1)}), s8[4194304]{0:T(1024)(128)(4,1)S(1)}, s32[]{:S(2)}) async-start(s8[27262976]{0:T(1024)(128)(4,1)} %bitcast.2), calls=%async_computation | async-start | bytes 8388608
  25.3 18.4 %slice-start.1 = ((s8[27262976]{0:T(1024)(128)(4,1)}), s8[4194304]{0:T(1024)(128)(4,1)S(1)}, s32[]{:S(2)}) async-start(s8[27262976]{0:T(1024)(128)(4,1)} %bitcast.2), calls=%async_computation.1 | async-start | bytes 8388608
  25.3 18.4 %slice-start.2 = ((s8[27262976]{0:T(1024)(128)(4,1)}), s8[4194304]{0:T(1024)(128)(4,1)S(1)}, s32[]{:S(2)}) async-start(s8[27262976]{0:T(1024)(128)(4,1)} %bitcast.2), calls=%async_computation.2 | async-start | bytes 8388608
  25.3 18.4 %slice-start.3 = ((s8[27262976]{0:T(1024)(128)(4,1)}), s8[4194304]{0:T(1024)(128)(4,1)S(1)}, s32[]{:S(2)}) async-start(s8[27262976]{0:T(1024)(128)(4,1)} %bitcast.2), calls=%async_computation.3 | async-start | bytes 8388608
  25.3 18.4 %slice-start.4 = ((s8[27262976]{0:T(1024)(128)(4,1)}), s8[4194304]{0:T(1024)(128)(4,1)S(1)}, s32[]{:S(2)}) async-start(s8[27262976]{0:T(1024)(128)(4,1)} %bitcast.2), calls=%async_computation.4 | async-start | bytes 8388608
  25.3 18.4 %slice-start.5 = ((s8[27262976]{0:T(1024)(128)(4,1)}), s8[4194304]{0:T(1024)(128)(4,1)S(1)}, s32[]{:S(2)}) async-start(s8[27262976]{0:T(1024)(128)(4,1)} %bitcast.2), calls=%async_computation.5 | async-start | bytes 8388608
  25.3 18.4 %slice-start.6 = ((s8[27262976]{0:T(1024)(128)(4,1)}), s8[2097152]{0:T(1024)(128)(4,1)S(1)}, s32[]{:S(2)}) async-start(s8[27262976]{0:T(1024)(128)(4,1)} %bitcast.2), calls=%async_computation.6 | async-start | bytes 4194304
  25.3 7.9 %collective-permute-start.8 = (bf16[2,32,1280]{2,1,0:T(8,128)(2,1)S(1)}, bf16[2,32,1280]{2,1,0:T(8,128)(2,1)S(1)}, u32[]{:S(2)}, u32[]{:S(2)}) collective-permute-start(bf16[2,32,1280]{2,1,0:T(8,128)(2,1)S(1)} %pair_sum.4.refs_5_), channel_id=1, source_target_pairs={{0,2},{1,3},{2,0},{3,1},{4,6},{5,7},{6,4},{7,5},{8,10},{9,11},{10,... | collective-permute-start | bytes 491528 | tf_op jit(solution)/shard_map/ppermute | solution.py:294
  33.3 3.6 %collective-permute-start.9 = (bf16[2,32,1536]{2,1,0:T(8,128)(2,1)S(1)}, bf16[2,32,1536]{2,1,0:T(8,128)(2,1)S(1)}, u32[]{:S(2)}, u32[]{:S(2)}) collective-permute-start(bf16[2,32,1536]{2,1,0:T(8,128)(2,1)S(1)} %later.1), channel_id=1, source_target_pairs={{0,1},{1,0},{2,3},{3,2},{4,5},{5,4},{6,7},{7,6},{8,9},{9,8},{10,11... | collective-permute-start | bytes 589832 | tf_op jit(solution)/shard_map/ppermute | solution.py:294
  33.6 4.9 %collective-permute-start.14 = (bf16[16,2560]{1,0:T(8,128)(2,1)S(1)}, bf16[16,2560]{1,0:T(8,128)(2,1)S(1)}, u32[]{:S(2)}, u32[]{:S(2)}) collective-permute-start(bf16[16,2560]{1,0:T(8,128)(2,1)S(1)} %get-tuple-element.31), channel_id=1, source_target_pairs={{0,16},{16,0},{1,17},{17,1},{2,18},{18,2},{3,19},{19,3},{4,20},{20... | collective-permute-start | bytes 245768 | tf_op jit(solution)/shard_map/ppermute | solution.py:294
  35.4 5.1 %collective-permute-start.17 = (bf16[16,2560]{1,0:T(8,128)(2,1)S(1)}, bf16[16,2560]{1,0:T(8,128)(2,1)S(1)}, u32[]{:S(2)}, u32[]{:S(2)}) collective-permute-start(bf16[16,2560]{1,0:T(8,128)(2,1)S(1)} %get-tuple-element.32.refs_0_), channel_id=1, source_target_pairs={{0,2},{1,3},{2,0},{3,1},{4,6},{5,7},{6,4},{7,5},{8,10},{9,11},{10,... | collective-permute-start | bytes 245768 | tf_op jit(solution)/shard_map/ppermute | solution.py:294
  36.9 5.3 %collective-permute-start.10 = (bf16[2,16,1536]{2,1,0:T(8,128)(2,1)S(1)}, bf16[2,16,1536]{2,1,0:T(8,128)(2,1)S(1)}, u32[]{:S(2)}, u32[]{:S(2)}) collective-permute-start(bf16[2,16,1536]{2,1,0:T(8,128)(2,1)S(1)} %pair_sum.5), channel_id=1, source_target_pairs={{0,2},{1,3},{2,0},{3,1},{4,6},{5,7},{6,4},{7,5},{8,10},{9,11},{10,... | collective-permute-start | bytes 294920 | tf_op jit(solution)/shard_map/ppermute | solution.py:294
  37.5 6.2 %collective-permute-start.18 = (bf16[16,2560]{1,0:T(8,128)(2,1)S(1)}, bf16[16,2560]{1,0:T(8,128)(2,1)S(1)}, u32[]{:S(2)}, u32[]{:S(2)}) collective-permute-start(bf16[16,2560]{1,0:T(8,128)(2,1)S(1)} %get-tuple-element.32.refs_0_), channel_id=1, source_target_pairs={{0,1},{1,0},{2,3},{3,2},{4,5},{5,4},{6,7},{7,6},{8,9},{9,8},{10,11... | collective-permute-start | bytes 245768 | tf_op jit(solution)/shard_map/ppermute | solution.py:294
  40.4 3.2 %collective-permute-start.19 = (bf16[16,2560]{1,0:T(8,128)(2,1)S(1)}, bf16[16,2560]{1,0:T(8,128)(2,1)S(1)}, u32[]{:S(2)}, u32[]{:S(2)}) collective-permute-start(bf16[16,2560]{1,0:T(8,128)(2,1)S(1)} %join.6), channel_id=1, source_target_pairs={{0,1},{1,0},{2,3},{3,2},{4,5},{5,4},{6,7},{7,6},{8,9},{9,8},{10,11... | collective-permute-start | bytes 245768 | tf_op jit(solution)/shard_map/ppermute | solution.py:294
  40.4 5.4 %collective-permute-start.15 = (bf16[16,2560]{1,0:T(8,128)(2,1)S(1)}, bf16[16,2560]{1,0:T(8,128)(2,1)S(1)}, u32[]{:S(2)}, u32[]{:S(2)}) collective-permute-start(bf16[16,2560]{1,0:T(8,128)(2,1)S(1)} %collective-permute-done.14.refs_1_.refs_0_), channel_id=1, source_target_pairs={{0,2},{1,3},{2,0},{3,1},{4,6},{5,7},{6,4},{7,5},{8,10},{9,11},{10,... | collective-permute-start | bytes 245768 | tf_op jit(solution)/shard_map/ppermute | solution.py:294
  42.3 4.2 %collective-permute-start.11 = (bf16[16,1536]{1,0:T(8,128)(2,1)S(1)}, bf16[16,1536]{1,0:T(8,128)(2,1)S(1)}, u32[]{:S(2)}, u32[]{:S(2)}) collective-permute-start(bf16[16,1536]{1,0:T(8,128)(2,1)S(1)} %combine.2.refs_0_), channel_id=1, source_target_pairs={{0,2},{1,3},{2,0},{3,1},{4,6},{5,7},{6,4},{7,5},{8,10},{9,11},{10,... | collective-permute-start | bytes 147464 | tf_op jit(solution)/shard_map/ppermute | solution.py:294
  43.7 3.4 %collective-permute-start.16 = (bf16[16,2560]{1,0:T(8,128)(2,1)S(1)}, bf16[16,2560]{1,0:T(8,128)(2,1)S(1)}, u32[]{:S(2)}, u32[]{:S(2)}) collective-permute-start(bf16[16,2560]{1,0:T(8,128)(2,1)S(1)} %collective-permute-done.14.refs_1_.refs_0_), channel_id=1, source_target_pairs={{0,1},{1,0},{2,3},{3,2},{4,5},{5,4},{6,7},{7,6},{8,9},{9,8},{10,11... | collective-permute-start | bytes 245768 | tf_op jit(solution)/shard_map/ppermute | solution.py:294
  45.9 1.5 %collective-permute-start.20 = (bf16[16,2560]{1,0:T(8,128)(2,1)S(1)}, bf16[16,2560]{1,0:T(8,128)(2,1)S(1)}, u32[]{:S(2)}, u32[]{:S(2)}) collective-permute-start(bf16[16,2560]{1,0:T(8,128)(2,1)S(1)} %join.7), channel_id=1, source_target_pairs={{0,1},{1,0},{2,3},{3,2},{4,5},{5,4},{6,7},{7,6},{8,9},{9,8},{10,11... | collective-permute-start | bytes 245768 | tf_op jit(solution)/shard_map/ppermute | solution.py:294
  46.4 3.0 %collective-permute-start.12 = (bf16[16,1536]{1,0:T(8,128)(2,1)S(1)}, bf16[16,1536]{1,0:T(8,128)(2,1)S(1)}, u32[]{:S(2)}, u32[]{:S(2)}) collective-permute-start(bf16[16,1536]{1,0:T(8,128)(2,1)S(1)} %combine.2.refs_0_), channel_id=1, source_target_pairs={{0,1},{1,0},{2,3},{3,2},{4,5},{5,4},{6,7},{7,6},{8,9},{9,8},{10,11... | collective-permute-start | bytes 147464 | tf_op jit(solution)/shard_map/ppermute | solution.py:294
  46.5 2.9 %collective-permute-start.13 = (bf16[16,1536]{1,0:T(8,128)(2,1)S(1)}, bf16[16,1536]{1,0:T(8,128)(2,1)S(1)}, u32[]{:S(2)}, u32[]{:S(2)}) collective-permute-start(bf16[16,1536]{1,0:T(8,128)(2,1)S(1)} %join.5), channel_id=1, source_target_pairs={{0,1},{1,0},{2,3},{3,2},{4,5},{5,4},{6,7},{7,6},{8,9},{9,8},{10,11... | collective-permute-start | bytes 147464 | tf_op jit(solution)/shard_map/ppermute | solution.py:294
  51.0 6.9 %collective-permute-start.21 = (bf16[16,2048]{1,0:T(8,128)(2,1)S(1)}, bf16[16,2048]{1,0:T(8,128)(2,1)S(1)}, u32[]{:S(2)}, u32[]{:S(2)}) collective-permute-start(bf16[16,2048]{1,0:T(8,128)(2,1)S(1)} %get-tuple-element.34), channel_id=1, source_target_pairs={{0,12},{4,8},{8,4},{12,0},{1,13},{5,9},{9,5},{13,1},{2,14},{6,10},... | collective-permute-start | bytes 196616 | tf_op jit(solution)/shard_map/ppermute | solution.py:294
  54.7 5.7 %collective-permute-start.22 = (bf16[16,2048]{1,0:T(8,128)(2,1)S(1)}, bf16[16,2048]{1,0:T(8,128)(2,1)S(1)}, u32[]{:S(2)}, u32[]{:S(2)}) collective-permute-start(bf16[16,2048]{1,0:T(8,128)(2,1)S(1)} %get-tuple-element.35), channel_id=1, source_target_pairs={{0,8},{4,12},{8,0},{12,4},{1,9},{5,13},{9,1},{13,5},{2,10},{6,14},... | collective-permute-start | bytes 196616 | tf_op jit(solution)/shard_map/ppermute | solution.py:294
  54.7 5.7 %collective-permute-start.23 = (bf16[16,2048]{1,0:T(8,128)(2,1)S(1)}, bf16[16,2048]{1,0:T(8,128)(2,1)S(1)}, u32[]{:S(2)}, u32[]{:S(2)}) collective-permute-start(bf16[16,2048]{1,0:T(8,128)(2,1)S(1)} %get-tuple-element.36), channel_id=1, source_target_pairs={{0,4},{4,0},{8,12},{12,8},{1,5},{5,1},{9,13},{13,9},{2,6},{6,2},{1... | collective-permute-start | bytes 196616 | tf_op jit(solution)/shard_map/ppermute | solution.py:294

commit v17 on v9

--- a/solution.py
+++ b/solution.py
@@ -214,7 +214,7 @@
     )(mine, got, from_chip, *left, *behind)
 
 
-def down_kernel(n_pieces, has_acc, last, segments, columns, where, *refs):
+def down_kernel(n_pieces, has_acc, last, segments, where, *refs):
     pieces, refs = refs[:n_pieces], refs[n_pieces:]
     down_ref, refs = refs[0], refs[1:]
     prev_ref, refs = (refs[0], refs[1:]) if has_acc else (None, refs)
@@ -223,13 +223,15 @@
     for piece in pieces:
         lhs_ref[at : at + piece.shape[0], :] = piece[...]
         at += piece.shape[0]
-    left = columns[0]
+    lhs_ref[at:, :] = jnp.zeros_like(lhs_ref[at:, :])
+    total = at
     for a, b in pieces_of(acc_ref.shape[1], 2 * TILE):
-        part = prev_ref[:, left + a : left + b] if has_acc else 0.0
+        part = prev_ref[:, a:b] if has_acc else 0.0
         at = 0
         for sign, start, depth in segments:
             rows = pl.ds(pl.multiple_of(sign * where[0] + start, TILE) if sign else start, depth)
-            part += jnp.dot(lhs_ref[:, at : at + depth], down_ref[rows, left + a : left + b], preferred_element_type=jnp.float32)
+            product = jnp.dot(lhs_ref[:, at : at + depth], down_ref[rows, a:b], preferred_element_type=jnp.float32)
+            part += product[:total]
             at += depth
         acc_ref[:, a:b] = part
     if last:
@@ -238,16 +240,16 @@
             out[...] = acc_ref[pl.ds(source, ROWS), :].astype(out.dtype)
 
 
-def down(where, pieces, down_weight, prev, segments, columns, last):
-    width = columns[1] - columns[0]
+def down(where, pieces, down_weight, prev, segments, last):
+    width = down_weight.shape[1]
     total = 4 * ROWS
     args = [*pieces, down_weight] + ([] if prev is None else [prev])
     sums = jax.ShapeDtypeStruct((total, width), jnp.float32)
-    scratch = [pltpu.VMEM((total, pieces[0].shape[1]), jnp.bfloat16)]
+    scratch = [pltpu.VMEM((max(total, 128), pieces[0].shape[1]), jnp.bfloat16)]
     if last:
         scratch = [pltpu.VMEM(sums.shape, sums.dtype)] + scratch
     return pl.pallas_call(
-        functools.partial(down_kernel, len(pieces), prev is not None, last, segments, columns),
+        functools.partial(down_kernel, len(pieces), prev is not None, last, segments),
         in_specs=[spec(pltpu.SMEM)] + [spec(pltpu.VMEM)] * len(args),
         out_specs=[spec(pltpu.VMEM)] * 4 if last else spec(pltpu.VMEM),
         scratch_shapes=scratch,
@@ -300,18 +302,14 @@
         other = swap(hidden, "wid", 2)
         return [hidden, other, swap(hidden, "wid", 1), swap(join([other], behind), "wid", 1)]
 
-    features = down_weight.shape[1]
-    acc = down(where, gather(keep, [rest]), down_weight, None, [(1, 0, bounds[2])], (0, features), False)
-    pieces = gather(rest, [acc])
+    acc = down(where, gather(keep, [rest]), down_weight, None, [(1, 0, bounds[2])], False)
     rest_segments = [(-1, half, bounds[2])] + [(0, start, width) for start, width in segments]
-    mixed = []
-    for columns in ((0, features // 2), (features // 2, features)):
-        out = down(where, pieces, down_weight, acc, rest_segments, columns, True)
-        total = out[0].astype(f32)
-        for d in (3, 2, 1):
-            total = total + swap(out[d], "hid", d).astype(f32)
-        mixed.append(total.astype(bf16))
-    return jnp.concatenate(mixed, 1)
+    acc = down(where, gather(rest, [acc]), down_weight, acc, rest_segments, True)
+
+    mixed = acc[0].astype(f32)
+    for d in (3, 2, 1):
+        mixed = mixed + swap(acc[d], "hid", d).astype(f32)
+    return mixed.astype(bf16)
 
 
 def solution(mesh):

time: 65.7 us -> 60.4 us (0.919)
  starting transfers between devices: 24 us -> 19.6 us
  Pallas kernels: 27.6 us -> 25.9 us
  waiting for transfers between devices: 12.9 us -> 13.8 us
    ppermute x22 -> x19, starting transfers between devices: 24 us -> 19.6 us  [swap(): return lax.ppermute(x, axis, [(i, i ^ step) for i in range(n)])]
    pallas_call x3 -> x2, Pallas kernels: 6.74 us -> 5.02 us  [down(): pl.pallas_call(functools.partial(down_kernel, len(pieces), prev is not No...]
    ppermute x22 -> x19, waiting for transfers between devices: 12.9 us -> 13.8 us  [swap(): return lax.ppermute(x, axis, [(i, i ^ step) for i in range(n)])]
  transfers between devices with their start and end apart: 22 -> 19, of which waited for: 8 -> 8; matrix products, arithmetic and copies ran while one was open for 0% -> 0% of each run, Pallas kernels for 33% -> 32%
where the time goes in v17:
time: 60.4 us; the launch traced here: 60.2 us
  Pallas kernels  25.9 us (43%)
  starting transfers between devices  19.6 us (32%)
  waiting for transfers between devices  13.8 us (23%)
  other arithmetic  0.74 us (1%)
    ppermute x19, starting transfers between devices, swap(): return lax.ppermute(x, axis, [(i, i ^ step) for i in range(n)])  19.6 us
    ppermute x19, waiting for transfers between devices, swap(): return lax.ppermute(x, axis, [(i, i ^ step) for i in range(n)])  13.8 us
    pallas_call x2, Pallas kernels, fetch(): pl.pallas_call(functools.partial(fetch_kernel, first), in_specs=[spec(plt...  10.2 us
    pallas_call x2, Pallas kernels, gate_up(): pl.pallas_call(functools.partial(gate_up_kernel, len(arrays), len(weights...  10.2 us
    pallas_call x2, Pallas kernels, down(): pl.pallas_call(functools.partial(down_kernel, len(pieces), prev is not No...  5.02 us
  transfers between devices with their start and end apart: 19, of which 8 were waited for; matrix products, arithmetic and copies ran while one was open for 0% of the time, Pallas kernels for 32%

profile of v17, /device:TPU:0, one launch (start us, length us, event | category | flops | bytes accessed | tf_op | source)
XLA Modules:
  0.0 60.2 jit_solution(163636932728141221)
XLA Ops:
  0.0 5.0 %collective-permute-start.2 = (bf16[16,2048]{1,0:T(8,128)(2,1)}, bf16[16,2048]{1,0:T(8,128)(2,1)S(1)}, u32[]{:S(2)}, u32[]{:S(2)}) collective-permute-start(bf16[16,2048]{1,0:T(8,128)(2,1)} %tokens_ref.3), channel_id=1, source_target_pairs={{0,12},{4,8},{8,4},{12,0},{1,13},{5,9},{9,5},{13,1},{2,14},{6,10},... | collective-permute-start | bytes 196616 | tf_op jit(solution)/shard_map/ppermute | solution.py:271
  5.0 0.0 collective-permute-start.1
  5.1 0.6 collective-permute-start
  5.6 1.7 %collective-permute-start.3 = (bf16[16,2048]{1,0:T(8,128)(2,1)}, bf16[16,2048]{1,0:T(8,128)(2,1)S(1)}, u32[]{:S(2)}, u32[]{:S(2)}) collective-permute-start(bf16[16,2048]{1,0:T(8,128)(2,1)} %tokens_ref.3), channel_id=1, source_target_pairs={{0,16},{16,0},{1,17},{17,1},{2,18},{18,2},{3,19},{19,3},{4,20},{20... | collective-permute-start | bytes 196616 | tf_op jit(solution)/shard_map/ppermute | solution.py:271
  7.4 0.1 pad_add_fusion.where
  7.4 4.8 %fetch.2 = (bf16[2048,1280]{1,0:T(8,128)(2,1)S(1)}, bf16[2048,1280]{1,0:T(8,128)(2,1)S(1)}, bf16[16,2048]{1,0:T(8,128)(2,1)S(1)}) custom-call(s32[2]{0:T(128)S(1)} %pad_add_fusion.where, bf16[2048,6656]{1,0:T(8,128)(2,1)} %refs_2_.1, bf16[2048,6656]{1,0:T(8,128)(2,1)} %refs_3_.1, bf16[16,2048]{1,0:T(8,128)(2,1)} %tokens_ref.3), custom_call_target="tpu_custom_call" | custom-call | bytes 1024 | tf_op jit(solution)/shard_map/fetch/pallas_call | solution.py:73
  12.2 0.0 collective-permute-done.2.refs_2_
  12.3 0.0 collective-permute-done.1.refs_1_
  12.3 0.0 collective-permute-done.refs_0_
  12.3 0.0 collective-permute-done.3.refs_4_.refs_2_
  12.3 0.4 collective-permute-start.4
  12.7 5.4 %fetch.3 = (bf16[2048,1280]{1,0:T(8,128)(2,1)S(1)}, bf16[2048,1280]{1,0:T(8,128)(2,1)S(1)}, bf16[16,2048]{1,0:T(8,128)(2,1)}) custom-call(s32[2]{0:T(128)S(1)} %pad_add_fusion.where, bf16[2048,6656]{1,0:T(8,128)(2,1)} %refs_2_.1, bf16[2048,6656]{1,0:T(8,128)(2,1)} %refs_3_.1, bf16[16,2048]{1,0:T(8,128)(2,1)} %tokens_ref.3), custom_call_target="tpu_custom_call" | custom-call | bytes 1024 | tf_op jit(solution)/shard_map/fetch/pallas_call | solution.py:73
  18.1 3.6 %gate_up.2 = (bf16[2,64,2560]{2,1,0:T(8,128)(2,1)S(1)}, bf16[2,64,2560]{2,1,0:T(8,128)(2,1)S(1)}) custom-call(s32[2]{0:T(128)S(1)} %pad_add_fusion.where, bf16[16,2048]{1,0:T(8,128)(2,1)S(1)} %get-tuple-element.20.refs_3_.refs_0_, bf16[48,2048]{1,0:T(8,128)(2,1)S(1)} %join.3.refs_1_, bf16[16,2048]{1,0:T(8,128)(2,1)S(1)} %collective-permute-done.3.refs_4_.refs_2_, ...), custom_call_target="tpu_custom_call" | custom-call | bytes 1024 | tf_op jit(solution)/shard_map/gate_up/pallas_call | solution.py:148
  21.7 0.1 collective-permute-start.5
  21.8 2.1 %collective-permute-done.5.got_ref = bf16[2,64,2560]{2,1,0:T(8,128)(2,1)S(1)} collective-permute-done((bf16[2,64,2560]{2,1,0:T(8,128)(2,1)S(1)}, bf16[2,64,2560]{2,1,0:T(8,128)(2,1)S(1)}, u32[]{:S(2)}, u32[]{:S(2)}) %collective-permute-start.5) | collective-permute-done | bytes 655392 | tf_op jit(solution)/shard_map/ppermute | solution.py:271
  23.9 0.1 pair_sum.2.refs_4_
  23.9 0.0 slice-start.1
  24.0 0.0 slice-start.3
  24.0 0.0 slice-start.4
  24.0 0.0 slice-start.6
  24.0 1.8 %collective-permute-start.7 = (bf16[2,32,2560]{2,1,0:T(8,128)(2,1)S(1)}, bf16[2,32,2560]{2,1,0:T(8,128)(2,1)S(1)}, u32[]{:S(2)}, u32[]{:S(2)}) collective-permute-start(bf16[2,32,2560]{2,1,0:T(8,128)(2,1)S(1)} %pair_sum.2.refs_4_), channel_id=1, source_target_pairs={{0,2},{1,3},{2,0},{3,1},{4,6},{5,7},{6,4},{7,5},{8,10},{9,11},{10,... | collective-permute-start | bytes 983048 | tf_op jit(solution)/shard_map/ppermute | solution.py:271
  25.8 6.6 %gate_up.3 = (bf16[2,32,1536]{2,1,0:T(8,128)(2,1)S(1)}, bf16[2,32,1536]{2,1,0:T(8,128)(2,1)S(1)}) custom-call(s32[2]{0:T(128)S(1)} %pad_add_fusion.where, bf16[16,2048]{1,0:T(8,128)(2,1)S(1)} %get-tuple-element.20.refs_3_.refs_0_, bf16[48,2048]{1,0:T(8,128)(2,1)S(1)} %join.3.refs_1_, bf16[2048,6656]{1,0:T(8,128)(2,1)} %refs_2_.1, ...), custom_call_target="tpu_custom_call" | custom-call | bytes 1024 | tf_op jit(solution)/shard_map/gate_up/pallas_call | solution.py:148
  32.4 0.1 collective-permute-start.6
  32.5 1.3 %collective-permute-done.7.chip_ref = bf16[2,32,2560]{2,1,0:T(8,128)(2,1)S(1)} collective-permute-done((bf16[2,32,2560]{2,1,0:T(8,128)(2,1)S(1)}, bf16[2,32,2560]{2,1,0:T(8,128)(2,1)S(1)}, u32[]{:S(2)}, u32[]{:S(2)}) %collective-permute-start.7) | collective-permute-done | bytes 327712 | tf_op jit(solution)/shard_map/ppermute | solution.py:271
  33.8 0.2 combine.2
  34.1 1.8 %collective-permute-start.8 = (bf16[2,16,1536]{2,1,0:T(8,128)(2,1)S(1)}, bf16[2,16,1536]{2,1,0:T(8,128)(2,1)S(1)}, u32[]{:S(2)}, u32[]{:S(2)}) collective-permute-start(bf16[2,16,1536]{2,1,0:T(8,128)(2,1)S(1)} %pair_sum.3), channel_id=1, source_target_pairs={{0,2},{1,3},{2,0},{3,1},{4,6},{5,7},{6,4},{7,5},{8,10},{9,11},{10,... | collective-permute-start | bytes 294920 | tf_op jit(solution)/shard_map/ppermute | solution.py:271
  35.8 1.5 %collective-permute-start.9 = (bf16[16,2560]{1,0:T(8,128)(2,1)S(1)}, bf16[16,2560]{1,0:T(8,128)(2,1)S(1)}, u32[]{:S(2)}, u32[]{:S(2)}) collective-permute-start(bf16[16,2560]{1,0:T(8,128)(2,1)S(1)} %get-tuple-element.29.refs_0_), channel_id=1, source_target_pairs={{0,16},{16,0},{1,17},{17,1},{2,18},{18,2},{3,19},{19,3},{4,20},{20... | collective-permute-start | bytes 245768 | tf_op jit(solution)/shard_map/ppermute | solution.py:271
  37.4 0.5 collective-permute-start.12
  37.9 2.4 %collective-permute-done.9.refs_0_ = bf16[16,2560]{1,0:T(8,128)(2,1)S(1)} collective-permute-done((bf16[16,2560]{1,0:T(8,128)(2,1)S(1)}, bf16[16,2560]{1,0:T(8,128)(2,1)S(1)}, u32[]{:S(2)}, u32[]{:S(2)}) %collective-permute-start.9) | collective-permute-done | bytes 81952 | tf_op jit(solution)/shard_map/ppermute | solution.py:271
  40.3 0.0 collective-permute-done.8.chip_ref
  40.3 0.1 combine.3.refs_1_.refs_0_
  40.4 1.0 %collective-permute-start.10 = (bf16[16,4096]{1,0:T(8,128)(2,1)S(1)}, bf16[16,4096]{1,0:T(8,128)(2,1)S(1)}, u32[]{:S(2)}, u32[]{:S(2)}) collective-permute-start(bf16[16,4096]{1,0:T(8,128)(2,1)S(1)} %combine.3.refs_1_.refs_0_), channel_id=1, source_target_pairs={{0,2},{1,3},{2,0},{3,1},{4,6},{5,7},{6,4},{7,5},{8,10},{9,11},{10,... | collective-permute-start | bytes 393224 | tf_op jit(solution)/shard_map/ppermute | solution.py:271
  41.3 1.1 %collective-permute-done.12.refs_0_.refs_1_ = bf16[16,2560]{1,0:T(8,128)(2,1)S(1)} collective-permute-done((bf16[16,2560]{1,0:T(8,128)(2,1)S(1)}, bf16[16,2560]{1,0:T(8,128)(2,1)S(1)}, u32[]{:S(2)}, u32[]{:S(2)}) %collective-permute-start.12) | collective-permute-done | bytes 81952 | tf_op jit(solution)/shard_map/ppermute | solution.py:271
  42.4 0.0 collective-permute-start.14
  42.4 0.5 collective-permute-start.11
  42.9 0.0 collective-permute-done.13.refs_2_
  42.9 0.8 %collective-permute-done.14.refs_3_ = bf16[16,2560]{1,0:T(8,128)(2,1)S(1)} collective-permute-done((bf16[16,2560]{1,0:T(8,128)(2,1)S(1)}, bf16[16,2560]{1,0:T(8,128)(2,1)S(1)}, u32[]{:S(2)}, u32[]{:S(2)}) %collective-permute-start.14) | collective-permute-done | bytes 81952 | tf_op jit(solution)/shard_map/ppermute | solution.py:271
  43.8 2.1 %down.2.refs_1_.refs_5_ = f32[64,2048]{1,0:T(8,128)S(1)} custom-call(s32[2]{0:T(128)S(1)} %pad_add_fusion.where, bf16[16,2560]{1,0:T(8,128)(2,1)S(1)} %get-tuple-element.30.refs_0_, bf16[16,2560]{1,0:T(8,128)(2,1)S(1)} %collective-permute-done.12.refs_0_.refs_1_, bf16[16,2560]{1,0:T(8,128)(2,1)S(1)} %collective-permute-done.13.refs_2_, ...), custom_call_target="tpu_custom_call" | custom-call | bytes 1024 | tf_op jit(solution)/shard_map/down/pallas_call | solution.py:251
  45.9 0.2 collective-permute-start.15
  46.1 1.2 %collective-permute-done.15.refs_3_ = bf16[16,4096]{1,0:T(8,128)(2,1)S(1)} collective-permute-done((bf16[16,4096]{1,0:T(8,128)(2,1)S(1)}, bf16[16,4096]{1,0:T(8,128)(2,1)S(1)}, u32[]{:S(2)}, u32[]{:S(2)}) %collective-permute-start.15) | collective-permute-done | bytes 131104 | tf_op jit(solution)/shard_map/ppermute | solution.py:271
  47.3 2.9 %down.3 = (bf16[16,2048]{1,0:T(8,128)(2,1)S(1)}, bf16[16,2048]{1,0:T(8,128)(2,1)S(1)}, bf16[16,2048]{1,0:T(8,128)(2,1)S(1)}, bf16[16,2048]{1,0:T(8,128)(2,1)S(1)}) custom-call(s32[2]{0:T(128)S(1)} %pad_add_fusion.where, bf16[16,4096]{1,0:T(8,128)(2,1)S(1)} %combine.3.refs_1_.refs_0_, bf16[16,4096]{1,0:T(8,128)(2,1)S(1)} %collective-permute-done.10.refs_0_.refs_1_, ...), custom_call_target="tpu_custom_call" | custom-call | bytes 1024 | tf_op jit(solution)/shard_map/down/pallas_call | solution.py:251
  50.2 3.7 %collective-permute-start.16 = (bf16[16,2048]{1,0:T(8,128)(2,1)S(1)}, bf16[16,2048]{1,0:T(8,128)(2,1)S(1)}, u32[]{:S(2)}, u32[]{:S(2)}) collective-permute-start(bf16[16,2048]{1,0:T(8,128)(2,1)S(1)} %get-tuple-element.32), channel_id=1, source_target_pairs={{0,12},{4,8},{8,4},{12,0},{1,13},{5,9},{9,5},{13,1},{2,14},{6,10},... | collective-permute-start | bytes 196616 | tf_op jit(solution)/shard_map/ppermute | solution.py:271
  53.9 0.0 collective-permute-start.17
  53.9 0.8 %collective-permute-start.18 = (bf16[16,2048]{1,0:T(8,128)(2,1)S(1)}, bf16[16,2048]{1,0:T(8,128)(2,1)S(1)}, u32[]{:S(2)}, u32[]{:S(2)}) collective-permute-start(bf16[16,2048]{1,0:T(8,128)(2,1)S(1)} %get-tuple-element.34), channel_id=1, source_target_pairs={{0,4},{4,0},{8,12},{12,8},{1,5},{5,1},{9,13},{13,9},{2,6},{6,2},{1... | collective-permute-start | bytes 196616 | tf_op jit(solution)/shard_map/ppermute | solution.py:271
  54.7 2.3 %collective-permute-done.16 = bf16[16,2048]{1,0:T(8,128)(2,1)S(1)} collective-permute-done((bf16[16,2048]{1,0:T(8,128)(2,1)S(1)}, bf16[16,2048]{1,0:T(8,128)(2,1)S(1)}, u32[]{:S(2)}, u32[]{:S(2)}) %collective-permute-start.16) | collective-permute-done | bytes 65568 | tf_op jit(solution)/shard_map/ppermute | solution.py:271
  57.0 2.6 %collective-permute-done.17 = bf16[16,2048]{1,0:T(8,128)(2,1)S(1)} collective-permute-done((bf16[16,2048]{1,0:T(8,128)(2,1)S(1)}, bf16[16,2048]{1,0:T(8,128)(2,1)S(1)}, u32[]{:S(2)}, u32[]{:S(2)}) %collective-permute-start.17) | collective-permute-done | bytes 65568 | tf_op jit(solution)/shard_map/ppermute | solution.py:271
  59.6 0.0 collective-permute-done.18
  59.6 0.7 %add_convert_fusion = bf16[16,2048]{1,0:T(8,128)(2,1)} fusion(bf16[16,2048]{1,0:T(8,128)(2,1)S(1)} %collective-permute-done.18, bf16[16,2048]{1,0:T(8,128)(2,1)S(1)} %collective-permute-done.17, bf16[16,2048]{1,0:T(8,128)(2,1)S(1)} %collective-permute-done.16, bf16[16,2048]{1,0:T(8,128)(2,1)S(1)} %get-tuple-element.31), kind=kLoop, calls=%fused_computation | loop fusion | flops 262144 | bytes 327680 | tf_op jit(solution)/shard_map/convert_element_type | solution.py:312
  (20 shorter events, 0.1 us)
Async XLA Ops:
  0.0 12.2 %collective-permute-start.2 = (bf16[16,2048]{1,0:T(8,128)(2,1)}, bf16[16,2048]{1,0:T(8,128)(2,1)S(1)}, u32[]{:S(2)}, u32[]{:S(2)}) collective-permute-start(bf16[16,2048]{1,0:T(8,128)(2,1)} %tokens_ref.3), channel_id=1, source_target_pairs={{0,12},{4,8},{8,4},{12,0},{1,13},{5,9},{9,5},{13,1},{2,14},{6,10},... | collective-permute-start | bytes 196616 | tf_op jit(solution)/shard_map/ppermute | solution.py:271
  5.0 7.2 %collective-permute-start.1 = (bf16[16,2048]{1,0:T(8,128)(2,1)}, bf16[16,2048]{1,0:T(8,128)(2,1)S(1)}, u32[]{:S(2)}, u32[]{:S(2)}) collective-permute-start(bf16[16,2048]{1,0:T(8,128)(2,1)} %tokens_ref.3), channel_id=1, source_target_pairs={{0,8},{4,12},{8,0},{12,4},{1,9},{5,13},{9,1},{13,5},{2,10},{6,14},... | collective-permute-start | bytes 196616 | tf_op jit(solution)/shard_map/ppermute | solution.py:271
  5.1 7.2 %collective-permute-start = (bf16[16,2048]{1,0:T(8,128)(2,1)}, bf16[16,2048]{1,0:T(8,128)(2,1)S(1)}, u32[]{:S(2)}, u32[]{:S(2)}) collective-permute-start(bf16[16,2048]{1,0:T(8,128)(2,1)} %tokens_ref.3), channel_id=1, source_target_pairs={{0,4},{4,0},{8,12},{12,8},{1,5},{5,1},{9,13},{13,9},{2,6},{6,2},{1... | collective-permute-start | bytes 196616 | tf_op jit(solution)/shard_map/ppermute | solution.py:271
  5.6 6.7 %collective-permute-start.3 = (bf16[16,2048]{1,0:T(8,128)(2,1)}, bf16[16,2048]{1,0:T(8,128)(2,1)S(1)}, u32[]{:S(2)}, u32[]{:S(2)}) collective-permute-start(bf16[16,2048]{1,0:T(8,128)(2,1)} %tokens_ref.3), channel_id=1, source_target_pairs={{0,16},{16,0},{1,17},{17,1},{2,18},{18,2},{3,19},{19,3},{4,20},{20... | collective-permute-start | bytes 196616 | tf_op jit(solution)/shard_map/ppermute | solution.py:271
  12.3 5.8 %collective-permute-start.4 = (bf16[48,2048]{1,0:T(8,128)(2,1)S(1)}, bf16[48,2048]{1,0:T(8,128)(2,1)S(1)}, u32[]{:S(2)}, u32[]{:S(2)}) collective-permute-start(bf16[48,2048]{1,0:T(8,128)(2,1)S(1)} %join.3.refs_1_), channel_id=1, source_target_pairs={{0,16},{16,0},{1,17},{17,1},{2,18},{18,2},{3,19},{19,3},{4,20},{20... | collective-permute-start | bytes 589832 | tf_op jit(solution)/shard_map/ppermute | solution.py:271
  21.7 2.2 %collective-permute-start.5 = (bf16[2,64,2560]{2,1,0:T(8,128)(2,1)S(1)}, bf16[2,64,2560]{2,1,0:T(8,128)(2,1)S(1)}, u32[]{:S(2)}, u32[]{:S(2)}) collective-permute-start(bf16[2,64,2560]{2,1,0:T(8,128)(2,1)S(1)} %get-tuple-element.26), channel_id=1, source_target_pairs={{0,1},{1,0},{2,3},{3,2},{4,5},{5,4},{6,7},{7,6},{8,9},{9,8},{10,11... | collective-permute-start | bytes 1966088 | tf_op jit(solution)/shard_map/ppermute | solution.py:271
  23.9 19.8 %slice-start = ((s8[27262976]{0:T(1024)(128)(4,1)}), s8[4194304]{0:T(1024)(128)(4,1)S(1)}, s32[]{:S(2)}) async-start(s8[27262976]{0:T(1024)(128)(4,1)} %bitcast.2), calls=%async_computation | async-start | bytes 8388608
  23.9 19.8 %slice-start.1 = ((s8[27262976]{0:T(1024)(128)(4,1)}), s8[4194304]{0:T(1024)(128)(4,1)S(1)}, s32[]{:S(2)}) async-start(s8[27262976]{0:T(1024)(128)(4,1)} %bitcast.2), calls=%async_computation.1 | async-start | bytes 8388608
  24.0 19.7 %slice-start.2 = ((s8[27262976]{0:T(1024)(128)(4,1)}), s8[4194304]{0:T(1024)(128)(4,1)S(1)}, s32[]{:S(2)}) async-start(s8[27262976]{0:T(1024)(128)(4,1)} %bitcast.2), calls=%async_computation.2 | async-start | bytes 8388608
  24.0 19.7 %slice-start.3 = ((s8[27262976]{0:T(1024)(128)(4,1)}), s8[4194304]{0:T(1024)(128)(4,1)S(1)}, s32[]{:S(2)}) async-start(s8[27262976]{0:T(1024)(128)(4,1)} %bitcast.2), calls=%async_computation.3 | async-start | bytes 8388608
  24.0 19.7 %slice-start.4 = ((s8[27262976]{0:T(1024)(128)(4,1)}), s8[4194304]{0:T(1024)(128)(4,1)S(1)}, s32[]{:S(2)}) async-start(s8[27262976]{0:T(1024)(128)(4,1)} %bitcast.2), calls=%async_computation.4 | async-start | bytes 8388608
  24.0 19.7 %slice-start.5 = ((s8[27262976]{0:T(1024)(128)(4,1)}), s8[4194304]{0:T(1024)(128)(4,1)S(1)}, s32[]{:S(2)}) async-start(s8[27262976]{0:T(1024)(128)(4,1)} %bitcast.2), calls=%async_computation.5 | async-start | bytes 8388608
  24.0 19.7 %slice-start.6 = ((s8[27262976]{0:T(1024)(128)(4,1)}), s8[2097152]{0:T(1024)(128)(4,1)S(1)}, s32[]{:S(2)}) async-start(s8[27262976]{0:T(1024)(128)(4,1)} %bitcast.2), calls=%async_computation.6 | async-start | bytes 4194304
  24.0 9.8 %collective-permute-start.7 = (bf16[2,32,2560]{2,1,0:T(8,128)(2,1)S(1)}, bf16[2,32,2560]{2,1,0:T(8,128)(2,1)S(1)}, u32[]{:S(2)}, u32[]{:S(2)}) collective-permute-start(bf16[2,32,2560]{2,1,0:T(8,128)(2,1)S(1)} %pair_sum.2.refs_4_), channel_id=1, source_target_pairs={{0,2},{1,3},{2,0},{3,1},{4,6},{5,7},{6,4},{7,5},{8,10},{9,11},{10,... | collective-permute-start | bytes 983048 | tf_op jit(solution)/shard_map/ppermute | solution.py:271
  32.4 1.6 %collective-permute-start.6 = (bf16[2,32,1536]{2,1,0:T(8,128)(2,1)S(1)}, bf16[2,32,1536]{2,1,0:T(8,128)(2,1)S(1)}, u32[]{:S(2)}, u32[]{:S(2)}) collective-permute-start(bf16[2,32,1536]{2,1,0:T(8,128)(2,1)S(1)} %get-tuple-element.28), channel_id=1, source_target_pairs={{0,1},{1,0},{2,3},{3,2},{4,5},{5,4},{6,7},{7,6},{8,9},{9,8},{10,11... | collective-permute-start | bytes 589832 | tf_op jit(solution)/shard_map/ppermute | solution.py:271
  34.1 6.2 %collective-permute-start.8 = (bf16[2,16,1536]{2,1,0:T(8,128)(2,1)S(1)}, bf16[2,16,1536]{2,1,0:T(8,128)(2,1)S(1)}, u32[]{:S(2)}, u32[]{:S(2)}) collective-permute-start(bf16[2,16,1536]{2,1,0:T(8,128)(2,1)S(1)} %pair_sum.3), channel_id=1, source_target_pairs={{0,2},{1,3},{2,0},{3,1},{4,6},{5,7},{6,4},{7,5},{8,10},{9,11},{10,... | collective-permute-start | bytes 294920 | tf_op jit(solution)/shard_map/ppermute | solution.py:271
  35.8 4.4 %collective-permute-start.9 = (bf16[16,2560]{1,0:T(8,128)(2,1)S(1)}, bf16[16,2560]{1,0:T(8,128)(2,1)S(1)}, u32[]{:S(2)}, u32[]{:S(2)}) collective-permute-start(bf16[16,2560]{1,0:T(8,128)(2,1)S(1)} %get-tuple-element.29.refs_0_), channel_id=1, source_target_pairs={{0,16},{16,0},{1,17},{17,1},{2,18},{18,2},{3,19},{19,3},{4,20},{20... | collective-permute-start | bytes 245768 | tf_op jit(solution)/shard_map/ppermute | solution.py:271
  37.4 5.0 %collective-permute-start.12 = (bf16[16,2560]{1,0:T(8,128)(2,1)S(1)}, bf16[16,2560]{1,0:T(8,128)(2,1)S(1)}, u32[]{:S(2)}, u32[]{:S(2)}) collective-permute-start(bf16[16,2560]{1,0:T(8,128)(2,1)S(1)} %get-tuple-element.30.refs_0_), channel_id=1, source_target_pairs={{0,2},{1,3},{2,0},{3,1},{4,6},{5,7},{6,4},{7,5},{8,10},{9,11},{10,... | collective-permute-start | bytes 245768 | tf_op jit(solution)/shard_map/ppermute | solution.py:271
  40.4 5.5 %collective-permute-start.10 = (bf16[16,4096]{1,0:T(8,128)(2,1)S(1)}, bf16[16,4096]{1,0:T(8,128)(2,1)S(1)}, u32[]{:S(2)}, u32[]{:S(2)}) collective-permute-start(bf16[16,4096]{1,0:T(8,128)(2,1)S(1)} %combine.3.refs_1_.refs_0_), channel_id=1, source_target_pairs={{0,2},{1,3},{2,0},{3,1},{4,6},{5,7},{6,4},{7,5},{8,10},{9,11},{10,... | collective-permute-start | bytes 393224 | tf_op jit(solution)/shard_map/ppermute | solution.py:271
  41.3 1.6 %collective-permute-start.13 = (bf16[16,2560]{1,0:T(8,128)(2,1)S(1)}, bf16[16,2560]{1,0:T(8,128)(2,1)S(1)}, u32[]{:S(2)}, u32[]{:S(2)}) collective-permute-start(bf16[16,2560]{1,0:T(8,128)(2,1)S(1)} %get-tuple-element.30.refs_0_), channel_id=1, source_target_pairs={{0,1},{1,0},{2,3},{3,2},{4,5},{5,4},{6,7},{7,6},{8,9},{9,8},{10,11... | collective-permute-start | bytes 245768 | tf_op jit(solution)/shard_map/ppermute | solution.py:271
  42.4 1.3 %collective-permute-start.14 = (bf16[16,2560]{1,0:T(8,128)(2,1)S(1)}, bf16[16,2560]{1,0:T(8,128)(2,1)S(1)}, u32[]{:S(2)}, u32[]{:S(2)}) collective-permute-start(bf16[16,2560]{1,0:T(8,128)(2,1)S(1)} %join.4), channel_id=1, source_target_pairs={{0,1},{1,0},{2,3},{3,2},{4,5},{5,4},{6,7},{7,6},{8,9},{9,8},{10,11... | collective-permute-start | bytes 245768 | tf_op jit(solution)/shard_map/ppermute | solution.py:271
  42.4 3.7 %collective-permute-start.11 = (bf16[16,4096]{1,0:T(8,128)(2,1)S(1)}, bf16[16,4096]{1,0:T(8,128)(2,1)S(1)}, u32[]{:S(2)}, u32[]{:S(2)}) collective-permute-start(bf16[16,4096]{1,0:T(8,128)(2,1)S(1)} %combine.3.refs_1_.refs_0_), channel_id=1, source_target_pairs={{0,1},{1,0},{2,3},{3,2},{4,5},{5,4},{6,7},{7,6},{8,9},{9,8},{10,11... | collective-permute-start | bytes 393224 | tf_op jit(solution)/shard_map/ppermute | solution.py:271
  45.9 1.4 %collective-permute-start.15 = (bf16[16,4096]{1,0:T(8,128)(2,1)S(1)}, bf16[16,4096]{1,0:T(8,128)(2,1)S(1)}, u32[]{:S(2)}, u32[]{:S(2)}) collective-permute-start(bf16[16,4096]{1,0:T(8,128)(2,1)S(1)} %join.5), channel_id=1, source_target_pairs={{0,1},{1,0},{2,3},{3,2},{4,5},{5,4},{6,7},{7,6},{8,9},{9,8},{10,11... | collective-permute-start | bytes 393224 | tf_op jit(solution)/shard_map/ppermute | solution.py:271
  50.2 6.7 %collective-permute-start.16 = (bf16[16,2048]{1,0:T(8,128)(2,1)S(1)}, bf16[16,2048]{1,0:T(8,128)(2,1)S(1)}, u32[]{:S(2)}, u32[]{:S(2)}) collective-permute-start(bf16[16,2048]{1,0:T(8,128)(2,1)S(1)} %get-tuple-element.32), channel_id=1, source_target_pairs={{0,12},{4,8},{8,4},{12,0},{1,13},{5,9},{9,5},{13,1},{2,14},{6,10},... | collective-permute-start | bytes 196616 | tf_op jit(solution)/shard_map/ppermute | solution.py:271
  53.9 5.7 %collective-permute-start.17 = (bf16[16,2048]{1,0:T(8,128)(2,1)S(1)}, bf16[16,2048]{1,0:T(8,128)(2,1)S(1)}, u32[]{:S(2)}, u32[]{:S(2)}) collective-permute-start(bf16[16,2048]{1,0:T(8,128)(2,1)S(1)} %get-tuple-element.33), channel_id=1, source_target_pairs={{0,8},{4,12},{8,0},{12,4},{1,9},{5,13},{9,1},{13,5},{2,10},{6,14},... | collective-permute-start | bytes 196616 | tf_op jit(solution)/shard_map/ppermute | solution.py:271
  53.9 5.7 %collective-permute-start.18 = (bf16[16,2048]{1,0:T(8,128)(2,1)S(1)}, bf16[16,2048]{1,0:T(8,128)(2,1)S(1)}, u32[]{:S(2)}, u32[]{:S(2)}) collective-permute-start(bf16[16,2048]{1,0:T(8,128)(2,1)S(1)} %get-tuple-element.34), channel_id=1, source_target_pairs={{0,4},{4,0},{8,12},{12,8},{1,5},{5,1},{9,13},{13,9},{2,6},{6,2},{1... | collective-permute-start | bytes 196616 | tf_op jit(solution)/shard_map/ppermute | solution.py:271

commit v18 on v17

--- a/solution.py
+++ b/solution.py
@@ -8,7 +8,7 @@
 from jax.sharding import PartitionSpec as P
 
 TILE = 256
-LAST = 3
+CHUNKS = (4, 4, 2, 3)
 ROWS = 16
 COST = pl.CostEstimate(flops=0, bytes_accessed=1024, transcendentals=0)
 
@@ -102,19 +102,25 @@
     )(*arrays, *behind)
 
 
-def gate_up_kernel(n_arrays, n_pairs, segments, where, *refs):
-    arrays, weights = refs[:n_arrays], refs[n_arrays : n_arrays + 2 * n_pairs]
+def gate_up_kernel(n_arrays, n_weights, segments, where, *refs):
+    arrays, weights = refs[:n_arrays], refs[n_arrays : n_arrays + n_weights]
+    pieces, at = [], 0
     if segments:
         mine_ref, theirs_ref, x_ref, w_ref, sems = refs[-5:]
-        copies = [column_copies(weights[k], w_ref.at[k], segments, sems.at[k]) for k in range(2)]
+        *weights, gate_ref, up_ref = weights
+    else:
+        mine_ref, theirs_ref, x_ref = refs[-3:]
+    for gate, up in zip(weights[::2], weights[1::2]):
+        pieces += [(at, a, b, (gate, up), None) for a, b in pieces_of(gate.shape[1], 2 * TILE)]
+        at += gate.shape[1]
+    if segments:
+        starts = [(sign * where[0] + start if sign else start, width) for sign, start, width in segments]
+        copies = [column_copies(ref, w_ref.at[k], starts, sems.at[k]) for k, ref in enumerate((gate_ref, up_ref))]
         cuts = copies[0][1]
         for i in range(len(cuts)):
             for k in range(2):
                 copies[k][0][i].start()
-    else:
-        mine_ref, theirs_ref, x_ref = refs[-3:]
-        step = weights[0].shape[1]
-        cuts = [(p * step + a, p * step + b) for p in range(n_pairs) for a, b in pieces_of(step, 2 * TILE)]
+        pieces += [(at, a, b, (w_ref.at[0], w_ref.at[1]), i) for i, (a, b) in enumerate(cuts)]
     per = x_ref.shape[0] // (4 * ROWS)
     b = 0
     for array in arrays:
@@ -123,38 +129,36 @@
             x_ref[pl.ds(pl.multiple_of(to, ROWS), ROWS), :] = array[at : at + ROWS, :]
             b += 1
     half = x_ref.shape[0] // 2
-    for i, (a, b) in enumerate(cuts):
+    for at, a, b, refs, i in pieces:
         for k in range(2):
-            if segments:
+            if i is not None:
                 copies[k][0][i].wait()
-                weight = w_ref[k, :, a:b]
-            else:
-                p = a // step
-                weight = weights[2 * p + k][:, a - p * step : b - p * step]
-            part = jnp.dot(x_ref[...], weight, preferred_element_type=jnp.float32).astype(jnp.bfloat16)
-            mine_ref[k, :, a:b] = part[:half]
-            theirs_ref[k, :, a:b] = part[half:]
+            part = jnp.dot(x_ref[...], refs[k][:, a:b], preferred_element_type=jnp.float32).astype(jnp.bfloat16)
+            mine_ref[k, :, at + a : at + b] = part[:half]
+            theirs_ref[k, :, at + a : at + b] = part[half:]
 
 
 def gate_up(where, arrays, weights, segments, behind):
     depth = weights[0].shape[0]
-    width = sum(w for _, w in segments) if segments else sum(w.shape[1] for w in weights[::2])
+    near = weights[:-2] if segments else weights
+    streamed = sum(width for _, _, width in segments)
+    width = sum(w.shape[1] for w in near[::2]) + streamed
     total = sum(a.shape[0] for a in arrays)
     scratch = [pltpu.VMEM((total, depth), jnp.bfloat16)]
     if segments:
-        n_cuts = sum(len(pieces_of(w, 2 * TILE)) for _, w in segments)
-        scratch.append(pltpu.VMEM((2, depth, width), jnp.bfloat16))
+        n_cuts = sum(len(pieces_of(w, 2 * TILE)) for _, _, w in segments)
+        scratch.append(pltpu.VMEM((2, depth, streamed), jnp.bfloat16))
         scratch.append(pltpu.SemaphoreType.DMA((2, n_cuts)))
     return pl.pallas_call(
-        functools.partial(gate_up_kernel, len(arrays), len(weights) // 2, segments),
+        functools.partial(gate_up_kernel, len(arrays), len(weights), segments),
         in_specs=[spec(pltpu.SMEM)]
-        + [spec(pltpu.VMEM)] * len(arrays)
-        + [spec(pltpu.HBM if segments else pltpu.VMEM)] * len(weights)
+        + [spec(pltpu.VMEM)] * (len(arrays) + len(near))
+        + [spec(pltpu.HBM)] * (len(weights) - len(near))
         + [spec(pl.ANY)] * len(behind),
         out_specs=[spec(pltpu.VMEM)] * 2,
         scratch_shapes=scratch,
         out_shape=[jax.ShapeDtypeStruct((2, total // 2, width), jnp.bfloat16)] * 2,
-        compiler_params=params(16 if segments else 4),
+        compiler_params=params(4 + 4 * depth * streamed // 2**20),
         cost_estimate=COST,
         name="gate_up",
     )(where, *arrays, *weights, *behind)
@@ -270,28 +274,29 @@
         n = {"rep": 2, "hid": 4, "wid": 4}[axis]
         return lax.ppermute(x, axis, [(i, i ^ step) for i in range(n)])
 
-    tiles = half // TILE
-    bounds = [0, (tiles - LAST) // 2 * TILE, (tiles - LAST) * TILE, half]
-    widths = [b - a for a, b in zip(bounds[:-1], bounds[1:])]
+    bounds = [sum(CHUNKS[:c]) * TILE for c in range(5)]
+    widths = [n * TILE for n in CHUNKS]
+    split = bounds[3]
     gate_weight, up_weight, hbm_tokens = (
         pltpu.with_memory_space_constraint(w, pltpu.HBM) for w in (gate_weight, up_weight, tokens)
     )
     down_weight = pltpu.with_memory_space_constraint(down_weight, pltpu.VMEM)
 
-    far_own = swap(tokens, "rep", 1)
-    by_hid = [swap(tokens, "hid", d) for d in (3, 2, 1)][::-1]
+    by_hid = {d: swap(tokens, "hid", d) for d in (1, 3, 2)}
+    far_own, far_1 = swap(tokens, "rep", 1), swap(by_hid[1], "rep", 1)
     early = [fetch(where, gate_weight, up_weight, hbm_tokens, bounds[c], widths[c]) for c in range(2)]
     own = early[0][2]
-    near = join(by_hid, [own, far_own])
+    near = join([by_hid[2], by_hid[3]], [own, far_own, far_1])
     far = swap(near, "rep", 1)
 
-    weights = [w for fetched in early for w in fetched[:2]]
-    mine, theirs = gate_up(where, [own, near, far_own, far], weights, [], [])
+    weights = [w for fetched in early for w in fetched[:2]] + [gate_weight, up_weight]
+    arrays = [own, by_hid[1], near, far_own, far_1, far]
+    mine, theirs = gate_up(where, arrays, weights, [(1, bounds[2], widths[2])], [])
     got = swap(theirs, "wid", 1)
     to_chip = pair_sum(mine, got, [])
     from_chip = swap(to_chip, "wid", 2)
-    segments = [(bounds[2], widths[2]), (half + bounds[2], widths[2])]
-    last_mine, theirs = gate_up(where, [own, near], [gate_weight, up_weight], segments, [to_chip])
+    segments = [(0, split, widths[3]), (0, half + split, widths[3])]
+    last_mine, theirs = gate_up(where, arrays[:3], [gate_weight, up_weight], segments, [to_chip])
     last_got = swap(theirs, "wid", 1)
     keep, give = combine(mine, got, from_chip, [], [])
     last_to_chip = pair_sum(last_mine, last_got, [give])
@@ -302,9 +307,8 @@
         other = swap(hidden, "wid", 2)
         return [hidden, other, swap(hidden, "wid", 1), swap(join([other], behind), "wid", 1)]
 
-    acc = down(where, gather(keep, [rest]), down_weight, None, [(1, 0, bounds[2])], False)
-    rest_segments = [(-1, half, bounds[2])] + [(0, start, width) for start, width in segments]
-    acc = down(where, gather(rest, [acc]), down_weight, acc, rest_segments, True)
+    acc = down(where, gather(keep, [rest]), down_weight, None, [(1, 0, split)], False)
+    acc = down(where, gather(rest, [acc]), down_weight, acc, [(-1, half, split)] + segments, True)
 
     mixed = acc[0].astype(f32)
     for d in (3, 2, 1):
@@ -318,7 +322,7 @@
     def on_device(tokens, gate_weight, up_weight, down_weight):
         fits = (
             (n_rep, n_hid, n_wid) == (2, 4, 4)
-            and gate_weight.shape[1] % (n_rep * TILE) == 0
+            and gate_weight.shape[1] == n_rep * sum(CHUNKS) * TILE
             and tokens.shape[0] == ROWS
         )
         if not fits:

time: 60.4 us -> 62.3 us (1.031)
  waiting for transfers between devices: 13.8 us -> 15.3 us
    pallas_call x2, Pallas kernels: 10.2 us -> 12.1 us  [gate_up(): pl.pallas_call(functools.partial(gate_up_kernel, len(arrays), len(weights...]
    ppermute x19 -> x20, waiting for transfers between devices: 13.8 us -> 15.3 us  [swap(): return lax.ppermute(x, axis, [(i, i ^ step) for i in range(n)])]
    pallas_call x2, Pallas kernels: 10.2 us -> 8.9 us  [fetch(): pl.pallas_call(functools.partial(fetch_kernel, first), in_specs=[spec(plt...]
    ppermute x19 -> x20, starting transfers between devices: 19.6 us -> 19.4 us  [swap(): return lax.ppermute(x, axis, [(i, i ^ step) for i in range(n)])]
  transfers between devices with their start and end apart: 19 -> 20, of which waited for: 8 -> 10; matrix products, arithmetic and copies ran while one was open for 0% -> 0% of each run, Pallas kernels for 32% -> 29%
where the time goes in v18:
time: 62.3 us; the launch traced here: 62.1 us
  Pallas kernels  26.4 us (42%)
  starting transfers between devices  19.4 us (31%)
  waiting for transfers between devices  15.3 us (25%)
  other arithmetic  0.74 us (1%)
    ppermute x20, starting transfers between devices, swap(): return lax.ppermute(x, axis, [(i, i ^ step) for i in range(n)])  19.4 us
    ppermute x20, waiting for transfers between devices, swap(): return lax.ppermute(x, axis, [(i, i ^ step) for i in range(n)])  15.3 us
    pallas_call x2, Pallas kernels, gate_up(): pl.pallas_call(functools.partial(gate_up_kernel, len(arrays), len(weights...  12.1 us
    pallas_call x2, Pallas kernels, fetch(): pl.pallas_call(functools.partial(fetch_kernel, first), in_specs=[spec(plt...  8.9 us
    pallas_call x2, Pallas kernels, down(): pl.pallas_call(functools.partial(down_kernel, len(pieces), prev is not No...  5.02 us
  transfers between devices with their start and end apart: 20, of which 10 were waited for; matrix products, arithmetic and copies ran while one was open for 0% of the time, Pallas kernels for 29%

profile of v18, /device:TPU:0, one launch (start us, length us, event | category | flops | bytes accessed | tf_op | source)
XLA Modules:
  0.0 62.1 jit_solution(10607080629660689870)
XLA Ops:
  0.0 3.0 %collective-permute-start = (bf16[16,2048]{1,0:T(8,128)(2,1)}, bf16[16,2048]{1,0:T(8,128)(2,1)S(1)}, u32[]{:S(2)}, u32[]{:S(2)}) collective-permute-start(bf16[16,2048]{1,0:T(8,128)(2,1)} %tokens_ref.3), channel_id=1, source_target_pairs={{0,4},{4,0},{8,12},{12,8},{1,5},{5,1},{9,13},{13,9},{2,6},{6,2},{1... | collective-permute-start | bytes 196616 | tf_op jit(solution)/shard_map/ppermute | solution.py:275
  3.0 2.5 %collective-permute-start.2 = (bf16[16,2048]{1,0:T(8,128)(2,1)}, bf16[16,2048]{1,0:T(8,128)(2,1)S(1)}, u32[]{:S(2)}, u32[]{:S(2)}) collective-permute-start(bf16[16,2048]{1,0:T(8,128)(2,1)} %tokens_ref.3), channel_id=1, source_target_pairs={{0,12},{4,8},{8,4},{12,0},{1,13},{5,9},{9,5},{13,1},{2,14},{6,10},... | collective-permute-start | bytes 196616 | tf_op jit(solution)/shard_map/ppermute | solution.py:275
  5.5 0.1 collective-permute-start.1
  5.6 1.5 %collective-permute-start.3 = (bf16[16,2048]{1,0:T(8,128)(2,1)}, bf16[16,2048]{1,0:T(8,128)(2,1)S(1)}, u32[]{:S(2)}, u32[]{:S(2)}) collective-permute-start(bf16[16,2048]{1,0:T(8,128)(2,1)} %tokens_ref.3), channel_id=1, source_target_pairs={{0,16},{16,0},{1,17},{17,1},{2,18},{18,2},{3,19},{19,3},{4,20},{20... | collective-permute-start | bytes 196616 | tf_op jit(solution)/shard_map/ppermute | solution.py:275
  7.1 0.5 collective-permute-start.4
  7.6 0.1 pad_add_fusion.where
  7.7 4.1 %fetch.2 = (bf16[2048,1024]{1,0:T(8,128)(2,1)S(1)}, bf16[2048,1024]{1,0:T(8,128)(2,1)S(1)}, bf16[16,2048]{1,0:T(8,128)(2,1)S(1)}) custom-call(s32[2]{0:T(128)S(1)} %pad_add_fusion.where, bf16[2048,6656]{1,0:T(8,128)(2,1)} %refs_3_.1, bf16[2048,6656]{1,0:T(8,128)(2,1)} %refs_4_.3, bf16[16,2048]{1,0:T(8,128)(2,1)} %tokens_ref.3), custom_call_target="tpu_custom_call" | custom-call | bytes 1024 | tf_op jit(solution)/shard_map/fetch/pallas_call | solution.py:73
  11.9 0.3 collective-permute-done.1.refs_0_
  12.2 0.0 collective-permute-done.3.refs_3_
  12.2 1.6 %collective-permute-start.5 = (bf16[32,2048]{1,0:T(8,128)(2,1)S(1)}, bf16[32,2048]{1,0:T(8,128)(2,1)S(1)}, u32[]{:S(2)}, u32[]{:S(2)}) collective-permute-start(bf16[32,2048]{1,0:T(8,128)(2,1)S(1)} %join.3.refs_2_), channel_id=1, source_target_pairs={{0,16},{16,0},{1,17},{17,1},{2,18},{18,2},{3,19},{19,3},{4,20},{20... | collective-permute-start | bytes 393224 | tf_op jit(solution)/shard_map/ppermute | solution.py:275
  13.8 4.8 %fetch.3 = (bf16[2048,1024]{1,0:T(8,128)(2,1)S(1)}, bf16[2048,1024]{1,0:T(8,128)(2,1)S(1)}, bf16[16,2048]{1,0:T(8,128)(2,1)}) custom-call(s32[2]{0:T(128)S(1)} %pad_add_fusion.where, bf16[2048,6656]{1,0:T(8,128)(2,1)} %refs_3_.1, bf16[2048,6656]{1,0:T(8,128)(2,1)} %refs_4_.3, bf16[16,2048]{1,0:T(8,128)(2,1)} %tokens_ref.3), custom_call_target="tpu_custom_call" | custom-call | bytes 1024 | tf_op jit(solution)/shard_map/fetch/pallas_call | solution.py:73
  18.6 0.0 collective-permute-done.5.refs_5_
  18.6 5.5 %gate_up.2 = (bf16[2,64,2560]{2,1,0:T(8,128)(2,1)S(1)}, bf16[2,64,2560]{2,1,0:T(8,128)(2,1)S(1)}) custom-call(s32[2]{0:T(128)S(1)} %pad_add_fusion.where, bf16[16,2048]{1,0:T(8,128)(2,1)S(1)} %get-tuple-element.20.refs_2_.refs_0_, bf16[16,2048]{1,0:T(8,128)(2,1)S(1)} %collective-permute-done.refs_1_, bf16[32,2048]{1,0:T(8,128)(2,1)S(1)} %join.3.refs_2_, ...), custom_call_target="tpu_custom_call" | custom-call | bytes 1024 | tf_op jit(solution)/shard_map/gate_up/pallas_call | solution.py:152
  24.1 0.1 collective-permute-start.6
  24.1 2.1 %collective-permute-done.6.got_ref = bf16[2,64,2560]{2,1,0:T(8,128)(2,1)S(1)} collective-permute-done((bf16[2,64,2560]{2,1,0:T(8,128)(2,1)S(1)}, bf16[2,64,2560]{2,1,0:T(8,128)(2,1)S(1)}, u32[]{:S(2)}, u32[]{:S(2)}) %collective-permute-start.6) | collective-permute-done | bytes 655392 | tf_op jit(solution)/shard_map/ppermute | solution.py:275
  26.2 0.1 pair_sum.2.refs_5_
  26.3 0.0 slice-start.1
  26.3 0.0 slice-start.3
  26.3 0.0 slice-start.4
  26.4 1.6 %collective-permute-start.8 = (bf16[2,32,2560]{2,1,0:T(8,128)(2,1)S(1)}, bf16[2,32,2560]{2,1,0:T(8,128)(2,1)S(1)}, u32[]{:S(2)}, u32[]{:S(2)}) collective-permute-start(bf16[2,32,2560]{2,1,0:T(8,128)(2,1)S(1)} %pair_sum.2.refs_5_), channel_id=1, source_target_pairs={{0,2},{1,3},{2,0},{3,1},{4,6},{5,7},{6,4},{7,5},{8,10},{9,11},{10,... | collective-permute-start | bytes 983048 | tf_op jit(solution)/shard_map/ppermute | solution.py:275
  27.9 6.6 %gate_up.3 = (bf16[2,32,1536]{2,1,0:T(8,128)(2,1)S(1)}, bf16[2,32,1536]{2,1,0:T(8,128)(2,1)S(1)}) custom-call(s32[2]{0:T(128)S(1)} %pad_add_fusion.where, bf16[16,2048]{1,0:T(8,128)(2,1)S(1)} %get-tuple-element.20.refs_2_.refs_0_, bf16[16,2048]{1,0:T(8,128)(2,1)S(1)} %collective-permute-done.refs_1_, bf16[32,2048]{1,0:T(8,128)(2,1)S(1)} %join.3.refs_2_, ...), custom_call_target="tpu_custom_call" | custom-call | bytes 1024 | tf_op jit(solution)/shard_map/gate_up/pallas_call | solution.py:152
  34.6 0.1 collective-permute-start.7
  34.6 1.6 %collective-permute-done.8.chip_ref = bf16[2,32,2560]{2,1,0:T(8,128)(2,1)S(1)} collective-permute-done((bf16[2,32,2560]{2,1,0:T(8,128)(2,1)S(1)}, bf16[2,32,2560]{2,1,0:T(8,128)(2,1)S(1)}, u32[]{:S(2)}, u32[]{:S(2)}) %collective-permute-start.8) | collective-permute-done | bytes 327712 | tf_op jit(solution)/shard_map/ppermute | solution.py:275
  36.2 0.2 combine.2
  36.4 0.0 collective-permute-done.7.got_ref
  36.4 1.6 %collective-permute-start.9 = (bf16[2,16,1536]{2,1,0:T(8,128)(2,1)S(1)}, bf16[2,16,1536]{2,1,0:T(8,128)(2,1)S(1)}, u32[]{:S(2)}, u32[]{:S(2)}) collective-permute-start(bf16[2,16,1536]{2,1,0:T(8,128)(2,1)S(1)} %pair_sum.3), channel_id=1, source_target_pairs={{0,2},{1,3},{2,0},{3,1},{4,6},{5,7},{6,4},{7,5},{8,10},{9,11},{10,... | collective-permute-start | bytes 294920 | tf_op jit(solution)/shard_map/ppermute | solution.py:275
  38.0 0.6 collective-permute-start.10
  38.6 0.5 collective-permute-start.13
  39.1 3.3 %collective-permute-done.10.refs_0_ = bf16[16,2560]{1,0:T(8,128)(2,1)S(1)} collective-permute-done((bf16[16,2560]{1,0:T(8,128)(2,1)S(1)}, bf16[16,2560]{1,0:T(8,128)(2,1)S(1)}, u32[]{:S(2)}, u32[]{:S(2)}) %collective-permute-start.10) | collective-permute-done | bytes 81952 | tf_op jit(solution)/shard_map/ppermute | solution.py:275
  42.5 0.1 combine.3.refs_1_.refs_0_
  42.5 0.6 collective-permute-start.11
  43.1 0.0 collective-permute-start.14
  43.1 0.0 collective-permute-done.13.refs_0_.refs_1_
  43.1 0.6 collective-permute-start.15
  43.7 0.1 collective-permute-start.12
  43.8 0.6 collective-permute-done.14.refs_2_
  44.4 0.2 collective-permute-done.15.refs_3_
  44.7 2.1 %down.2.refs_1_.refs_5_ = f32[64,2048]{1,0:T(8,128)S(1)} custom-call(s32[2]{0:T(128)S(1)} %pad_add_fusion.where, bf16[16,2560]{1,0:T(8,128)(2,1)S(1)} %get-tuple-element.30.refs_0_, bf16[16,2560]{1,0:T(8,128)(2,1)S(1)} %collective-permute-done.13.refs_0_.refs_1_, bf16[16,2560]{1,0:T(8,128)(2,1)S(1)} %collective-permute-done.14.refs_2_, ...), custom_call_target="tpu_custom_call" | custom-call | bytes 1024 | tf_op jit(solution)/shard_map/down/pallas_call | solution.py:255
  46.8 0.8 %collective-permute-done.11.refs_0_.refs_1_ = bf16[16,4096]{1,0:T(8,128)(2,1)S(1)} collective-permute-done((bf16[16,4096]{1,0:T(8,128)(2,1)S(1)}, bf16[16,4096]{1,0:T(8,128)(2,1)S(1)}, u32[]{:S(2)}, u32[]{:S(2)}) %collective-permute-start.11) | collective-permute-done | bytes 131104 | tf_op jit(solution)/shard_map/ppermute | solution.py:275
  47.6 0.1 collective-permute-start.16
  47.7 1.3 %collective-permute-done.16.refs_3_ = bf16[16,4096]{1,0:T(8,128)(2,1)S(1)} collective-permute-done((bf16[16,4096]{1,0:T(8,128)(2,1)S(1)}, bf16[16,4096]{1,0:T(8,128)(2,1)S(1)}, u32[]{:S(2)}, u32[]{:S(2)}) %collective-permute-start.16) | collective-permute-done | bytes 131104 | tf_op jit(solution)/shard_map/ppermute | solution.py:275
  49.0 2.9 %down.3 = (bf16[16,2048]{1,0:T(8,128)(2,1)S(1)}, bf16[16,2048]{1,0:T(8,128)(2,1)S(1)}, bf16[16,2048]{1,0:T(8,128)(2,1)S(1)}, bf16[16,2048]{1,0:T(8,128)(2,1)S(1)}) custom-call(s32[2]{0:T(128)S(1)} %pad_add_fusion.where, bf16[16,4096]{1,0:T(8,128)(2,1)S(1)} %combine.3.refs_1_.refs_0_, bf16[16,4096]{1,0:T(8,128)(2,1)S(1)} %collective-permute-done.11.refs_0_.refs_1_, ...), custom_call_target="tpu_custom_call" | custom-call | bytes 1024 | tf_op jit(solution)/shard_map/down/pallas_call | solution.py:255
  51.9 2.7 %collective-permute-start.17 = (bf16[16,2048]{1,0:T(8,128)(2,1)S(1)}, bf16[16,2048]{1,0:T(8,128)(2,1)S(1)}, u32[]{:S(2)}, u32[]{:S(2)}) collective-permute-start(bf16[16,2048]{1,0:T(8,128)(2,1)S(1)} %get-tuple-element.32), channel_id=1, source_target_pairs={{0,12},{4,8},{8,4},{12,0},{1,13},{5,9},{9,5},{13,1},{2,14},{6,10},... | collective-permute-start | bytes 196616 | tf_op jit(solution)/shard_map/ppermute | solution.py:275
  54.7 0.3 collective-permute-start.18
  55.0 1.4 %collective-permute-start.19 = (bf16[16,2048]{1,0:T(8,128)(2,1)S(1)}, bf16[16,2048]{1,0:T(8,128)(2,1)S(1)}, u32[]{:S(2)}, u32[]{:S(2)}) collective-permute-start(bf16[16,2048]{1,0:T(8,128)(2,1)S(1)} %get-tuple-element.34), channel_id=1, source_target_pairs={{0,4},{4,0},{8,12},{12,8},{1,5},{5,1},{9,13},{13,9},{2,6},{6,2},{1... | collective-permute-start | bytes 196616 | tf_op jit(solution)/shard_map/ppermute | solution.py:275
  56.4 2.0 %collective-permute-done.17 = bf16[16,2048]{1,0:T(8,128)(2,1)S(1)} collective-permute-done((bf16[16,2048]{1,0:T(8,128)(2,1)S(1)}, bf16[16,2048]{1,0:T(8,128)(2,1)S(1)}, u32[]{:S(2)}, u32[]{:S(2)}) %collective-permute-start.17) | collective-permute-done | bytes 65568 | tf_op jit(solution)/shard_map/ppermute | solution.py:275
  58.4 3.1 %collective-permute-done.18 = bf16[16,2048]{1,0:T(8,128)(2,1)S(1)} collective-permute-done((bf16[16,2048]{1,0:T(8,128)(2,1)S(1)}, bf16[16,2048]{1,0:T(8,128)(2,1)S(1)}, u32[]{:S(2)}, u32[]{:S(2)}) %collective-permute-start.18) | collective-permute-done | bytes 65568 | tf_op jit(solution)/shard_map/ppermute | solution.py:275
  61.4 0.7 %add_convert_fusion = bf16[16,2048]{1,0:T(8,128)(2,1)} fusion(bf16[16,2048]{1,0:T(8,128)(2,1)S(1)} %collective-permute-done.19, bf16[16,2048]{1,0:T(8,128)(2,1)S(1)} %collective-permute-done.18, bf16[16,2048]{1,0:T(8,128)(2,1)S(1)} %collective-permute-done.17, bf16[16,2048]{1,0:T(8,128)(2,1)S(1)} %get-tuple-element.31), kind=kLoop, calls=%fused_computation | loop fusion | flops 262144 | bytes 327680 | tf_op jit(solution)/shard_map/convert_element_type | solution.py:316
  (22 shorter events, 0.1 us)
Async XLA Ops:
  0.0 7.1 %collective-permute-start = (bf16[16,2048]{1,0:T(8,128)(2,1)}, bf16[16,2048]{1,0:T(8,128)(2,1)S(1)}, u32[]{:S(2)}, u32[]{:S(2)}) collective-permute-start(bf16[16,2048]{1,0:T(8,128)(2,1)} %tokens_ref.3), channel_id=1, source_target_pairs={{0,4},{4,0},{8,12},{12,8},{1,5},{5,1},{9,13},{13,9},{2,6},{6,2},{1... | collective-permute-start | bytes 196616 | tf_op jit(solution)/shard_map/ppermute | solution.py:275
  3.0 8.8 %collective-permute-start.2 = (bf16[16,2048]{1,0:T(8,128)(2,1)}, bf16[16,2048]{1,0:T(8,128)(2,1)S(1)}, u32[]{:S(2)}, u32[]{:S(2)}) collective-permute-start(bf16[16,2048]{1,0:T(8,128)(2,1)} %tokens_ref.3), channel_id=1, source_target_pairs={{0,12},{4,8},{8,4},{12,0},{1,13},{5,9},{9,5},{13,1},{2,14},{6,10},... | collective-permute-start | bytes 196616 | tf_op jit(solution)/shard_map/ppermute | solution.py:275
  5.5 6.7 %collective-permute-start.1 = (bf16[16,2048]{1,0:T(8,128)(2,1)}, bf16[16,2048]{1,0:T(8,128)(2,1)S(1)}, u32[]{:S(2)}, u32[]{:S(2)}) collective-permute-start(bf16[16,2048]{1,0:T(8,128)(2,1)} %tokens_ref.3), channel_id=1, source_target_pairs={{0,8},{4,12},{8,0},{12,4},{1,9},{5,13},{9,1},{13,5},{2,10},{6,14},... | collective-permute-start | bytes 196616 | tf_op jit(solution)/shard_map/ppermute | solution.py:275
  5.6 6.6 %collective-permute-start.3 = (bf16[16,2048]{1,0:T(8,128)(2,1)}, bf16[16,2048]{1,0:T(8,128)(2,1)S(1)}, u32[]{:S(2)}, u32[]{:S(2)}) collective-permute-start(bf16[16,2048]{1,0:T(8,128)(2,1)} %tokens_ref.3), channel_id=1, source_target_pairs={{0,16},{16,0},{1,17},{17,1},{2,18},{18,2},{3,19},{19,3},{4,20},{20... | collective-permute-start | bytes 196616 | tf_op jit(solution)/shard_map/ppermute | solution.py:275
  7.1 5.0 %collective-permute-start.4 = (bf16[16,2048]{1,0:T(8,128)(2,1)S(1)}, bf16[16,2048]{1,0:T(8,128)(2,1)S(1)}, u32[]{:S(2)}, u32[]{:S(2)}) collective-permute-start(bf16[16,2048]{1,0:T(8,128)(2,1)S(1)} %collective-permute-done.refs_1_), channel_id=1, source_target_pairs={{0,16},{16,0},{1,17},{17,1},{2,18},{18,2},{3,19},{19,3},{4,20},{20... | collective-permute-start | bytes 196616 | tf_op jit(solution)/shard_map/ppermute | solution.py:275
  12.2 6.4 %collective-permute-start.5 = (bf16[32,2048]{1,0:T(8,128)(2,1)S(1)}, bf16[32,2048]{1,0:T(8,128)(2,1)S(1)}, u32[]{:S(2)}, u32[]{:S(2)}) collective-permute-start(bf16[32,2048]{1,0:T(8,128)(2,1)S(1)} %join.3.refs_2_), channel_id=1, source_target_pairs={{0,16},{16,0},{1,17},{17,1},{2,18},{18,2},{3,19},{19,3},{4,20},{20... | collective-permute-start | bytes 393224 | tf_op jit(solution)/shard_map/ppermute | solution.py:275
  24.1 2.2 %collective-permute-start.6 = (bf16[2,64,2560]{2,1,0:T(8,128)(2,1)S(1)}, bf16[2,64,2560]{2,1,0:T(8,128)(2,1)S(1)}, u32[]{:S(2)}, u32[]{:S(2)}) collective-permute-start(bf16[2,64,2560]{2,1,0:T(8,128)(2,1)S(1)} %get-tuple-element.26), channel_id=1, source_target_pairs={{0,1},{1,0},{2,3},{3,2},{4,5},{5,4},{6,7},{7,6},{8,9},{9,8},{10,11... | collective-permute-start | bytes 1966088 | tf_op jit(solution)/shard_map/ppermute | solution.py:275
  26.2 18.4 %slice-start = ((s8[27262976]{0:T(1024)(128)(4,1)}), s8[4194304]{0:T(1024)(128)(4,1)S(1)}, s32[]{:S(2)}) async-start(s8[27262976]{0:T(1024)(128)(4,1)} %bitcast.2), calls=%async_computation | async-start | bytes 8388608
  26.3 18.3 %slice-start.1 = ((s8[27262976]{0:T(1024)(128)(4,1)}), s8[4194304]{0:T(1024)(128)(4,1)S(1)}, s32[]{:S(2)}) async-start(s8[27262976]{0:T(1024)(128)(4,1)} %bitcast.2), calls=%async_computation.1 | async-start | bytes 8388608
  26.3 18.3 %slice-start.2 = ((s8[27262976]{0:T(1024)(128)(4,1)}), s8[4194304]{0:T(1024)(128)(4,1)S(1)}, s32[]{:S(2)}) async-start(s8[27262976]{0:T(1024)(128)(4,1)} %bitcast.2), calls=%async_computation.2 | async-start | bytes 8388608
  26.3 18.3 %slice-start.3 = ((s8[27262976]{0:T(1024)(128)(4,1)}), s8[4194304]{0:T(1024)(128)(4,1)S(1)}, s32[]{:S(2)}) async-start(s8[27262976]{0:T(1024)(128)(4,1)} %bitcast.2), calls=%async_computation.3 | async-start | bytes 8388608
  26.3 18.3 %slice-start.4 = ((s8[27262976]{0:T(1024)(128)(4,1)}), s8[4194304]{0:T(1024)(128)(4,1)S(1)}, s32[]{:S(2)}) async-start(s8[27262976]{0:T(1024)(128)(4,1)} %bitcast.2), calls=%async_computation.4 | async-start | bytes 8388608
  26.4 18.3 %slice-start.5 = ((s8[27262976]{0:T(1024)(128)(4,1)}), s8[4194304]{0:T(1024)(128)(4,1)S(1)}, s32[]{:S(2)}) async-start(s8[27262976]{0:T(1024)(128)(4,1)} %bitcast.2), calls=%async_computation.5 | async-start | bytes 8388608
  26.4 18.3 %slice-start.6 = ((s8[27262976]{0:T(1024)(128)(4,1)}), s8[2097152]{0:T(1024)(128)(4,1)S(1)}, s32[]{:S(2)}) async-start(s8[27262976]{0:T(1024)(128)(4,1)} %bitcast.2), calls=%async_computation.6 | async-start | bytes 4194304
  26.4 9.8 %collective-permute-start.8 = (bf16[2,32,2560]{2,1,0:T(8,128)(2,1)S(1)}, bf16[2,32,2560]{2,1,0:T(8,128)(2,1)S(1)}, u32[]{:S(2)}, u32[]{:S(2)}) collective-permute-start(bf16[2,32,2560]{2,1,0:T(8,128)(2,1)S(1)} %pair_sum.2.refs_5_), channel_id=1, source_target_pairs={{0,2},{1,3},{2,0},{3,1},{4,6},{5,7},{6,4},{7,5},{8,10},{9,11},{10,... | collective-permute-start | bytes 983048 | tf_op jit(solution)/shard_map/ppermute | solution.py:275
  34.6 1.8 %collective-permute-start.7 = (bf16[2,32,1536]{2,1,0:T(8,128)(2,1)S(1)}, bf16[2,32,1536]{2,1,0:T(8,128)(2,1)S(1)}, u32[]{:S(2)}, u32[]{:S(2)}) collective-permute-start(bf16[2,32,1536]{2,1,0:T(8,128)(2,1)S(1)} %get-tuple-element.28), channel_id=1, source_target_pairs={{0,1},{1,0},{2,3},{3,2},{4,5},{5,4},{6,7},{7,6},{8,9},{9,8},{10,11... | collective-permute-start | bytes 589832 | tf_op jit(solution)/shard_map/ppermute | solution.py:275
  36.4 6.0 %collective-permute-start.9 = (bf16[2,16,1536]{2,1,0:T(8,128)(2,1)S(1)}, bf16[2,16,1536]{2,1,0:T(8,128)(2,1)S(1)}, u32[]{:S(2)}, u32[]{:S(2)}) collective-permute-start(bf16[2,16,1536]{2,1,0:T(8,128)(2,1)S(1)} %pair_sum.3), channel_id=1, source_target_pairs={{0,2},{1,3},{2,0},{3,1},{4,6},{5,7},{6,4},{7,5},{8,10},{9,11},{10,... | collective-permute-start | bytes 294920 | tf_op jit(solution)/shard_map/ppermute | solution.py:275
  38.0 4.4 %collective-permute-start.10 = (bf16[16,2560]{1,0:T(8,128)(2,1)S(1)}, bf16[16,2560]{1,0:T(8,128)(2,1)S(1)}, u32[]{:S(2)}, u32[]{:S(2)}) collective-permute-start(bf16[16,2560]{1,0:T(8,128)(2,1)S(1)} %get-tuple-element.29.refs_0_), channel_id=1, source_target_pairs={{0,16},{16,0},{1,17},{17,1},{2,18},{18,2},{3,19},{19,3},{4,20},{20... | collective-permute-start | bytes 245768 | tf_op jit(solution)/shard_map/ppermute | solution.py:275
  38.6 4.6 %collective-permute-start.13 = (bf16[16,2560]{1,0:T(8,128)(2,1)S(1)}, bf16[16,2560]{1,0:T(8,128)(2,1)S(1)}, u32[]{:S(2)}, u32[]{:S(2)}) collective-permute-start(bf16[16,2560]{1,0:T(8,128)(2,1)S(1)} %get-tuple-element.30.refs_0_), channel_id=1, source_target_pairs={{0,2},{1,3},{2,0},{3,1},{4,6},{5,7},{6,4},{7,5},{8,10},{9,11},{10,... | collective-permute-start | bytes 245768 | tf_op jit(solution)/shard_map/ppermute | solution.py:275
  42.5 5.0 %collective-permute-start.11 = (bf16[16,4096]{1,0:T(8,128)(2,1)S(1)}, bf16[16,4096]{1,0:T(8,128)(2,1)S(1)}, u32[]{:S(2)}, u32[]{:S(2)}) collective-permute-start(bf16[16,4096]{1,0:T(8,128)(2,1)S(1)} %combine.3.refs_1_.refs_0_), channel_id=1, source_target_pairs={{0,2},{1,3},{2,0},{3,1},{4,6},{5,7},{6,4},{7,5},{8,10},{9,11},{10,... | collective-permute-start | bytes 393224 | tf_op jit(solution)/shard_map/ppermute | solution.py:275
  43.1 1.3 %collective-permute-start.14 = (bf16[16,2560]{1,0:T(8,128)(2,1)S(1)}, bf16[16,2560]{1,0:T(8,128)(2,1)S(1)}, u32[]{:S(2)}, u32[]{:S(2)}) collective-permute-start(bf16[16,2560]{1,0:T(8,128)(2,1)S(1)} %get-tuple-element.30.refs_0_), channel_id=1, source_target_pairs={{0,1},{1,0},{2,3},{3,2},{4,5},{5,4},{6,7},{7,6},{8,9},{9,8},{10,11... | collective-permute-start | bytes 245768 | tf_op jit(solution)/shard_map/ppermute | solution.py:275
  43.1 1.5 %collective-permute-start.15 = (bf16[16,2560]{1,0:T(8,128)(2,1)S(1)}, bf16[16,2560]{1,0:T(8,128)(2,1)S(1)}, u32[]{:S(2)}, u32[]{:S(2)}) collective-permute-start(bf16[16,2560]{1,0:T(8,128)(2,1)S(1)} %join.4), channel_id=1, source_target_pairs={{0,1},{1,0},{2,3},{3,2},{4,5},{5,4},{6,7},{7,6},{8,9},{9,8},{10,11... | collective-permute-start | bytes 245768 | tf_op jit(solution)/shard_map/ppermute | solution.py:275
  43.7 4.0 %collective-permute-start.12 = (bf16[16,4096]{1,0:T(8,128)(2,1)S(1)}, bf16[16,4096]{1,0:T(8,128)(2,1)S(1)}, u32[]{:S(2)}, u32[]{:S(2)}) collective-permute-start(bf16[16,4096]{1,0:T(8,128)(2,1)S(1)} %combine.3.refs_1_.refs_0_), channel_id=1, source_target_pairs={{0,1},{1,0},{2,3},{3,2},{4,5},{5,4},{6,7},{7,6},{8,9},{9,8},{10,11... | collective-permute-start | bytes 393224 | tf_op jit(solution)/shard_map/ppermute | solution.py:275
  47.6 1.4 %collective-permute-start.16 = (bf16[16,4096]{1,0:T(8,128)(2,1)S(1)}, bf16[16,4096]{1,0:T(8,128)(2,1)S(1)}, u32[]{:S(2)}, u32[]{:S(2)}) collective-permute-start(bf16[16,4096]{1,0:T(8,128)(2,1)S(1)} %join.5), channel_id=1, source_target_pairs={{0,1},{1,0},{2,3},{3,2},{4,5},{5,4},{6,7},{7,6},{8,9},{9,8},{10,11... | collective-permute-start | bytes 393224 | tf_op jit(solution)/shard_map/ppermute | solution.py:275
  51.9 6.4 %collective-permute-start.17 = (bf16[16,2048]{1,0:T(8,128)(2,1)S(1)}, bf16[16,2048]{1,0:T(8,128)(2,1)S(1)}, u32[]{:S(2)}, u32[]{:S(2)}) collective-permute-start(bf16[16,2048]{1,0:T(8,128)(2,1)S(1)} %get-tuple-element.32), channel_id=1, source_target_pairs={{0,12},{4,8},{8,4},{12,0},{1,13},{5,9},{9,5},{13,1},{2,14},{6,10},... | collective-permute-start | bytes 196616 | tf_op jit(solution)/shard_map/ppermute | solution.py:275
  54.7 6.8 %collective-permute-start.18 = (bf16[16,2048]{1,0:T(8,128)(2,1)S(1)}, bf16[16,2048]{1,0:T(8,128)(2,1)S(1)}, u32[]{:S(2)}, u32[]{:S(2)}) collective-permute-start(bf16[16,2048]{1,0:T(8,128)(2,1)S(1)} %get-tuple-element.33), channel_id=1, source_target_pairs={{0,8},{4,12},{8,0},{12,4},{1,9},{5,13},{9,1},{13,5},{2,10},{6,14},... | collective-permute-start | bytes 196616 | tf_op jit(solution)/shard_map/ppermute | solution.py:275
  55.0 6.5 %collective-permute-start.19 = (bf16[16,2048]{1,0:T(8,128)(2,1)S(1)}, bf16[16,2048]{1,0:T(8,128)(2,1)S(1)}, u32[]{:S(2)}, u32[]{:S(2)}) collective-permute-start(bf16[16,2048]{1,0:T(8,128)(2,1)S(1)} %get-tuple-element.34), channel_id=1, source_target_pairs={{0,4},{4,0},{8,12},{12,8},{1,5},{5,1},{9,13},{13,9},{2,6},{6,2},{1... | collective-permute-start | bytes 196616 | tf_op jit(solution)/shard_map/ppermute | solution.py:275

commit v19 on v17

--- a/solution.py
+++ b/solution.py
@@ -39,6 +39,10 @@
     return (step % 2) * 2 + step // 2
 
 
+def here(half):
+    return lax.axis_index("rep") * half, lax.axis_index("wid")
+
+
 def spec(space):
     return pl.BlockSpec(memory_space=space)
 
@@ -58,7 +62,8 @@
     return copies, cuts
 
 
-def fetch_kernel(first, where, gate_ref, up_ref, tokens_ref, gate_out, up_out, tokens_out, sems):
+def fetch_kernel(first, gate_ref, up_ref, tokens_ref, gate_out, up_out, tokens_out, sems):
+    where = here(gate_ref.shape[1] // 2)
     copies = [pltpu.make_async_copy(tokens_ref, tokens_out, sems.at[2, 0])]
     for k, (source, out) in enumerate(((gate_ref, gate_out), (up_ref, up_out))):
         copies += column_copies(source, out, [(where[0] + first, out.shape[1])], sems.at[k])[0]
@@ -68,18 +73,18 @@
         copy.wait()
 
 
-def fetch(where, gate, up, tokens, first, width):
+def fetch(gate, up, tokens, first, width):
     depth = gate.shape[0]
     return pl.pallas_call(
         functools.partial(fetch_kernel, first),
-        in_specs=[spec(pltpu.SMEM)] + [spec(pltpu.HBM)] * 3,
+        in_specs=[spec(pltpu.HBM)] * 3,
         out_specs=[spec(pltpu.VMEM)] * 3,
         out_shape=[pltpu.VMEM(x, jnp.bfloat16) for x in ((depth, width), (depth, width), tokens.shape)],
         scratch_shapes=[pltpu.SemaphoreType.DMA((3, len(pieces_of(width, 2 * TILE))))],
         compiler_params=params(1),
         cost_estimate=COST,
         name="fetch",
-    )(where, gate, up, tokens)
+    )(gate, up, tokens)
 
 
 def join_kernel(n, first, *refs):
@@ -102,7 +107,8 @@
     )(*arrays, *behind)
 
 
-def gate_up_kernel(n_arrays, n_pairs, segments, where, *refs):
+def gate_up_kernel(n_arrays, n_pairs, segments, *refs):
+    where = here(0)
     arrays, weights = refs[:n_arrays], refs[n_arrays : n_arrays + 2 * n_pairs]
     if segments:
         mine_ref, theirs_ref, x_ref, w_ref, sems = refs[-5:]
@@ -136,7 +142,7 @@
             theirs_ref[k, :, a:b] = part[half:]
 
 
-def gate_up(where, arrays, weights, segments, behind):
+def gate_up(arrays, weights, segments, behind):
     depth = weights[0].shape[0]
     width = sum(w for _, w in segments) if segments else sum(w.shape[1] for w in weights[::2])
     total = sum(a.shape[0] for a in arrays)
@@ -147,8 +153,7 @@
         scratch.append(pltpu.SemaphoreType.DMA((2, n_cuts)))
     return pl.pallas_call(
         functools.partial(gate_up_kernel, len(arrays), len(weights) // 2, segments),
-        in_specs=[spec(pltpu.SMEM)]
-        + [spec(pltpu.VMEM)] * len(arrays)
+        in_specs=[spec(pltpu.VMEM)] * len(arrays)
         + [spec(pltpu.HBM if segments else pltpu.VMEM)] * len(weights)
         + [spec(pl.ANY)] * len(behind),
         out_specs=[spec(pltpu.VMEM)] * 2,
@@ -157,7 +162,7 @@
         compiler_params=params(16 if segments else 4),
         cost_estimate=COST,
         name="gate_up",
-    )(where, *arrays, *weights, *behind)
+    )(*arrays, *weights, *behind)
 
 
 def pair_sum_kernel(mine_ref, got_ref, *refs):
@@ -214,9 +219,10 @@
     )(mine, got, from_chip, *left, *behind)
 
 
-def down_kernel(n_pieces, has_acc, last, segments, where, *refs):
+def down_kernel(n_pieces, has_acc, last, segments, *refs):
     pieces, refs = refs[:n_pieces], refs[n_pieces:]
     down_ref, refs = refs[0], refs[1:]
+    where = here(down_ref.shape[0] // 2)
     prev_ref, refs = (refs[0], refs[1:]) if has_acc else (None, refs)
     outs, (acc_ref, lhs_ref) = refs[:-2], refs[-2:]
     at = 0
@@ -240,7 +246,7 @@
             out[...] = acc_ref[pl.ds(source, ROWS), :].astype(out.dtype)
 
 
-def down(where, pieces, down_weight, prev, segments, last):
+def down(pieces, down_weight, prev, segments, last):
     width = down_weight.shape[1]
     total = 4 * ROWS
     args = [*pieces, down_weight] + ([] if prev is None else [prev])
@@ -250,21 +256,19 @@
         scratch = [pltpu.VMEM(sums.shape, sums.dtype)] + scratch
     return pl.pallas_call(
         functools.partial(down_kernel, len(pieces), prev is not None, last, segments),
-        in_specs=[spec(pltpu.SMEM)] + [spec(pltpu.VMEM)] * len(args),
+        in_specs=[spec(pltpu.VMEM)] * len(args),
         out_specs=[spec(pltpu.VMEM)] * 4 if last else spec(pltpu.VMEM),
         scratch_shapes=scratch,
         out_shape=[jax.ShapeDtypeStruct((ROWS, width), jnp.bfloat16)] * 4 if last else sums,
         compiler_params=params(4),
         cost_estimate=COST,
         name="down",
-    )(where, *args)
+    )(*args)
 
 
 def split_by_rep(tokens, gate_weight, up_weight, down_weight):
-    rep, wid = lax.axis_index("rep"), lax.axis_index("wid")
     f32, bf16 = jnp.float32, jnp.bfloat16
     half = gate_weight.shape[1] // 2
-    where = jnp.stack([rep * half, wid]).astype(jnp.int32)
 
     def swap(x, axis, step):
         n = {"rep": 2, "hid": 4, "wid": 4}[axis]
@@ -280,18 +284,18 @@
 
     far_own = swap(tokens, "rep", 1)
     by_hid = [swap(tokens, "hid", d) for d in (3, 2, 1)][::-1]
-    early = [fetch(where, gate_weight, up_weight, hbm_tokens, bounds[c], widths[c]) for c in range(2)]
+    early = [fetch(gate_weight, up_weight, hbm_tokens, bounds[c], widths[c]) for c in range(2)]
     own = early[0][2]
     near = join(by_hid, [own, far_own])
     far = swap(near, "rep", 1)
 
     weights = [w for fetched in early for w in fetched[:2]]
-    mine, theirs = gate_up(where, [own, near, far_own, far], weights, [], [])
+    mine, theirs = gate_up([own, near, far_own, far], weights, [], [])
     got = swap(theirs, "wid", 1)
     to_chip = pair_sum(mine, got, [])
     from_chip = swap(to_chip, "wid", 2)
     segments = [(bounds[2], widths[2]), (half + bounds[2], widths[2])]
-    last_mine, theirs = gate_up(where, [own, near], [gate_weight, up_weight], segments, [to_chip])
+    last_mine, theirs = gate_up([own, near], [gate_weight, up_weight], segments, [to_chip])
     last_got = swap(theirs, "wid", 1)
     keep, give = combine(mine, got, from_chip, [], [])
     last_to_chip = pair_sum(last_mine, last_got, [give])
@@ -302,9 +306,9 @@
         other = swap(hidden, "wid", 2)
         return [hidden, other, swap(hidden, "wid", 1), swap(join([other], behind), "wid", 1)]
 
-    acc = down(where, gather(keep, [rest]), down_weight, None, [(1, 0, bounds[2])], False)
+    acc = down(gather(keep, [rest]), down_weight, None, [(1, 0, bounds[2])], False)
     rest_segments = [(-1, half, bounds[2])] + [(0, start, width) for start, width in segments]
-    acc = down(where, gather(rest, [acc]), down_weight, acc, rest_segments, True)
+    acc = down(gather(rest, [acc]), down_weight, acc, rest_segments, True)
 
     mixed = acc[0].astype(f32)
     for d in (3, 2, 1):

time: 60.4 us -> 57.8 us (0.957)
  Pallas kernels: 25.9 us -> 22.5 us
    pallas_call x2, Pallas kernels: 10.2 us -> 9 us  [gate_up(): pl.pallas_call(functools.partial(gate_up_kernel, len(arrays), len(weights...]
    pallas_call x2, Pallas kernels: 5.02 us -> 3.92 us  [down(): pl.pallas_call(functools.partial(down_kernel, len(pieces), prev is not No...]
    pallas_call x2, Pallas kernels: 10.2 us -> 9.16 us  [fetch(): pl.pallas_call(functools.partial(fetch_kernel, first), in_specs=[spec(plt...]
    ppermute x19, waiting for transfers between devices: 13.8 us -> 14.4 us  [swap(): return lax.ppermute(x, axis, [(i, i ^ step) for i in range(n)])]
  transfers between devices with their start and end apart: 19 -> 19, of which waited for: 8 -> 10; matrix products, arithmetic and copies ran while one was open for 0% -> 0% of each run, Pallas kernels for 32% -> 30%
where the time goes in v19:
time: 57.8 us; the launch traced here: 57.7 us
  Pallas kernels  22.5 us (39%)
  starting transfers between devices  19.8 us (34%)
  waiting for transfers between devices  14.4 us (25%)
  other arithmetic  0.67 us (1%)
    ppermute x19, starting transfers between devices, swap(): return lax.ppermute(x, axis, [(i, i ^ step) for i in range(n)])  19.8 us
    ppermute x19, waiting for transfers between devices, swap(): return lax.ppermute(x, axis, [(i, i ^ step) for i in range(n)])  14.4 us
    pallas_call x2, Pallas kernels, fetch(): pl.pallas_call(functools.partial(fetch_kernel, first), in_specs=[spec(plt...  9.16 us
    pallas_call x2, Pallas kernels, gate_up(): pl.pallas_call(functools.partial(gate_up_kernel, len(arrays), len(weights...  9 us
    pallas_call x2, Pallas kernels, down(): pl.pallas_call(functools.partial(down_kernel, len(pieces), prev is not No...  3.92 us
  transfers between devices with their start and end apart: 19, of which 10 were waited for; matrix products, arithmetic and copies ran while one was open for 0% of the time, Pallas kernels for 30%

profile of v19, /device:TPU:0, one launch (start us, length us, event | category | flops | bytes accessed | tf_op | source)
XLA Modules:
  0.0 57.7 jit_solution(3426256185101031154)
XLA Ops:
  0.0 5.0 %collective-permute-start.2 = (bf16[16,2048]{1,0:T(8,128)(2,1)}, bf16[16,2048]{1,0:T(8,128)(2,1)S(1)}, u32[]{:S(2)}, u32[]{:S(2)}) collective-permute-start(bf16[16,2048]{1,0:T(8,128)(2,1)} %tokens_ref.3), channel_id=1, source_target_pairs={{0,12},{4,8},{8,4},{12,0},{1,13},{5,9},{9,5},{13,1},{2,14},{6,10},... | collective-permute-start | bytes 196616 | tf_op jit(solution)/shard_map/ppermute | solution.py:275
  5.0 0.0 collective-permute-start.1
  5.1 0.6 collective-permute-start
  5.6 1.7 %collective-permute-start.3 = (bf16[16,2048]{1,0:T(8,128)(2,1)}, bf16[16,2048]{1,0:T(8,128)(2,1)S(1)}, u32[]{:S(2)}, u32[]{:S(2)}) collective-permute-start(bf16[16,2048]{1,0:T(8,128)(2,1)} %tokens_ref.3), channel_id=1, source_target_pairs={{0,16},{16,0},{1,17},{17,1},{2,18},{18,2},{3,19},{19,3},{4,20},{20... | collective-permute-start | bytes 196616 | tf_op jit(solution)/shard_map/ppermute | solution.py:275
  7.4 4.3 %fetch.2 = (bf16[2048,1280]{1,0:T(8,128)(2,1)S(1)}, bf16[2048,1280]{1,0:T(8,128)(2,1)S(1)}, bf16[16,2048]{1,0:T(8,128)(2,1)S(1)}) custom-call(bf16[2048,6656]{1,0:T(8,128)(2,1)} %refs_2_.1, bf16[2048,6656]{1,0:T(8,128)(2,1)} %refs_3_.1, bf16[16,2048]{1,0:T(8,128)(2,1)} %tokens_ref.3), custom_call_target="tpu_custom_call" | custom-call | bytes 1024 | tf_op jit(solution)/shard_map/fetch/pallas_call | solution.py:78
  11.6 0.0 collective-permute-done.2.refs_2_
  11.6 0.0 collective-permute-done.1.refs_1_
  11.7 0.0 collective-permute-done.refs_0_
  11.7 0.0 collective-permute-done.3.refs_4_.refs_2_
  11.7 0.8 %collective-permute-start.4 = (bf16[48,2048]{1,0:T(8,128)(2,1)S(1)}, bf16[48,2048]{1,0:T(8,128)(2,1)S(1)}, u32[]{:S(2)}, u32[]{:S(2)}) collective-permute-start(bf16[48,2048]{1,0:T(8,128)(2,1)S(1)} %join.3.refs_1_), channel_id=1, source_target_pairs={{0,16},{16,0},{1,17},{17,1},{2,18},{18,2},{3,19},{19,3},{4,20},{20... | collective-permute-start | bytes 589832 | tf_op jit(solution)/shard_map/ppermute | solution.py:275
  12.5 4.9 %fetch.3 = (bf16[2048,1280]{1,0:T(8,128)(2,1)S(1)}, bf16[2048,1280]{1,0:T(8,128)(2,1)S(1)}, bf16[16,2048]{1,0:T(8,128)(2,1)}) custom-call(bf16[2048,6656]{1,0:T(8,128)(2,1)} %refs_2_.1, bf16[2048,6656]{1,0:T(8,128)(2,1)} %refs_3_.1, bf16[16,2048]{1,0:T(8,128)(2,1)} %tokens_ref.3), custom_call_target="tpu_custom_call" | custom-call | bytes 1024 | tf_op jit(solution)/shard_map/fetch/pallas_call | solution.py:78
  17.4 0.1 collective-permute-done.4.refs_3_
  17.4 2.9 %gate_up.2 = (bf16[2,64,2560]{2,1,0:T(8,128)(2,1)S(1)}, bf16[2,64,2560]{2,1,0:T(8,128)(2,1)S(1)}) custom-call(bf16[16,2048]{1,0:T(8,128)(2,1)S(1)} %get-tuple-element.20.refs_3_.refs_0_, bf16[48,2048]{1,0:T(8,128)(2,1)S(1)} %join.3.refs_1_, bf16[16,2048]{1,0:T(8,128)(2,1)S(1)} %collective-permute-done.3.refs_4_.refs_2_, ...), custom_call_target="tpu_custom_call" | custom-call | bytes 1024 | tf_op jit(solution)/shard_map/gate_up/pallas_call | solution.py:154
  20.4 0.1 collective-permute-start.5
  20.4 2.1 %collective-permute-done.5.got_ref = bf16[2,64,2560]{2,1,0:T(8,128)(2,1)S(1)} collective-permute-done((bf16[2,64,2560]{2,1,0:T(8,128)(2,1)S(1)}, bf16[2,64,2560]{2,1,0:T(8,128)(2,1)S(1)}, u32[]{:S(2)}, u32[]{:S(2)}) %collective-permute-start.5) | collective-permute-done | bytes 655392 | tf_op jit(solution)/shard_map/ppermute | solution.py:275
  22.5 0.1 pair_sum.2.refs_4_
  22.6 0.0 slice-start.1
  22.6 0.0 slice-start.2
  22.6 0.0 slice-start.3
  22.6 0.0 slice-start.4
  22.7 1.7 %collective-permute-start.7 = (bf16[2,32,2560]{2,1,0:T(8,128)(2,1)S(1)}, bf16[2,32,2560]{2,1,0:T(8,128)(2,1)S(1)}, u32[]{:S(2)}, u32[]{:S(2)}) collective-permute-start(bf16[2,32,2560]{2,1,0:T(8,128)(2,1)S(1)} %pair_sum.2.refs_4_), channel_id=1, source_target_pairs={{0,2},{1,3},{2,0},{3,1},{4,6},{5,7},{6,4},{7,5},{8,10},{9,11},{10,... | collective-permute-start | bytes 983048 | tf_op jit(solution)/shard_map/ppermute | solution.py:275
  24.4 6.1 %gate_up.3 = (bf16[2,32,1536]{2,1,0:T(8,128)(2,1)S(1)}, bf16[2,32,1536]{2,1,0:T(8,128)(2,1)S(1)}) custom-call(bf16[16,2048]{1,0:T(8,128)(2,1)S(1)} %get-tuple-element.20.refs_3_.refs_0_, bf16[48,2048]{1,0:T(8,128)(2,1)S(1)} %join.3.refs_1_, bf16[2048,6656]{1,0:T(8,128)(2,1)} %refs_2_.1, bf16[2048,6656]{1,0:T(8,128)(2,1)} %refs_3_.1, ...), custom_call_target="tpu_custom_call" | custom-call | bytes 1024 | tf_op jit(solution)/shard_map/gate_up/pallas_call | solution.py:154
  30.5 0.1 collective-permute-start.6
  30.6 1.9 %collective-permute-done.7.chip_ref = bf16[2,32,2560]{2,1,0:T(8,128)(2,1)S(1)} collective-permute-done((bf16[2,32,2560]{2,1,0:T(8,128)(2,1)S(1)}, bf16[2,32,2560]{2,1,0:T(8,128)(2,1)S(1)}, u32[]{:S(2)}, u32[]{:S(2)}) %collective-permute-start.7) | collective-permute-done | bytes 327712 | tf_op jit(solution)/shard_map/ppermute | solution.py:275
  32.5 0.2 combine.2
  32.7 0.0 collective-permute-done.6.got_ref
  32.7 1.7 %collective-permute-start.8 = (bf16[2,16,1536]{2,1,0:T(8,128)(2,1)S(1)}, bf16[2,16,1536]{2,1,0:T(8,128)(2,1)S(1)}, u32[]{:S(2)}, u32[]{:S(2)}) collective-permute-start(bf16[2,16,1536]{2,1,0:T(8,128)(2,1)S(1)} %pair_sum.3), channel_id=1, source_target_pairs={{0,2},{1,3},{2,0},{3,1},{4,6},{5,7},{6,4},{7,5},{8,10},{9,11},{10,... | collective-permute-start | bytes 294920 | tf_op jit(solution)/shard_map/ppermute | solution.py:275
  34.5 1.5 %collective-permute-start.9 = (bf16[16,2560]{1,0:T(8,128)(2,1)S(1)}, bf16[16,2560]{1,0:T(8,128)(2,1)S(1)}, u32[]{:S(2)}, u32[]{:S(2)}) collective-permute-start(bf16[16,2560]{1,0:T(8,128)(2,1)S(1)} %get-tuple-element.29.refs_0_), channel_id=1, source_target_pairs={{0,16},{16,0},{1,17},{17,1},{2,18},{18,2},{3,19},{19,3},{4,20},{20... | collective-permute-start | bytes 245768 | tf_op jit(solution)/shard_map/ppermute | solution.py:275
  36.0 0.5 collective-permute-start.12
  36.5 2.4 %collective-permute-done.9.refs_0_ = bf16[16,2560]{1,0:T(8,128)(2,1)S(1)} collective-permute-done((bf16[16,2560]{1,0:T(8,128)(2,1)S(1)}, bf16[16,2560]{1,0:T(8,128)(2,1)S(1)}, u32[]{:S(2)}, u32[]{:S(2)}) %collective-permute-start.9) | collective-permute-done | bytes 81952 | tf_op jit(solution)/shard_map/ppermute | solution.py:275
  38.9 0.1 combine.3.refs_1_.refs_0_
  39.0 1.0 %collective-permute-start.10 = (bf16[16,4096]{1,0:T(8,128)(2,1)S(1)}, bf16[16,4096]{1,0:T(8,128)(2,1)S(1)}, u32[]{:S(2)}, u32[]{:S(2)}) collective-permute-start(bf16[16,4096]{1,0:T(8,128)(2,1)S(1)} %combine.3.refs_1_.refs_0_), channel_id=1, source_target_pairs={{0,2},{1,3},{2,0},{3,1},{4,6},{5,7},{6,4},{7,5},{8,10},{9,11},{10,... | collective-permute-start | bytes 393224 | tf_op jit(solution)/shard_map/ppermute | solution.py:275
  39.9 0.0 collective-permute-start.13
  39.9 1.1 %collective-permute-done.12.refs_0_.refs_1_ = bf16[16,2560]{1,0:T(8,128)(2,1)S(1)} collective-permute-done((bf16[16,2560]{1,0:T(8,128)(2,1)S(1)}, bf16[16,2560]{1,0:T(8,128)(2,1)S(1)}, u32[]{:S(2)}, u32[]{:S(2)}) %collective-permute-start.12) | collective-permute-done | bytes 81952 | tf_op jit(solution)/shard_map/ppermute | solution.py:275
  41.0 0.5 collective-permute-start.11
  41.5 0.0 collective-permute-done.13.refs_2_
  41.5 0.8 %collective-permute-done.14.refs_3_ = bf16[16,2560]{1,0:T(8,128)(2,1)S(1)} collective-permute-done((bf16[16,2560]{1,0:T(8,128)(2,1)S(1)}, bf16[16,2560]{1,0:T(8,128)(2,1)S(1)}, u32[]{:S(2)}, u32[]{:S(2)}) %collective-permute-start.14) | collective-permute-done | bytes 81952 | tf_op jit(solution)/shard_map/ppermute | solution.py:275
  42.4 1.5 %down.2.refs_1_.refs_5_ = f32[64,2048]{1,0:T(8,128)S(1)} custom-call(bf16[16,2560]{1,0:T(8,128)(2,1)S(1)} %get-tuple-element.30.refs_0_, bf16[16,2560]{1,0:T(8,128)(2,1)S(1)} %collective-permute-done.12.refs_0_.refs_1_, bf16[16,2560]{1,0:T(8,128)(2,1)S(1)} %collective-permute-done.13.refs_2_, bf16[16,2560]{1,0:T(8,128)(2,1)S(1)} %collective-permute-done.14.refs_3_, ...), custom_call_target="tpu_custom_call" | custom-call | bytes 1024 | tf_op jit(solution)/shard_map/down/pallas_call | solution.py:257
  43.9 0.1 collective-permute-done.10.refs_0_.refs_1_
  44.0 0.1 collective-permute-start.15
  44.2 0.0 collective-permute-done.11.refs_2_
  44.2 1.3 %collective-permute-done.15.refs_3_ = bf16[16,4096]{1,0:T(8,128)(2,1)S(1)} collective-permute-done((bf16[16,4096]{1,0:T(8,128)(2,1)S(1)}, bf16[16,4096]{1,0:T(8,128)(2,1)S(1)}, u32[]{:S(2)}, u32[]{:S(2)}) %collective-permute-start.15) | collective-permute-done | bytes 131104 | tf_op jit(solution)/shard_map/ppermute | solution.py:275
  45.4 2.4 %down.3 = (bf16[16,2048]{1,0:T(8,128)(2,1)S(1)}, bf16[16,2048]{1,0:T(8,128)(2,1)S(1)}, bf16[16,2048]{1,0:T(8,128)(2,1)S(1)}, bf16[16,2048]{1,0:T(8,128)(2,1)S(1)}) custom-call(bf16[16,4096]{1,0:T(8,128)(2,1)S(1)} %combine.3.refs_1_.refs_0_, bf16[16,4096]{1,0:T(8,128)(2,1)S(1)} %collective-permute-done.10.refs_0_.refs_1_, ...), custom_call_target="tpu_custom_call" | custom-call | bytes 1024 | tf_op jit(solution)/shard_map/down/pallas_call | solution.py:257
  47.8 3.5 %collective-permute-start.16 = (bf16[16,2048]{1,0:T(8,128)(2,1)S(1)}, bf16[16,2048]{1,0:T(8,128)(2,1)S(1)}, u32[]{:S(2)}, u32[]{:S(2)}) collective-permute-start(bf16[16,2048]{1,0:T(8,128)(2,1)S(1)} %get-tuple-element.32), channel_id=1, source_target_pairs={{0,12},{4,8},{8,4},{12,0},{1,13},{5,9},{9,5},{13,1},{2,14},{6,10},... | collective-permute-start | bytes 196616 | tf_op jit(solution)/shard_map/ppermute | solution.py:275
  51.3 1.0 %collective-permute-start.18 = (bf16[16,2048]{1,0:T(8,128)(2,1)S(1)}, bf16[16,2048]{1,0:T(8,128)(2,1)S(1)}, u32[]{:S(2)}, u32[]{:S(2)}) collective-permute-start(bf16[16,2048]{1,0:T(8,128)(2,1)S(1)} %get-tuple-element.34), channel_id=1, source_target_pairs={{0,4},{4,0},{8,12},{12,8},{1,5},{5,1},{9,13},{13,9},{2,6},{6,2},{1... | collective-permute-start | bytes 196616 | tf_op jit(solution)/shard_map/ppermute | solution.py:275
  52.3 2.3 %collective-permute-done.16 = bf16[16,2048]{1,0:T(8,128)(2,1)S(1)} collective-permute-done((bf16[16,2048]{1,0:T(8,128)(2,1)S(1)}, bf16[16,2048]{1,0:T(8,128)(2,1)S(1)}, u32[]{:S(2)}, u32[]{:S(2)}) %collective-permute-start.16) | collective-permute-done | bytes 65568 | tf_op jit(solution)/shard_map/ppermute | solution.py:275
  54.6 2.4 %collective-permute-done.17 = bf16[16,2048]{1,0:T(8,128)(2,1)S(1)} collective-permute-done((bf16[16,2048]{1,0:T(8,128)(2,1)S(1)}, bf16[16,2048]{1,0:T(8,128)(2,1)S(1)}, u32[]{:S(2)}, u32[]{:S(2)}) %collective-permute-start.17) | collective-permute-done | bytes 65568 | tf_op jit(solution)/shard_map/ppermute | solution.py:275
  57.0 0.7 %add_convert_fusion = bf16[16,2048]{1,0:T(8,128)(2,1)} fusion(bf16[16,2048]{1,0:T(8,128)(2,1)S(1)} %collective-permute-done.18, bf16[16,2048]{1,0:T(8,128)(2,1)S(1)} %collective-permute-done.17, bf16[16,2048]{1,0:T(8,128)(2,1)S(1)} %collective-permute-done.16, bf16[16,2048]{1,0:T(8,128)(2,1)S(1)} %get-tuple-element.31), kind=kLoop, calls=%fused_computation | loop fusion | flops 262144 | bytes 327680 | tf_op jit(solution)/shard_map/convert_element_type | solution.py:316
  (19 shorter events, 0.1 us)
Async XLA Ops:
  0.0 11.6 %collective-permute-start.2 = (bf16[16,2048]{1,0:T(8,128)(2,1)}, bf16[16,2048]{1,0:T(8,128)(2,1)S(1)}, u32[]{:S(2)}, u32[]{:S(2)}) collective-permute-start(bf16[16,2048]{1,0:T(8,128)(2,1)} %tokens_ref.3), channel_id=1, source_target_pairs={{0,12},{4,8},{8,4},{12,0},{1,13},{5,9},{9,5},{13,1},{2,14},{6,10},... | collective-permute-start | bytes 196616 | tf_op jit(solution)/shard_map/ppermute | solution.py:275
  5.0 6.6 %collective-permute-start.1 = (bf16[16,2048]{1,0:T(8,128)(2,1)}, bf16[16,2048]{1,0:T(8,128)(2,1)S(1)}, u32[]{:S(2)}, u32[]{:S(2)}) collective-permute-start(bf16[16,2048]{1,0:T(8,128)(2,1)} %tokens_ref.3), channel_id=1, source_target_pairs={{0,8},{4,12},{8,0},{12,4},{1,9},{5,13},{9,1},{13,5},{2,10},{6,14},... | collective-permute-start | bytes 196616 | tf_op jit(solution)/shard_map/ppermute | solution.py:275
  5.1 6.6 %collective-permute-start = (bf16[16,2048]{1,0:T(8,128)(2,1)}, bf16[16,2048]{1,0:T(8,128)(2,1)S(1)}, u32[]{:S(2)}, u32[]{:S(2)}) collective-permute-start(bf16[16,2048]{1,0:T(8,128)(2,1)} %tokens_ref.3), channel_id=1, source_target_pairs={{0,4},{4,0},{8,12},{12,8},{1,5},{5,1},{9,13},{13,9},{2,6},{6,2},{1... | collective-permute-start | bytes 196616 | tf_op jit(solution)/shard_map/ppermute | solution.py:275
  5.6 6.0 %collective-permute-start.3 = (bf16[16,2048]{1,0:T(8,128)(2,1)}, bf16[16,2048]{1,0:T(8,128)(2,1)S(1)}, u32[]{:S(2)}, u32[]{:S(2)}) collective-permute-start(bf16[16,2048]{1,0:T(8,128)(2,1)} %tokens_ref.3), channel_id=1, source_target_pairs={{0,16},{16,0},{1,17},{17,1},{2,18},{18,2},{3,19},{19,3},{4,20},{20... | collective-permute-start | bytes 196616 | tf_op jit(solution)/shard_map/ppermute | solution.py:275
  11.7 5.7 %collective-permute-start.4 = (bf16[48,2048]{1,0:T(8,128)(2,1)S(1)}, bf16[48,2048]{1,0:T(8,128)(2,1)S(1)}, u32[]{:S(2)}, u32[]{:S(2)}) collective-permute-start(bf16[48,2048]{1,0:T(8,128)(2,1)S(1)} %join.3.refs_1_), channel_id=1, source_target_pairs={{0,16},{16,0},{1,17},{17,1},{2,18},{18,2},{3,19},{19,3},{4,20},{20... | collective-permute-start | bytes 589832 | tf_op jit(solution)/shard_map/ppermute | solution.py:275
  20.4 2.2 %collective-permute-start.5 = (bf16[2,64,2560]{2,1,0:T(8,128)(2,1)S(1)}, bf16[2,64,2560]{2,1,0:T(8,128)(2,1)S(1)}, u32[]{:S(2)}, u32[]{:S(2)}) collective-permute-start(bf16[2,64,2560]{2,1,0:T(8,128)(2,1)S(1)} %get-tuple-element.26), channel_id=1, source_target_pairs={{0,1},{1,0},{2,3},{3,2},{4,5},{5,4},{6,7},{7,6},{8,9},{9,8},{10,11... | collective-permute-start | bytes 1966088 | tf_op jit(solution)/shard_map/ppermute | solution.py:275
  22.5 19.8 %slice-start = ((s8[27262976]{0:T(1024)(128)(4,1)}), s8[4194304]{0:T(1024)(128)(4,1)S(1)}, s32[]{:S(2)}) async-start(s8[27262976]{0:T(1024)(128)(4,1)} %bitcast), calls=%async_computation | async-start | bytes 8388608
  22.6 19.7 %slice-start.1 = ((s8[27262976]{0:T(1024)(128)(4,1)}), s8[4194304]{0:T(1024)(128)(4,1)S(1)}, s32[]{:S(2)}) async-start(s8[27262976]{0:T(1024)(128)(4,1)} %bitcast), calls=%async_computation.1 | async-start | bytes 8388608
  22.6 19.7 %slice-start.2 = ((s8[27262976]{0:T(1024)(128)(4,1)}), s8[4194304]{0:T(1024)(128)(4,1)S(1)}, s32[]{:S(2)}) async-start(s8[27262976]{0:T(1024)(128)(4,1)} %bitcast), calls=%async_computation.2 | async-start | bytes 8388608
  22.6 19.7 %slice-start.3 = ((s8[27262976]{0:T(1024)(128)(4,1)}), s8[4194304]{0:T(1024)(128)(4,1)S(1)}, s32[]{:S(2)}) async-start(s8[27262976]{0:T(1024)(128)(4,1)} %bitcast), calls=%async_computation.3 | async-start | bytes 8388608
  22.6 19.7 %slice-start.4 = ((s8[27262976]{0:T(1024)(128)(4,1)}), s8[4194304]{0:T(1024)(128)(4,1)S(1)}, s32[]{:S(2)}) async-start(s8[27262976]{0:T(1024)(128)(4,1)} %bitcast), calls=%async_computation.4 | async-start | bytes 8388608
  22.7 19.7 %slice-start.5 = ((s8[27262976]{0:T(1024)(128)(4,1)}), s8[4194304]{0:T(1024)(128)(4,1)S(1)}, s32[]{:S(2)}) async-start(s8[27262976]{0:T(1024)(128)(4,1)} %bitcast), calls=%async_computation.5 | async-start | bytes 8388608
  22.7 19.7 %slice-start.6 = ((s8[27262976]{0:T(1024)(128)(4,1)}), s8[2097152]{0:T(1024)(128)(4,1)S(1)}, s32[]{:S(2)}) async-start(s8[27262976]{0:T(1024)(128)(4,1)} %bitcast), calls=%async_computation.6 | async-start | bytes 4194304
  22.7 9.8 %collective-permute-start.7 = (bf16[2,32,2560]{2,1,0:T(8,128)(2,1)S(1)}, bf16[2,32,2560]{2,1,0:T(8,128)(2,1)S(1)}, u32[]{:S(2)}, u32[]{:S(2)}) collective-permute-start(bf16[2,32,2560]{2,1,0:T(8,128)(2,1)S(1)} %pair_sum.2.refs_4_), channel_id=1, source_target_pairs={{0,2},{1,3},{2,0},{3,1},{4,6},{5,7},{6,4},{7,5},{8,10},{9,11},{10,... | collective-permute-start | bytes 983048 | tf_op jit(solution)/shard_map/ppermute | solution.py:275
  30.5 2.2 %collective-permute-start.6 = (bf16[2,32,1536]{2,1,0:T(8,128)(2,1)S(1)}, bf16[2,32,1536]{2,1,0:T(8,128)(2,1)S(1)}, u32[]{:S(2)}, u32[]{:S(2)}) collective-permute-start(bf16[2,32,1536]{2,1,0:T(8,128)(2,1)S(1)} %get-tuple-element.28), channel_id=1, source_target_pairs={{0,1},{1,0},{2,3},{3,2},{4,5},{5,4},{6,7},{7,6},{8,9},{9,8},{10,11... | collective-permute-start | bytes 589832 | tf_op jit(solution)/shard_map/ppermute | solution.py:275
  32.7 6.2 %collective-permute-start.8 = (bf16[2,16,1536]{2,1,0:T(8,128)(2,1)S(1)}, bf16[2,16,1536]{2,1,0:T(8,128)(2,1)S(1)}, u32[]{:S(2)}, u32[]{:S(2)}) collective-permute-start(bf16[2,16,1536]{2,1,0:T(8,128)(2,1)S(1)} %pair_sum.3), channel_id=1, source_target_pairs={{0,2},{1,3},{2,0},{3,1},{4,6},{5,7},{6,4},{7,5},{8,10},{9,11},{10,... | collective-permute-start | bytes 294920 | tf_op jit(solution)/shard_map/ppermute | solution.py:275
  34.5 4.4 %collective-permute-start.9 = (bf16[16,2560]{1,0:T(8,128)(2,1)S(1)}, bf16[16,2560]{1,0:T(8,128)(2,1)S(1)}, u32[]{:S(2)}, u32[]{:S(2)}) collective-permute-start(bf16[16,2560]{1,0:T(8,128)(2,1)S(1)} %get-tuple-element.29.refs_0_), channel_id=1, source_target_pairs={{0,16},{16,0},{1,17},{17,1},{2,18},{18,2},{3,19},{19,3},{4,20},{20... | collective-permute-start | bytes 245768 | tf_op jit(solution)/shard_map/ppermute | solution.py:275
  36.0 5.0 %collective-permute-start.12 = (bf16[16,2560]{1,0:T(8,128)(2,1)S(1)}, bf16[16,2560]{1,0:T(8,128)(2,1)S(1)}, u32[]{:S(2)}, u32[]{:S(2)}) collective-permute-start(bf16[16,2560]{1,0:T(8,128)(2,1)S(1)} %get-tuple-element.30.refs_0_), channel_id=1, source_target_pairs={{0,2},{1,3},{2,0},{3,1},{4,6},{5,7},{6,4},{7,5},{8,10},{9,11},{10,... | collective-permute-start | bytes 245768 | tf_op jit(solution)/shard_map/ppermute | solution.py:275
  39.0 5.0 %collective-permute-start.10 = (bf16[16,4096]{1,0:T(8,128)(2,1)S(1)}, bf16[16,4096]{1,0:T(8,128)(2,1)S(1)}, u32[]{:S(2)}, u32[]{:S(2)}) collective-permute-start(bf16[16,4096]{1,0:T(8,128)(2,1)S(1)} %combine.3.refs_1_.refs_0_), channel_id=1, source_target_pairs={{0,2},{1,3},{2,0},{3,1},{4,6},{5,7},{6,4},{7,5},{8,10},{9,11},{10,... | collective-permute-start | bytes 393224 | tf_op jit(solution)/shard_map/ppermute | solution.py:275
  39.9 1.6 %collective-permute-start.13 = (bf16[16,2560]{1,0:T(8,128)(2,1)S(1)}, bf16[16,2560]{1,0:T(8,128)(2,1)S(1)}, u32[]{:S(2)}, u32[]{:S(2)}) collective-permute-start(bf16[16,2560]{1,0:T(8,128)(2,1)S(1)} %get-tuple-element.30.refs_0_), channel_id=1, source_target_pairs={{0,1},{1,0},{2,3},{3,2},{4,5},{5,4},{6,7},{7,6},{8,9},{9,8},{10,11... | collective-permute-start | bytes 245768 | tf_op jit(solution)/shard_map/ppermute | solution.py:275
  41.0 1.3 %collective-permute-start.14 = (bf16[16,2560]{1,0:T(8,128)(2,1)S(1)}, bf16[16,2560]{1,0:T(8,128)(2,1)S(1)}, u32[]{:S(2)}, u32[]{:S(2)}) collective-permute-start(bf16[16,2560]{1,0:T(8,128)(2,1)S(1)} %join.4), channel_id=1, source_target_pairs={{0,1},{1,0},{2,3},{3,2},{4,5},{5,4},{6,7},{7,6},{8,9},{9,8},{10,11... | collective-permute-start | bytes 245768 | tf_op jit(solution)/shard_map/ppermute | solution.py:275
  41.0 3.1 %collective-permute-start.11 = (bf16[16,4096]{1,0:T(8,128)(2,1)S(1)}, bf16[16,4096]{1,0:T(8,128)(2,1)S(1)}, u32[]{:S(2)}, u32[]{:S(2)}) collective-permute-start(bf16[16,4096]{1,0:T(8,128)(2,1)S(1)} %combine.3.refs_1_.refs_0_), channel_id=1, source_target_pairs={{0,1},{1,0},{2,3},{3,2},{4,5},{5,4},{6,7},{7,6},{8,9},{9,8},{10,11... | collective-permute-start | bytes 393224 | tf_op jit(solution)/shard_map/ppermute | solution.py:275
  44.0 1.4 %collective-permute-start.15 = (bf16[16,4096]{1,0:T(8,128)(2,1)S(1)}, bf16[16,4096]{1,0:T(8,128)(2,1)S(1)}, u32[]{:S(2)}, u32[]{:S(2)}) collective-permute-start(bf16[16,4096]{1,0:T(8,128)(2,1)S(1)} %join.5), channel_id=1, source_target_pairs={{0,1},{1,0},{2,3},{3,2},{4,5},{5,4},{6,7},{7,6},{8,9},{9,8},{10,11... | collective-permute-start | bytes 393224 | tf_op jit(solution)/shard_map/ppermute | solution.py:275
  47.8 6.8 %collective-permute-start.16 = (bf16[16,2048]{1,0:T(8,128)(2,1)S(1)}, bf16[16,2048]{1,0:T(8,128)(2,1)S(1)}, u32[]{:S(2)}, u32[]{:S(2)}) collective-permute-start(bf16[16,2048]{1,0:T(8,128)(2,1)S(1)} %get-tuple-element.32), channel_id=1, source_target_pairs={{0,12},{4,8},{8,4},{12,0},{1,13},{5,9},{9,5},{13,1},{2,14},{6,10},... | collective-permute-start | bytes 196616 | tf_op jit(solution)/shard_map/ppermute | solution.py:275
  51.3 5.7 %collective-permute-start.17 = (bf16[16,2048]{1,0:T(8,128)(2,1)S(1)}, bf16[16,2048]{1,0:T(8,128)(2,1)S(1)}, u32[]{:S(2)}, u32[]{:S(2)}) collective-permute-start(bf16[16,2048]{1,0:T(8,128)(2,1)S(1)} %get-tuple-element.33), channel_id=1, source_target_pairs={{0,8},{4,12},{8,0},{12,4},{1,9},{5,13},{9,1},{13,5},{2,10},{6,14},... | collective-permute-start | bytes 196616 | tf_op jit(solution)/shard_map/ppermute | solution.py:275
  51.3 5.7 %collective-permute-start.18 = (bf16[16,2048]{1,0:T(8,128)(2,1)S(1)}, bf16[16,2048]{1,0:T(8,128)(2,1)S(1)}, u32[]{:S(2)}, u32[]{:S(2)}) collective-permute-start(bf16[16,2048]{1,0:T(8,128)(2,1)S(1)} %get-tuple-element.34), channel_id=1, source_target_pairs={{0,4},{4,0},{8,12},{12,8},{1,5},{5,1},{9,13},{13,9},{2,6},{6,2},{1... | collective-permute-start | bytes 196616 | tf_op jit(solution)/shard_map/ppermute | solution.py:275

commit v20 on v19

--- a/solution.py
+++ b/solution.py
@@ -8,7 +8,7 @@
 from jax.sharding import PartitionSpec as P
 
 TILE = 256
-LAST = 3
+LAST = 4
 ROWS = 16
 COST = pl.CostEstimate(flops=0, bytes_accessed=1024, transcendentals=0)
 
@@ -119,8 +119,13 @@
                 copies[k][0][i].start()
     else:
         mine_ref, theirs_ref, x_ref = refs[-3:]
-        step = weights[0].shape[1]
-        cuts = [(p * step + a, p * step + b) for p in range(n_pairs) for a, b in pieces_of(step, 2 * TILE)]
+        cuts, at, pair_of = [], 0, {}
+        for p in range(n_pairs):
+            width = weights[2 * p].shape[1]
+            for a, b in pieces_of(width, 2 * TILE):
+                pair_of[at + a] = p, a, b
+                cuts.append((at + a, at + b))
+            at += width
     per = x_ref.shape[0] // (4 * ROWS)
     b = 0
     for array in arrays:
@@ -135,8 +140,8 @@
                 copies[k][0][i].wait()
                 weight = w_ref[k, :, a:b]
             else:
-                p = a // step
-                weight = weights[2 * p + k][:, a - p * step : b - p * step]
+                p, first, end = pair_of[a]
+                weight = weights[2 * p + k][:, first:end]
             part = jnp.dot(x_ref[...], weight, preferred_element_type=jnp.float32).astype(jnp.bfloat16)
             mine_ref[k, :, a:b] = part[:half]
             theirs_ref[k, :, a:b] = part[half:]
@@ -159,7 +164,7 @@
         out_specs=[spec(pltpu.VMEM)] * 2,
         scratch_shapes=scratch,
         out_shape=[jax.ShapeDtypeStruct((2, total // 2, width), jnp.bfloat16)] * 2,
-        compiler_params=params(16 if segments else 4),
+        compiler_params=params(18 if segments else 4),
         cost_estimate=COST,
         name="gate_up",
     )(*arrays, *weights, *behind)
@@ -275,27 +280,28 @@
         return lax.ppermute(x, axis, [(i, i ^ step) for i in range(n)])
 
     tiles = half // TILE
-    bounds = [0, (tiles - LAST) // 2 * TILE, (tiles - LAST) * TILE, half]
+    bounds = [0, (tiles - LAST + 1) // 2 * TILE, (tiles - LAST) * TILE, half]
     widths = [b - a for a, b in zip(bounds[:-1], bounds[1:])]
     gate_weight, up_weight, hbm_tokens = (
         pltpu.with_memory_space_constraint(w, pltpu.HBM) for w in (gate_weight, up_weight, tokens)
     )
     down_weight = pltpu.with_memory_space_constraint(down_weight, pltpu.VMEM)
 
-    far_own = swap(tokens, "rep", 1)
-    by_hid = [swap(tokens, "hid", d) for d in (3, 2, 1)][::-1]
+    by_hid = {d: swap(tokens, "hid", d) for d in (1, 3, 2)}
+    far_own, far_1 = swap(tokens, "rep", 1), swap(by_hid[1], "rep", 1)
     early = [fetch(gate_weight, up_weight, hbm_tokens, bounds[c], widths[c]) for c in range(2)]
     own = early[0][2]
-    near = join(by_hid, [own, far_own])
+    near = join([by_hid[2], by_hid[3]], [own, far_own, far_1])
     far = swap(near, "rep", 1)
+    arrays = [own, by_hid[1], near, far_own, far_1, far]
 
     weights = [w for fetched in early for w in fetched[:2]]
-    mine, theirs = gate_up([own, near, far_own, far], weights, [], [])
+    mine, theirs = gate_up(arrays, weights, [], [])
     got = swap(theirs, "wid", 1)
     to_chip = pair_sum(mine, got, [])
     from_chip = swap(to_chip, "wid", 2)
     segments = [(bounds[2], widths[2]), (half + bounds[2], widths[2])]
-    last_mine, theirs = gate_up([own, near], [gate_weight, up_weight], segments, [to_chip])
+    last_mine, theirs = gate_up(arrays[:3], [gate_weight, up_weight], segments, [to_chip])
     last_got = swap(theirs, "wid", 1)
     keep, give = combine(mine, got, from_chip, [], [])
     last_to_chip = pair_sum(last_mine, last_got, [give])

time: 57.8 us -> 59.3 us (1.026)
  waiting for transfers between devices: 14.4 us -> 16.2 us
    ppermute x19 -> x20, waiting for transfers between devices: 14.4 us -> 16.2 us  [swap(): return lax.ppermute(x, axis, [(i, i ^ step) for i in range(n)])]
    pallas_call x2, Pallas kernels: 9 us -> 9.93 us  [gate_up(): pl.pallas_call(functools.partial(gate_up_kernel, len(arrays), len(weights...]
    pallas_call x2, Pallas kernels: 9.16 us -> 8.49 us  [fetch(): pl.pallas_call(functools.partial(fetch_kernel, first), in_specs=[spec(plt...]
    ppermute x19 -> x20, starting transfers between devices: 19.8 us -> 19.3 us  [swap(): return lax.ppermute(x, axis, [(i, i ^ step) for i in range(n)])]
  transfers between devices with their start and end apart: 19 -> 20, of which waited for: 10 -> 13; matrix products, arithmetic and copies ran while one was open for 0% -> 0% of each run, Pallas kernels for 30% -> 30%
where the time goes in v20:
time: 59.3 us; the launch traced here: 59.1 us
  Pallas kernels  22.8 us (38%)
  starting transfers between devices  19.3 us (33%)
  waiting for transfers between devices  16.2 us (27%)
  other arithmetic  0.67 us (1%)
    ppermute x20, starting transfers between devices, swap(): return lax.ppermute(x, axis, [(i, i ^ step) for i in range(n)])  19.3 us
    ppermute x20, waiting for transfers between devices, swap(): return lax.ppermute(x, axis, [(i, i ^ step) for i in range(n)])  16.2 us
    pallas_call x2, Pallas kernels, gate_up(): pl.pallas_call(functools.partial(gate_up_kernel, len(arrays), len(weights...  9.93 us
    pallas_call x2, Pallas kernels, fetch(): pl.pallas_call(functools.partial(fetch_kernel, first), in_specs=[spec(plt...  8.49 us
    pallas_call x2, Pallas kernels, down(): pl.pallas_call(functools.partial(down_kernel, len(pieces), prev is not No...  3.94 us
  transfers between devices with their start and end apart: 20, of which 13 were waited for; matrix products, arithmetic and copies ran while one was open for 0% of the time, Pallas kernels for 30%

profile of v20, /device:TPU:0, one launch (start us, length us, event | category | flops | bytes accessed | tf_op | source)
XLA Modules:
  0.0 59.1 jit_solution(7816241817396005634)
XLA Ops:
  0.0 3.0 %collective-permute-start = (bf16[16,2048]{1,0:T(8,128)(2,1)}, bf16[16,2048]{1,0:T(8,128)(2,1)S(1)}, u32[]{:S(2)}, u32[]{:S(2)}) collective-permute-start(bf16[16,2048]{1,0:T(8,128)(2,1)} %tokens_ref.3), channel_id=1, source_target_pairs={{0,4},{4,0},{8,12},{12,8},{1,5},{5,1},{9,13},{13,9},{2,6},{6,2},{1... | collective-permute-start | bytes 196616 | tf_op jit(solution)/shard_map/ppermute | solution.py:280
  3.0 2.5 %collective-permute-start.2 = (bf16[16,2048]{1,0:T(8,128)(2,1)}, bf16[16,2048]{1,0:T(8,128)(2,1)S(1)}, u32[]{:S(2)}, u32[]{:S(2)}) collective-permute-start(bf16[16,2048]{1,0:T(8,128)(2,1)} %tokens_ref.3), channel_id=1, source_target_pairs={{0,12},{4,8},{8,4},{12,0},{1,13},{5,9},{9,5},{13,1},{2,14},{6,10},... | collective-permute-start | bytes 196616 | tf_op jit(solution)/shard_map/ppermute | solution.py:280
  5.5 0.1 collective-permute-start.1
  5.6 1.5 %collective-permute-start.3 = (bf16[16,2048]{1,0:T(8,128)(2,1)}, bf16[16,2048]{1,0:T(8,128)(2,1)S(1)}, u32[]{:S(2)}, u32[]{:S(2)}) collective-permute-start(bf16[16,2048]{1,0:T(8,128)(2,1)} %tokens_ref.3), channel_id=1, source_target_pairs={{0,16},{16,0},{1,17},{17,1},{2,18},{18,2},{3,19},{19,3},{4,20},{20... | collective-permute-start | bytes 196616 | tf_op jit(solution)/shard_map/ppermute | solution.py:280
  7.1 0.5 collective-permute-start.4
  7.6 4.3 %fetch.2 = (bf16[2048,1280]{1,0:T(8,128)(2,1)S(1)}, bf16[2048,1280]{1,0:T(8,128)(2,1)S(1)}, bf16[16,2048]{1,0:T(8,128)(2,1)S(1)}) custom-call(bf16[2048,6656]{1,0:T(8,128)(2,1)} %refs_3_.1, bf16[2048,6656]{1,0:T(8,128)(2,1)} %refs_4_.3, bf16[16,2048]{1,0:T(8,128)(2,1)} %tokens_ref.3), custom_call_target="tpu_custom_call" | custom-call | bytes 1024 | tf_op jit(solution)/shard_map/fetch/pallas_call | solution.py:78
  11.9 0.0 collective-permute-done.2.refs_1_
  11.9 0.2 collective-permute-done.1.refs_0_
  12.2 0.0 collective-permute-done.3.refs_3_
  12.2 1.6 %collective-permute-start.5 = (bf16[32,2048]{1,0:T(8,128)(2,1)S(1)}, bf16[32,2048]{1,0:T(8,128)(2,1)S(1)}, u32[]{:S(2)}, u32[]{:S(2)}) collective-permute-start(bf16[32,2048]{1,0:T(8,128)(2,1)S(1)} %join.3.refs_2_), channel_id=1, source_target_pairs={{0,16},{16,0},{1,17},{17,1},{2,18},{18,2},{3,19},{19,3},{4,20},{20... | collective-permute-start | bytes 393224 | tf_op jit(solution)/shard_map/ppermute | solution.py:280
  13.8 4.2 %fetch.3 = (bf16[2048,1024]{1,0:T(8,128)(2,1)S(1)}, bf16[2048,1024]{1,0:T(8,128)(2,1)S(1)}, bf16[16,2048]{1,0:T(8,128)(2,1)}) custom-call(bf16[2048,6656]{1,0:T(8,128)(2,1)} %refs_3_.1, bf16[2048,6656]{1,0:T(8,128)(2,1)} %refs_4_.3, bf16[16,2048]{1,0:T(8,128)(2,1)} %tokens_ref.3), custom_call_target="tpu_custom_call" | custom-call | bytes 1024 | tf_op jit(solution)/shard_map/fetch/pallas_call | solution.py:78
  18.0 0.0 collective-permute-done.5.refs_5_
  18.0 2.7 %gate_up.2 = (bf16[2,64,2304]{2,1,0:T(8,128)(2,1)S(1)}, bf16[2,64,2304]{2,1,0:T(8,128)(2,1)S(1)}) custom-call(bf16[16,2048]{1,0:T(8,128)(2,1)S(1)} %get-tuple-element.20.refs_2_.refs_0_, bf16[16,2048]{1,0:T(8,128)(2,1)S(1)} %collective-permute-done.refs_1_, bf16[32,2048]{1,0:T(8,128)(2,1)S(1)} %join.3.refs_2_, ...), custom_call_target="tpu_custom_call" | custom-call | bytes 1024 | tf_op jit(solution)/shard_map/gate_up/pallas_call | solution.py:159
  20.7 0.1 collective-permute-start.6
  20.8 2.0 %collective-permute-done.6.got_ref = bf16[2,64,2304]{2,1,0:T(8,128)(2,1)S(1)} collective-permute-done((bf16[2,64,2304]{2,1,0:T(8,128)(2,1)S(1)}, bf16[2,64,2304]{2,1,0:T(8,128)(2,1)S(1)}, u32[]{:S(2)}, u32[]{:S(2)}) %collective-permute-start.6) | collective-permute-done | bytes 589856 | tf_op jit(solution)/shard_map/ppermute | solution.py:280
  22.8 0.1 pair_sum.2.refs_5_
  22.8 0.0 slice-start.1
  22.9 0.0 slice-start.3
  22.9 1.5 %collective-permute-start.8 = (bf16[2,32,2304]{2,1,0:T(8,128)(2,1)S(1)}, bf16[2,32,2304]{2,1,0:T(8,128)(2,1)S(1)}, u32[]{:S(2)}, u32[]{:S(2)}) collective-permute-start(bf16[2,32,2304]{2,1,0:T(8,128)(2,1)S(1)} %pair_sum.2.refs_5_), channel_id=1, source_target_pairs={{0,2},{1,3},{2,0},{3,1},{4,6},{5,7},{6,4},{7,5},{8,10},{9,11},{10,... | collective-permute-start | bytes 884744 | tf_op jit(solution)/shard_map/ppermute | solution.py:280
  24.4 7.3 %gate_up.3 = (bf16[2,32,2048]{2,1,0:T(8,128)(2,1)S(1)}, bf16[2,32,2048]{2,1,0:T(8,128)(2,1)S(1)}) custom-call(bf16[16,2048]{1,0:T(8,128)(2,1)S(1)} %get-tuple-element.20.refs_2_.refs_0_, bf16[16,2048]{1,0:T(8,128)(2,1)S(1)} %collective-permute-done.refs_1_, bf16[32,2048]{1,0:T(8,128)(2,1)S(1)} %join.3.refs_2_, bf16[2048,6656]{1,0:T(8,128)(2,1)} %refs_3_.1, ...), custom_call_target="tpu_custom_call" | custom-call | bytes 1024 | tf_op jit(solution)/shard_map/gate_up/pallas_call | solution.py:159
  31.7 0.1 collective-permute-start.7
  31.8 0.2 collective-permute-done.8.chip_ref
  32.0 0.2 combine.2
  32.2 1.1 %collective-permute-done.7.got_ref = bf16[2,32,2048]{2,1,0:T(8,128)(2,1)S(1)} collective-permute-done((bf16[2,32,2048]{2,1,0:T(8,128)(2,1)S(1)}, bf16[2,32,2048]{2,1,0:T(8,128)(2,1)S(1)}, u32[]{:S(2)}, u32[]{:S(2)}) %collective-permute-start.7) | collective-permute-done | bytes 262176 | tf_op jit(solution)/shard_map/ppermute | solution.py:280
  33.4 0.4 collective-permute-start.9
  33.8 1.1 %collective-permute-start.10 = (bf16[16,2304]{1,0:T(8,128)(2,1)S(1)}, bf16[16,2304]{1,0:T(8,128)(2,1)S(1)}, u32[]{:S(2)}, u32[]{:S(2)}) collective-permute-start(bf16[16,2304]{1,0:T(8,128)(2,1)S(1)} %get-tuple-element.29.refs_0_), channel_id=1, source_target_pairs={{0,16},{16,0},{1,17},{17,1},{2,18},{18,2},{3,19},{19,3},{4,20},{20... | collective-permute-start | bytes 221192 | tf_op jit(solution)/shard_map/ppermute | solution.py:280
  34.9 1.7 %collective-permute-start.13 = (bf16[16,2304]{1,0:T(8,128)(2,1)S(1)}, bf16[16,2304]{1,0:T(8,128)(2,1)S(1)}, u32[]{:S(2)}, u32[]{:S(2)}) collective-permute-start(bf16[16,2304]{1,0:T(8,128)(2,1)S(1)} %get-tuple-element.30.refs_0_), channel_id=1, source_target_pairs={{0,2},{1,3},{2,0},{3,1},{4,6},{5,7},{6,4},{7,5},{8,10},{9,11},{10,... | collective-permute-start | bytes 221192 | tf_op jit(solution)/shard_map/ppermute | solution.py:280
  36.6 1.6 %collective-permute-done.10.refs_0_ = bf16[16,2304]{1,0:T(8,128)(2,1)S(1)} collective-permute-done((bf16[16,2304]{1,0:T(8,128)(2,1)S(1)}, bf16[16,2304]{1,0:T(8,128)(2,1)S(1)}, u32[]{:S(2)}, u32[]{:S(2)}) %collective-permute-start.10) | collective-permute-done | bytes 73760 | tf_op jit(solution)/shard_map/ppermute | solution.py:280
  38.1 1.6 %collective-permute-done.9.chip_ref = bf16[2,16,2048]{2,1,0:T(8,128)(2,1)S(1)} collective-permute-done((bf16[2,16,2048]{2,1,0:T(8,128)(2,1)S(1)}, bf16[2,16,2048]{2,1,0:T(8,128)(2,1)S(1)}, u32[]{:S(2)}, u32[]{:S(2)}) %collective-permute-start.9) | collective-permute-done | bytes 131104 | tf_op jit(solution)/shard_map/ppermute | solution.py:280
  39.8 0.1 combine.3.refs_1_.refs_0_
  39.9 0.1 collective-permute-start.11
  40.0 0.0 collective-permute-start.14
  40.0 0.5 collective-permute-done.13.refs_0_.refs_1_
  40.6 0.0 collective-permute-start.15
  40.6 0.5 collective-permute-start.12
  41.1 0.2 collective-permute-done.14.refs_2_
  41.3 0.6 collective-permute-done.15.refs_3_
  41.9 1.4 %down.2.refs_1_.refs_5_ = f32[64,2048]{1,0:T(8,128)S(1)} custom-call(bf16[16,2304]{1,0:T(8,128)(2,1)S(1)} %get-tuple-element.30.refs_0_, bf16[16,2304]{1,0:T(8,128)(2,1)S(1)} %collective-permute-done.13.refs_0_.refs_1_, bf16[16,2304]{1,0:T(8,128)(2,1)S(1)} %collective-permute-done.14.refs_2_, bf16[16,2304]{1,0:T(8,128)(2,1)S(1)} %collective-permute-done.15.refs_3_, ...), custom_call_target="tpu_custom_call" | custom-call | bytes 1024 | tf_op jit(solution)/shard_map/down/pallas_call | solution.py:262
  43.3 1.7 %collective-permute-done.11.refs_0_.refs_1_ = bf16[16,4352]{1,0:T(8,128)(2,1)S(1)} collective-permute-done((bf16[16,4352]{1,0:T(8,128)(2,1)S(1)}, bf16[16,4352]{1,0:T(8,128)(2,1)S(1)}, u32[]{:S(2)}, u32[]{:S(2)}) %collective-permute-start.11) | collective-permute-done | bytes 139296 | tf_op jit(solution)/shard_map/ppermute | solution.py:280
  45.0 0.1 collective-permute-start.16
  45.1 1.3 %collective-permute-done.16.refs_3_ = bf16[16,4352]{1,0:T(8,128)(2,1)S(1)} collective-permute-done((bf16[16,4352]{1,0:T(8,128)(2,1)S(1)}, bf16[16,4352]{1,0:T(8,128)(2,1)S(1)}, u32[]{:S(2)}, u32[]{:S(2)}) %collective-permute-start.16) | collective-permute-done | bytes 139296 | tf_op jit(solution)/shard_map/ppermute | solution.py:280
  46.4 2.5 %down.3 = (bf16[16,2048]{1,0:T(8,128)(2,1)S(1)}, bf16[16,2048]{1,0:T(8,128)(2,1)S(1)}, bf16[16,2048]{1,0:T(8,128)(2,1)S(1)}, bf16[16,2048]{1,0:T(8,128)(2,1)S(1)}) custom-call(bf16[16,4352]{1,0:T(8,128)(2,1)S(1)} %combine.3.refs_1_.refs_0_, bf16[16,4352]{1,0:T(8,128)(2,1)S(1)} %collective-permute-done.11.refs_0_.refs_1_, ...), custom_call_target="tpu_custom_call" | custom-call | bytes 1024 | tf_op jit(solution)/shard_map/down/pallas_call | solution.py:262
  49.0 2.8 %collective-permute-start.17 = (bf16[16,2048]{1,0:T(8,128)(2,1)S(1)}, bf16[16,2048]{1,0:T(8,128)(2,1)S(1)}, u32[]{:S(2)}, u32[]{:S(2)}) collective-permute-start(bf16[16,2048]{1,0:T(8,128)(2,1)S(1)} %get-tuple-element.32), channel_id=1, source_target_pairs={{0,12},{4,8},{8,4},{12,0},{1,13},{5,9},{9,5},{13,1},{2,14},{6,10},... | collective-permute-start | bytes 196616 | tf_op jit(solution)/shard_map/ppermute | solution.py:280
  51.7 0.3 collective-permute-start.18
  52.1 1.3 %collective-permute-start.19 = (bf16[16,2048]{1,0:T(8,128)(2,1)S(1)}, bf16[16,2048]{1,0:T(8,128)(2,1)S(1)}, u32[]{:S(2)}, u32[]{:S(2)}) collective-permute-start(bf16[16,2048]{1,0:T(8,128)(2,1)S(1)} %get-tuple-element.34), channel_id=1, source_target_pairs={{0,4},{4,0},{8,12},{12,8},{1,5},{5,1},{9,13},{13,9},{2,6},{6,2},{1... | collective-permute-start | bytes 196616 | tf_op jit(solution)/shard_map/ppermute | solution.py:280
  53.4 1.9 %collective-permute-done.17 = bf16[16,2048]{1,0:T(8,128)(2,1)S(1)} collective-permute-done((bf16[16,2048]{1,0:T(8,128)(2,1)S(1)}, bf16[16,2048]{1,0:T(8,128)(2,1)S(1)}, u32[]{:S(2)}, u32[]{:S(2)}) %collective-permute-start.17) | collective-permute-done | bytes 65568 | tf_op jit(solution)/shard_map/ppermute | solution.py:280
  55.3 3.2 %collective-permute-done.18 = bf16[16,2048]{1,0:T(8,128)(2,1)S(1)} collective-permute-done((bf16[16,2048]{1,0:T(8,128)(2,1)S(1)}, bf16[16,2048]{1,0:T(8,128)(2,1)S(1)}, u32[]{:S(2)}, u32[]{:S(2)}) %collective-permute-start.18) | collective-permute-done | bytes 65568 | tf_op jit(solution)/shard_map/ppermute | solution.py:280
  58.5 0.7 %add_convert_fusion = bf16[16,2048]{1,0:T(8,128)(2,1)} fusion(bf16[16,2048]{1,0:T(8,128)(2,1)S(1)} %collective-permute-done.19, bf16[16,2048]{1,0:T(8,128)(2,1)S(1)} %collective-permute-done.18, bf16[16,2048]{1,0:T(8,128)(2,1)S(1)} %collective-permute-done.17, bf16[16,2048]{1,0:T(8,128)(2,1)S(1)} %get-tuple-element.31), kind=kLoop, calls=%fused_computation | loop fusion | flops 262144 | bytes 327680 | tf_op jit(solution)/shard_map/convert_element_type | solution.py:322
  (21 shorter events, 0.1 us)
Async XLA Ops:
  0.0 7.1 %collective-permute-start = (bf16[16,2048]{1,0:T(8,128)(2,1)}, bf16[16,2048]{1,0:T(8,128)(2,1)S(1)}, u32[]{:S(2)}, u32[]{:S(2)}) collective-permute-start(bf16[16,2048]{1,0:T(8,128)(2,1)} %tokens_ref.3), channel_id=1, source_target_pairs={{0,4},{4,0},{8,12},{12,8},{1,5},{5,1},{9,13},{13,9},{2,6},{6,2},{1... | collective-permute-start | bytes 196616 | tf_op jit(solution)/shard_map/ppermute | solution.py:280
  3.0 8.9 %collective-permute-start.2 = (bf16[16,2048]{1,0:T(8,128)(2,1)}, bf16[16,2048]{1,0:T(8,128)(2,1)S(1)}, u32[]{:S(2)}, u32[]{:S(2)}) collective-permute-start(bf16[16,2048]{1,0:T(8,128)(2,1)} %tokens_ref.3), channel_id=1, source_target_pairs={{0,12},{4,8},{8,4},{12,0},{1,13},{5,9},{9,5},{13,1},{2,14},{6,10},... | collective-permute-start | bytes 196616 | tf_op jit(solution)/shard_map/ppermute | solution.py:280
  5.5 6.7 %collective-permute-start.1 = (bf16[16,2048]{1,0:T(8,128)(2,1)}, bf16[16,2048]{1,0:T(8,128)(2,1)S(1)}, u32[]{:S(2)}, u32[]{:S(2)}) collective-permute-start(bf16[16,2048]{1,0:T(8,128)(2,1)} %tokens_ref.3), channel_id=1, source_target_pairs={{0,8},{4,12},{8,0},{12,4},{1,9},{5,13},{9,1},{13,5},{2,10},{6,14},... | collective-permute-start | bytes 196616 | tf_op jit(solution)/shard_map/ppermute | solution.py:280
  5.6 6.6 %collective-permute-start.3 = (bf16[16,2048]{1,0:T(8,128)(2,1)}, bf16[16,2048]{1,0:T(8,128)(2,1)S(1)}, u32[]{:S(2)}, u32[]{:S(2)}) collective-permute-start(bf16[16,2048]{1,0:T(8,128)(2,1)} %tokens_ref.3), channel_id=1, source_target_pairs={{0,16},{16,0},{1,17},{17,1},{2,18},{18,2},{3,19},{19,3},{4,20},{20... | collective-permute-start | bytes 196616 | tf_op jit(solution)/shard_map/ppermute | solution.py:280
  7.1 5.0 %collective-permute-start.4 = (bf16[16,2048]{1,0:T(8,128)(2,1)S(1)}, bf16[16,2048]{1,0:T(8,128)(2,1)S(1)}, u32[]{:S(2)}, u32[]{:S(2)}) collective-permute-start(bf16[16,2048]{1,0:T(8,128)(2,1)S(1)} %collective-permute-done.refs_1_), channel_id=1, source_target_pairs={{0,16},{16,0},{1,17},{17,1},{2,18},{18,2},{3,19},{19,3},{4,20},{20... | collective-permute-start | bytes 196616 | tf_op jit(solution)/shard_map/ppermute | solution.py:280
  12.2 5.8 %collective-permute-start.5 = (bf16[32,2048]{1,0:T(8,128)(2,1)S(1)}, bf16[32,2048]{1,0:T(8,128)(2,1)S(1)}, u32[]{:S(2)}, u32[]{:S(2)}) collective-permute-start(bf16[32,2048]{1,0:T(8,128)(2,1)S(1)} %join.3.refs_2_), channel_id=1, source_target_pairs={{0,16},{16,0},{1,17},{17,1},{2,18},{18,2},{3,19},{19,3},{4,20},{20... | collective-permute-start | bytes 393224 | tf_op jit(solution)/shard_map/ppermute | solution.py:280
  20.7 2.1 %collective-permute-start.6 = (bf16[2,64,2304]{2,1,0:T(8,128)(2,1)S(1)}, bf16[2,64,2304]{2,1,0:T(8,128)(2,1)S(1)}, u32[]{:S(2)}, u32[]{:S(2)}) collective-permute-start(bf16[2,64,2304]{2,1,0:T(8,128)(2,1)S(1)} %get-tuple-element.26), channel_id=1, source_target_pairs={{0,1},{1,0},{2,3},{3,2},{4,5},{5,4},{6,7},{7,6},{8,9},{9,8},{10,11... | collective-permute-start | bytes 1769480 | tf_op jit(solution)/shard_map/ppermute | solution.py:280
  22.8 19.1 %slice-start = ((s8[27262976]{0:T(1024)(128)(4,1)}), s8[4194304]{0:T(1024)(128)(4,1)S(1)}, s32[]{:S(2)}) async-start(s8[27262976]{0:T(1024)(128)(4,1)} %bitcast), calls=%async_computation | async-start | bytes 8388608
  22.8 19.0 %slice-start.1 = ((s8[27262976]{0:T(1024)(128)(4,1)}), s8[4194304]{0:T(1024)(128)(4,1)S(1)}, s32[]{:S(2)}) async-start(s8[27262976]{0:T(1024)(128)(4,1)} %bitcast), calls=%async_computation.1 | async-start | bytes 8388608
  22.8 19.0 %slice-start.2 = ((s8[27262976]{0:T(1024)(128)(4,1)}), s8[4194304]{0:T(1024)(128)(4,1)S(1)}, s32[]{:S(2)}) async-start(s8[27262976]{0:T(1024)(128)(4,1)} %bitcast), calls=%async_computation.2 | async-start | bytes 8388608
  22.9 19.0 %slice-start.3 = ((s8[27262976]{0:T(1024)(128)(4,1)}), s8[4194304]{0:T(1024)(128)(4,1)S(1)}, s32[]{:S(2)}) async-start(s8[27262976]{0:T(1024)(128)(4,1)} %bitcast), calls=%async_computation.3 | async-start | bytes 8388608
  22.9 19.0 %slice-start.4 = ((s8[27262976]{0:T(1024)(128)(4,1)}), s8[4194304]{0:T(1024)(128)(4,1)S(1)}, s32[]{:S(2)}) async-start(s8[27262976]{0:T(1024)(128)(4,1)} %bitcast), calls=%async_computation.4 | async-start | bytes 8388608
  22.9 19.0 %slice-start.5 = ((s8[27262976]{0:T(1024)(128)(4,1)}), s8[4194304]{0:T(1024)(128)(4,1)S(1)}, s32[]{:S(2)}) async-start(s8[27262976]{0:T(1024)(128)(4,1)} %bitcast), calls=%async_computation.5 | async-start | bytes 8388608
  22.9 19.0 %slice-start.6 = ((s8[27262976]{0:T(1024)(128)(4,1)}), s8[2097152]{0:T(1024)(128)(4,1)S(1)}, s32[]{:S(2)}) async-start(s8[27262976]{0:T(1024)(128)(4,1)} %bitcast), calls=%async_computation.6 | async-start | bytes 4194304
  22.9 9.1 %collective-permute-start.8 = (bf16[2,32,2304]{2,1,0:T(8,128)(2,1)S(1)}, bf16[2,32,2304]{2,1,0:T(8,128)(2,1)S(1)}, u32[]{:S(2)}, u32[]{:S(2)}) collective-permute-start(bf16[2,32,2304]{2,1,0:T(8,128)(2,1)S(1)} %pair_sum.2.refs_5_), channel_id=1, source_target_pairs={{0,2},{1,3},{2,0},{3,1},{4,6},{5,7},{6,4},{7,5},{8,10},{9,11},{10,... | collective-permute-start | bytes 884744 | tf_op jit(solution)/shard_map/ppermute | solution.py:280
  31.7 1.6 %collective-permute-start.7 = (bf16[2,32,2048]{2,1,0:T(8,128)(2,1)S(1)}, bf16[2,32,2048]{2,1,0:T(8,128)(2,1)S(1)}, u32[]{:S(2)}, u32[]{:S(2)}) collective-permute-start(bf16[2,32,2048]{2,1,0:T(8,128)(2,1)S(1)} %get-tuple-element.28), channel_id=1, source_target_pairs={{0,1},{1,0},{2,3},{3,2},{4,5},{5,4},{6,7},{7,6},{8,9},{9,8},{10,11... | collective-permute-start | bytes 786440 | tf_op jit(solution)/shard_map/ppermute | solution.py:280
  33.4 6.4 %collective-permute-start.9 = (bf16[2,16,2048]{2,1,0:T(8,128)(2,1)S(1)}, bf16[2,16,2048]{2,1,0:T(8,128)(2,1)S(1)}, u32[]{:S(2)}, u32[]{:S(2)}) collective-permute-start(bf16[2,16,2048]{2,1,0:T(8,128)(2,1)S(1)} %pair_sum.3), channel_id=1, source_target_pairs={{0,2},{1,3},{2,0},{3,1},{4,6},{5,7},{6,4},{7,5},{8,10},{9,11},{10,... | collective-permute-start | bytes 393224 | tf_op jit(solution)/shard_map/ppermute | solution.py:280
  33.8 4.4 %collective-permute-start.10 = (bf16[16,2304]{1,0:T(8,128)(2,1)S(1)}, bf16[16,2304]{1,0:T(8,128)(2,1)S(1)}, u32[]{:S(2)}, u32[]{:S(2)}) collective-permute-start(bf16[16,2304]{1,0:T(8,128)(2,1)S(1)} %get-tuple-element.29.refs_0_), channel_id=1, source_target_pairs={{0,16},{16,0},{1,17},{17,1},{2,18},{18,2},{3,19},{19,3},{4,20},{20... | collective-permute-start | bytes 221192 | tf_op jit(solution)/shard_map/ppermute | solution.py:280
  34.9 5.6 %collective-permute-start.13 = (bf16[16,2304]{1,0:T(8,128)(2,1)S(1)}, bf16[16,2304]{1,0:T(8,128)(2,1)S(1)}, u32[]{:S(2)}, u32[]{:S(2)}) collective-permute-start(bf16[16,2304]{1,0:T(8,128)(2,1)S(1)} %get-tuple-element.30.refs_0_), channel_id=1, source_target_pairs={{0,2},{1,3},{2,0},{3,1},{4,6},{5,7},{6,4},{7,5},{8,10},{9,11},{10,... | collective-permute-start | bytes 221192 | tf_op jit(solution)/shard_map/ppermute | solution.py:280
  39.9 5.1 %collective-permute-start.11 = (bf16[16,4352]{1,0:T(8,128)(2,1)S(1)}, bf16[16,4352]{1,0:T(8,128)(2,1)S(1)}, u32[]{:S(2)}, u32[]{:S(2)}) collective-permute-start(bf16[16,4352]{1,0:T(8,128)(2,1)S(1)} %combine.3.refs_1_.refs_0_), channel_id=1, source_target_pairs={{0,2},{1,3},{2,0},{3,1},{4,6},{5,7},{6,4},{7,5},{8,10},{9,11},{10,... | collective-permute-start | bytes 417800 | tf_op jit(solution)/shard_map/ppermute | solution.py:280
  40.0 1.3 %collective-permute-start.14 = (bf16[16,2304]{1,0:T(8,128)(2,1)S(1)}, bf16[16,2304]{1,0:T(8,128)(2,1)S(1)}, u32[]{:S(2)}, u32[]{:S(2)}) collective-permute-start(bf16[16,2304]{1,0:T(8,128)(2,1)S(1)} %get-tuple-element.30.refs_0_), channel_id=1, source_target_pairs={{0,1},{1,0},{2,3},{3,2},{4,5},{5,4},{6,7},{7,6},{8,9},{9,8},{10,11... | collective-permute-start | bytes 221192 | tf_op jit(solution)/shard_map/ppermute | solution.py:280
  40.6 1.3 %collective-permute-start.15 = (bf16[16,2304]{1,0:T(8,128)(2,1)S(1)}, bf16[16,2304]{1,0:T(8,128)(2,1)S(1)}, u32[]{:S(2)}, u32[]{:S(2)}) collective-permute-start(bf16[16,2304]{1,0:T(8,128)(2,1)S(1)} %join.4), channel_id=1, source_target_pairs={{0,1},{1,0},{2,3},{3,2},{4,5},{5,4},{6,7},{7,6},{8,9},{9,8},{10,11... | collective-permute-start | bytes 221192 | tf_op jit(solution)/shard_map/ppermute | solution.py:280
  40.6 4.5 %collective-permute-start.12 = (bf16[16,4352]{1,0:T(8,128)(2,1)S(1)}, bf16[16,4352]{1,0:T(8,128)(2,1)S(1)}, u32[]{:S(2)}, u32[]{:S(2)}) collective-permute-start(bf16[16,4352]{1,0:T(8,128)(2,1)S(1)} %combine.3.refs_1_.refs_0_), channel_id=1, source_target_pairs={{0,1},{1,0},{2,3},{3,2},{4,5},{5,4},{6,7},{7,6},{8,9},{9,8},{10,11... | collective-permute-start | bytes 417800 | tf_op jit(solution)/shard_map/ppermute | solution.py:280
  45.0 1.4 %collective-permute-start.16 = (bf16[16,4352]{1,0:T(8,128)(2,1)S(1)}, bf16[16,4352]{1,0:T(8,128)(2,1)S(1)}, u32[]{:S(2)}, u32[]{:S(2)}) collective-permute-start(bf16[16,4352]{1,0:T(8,128)(2,1)S(1)} %join.5), channel_id=1, source_target_pairs={{0,1},{1,0},{2,3},{3,2},{4,5},{5,4},{6,7},{7,6},{8,9},{9,8},{10,11... | collective-permute-start | bytes 417800 | tf_op jit(solution)/shard_map/ppermute | solution.py:280
  49.0 6.3 %collective-permute-start.17 = (bf16[16,2048]{1,0:T(8,128)(2,1)S(1)}, bf16[16,2048]{1,0:T(8,128)(2,1)S(1)}, u32[]{:S(2)}, u32[]{:S(2)}) collective-permute-start(bf16[16,2048]{1,0:T(8,128)(2,1)S(1)} %get-tuple-element.32), channel_id=1, source_target_pairs={{0,12},{4,8},{8,4},{12,0},{1,13},{5,9},{9,5},{13,1},{2,14},{6,10},... | collective-permute-start | bytes 196616 | tf_op jit(solution)/shard_map/ppermute | solution.py:280
  51.7 6.7 %collective-permute-start.18 = (bf16[16,2048]{1,0:T(8,128)(2,1)S(1)}, bf16[16,2048]{1,0:T(8,128)(2,1)S(1)}, u32[]{:S(2)}, u32[]{:S(2)}) collective-permute-start(bf16[16,2048]{1,0:T(8,128)(2,1)S(1)} %get-tuple-element.33), channel_id=1, source_target_pairs={{0,8},{4,12},{8,0},{12,4},{1,9},{5,13},{9,1},{13,5},{2,10},{6,14},... | collective-permute-start | bytes 196616 | tf_op jit(solution)/shard_map/ppermute | solution.py:280
  52.1 6.4 %collective-permute-start.19 = (bf16[16,2048]{1,0:T(8,128)(2,1)S(1)}, bf16[16,2048]{1,0:T(8,128)(2,1)S(1)}, u32[]{:S(2)}, u32[]{:S(2)}) collective-permute-start(bf16[16,2048]{1,0:T(8,128)(2,1)S(1)} %get-tuple-element.34), channel_id=1, source_target_pairs={{0,4},{4,0},{8,12},{12,8},{1,5},{5,1},{9,13},{13,9},{2,6},{6,2},{1... | collective-permute-start | bytes 196616 | tf_op jit(solution)/shard_map/ppermute | solution.py:280

commit v21 on v19

--- a/solution.py
+++ b/solution.py
@@ -219,11 +219,12 @@
     )(mine, got, from_chip, *left, *behind)
 
 
-def down_kernel(n_pieces, has_acc, last, segments, *refs):
+def down_kernel(n_pieces, n_behind, has_acc, last, segments, *refs):
     pieces, refs = refs[:n_pieces], refs[n_pieces:]
     down_ref, refs = refs[0], refs[1:]
     where = here(down_ref.shape[0] // 2)
     prev_ref, refs = (refs[0], refs[1:]) if has_acc else (None, refs)
+    refs = refs[n_behind:]
     outs, (acc_ref, lhs_ref) = refs[:-2], refs[-2:]
     at = 0
     for piece in pieces:
@@ -246,7 +247,7 @@
             out[...] = acc_ref[pl.ds(source, ROWS), :].astype(out.dtype)
 
 
-def down(pieces, down_weight, prev, segments, last):
+def down(pieces, down_weight, prev, segments, last, behind):
     width = down_weight.shape[1]
     total = 4 * ROWS
     args = [*pieces, down_weight] + ([] if prev is None else [prev])
@@ -255,15 +256,15 @@
     if last:
         scratch = [pltpu.VMEM(sums.shape, sums.dtype)] + scratch
     return pl.pallas_call(
-        functools.partial(down_kernel, len(pieces), prev is not None, last, segments),
-        in_specs=[spec(pltpu.VMEM)] * len(args),
+        functools.partial(down_kernel, len(pieces), len(behind), prev is not None, last, segments),
+        in_specs=[spec(pltpu.VMEM)] * len(args) + [spec(pl.ANY)] * len(behind),
         out_specs=[spec(pltpu.VMEM)] * 4 if last else spec(pltpu.VMEM),
         scratch_shapes=scratch,
         out_shape=[jax.ShapeDtypeStruct((ROWS, width), jnp.bfloat16)] * 4 if last else sums,
         compiler_params=params(4),
         cost_estimate=COST,
         name="down",
-    )(*args)
+    )(*args, *behind)
 
 
 def split_by_rep(tokens, gate_weight, up_weight, down_weight):
@@ -298,17 +299,22 @@
     last_mine, theirs = gate_up([own, near], [gate_weight, up_weight], segments, [to_chip])
     last_got = swap(theirs, "wid", 1)
     keep, give = combine(mine, got, from_chip, [], [])
+    far_columns = swap(give, "rep", 1)
     last_to_chip = pair_sum(last_mine, last_got, [give])
     last_from_chip = swap(last_to_chip, "wid", 2)
-    (rest,) = combine(last_mine, last_got, last_from_chip, [swap(give, "rep", 1)], [])
+    (rest,) = combine(last_mine, last_got, last_from_chip, [], [])
 
     def gather(hidden, behind):
         other = swap(hidden, "wid", 2)
-        return [hidden, other, swap(hidden, "wid", 1), swap(join([other], behind), "wid", 1)]
-
-    acc = down(gather(keep, [rest]), down_weight, None, [(1, 0, bounds[2])], False)
-    rest_segments = [(-1, half, bounds[2])] + [(0, start, width) for start, width in segments]
-    acc = down(gather(rest, [acc]), down_weight, acc, rest_segments, True)
+        held = join([other], behind)
+        return (hidden, other, swap(hidden, "wid", 1), swap(held, "wid", 1)), [held]
+
+    first, _ = gather(keep, [rest])
+    second, held = gather(far_columns, [])
+    acc = down(first, down_weight, None, [(1, 0, bounds[2])], False, held)
+    third, held = gather(rest, [acc])
+    acc = down(second, down_weight, acc, [(-1, half, bounds[2])], False, held)
+    acc = down(third, down_weight, acc, [(0, start, width) for start, width in segments], True, [])
 
     mixed = acc[0].astype(f32)
     for d in (3, 2, 1):

time: 57.8 us -> 57.9 us (level)
  waiting for transfers between devices: 14.4 us -> 12 us
  starting transfers between devices: 19.8 us -> 22.2 us
    ppermute x19 -> x22, waiting for transfers between devices: 14.4 us -> 12 us  [swap(): return lax.ppermute(x, axis, [(i, i ^ step) for i in range(n)])]
    ppermute x19 -> x22, starting transfers between devices: 19.8 us -> 22.2 us  [swap(): return lax.ppermute(x, axis, [(i, i ^ step) for i in range(n)])]
    pallas_call x2 -> x3, Pallas kernels: 3.92 us -> 4.09 us  [down(): pl.pallas_call(functools.partial(down_kernel, len(pieces), len(behind), p...]
  transfers between devices with their start and end apart: 19 -> 22, of which waited for: 10 -> 9; matrix products, arithmetic and copies ran while one was open for 0% -> 0% of each run, Pallas kernels for 30% -> 32%
where the time goes in v21:
time: 57.9 us; the launch traced here: 57.8 us
  Pallas kernels  22.7 us (39%)
  starting transfers between devices  22.2 us (38%)
  waiting for transfers between devices  12 us (21%)
  other arithmetic  0.67 us (1%)
    ppermute x22, starting transfers between devices, swap(): return lax.ppermute(x, axis, [(i, i ^ step) for i in range(n)])  22.2 us
    ppermute x22, waiting for transfers between devices, swap(): return lax.ppermute(x, axis, [(i, i ^ step) for i in range(n)])  12 us
    pallas_call x2, Pallas kernels, fetch(): pl.pallas_call(functools.partial(fetch_kernel, first), in_specs=[spec(plt...  9.16 us
    pallas_call x2, Pallas kernels, gate_up(): pl.pallas_call(functools.partial(gate_up_kernel, len(arrays), len(weights...  9 us
    pallas_call x3, Pallas kernels, down(): pl.pallas_call(functools.partial(down_kernel, len(pieces), len(behind), p...  4.09 us
  transfers between devices with their start and end apart: 22, of which 9 were waited for; matrix products, arithmetic and copies ran while one was open for 0% of the time, Pallas kernels for 32%

profile of v21, /device:TPU:0, one launch (start us, length us, event | category | flops | bytes accessed | tf_op | source)
XLA Modules:
  0.0 57.8 jit_solution(14619464558247599546)
XLA Ops:
  0.0 5.0 %collective-permute-start.2 = (bf16[16,2048]{1,0:T(8,128)(2,1)}, bf16[16,2048]{1,0:T(8,128)(2,1)S(1)}, u32[]{:S(2)}, u32[]{:S(2)}) collective-permute-start(bf16[16,2048]{1,0:T(8,128)(2,1)} %tokens_ref.3), channel_id=1, source_target_pairs={{0,12},{4,8},{8,4},{12,0},{1,13},{5,9},{9,5},{13,1},{2,14},{6,10},... | collective-permute-start | bytes 196616 | tf_op jit(solution)/shard_map/ppermute | solution.py:276
  5.0 0.0 collective-permute-start.1
  5.1 0.6 collective-permute-start
  5.6 1.7 %collective-permute-start.3 = (bf16[16,2048]{1,0:T(8,128)(2,1)}, bf16[16,2048]{1,0:T(8,128)(2,1)S(1)}, u32[]{:S(2)}, u32[]{:S(2)}) collective-permute-start(bf16[16,2048]{1,0:T(8,128)(2,1)} %tokens_ref.3), channel_id=1, source_target_pairs={{0,16},{16,0},{1,17},{17,1},{2,18},{18,2},{3,19},{19,3},{4,20},{20... | collective-permute-start | bytes 196616 | tf_op jit(solution)/shard_map/ppermute | solution.py:276
  7.4 4.3 %fetch.2 = (bf16[2048,1280]{1,0:T(8,128)(2,1)S(1)}, bf16[2048,1280]{1,0:T(8,128)(2,1)S(1)}, bf16[16,2048]{1,0:T(8,128)(2,1)S(1)}) custom-call(bf16[2048,6656]{1,0:T(8,128)(2,1)} %refs_2_.1, bf16[2048,6656]{1,0:T(8,128)(2,1)} %refs_3_.1, bf16[16,2048]{1,0:T(8,128)(2,1)} %tokens_ref.3), custom_call_target="tpu_custom_call" | custom-call | bytes 1024 | tf_op jit(solution)/shard_map/fetch/pallas_call | solution.py:78
  11.6 0.0 collective-permute-done.2.refs_2_
  11.7 0.0 collective-permute-done.refs_0_
  11.7 0.0 collective-permute-done.3.refs_4_.refs_2_
  11.7 0.8 %collective-permute-start.4 = (bf16[48,2048]{1,0:T(8,128)(2,1)S(1)}, bf16[48,2048]{1,0:T(8,128)(2,1)S(1)}, u32[]{:S(2)}, u32[]{:S(2)}) collective-permute-start(bf16[48,2048]{1,0:T(8,128)(2,1)S(1)} %join.4.refs_1_), channel_id=1, source_target_pairs={{0,16},{16,0},{1,17},{17,1},{2,18},{18,2},{3,19},{19,3},{4,20},{20... | collective-permute-start | bytes 589832 | tf_op jit(solution)/shard_map/ppermute | solution.py:276
  12.5 4.9 %fetch.3 = (bf16[2048,1280]{1,0:T(8,128)(2,1)S(1)}, bf16[2048,1280]{1,0:T(8,128)(2,1)S(1)}, bf16[16,2048]{1,0:T(8,128)(2,1)}) custom-call(bf16[2048,6656]{1,0:T(8,128)(2,1)} %refs_2_.1, bf16[2048,6656]{1,0:T(8,128)(2,1)} %refs_3_.1, bf16[16,2048]{1,0:T(8,128)(2,1)} %tokens_ref.3), custom_call_target="tpu_custom_call" | custom-call | bytes 1024 | tf_op jit(solution)/shard_map/fetch/pallas_call | solution.py:78
  17.4 0.1 collective-permute-done.4.refs_3_
  17.4 2.9 %gate_up.2 = (bf16[2,64,2560]{2,1,0:T(8,128)(2,1)S(1)}, bf16[2,64,2560]{2,1,0:T(8,128)(2,1)S(1)}) custom-call(bf16[16,2048]{1,0:T(8,128)(2,1)S(1)} %get-tuple-element.20.refs_3_.refs_0_, bf16[48,2048]{1,0:T(8,128)(2,1)S(1)} %join.4.refs_1_, bf16[16,2048]{1,0:T(8,128)(2,1)S(1)} %collective-permute-done.3.refs_4_.refs_2_, ...), custom_call_target="tpu_custom_call" | custom-call | bytes 1024 | tf_op jit(solution)/shard_map/gate_up/pallas_call | solution.py:154
  20.4 0.1 collective-permute-start.5
  20.4 2.1 %collective-permute-done.5.got_ref = bf16[2,64,2560]{2,1,0:T(8,128)(2,1)S(1)} collective-permute-done((bf16[2,64,2560]{2,1,0:T(8,128)(2,1)S(1)}, bf16[2,64,2560]{2,1,0:T(8,128)(2,1)S(1)}, u32[]{:S(2)}, u32[]{:S(2)}) %collective-permute-start.5) | collective-permute-done | bytes 655392 | tf_op jit(solution)/shard_map/ppermute | solution.py:276
  22.5 0.1 pair_sum.2.refs_4_
  22.6 0.0 slice-start.1
  22.6 0.0 slice-start.2
  22.6 0.0 slice-start.4
  22.7 0.0 slice-start.5
  22.7 1.7 %collective-permute-start.7 = (bf16[2,32,2560]{2,1,0:T(8,128)(2,1)S(1)}, bf16[2,32,2560]{2,1,0:T(8,128)(2,1)S(1)}, u32[]{:S(2)}, u32[]{:S(2)}) collective-permute-start(bf16[2,32,2560]{2,1,0:T(8,128)(2,1)S(1)} %pair_sum.2.refs_4_), channel_id=1, source_target_pairs={{0,2},{1,3},{2,0},{3,1},{4,6},{5,7},{6,4},{7,5},{8,10},{9,11},{10,... | collective-permute-start | bytes 983048 | tf_op jit(solution)/shard_map/ppermute | solution.py:276
  24.4 6.1 %gate_up.3 = (bf16[2,32,1536]{2,1,0:T(8,128)(2,1)S(1)}, bf16[2,32,1536]{2,1,0:T(8,128)(2,1)S(1)}) custom-call(bf16[16,2048]{1,0:T(8,128)(2,1)S(1)} %get-tuple-element.20.refs_3_.refs_0_, bf16[48,2048]{1,0:T(8,128)(2,1)S(1)} %join.4.refs_1_, bf16[2048,6656]{1,0:T(8,128)(2,1)} %refs_2_.1, bf16[2048,6656]{1,0:T(8,128)(2,1)} %refs_3_.1, ...), custom_call_target="tpu_custom_call" | custom-call | bytes 1024 | tf_op jit(solution)/shard_map/gate_up/pallas_call | solution.py:154
  30.5 0.1 collective-permute-start.6
  30.6 1.9 %collective-permute-done.7.chip_ref = bf16[2,32,2560]{2,1,0:T(8,128)(2,1)S(1)} collective-permute-done((bf16[2,32,2560]{2,1,0:T(8,128)(2,1)S(1)}, bf16[2,32,2560]{2,1,0:T(8,128)(2,1)S(1)}, u32[]{:S(2)}, u32[]{:S(2)}) %collective-permute-start.7) | collective-permute-done | bytes 327712 | tf_op jit(solution)/shard_map/ppermute | solution.py:276
  32.5 0.2 combine.2
  32.7 1.8 %collective-permute-start.14 = (bf16[16,2560]{1,0:T(8,128)(2,1)S(1)}, bf16[16,2560]{1,0:T(8,128)(2,1)S(1)}, u32[]{:S(2)}, u32[]{:S(2)}) collective-permute-start(bf16[16,2560]{1,0:T(8,128)(2,1)S(1)} %get-tuple-element.29.refs_0_), channel_id=1, source_target_pairs={{0,16},{16,0},{1,17},{17,1},{2,18},{18,2},{3,19},{19,3},{4,20},{20... | collective-permute-start | bytes 245768 | tf_op jit(solution)/shard_map/ppermute | solution.py:276
  34.5 1.5 %collective-permute-start.8 = (bf16[2,16,1536]{2,1,0:T(8,128)(2,1)S(1)}, bf16[2,16,1536]{2,1,0:T(8,128)(2,1)S(1)}, u32[]{:S(2)}, u32[]{:S(2)}) collective-permute-start(bf16[2,16,1536]{2,1,0:T(8,128)(2,1)S(1)} %pair_sum.3), channel_id=1, source_target_pairs={{0,2},{1,3},{2,0},{3,1},{4,6},{5,7},{6,4},{7,5},{8,10},{9,11},{10,... | collective-permute-start | bytes 294920 | tf_op jit(solution)/shard_map/ppermute | solution.py:276
  36.0 0.5 collective-permute-start.11
  36.6 0.6 %collective-permute-done.14.refs_0_ = bf16[16,2560]{1,0:T(8,128)(2,1)S(1)} collective-permute-done((bf16[16,2560]{1,0:T(8,128)(2,1)S(1)}, bf16[16,2560]{1,0:T(8,128)(2,1)S(1)}, u32[]{:S(2)}, u32[]{:S(2)}) %collective-permute-start.14) | collective-permute-done | bytes 81952 | tf_op jit(solution)/shard_map/ppermute | solution.py:276
  37.2 1.7 %collective-permute-start.15 = (bf16[16,2560]{1,0:T(8,128)(2,1)S(1)}, bf16[16,2560]{1,0:T(8,128)(2,1)S(1)}, u32[]{:S(2)}, u32[]{:S(2)}) collective-permute-start(bf16[16,2560]{1,0:T(8,128)(2,1)S(1)} %collective-permute-done.14.refs_0_), channel_id=1, source_target_pairs={{0,2},{1,3},{2,0},{3,1},{4,6},{5,7},{6,4},{7,5},{8,10},{9,11},{10,... | collective-permute-start | bytes 245768 | tf_op jit(solution)/shard_map/ppermute | solution.py:276
  38.9 1.3 %collective-permute-done.8.chip_ref = bf16[2,16,1536]{2,1,0:T(8,128)(2,1)S(1)} collective-permute-done((bf16[2,16,1536]{2,1,0:T(8,128)(2,1)S(1)}, bf16[2,16,1536]{2,1,0:T(8,128)(2,1)S(1)}, u32[]{:S(2)}, u32[]{:S(2)}) %collective-permute-start.8) | collective-permute-done | bytes 98336 | tf_op jit(solution)/shard_map/ppermute | solution.py:276
  40.2 0.1 combine.3.refs_1_.refs_0_
  40.2 0.8 %collective-permute-done.11.refs_0_.refs_1_ = bf16[16,2560]{1,0:T(8,128)(2,1)S(1)} collective-permute-done((bf16[16,2560]{1,0:T(8,128)(2,1)S(1)}, bf16[16,2560]{1,0:T(8,128)(2,1)S(1)}, u32[]{:S(2)}, u32[]{:S(2)}) %collective-permute-start.11) | collective-permute-done | bytes 81952 | tf_op jit(solution)/shard_map/ppermute | solution.py:276
  41.1 0.0 collective-permute-start.13
  41.1 1.4 %collective-permute-start.9 = (bf16[16,1536]{1,0:T(8,128)(2,1)S(1)}, bf16[16,1536]{1,0:T(8,128)(2,1)S(1)}, u32[]{:S(2)}, u32[]{:S(2)}) collective-permute-start(bf16[16,1536]{1,0:T(8,128)(2,1)S(1)} %combine.3.refs_1_.refs_0_), channel_id=1, source_target_pairs={{0,2},{1,3},{2,0},{3,1},{4,6},{5,7},{6,4},{7,5},{8,10},{9,11},{10,... | collective-permute-start | bytes 147464 | tf_op jit(solution)/shard_map/ppermute | solution.py:276
  42.5 0.2 collective-permute-start.17
  42.6 0.0 collective-permute-done.15.refs_0_.refs_1_
  42.7 0.4 collective-permute-start.18
  43.1 0.2 collective-permute-start.10
  43.3 1.5 %down.3.refs_1_.refs_5_ = f32[64,2048]{1,0:T(8,128)S(1)} custom-call(bf16[16,2560]{1,0:T(8,128)(2,1)S(1)} %get-tuple-element.30.refs_0_, bf16[16,2560]{1,0:T(8,128)(2,1)S(1)} %collective-permute-done.11.refs_0_.refs_1_, bf16[16,2560]{1,0:T(8,128)(2,1)S(1)} %collective-permute-done.12.refs_2_, bf16[16,2560]{1,0:T(8,128)(2,1)S(1)} %collective-permute-done.13.refs_3_, ...), custom_call_target="tpu_custom_call" | custom-call | bytes 1024 | tf_op jit(solution)/shard_map/down/pallas_call | solution.py:258
  44.9 0.4 collective-permute-done.9.refs_0_.refs_1_
  45.2 0.1 collective-permute-start.16
  45.3 1.5 %down.4.refs_5_ = f32[64,2048]{1,0:T(8,128)S(1)} custom-call(bf16[16,2560]{1,0:T(8,128)(2,1)S(1)} %collective-permute-done.14.refs_0_, bf16[16,2560]{1,0:T(8,128)(2,1)S(1)} %collective-permute-done.15.refs_0_.refs_1_, bf16[16,2560]{1,0:T(8,128)(2,1)S(1)} %collective-permute-done.17.refs_2_, bf16[16,2560]{1,0:T(8,128)(2,1)S(1)} %collective-permute-done.18.refs_3_, ...), custom_call_target="tpu_custom_call" | custom-call | bytes 1024 | tf_op jit(solution)/shard_map/down/pallas_call | solution.py:258
  46.9 1.0 %down.5 = (bf16[16,2048]{1,0:T(8,128)(2,1)S(1)}, bf16[16,2048]{1,0:T(8,128)(2,1)S(1)}, bf16[16,2048]{1,0:T(8,128)(2,1)S(1)}, bf16[16,2048]{1,0:T(8,128)(2,1)S(1)}) custom-call(bf16[16,1536]{1,0:T(8,128)(2,1)S(1)} %combine.3.refs_1_.refs_0_, bf16[16,1536]{1,0:T(8,128)(2,1)S(1)} %collective-permute-done.9.refs_0_.refs_1_, ...), custom_call_target="tpu_custom_call" | custom-call | bytes 1024 | tf_op jit(solution)/shard_map/down/pallas_call | solution.py:258
  47.9 3.2 %collective-permute-start.19 = (bf16[16,2048]{1,0:T(8,128)(2,1)S(1)}, bf16[16,2048]{1,0:T(8,128)(2,1)S(1)}, u32[]{:S(2)}, u32[]{:S(2)}) collective-permute-start(bf16[16,2048]{1,0:T(8,128)(2,1)S(1)} %get-tuple-element.32), channel_id=1, source_target_pairs={{0,12},{4,8},{8,4},{12,0},{1,13},{5,9},{9,5},{13,1},{2,14},{6,10},... | collective-permute-start | bytes 196616 | tf_op jit(solution)/shard_map/ppermute | solution.py:276
  51.1 1.2 %collective-permute-start.21 = (bf16[16,2048]{1,0:T(8,128)(2,1)S(1)}, bf16[16,2048]{1,0:T(8,128)(2,1)S(1)}, u32[]{:S(2)}, u32[]{:S(2)}) collective-permute-start(bf16[16,2048]{1,0:T(8,128)(2,1)S(1)} %get-tuple-element.34), channel_id=1, source_target_pairs={{0,4},{4,0},{8,12},{12,8},{1,5},{5,1},{9,13},{13,9},{2,6},{6,2},{1... | collective-permute-start | bytes 196616 | tf_op jit(solution)/shard_map/ppermute | solution.py:276
  52.3 2.3 %collective-permute-done.19 = bf16[16,2048]{1,0:T(8,128)(2,1)S(1)} collective-permute-done((bf16[16,2048]{1,0:T(8,128)(2,1)S(1)}, bf16[16,2048]{1,0:T(8,128)(2,1)S(1)}, u32[]{:S(2)}, u32[]{:S(2)}) %collective-permute-start.19) | collective-permute-done | bytes 65568 | tf_op jit(solution)/shard_map/ppermute | solution.py:276
  54.6 2.4 %collective-permute-done.20 = bf16[16,2048]{1,0:T(8,128)(2,1)S(1)} collective-permute-done((bf16[16,2048]{1,0:T(8,128)(2,1)S(1)}, bf16[16,2048]{1,0:T(8,128)(2,1)S(1)}, u32[]{:S(2)}, u32[]{:S(2)}) %collective-permute-start.20) | collective-permute-done | bytes 65568 | tf_op jit(solution)/shard_map/ppermute | solution.py:276
  57.1 0.7 %add_convert_fusion = bf16[16,2048]{1,0:T(8,128)(2,1)} fusion(bf16[16,2048]{1,0:T(8,128)(2,1)S(1)} %collective-permute-done.21, bf16[16,2048]{1,0:T(8,128)(2,1)S(1)} %collective-permute-done.20, bf16[16,2048]{1,0:T(8,128)(2,1)S(1)} %collective-permute-done.19, bf16[16,2048]{1,0:T(8,128)(2,1)S(1)} %get-tuple-element.31), kind=kLoop, calls=%fused_computation | loop fusion | flops 262144 | bytes 327680 | tf_op jit(solution)/shard_map/convert_element_type | solution.py:322
  (27 shorter events, 0.1 us)
Async XLA Ops:
  0.0 11.6 %collective-permute-start.2 = (bf16[16,2048]{1,0:T(8,128)(2,1)}, bf16[16,2048]{1,0:T(8,128)(2,1)S(1)}, u32[]{:S(2)}, u32[]{:S(2)}) collective-permute-start(bf16[16,2048]{1,0:T(8,128)(2,1)} %tokens_ref.3), channel_id=1, source_target_pairs={{0,12},{4,8},{8,4},{12,0},{1,13},{5,9},{9,5},{13,1},{2,14},{6,10},... | collective-permute-start | bytes 196616 | tf_op jit(solution)/shard_map/ppermute | solution.py:276
  5.0 6.6 %collective-permute-start.1 = (bf16[16,2048]{1,0:T(8,128)(2,1)}, bf16[16,2048]{1,0:T(8,128)(2,1)S(1)}, u32[]{:S(2)}, u32[]{:S(2)}) collective-permute-start(bf16[16,2048]{1,0:T(8,128)(2,1)} %tokens_ref.3), channel_id=1, source_target_pairs={{0,8},{4,12},{8,0},{12,4},{1,9},{5,13},{9,1},{13,5},{2,10},{6,14},... | collective-permute-start | bytes 196616 | tf_op jit(solution)/shard_map/ppermute | solution.py:276
  5.1 6.6 %collective-permute-start = (bf16[16,2048]{1,0:T(8,128)(2,1)}, bf16[16,2048]{1,0:T(8,128)(2,1)S(1)}, u32[]{:S(2)}, u32[]{:S(2)}) collective-permute-start(bf16[16,2048]{1,0:T(8,128)(2,1)} %tokens_ref.3), channel_id=1, source_target_pairs={{0,4},{4,0},{8,12},{12,8},{1,5},{5,1},{9,13},{13,9},{2,6},{6,2},{1... | collective-permute-start | bytes 196616 | tf_op jit(solution)/shard_map/ppermute | solution.py:276
  5.6 6.0 %collective-permute-start.3 = (bf16[16,2048]{1,0:T(8,128)(2,1)}, bf16[16,2048]{1,0:T(8,128)(2,1)S(1)}, u32[]{:S(2)}, u32[]{:S(2)}) collective-permute-start(bf16[16,2048]{1,0:T(8,128)(2,1)} %tokens_ref.3), channel_id=1, source_target_pairs={{0,16},{16,0},{1,17},{17,1},{2,18},{18,2},{3,19},{19,3},{4,20},{20... | collective-permute-start | bytes 196616 | tf_op jit(solution)/shard_map/ppermute | solution.py:276
  11.7 5.7 %collective-permute-start.4 = (bf16[48,2048]{1,0:T(8,128)(2,1)S(1)}, bf16[48,2048]{1,0:T(8,128)(2,1)S(1)}, u32[]{:S(2)}, u32[]{:S(2)}) collective-permute-start(bf16[48,2048]{1,0:T(8,128)(2,1)S(1)} %join.4.refs_1_), channel_id=1, source_target_pairs={{0,16},{16,0},{1,17},{17,1},{2,18},{18,2},{3,19},{19,3},{4,20},{20... | collective-permute-start | bytes 589832 | tf_op jit(solution)/shard_map/ppermute | solution.py:276
  20.4 2.2 %collective-permute-start.5 = (bf16[2,64,2560]{2,1,0:T(8,128)(2,1)S(1)}, bf16[2,64,2560]{2,1,0:T(8,128)(2,1)S(1)}, u32[]{:S(2)}, u32[]{:S(2)}) collective-permute-start(bf16[2,64,2560]{2,1,0:T(8,128)(2,1)S(1)} %get-tuple-element.26), channel_id=1, source_target_pairs={{0,1},{1,0},{2,3},{3,2},{4,5},{5,4},{6,7},{7,6},{8,9},{9,8},{10,11... | collective-permute-start | bytes 1966088 | tf_op jit(solution)/shard_map/ppermute | solution.py:276
  22.5 20.7 %slice-start = ((s8[27262976]{0:T(1024)(128)(4,1)}), s8[4194304]{0:T(1024)(128)(4,1)S(1)}, s32[]{:S(2)}) async-start(s8[27262976]{0:T(1024)(128)(4,1)} %bitcast), calls=%async_computation | async-start | bytes 8388608
  22.6 20.6 %slice-start.1 = ((s8[27262976]{0:T(1024)(128)(4,1)}), s8[4194304]{0:T(1024)(128)(4,1)S(1)}, s32[]{:S(2)}) async-start(s8[27262976]{0:T(1024)(128)(4,1)} %bitcast), calls=%async_computation.1 | async-start | bytes 8388608
  22.6 20.6 %slice-start.2 = ((s8[27262976]{0:T(1024)(128)(4,1)}), s8[4194304]{0:T(1024)(128)(4,1)S(1)}, s32[]{:S(2)}) async-start(s8[27262976]{0:T(1024)(128)(4,1)} %bitcast), calls=%async_computation.2 | async-start | bytes 8388608
  22.6 20.6 %slice-start.3 = ((s8[27262976]{0:T(1024)(128)(4,1)}), s8[4194304]{0:T(1024)(128)(4,1)S(1)}, s32[]{:S(2)}) async-start(s8[27262976]{0:T(1024)(128)(4,1)} %bitcast), calls=%async_computation.3 | async-start | bytes 8388608
  22.6 20.6 %slice-start.4 = ((s8[27262976]{0:T(1024)(128)(4,1)}), s8[4194304]{0:T(1024)(128)(4,1)S(1)}, s32[]{:S(2)}) async-start(s8[27262976]{0:T(1024)(128)(4,1)} %bitcast), calls=%async_computation.4 | async-start | bytes 8388608
  22.7 20.6 %slice-start.5 = ((s8[27262976]{0:T(1024)(128)(4,1)}), s8[4194304]{0:T(1024)(128)(4,1)S(1)}, s32[]{:S(2)}) async-start(s8[27262976]{0:T(1024)(128)(4,1)} %bitcast), calls=%async_computation.5 | async-start | bytes 8388608
  22.7 20.6 %slice-start.6 = ((s8[27262976]{0:T(1024)(128)(4,1)}), s8[2097152]{0:T(1024)(128)(4,1)S(1)}, s32[]{:S(2)}) async-start(s8[27262976]{0:T(1024)(128)(4,1)} %bitcast), calls=%async_computation.6 | async-start | bytes 4194304
  22.7 9.8 %collective-permute-start.7 = (bf16[2,32,2560]{2,1,0:T(8,128)(2,1)S(1)}, bf16[2,32,2560]{2,1,0:T(8,128)(2,1)S(1)}, u32[]{:S(2)}, u32[]{:S(2)}) collective-permute-start(bf16[2,32,2560]{2,1,0:T(8,128)(2,1)S(1)} %pair_sum.2.refs_4_), channel_id=1, source_target_pairs={{0,2},{1,3},{2,0},{3,1},{4,6},{5,7},{6,4},{7,5},{8,10},{9,11},{10,... | collective-permute-start | bytes 983048 | tf_op jit(solution)/shard_map/ppermute | solution.py:276
  30.5 4.0 %collective-permute-start.6 = (bf16[2,32,1536]{2,1,0:T(8,128)(2,1)S(1)}, bf16[2,32,1536]{2,1,0:T(8,128)(2,1)S(1)}, u32[]{:S(2)}, u32[]{:S(2)}) collective-permute-start(bf16[2,32,1536]{2,1,0:T(8,128)(2,1)S(1)} %get-tuple-element.28), channel_id=1, source_target_pairs={{0,1},{1,0},{2,3},{3,2},{4,5},{5,4},{6,7},{7,6},{8,9},{9,8},{10,11... | collective-permute-start | bytes 589832 | tf_op jit(solution)/shard_map/ppermute | solution.py:276
  32.7 4.5 %collective-permute-start.14 = (bf16[16,2560]{1,0:T(8,128)(2,1)S(1)}, bf16[16,2560]{1,0:T(8,128)(2,1)S(1)}, u32[]{:S(2)}, u32[]{:S(2)}) collective-permute-start(bf16[16,2560]{1,0:T(8,128)(2,1)S(1)} %get-tuple-element.29.refs_0_), channel_id=1, source_target_pairs={{0,16},{16,0},{1,17},{17,1},{2,18},{18,2},{3,19},{19,3},{4,20},{20... | collective-permute-start | bytes 245768 | tf_op jit(solution)/shard_map/ppermute | solution.py:276
  34.5 5.7 %collective-permute-start.8 = (bf16[2,16,1536]{2,1,0:T(8,128)(2,1)S(1)}, bf16[2,16,1536]{2,1,0:T(8,128)(2,1)S(1)}, u32[]{:S(2)}, u32[]{:S(2)}) collective-permute-start(bf16[2,16,1536]{2,1,0:T(8,128)(2,1)S(1)} %pair_sum.3), channel_id=1, source_target_pairs={{0,2},{1,3},{2,0},{3,1},{4,6},{5,7},{6,4},{7,5},{8,10},{9,11},{10,... | collective-permute-start | bytes 294920 | tf_op jit(solution)/shard_map/ppermute | solution.py:276
  36.0 5.0 %collective-permute-start.11 = (bf16[16,2560]{1,0:T(8,128)(2,1)S(1)}, bf16[16,2560]{1,0:T(8,128)(2,1)S(1)}, u32[]{:S(2)}, u32[]{:S(2)}) collective-permute-start(bf16[16,2560]{1,0:T(8,128)(2,1)S(1)} %get-tuple-element.30.refs_0_), channel_id=1, source_target_pairs={{0,2},{1,3},{2,0},{3,1},{4,6},{5,7},{6,4},{7,5},{8,10},{9,11},{10,... | collective-permute-start | bytes 245768 | tf_op jit(solution)/shard_map/ppermute | solution.py:276
  37.2 5.4 %collective-permute-start.15 = (bf16[16,2560]{1,0:T(8,128)(2,1)S(1)}, bf16[16,2560]{1,0:T(8,128)(2,1)S(1)}, u32[]{:S(2)}, u32[]{:S(2)}) collective-permute-start(bf16[16,2560]{1,0:T(8,128)(2,1)S(1)} %collective-permute-done.14.refs_0_), channel_id=1, source_target_pairs={{0,2},{1,3},{2,0},{3,1},{4,6},{5,7},{6,4},{7,5},{8,10},{9,11},{10,... | collective-permute-start | bytes 245768 | tf_op jit(solution)/shard_map/ppermute | solution.py:276
  38.9 4.2 %collective-permute-start.12 = (bf16[16,2560]{1,0:T(8,128)(2,1)S(1)}, bf16[16,2560]{1,0:T(8,128)(2,1)S(1)}, u32[]{:S(2)}, u32[]{:S(2)}) collective-permute-start(bf16[16,2560]{1,0:T(8,128)(2,1)S(1)} %get-tuple-element.30.refs_0_), channel_id=1, source_target_pairs={{0,1},{1,0},{2,3},{3,2},{4,5},{5,4},{6,7},{7,6},{8,9},{9,8},{10,11... | collective-permute-start | bytes 245768 | tf_op jit(solution)/shard_map/ppermute | solution.py:276
  41.1 2.2 %collective-permute-start.13 = (bf16[16,2560]{1,0:T(8,128)(2,1)S(1)}, bf16[16,2560]{1,0:T(8,128)(2,1)S(1)}, u32[]{:S(2)}, u32[]{:S(2)}) collective-permute-start(bf16[16,2560]{1,0:T(8,128)(2,1)S(1)} %join.5), channel_id=1, source_target_pairs={{0,1},{1,0},{2,3},{3,2},{4,5},{5,4},{6,7},{7,6},{8,9},{9,8},{10,11... | collective-permute-start | bytes 245768 | tf_op jit(solution)/shard_map/ppermute | solution.py:276
  41.1 4.2 %collective-permute-start.9 = (bf16[16,1536]{1,0:T(8,128)(2,1)S(1)}, bf16[16,1536]{1,0:T(8,128)(2,1)S(1)}, u32[]{:S(2)}, u32[]{:S(2)}) collective-permute-start(bf16[16,1536]{1,0:T(8,128)(2,1)S(1)} %combine.3.refs_1_.refs_0_), channel_id=1, source_target_pairs={{0,2},{1,3},{2,0},{3,1},{4,6},{5,7},{6,4},{7,5},{8,10},{9,11},{10,... | collective-permute-start | bytes 147464 | tf_op jit(solution)/shard_map/ppermute | solution.py:276
  42.5 2.8 %collective-permute-start.17 = (bf16[16,2560]{1,0:T(8,128)(2,1)S(1)}, bf16[16,2560]{1,0:T(8,128)(2,1)S(1)}, u32[]{:S(2)}, u32[]{:S(2)}) collective-permute-start(bf16[16,2560]{1,0:T(8,128)(2,1)S(1)} %collective-permute-done.14.refs_0_), channel_id=1, source_target_pairs={{0,1},{1,0},{2,3},{3,2},{4,5},{5,4},{6,7},{7,6},{8,9},{9,8},{10,11... | collective-permute-start | bytes 245768 | tf_op jit(solution)/shard_map/ppermute | solution.py:276
  42.7 2.7 %collective-permute-start.18 = (bf16[16,2560]{1,0:T(8,128)(2,1)S(1)}, bf16[16,2560]{1,0:T(8,128)(2,1)S(1)}, u32[]{:S(2)}, u32[]{:S(2)}) collective-permute-start(bf16[16,2560]{1,0:T(8,128)(2,1)S(1)} %join.6.refs_5_), channel_id=1, source_target_pairs={{0,1},{1,0},{2,3},{3,2},{4,5},{5,4},{6,7},{7,6},{8,9},{9,8},{10,11... | collective-permute-start | bytes 245768 | tf_op jit(solution)/shard_map/ppermute | solution.py:276
  43.1 3.8 %collective-permute-start.10 = (bf16[16,1536]{1,0:T(8,128)(2,1)S(1)}, bf16[16,1536]{1,0:T(8,128)(2,1)S(1)}, u32[]{:S(2)}, u32[]{:S(2)}) collective-permute-start(bf16[16,1536]{1,0:T(8,128)(2,1)S(1)} %combine.3.refs_1_.refs_0_), channel_id=1, source_target_pairs={{0,1},{1,0},{2,3},{3,2},{4,5},{5,4},{6,7},{7,6},{8,9},{9,8},{10,11... | collective-permute-start | bytes 147464 | tf_op jit(solution)/shard_map/ppermute | solution.py:276
  45.2 1.6 %collective-permute-start.16 = (bf16[16,1536]{1,0:T(8,128)(2,1)S(1)}, bf16[16,1536]{1,0:T(8,128)(2,1)S(1)}, u32[]{:S(2)}, u32[]{:S(2)}) collective-permute-start(bf16[16,1536]{1,0:T(8,128)(2,1)S(1)} %join.7.refs_6_), channel_id=1, source_target_pairs={{0,1},{1,0},{2,3},{3,2},{4,5},{5,4},{6,7},{7,6},{8,9},{9,8},{10,11... | collective-permute-start | bytes 147464 | tf_op jit(solution)/shard_map/ppermute | solution.py:276
  47.9 6.8 %collective-permute-start.19 = (bf16[16,2048]{1,0:T(8,128)(2,1)S(1)}, bf16[16,2048]{1,0:T(8,128)(2,1)S(1)}, u32[]{:S(2)}, u32[]{:S(2)}) collective-permute-start(bf16[16,2048]{1,0:T(8,128)(2,1)S(1)} %get-tuple-element.32), channel_id=1, source_target_pairs={{0,12},{4,8},{8,4},{12,0},{1,13},{5,9},{9,5},{13,1},{2,14},{6,10},... | collective-permute-start | bytes 196616 | tf_op jit(solution)/shard_map/ppermute | solution.py:276
  51.1 6.0 %collective-permute-start.20 = (bf16[16,2048]{1,0:T(8,128)(2,1)S(1)}, bf16[16,2048]{1,0:T(8,128)(2,1)S(1)}, u32[]{:S(2)}, u32[]{:S(2)}) collective-permute-start(bf16[16,2048]{1,0:T(8,128)(2,1)S(1)} %get-tuple-element.33), channel_id=1, source_target_pairs={{0,8},{4,12},{8,0},{12,4},{1,9},{5,13},{9,1},{13,5},{2,10},{6,14},... | collective-permute-start | bytes 196616 | tf_op jit(solution)/shard_map/ppermute | solution.py:276
  51.1 6.0 %collective-permute-start.21 = (bf16[16,2048]{1,0:T(8,128)(2,1)S(1)}, bf16[16,2048]{1,0:T(8,128)(2,1)S(1)}, u32[]{:S(2)}, u32[]{:S(2)}) collective-permute-start(bf16[16,2048]{1,0:T(8,128)(2,1)S(1)} %get-tuple-element.34), channel_id=1, source_target_pairs={{0,4},{4,0},{8,12},{12,8},{1,5},{5,1},{9,13},{13,9},{2,6},{6,2},{1... | collective-permute-start | bytes 196616 | tf_op jit(solution)/shard_map/ppermute | solution.py:276

commit v22 on v21

--- a/solution.py
+++ b/solution.py
@@ -186,6 +186,22 @@
     )(mine, got, *behind)
 
 
+def later_kernel(array_ref, *refs):
+    refs[-1][...] = array_ref[...]
+
+
+def later(array, behind):
+    return pl.pallas_call(
+        later_kernel,
+        in_specs=[spec(pltpu.VMEM)] + [spec(pl.ANY)] * len(behind),
+        out_specs=spec(pltpu.VMEM),
+        out_shape=jax.ShapeDtypeStruct(array.shape, array.dtype),
+        compiler_params=params(1),
+        cost_estimate=COST,
+        name="later",
+    )(array, *behind)
+
+
 def combine_kernel(n_left, n_outs, mine_ref, got_ref, chip_ref, *refs):
     outs = refs[-n_outs:]
     rows, first = chip_ref.shape[1], 0
@@ -310,14 +326,14 @@
         return (hidden, other, swap(hidden, "wid", 1), swap(held, "wid", 1)), [held]
 
     first, _ = gather(keep, [rest])
-    second, held = gather(far_columns, [])
+    second, held = gather(later(far_columns, [rest]), [])
     acc = down(first, down_weight, None, [(1, 0, bounds[2])], False, held)
     third, held = gather(rest, [acc])
     acc = down(second, down_weight, acc, [(-1, half, bounds[2])], False, held)
     acc = down(third, down_weight, acc, [(0, start, width) for start, width in segments], True, [])
 
     mixed = acc[0].astype(f32)
-    for d in (3, 2, 1):
+    for d in (2, 3, 1):
         mixed = mixed + swap(acc[d], "hid", d).astype(f32)
     return mixed.astype(bf16)
 

time: 57.9 us -> 58.7 us (1.014)
  waiting for transfers between devices: 12 us -> 14.5 us
  starting transfers between devices: 22.2 us -> 20.4 us
    ppermute x22, waiting for transfers between devices: 12 us -> 14.5 us  [swap(): return lax.ppermute(x, axis, [(i, i ^ step) for i in range(n)])]
    ppermute x22, starting transfers between devices: 22.2 us -> 20.4 us  [swap(): return lax.ppermute(x, axis, [(i, i ^ step) for i in range(n)])]
  transfers between devices with their start and end apart: 22 -> 22, of which waited for: 9 -> 10; matrix products, arithmetic and copies ran while one was open for 0% -> 0% of each run, Pallas kernels for 32% -> 32%
where the time goes in v22:
time: 58.7 us; the launch traced here: 58.5 us
  Pallas kernels  22.7 us (39%)
  starting transfers between devices  20.4 us (35%)
  waiting for transfers between devices  14.5 us (25%)
  other arithmetic  0.67 us (1%)
    ppermute x22, starting transfers between devices, swap(): return lax.ppermute(x, axis, [(i, i ^ step) for i in range(n)])  20.4 us
    ppermute x22, waiting for transfers between devices, swap(): return lax.ppermute(x, axis, [(i, i ^ step) for i in range(n)])  14.5 us
    pallas_call x2, Pallas kernels, fetch(): pl.pallas_call(functools.partial(fetch_kernel, first), in_specs=[spec(plt...  9.16 us
    pallas_call x2, Pallas kernels, gate_up(): pl.pallas_call(functools.partial(gate_up_kernel, len(arrays), len(weights...  9 us
    pallas_call x3, Pallas kernels, down(): pl.pallas_call(functools.partial(down_kernel, len(pieces), len(behind), p...  4.08 us
  transfers between devices with their start and end apart: 22, of which 10 were waited for; matrix products, arithmetic and copies ran while one was open for 0% of the time, Pallas kernels for 32%

profile of v22, /device:TPU:0, one launch (start us, length us, event | category | flops | bytes accessed | tf_op | source)
XLA Modules:
  0.0 58.5 jit_solution(10171763311421571965)
XLA Ops:
  0.0 5.0 %collective-permute-start.2 = (bf16[16,2048]{1,0:T(8,128)(2,1)}, bf16[16,2048]{1,0:T(8,128)(2,1)S(1)}, u32[]{:S(2)}, u32[]{:S(2)}) collective-permute-start(bf16[16,2048]{1,0:T(8,128)(2,1)} %tokens_ref.3), channel_id=1, source_target_pairs={{0,12},{4,8},{8,4},{12,0},{1,13},{5,9},{9,5},{13,1},{2,14},{6,10},... | collective-permute-start | bytes 196616 | tf_op jit(solution)/shard_map/ppermute | solution.py:292
  5.1 0.6 collective-permute-start
  5.6 1.7 %collective-permute-start.3 = (bf16[16,2048]{1,0:T(8,128)(2,1)}, bf16[16,2048]{1,0:T(8,128)(2,1)S(1)}, u32[]{:S(2)}, u32[]{:S(2)}) collective-permute-start(bf16[16,2048]{1,0:T(8,128)(2,1)} %tokens_ref.3), channel_id=1, source_target_pairs={{0,16},{16,0},{1,17},{17,1},{2,18},{18,2},{3,19},{19,3},{4,20},{20... | collective-permute-start | bytes 196616 | tf_op jit(solution)/shard_map/ppermute | solution.py:292
  7.4 4.3 %fetch.2 = (bf16[2048,1280]{1,0:T(8,128)(2,1)S(1)}, bf16[2048,1280]{1,0:T(8,128)(2,1)S(1)}, bf16[16,2048]{1,0:T(8,128)(2,1)S(1)}) custom-call(bf16[2048,6656]{1,0:T(8,128)(2,1)} %refs_2_.1, bf16[2048,6656]{1,0:T(8,128)(2,1)} %refs_3_.1, bf16[16,2048]{1,0:T(8,128)(2,1)} %tokens_ref.3), custom_call_target="tpu_custom_call" | custom-call | bytes 1024 | tf_op jit(solution)/shard_map/fetch/pallas_call | solution.py:78
  11.6 0.0 collective-permute-done.1.refs_1_
  11.7 0.8 %collective-permute-start.4 = (bf16[48,2048]{1,0:T(8,128)(2,1)S(1)}, bf16[48,2048]{1,0:T(8,128)(2,1)S(1)}, u32[]{:S(2)}, u32[]{:S(2)}) collective-permute-start(bf16[48,2048]{1,0:T(8,128)(2,1)S(1)} %join.4.refs_1_), channel_id=1, source_target_pairs={{0,16},{16,0},{1,17},{17,1},{2,18},{18,2},{3,19},{19,3},{4,20},{20... | collective-permute-start | bytes 589832 | tf_op jit(solution)/shard_map/ppermute | solution.py:292
  12.5 4.9 %fetch.3 = (bf16[2048,1280]{1,0:T(8,128)(2,1)S(1)}, bf16[2048,1280]{1,0:T(8,128)(2,1)S(1)}, bf16[16,2048]{1,0:T(8,128)(2,1)}) custom-call(bf16[2048,6656]{1,0:T(8,128)(2,1)} %refs_2_.1, bf16[2048,6656]{1,0:T(8,128)(2,1)} %refs_3_.1, bf16[16,2048]{1,0:T(8,128)(2,1)} %tokens_ref.3), custom_call_target="tpu_custom_call" | custom-call | bytes 1024 | tf_op jit(solution)/shard_map/fetch/pallas_call | solution.py:78
  17.4 0.1 collective-permute-done.4.refs_3_
  17.4 2.9 %gate_up.2 = (bf16[2,64,2560]{2,1,0:T(8,128)(2,1)S(1)}, bf16[2,64,2560]{2,1,0:T(8,128)(2,1)S(1)}) custom-call(bf16[16,2048]{1,0:T(8,128)(2,1)S(1)} %get-tuple-element.20.refs_3_.refs_0_, bf16[48,2048]{1,0:T(8,128)(2,1)S(1)} %join.4.refs_1_, bf16[16,2048]{1,0:T(8,128)(2,1)S(1)} %collective-permute-done.3.refs_4_.refs_2_, ...), custom_call_target="tpu_custom_call" | custom-call | bytes 1024 | tf_op jit(solution)/shard_map/gate_up/pallas_call | solution.py:154
  20.4 0.1 collective-permute-start.5
  20.4 2.1 %collective-permute-done.5.got_ref = bf16[2,64,2560]{2,1,0:T(8,128)(2,1)S(1)} collective-permute-done((bf16[2,64,2560]{2,1,0:T(8,128)(2,1)S(1)}, bf16[2,64,2560]{2,1,0:T(8,128)(2,1)S(1)}, u32[]{:S(2)}, u32[]{:S(2)}) %collective-permute-start.5) | collective-permute-done | bytes 655392 | tf_op jit(solution)/shard_map/ppermute | solution.py:292
  22.5 0.1 pair_sum.2.refs_4_
  22.6 0.0 slice-start.1
  22.6 0.0 slice-start.3
  22.7 0.0 slice-start.6
  22.7 1.7 %collective-permute-start.7 = (bf16[2,32,2560]{2,1,0:T(8,128)(2,1)S(1)}, bf16[2,32,2560]{2,1,0:T(8,128)(2,1)S(1)}, u32[]{:S(2)}, u32[]{:S(2)}) collective-permute-start(bf16[2,32,2560]{2,1,0:T(8,128)(2,1)S(1)} %pair_sum.2.refs_4_), channel_id=1, source_target_pairs={{0,2},{1,3},{2,0},{3,1},{4,6},{5,7},{6,4},{7,5},{8,10},{9,11},{10,... | collective-permute-start | bytes 983048 | tf_op jit(solution)/shard_map/ppermute | solution.py:292
  24.4 6.1 %gate_up.3 = (bf16[2,32,1536]{2,1,0:T(8,128)(2,1)S(1)}, bf16[2,32,1536]{2,1,0:T(8,128)(2,1)S(1)}) custom-call(bf16[16,2048]{1,0:T(8,128)(2,1)S(1)} %get-tuple-element.20.refs_3_.refs_0_, bf16[48,2048]{1,0:T(8,128)(2,1)S(1)} %join.4.refs_1_, bf16[2048,6656]{1,0:T(8,128)(2,1)} %refs_2_.1, bf16[2048,6656]{1,0:T(8,128)(2,1)} %refs_3_.1, ...), custom_call_target="tpu_custom_call" | custom-call | bytes 1024 | tf_op jit(solution)/shard_map/gate_up/pallas_call | solution.py:154
  30.5 0.1 collective-permute-start.6
  30.6 1.9 %collective-permute-done.7.chip_ref = bf16[2,32,2560]{2,1,0:T(8,128)(2,1)S(1)} collective-permute-done((bf16[2,32,2560]{2,1,0:T(8,128)(2,1)S(1)}, bf16[2,32,2560]{2,1,0:T(8,128)(2,1)S(1)}, u32[]{:S(2)}, u32[]{:S(2)}) %collective-permute-start.7) | collective-permute-done | bytes 327712 | tf_op jit(solution)/shard_map/ppermute | solution.py:292
  32.5 0.2 combine.2
  32.7 1.7 %collective-permute-start.8 = (bf16[2,16,1536]{2,1,0:T(8,128)(2,1)S(1)}, bf16[2,16,1536]{2,1,0:T(8,128)(2,1)S(1)}, u32[]{:S(2)}, u32[]{:S(2)}) collective-permute-start(bf16[2,16,1536]{2,1,0:T(8,128)(2,1)S(1)} %pair_sum.3), channel_id=1, source_target_pairs={{0,2},{1,3},{2,0},{3,1},{4,6},{5,7},{6,4},{7,5},{8,10},{9,11},{10,... | collective-permute-start | bytes 294920 | tf_op jit(solution)/shard_map/ppermute | solution.py:292
  34.5 1.5 %collective-permute-start.14 = (bf16[16,2560]{1,0:T(8,128)(2,1)S(1)}, bf16[16,2560]{1,0:T(8,128)(2,1)S(1)}, u32[]{:S(2)}, u32[]{:S(2)}) collective-permute-start(bf16[16,2560]{1,0:T(8,128)(2,1)S(1)} %get-tuple-element.29.refs_0_), channel_id=1, source_target_pairs={{0,16},{16,0},{1,17},{17,1},{2,18},{18,2},{3,19},{19,3},{4,20},{20... | collective-permute-start | bytes 245768 | tf_op jit(solution)/shard_map/ppermute | solution.py:292
  36.0 0.5 collective-permute-start.11
  36.5 1.0 %collective-permute-done.8.chip_ref = bf16[2,16,1536]{2,1,0:T(8,128)(2,1)S(1)} collective-permute-done((bf16[2,16,1536]{2,1,0:T(8,128)(2,1)S(1)}, bf16[2,16,1536]{2,1,0:T(8,128)(2,1)S(1)}, u32[]{:S(2)}, u32[]{:S(2)}) %collective-permute-start.8) | collective-permute-done | bytes 98336 | tf_op jit(solution)/shard_map/ppermute | solution.py:292
  37.5 0.1 combine.3.refs_1_.refs_0_
  37.6 1.3 %collective-permute-done.14.array_ref = bf16[16,2560]{1,0:T(8,128)(2,1)S(1)} collective-permute-done((bf16[16,2560]{1,0:T(8,128)(2,1)S(1)}, bf16[16,2560]{1,0:T(8,128)(2,1)S(1)}, u32[]{:S(2)}, u32[]{:S(2)}) %collective-permute-start.14) | collective-permute-done | bytes 81952 | tf_op jit(solution)/shard_map/ppermute | solution.py:292
  38.9 1.1 %collective-permute-start.15 = (bf16[16,2560]{1,0:T(8,128)(2,1)S(1)}, bf16[16,2560]{1,0:T(8,128)(2,1)S(1)}, u32[]{:S(2)}, u32[]{:S(2)}) collective-permute-start(bf16[16,2560]{1,0:T(8,128)(2,1)S(1)} %later.1.refs_0_), channel_id=1, source_target_pairs={{0,2},{1,3},{2,0},{3,1},{4,6},{5,7},{6,4},{7,5},{8,10},{9,11},{10,... | collective-permute-start | bytes 245768 | tf_op jit(solution)/shard_map/ppermute | solution.py:292
  40.0 0.0 collective-permute-start.12
  40.0 1.2 %collective-permute-done.11.refs_0_.refs_1_ = bf16[16,2560]{1,0:T(8,128)(2,1)S(1)} collective-permute-done((bf16[16,2560]{1,0:T(8,128)(2,1)S(1)}, bf16[16,2560]{1,0:T(8,128)(2,1)S(1)}, u32[]{:S(2)}, u32[]{:S(2)}) %collective-permute-start.11) | collective-permute-done | bytes 81952 | tf_op jit(solution)/shard_map/ppermute | solution.py:292
  41.2 0.0 collective-permute-start.13
  41.2 0.7 %collective-permute-start.9 = (bf16[16,1536]{1,0:T(8,128)(2,1)S(1)}, bf16[16,1536]{1,0:T(8,128)(2,1)S(1)}, u32[]{:S(2)}, u32[]{:S(2)}) collective-permute-start(bf16[16,1536]{1,0:T(8,128)(2,1)S(1)} %combine.3.refs_1_.refs_0_), channel_id=1, source_target_pairs={{0,2},{1,3},{2,0},{3,1},{4,6},{5,7},{6,4},{7,5},{8,10},{9,11},{10,... | collective-permute-start | bytes 147464 | tf_op jit(solution)/shard_map/ppermute | solution.py:292
  41.8 0.2 collective-permute-start.17
  42.0 1.4 %collective-permute-done.15.refs_0_.refs_1_ = bf16[16,2560]{1,0:T(8,128)(2,1)S(1)} collective-permute-done((bf16[16,2560]{1,0:T(8,128)(2,1)S(1)}, bf16[16,2560]{1,0:T(8,128)(2,1)S(1)}, u32[]{:S(2)}, u32[]{:S(2)}) %collective-permute-start.15) | collective-permute-done | bytes 81952 | tf_op jit(solution)/shard_map/ppermute | solution.py:292
  43.4 0.0 collective-permute-start.18
  43.4 0.5 collective-permute-start.10
  43.9 0.0 collective-permute-done.13.refs_3_
  43.9 1.5 %down.3.refs_1_.refs_5_ = f32[64,2048]{1,0:T(8,128)S(1)} custom-call(bf16[16,2560]{1,0:T(8,128)(2,1)S(1)} %get-tuple-element.30.refs_0_, bf16[16,2560]{1,0:T(8,128)(2,1)S(1)} %collective-permute-done.11.refs_0_.refs_1_, bf16[16,2560]{1,0:T(8,128)(2,1)S(1)} %collective-permute-done.12.refs_2_, bf16[16,2560]{1,0:T(8,128)(2,1)S(1)} %collective-permute-done.13.refs_3_, ...), custom_call_target="tpu_custom_call" | custom-call | bytes 1024 | tf_op jit(solution)/shard_map/down/pallas_call | solution.py:274
  45.5 0.0 collective-permute-done.9.refs_0_.refs_1_
  45.5 0.1 collective-permute-start.16
  45.7 1.5 %down.4.refs_5_ = f32[64,2048]{1,0:T(8,128)S(1)} custom-call(bf16[16,2560]{1,0:T(8,128)(2,1)S(1)} %later.1.refs_0_, bf16[16,2560]{1,0:T(8,128)(2,1)S(1)} %collective-permute-done.15.refs_0_.refs_1_, bf16[16,2560]{1,0:T(8,128)(2,1)S(1)} %collective-permute-done.17.refs_2_, bf16[16,2560]{1,0:T(8,128)(2,1)S(1)} %collective-permute-done.18.refs_3_, ...), custom_call_target="tpu_custom_call" | custom-call | bytes 1024 | tf_op jit(solution)/shard_map/down/pallas_call | solution.py:274
  47.2 1.0 %down.5 = (bf16[16,2048]{1,0:T(8,128)(2,1)S(1)}, bf16[16,2048]{1,0:T(8,128)(2,1)S(1)}, bf16[16,2048]{1,0:T(8,128)(2,1)S(1)}, bf16[16,2048]{1,0:T(8,128)(2,1)S(1)}) custom-call(bf16[16,1536]{1,0:T(8,128)(2,1)S(1)} %combine.3.refs_1_.refs_0_, bf16[16,1536]{1,0:T(8,128)(2,1)S(1)} %collective-permute-done.9.refs_0_.refs_1_, ...), custom_call_target="tpu_custom_call" | custom-call | bytes 1024 | tf_op jit(solution)/shard_map/down/pallas_call | solution.py:274
  48.2 2.2 %collective-permute-start.19 = (bf16[16,2048]{1,0:T(8,128)(2,1)S(1)}, bf16[16,2048]{1,0:T(8,128)(2,1)S(1)}, u32[]{:S(2)}, u32[]{:S(2)}) collective-permute-start(bf16[16,2048]{1,0:T(8,128)(2,1)S(1)} %get-tuple-element.32), channel_id=1, source_target_pairs={{0,8},{4,12},{8,0},{12,4},{1,9},{5,13},{9,1},{13,5},{2,10},{6,14},... | collective-permute-start | bytes 196616 | tf_op jit(solution)/shard_map/ppermute | solution.py:292
  50.4 1.5 %collective-permute-start.20 = (bf16[16,2048]{1,0:T(8,128)(2,1)S(1)}, bf16[16,2048]{1,0:T(8,128)(2,1)S(1)}, u32[]{:S(2)}, u32[]{:S(2)}) collective-permute-start(bf16[16,2048]{1,0:T(8,128)(2,1)S(1)} %get-tuple-element.33), channel_id=1, source_target_pairs={{0,12},{4,8},{8,4},{12,0},{1,13},{5,9},{9,5},{13,1},{2,14},{6,10},... | collective-permute-start | bytes 196616 | tf_op jit(solution)/shard_map/ppermute | solution.py:292
  51.9 0.4 collective-permute-start.21
  52.3 4.3 %collective-permute-done.19 = bf16[16,2048]{1,0:T(8,128)(2,1)S(1)} collective-permute-done((bf16[16,2048]{1,0:T(8,128)(2,1)S(1)}, bf16[16,2048]{1,0:T(8,128)(2,1)S(1)}, u32[]{:S(2)}, u32[]{:S(2)}) %collective-permute-start.19) | collective-permute-done | bytes 65568 | tf_op jit(solution)/shard_map/ppermute | solution.py:292
  56.6 0.4 collective-permute-done.20
  57.1 0.8 %collective-permute-done.21 = bf16[16,2048]{1,0:T(8,128)(2,1)S(1)} collective-permute-done((bf16[16,2048]{1,0:T(8,128)(2,1)S(1)}, bf16[16,2048]{1,0:T(8,128)(2,1)S(1)}, u32[]{:S(2)}, u32[]{:S(2)}) %collective-permute-start.21) | collective-permute-done | bytes 65568 | tf_op jit(solution)/shard_map/ppermute | solution.py:292
  57.9 0.7 %add_convert_fusion = bf16[16,2048]{1,0:T(8,128)(2,1)} fusion(bf16[16,2048]{1,0:T(8,128)(2,1)S(1)} %collective-permute-done.21, bf16[16,2048]{1,0:T(8,128)(2,1)S(1)} %collective-permute-done.20, bf16[16,2048]{1,0:T(8,128)(2,1)S(1)} %collective-permute-done.19, bf16[16,2048]{1,0:T(8,128)(2,1)S(1)} %get-tuple-element.31), kind=kLoop, calls=%fused_computation | loop fusion | flops 262144 | bytes 327680 | tf_op jit(solution)/shard_map/convert_element_type | solution.py:338
  (28 shorter events, 0.1 us)
Async XLA Ops:
  0.0 11.6 %collective-permute-start.2 = (bf16[16,2048]{1,0:T(8,128)(2,1)}, bf16[16,2048]{1,0:T(8,128)(2,1)S(1)}, u32[]{:S(2)}, u32[]{:S(2)}) collective-permute-start(bf16[16,2048]{1,0:T(8,128)(2,1)} %tokens_ref.3), channel_id=1, source_target_pairs={{0,12},{4,8},{8,4},{12,0},{1,13},{5,9},{9,5},{13,1},{2,14},{6,10},... | collective-permute-start | bytes 196616 | tf_op jit(solution)/shard_map/ppermute | solution.py:292
  5.0 6.6 %collective-permute-start.1 = (bf16[16,2048]{1,0:T(8,128)(2,1)}, bf16[16,2048]{1,0:T(8,128)(2,1)S(1)}, u32[]{:S(2)}, u32[]{:S(2)}) collective-permute-start(bf16[16,2048]{1,0:T(8,128)(2,1)} %tokens_ref.3), channel_id=1, source_target_pairs={{0,8},{4,12},{8,0},{12,4},{1,9},{5,13},{9,1},{13,5},{2,10},{6,14},... | collective-permute-start | bytes 196616 | tf_op jit(solution)/shard_map/ppermute | solution.py:292
  5.1 6.6 %collective-permute-start = (bf16[16,2048]{1,0:T(8,128)(2,1)}, bf16[16,2048]{1,0:T(8,128)(2,1)S(1)}, u32[]{:S(2)}, u32[]{:S(2)}) collective-permute-start(bf16[16,2048]{1,0:T(8,128)(2,1)} %tokens_ref.3), channel_id=1, source_target_pairs={{0,4},{4,0},{8,12},{12,8},{1,5},{5,1},{9,13},{13,9},{2,6},{6,2},{1... | collective-permute-start | bytes 196616 | tf_op jit(solution)/shard_map/ppermute | solution.py:292
  5.6 6.0 %collective-permute-start.3 = (bf16[16,2048]{1,0:T(8,128)(2,1)}, bf16[16,2048]{1,0:T(8,128)(2,1)S(1)}, u32[]{:S(2)}, u32[]{:S(2)}) collective-permute-start(bf16[16,2048]{1,0:T(8,128)(2,1)} %tokens_ref.3), channel_id=1, source_target_pairs={{0,16},{16,0},{1,17},{17,1},{2,18},{18,2},{3,19},{19,3},{4,20},{20... | collective-permute-start | bytes 196616 | tf_op jit(solution)/shard_map/ppermute | solution.py:292
  11.7 5.7 %collective-permute-start.4 = (bf16[48,2048]{1,0:T(8,128)(2,1)S(1)}, bf16[48,2048]{1,0:T(8,128)(2,1)S(1)}, u32[]{:S(2)}, u32[]{:S(2)}) collective-permute-start(bf16[48,2048]{1,0:T(8,128)(2,1)S(1)} %join.4.refs_1_), channel_id=1, source_target_pairs={{0,16},{16,0},{1,17},{17,1},{2,18},{18,2},{3,19},{19,3},{4,20},{20... | collective-permute-start | bytes 589832 | tf_op jit(solution)/shard_map/ppermute | solution.py:292
  20.4 2.2 %collective-permute-start.5 = (bf16[2,64,2560]{2,1,0:T(8,128)(2,1)S(1)}, bf16[2,64,2560]{2,1,0:T(8,128)(2,1)S(1)}, u32[]{:S(2)}, u32[]{:S(2)}) collective-permute-start(bf16[2,64,2560]{2,1,0:T(8,128)(2,1)S(1)} %get-tuple-element.26), channel_id=1, source_target_pairs={{0,1},{1,0},{2,3},{3,2},{4,5},{5,4},{6,7},{7,6},{8,9},{9,8},{10,11... | collective-permute-start | bytes 1966088 | tf_op jit(solution)/shard_map/ppermute | solution.py:292
  22.5 21.3 %slice-start = ((s8[27262976]{0:T(1024)(128)(4,1)}), s8[4194304]{0:T(1024)(128)(4,1)S(1)}, s32[]{:S(2)}) async-start(s8[27262976]{0:T(1024)(128)(4,1)} %bitcast), calls=%async_computation | async-start | bytes 8388608
  22.6 21.3 %slice-start.1 = ((s8[27262976]{0:T(1024)(128)(4,1)}), s8[4194304]{0:T(1024)(128)(4,1)S(1)}, s32[]{:S(2)}) async-start(s8[27262976]{0:T(1024)(128)(4,1)} %bitcast), calls=%async_computation.1 | async-start | bytes 8388608
  22.6 21.3 %slice-start.2 = ((s8[27262976]{0:T(1024)(128)(4,1)}), s8[4194304]{0:T(1024)(128)(4,1)S(1)}, s32[]{:S(2)}) async-start(s8[27262976]{0:T(1024)(128)(4,1)} %bitcast), calls=%async_computation.2 | async-start | bytes 8388608
  22.6 21.3 %slice-start.3 = ((s8[27262976]{0:T(1024)(128)(4,1)}), s8[4194304]{0:T(1024)(128)(4,1)S(1)}, s32[]{:S(2)}) async-start(s8[27262976]{0:T(1024)(128)(4,1)} %bitcast), calls=%async_computation.3 | async-start | bytes 8388608
  22.6 21.3 %slice-start.4 = ((s8[27262976]{0:T(1024)(128)(4,1)}), s8[4194304]{0:T(1024)(128)(4,1)S(1)}, s32[]{:S(2)}) async-start(s8[27262976]{0:T(1024)(128)(4,1)} %bitcast), calls=%async_computation.4 | async-start | bytes 8388608
  22.7 21.3 %slice-start.5 = ((s8[27262976]{0:T(1024)(128)(4,1)}), s8[4194304]{0:T(1024)(128)(4,1)S(1)}, s32[]{:S(2)}) async-start(s8[27262976]{0:T(1024)(128)(4,1)} %bitcast), calls=%async_computation.5 | async-start | bytes 8388608
  22.7 21.3 %slice-start.6 = ((s8[27262976]{0:T(1024)(128)(4,1)}), s8[2097152]{0:T(1024)(128)(4,1)S(1)}, s32[]{:S(2)}) async-start(s8[27262976]{0:T(1024)(128)(4,1)} %bitcast), calls=%async_computation.6 | async-start | bytes 4194304
  22.7 9.8 %collective-permute-start.7 = (bf16[2,32,2560]{2,1,0:T(8,128)(2,1)S(1)}, bf16[2,32,2560]{2,1,0:T(8,128)(2,1)S(1)}, u32[]{:S(2)}, u32[]{:S(2)}) collective-permute-start(bf16[2,32,2560]{2,1,0:T(8,128)(2,1)S(1)} %pair_sum.2.refs_4_), channel_id=1, source_target_pairs={{0,2},{1,3},{2,0},{3,1},{4,6},{5,7},{6,4},{7,5},{8,10},{9,11},{10,... | collective-permute-start | bytes 983048 | tf_op jit(solution)/shard_map/ppermute | solution.py:292
  30.5 2.2 %collective-permute-start.6 = (bf16[2,32,1536]{2,1,0:T(8,128)(2,1)S(1)}, bf16[2,32,1536]{2,1,0:T(8,128)(2,1)S(1)}, u32[]{:S(2)}, u32[]{:S(2)}) collective-permute-start(bf16[2,32,1536]{2,1,0:T(8,128)(2,1)S(1)} %get-tuple-element.28), channel_id=1, source_target_pairs={{0,1},{1,0},{2,3},{3,2},{4,5},{5,4},{6,7},{7,6},{8,9},{9,8},{10,11... | collective-permute-start | bytes 589832 | tf_op jit(solution)/shard_map/ppermute | solution.py:292
  32.7 4.8 %collective-permute-start.8 = (bf16[2,16,1536]{2,1,0:T(8,128)(2,1)S(1)}, bf16[2,16,1536]{2,1,0:T(8,128)(2,1)S(1)}, u32[]{:S(2)}, u32[]{:S(2)}) collective-permute-start(bf16[2,16,1536]{2,1,0:T(8,128)(2,1)S(1)} %pair_sum.3), channel_id=1, source_target_pairs={{0,2},{1,3},{2,0},{3,1},{4,6},{5,7},{6,4},{7,5},{8,10},{9,11},{10,... | collective-permute-start | bytes 294920 | tf_op jit(solution)/shard_map/ppermute | solution.py:292
  34.5 4.4 %collective-permute-start.14 = (bf16[16,2560]{1,0:T(8,128)(2,1)S(1)}, bf16[16,2560]{1,0:T(8,128)(2,1)S(1)}, u32[]{:S(2)}, u32[]{:S(2)}) collective-permute-start(bf16[16,2560]{1,0:T(8,128)(2,1)S(1)} %get-tuple-element.29.refs_0_), channel_id=1, source_target_pairs={{0,16},{16,0},{1,17},{17,1},{2,18},{18,2},{3,19},{19,3},{4,20},{20... | collective-permute-start | bytes 245768 | tf_op jit(solution)/shard_map/ppermute | solution.py:292
  36.0 5.2 %collective-permute-start.11 = (bf16[16,2560]{1,0:T(8,128)(2,1)S(1)}, bf16[16,2560]{1,0:T(8,128)(2,1)S(1)}, u32[]{:S(2)}, u32[]{:S(2)}) collective-permute-start(bf16[16,2560]{1,0:T(8,128)(2,1)S(1)} %get-tuple-element.30.refs_0_), channel_id=1, source_target_pairs={{0,2},{1,3},{2,0},{3,1},{4,6},{5,7},{6,4},{7,5},{8,10},{9,11},{10,... | collective-permute-start | bytes 245768 | tf_op jit(solution)/shard_map/ppermute | solution.py:292
  38.9 4.4 %collective-permute-start.15 = (bf16[16,2560]{1,0:T(8,128)(2,1)S(1)}, bf16[16,2560]{1,0:T(8,128)(2,1)S(1)}, u32[]{:S(2)}, u32[]{:S(2)}) collective-permute-start(bf16[16,2560]{1,0:T(8,128)(2,1)S(1)} %later.1.refs_0_), channel_id=1, source_target_pairs={{0,2},{1,3},{2,0},{3,1},{4,6},{5,7},{6,4},{7,5},{8,10},{9,11},{10,... | collective-permute-start | bytes 245768 | tf_op jit(solution)/shard_map/ppermute | solution.py:292
  40.0 3.4 %collective-permute-start.12 = (bf16[16,2560]{1,0:T(8,128)(2,1)S(1)}, bf16[16,2560]{1,0:T(8,128)(2,1)S(1)}, u32[]{:S(2)}, u32[]{:S(2)}) collective-permute-start(bf16[16,2560]{1,0:T(8,128)(2,1)S(1)} %get-tuple-element.30.refs_0_), channel_id=1, source_target_pairs={{0,1},{1,0},{2,3},{3,2},{4,5},{5,4},{6,7},{7,6},{8,9},{9,8},{10,11... | collective-permute-start | bytes 245768 | tf_op jit(solution)/shard_map/ppermute | solution.py:292
  41.2 2.7 %collective-permute-start.13 = (bf16[16,2560]{1,0:T(8,128)(2,1)S(1)}, bf16[16,2560]{1,0:T(8,128)(2,1)S(1)}, u32[]{:S(2)}, u32[]{:S(2)}) collective-permute-start(bf16[16,2560]{1,0:T(8,128)(2,1)S(1)} %join.5), channel_id=1, source_target_pairs={{0,1},{1,0},{2,3},{3,2},{4,5},{5,4},{6,7},{7,6},{8,9},{9,8},{10,11... | collective-permute-start | bytes 245768 | tf_op jit(solution)/shard_map/ppermute | solution.py:292
  41.2 4.3 %collective-permute-start.9 = (bf16[16,1536]{1,0:T(8,128)(2,1)S(1)}, bf16[16,1536]{1,0:T(8,128)(2,1)S(1)}, u32[]{:S(2)}, u32[]{:S(2)}) collective-permute-start(bf16[16,1536]{1,0:T(8,128)(2,1)S(1)} %combine.3.refs_1_.refs_0_), channel_id=1, source_target_pairs={{0,2},{1,3},{2,0},{3,1},{4,6},{5,7},{6,4},{7,5},{8,10},{9,11},{10,... | collective-permute-start | bytes 147464 | tf_op jit(solution)/shard_map/ppermute | solution.py:292
  41.8 3.8 %collective-permute-start.17 = (bf16[16,2560]{1,0:T(8,128)(2,1)S(1)}, bf16[16,2560]{1,0:T(8,128)(2,1)S(1)}, u32[]{:S(2)}, u32[]{:S(2)}) collective-permute-start(bf16[16,2560]{1,0:T(8,128)(2,1)S(1)} %later.1.refs_0_), channel_id=1, source_target_pairs={{0,1},{1,0},{2,3},{3,2},{4,5},{5,4},{6,7},{7,6},{8,9},{9,8},{10,11... | collective-permute-start | bytes 245768 | tf_op jit(solution)/shard_map/ppermute | solution.py:292
  43.4 2.3 %collective-permute-start.18 = (bf16[16,2560]{1,0:T(8,128)(2,1)S(1)}, bf16[16,2560]{1,0:T(8,128)(2,1)S(1)}, u32[]{:S(2)}, u32[]{:S(2)}) collective-permute-start(bf16[16,2560]{1,0:T(8,128)(2,1)S(1)} %join.6.refs_5_), channel_id=1, source_target_pairs={{0,1},{1,0},{2,3},{3,2},{4,5},{5,4},{6,7},{7,6},{8,9},{9,8},{10,11... | collective-permute-start | bytes 245768 | tf_op jit(solution)/shard_map/ppermute | solution.py:292
  43.4 3.8 %collective-permute-start.10 = (bf16[16,1536]{1,0:T(8,128)(2,1)S(1)}, bf16[16,1536]{1,0:T(8,128)(2,1)S(1)}, u32[]{:S(2)}, u32[]{:S(2)}) collective-permute-start(bf16[16,1536]{1,0:T(8,128)(2,1)S(1)} %combine.3.refs_1_.refs_0_), channel_id=1, source_target_pairs={{0,1},{1,0},{2,3},{3,2},{4,5},{5,4},{6,7},{7,6},{8,9},{9,8},{10,11... | collective-permute-start | bytes 147464 | tf_op jit(solution)/shard_map/ppermute | solution.py:292
  45.5 1.7 %collective-permute-start.16 = (bf16[16,1536]{1,0:T(8,128)(2,1)S(1)}, bf16[16,1536]{1,0:T(8,128)(2,1)S(1)}, u32[]{:S(2)}, u32[]{:S(2)}) collective-permute-start(bf16[16,1536]{1,0:T(8,128)(2,1)S(1)} %join.7.refs_6_), channel_id=1, source_target_pairs={{0,1},{1,0},{2,3},{3,2},{4,5},{5,4},{6,7},{7,6},{8,9},{9,8},{10,11... | collective-permute-start | bytes 147464 | tf_op jit(solution)/shard_map/ppermute | solution.py:292
  48.2 8.4 %collective-permute-start.19 = (bf16[16,2048]{1,0:T(8,128)(2,1)S(1)}, bf16[16,2048]{1,0:T(8,128)(2,1)S(1)}, u32[]{:S(2)}, u32[]{:S(2)}) collective-permute-start(bf16[16,2048]{1,0:T(8,128)(2,1)S(1)} %get-tuple-element.32), channel_id=1, source_target_pairs={{0,8},{4,12},{8,0},{12,4},{1,9},{5,13},{9,1},{13,5},{2,10},{6,14},... | collective-permute-start | bytes 196616 | tf_op jit(solution)/shard_map/ppermute | solution.py:292
  50.4 6.7 %collective-permute-start.20 = (bf16[16,2048]{1,0:T(8,128)(2,1)S(1)}, bf16[16,2048]{1,0:T(8,128)(2,1)S(1)}, u32[]{:S(2)}, u32[]{:S(2)}) collective-permute-start(bf16[16,2048]{1,0:T(8,128)(2,1)S(1)} %get-tuple-element.33), channel_id=1, source_target_pairs={{0,12},{4,8},{8,4},{12,0},{1,13},{5,9},{9,5},{13,1},{2,14},{6,10},... | collective-permute-start | bytes 196616 | tf_op jit(solution)/shard_map/ppermute | solution.py:292
  51.9 6.0 %collective-permute-start.21 = (bf16[16,2048]{1,0:T(8,128)(2,1)S(1)}, bf16[16,2048]{1,0:T(8,128)(2,1)S(1)}, u32[]{:S(2)}, u32[]{:S(2)}) collective-permute-start(bf16[16,2048]{1,0:T(8,128)(2,1)S(1)} %get-tuple-element.34), channel_id=1, source_target_pairs={{0,4},{4,0},{8,12},{12,8},{1,5},{5,1},{9,13},{13,9},{2,6},{6,2},{1... | collective-permute-start | bytes 196616 | tf_op jit(solution)/shard_map/ppermute | solution.py:292

commit v23 on v19

--- a/solution.py
+++ b/solution.py
@@ -165,58 +165,87 @@
     )(*arrays, *weights, *behind)
 
 
-def pair_sum_kernel(mine_ref, got_ref, *refs):
-    out_ref = refs[-1]
+def pair_sum_kernel(n_parts, *refs):
+    out_ref, at = refs[2 * n_parts], 0
     rows = out_ref.shape[1]
-    for k in range(2):
-        total = mine_ref[k, rows:].astype(jnp.float32) + got_ref[k, rows:].astype(jnp.float32)
-        out_ref[k] = total.astype(out_ref.dtype)
-
-
-def pair_sum(mine, got, behind):
-    _, rows, width = mine.shape
-    return pl.pallas_call(
-        pair_sum_kernel,
-        in_specs=[spec(pltpu.VMEM)] * 2 + [spec(pl.ANY)] * len(behind),
+    for mine_ref, got_ref in zip(refs[:n_parts], refs[n_parts : 2 * n_parts]):
+        width = got_ref.shape[2]
+        for k in range(2):
+            total = mine_ref[k, rows:].astype(jnp.float32) + got_ref[k, rows:].astype(jnp.float32)
+            out_ref[k, :, at : at + width] = total.astype(out_ref.dtype)
+        at += width
+
+
+def pair_sum(mines, gots, behind):
+    _, rows, _ = mines[0].shape
+    width = sum(x.shape[2] for x in gots)
+
+    def kernel(*refs):
+        inputs, rest = refs[: 2 * len(mines)], refs[2 * len(mines) + len(behind) :]
+        pair_sum_kernel(len(mines), *inputs, *rest)
+
+    return pl.pallas_call(
+        kernel,
+        in_specs=[spec(pltpu.VMEM)] * (2 * len(mines)) + [spec(pl.ANY)] * len(behind),
         out_specs=spec(pltpu.VMEM),
-        out_shape=jax.ShapeDtypeStruct((2, rows // 2, width), mine.dtype),
+        out_shape=jax.ShapeDtypeStruct((2, rows // 2, width), jnp.bfloat16),
         compiler_params=params(2),
         cost_estimate=COST,
         name="pair_sum",
-    )(mine, got, *behind)
-
-
-def combine_kernel(n_left, n_outs, mine_ref, got_ref, chip_ref, *refs):
-    outs = refs[-n_outs:]
-    rows, first = chip_ref.shape[1], 0
-    for left in refs[:n_left]:
-        first = left.shape[1]
-        outs[0][:, :first] = left[...]
-    for a, b in pieces_of(chip_ref.shape[2], TILE):
-        gate, up = (
-            mine_ref[k, :rows, a:b].astype(jnp.float32)
-            + got_ref[k, :rows, a:b].astype(jnp.float32)
-            + chip_ref[k, :, a:b].astype(jnp.float32)
-            for k in range(2)
-        )
-        hidden = (gate / (1 + jnp.exp(-gate)) * up).astype(jnp.bfloat16)
-        for i, out in enumerate(outs):
-            out[:, first + a : first + b] = hidden[i * ROWS : (i + 1) * ROWS]
-
-
-def combine(mine, got, from_chip, left, behind):
+    )(*mines, *gots, *behind)
+
+
+def later_kernel(array_ref, *refs):
+    refs[-1][...] = array_ref[...]
+
+
+def later(array, behind):
+    return pl.pallas_call(
+        later_kernel,
+        in_specs=[spec(pltpu.VMEM)] + [spec(pl.ANY)] * len(behind),
+        out_specs=spec(pltpu.VMEM),
+        out_shape=jax.ShapeDtypeStruct(array.shape, array.dtype),
+        compiler_params=params(1),
+        cost_estimate=COST,
+        name="later",
+    )(array, *behind)
+
+
+def combine_kernel(n_parts, n_left, n_outs, *refs):
+    mines, gots, chip_ref, refs = refs[:n_parts], refs[n_parts : 2 * n_parts], refs[2 * n_parts], refs[2 * n_parts + 1 :]
+    lefts, outs = refs[:n_left], refs[n_left:]
+    rows, at = chip_ref.shape[1], 0
+    for left in lefts:
+        outs[0][:, : left.shape[1]] = left[...]
+    first = sum(left.shape[1] for left in lefts)
+    for mine_ref, got_ref in zip(mines, gots):
+        for a, b in pieces_of(got_ref.shape[2], TILE):
+            gate, up = (
+                mine_ref[k, :rows, a:b].astype(jnp.float32)
+                + got_ref[k, :rows, a:b].astype(jnp.float32)
+                + chip_ref[k, :, at + a : at + b].astype(jnp.float32)
+                for k in range(2)
+            )
+            hidden = (gate / (1 + jnp.exp(-gate)) * up).astype(jnp.bfloat16)
+            for i, out in enumerate(outs):
+                out[:, first + at + a : first + at + b] = hidden[i * ROWS : (i + 1) * ROWS]
+        at += got_ref.shape[2]
+
+
+def combine(mines, gots, from_chip, left):
     _, rows, width = from_chip.shape
     n_outs = rows // ROWS
     width += sum(x.shape[1] for x in left)
-    return pl.pallas_call(
-        functools.partial(combine_kernel, len(left), n_outs),
-        in_specs=[spec(pltpu.VMEM)] * (3 + len(left)) + [spec(pl.ANY)] * len(behind),
+    args = [*mines, *gots, from_chip, *left]
+    return pl.pallas_call(
+        functools.partial(combine_kernel, len(mines), len(left), n_outs),
+        in_specs=[spec(pltpu.VMEM)] * len(args),
         out_specs=[spec(pltpu.VMEM)] * n_outs,
         out_shape=[jax.ShapeDtypeStruct((ROWS, width), jnp.bfloat16)] * n_outs,
         compiler_params=params(2),
         cost_estimate=COST,
         name="combine",
-    )(mine, got, from_chip, *left, *behind)
+    )(*args)
 
 
 def down_kernel(n_pieces, has_acc, last, segments, *refs):
@@ -289,18 +318,22 @@
     near = join(by_hid, [own, far_own])
     far = swap(near, "rep", 1)
 
-    weights = [w for fetched in early for w in fetched[:2]]
-    mine, theirs = gate_up([own, near, far_own, far], weights, [], [])
-    got = swap(theirs, "wid", 1)
-    to_chip = pair_sum(mine, got, [])
+    arrays = [own, near, far_own, far]
+    mine_0, theirs = gate_up(arrays, early[0][:2], [], [early[1][0]])
+    got_0 = swap(theirs, "wid", 1)
+    mine_1, theirs = gate_up(arrays, early[1][:2], [], [mine_0])
+    got_1 = swap(later(theirs, [got_0]), "wid", 1)
+    mines, gots = [mine_0, mine_1], [got_0, got_1]
+    to_chip = pair_sum(mines, gots, [])
     from_chip = swap(to_chip, "wid", 2)
     segments = [(bounds[2], widths[2]), (half + bounds[2], widths[2])]
-    last_mine, theirs = gate_up([own, near], [gate_weight, up_weight], segments, [to_chip])
+    last_mine, theirs = gate_up(arrays[:2], [gate_weight, up_weight], segments, [to_chip])
     last_got = swap(theirs, "wid", 1)
-    keep, give = combine(mine, got, from_chip, [], [])
-    last_to_chip = pair_sum(last_mine, last_got, [give])
+
+    keep, give = combine(mines, gots, from_chip, [])
+    last_to_chip = pair_sum([last_mine], [last_got], [give])
     last_from_chip = swap(last_to_chip, "wid", 2)
-    (rest,) = combine(last_mine, last_got, last_from_chip, [swap(give, "rep", 1)], [])
+    (rest,) = combine([last_mine], [last_got], last_from_chip, [swap(give, "rep", 1)])
 
     def gather(hidden, behind):
         other = swap(hidden, "wid", 2)

time: 57.8 us -> 58 us (level)
  waiting for transfers between devices: 14.4 us -> 13.7 us
  starting transfers between devices: 19.8 us -> 20.5 us
    ppermute x19 -> x20, waiting for transfers between devices: 14.4 us -> 13.7 us  [swap(): return lax.ppermute(x, axis, [(i, i ^ step) for i in range(n)])]
    ppermute x19 -> x20, starting transfers between devices: 19.8 us -> 20.5 us  [swap(): return lax.ppermute(x, axis, [(i, i ^ step) for i in range(n)])]
    pallas_call x2 -> x3, Pallas kernels: 9 us -> 9.22 us  [gate_up(): pl.pallas_call(functools.partial(gate_up_kernel, len(arrays), len(weights...]
  transfers between devices with their start and end apart: 19 -> 20, of which waited for: 10 -> 10; matrix products, arithmetic and copies ran while one was open for 0% -> 0% of each run, Pallas kernels for 30% -> 32%
where the time goes in v23:
time: 58 us; the launch traced here: 57.9 us
  Pallas kernels  22.7 us (39%)
  starting transfers between devices  20.5 us (35%)
  waiting for transfers between devices  13.7 us (24%)
  other arithmetic  0.67 us (1%)
    ppermute x20, starting transfers between devices, swap(): return lax.ppermute(x, axis, [(i, i ^ step) for i in range(n)])  20.5 us
    ppermute x20, waiting for transfers between devices, swap(): return lax.ppermute(x, axis, [(i, i ^ step) for i in range(n)])  13.7 us
    pallas_call x3, Pallas kernels, gate_up(): pl.pallas_call(functools.partial(gate_up_kernel, len(arrays), len(weights...  9.22 us
    pallas_call x2, Pallas kernels, fetch(): pl.pallas_call(functools.partial(fetch_kernel, first), in_specs=[spec(plt...  9.16 us
    pallas_call x2, Pallas kernels, down(): pl.pallas_call(functools.partial(down_kernel, len(pieces), prev is not No...  3.92 us
  transfers between devices with their start and end apart: 20, of which 10 were waited for; matrix products, arithmetic and copies ran while one was open for 0% of the time, Pallas kernels for 32%

profile of v23, /device:TPU:0, one launch (start us, length us, event | category | flops | bytes accessed | tf_op | source)
XLA Modules:
  0.0 57.9 jit_solution(9989600295883340750)
XLA Ops:
  0.0 5.0 %collective-permute-start.2 = (bf16[16,2048]{1,0:T(8,128)(2,1)}, bf16[16,2048]{1,0:T(8,128)(2,1)S(1)}, u32[]{:S(2)}, u32[]{:S(2)}) collective-permute-start(bf16[16,2048]{1,0:T(8,128)(2,1)} %tokens_ref.3), channel_id=1, source_target_pairs={{0,12},{4,8},{8,4},{12,0},{1,13},{5,9},{9,5},{13,1},{2,14},{6,10},... | collective-permute-start | bytes 196616 | tf_op jit(solution)/shard_map/ppermute | solution.py:304
  5.1 0.6 collective-permute-start
  5.6 1.7 %collective-permute-start.3 = (bf16[16,2048]{1,0:T(8,128)(2,1)}, bf16[16,2048]{1,0:T(8,128)(2,1)S(1)}, u32[]{:S(2)}, u32[]{:S(2)}) collective-permute-start(bf16[16,2048]{1,0:T(8,128)(2,1)} %tokens_ref.3), channel_id=1, source_target_pairs={{0,16},{16,0},{1,17},{17,1},{2,18},{18,2},{3,19},{19,3},{4,20},{20... | collective-permute-start | bytes 196616 | tf_op jit(solution)/shard_map/ppermute | solution.py:304
  7.4 4.3 %fetch.2 = (bf16[2048,1280]{1,0:T(8,128)(2,1)S(1)}, bf16[2048,1280]{1,0:T(8,128)(2,1)S(1)}, bf16[16,2048]{1,0:T(8,128)(2,1)S(1)}) custom-call(bf16[2048,6656]{1,0:T(8,128)(2,1)} %refs_2_.1, bf16[2048,6656]{1,0:T(8,128)(2,1)} %refs_3_.1, bf16[16,2048]{1,0:T(8,128)(2,1)} %tokens_ref.3), custom_call_target="tpu_custom_call" | custom-call | bytes 1024 | tf_op jit(solution)/shard_map/fetch/pallas_call | solution.py:78
  11.6 0.0 collective-permute-done.1.refs_1_
  11.7 0.0 collective-permute-done.refs_0_
  11.7 0.8 %collective-permute-start.4 = (bf16[48,2048]{1,0:T(8,128)(2,1)S(1)}, bf16[48,2048]{1,0:T(8,128)(2,1)S(1)}, u32[]{:S(2)}, u32[]{:S(2)}) collective-permute-start(bf16[48,2048]{1,0:T(8,128)(2,1)S(1)} %join.3.refs_1_), channel_id=1, source_target_pairs={{0,16},{16,0},{1,17},{17,1},{2,18},{18,2},{3,19},{19,3},{4,20},{20... | collective-permute-start | bytes 589832 | tf_op jit(solution)/shard_map/ppermute | solution.py:304
  12.5 4.9 %fetch.3 = (bf16[2048,1280]{1,0:T(8,128)(2,1)S(1)}, bf16[2048,1280]{1,0:T(8,128)(2,1)S(1)}, bf16[16,2048]{1,0:T(8,128)(2,1)}) custom-call(bf16[2048,6656]{1,0:T(8,128)(2,1)} %refs_2_.1, bf16[2048,6656]{1,0:T(8,128)(2,1)} %refs_3_.1, bf16[16,2048]{1,0:T(8,128)(2,1)} %tokens_ref.3), custom_call_target="tpu_custom_call" | custom-call | bytes 1024 | tf_op jit(solution)/shard_map/fetch/pallas_call | solution.py:78
  17.4 0.1 collective-permute-done.4.refs_3_
  17.4 1.6 %gate_up.3 = (bf16[2,64,1280]{2,1,0:T(8,128)(2,1)S(1)}, bf16[2,64,1280]{2,1,0:T(8,128)(2,1)S(1)}) custom-call(bf16[16,2048]{1,0:T(8,128)(2,1)S(1)} %get-tuple-element.22.refs_3_.refs_0_, bf16[48,2048]{1,0:T(8,128)(2,1)S(1)} %join.3.refs_1_, bf16[16,2048]{1,0:T(8,128)(2,1)S(1)} %collective-permute-done.3.refs_4_.refs_2_, ...), custom_call_target="tpu_custom_call" | custom-call | bytes 1024 | tf_op jit(solution)/shard_map/gate_up/pallas_call | solution.py:154
  19.0 0.1 collective-permute-start.5
  19.1 1.6 %gate_up.4 = (bf16[2,64,1280]{2,1,0:T(8,128)(2,1)S(1)}, bf16[2,64,1280]{2,1,0:T(8,128)(2,1)S(1)}) custom-call(bf16[16,2048]{1,0:T(8,128)(2,1)S(1)} %get-tuple-element.22.refs_3_.refs_0_, bf16[48,2048]{1,0:T(8,128)(2,1)S(1)} %join.3.refs_1_, bf16[16,2048]{1,0:T(8,128)(2,1)S(1)} %collective-permute-done.3.refs_4_.refs_2_, ...), custom_call_target="tpu_custom_call" | custom-call | bytes 1024 | tf_op jit(solution)/shard_map/gate_up/pallas_call | solution.py:154
  20.7 0.0 collective-permute-done.5.refs_0_.refs_2_
  20.7 0.5 collective-permute-start.6
  21.3 1.3 %collective-permute-done.6.refs_3_ = bf16[2,64,1280]{2,1,0:T(8,128)(2,1)S(1)} collective-permute-done((bf16[2,64,1280]{2,1,0:T(8,128)(2,1)S(1)}, bf16[2,64,1280]{2,1,0:T(8,128)(2,1)S(1)}, u32[]{:S(2)}, u32[]{:S(2)}) %collective-permute-start.6) | collective-permute-done | bytes 327712 | tf_op jit(solution)/shard_map/ppermute | solution.py:304
  22.5 0.1 pair_sum.2.refs_4_
  22.6 0.0 slice-start.1
  22.6 0.0 slice-start.3
  22.6 0.0 slice-start.4
  22.6 0.0 slice-start.6
  22.7 1.7 %collective-permute-start.8 = (bf16[2,32,2560]{2,1,0:T(8,128)(2,1)S(1)}, bf16[2,32,2560]{2,1,0:T(8,128)(2,1)S(1)}, u32[]{:S(2)}, u32[]{:S(2)}) collective-permute-start(bf16[2,32,2560]{2,1,0:T(8,128)(2,1)S(1)} %pair_sum.2.refs_4_), channel_id=1, source_target_pairs={{0,2},{1,3},{2,0},{3,1},{4,6},{5,7},{6,4},{7,5},{8,10},{9,11},{10,... | collective-permute-start | bytes 983048 | tf_op jit(solution)/shard_map/ppermute | solution.py:304
  24.4 6.1 %gate_up.5 = (bf16[2,32,1536]{2,1,0:T(8,128)(2,1)S(1)}, bf16[2,32,1536]{2,1,0:T(8,128)(2,1)S(1)}) custom-call(bf16[16,2048]{1,0:T(8,128)(2,1)S(1)} %get-tuple-element.22.refs_3_.refs_0_, bf16[48,2048]{1,0:T(8,128)(2,1)S(1)} %join.3.refs_1_, bf16[2048,6656]{1,0:T(8,128)(2,1)} %refs_2_.1, bf16[2048,6656]{1,0:T(8,128)(2,1)} %refs_3_.1, ...), custom_call_target="tpu_custom_call" | custom-call | bytes 1024 | tf_op jit(solution)/shard_map/gate_up/pallas_call | solution.py:154
  30.5 0.1 collective-permute-start.7
  30.6 2.1 %collective-permute-done.8.refs_4_ = bf16[2,32,2560]{2,1,0:T(8,128)(2,1)S(1)} collective-permute-done((bf16[2,32,2560]{2,1,0:T(8,128)(2,1)S(1)}, bf16[2,32,2560]{2,1,0:T(8,128)(2,1)S(1)}, u32[]{:S(2)}, u32[]{:S(2)}) %collective-permute-start.8) | collective-permute-done | bytes 327712 | tf_op jit(solution)/shard_map/ppermute | solution.py:304
  32.7 0.2 combine.2
  32.9 0.0 collective-permute-done.7.refs_1_
  33.0 1.7 %collective-permute-start.9 = (bf16[2,16,1536]{2,1,0:T(8,128)(2,1)S(1)}, bf16[2,16,1536]{2,1,0:T(8,128)(2,1)S(1)}, u32[]{:S(2)}, u32[]{:S(2)}) collective-permute-start(bf16[2,16,1536]{2,1,0:T(8,128)(2,1)S(1)} %pair_sum.3), channel_id=1, source_target_pairs={{0,2},{1,3},{2,0},{3,1},{4,6},{5,7},{6,4},{7,5},{8,10},{9,11},{10,... | collective-permute-start | bytes 294920 | tf_op jit(solution)/shard_map/ppermute | solution.py:304
  34.7 1.5 %collective-permute-start.10 = (bf16[16,2560]{1,0:T(8,128)(2,1)S(1)}, bf16[16,2560]{1,0:T(8,128)(2,1)S(1)}, u32[]{:S(2)}, u32[]{:S(2)}) collective-permute-start(bf16[16,2560]{1,0:T(8,128)(2,1)S(1)} %get-tuple-element.33.refs_2_), channel_id=1, source_target_pairs={{0,16},{16,0},{1,17},{17,1},{2,18},{18,2},{3,19},{19,3},{4,20},{20... | collective-permute-start | bytes 245768 | tf_op jit(solution)/shard_map/ppermute | solution.py:304
  36.2 0.5 collective-permute-start.13
  36.7 2.4 %collective-permute-done.10.refs_3_ = bf16[16,2560]{1,0:T(8,128)(2,1)S(1)} collective-permute-done((bf16[16,2560]{1,0:T(8,128)(2,1)S(1)}, bf16[16,2560]{1,0:T(8,128)(2,1)S(1)}, u32[]{:S(2)}, u32[]{:S(2)}) %collective-permute-start.10) | collective-permute-done | bytes 81952 | tf_op jit(solution)/shard_map/ppermute | solution.py:304
  39.1 0.1 combine.3.refs_1_.refs_0_
  39.2 1.1 %collective-permute-start.11 = (bf16[16,4096]{1,0:T(8,128)(2,1)S(1)}, bf16[16,4096]{1,0:T(8,128)(2,1)S(1)}, u32[]{:S(2)}, u32[]{:S(2)}) collective-permute-start(bf16[16,4096]{1,0:T(8,128)(2,1)S(1)} %combine.3.refs_1_.refs_0_), channel_id=1, source_target_pairs={{0,2},{1,3},{2,0},{3,1},{4,6},{5,7},{6,4},{7,5},{8,10},{9,11},{10,... | collective-permute-start | bytes 393224 | tf_op jit(solution)/shard_map/ppermute | solution.py:304
  40.3 0.0 collective-permute-start.14
  40.3 0.7 %collective-permute-done.13.refs_0_.refs_1_ = bf16[16,2560]{1,0:T(8,128)(2,1)S(1)} collective-permute-done((bf16[16,2560]{1,0:T(8,128)(2,1)S(1)}, bf16[16,2560]{1,0:T(8,128)(2,1)S(1)}, u32[]{:S(2)}, u32[]{:S(2)}) %collective-permute-start.13) | collective-permute-done | bytes 81952 | tf_op jit(solution)/shard_map/ppermute | solution.py:304
  41.1 0.0 collective-permute-start.15
  41.1 0.5 collective-permute-start.12
  41.6 0.0 collective-permute-done.14.refs_2_
  41.6 0.8 %collective-permute-done.15.refs_3_ = bf16[16,2560]{1,0:T(8,128)(2,1)S(1)} collective-permute-done((bf16[16,2560]{1,0:T(8,128)(2,1)S(1)}, bf16[16,2560]{1,0:T(8,128)(2,1)S(1)}, u32[]{:S(2)}, u32[]{:S(2)}) %collective-permute-start.15) | collective-permute-done | bytes 81952 | tf_op jit(solution)/shard_map/ppermute | solution.py:304
  42.4 1.5 %down.2.refs_1_.refs_5_ = f32[64,2048]{1,0:T(8,128)S(1)} custom-call(bf16[16,2560]{1,0:T(8,128)(2,1)S(1)} %get-tuple-element.34.refs_0_, bf16[16,2560]{1,0:T(8,128)(2,1)S(1)} %collective-permute-done.13.refs_0_.refs_1_, bf16[16,2560]{1,0:T(8,128)(2,1)S(1)} %collective-permute-done.14.refs_2_, bf16[16,2560]{1,0:T(8,128)(2,1)S(1)} %collective-permute-done.15.refs_3_, ...), custom_call_target="tpu_custom_call" | custom-call | bytes 1024 | tf_op jit(solution)/shard_map/down/pallas_call | solution.py:286
  44.0 0.3 collective-permute-done.11.refs_0_.refs_1_
  44.3 0.1 collective-permute-start.16
  44.3 1.3 %collective-permute-done.16.refs_3_ = bf16[16,4096]{1,0:T(8,128)(2,1)S(1)} collective-permute-done((bf16[16,4096]{1,0:T(8,128)(2,1)S(1)}, bf16[16,4096]{1,0:T(8,128)(2,1)S(1)}, u32[]{:S(2)}, u32[]{:S(2)}) %collective-permute-start.16) | collective-permute-done | bytes 131104 | tf_op jit(solution)/shard_map/ppermute | solution.py:304
  45.7 2.4 %down.3 = (bf16[16,2048]{1,0:T(8,128)(2,1)S(1)}, bf16[16,2048]{1,0:T(8,128)(2,1)S(1)}, bf16[16,2048]{1,0:T(8,128)(2,1)S(1)}, bf16[16,2048]{1,0:T(8,128)(2,1)S(1)}) custom-call(bf16[16,4096]{1,0:T(8,128)(2,1)S(1)} %combine.3.refs_1_.refs_0_, bf16[16,4096]{1,0:T(8,128)(2,1)S(1)} %collective-permute-done.11.refs_0_.refs_1_, ...), custom_call_target="tpu_custom_call" | custom-call | bytes 1024 | tf_op jit(solution)/shard_map/down/pallas_call | solution.py:286
  48.0 3.5 %collective-permute-start.17 = (bf16[16,2048]{1,0:T(8,128)(2,1)S(1)}, bf16[16,2048]{1,0:T(8,128)(2,1)S(1)}, u32[]{:S(2)}, u32[]{:S(2)}) collective-permute-start(bf16[16,2048]{1,0:T(8,128)(2,1)S(1)} %get-tuple-element.36), channel_id=1, source_target_pairs={{0,12},{4,8},{8,4},{12,0},{1,13},{5,9},{9,5},{13,1},{2,14},{6,10},... | collective-permute-start | bytes 196616 | tf_op jit(solution)/shard_map/ppermute | solution.py:304
  51.5 1.0 %collective-permute-start.19 = (bf16[16,2048]{1,0:T(8,128)(2,1)S(1)}, bf16[16,2048]{1,0:T(8,128)(2,1)S(1)}, u32[]{:S(2)}, u32[]{:S(2)}) collective-permute-start(bf16[16,2048]{1,0:T(8,128)(2,1)S(1)} %get-tuple-element.38), channel_id=1, source_target_pairs={{0,4},{4,0},{8,12},{12,8},{1,5},{5,1},{9,13},{13,9},{2,6},{6,2},{1... | collective-permute-start | bytes 196616 | tf_op jit(solution)/shard_map/ppermute | solution.py:304
  52.5 2.3 %collective-permute-done.17 = bf16[16,2048]{1,0:T(8,128)(2,1)S(1)} collective-permute-done((bf16[16,2048]{1,0:T(8,128)(2,1)S(1)}, bf16[16,2048]{1,0:T(8,128)(2,1)S(1)}, u32[]{:S(2)}, u32[]{:S(2)}) %collective-permute-start.17) | collective-permute-done | bytes 65568 | tf_op jit(solution)/shard_map/ppermute | solution.py:304
  54.8 2.4 %collective-permute-done.18 = bf16[16,2048]{1,0:T(8,128)(2,1)S(1)} collective-permute-done((bf16[16,2048]{1,0:T(8,128)(2,1)S(1)}, bf16[16,2048]{1,0:T(8,128)(2,1)S(1)}, u32[]{:S(2)}, u32[]{:S(2)}) %collective-permute-start.18) | collective-permute-done | bytes 65568 | tf_op jit(solution)/shard_map/ppermute | solution.py:304
  57.2 0.7 %add_convert_fusion = bf16[16,2048]{1,0:T(8,128)(2,1)} fusion(bf16[16,2048]{1,0:T(8,128)(2,1)S(1)} %collective-permute-done.19, bf16[16,2048]{1,0:T(8,128)(2,1)S(1)} %collective-permute-done.18, bf16[16,2048]{1,0:T(8,128)(2,1)S(1)} %collective-permute-done.17, bf16[16,2048]{1,0:T(8,128)(2,1)S(1)} %get-tuple-element.35), kind=kLoop, calls=%fused_computation | loop fusion | flops 262144 | bytes 327680 | tf_op jit(solution)/shard_map/convert_element_type | solution.py:349
  (23 shorter events, 0.1 us)
Async XLA Ops:
  0.0 11.6 %collective-permute-start.2 = (bf16[16,2048]{1,0:T(8,128)(2,1)}, bf16[16,2048]{1,0:T(8,128)(2,1)S(1)}, u32[]{:S(2)}, u32[]{:S(2)}) collective-permute-start(bf16[16,2048]{1,0:T(8,128)(2,1)} %tokens_ref.3), channel_id=1, source_target_pairs={{0,12},{4,8},{8,4},{12,0},{1,13},{5,9},{9,5},{13,1},{2,14},{6,10},... | collective-permute-start | bytes 196616 | tf_op jit(solution)/shard_map/ppermute | solution.py:304
  5.0 6.6 %collective-permute-start.1 = (bf16[16,2048]{1,0:T(8,128)(2,1)}, bf16[16,2048]{1,0:T(8,128)(2,1)S(1)}, u32[]{:S(2)}, u32[]{:S(2)}) collective-permute-start(bf16[16,2048]{1,0:T(8,128)(2,1)} %tokens_ref.3), channel_id=1, source_target_pairs={{0,8},{4,12},{8,0},{12,4},{1,9},{5,13},{9,1},{13,5},{2,10},{6,14},... | collective-permute-start | bytes 196616 | tf_op jit(solution)/shard_map/ppermute | solution.py:304
  5.1 6.6 %collective-permute-start = (bf16[16,2048]{1,0:T(8,128)(2,1)}, bf16[16,2048]{1,0:T(8,128)(2,1)S(1)}, u32[]{:S(2)}, u32[]{:S(2)}) collective-permute-start(bf16[16,2048]{1,0:T(8,128)(2,1)} %tokens_ref.3), channel_id=1, source_target_pairs={{0,4},{4,0},{8,12},{12,8},{1,5},{5,1},{9,13},{13,9},{2,6},{6,2},{1... | collective-permute-start | bytes 196616 | tf_op jit(solution)/shard_map/ppermute | solution.py:304
  5.6 6.0 %collective-permute-start.3 = (bf16[16,2048]{1,0:T(8,128)(2,1)}, bf16[16,2048]{1,0:T(8,128)(2,1)S(1)}, u32[]{:S(2)}, u32[]{:S(2)}) collective-permute-start(bf16[16,2048]{1,0:T(8,128)(2,1)} %tokens_ref.3), channel_id=1, source_target_pairs={{0,16},{16,0},{1,17},{17,1},{2,18},{18,2},{3,19},{19,3},{4,20},{20... | collective-permute-start | bytes 196616 | tf_op jit(solution)/shard_map/ppermute | solution.py:304
  11.7 5.7 %collective-permute-start.4 = (bf16[48,2048]{1,0:T(8,128)(2,1)S(1)}, bf16[48,2048]{1,0:T(8,128)(2,1)S(1)}, u32[]{:S(2)}, u32[]{:S(2)}) collective-permute-start(bf16[48,2048]{1,0:T(8,128)(2,1)S(1)} %join.3.refs_1_), channel_id=1, source_target_pairs={{0,16},{16,0},{1,17},{17,1},{2,18},{18,2},{3,19},{19,3},{4,20},{20... | collective-permute-start | bytes 589832 | tf_op jit(solution)/shard_map/ppermute | solution.py:304
  19.0 1.7 %collective-permute-start.5 = (bf16[2,64,1280]{2,1,0:T(8,128)(2,1)S(1)}, bf16[2,64,1280]{2,1,0:T(8,128)(2,1)S(1)}, u32[]{:S(2)}, u32[]{:S(2)}) collective-permute-start(bf16[2,64,1280]{2,1,0:T(8,128)(2,1)S(1)} %get-tuple-element.29), channel_id=1, source_target_pairs={{0,1},{1,0},{2,3},{3,2},{4,5},{5,4},{6,7},{7,6},{8,9},{9,8},{10,11... | collective-permute-start | bytes 983048 | tf_op jit(solution)/shard_map/ppermute | solution.py:304
  20.7 1.8 %collective-permute-start.6 = (bf16[2,64,1280]{2,1,0:T(8,128)(2,1)S(1)}, bf16[2,64,1280]{2,1,0:T(8,128)(2,1)S(1)}, u32[]{:S(2)}, u32[]{:S(2)}) collective-permute-start(bf16[2,64,1280]{2,1,0:T(8,128)(2,1)S(1)} %later.1), channel_id=1, source_target_pairs={{0,1},{1,0},{2,3},{3,2},{4,5},{5,4},{6,7},{7,6},{8,9},{9,8},{10,11... | collective-permute-start | bytes 983048 | tf_op jit(solution)/shard_map/ppermute | solution.py:304
  22.5 19.9 %slice-start = ((s8[27262976]{0:T(1024)(128)(4,1)}), s8[4194304]{0:T(1024)(128)(4,1)S(1)}, s32[]{:S(2)}) async-start(s8[27262976]{0:T(1024)(128)(4,1)} %bitcast), calls=%async_computation | async-start | bytes 8388608
  22.6 19.8 %slice-start.1 = ((s8[27262976]{0:T(1024)(128)(4,1)}), s8[4194304]{0:T(1024)(128)(4,1)S(1)}, s32[]{:S(2)}) async-start(s8[27262976]{0:T(1024)(128)(4,1)} %bitcast), calls=%async_computation.1 | async-start | bytes 8388608
  22.6 19.8 %slice-start.2 = ((s8[27262976]{0:T(1024)(128)(4,1)}), s8[4194304]{0:T(1024)(128)(4,1)S(1)}, s32[]{:S(2)}) async-start(s8[27262976]{0:T(1024)(128)(4,1)} %bitcast), calls=%async_computation.2 | async-start | bytes 8388608
  22.6 19.8 %slice-start.3 = ((s8[27262976]{0:T(1024)(128)(4,1)}), s8[4194304]{0:T(1024)(128)(4,1)S(1)}, s32[]{:S(2)}) async-start(s8[27262976]{0:T(1024)(128)(4,1)} %bitcast), calls=%async_computation.3 | async-start | bytes 8388608
  22.6 19.8 %slice-start.4 = ((s8[27262976]{0:T(1024)(128)(4,1)}), s8[4194304]{0:T(1024)(128)(4,1)S(1)}, s32[]{:S(2)}) async-start(s8[27262976]{0:T(1024)(128)(4,1)} %bitcast), calls=%async_computation.4 | async-start | bytes 8388608
  22.6 19.8 %slice-start.5 = ((s8[27262976]{0:T(1024)(128)(4,1)}), s8[4194304]{0:T(1024)(128)(4,1)S(1)}, s32[]{:S(2)}) async-start(s8[27262976]{0:T(1024)(128)(4,1)} %bitcast), calls=%async_computation.5 | async-start | bytes 8388608
  22.6 19.8 %slice-start.6 = ((s8[27262976]{0:T(1024)(128)(4,1)}), s8[2097152]{0:T(1024)(128)(4,1)S(1)}, s32[]{:S(2)}) async-start(s8[27262976]{0:T(1024)(128)(4,1)} %bitcast), calls=%async_computation.6 | async-start | bytes 4194304
  22.7 10.1 %collective-permute-start.8 = (bf16[2,32,2560]{2,1,0:T(8,128)(2,1)S(1)}, bf16[2,32,2560]{2,1,0:T(8,128)(2,1)S(1)}, u32[]{:S(2)}, u32[]{:S(2)}) collective-permute-start(bf16[2,32,2560]{2,1,0:T(8,128)(2,1)S(1)} %pair_sum.2.refs_4_), channel_id=1, source_target_pairs={{0,2},{1,3},{2,0},{3,1},{4,6},{5,7},{6,4},{7,5},{8,10},{9,11},{10,... | collective-permute-start | bytes 983048 | tf_op jit(solution)/shard_map/ppermute | solution.py:304
  30.5 2.4 %collective-permute-start.7 = (bf16[2,32,1536]{2,1,0:T(8,128)(2,1)S(1)}, bf16[2,32,1536]{2,1,0:T(8,128)(2,1)S(1)}, u32[]{:S(2)}, u32[]{:S(2)}) collective-permute-start(bf16[2,32,1536]{2,1,0:T(8,128)(2,1)S(1)} %get-tuple-element.32), channel_id=1, source_target_pairs={{0,1},{1,0},{2,3},{3,2},{4,5},{5,4},{6,7},{7,6},{8,9},{9,8},{10,11... | collective-permute-start | bytes 589832 | tf_op jit(solution)/shard_map/ppermute | solution.py:304
  33.0 6.2 %collective-permute-start.9 = (bf16[2,16,1536]{2,1,0:T(8,128)(2,1)S(1)}, bf16[2,16,1536]{2,1,0:T(8,128)(2,1)S(1)}, u32[]{:S(2)}, u32[]{:S(2)}) collective-permute-start(bf16[2,16,1536]{2,1,0:T(8,128)(2,1)S(1)} %pair_sum.3), channel_id=1, source_target_pairs={{0,2},{1,3},{2,0},{3,1},{4,6},{5,7},{6,4},{7,5},{8,10},{9,11},{10,... | collective-permute-start | bytes 294920 | tf_op jit(solution)/shard_map/ppermute | solution.py:304
  34.7 4.4 %collective-permute-start.10 = (bf16[16,2560]{1,0:T(8,128)(2,1)S(1)}, bf16[16,2560]{1,0:T(8,128)(2,1)S(1)}, u32[]{:S(2)}, u32[]{:S(2)}) collective-permute-start(bf16[16,2560]{1,0:T(8,128)(2,1)S(1)} %get-tuple-element.33.refs_2_), channel_id=1, source_target_pairs={{0,16},{16,0},{1,17},{17,1},{2,18},{18,2},{3,19},{19,3},{4,20},{20... | collective-permute-start | bytes 245768 | tf_op jit(solution)/shard_map/ppermute | solution.py:304
  36.2 4.9 %collective-permute-start.13 = (bf16[16,2560]{1,0:T(8,128)(2,1)S(1)}, bf16[16,2560]{1,0:T(8,128)(2,1)S(1)}, u32[]{:S(2)}, u32[]{:S(2)}) collective-permute-start(bf16[16,2560]{1,0:T(8,128)(2,1)S(1)} %get-tuple-element.34.refs_0_), channel_id=1, source_target_pairs={{0,2},{1,3},{2,0},{3,1},{4,6},{5,7},{6,4},{7,5},{8,10},{9,11},{10,... | collective-permute-start | bytes 245768 | tf_op jit(solution)/shard_map/ppermute | solution.py:304
  39.2 5.0 %collective-permute-start.11 = (bf16[16,4096]{1,0:T(8,128)(2,1)S(1)}, bf16[16,4096]{1,0:T(8,128)(2,1)S(1)}, u32[]{:S(2)}, u32[]{:S(2)}) collective-permute-start(bf16[16,4096]{1,0:T(8,128)(2,1)S(1)} %combine.3.refs_1_.refs_0_), channel_id=1, source_target_pairs={{0,2},{1,3},{2,0},{3,1},{4,6},{5,7},{6,4},{7,5},{8,10},{9,11},{10,... | collective-permute-start | bytes 393224 | tf_op jit(solution)/shard_map/ppermute | solution.py:304
  40.3 1.3 %collective-permute-start.14 = (bf16[16,2560]{1,0:T(8,128)(2,1)S(1)}, bf16[16,2560]{1,0:T(8,128)(2,1)S(1)}, u32[]{:S(2)}, u32[]{:S(2)}) collective-permute-start(bf16[16,2560]{1,0:T(8,128)(2,1)S(1)} %get-tuple-element.34.refs_0_), channel_id=1, source_target_pairs={{0,1},{1,0},{2,3},{3,2},{4,5},{5,4},{6,7},{7,6},{8,9},{9,8},{10,11... | collective-permute-start | bytes 245768 | tf_op jit(solution)/shard_map/ppermute | solution.py:304
  41.1 1.3 %collective-permute-start.15 = (bf16[16,2560]{1,0:T(8,128)(2,1)S(1)}, bf16[16,2560]{1,0:T(8,128)(2,1)S(1)}, u32[]{:S(2)}, u32[]{:S(2)}) collective-permute-start(bf16[16,2560]{1,0:T(8,128)(2,1)S(1)} %join.4), channel_id=1, source_target_pairs={{0,1},{1,0},{2,3},{3,2},{4,5},{5,4},{6,7},{7,6},{8,9},{9,8},{10,11... | collective-permute-start | bytes 245768 | tf_op jit(solution)/shard_map/ppermute | solution.py:304
  41.1 3.2 %collective-permute-start.12 = (bf16[16,4096]{1,0:T(8,128)(2,1)S(1)}, bf16[16,4096]{1,0:T(8,128)(2,1)S(1)}, u32[]{:S(2)}, u32[]{:S(2)}) collective-permute-start(bf16[16,4096]{1,0:T(8,128)(2,1)S(1)} %combine.3.refs_1_.refs_0_), channel_id=1, source_target_pairs={{0,1},{1,0},{2,3},{3,2},{4,5},{5,4},{6,7},{7,6},{8,9},{9,8},{10,11... | collective-permute-start | bytes 393224 | tf_op jit(solution)/shard_map/ppermute | solution.py:304
  44.3 1.4 %collective-permute-start.16 = (bf16[16,4096]{1,0:T(8,128)(2,1)S(1)}, bf16[16,4096]{1,0:T(8,128)(2,1)S(1)}, u32[]{:S(2)}, u32[]{:S(2)}) collective-permute-start(bf16[16,4096]{1,0:T(8,128)(2,1)S(1)} %join.5), channel_id=1, source_target_pairs={{0,1},{1,0},{2,3},{3,2},{4,5},{5,4},{6,7},{7,6},{8,9},{9,8},{10,11... | collective-permute-start | bytes 393224 | tf_op jit(solution)/shard_map/ppermute | solution.py:304
  48.0 6.8 %collective-permute-start.17 = (bf16[16,2048]{1,0:T(8,128)(2,1)S(1)}, bf16[16,2048]{1,0:T(8,128)(2,1)S(1)}, u32[]{:S(2)}, u32[]{:S(2)}) collective-permute-start(bf16[16,2048]{1,0:T(8,128)(2,1)S(1)} %get-tuple-element.36), channel_id=1, source_target_pairs={{0,12},{4,8},{8,4},{12,0},{1,13},{5,9},{9,5},{13,1},{2,14},{6,10},... | collective-permute-start | bytes 196616 | tf_op jit(solution)/shard_map/ppermute | solution.py:304
  51.5 5.7 %collective-permute-start.18 = (bf16[16,2048]{1,0:T(8,128)(2,1)S(1)}, bf16[16,2048]{1,0:T(8,128)(2,1)S(1)}, u32[]{:S(2)}, u32[]{:S(2)}) collective-permute-start(bf16[16,2048]{1,0:T(8,128)(2,1)S(1)} %get-tuple-element.37), channel_id=1, source_target_pairs={{0,8},{4,12},{8,0},{12,4},{1,9},{5,13},{9,1},{13,5},{2,10},{6,14},... | collective-permute-start | bytes 196616 | tf_op jit(solution)/shard_map/ppermute | solution.py:304
  51.5 5.7 %collective-permute-start.19 = (bf16[16,2048]{1,0:T(8,128)(2,1)S(1)}, bf16[16,2048]{1,0:T(8,128)(2,1)S(1)}, u32[]{:S(2)}, u32[]{:S(2)}) collective-permute-start(bf16[16,2048]{1,0:T(8,128)(2,1)S(1)} %get-tuple-element.38), channel_id=1, source_target_pairs={{0,4},{4,0},{8,12},{12,8},{1,5},{5,1},{9,13},{13,9},{2,6},{6,2},{1... | collective-permute-start | bytes 196616 | tf_op jit(solution)/shard_map/ppermute | solution.py:304

commit v24 on v23

--- a/solution.py
+++ b/solution.py
@@ -324,13 +324,13 @@
     mine_1, theirs = gate_up(arrays, early[1][:2], [], [mine_0])
     got_1 = swap(later(theirs, [got_0]), "wid", 1)
     mines, gots = [mine_0, mine_1], [got_0, got_1]
-    to_chip = pair_sum(mines, gots, [])
-    from_chip = swap(to_chip, "wid", 2)
+    to_chips = [pair_sum([mine], [got], []) for mine, got in zip(mines, gots)]
+    from_chips = [swap(x, "wid", 2) for x in to_chips]
     segments = [(bounds[2], widths[2]), (half + bounds[2], widths[2])]
-    last_mine, theirs = gate_up(arrays[:2], [gate_weight, up_weight], segments, [to_chip])
-    last_got = swap(theirs, "wid", 1)
-
-    keep, give = combine(mines, gots, from_chip, [])
+    last_mine, theirs = gate_up(arrays[:2], [gate_weight, up_weight], segments, to_chips)
+    last_got = swap(later(theirs, from_chips), "wid", 1)
+
+    keep, give = combine(mines, gots, jnp.concatenate(from_chips, 2), [])
     last_to_chip = pair_sum([last_mine], [last_got], [give])
     last_from_chip = swap(last_to_chip, "wid", 2)
     (rest,) = combine([last_mine], [last_got], last_from_chip, [swap(give, "rep", 1)])

time: 58 us -> 57.7 us (level)
  waiting for transfers between devices: 13.7 us -> 12.2 us
  starting transfers between devices: 20.5 us -> 21.7 us
    ppermute x20 -> x21, waiting for transfers between devices: 13.7 us -> 12.2 us  [swap(): return lax.ppermute(x, axis, [(i, i ^ step) for i in range(n)])]
    ppermute x20 -> x21, starting transfers between devices: 20.5 us -> 21.7 us  [swap(): return lax.ppermute(x, axis, [(i, i ^ step) for i in range(n)])]
  transfers between devices with their start and end apart: 20 -> 21, of which waited for: 10 -> 11; matrix products, arithmetic and copies ran while one was open for 0% -> 0% of each run, Pallas kernels for 32% -> 32%
where the time goes in v24:
time: 57.7 us; the launch traced here: 57.5 us
  Pallas kernels  22.6 us (39%)
  starting transfers between devices  21.7 us (38%)
  waiting for transfers between devices  12.2 us (21%)
  other arithmetic  0.69 us (1%)
    ppermute x21, starting transfers between devices, swap(): return lax.ppermute(x, axis, [(i, i ^ step) for i in range(n)])  21.7 us
    ppermute x21, waiting for transfers between devices, swap(): return lax.ppermute(x, axis, [(i, i ^ step) for i in range(n)])  12.2 us
    pallas_call x2, Pallas kernels, fetch(): pl.pallas_call(functools.partial(fetch_kernel, first), in_specs=[spec(plt...  9.16 us
    pallas_call x3, Pallas kernels, gate_up(): pl.pallas_call(functools.partial(gate_up_kernel, len(arrays), len(weights...  9.06 us
    pallas_call x2, Pallas kernels, down(): pl.pallas_call(functools.partial(down_kernel, len(pieces), prev is not No...  3.93 us
  transfers between devices with their start and end apart: 21, of which 11 were waited for; matrix products, arithmetic and copies ran while one was open for 0% of the time, Pallas kernels for 32%

profile of v24, /device:TPU:0, one launch (start us, length us, event | category | flops | bytes accessed | tf_op | source)
XLA Modules:
  0.0 57.5 jit_solution(3951017999020196348)
XLA Ops:
  0.0 5.0 %collective-permute-start.2 = (bf16[16,2048]{1,0:T(8,128)(2,1)}, bf16[16,2048]{1,0:T(8,128)(2,1)S(1)}, u32[]{:S(2)}, u32[]{:S(2)}) collective-permute-start(bf16[16,2048]{1,0:T(8,128)(2,1)} %tokens_ref.3), channel_id=1, source_target_pairs={{0,12},{4,8},{8,4},{12,0},{1,13},{5,9},{9,5},{13,1},{2,14},{6,10},... | collective-permute-start | bytes 196616 | tf_op jit(solution)/shard_map/ppermute | solution.py:304
  5.1 0.6 collective-permute-start
  5.6 1.7 %collective-permute-start.3 = (bf16[16,2048]{1,0:T(8,128)(2,1)}, bf16[16,2048]{1,0:T(8,128)(2,1)S(1)}, u32[]{:S(2)}, u32[]{:S(2)}) collective-permute-start(bf16[16,2048]{1,0:T(8,128)(2,1)} %tokens_ref.3), channel_id=1, source_target_pairs={{0,16},{16,0},{1,17},{17,1},{2,18},{18,2},{3,19},{19,3},{4,20},{20... | collective-permute-start | bytes 196616 | tf_op jit(solution)/shard_map/ppermute | solution.py:304
  7.4 4.3 %fetch.2 = (bf16[2048,1280]{1,0:T(8,128)(2,1)S(1)}, bf16[2048,1280]{1,0:T(8,128)(2,1)S(1)}, bf16[16,2048]{1,0:T(8,128)(2,1)S(1)}) custom-call(bf16[2048,6656]{1,0:T(8,128)(2,1)} %refs_2_.1, bf16[2048,6656]{1,0:T(8,128)(2,1)} %refs_3_.1, bf16[16,2048]{1,0:T(8,128)(2,1)} %tokens_ref.3), custom_call_target="tpu_custom_call" | custom-call | bytes 1024 | tf_op jit(solution)/shard_map/fetch/pallas_call | solution.py:78
  11.7 0.0 collective-permute-done.refs_0_
  11.7 0.8 %collective-permute-start.4 = (bf16[48,2048]{1,0:T(8,128)(2,1)S(1)}, bf16[48,2048]{1,0:T(8,128)(2,1)S(1)}, u32[]{:S(2)}, u32[]{:S(2)}) collective-permute-start(bf16[48,2048]{1,0:T(8,128)(2,1)S(1)} %join.3.refs_1_), channel_id=1, source_target_pairs={{0,16},{16,0},{1,17},{17,1},{2,18},{18,2},{3,19},{19,3},{4,20},{20... | collective-permute-start | bytes 589832 | tf_op jit(solution)/shard_map/ppermute | solution.py:304
  12.5 4.9 %fetch.3 = (bf16[2048,1280]{1,0:T(8,128)(2,1)S(1)}, bf16[2048,1280]{1,0:T(8,128)(2,1)S(1)}, bf16[16,2048]{1,0:T(8,128)(2,1)}) custom-call(bf16[2048,6656]{1,0:T(8,128)(2,1)} %refs_2_.1, bf16[2048,6656]{1,0:T(8,128)(2,1)} %refs_3_.1, bf16[16,2048]{1,0:T(8,128)(2,1)} %tokens_ref.3), custom_call_target="tpu_custom_call" | custom-call | bytes 1024 | tf_op jit(solution)/shard_map/fetch/pallas_call | solution.py:78
  17.4 0.1 collective-permute-done.4.refs_3_
  17.4 1.6 %gate_up.3 = (bf16[2,64,1280]{2,1,0:T(8,128)(2,1)S(1)}, bf16[2,64,1280]{2,1,0:T(8,128)(2,1)S(1)}) custom-call(bf16[16,2048]{1,0:T(8,128)(2,1)S(1)} %get-tuple-element.22.refs_3_.refs_0_, bf16[48,2048]{1,0:T(8,128)(2,1)S(1)} %join.3.refs_1_, bf16[16,2048]{1,0:T(8,128)(2,1)S(1)} %collective-permute-done.3.refs_4_.refs_2_, ...), custom_call_target="tpu_custom_call" | custom-call | bytes 1024 | tf_op jit(solution)/shard_map/gate_up/pallas_call | solution.py:154
  19.0 0.1 collective-permute-start.5
  19.1 1.6 %gate_up.4 = (bf16[2,64,1280]{2,1,0:T(8,128)(2,1)S(1)}, bf16[2,64,1280]{2,1,0:T(8,128)(2,1)S(1)}) custom-call(bf16[16,2048]{1,0:T(8,128)(2,1)S(1)} %get-tuple-element.22.refs_3_.refs_0_, bf16[48,2048]{1,0:T(8,128)(2,1)S(1)} %join.3.refs_1_, bf16[16,2048]{1,0:T(8,128)(2,1)S(1)} %collective-permute-done.3.refs_4_.refs_2_, ...), custom_call_target="tpu_custom_call" | custom-call | bytes 1024 | tf_op jit(solution)/shard_map/gate_up/pallas_call | solution.py:154
  20.7 0.0 collective-permute-done.5.refs_1_.refs_0_.refs_2_
  20.7 0.5 collective-permute-start.6
  21.3 1.7 %collective-permute-start.7 = (bf16[2,32,1280]{2,1,0:T(8,128)(2,1)S(1)}, bf16[2,32,1280]{2,1,0:T(8,128)(2,1)S(1)}, u32[]{:S(2)}, u32[]{:S(2)}) collective-permute-start(bf16[2,32,1280]{2,1,0:T(8,128)(2,1)S(1)} %pair_sum.3.refs_4_), channel_id=1, source_target_pairs={{0,2},{1,3},{2,0},{3,1},{4,6},{5,7},{6,4},{7,5},{8,10},{9,11},{10,... | collective-permute-start | bytes 491528 | tf_op jit(solution)/shard_map/ppermute | solution.py:304
  23.0 0.0 collective-permute-done.6.refs_1_.refs_3_
  23.1 0.0 slice-start.1
  23.1 0.0 slice-start.2
  23.1 0.0 slice-start.3
  23.1 0.0 slice-start.5
  23.1 0.0 slice-start.6
  23.1 1.2 %collective-permute-start.8 = (bf16[2,32,1280]{2,1,0:T(8,128)(2,1)S(1)}, bf16[2,32,1280]{2,1,0:T(8,128)(2,1)S(1)}, u32[]{:S(2)}, u32[]{:S(2)}) collective-permute-start(bf16[2,32,1280]{2,1,0:T(8,128)(2,1)S(1)} %pair_sum.4.refs_5_), channel_id=1, source_target_pairs={{0,2},{1,3},{2,0},{3,1},{4,6},{5,7},{6,4},{7,5},{8,10},{9,11},{10,... | collective-permute-start | bytes 491528 | tf_op jit(solution)/shard_map/ppermute | solution.py:304
  24.4 5.9 %gate_up.5 = (bf16[2,32,1536]{2,1,0:T(8,128)(2,1)S(1)}, bf16[2,32,1536]{2,1,0:T(8,128)(2,1)S(1)}) custom-call(bf16[16,2048]{1,0:T(8,128)(2,1)S(1)} %get-tuple-element.22.refs_3_.refs_0_, bf16[48,2048]{1,0:T(8,128)(2,1)S(1)} %join.3.refs_1_, bf16[2048,6656]{1,0:T(8,128)(2,1)} %refs_2_.1, bf16[2048,6656]{1,0:T(8,128)(2,1)} %refs_3_.1, ...), custom_call_target="tpu_custom_call" | custom-call | bytes 1024 | tf_op jit(solution)/shard_map/gate_up/pallas_call | solution.py:154
  30.3 0.0 collective-permute-done.7.refs_0_
  30.3 0.7 %collective-permute-done.8.refs_1_ = bf16[2,32,1280]{2,1,0:T(8,128)(2,1)S(1)} collective-permute-done((bf16[2,32,1280]{2,1,0:T(8,128)(2,1)S(1)}, bf16[2,32,1280]{2,1,0:T(8,128)(2,1)S(1)}, u32[]{:S(2)}, u32[]{:S(2)}) %collective-permute-start.8) | collective-permute-done | bytes 163872 | tf_op jit(solution)/shard_map/ppermute | solution.py:304
  31.0 0.1 collective-permute-start.9
  31.2 0.2 combine.2
  31.4 1.2 %collective-permute-done.9.refs_1_ = bf16[2,32,1536]{2,1,0:T(8,128)(2,1)S(1)} collective-permute-done((bf16[2,32,1536]{2,1,0:T(8,128)(2,1)S(1)}, bf16[2,32,1536]{2,1,0:T(8,128)(2,1)S(1)}, u32[]{:S(2)}, u32[]{:S(2)}) %collective-permute-start.9) | collective-permute-done | bytes 196640 | tf_op jit(solution)/shard_map/ppermute | solution.py:304
  32.6 1.7 %collective-permute-start.10 = (bf16[2,16,1536]{2,1,0:T(8,128)(2,1)S(1)}, bf16[2,16,1536]{2,1,0:T(8,128)(2,1)S(1)}, u32[]{:S(2)}, u32[]{:S(2)}) collective-permute-start(bf16[2,16,1536]{2,1,0:T(8,128)(2,1)S(1)} %pair_sum.5), channel_id=1, source_target_pairs={{0,2},{1,3},{2,0},{3,1},{4,6},{5,7},{6,4},{7,5},{8,10},{9,11},{10,... | collective-permute-start | bytes 294920 | tf_op jit(solution)/shard_map/ppermute | solution.py:304
  34.3 1.5 %collective-permute-start.11 = (bf16[16,2560]{1,0:T(8,128)(2,1)S(1)}, bf16[16,2560]{1,0:T(8,128)(2,1)S(1)}, u32[]{:S(2)}, u32[]{:S(2)}) collective-permute-start(bf16[16,2560]{1,0:T(8,128)(2,1)S(1)} %get-tuple-element.33.refs_2_), channel_id=1, source_target_pairs={{0,16},{16,0},{1,17},{17,1},{2,18},{18,2},{3,19},{19,3},{4,20},{20... | collective-permute-start | bytes 245768 | tf_op jit(solution)/shard_map/ppermute | solution.py:304
  35.8 0.5 collective-permute-start.14
  36.4 2.4 %collective-permute-done.11.refs_3_ = bf16[16,2560]{1,0:T(8,128)(2,1)S(1)} collective-permute-done((bf16[16,2560]{1,0:T(8,128)(2,1)S(1)}, bf16[16,2560]{1,0:T(8,128)(2,1)S(1)}, u32[]{:S(2)}, u32[]{:S(2)}) %collective-permute-start.11) | collective-permute-done | bytes 81952 | tf_op jit(solution)/shard_map/ppermute | solution.py:304
  38.7 0.1 combine.3.refs_1_.refs_0_
  38.8 1.1 %collective-permute-start.12 = (bf16[16,4096]{1,0:T(8,128)(2,1)S(1)}, bf16[16,4096]{1,0:T(8,128)(2,1)S(1)}, u32[]{:S(2)}, u32[]{:S(2)}) collective-permute-start(bf16[16,4096]{1,0:T(8,128)(2,1)S(1)} %combine.3.refs_1_.refs_0_), channel_id=1, source_target_pairs={{0,2},{1,3},{2,0},{3,1},{4,6},{5,7},{6,4},{7,5},{8,10},{9,11},{10,... | collective-permute-start | bytes 393224 | tf_op jit(solution)/shard_map/ppermute | solution.py:304
  39.9 0.3 collective-permute-done.14.refs_0_.refs_1_
  40.3 0.2 collective-permute-start.16
  40.5 0.3 collective-permute-start.13
  40.8 0.4 collective-permute-done.15.refs_2_
  41.2 0.3 collective-permute-done.16.refs_3_
  41.6 1.6 %down.2.refs_1_.refs_5_ = f32[64,2048]{1,0:T(8,128)S(1)} custom-call(bf16[16,2560]{1,0:T(8,128)(2,1)S(1)} %get-tuple-element.34.refs_0_, bf16[16,2560]{1,0:T(8,128)(2,1)S(1)} %collective-permute-done.14.refs_0_.refs_1_, bf16[16,2560]{1,0:T(8,128)(2,1)S(1)} %collective-permute-done.15.refs_2_, bf16[16,2560]{1,0:T(8,128)(2,1)S(1)} %collective-permute-done.16.refs_3_, ...), custom_call_target="tpu_custom_call" | custom-call | bytes 1024 | tf_op jit(solution)/shard_map/down/pallas_call | solution.py:286
  43.2 0.7 %collective-permute-done.12.refs_0_.refs_1_ = bf16[16,4096]{1,0:T(8,128)(2,1)S(1)} collective-permute-done((bf16[16,4096]{1,0:T(8,128)(2,1)S(1)}, bf16[16,4096]{1,0:T(8,128)(2,1)S(1)}, u32[]{:S(2)}, u32[]{:S(2)}) %collective-permute-start.12) | collective-permute-done | bytes 131104 | tf_op jit(solution)/shard_map/ppermute | solution.py:304
  43.9 0.1 collective-permute-start.17
  44.0 1.3 %collective-permute-done.17.refs_3_ = bf16[16,4096]{1,0:T(8,128)(2,1)S(1)} collective-permute-done((bf16[16,4096]{1,0:T(8,128)(2,1)S(1)}, bf16[16,4096]{1,0:T(8,128)(2,1)S(1)}, u32[]{:S(2)}, u32[]{:S(2)}) %collective-permute-start.17) | collective-permute-done | bytes 131104 | tf_op jit(solution)/shard_map/ppermute | solution.py:304
  45.3 2.4 %down.3 = (bf16[16,2048]{1,0:T(8,128)(2,1)S(1)}, bf16[16,2048]{1,0:T(8,128)(2,1)S(1)}, bf16[16,2048]{1,0:T(8,128)(2,1)S(1)}, bf16[16,2048]{1,0:T(8,128)(2,1)S(1)}) custom-call(bf16[16,4096]{1,0:T(8,128)(2,1)S(1)} %combine.3.refs_1_.refs_0_, bf16[16,4096]{1,0:T(8,128)(2,1)S(1)} %collective-permute-done.12.refs_0_.refs_1_, ...), custom_call_target="tpu_custom_call" | custom-call | bytes 1024 | tf_op jit(solution)/shard_map/down/pallas_call | solution.py:286
  47.7 3.5 %collective-permute-start.18 = (bf16[16,2048]{1,0:T(8,128)(2,1)S(1)}, bf16[16,2048]{1,0:T(8,128)(2,1)S(1)}, u32[]{:S(2)}, u32[]{:S(2)}) collective-permute-start(bf16[16,2048]{1,0:T(8,128)(2,1)S(1)} %get-tuple-element.36), channel_id=1, source_target_pairs={{0,12},{4,8},{8,4},{12,0},{1,13},{5,9},{9,5},{13,1},{2,14},{6,10},... | collective-permute-start | bytes 196616 | tf_op jit(solution)/shard_map/ppermute | solution.py:304
  51.2 1.0 %collective-permute-start.20 = (bf16[16,2048]{1,0:T(8,128)(2,1)S(1)}, bf16[16,2048]{1,0:T(8,128)(2,1)S(1)}, u32[]{:S(2)}, u32[]{:S(2)}) collective-permute-start(bf16[16,2048]{1,0:T(8,128)(2,1)S(1)} %get-tuple-element.38), channel_id=1, source_target_pairs={{0,4},{4,0},{8,12},{12,8},{1,5},{5,1},{9,13},{13,9},{2,6},{6,2},{1... | collective-permute-start | bytes 196616 | tf_op jit(solution)/shard_map/ppermute | solution.py:304
  52.1 2.3 %collective-permute-done.18 = bf16[16,2048]{1,0:T(8,128)(2,1)S(1)} collective-permute-done((bf16[16,2048]{1,0:T(8,128)(2,1)S(1)}, bf16[16,2048]{1,0:T(8,128)(2,1)S(1)}, u32[]{:S(2)}, u32[]{:S(2)}) %collective-permute-start.18) | collective-permute-done | bytes 65568 | tf_op jit(solution)/shard_map/ppermute | solution.py:304
  54.5 2.4 %collective-permute-done.19 = bf16[16,2048]{1,0:T(8,128)(2,1)S(1)} collective-permute-done((bf16[16,2048]{1,0:T(8,128)(2,1)S(1)}, bf16[16,2048]{1,0:T(8,128)(2,1)S(1)}, u32[]{:S(2)}, u32[]{:S(2)}) %collective-permute-start.19) | collective-permute-done | bytes 65568 | tf_op jit(solution)/shard_map/ppermute | solution.py:304
  56.9 0.7 %add_convert_fusion = bf16[16,2048]{1,0:T(8,128)(2,1)} fusion(bf16[16,2048]{1,0:T(8,128)(2,1)S(1)} %collective-permute-done.20, bf16[16,2048]{1,0:T(8,128)(2,1)S(1)} %collective-permute-done.19, bf16[16,2048]{1,0:T(8,128)(2,1)S(1)} %collective-permute-done.18, bf16[16,2048]{1,0:T(8,128)(2,1)S(1)} %get-tuple-element.35), kind=kLoop, calls=%fused_computation.1 | loop fusion | flops 262144 | bytes 327680 | tf_op jit(solution)/shard_map/convert_element_type | solution.py:349
  (28 shorter events, 0.2 us)
Async XLA Ops:
  0.0 11.6 %collective-permute-start.2 = (bf16[16,2048]{1,0:T(8,128)(2,1)}, bf16[16,2048]{1,0:T(8,128)(2,1)S(1)}, u32[]{:S(2)}, u32[]{:S(2)}) collective-permute-start(bf16[16,2048]{1,0:T(8,128)(2,1)} %tokens_ref.3), channel_id=1, source_target_pairs={{0,12},{4,8},{8,4},{12,0},{1,13},{5,9},{9,5},{13,1},{2,14},{6,10},... | collective-permute-start | bytes 196616 | tf_op jit(solution)/shard_map/ppermute | solution.py:304
  5.0 6.6 %collective-permute-start.1 = (bf16[16,2048]{1,0:T(8,128)(2,1)}, bf16[16,2048]{1,0:T(8,128)(2,1)S(1)}, u32[]{:S(2)}, u32[]{:S(2)}) collective-permute-start(bf16[16,2048]{1,0:T(8,128)(2,1)} %tokens_ref.3), channel_id=1, source_target_pairs={{0,8},{4,12},{8,0},{12,4},{1,9},{5,13},{9,1},{13,5},{2,10},{6,14},... | collective-permute-start | bytes 196616 | tf_op jit(solution)/shard_map/ppermute | solution.py:304
  5.1 6.6 %collective-permute-start = (bf16[16,2048]{1,0:T(8,128)(2,1)}, bf16[16,2048]{1,0:T(8,128)(2,1)S(1)}, u32[]{:S(2)}, u32[]{:S(2)}) collective-permute-start(bf16[16,2048]{1,0:T(8,128)(2,1)} %tokens_ref.3), channel_id=1, source_target_pairs={{0,4},{4,0},{8,12},{12,8},{1,5},{5,1},{9,13},{13,9},{2,6},{6,2},{1... | collective-permute-start | bytes 196616 | tf_op jit(solution)/shard_map/ppermute | solution.py:304
  5.6 6.0 %collective-permute-start.3 = (bf16[16,2048]{1,0:T(8,128)(2,1)}, bf16[16,2048]{1,0:T(8,128)(2,1)S(1)}, u32[]{:S(2)}, u32[]{:S(2)}) collective-permute-start(bf16[16,2048]{1,0:T(8,128)(2,1)} %tokens_ref.3), channel_id=1, source_target_pairs={{0,16},{16,0},{1,17},{17,1},{2,18},{18,2},{3,19},{19,3},{4,20},{20... | collective-permute-start | bytes 196616 | tf_op jit(solution)/shard_map/ppermute | solution.py:304
  11.7 5.7 %collective-permute-start.4 = (bf16[48,2048]{1,0:T(8,128)(2,1)S(1)}, bf16[48,2048]{1,0:T(8,128)(2,1)S(1)}, u32[]{:S(2)}, u32[]{:S(2)}) collective-permute-start(bf16[48,2048]{1,0:T(8,128)(2,1)S(1)} %join.3.refs_1_), channel_id=1, source_target_pairs={{0,16},{16,0},{1,17},{17,1},{2,18},{18,2},{3,19},{19,3},{4,20},{20... | collective-permute-start | bytes 589832 | tf_op jit(solution)/shard_map/ppermute | solution.py:304
  19.0 1.7 %collective-permute-start.5 = (bf16[2,64,1280]{2,1,0:T(8,128)(2,1)S(1)}, bf16[2,64,1280]{2,1,0:T(8,128)(2,1)S(1)}, u32[]{:S(2)}, u32[]{:S(2)}) collective-permute-start(bf16[2,64,1280]{2,1,0:T(8,128)(2,1)S(1)} %get-tuple-element.27), channel_id=1, source_target_pairs={{0,1},{1,0},{2,3},{3,2},{4,5},{5,4},{6,7},{7,6},{8,9},{9,8},{10,11... | collective-permute-start | bytes 983048 | tf_op jit(solution)/shard_map/ppermute | solution.py:304
  20.7 2.3 %collective-permute-start.6 = (bf16[2,64,1280]{2,1,0:T(8,128)(2,1)S(1)}, bf16[2,64,1280]{2,1,0:T(8,128)(2,1)S(1)}, u32[]{:S(2)}, u32[]{:S(2)}) collective-permute-start(bf16[2,64,1280]{2,1,0:T(8,128)(2,1)S(1)} %later.2), channel_id=1, source_target_pairs={{0,1},{1,0},{2,3},{3,2},{4,5},{5,4},{6,7},{7,6},{8,9},{9,8},{10,11... | collective-permute-start | bytes 983048 | tf_op jit(solution)/shard_map/ppermute | solution.py:304
  21.3 9.0 %collective-permute-start.7 = (bf16[2,32,1280]{2,1,0:T(8,128)(2,1)S(1)}, bf16[2,32,1280]{2,1,0:T(8,128)(2,1)S(1)}, u32[]{:S(2)}, u32[]{:S(2)}) collective-permute-start(bf16[2,32,1280]{2,1,0:T(8,128)(2,1)S(1)} %pair_sum.3.refs_4_), channel_id=1, source_target_pairs={{0,2},{1,3},{2,0},{3,1},{4,6},{5,7},{6,4},{7,5},{8,10},{9,11},{10,... | collective-permute-start | bytes 491528 | tf_op jit(solution)/shard_map/ppermute | solution.py:304
  23.0 18.5 %slice-start = ((s8[27262976]{0:T(1024)(128)(4,1)}), s8[4194304]{0:T(1024)(128)(4,1)S(1)}, s32[]{:S(2)}) async-start(s8[27262976]{0:T(1024)(128)(4,1)} %bitcast), calls=%async_computation | async-start | bytes 8388608
  23.1 18.5 %slice-start.1 = ((s8[27262976]{0:T(1024)(128)(4,1)}), s8[4194304]{0:T(1024)(128)(4,1)S(1)}, s32[]{:S(2)}) async-start(s8[27262976]{0:T(1024)(128)(4,1)} %bitcast), calls=%async_computation.1 | async-start | bytes 8388608
  23.1 18.5 %slice-start.2 = ((s8[27262976]{0:T(1024)(128)(4,1)}), s8[4194304]{0:T(1024)(128)(4,1)S(1)}, s32[]{:S(2)}) async-start(s8[27262976]{0:T(1024)(128)(4,1)} %bitcast), calls=%async_computation.2 | async-start | bytes 8388608
  23.1 18.5 %slice-start.3 = ((s8[27262976]{0:T(1024)(128)(4,1)}), s8[4194304]{0:T(1024)(128)(4,1)S(1)}, s32[]{:S(2)}) async-start(s8[27262976]{0:T(1024)(128)(4,1)} %bitcast), calls=%async_computation.3 | async-start | bytes 8388608
  23.1 18.5 %slice-start.4 = ((s8[27262976]{0:T(1024)(128)(4,1)}), s8[4194304]{0:T(1024)(128)(4,1)S(1)}, s32[]{:S(2)}) async-start(s8[27262976]{0:T(1024)(128)(4,1)} %bitcast), calls=%async_computation.4 | async-start | bytes 8388608
  23.1 18.5 %slice-start.5 = ((s8[27262976]{0:T(1024)(128)(4,1)}), s8[4194304]{0:T(1024)(128)(4,1)S(1)}, s32[]{:S(2)}) async-start(s8[27262976]{0:T(1024)(128)(4,1)} %bitcast), calls=%async_computation.5 | async-start | bytes 8388608
  23.1 18.5 %slice-start.6 = ((s8[27262976]{0:T(1024)(128)(4,1)}), s8[2097152]{0:T(1024)(128)(4,1)S(1)}, s32[]{:S(2)}) async-start(s8[27262976]{0:T(1024)(128)(4,1)} %bitcast), calls=%async_computation.6 | async-start | bytes 4194304
  23.1 7.9 %collective-permute-start.8 = (bf16[2,32,1280]{2,1,0:T(8,128)(2,1)S(1)}, bf16[2,32,1280]{2,1,0:T(8,128)(2,1)S(1)}, u32[]{:S(2)}, u32[]{:S(2)}) collective-permute-start(bf16[2,32,1280]{2,1,0:T(8,128)(2,1)S(1)} %pair_sum.4.refs_5_), channel_id=1, source_target_pairs={{0,2},{1,3},{2,0},{3,1},{4,6},{5,7},{6,4},{7,5},{8,10},{9,11},{10,... | collective-permute-start | bytes 491528 | tf_op jit(solution)/shard_map/ppermute | solution.py:304
  31.0 1.5 %collective-permute-start.9 = (bf16[2,32,1536]{2,1,0:T(8,128)(2,1)S(1)}, bf16[2,32,1536]{2,1,0:T(8,128)(2,1)S(1)}, u32[]{:S(2)}, u32[]{:S(2)}) collective-permute-start(bf16[2,32,1536]{2,1,0:T(8,128)(2,1)S(1)} %later.3), channel_id=1, source_target_pairs={{0,1},{1,0},{2,3},{3,2},{4,5},{5,4},{6,7},{7,6},{8,9},{9,8},{10,11... | collective-permute-start | bytes 589832 | tf_op jit(solution)/shard_map/ppermute | solution.py:304
  32.6 6.2 %collective-permute-start.10 = (bf16[2,16,1536]{2,1,0:T(8,128)(2,1)S(1)}, bf16[2,16,1536]{2,1,0:T(8,128)(2,1)S(1)}, u32[]{:S(2)}, u32[]{:S(2)}) collective-permute-start(bf16[2,16,1536]{2,1,0:T(8,128)(2,1)S(1)} %pair_sum.5), channel_id=1, source_target_pairs={{0,2},{1,3},{2,0},{3,1},{4,6},{5,7},{6,4},{7,5},{8,10},{9,11},{10,... | collective-permute-start | bytes 294920 | tf_op jit(solution)/shard_map/ppermute | solution.py:304
  34.3 4.4 %collective-permute-start.11 = (bf16[16,2560]{1,0:T(8,128)(2,1)S(1)}, bf16[16,2560]{1,0:T(8,128)(2,1)S(1)}, u32[]{:S(2)}, u32[]{:S(2)}) collective-permute-start(bf16[16,2560]{1,0:T(8,128)(2,1)S(1)} %get-tuple-element.33.refs_2_), channel_id=1, source_target_pairs={{0,16},{16,0},{1,17},{17,1},{2,18},{18,2},{3,19},{19,3},{4,20},{20... | collective-permute-start | bytes 245768 | tf_op jit(solution)/shard_map/ppermute | solution.py:304
  35.8 4.4 %collective-permute-start.14 = (bf16[16,2560]{1,0:T(8,128)(2,1)S(1)}, bf16[16,2560]{1,0:T(8,128)(2,1)S(1)}, u32[]{:S(2)}, u32[]{:S(2)}) collective-permute-start(bf16[16,2560]{1,0:T(8,128)(2,1)S(1)} %get-tuple-element.34.refs_0_), channel_id=1, source_target_pairs={{0,2},{1,3},{2,0},{3,1},{4,6},{5,7},{6,4},{7,5},{8,10},{9,11},{10,... | collective-permute-start | bytes 245768 | tf_op jit(solution)/shard_map/ppermute | solution.py:304
  38.8 5.0 %collective-permute-start.12 = (bf16[16,4096]{1,0:T(8,128)(2,1)S(1)}, bf16[16,4096]{1,0:T(8,128)(2,1)S(1)}, u32[]{:S(2)}, u32[]{:S(2)}) collective-permute-start(bf16[16,4096]{1,0:T(8,128)(2,1)S(1)} %combine.3.refs_1_.refs_0_), channel_id=1, source_target_pairs={{0,2},{1,3},{2,0},{3,1},{4,6},{5,7},{6,4},{7,5},{8,10},{9,11},{10,... | collective-permute-start | bytes 393224 | tf_op jit(solution)/shard_map/ppermute | solution.py:304
  39.9 1.3 %collective-permute-start.15 = (bf16[16,2560]{1,0:T(8,128)(2,1)S(1)}, bf16[16,2560]{1,0:T(8,128)(2,1)S(1)}, u32[]{:S(2)}, u32[]{:S(2)}) collective-permute-start(bf16[16,2560]{1,0:T(8,128)(2,1)S(1)} %get-tuple-element.34.refs_0_), channel_id=1, source_target_pairs={{0,1},{1,0},{2,3},{3,2},{4,5},{5,4},{6,7},{7,6},{8,9},{9,8},{10,11... | collective-permute-start | bytes 245768 | tf_op jit(solution)/shard_map/ppermute | solution.py:304
  40.3 1.3 %collective-permute-start.16 = (bf16[16,2560]{1,0:T(8,128)(2,1)S(1)}, bf16[16,2560]{1,0:T(8,128)(2,1)S(1)}, u32[]{:S(2)}, u32[]{:S(2)}) collective-permute-start(bf16[16,2560]{1,0:T(8,128)(2,1)S(1)} %join.4), channel_id=1, source_target_pairs={{0,1},{1,0},{2,3},{3,2},{4,5},{5,4},{6,7},{7,6},{8,9},{9,8},{10,11... | collective-permute-start | bytes 245768 | tf_op jit(solution)/shard_map/ppermute | solution.py:304
  40.5 3.4 %collective-permute-start.13 = (bf16[16,4096]{1,0:T(8,128)(2,1)S(1)}, bf16[16,4096]{1,0:T(8,128)(2,1)S(1)}, u32[]{:S(2)}, u32[]{:S(2)}) collective-permute-start(bf16[16,4096]{1,0:T(8,128)(2,1)S(1)} %combine.3.refs_1_.refs_0_), channel_id=1, source_target_pairs={{0,1},{1,0},{2,3},{3,2},{4,5},{5,4},{6,7},{7,6},{8,9},{9,8},{10,11... | collective-permute-start | bytes 393224 | tf_op jit(solution)/shard_map/ppermute | solution.py:304
  43.9 1.4 %collective-permute-start.17 = (bf16[16,4096]{1,0:T(8,128)(2,1)S(1)}, bf16[16,4096]{1,0:T(8,128)(2,1)S(1)}, u32[]{:S(2)}, u32[]{:S(2)}) collective-permute-start(bf16[16,4096]{1,0:T(8,128)(2,1)S(1)} %join.5), channel_id=1, source_target_pairs={{0,1},{1,0},{2,3},{3,2},{4,5},{5,4},{6,7},{7,6},{8,9},{9,8},{10,11... | collective-permute-start | bytes 393224 | tf_op jit(solution)/shard_map/ppermute | solution.py:304
  47.7 6.8 %collective-permute-start.18 = (bf16[16,2048]{1,0:T(8,128)(2,1)S(1)}, bf16[16,2048]{1,0:T(8,128)(2,1)S(1)}, u32[]{:S(2)}, u32[]{:S(2)}) collective-permute-start(bf16[16,2048]{1,0:T(8,128)(2,1)S(1)} %get-tuple-element.36), channel_id=1, source_target_pairs={{0,12},{4,8},{8,4},{12,0},{1,13},{5,9},{9,5},{13,1},{2,14},{6,10},... | collective-permute-start | bytes 196616 | tf_op jit(solution)/shard_map/ppermute | solution.py:304
  51.2 5.7 %collective-permute-start.19 = (bf16[16,2048]{1,0:T(8,128)(2,1)S(1)}, bf16[16,2048]{1,0:T(8,128)(2,1)S(1)}, u32[]{:S(2)}, u32[]{:S(2)}) collective-permute-start(bf16[16,2048]{1,0:T(8,128)(2,1)S(1)} %get-tuple-element.37), channel_id=1, source_target_pairs={{0,8},{4,12},{8,0},{12,4},{1,9},{5,13},{9,1},{13,5},{2,10},{6,14},... | collective-permute-start | bytes 196616 | tf_op jit(solution)/shard_map/ppermute | solution.py:304
  51.2 5.7 %collective-permute-start.20 = (bf16[16,2048]{1,0:T(8,128)(2,1)S(1)}, bf16[16,2048]{1,0:T(8,128)(2,1)S(1)}, u32[]{:S(2)}, u32[]{:S(2)}) collective-permute-start(bf16[16,2048]{1,0:T(8,128)(2,1)S(1)} %get-tuple-element.38), channel_id=1, source_target_pairs={{0,4},{4,0},{8,12},{12,8},{1,5},{5,1},{9,13},{13,9},{2,6},{6,2},{1... | collective-permute-start | bytes 196616 | tf_op jit(solution)/shard_map/ppermute | solution.py:304

commit v25 on v24

--- a/solution.py
+++ b/solution.py
@@ -328,7 +328,7 @@
     from_chips = [swap(x, "wid", 2) for x in to_chips]
     segments = [(bounds[2], widths[2]), (half + bounds[2], widths[2])]
     last_mine, theirs = gate_up(arrays[:2], [gate_weight, up_weight], segments, to_chips)
-    last_got = swap(later(theirs, from_chips), "wid", 1)
+    last_got = swap(later(theirs, from_chips[:1]), "wid", 1)
 
     keep, give = combine(mines, gots, jnp.concatenate(from_chips, 2), [])
     last_to_chip = pair_sum([last_mine], [last_got], [give])

time: 57.7 us -> 56.4 us (0.977)
  waiting for transfers between devices: 12.2 us -> 11.2 us
    ppermute x21, waiting for transfers between devices: 12.2 us -> 11.2 us  [swap(): return lax.ppermute(x, axis, [(i, i ^ step) for i in range(n)])]
  transfers between devices with their start and end apart: 21 -> 21, of which waited for: 11 -> 11; matrix products, arithmetic and copies ran while one was open for 0% -> 0% of each run, Pallas kernels for 32% -> 33%
where the time goes in v25:
time: 56.4 us; the launch traced here: 56.3 us
  Pallas kernels  22.6 us (40%)
  starting transfers between devices  21.6 us (38%)
  waiting for transfers between devices  11.2 us (20%)
  other arithmetic  0.69 us (1%)
    ppermute x21, starting transfers between devices, swap(): return lax.ppermute(x, axis, [(i, i ^ step) for i in range(n)])  21.6 us
    ppermute x21, waiting for transfers between devices, swap(): return lax.ppermute(x, axis, [(i, i ^ step) for i in range(n)])  11.2 us
    pallas_call x2, Pallas kernels, fetch(): pl.pallas_call(functools.partial(fetch_kernel, first), in_specs=[spec(plt...  9.16 us
    pallas_call x3, Pallas kernels, gate_up(): pl.pallas_call(functools.partial(gate_up_kernel, len(arrays), len(weights...  9.06 us
    pallas_call x2, Pallas kernels, down(): pl.pallas_call(functools.partial(down_kernel, len(pieces), prev is not No...  3.92 us
  transfers between devices with their start and end apart: 21, of which 11 were waited for; matrix products, arithmetic and copies ran while one was open for 0% of the time, Pallas kernels for 33%

profile of v25, /device:TPU:0, one launch (start us, length us, event | category | flops | bytes accessed | tf_op | source)
XLA Modules:
  0.0 56.3 jit_solution(18302345583960898517)
XLA Ops:
  0.0 5.0 %collective-permute-start.2 = (bf16[16,2048]{1,0:T(8,128)(2,1)}, bf16[16,2048]{1,0:T(8,128)(2,1)S(1)}, u32[]{:S(2)}, u32[]{:S(2)}) collective-permute-start(bf16[16,2048]{1,0:T(8,128)(2,1)} %tokens_ref.3), channel_id=1, source_target_pairs={{0,12},{4,8},{8,4},{12,0},{1,13},{5,9},{9,5},{13,1},{2,14},{6,10},... | collective-permute-start | bytes 196616 | tf_op jit(solution)/shard_map/ppermute | solution.py:304
  5.1 0.6 %collective-permute-start = (bf16[16,2048]{1,0:T(8,128)(2,1)}, bf16[16,2048]{1,0:T(8,128)(2,1)S(1)}, u32[]{:S(2)}, u32[]{:S(2)}) collective-permute-start(bf16[16,2048]{1,0:T(8,128)(2,1)} %tokens_ref.3), channel_id=1, source_target_pairs={{0,4},{4,0},{8,12},{12,8},{1,5},{5,1},{9,13},{13,9},{2,6},{6,2},{1... | collective-permute-start | bytes 196616 | tf_op jit(solution)/shard_map/ppermute | solution.py:304
  5.6 1.7 %collective-permute-start.3 = (bf16[16,2048]{1,0:T(8,128)(2,1)}, bf16[16,2048]{1,0:T(8,128)(2,1)S(1)}, u32[]{:S(2)}, u32[]{:S(2)}) collective-permute-start(bf16[16,2048]{1,0:T(8,128)(2,1)} %tokens_ref.3), channel_id=1, source_target_pairs={{0,16},{16,0},{1,17},{17,1},{2,18},{18,2},{3,19},{19,3},{4,20},{20... | collective-permute-start | bytes 196616 | tf_op jit(solution)/shard_map/ppermute | solution.py:304
  7.4 4.3 %fetch.2 = (bf16[2048,1280]{1,0:T(8,128)(2,1)S(1)}, bf16[2048,1280]{1,0:T(8,128)(2,1)S(1)}, bf16[16,2048]{1,0:T(8,128)(2,1)S(1)}) custom-call(bf16[2048,6656]{1,0:T(8,128)(2,1)} %refs_2_.1, bf16[2048,6656]{1,0:T(8,128)(2,1)} %refs_3_.1, bf16[16,2048]{1,0:T(8,128)(2,1)} %tokens_ref.3), custom_call_target="tpu_custom_call" | custom-call | bytes 1024 | tf_op jit(solution)/shard_map/fetch/pallas_call | solution.py:78
  11.6 0.0 collective-permute-done.1.refs_1_
  11.7 0.0 collective-permute-done.refs_0_
  11.7 0.8 %collective-permute-start.4 = (bf16[48,2048]{1,0:T(8,128)(2,1)S(1)}, bf16[48,2048]{1,0:T(8,128)(2,1)S(1)}, u32[]{:S(2)}, u32[]{:S(2)}) collective-permute-start(bf16[48,2048]{1,0:T(8,128)(2,1)S(1)} %join.3.refs_1_), channel_id=1, source_target_pairs={{0,16},{16,0},{1,17},{17,1},{2,18},{18,2},{3,19},{19,3},{4,20},{20... | collective-permute-start | bytes 589832 | tf_op jit(solution)/shard_map/ppermute | solution.py:304
  12.5 4.9 %fetch.3 = (bf16[2048,1280]{1,0:T(8,128)(2,1)S(1)}, bf16[2048,1280]{1,0:T(8,128)(2,1)S(1)}, bf16[16,2048]{1,0:T(8,128)(2,1)}) custom-call(bf16[2048,6656]{1,0:T(8,128)(2,1)} %refs_2_.1, bf16[2048,6656]{1,0:T(8,128)(2,1)} %refs_3_.1, bf16[16,2048]{1,0:T(8,128)(2,1)} %tokens_ref.3), custom_call_target="tpu_custom_call" | custom-call | bytes 1024 | tf_op jit(solution)/shard_map/fetch/pallas_call | solution.py:78
  17.4 0.1 collective-permute-done.4.refs_3_
  17.4 1.6 %gate_up.3 = (bf16[2,64,1280]{2,1,0:T(8,128)(2,1)S(1)}, bf16[2,64,1280]{2,1,0:T(8,128)(2,1)S(1)}) custom-call(bf16[16,2048]{1,0:T(8,128)(2,1)S(1)} %get-tuple-element.22.refs_3_.refs_0_, bf16[48,2048]{1,0:T(8,128)(2,1)S(1)} %join.3.refs_1_, bf16[16,2048]{1,0:T(8,128)(2,1)S(1)} %collective-permute-done.3.refs_4_.refs_2_, ...), custom_call_target="tpu_custom_call" | custom-call | bytes 1024 | tf_op jit(solution)/shard_map/gate_up/pallas_call | solution.py:154
  19.0 0.1 collective-permute-start.5
  19.1 1.6 %gate_up.4 = (bf16[2,64,1280]{2,1,0:T(8,128)(2,1)S(1)}, bf16[2,64,1280]{2,1,0:T(8,128)(2,1)S(1)}) custom-call(bf16[16,2048]{1,0:T(8,128)(2,1)S(1)} %get-tuple-element.22.refs_3_.refs_0_, bf16[48,2048]{1,0:T(8,128)(2,1)S(1)} %join.3.refs_1_, bf16[16,2048]{1,0:T(8,128)(2,1)S(1)} %collective-permute-done.3.refs_4_.refs_2_, ...), custom_call_target="tpu_custom_call" | custom-call | bytes 1024 | tf_op jit(solution)/shard_map/gate_up/pallas_call | solution.py:154
  20.7 0.0 collective-permute-done.5.refs_1_.refs_0_.refs_2_
  20.7 0.5 collective-permute-start.6
  21.3 1.7 %collective-permute-start.7 = (bf16[2,32,1280]{2,1,0:T(8,128)(2,1)S(1)}, bf16[2,32,1280]{2,1,0:T(8,128)(2,1)S(1)}, u32[]{:S(2)}, u32[]{:S(2)}) collective-permute-start(bf16[2,32,1280]{2,1,0:T(8,128)(2,1)S(1)} %pair_sum.3.refs_4_), channel_id=1, source_target_pairs={{0,2},{1,3},{2,0},{3,1},{4,6},{5,7},{6,4},{7,5},{8,10},{9,11},{10,... | collective-permute-start | bytes 491528 | tf_op jit(solution)/shard_map/ppermute | solution.py:304
  23.1 0.0 slice-start.1
  23.1 0.0 slice-start.2
  23.1 0.0 slice-start.4
  23.1 0.0 slice-start.5
  23.1 1.2 %collective-permute-start.9 = (bf16[2,32,1280]{2,1,0:T(8,128)(2,1)S(1)}, bf16[2,32,1280]{2,1,0:T(8,128)(2,1)S(1)}, u32[]{:S(2)}, u32[]{:S(2)}) collective-permute-start(bf16[2,32,1280]{2,1,0:T(8,128)(2,1)S(1)} %pair_sum.4.refs_5_), channel_id=1, source_target_pairs={{0,2},{1,3},{2,0},{3,1},{4,6},{5,7},{6,4},{7,5},{8,10},{9,11},{10,... | collective-permute-start | bytes 491528 | tf_op jit(solution)/shard_map/ppermute | solution.py:304
  24.4 5.9 %gate_up.5 = (bf16[2,32,1536]{2,1,0:T(8,128)(2,1)S(1)}, bf16[2,32,1536]{2,1,0:T(8,128)(2,1)S(1)}) custom-call(bf16[16,2048]{1,0:T(8,128)(2,1)S(1)} %get-tuple-element.22.refs_3_.refs_0_, bf16[48,2048]{1,0:T(8,128)(2,1)S(1)} %join.3.refs_1_, bf16[2048,6656]{1,0:T(8,128)(2,1)} %refs_2_.1, bf16[2048,6656]{1,0:T(8,128)(2,1)} %refs_3_.1, ...), custom_call_target="tpu_custom_call" | custom-call | bytes 1024 | tf_op jit(solution)/shard_map/gate_up/pallas_call | solution.py:154
  30.3 0.2 collective-permute-start.8
  30.6 0.5 collective-permute-done.9
  31.1 0.2 combine.2
  31.3 0.6 %collective-permute-done.8.refs_1_ = bf16[2,32,1536]{2,1,0:T(8,128)(2,1)S(1)} collective-permute-done((bf16[2,32,1536]{2,1,0:T(8,128)(2,1)S(1)}, bf16[2,32,1536]{2,1,0:T(8,128)(2,1)S(1)}, u32[]{:S(2)}, u32[]{:S(2)}) %collective-permute-start.8) | collective-permute-done | bytes 196640 | tf_op jit(solution)/shard_map/ppermute | solution.py:304
  31.9 1.2 %collective-permute-start.10 = (bf16[2,16,1536]{2,1,0:T(8,128)(2,1)S(1)}, bf16[2,16,1536]{2,1,0:T(8,128)(2,1)S(1)}, u32[]{:S(2)}, u32[]{:S(2)}) collective-permute-start(bf16[2,16,1536]{2,1,0:T(8,128)(2,1)S(1)} %pair_sum.5), channel_id=1, source_target_pairs={{0,2},{1,3},{2,0},{3,1},{4,6},{5,7},{6,4},{7,5},{8,10},{9,11},{10,... | collective-permute-start | bytes 294920 | tf_op jit(solution)/shard_map/ppermute | solution.py:304
  33.0 1.5 %collective-permute-start.11 = (bf16[16,2560]{1,0:T(8,128)(2,1)S(1)}, bf16[16,2560]{1,0:T(8,128)(2,1)S(1)}, u32[]{:S(2)}, u32[]{:S(2)}) collective-permute-start(bf16[16,2560]{1,0:T(8,128)(2,1)S(1)} %get-tuple-element.33.refs_2_), channel_id=1, source_target_pairs={{0,16},{16,0},{1,17},{17,1},{2,18},{18,2},{3,19},{19,3},{4,20},{20... | collective-permute-start | bytes 245768 | tf_op jit(solution)/shard_map/ppermute | solution.py:304
  34.5 0.9 %collective-permute-start.14 = (bf16[16,2560]{1,0:T(8,128)(2,1)S(1)}, bf16[16,2560]{1,0:T(8,128)(2,1)S(1)}, u32[]{:S(2)}, u32[]{:S(2)}) collective-permute-start(bf16[16,2560]{1,0:T(8,128)(2,1)S(1)} %get-tuple-element.34.refs_0_), channel_id=1, source_target_pairs={{0,2},{1,3},{2,0},{3,1},{4,6},{5,7},{6,4},{7,5},{8,10},{9,11},{10,... | collective-permute-start | bytes 245768 | tf_op jit(solution)/shard_map/ppermute | solution.py:304
  35.5 2.0 %collective-permute-done.11.refs_3_ = bf16[16,2560]{1,0:T(8,128)(2,1)S(1)} collective-permute-done((bf16[16,2560]{1,0:T(8,128)(2,1)S(1)}, bf16[16,2560]{1,0:T(8,128)(2,1)S(1)}, u32[]{:S(2)}, u32[]{:S(2)}) %collective-permute-start.11) | collective-permute-done | bytes 81952 | tf_op jit(solution)/shard_map/ppermute | solution.py:304
  37.5 0.0 collective-permute-done.10.refs_2_
  37.5 0.1 combine.3.refs_1_.refs_0_
  37.5 1.0 %collective-permute-start.12 = (bf16[16,4096]{1,0:T(8,128)(2,1)S(1)}, bf16[16,4096]{1,0:T(8,128)(2,1)S(1)}, u32[]{:S(2)}, u32[]{:S(2)}) collective-permute-start(bf16[16,4096]{1,0:T(8,128)(2,1)S(1)} %combine.3.refs_1_.refs_0_), channel_id=1, source_target_pairs={{0,2},{1,3},{2,0},{3,1},{4,6},{5,7},{6,4},{7,5},{8,10},{9,11},{10,... | collective-permute-start | bytes 393224 | tf_op jit(solution)/shard_map/ppermute | solution.py:304
  38.5 0.6 %collective-permute-done.14.refs_0_.refs_1_ = bf16[16,2560]{1,0:T(8,128)(2,1)S(1)} collective-permute-done((bf16[16,2560]{1,0:T(8,128)(2,1)S(1)}, bf16[16,2560]{1,0:T(8,128)(2,1)S(1)}, u32[]{:S(2)}, u32[]{:S(2)}) %collective-permute-start.14) | collective-permute-done | bytes 81952 | tf_op jit(solution)/shard_map/ppermute | solution.py:304
  39.1 0.0 collective-permute-start.16
  39.1 0.5 collective-permute-start.13
  39.6 0.2 collective-permute-done.15.refs_2_
  39.8 0.6 %collective-permute-done.16.refs_3_ = bf16[16,2560]{1,0:T(8,128)(2,1)S(1)} collective-permute-done((bf16[16,2560]{1,0:T(8,128)(2,1)S(1)}, bf16[16,2560]{1,0:T(8,128)(2,1)S(1)}, u32[]{:S(2)}, u32[]{:S(2)}) %collective-permute-start.16) | collective-permute-done | bytes 81952 | tf_op jit(solution)/shard_map/ppermute | solution.py:304
  40.5 1.5 %down.2.refs_1_.refs_5_ = f32[64,2048]{1,0:T(8,128)S(1)} custom-call(bf16[16,2560]{1,0:T(8,128)(2,1)S(1)} %get-tuple-element.34.refs_0_, bf16[16,2560]{1,0:T(8,128)(2,1)S(1)} %collective-permute-done.14.refs_0_.refs_1_, bf16[16,2560]{1,0:T(8,128)(2,1)S(1)} %collective-permute-done.15.refs_2_, bf16[16,2560]{1,0:T(8,128)(2,1)S(1)} %collective-permute-done.16.refs_3_, ...), custom_call_target="tpu_custom_call" | custom-call | bytes 1024 | tf_op jit(solution)/shard_map/down/pallas_call | solution.py:286
  42.0 0.6 %collective-permute-done.12.refs_0_.refs_1_ = bf16[16,4096]{1,0:T(8,128)(2,1)S(1)} collective-permute-done((bf16[16,4096]{1,0:T(8,128)(2,1)S(1)}, bf16[16,4096]{1,0:T(8,128)(2,1)S(1)}, u32[]{:S(2)}, u32[]{:S(2)}) %collective-permute-start.12) | collective-permute-done | bytes 131104 | tf_op jit(solution)/shard_map/ppermute | solution.py:304
  42.6 0.1 collective-permute-start.17
  42.7 0.0 collective-permute-done.13.refs_2_
  42.7 1.3 %collective-permute-done.17.refs_3_ = bf16[16,4096]{1,0:T(8,128)(2,1)S(1)} collective-permute-done((bf16[16,4096]{1,0:T(8,128)(2,1)S(1)}, bf16[16,4096]{1,0:T(8,128)(2,1)S(1)}, u32[]{:S(2)}, u32[]{:S(2)}) %collective-permute-start.17) | collective-permute-done | bytes 131104 | tf_op jit(solution)/shard_map/ppermute | solution.py:304
  44.0 2.4 %down.3 = (bf16[16,2048]{1,0:T(8,128)(2,1)S(1)}, bf16[16,2048]{1,0:T(8,128)(2,1)S(1)}, bf16[16,2048]{1,0:T(8,128)(2,1)S(1)}, bf16[16,2048]{1,0:T(8,128)(2,1)S(1)}) custom-call(bf16[16,4096]{1,0:T(8,128)(2,1)S(1)} %combine.3.refs_1_.refs_0_, bf16[16,4096]{1,0:T(8,128)(2,1)S(1)} %collective-permute-done.12.refs_0_.refs_1_, ...), custom_call_target="tpu_custom_call" | custom-call | bytes 1024 | tf_op jit(solution)/shard_map/down/pallas_call | solution.py:286
  46.4 3.5 %collective-permute-start.18 = (bf16[16,2048]{1,0:T(8,128)(2,1)S(1)}, bf16[16,2048]{1,0:T(8,128)(2,1)S(1)}, u32[]{:S(2)}, u32[]{:S(2)}) collective-permute-start(bf16[16,2048]{1,0:T(8,128)(2,1)S(1)} %get-tuple-element.36), channel_id=1, source_target_pairs={{0,12},{4,8},{8,4},{12,0},{1,13},{5,9},{9,5},{13,1},{2,14},{6,10},... | collective-permute-start | bytes 196616 | tf_op jit(solution)/shard_map/ppermute | solution.py:304
  49.9 1.0 %collective-permute-start.20 = (bf16[16,2048]{1,0:T(8,128)(2,1)S(1)}, bf16[16,2048]{1,0:T(8,128)(2,1)S(1)}, u32[]{:S(2)}, u32[]{:S(2)}) collective-permute-start(bf16[16,2048]{1,0:T(8,128)(2,1)S(1)} %get-tuple-element.38), channel_id=1, source_target_pairs={{0,4},{4,0},{8,12},{12,8},{1,5},{5,1},{9,13},{13,9},{2,6},{6,2},{1... | collective-permute-start | bytes 196616 | tf_op jit(solution)/shard_map/ppermute | solution.py:304
  50.8 2.3 %collective-permute-done.18 = bf16[16,2048]{1,0:T(8,128)(2,1)S(1)} collective-permute-done((bf16[16,2048]{1,0:T(8,128)(2,1)S(1)}, bf16[16,2048]{1,0:T(8,128)(2,1)S(1)}, u32[]{:S(2)}, u32[]{:S(2)}) %collective-permute-start.18) | collective-permute-done | bytes 65568 | tf_op jit(solution)/shard_map/ppermute | solution.py:304
  53.1 2.5 %collective-permute-done.19 = bf16[16,2048]{1,0:T(8,128)(2,1)S(1)} collective-permute-done((bf16[16,2048]{1,0:T(8,128)(2,1)S(1)}, bf16[16,2048]{1,0:T(8,128)(2,1)S(1)}, u32[]{:S(2)}, u32[]{:S(2)}) %collective-permute-start.19) | collective-permute-done | bytes 65568 | tf_op jit(solution)/shard_map/ppermute | solution.py:304
  55.6 0.7 %add_convert_fusion = bf16[16,2048]{1,0:T(8,128)(2,1)} fusion(bf16[16,2048]{1,0:T(8,128)(2,1)S(1)} %collective-permute-done.20, bf16[16,2048]{1,0:T(8,128)(2,1)S(1)} %collective-permute-done.19, bf16[16,2048]{1,0:T(8,128)(2,1)S(1)} %collective-permute-done.18, bf16[16,2048]{1,0:T(8,128)(2,1)S(1)} %get-tuple-element.35), kind=kLoop, calls=%fused_computation.1 | loop fusion | flops 262144 | bytes 327680 | tf_op jit(solution)/shard_map/convert_element_type | solution.py:349
  (28 shorter events, 0.2 us)
Async XLA Ops:
  0.0 11.6 %collective-permute-start.2 = (bf16[16,2048]{1,0:T(8,128)(2,1)}, bf16[16,2048]{1,0:T(8,128)(2,1)S(1)}, u32[]{:S(2)}, u32[]{:S(2)}) collective-permute-start(bf16[16,2048]{1,0:T(8,128)(2,1)} %tokens_ref.3), channel_id=1, source_target_pairs={{0,12},{4,8},{8,4},{12,0},{1,13},{5,9},{9,5},{13,1},{2,14},{6,10},... | collective-permute-start | bytes 196616 | tf_op jit(solution)/shard_map/ppermute | solution.py:304
  5.0 6.6 %collective-permute-start.1 = (bf16[16,2048]{1,0:T(8,128)(2,1)}, bf16[16,2048]{1,0:T(8,128)(2,1)S(1)}, u32[]{:S(2)}, u32[]{:S(2)}) collective-permute-start(bf16[16,2048]{1,0:T(8,128)(2,1)} %tokens_ref.3), channel_id=1, source_target_pairs={{0,8},{4,12},{8,0},{12,4},{1,9},{5,13},{9,1},{13,5},{2,10},{6,14},... | collective-permute-start | bytes 196616 | tf_op jit(solution)/shard_map/ppermute | solution.py:304
  5.1 6.6 %collective-permute-start = (bf16[16,2048]{1,0:T(8,128)(2,1)}, bf16[16,2048]{1,0:T(8,128)(2,1)S(1)}, u32[]{:S(2)}, u32[]{:S(2)}) collective-permute-start(bf16[16,2048]{1,0:T(8,128)(2,1)} %tokens_ref.3), channel_id=1, source_target_pairs={{0,4},{4,0},{8,12},{12,8},{1,5},{5,1},{9,13},{13,9},{2,6},{6,2},{1... | collective-permute-start | bytes 196616 | tf_op jit(solution)/shard_map/ppermute | solution.py:304
  5.6 6.0 %collective-permute-start.3 = (bf16[16,2048]{1,0:T(8,128)(2,1)}, bf16[16,2048]{1,0:T(8,128)(2,1)S(1)}, u32[]{:S(2)}, u32[]{:S(2)}) collective-permute-start(bf16[16,2048]{1,0:T(8,128)(2,1)} %tokens_ref.3), channel_id=1, source_target_pairs={{0,16},{16,0},{1,17},{17,1},{2,18},{18,2},{3,19},{19,3},{4,20},{20... | collective-permute-start | bytes 196616 | tf_op jit(solution)/shard_map/ppermute | solution.py:304
  11.7 5.7 %collective-permute-start.4 = (bf16[48,2048]{1,0:T(8,128)(2,1)S(1)}, bf16[48,2048]{1,0:T(8,128)(2,1)S(1)}, u32[]{:S(2)}, u32[]{:S(2)}) collective-permute-start(bf16[48,2048]{1,0:T(8,128)(2,1)S(1)} %join.3.refs_1_), channel_id=1, source_target_pairs={{0,16},{16,0},{1,17},{17,1},{2,18},{18,2},{3,19},{19,3},{4,20},{20... | collective-permute-start | bytes 589832 | tf_op jit(solution)/shard_map/ppermute | solution.py:304
  19.0 1.7 %collective-permute-start.5 = (bf16[2,64,1280]{2,1,0:T(8,128)(2,1)S(1)}, bf16[2,64,1280]{2,1,0:T(8,128)(2,1)S(1)}, u32[]{:S(2)}, u32[]{:S(2)}) collective-permute-start(bf16[2,64,1280]{2,1,0:T(8,128)(2,1)S(1)} %get-tuple-element.27), channel_id=1, source_target_pairs={{0,1},{1,0},{2,3},{3,2},{4,5},{5,4},{6,7},{7,6},{8,9},{9,8},{10,11... | collective-permute-start | bytes 983048 | tf_op jit(solution)/shard_map/ppermute | solution.py:304
  20.7 2.3 %collective-permute-start.6 = (bf16[2,64,1280]{2,1,0:T(8,128)(2,1)S(1)}, bf16[2,64,1280]{2,1,0:T(8,128)(2,1)S(1)}, u32[]{:S(2)}, u32[]{:S(2)}) collective-permute-start(bf16[2,64,1280]{2,1,0:T(8,128)(2,1)S(1)} %later.2), channel_id=1, source_target_pairs={{0,1},{1,0},{2,3},{3,2},{4,5},{5,4},{6,7},{7,6},{8,9},{9,8},{10,11... | collective-permute-start | bytes 983048 | tf_op jit(solution)/shard_map/ppermute | solution.py:304
  21.3 9.0 %collective-permute-start.7 = (bf16[2,32,1280]{2,1,0:T(8,128)(2,1)S(1)}, bf16[2,32,1280]{2,1,0:T(8,128)(2,1)S(1)}, u32[]{:S(2)}, u32[]{:S(2)}) collective-permute-start(bf16[2,32,1280]{2,1,0:T(8,128)(2,1)S(1)} %pair_sum.3.refs_4_), channel_id=1, source_target_pairs={{0,2},{1,3},{2,0},{3,1},{4,6},{5,7},{6,4},{7,5},{8,10},{9,11},{10,... | collective-permute-start | bytes 491528 | tf_op jit(solution)/shard_map/ppermute | solution.py:304
  23.0 17.4 %slice-start = ((s8[27262976]{0:T(1024)(128)(4,1)}), s8[4194304]{0:T(1024)(128)(4,1)S(1)}, s32[]{:S(2)}) async-start(s8[27262976]{0:T(1024)(128)(4,1)} %bitcast), calls=%async_computation | async-start | bytes 8388608
  23.1 17.3 %slice-start.1 = ((s8[27262976]{0:T(1024)(128)(4,1)}), s8[4194304]{0:T(1024)(128)(4,1)S(1)}, s32[]{:S(2)}) async-start(s8[27262976]{0:T(1024)(128)(4,1)} %bitcast), calls=%async_computation.1 | async-start | bytes 8388608
  23.1 17.3 %slice-start.2 = ((s8[27262976]{0:T(1024)(128)(4,1)}), s8[4194304]{0:T(1024)(128)(4,1)S(1)}, s32[]{:S(2)}) async-start(s8[27262976]{0:T(1024)(128)(4,1)} %bitcast), calls=%async_computation.2 | async-start | bytes 8388608
  23.1 17.3 %slice-start.3 = ((s8[27262976]{0:T(1024)(128)(4,1)}), s8[4194304]{0:T(1024)(128)(4,1)S(1)}, s32[]{:S(2)}) async-start(s8[27262976]{0:T(1024)(128)(4,1)} %bitcast), calls=%async_computation.3 | async-start | bytes 8388608
  23.1 17.3 %slice-start.4 = ((s8[27262976]{0:T(1024)(128)(4,1)}), s8[4194304]{0:T(1024)(128)(4,1)S(1)}, s32[]{:S(2)}) async-start(s8[27262976]{0:T(1024)(128)(4,1)} %bitcast), calls=%async_computation.4 | async-start | bytes 8388608
  23.1 17.3 %slice-start.5 = ((s8[27262976]{0:T(1024)(128)(4,1)}), s8[4194304]{0:T(1024)(128)(4,1)S(1)}, s32[]{:S(2)}) async-start(s8[27262976]{0:T(1024)(128)(4,1)} %bitcast), calls=%async_computation.5 | async-start | bytes 8388608
  23.1 17.3 %slice-start.6 = ((s8[27262976]{0:T(1024)(128)(4,1)}), s8[2097152]{0:T(1024)(128)(4,1)S(1)}, s32[]{:S(2)}) async-start(s8[27262976]{0:T(1024)(128)(4,1)} %bitcast), calls=%async_computation.6 | async-start | bytes 4194304
  23.1 7.9 %collective-permute-start.9 = (bf16[2,32,1280]{2,1,0:T(8,128)(2,1)S(1)}, bf16[2,32,1280]{2,1,0:T(8,128)(2,1)S(1)}, u32[]{:S(2)}, u32[]{:S(2)}) collective-permute-start(bf16[2,32,1280]{2,1,0:T(8,128)(2,1)S(1)} %pair_sum.4.refs_5_), channel_id=1, source_target_pairs={{0,2},{1,3},{2,0},{3,1},{4,6},{5,7},{6,4},{7,5},{8,10},{9,11},{10,... | collective-permute-start | bytes 491528 | tf_op jit(solution)/shard_map/ppermute | solution.py:304
  30.3 1.5 %collective-permute-start.8 = (bf16[2,32,1536]{2,1,0:T(8,128)(2,1)S(1)}, bf16[2,32,1536]{2,1,0:T(8,128)(2,1)S(1)}, u32[]{:S(2)}, u32[]{:S(2)}) collective-permute-start(bf16[2,32,1536]{2,1,0:T(8,128)(2,1)S(1)} %later.3), channel_id=1, source_target_pairs={{0,1},{1,0},{2,3},{3,2},{4,5},{5,4},{6,7},{7,6},{8,9},{9,8},{10,11... | collective-permute-start | bytes 589832 | tf_op jit(solution)/shard_map/ppermute | solution.py:304
  31.9 5.6 %collective-permute-start.10 = (bf16[2,16,1536]{2,1,0:T(8,128)(2,1)S(1)}, bf16[2,16,1536]{2,1,0:T(8,128)(2,1)S(1)}, u32[]{:S(2)}, u32[]{:S(2)}) collective-permute-start(bf16[2,16,1536]{2,1,0:T(8,128)(2,1)S(1)} %pair_sum.5), channel_id=1, source_target_pairs={{0,2},{1,3},{2,0},{3,1},{4,6},{5,7},{6,4},{7,5},{8,10},{9,11},{10,... | collective-permute-start | bytes 294920 | tf_op jit(solution)/shard_map/ppermute | solution.py:304
  33.0 4.4 %collective-permute-start.11 = (bf16[16,2560]{1,0:T(8,128)(2,1)S(1)}, bf16[16,2560]{1,0:T(8,128)(2,1)S(1)}, u32[]{:S(2)}, u32[]{:S(2)}) collective-permute-start(bf16[16,2560]{1,0:T(8,128)(2,1)S(1)} %get-tuple-element.33.refs_2_), channel_id=1, source_target_pairs={{0,16},{16,0},{1,17},{17,1},{2,18},{18,2},{3,19},{19,3},{4,20},{20... | collective-permute-start | bytes 245768 | tf_op jit(solution)/shard_map/ppermute | solution.py:304
  34.5 4.6 %collective-permute-start.14 = (bf16[16,2560]{1,0:T(8,128)(2,1)S(1)}, bf16[16,2560]{1,0:T(8,128)(2,1)S(1)}, u32[]{:S(2)}, u32[]{:S(2)}) collective-permute-start(bf16[16,2560]{1,0:T(8,128)(2,1)S(1)} %get-tuple-element.34.refs_0_), channel_id=1, source_target_pairs={{0,2},{1,3},{2,0},{3,1},{4,6},{5,7},{6,4},{7,5},{8,10},{9,11},{10,... | collective-permute-start | bytes 245768 | tf_op jit(solution)/shard_map/ppermute | solution.py:304
  37.5 5.0 %collective-permute-start.12 = (bf16[16,4096]{1,0:T(8,128)(2,1)S(1)}, bf16[16,4096]{1,0:T(8,128)(2,1)S(1)}, u32[]{:S(2)}, u32[]{:S(2)}) collective-permute-start(bf16[16,4096]{1,0:T(8,128)(2,1)S(1)} %combine.3.refs_1_.refs_0_), channel_id=1, source_target_pairs={{0,2},{1,3},{2,0},{3,1},{4,6},{5,7},{6,4},{7,5},{8,10},{9,11},{10,... | collective-permute-start | bytes 393224 | tf_op jit(solution)/shard_map/ppermute | solution.py:304
  38.5 1.3 %collective-permute-start.15 = (bf16[16,2560]{1,0:T(8,128)(2,1)S(1)}, bf16[16,2560]{1,0:T(8,128)(2,1)S(1)}, u32[]{:S(2)}, u32[]{:S(2)}) collective-permute-start(bf16[16,2560]{1,0:T(8,128)(2,1)S(1)} %get-tuple-element.34.refs_0_), channel_id=1, source_target_pairs={{0,1},{1,0},{2,3},{3,2},{4,5},{5,4},{6,7},{7,6},{8,9},{9,8},{10,11... | collective-permute-start | bytes 245768 | tf_op jit(solution)/shard_map/ppermute | solution.py:304
  39.1 1.3 %collective-permute-start.16 = (bf16[16,2560]{1,0:T(8,128)(2,1)S(1)}, bf16[16,2560]{1,0:T(8,128)(2,1)S(1)}, u32[]{:S(2)}, u32[]{:S(2)}) collective-permute-start(bf16[16,2560]{1,0:T(8,128)(2,1)S(1)} %join.4), channel_id=1, source_target_pairs={{0,1},{1,0},{2,3},{3,2},{4,5},{5,4},{6,7},{7,6},{8,9},{9,8},{10,11... | collective-permute-start | bytes 245768 | tf_op jit(solution)/shard_map/ppermute | solution.py:304
  39.1 3.5 %collective-permute-start.13 = (bf16[16,4096]{1,0:T(8,128)(2,1)S(1)}, bf16[16,4096]{1,0:T(8,128)(2,1)S(1)}, u32[]{:S(2)}, u32[]{:S(2)}) collective-permute-start(bf16[16,4096]{1,0:T(8,128)(2,1)S(1)} %combine.3.refs_1_.refs_0_), channel_id=1, source_target_pairs={{0,1},{1,0},{2,3},{3,2},{4,5},{5,4},{6,7},{7,6},{8,9},{9,8},{10,11... | collective-permute-start | bytes 393224 | tf_op jit(solution)/shard_map/ppermute | solution.py:304
  42.6 1.4 %collective-permute-start.17 = (bf16[16,4096]{1,0:T(8,128)(2,1)S(1)}, bf16[16,4096]{1,0:T(8,128)(2,1)S(1)}, u32[]{:S(2)}, u32[]{:S(2)}) collective-permute-start(bf16[16,4096]{1,0:T(8,128)(2,1)S(1)} %join.5), channel_id=1, source_target_pairs={{0,1},{1,0},{2,3},{3,2},{4,5},{5,4},{6,7},{7,6},{8,9},{9,8},{10,11... | collective-permute-start | bytes 393224 | tf_op jit(solution)/shard_map/ppermute | solution.py:304
  46.4 6.7 %collective-permute-start.18 = (bf16[16,2048]{1,0:T(8,128)(2,1)S(1)}, bf16[16,2048]{1,0:T(8,128)(2,1)S(1)}, u32[]{:S(2)}, u32[]{:S(2)}) collective-permute-start(bf16[16,2048]{1,0:T(8,128)(2,1)S(1)} %get-tuple-element.36), channel_id=1, source_target_pairs={{0,12},{4,8},{8,4},{12,0},{1,13},{5,9},{9,5},{13,1},{2,14},{6,10},... | collective-permute-start | bytes 196616 | tf_op jit(solution)/shard_map/ppermute | solution.py:304
  49.9 5.8 %collective-permute-start.19 = (bf16[16,2048]{1,0:T(8,128)(2,1)S(1)}, bf16[16,2048]{1,0:T(8,128)(2,1)S(1)}, u32[]{:S(2)}, u32[]{:S(2)}) collective-permute-start(bf16[16,2048]{1,0:T(8,128)(2,1)S(1)} %get-tuple-element.37), channel_id=1, source_target_pairs={{0,8},{4,12},{8,0},{12,4},{1,9},{5,13},{9,1},{13,5},{2,10},{6,14},... | collective-permute-start | bytes 196616 | tf_op jit(solution)/shard_map/ppermute | solution.py:304
  49.9 5.8 %collective-permute-start.20 = (bf16[16,2048]{1,0:T(8,128)(2,1)S(1)}, bf16[16,2048]{1,0:T(8,128)(2,1)S(1)}, u32[]{:S(2)}, u32[]{:S(2)}) collective-permute-start(bf16[16,2048]{1,0:T(8,128)(2,1)S(1)} %get-tuple-element.38), channel_id=1, source_target_pairs={{0,4},{4,0},{8,12},{12,8},{1,5},{5,1},{9,13},{13,9},{2,6},{6,2},{1... | collective-permute-start | bytes 196616 | tf_op jit(solution)/shard_map/ppermute | solution.py:304
